TPU v7x, 32 devices: a whole 2x2x4 slice. The times are simulated.
32 devices in a mesh: dp: 8 (over z, x), tensor: 4 (over y, core).
Axes of the slice: x: 2, y: 2, z: 4, core: 2. Of those that a mesh axis runs over, the one named last changes fastest.
Arguments:
- hidden_pre: bfloat16 [8256, 6144], P('dp', 'tensor'), may hold values from -6 to 6
- cotangent: bfloat16 [8256, 1536], P('dp', 'tensor'), may hold values from -6 to 6
- down_weight: bfloat16 [1536, 6144], P(None, 'tensor'), may hold values from -0.078125 to 0.078125
- layer_scale: float32 [1536], replicated, may hold values from 0.3 to 3
- crop_lengths: int32 [8, 4], replicated, may hold values from 0 to 257, as said below
- crop_moves: int32 [8, 4], replicated, may hold values from 0 to 1, as said below
Outputs:
- hidden_grad: bfloat16 [5760, 6144], P('dp', 'tensor')
- down_grad: float32 [1536, 6144], P('dp', 'tensor')
Inputs may be any that keep to these rules, and one draw needn't show every extreme that they name: `crop_lengths`: devices d and d + 4 form a pair: in each pair one device holds crops of 257 or 50 tokens in every slot, the other crops of 50 tokens or empty slots (0). Some device holds 1028 tokens. `crop_moves`: only the first kind of device of a pair moves crops, exactly 2 of its slots, to its partner; a device holds at most 714 tokens after the moves and sends at most 514, and both are reached.
All inputs are finite; a program needn't handle non-finite values.
Results may differ from a plain program's by a relative error of at most 0.005.
Values may be sent and summed in bfloat16 or wider, within the bound.
No kernel may reach another device: no remote copies, remote signals or barrier semaphores. Data moves between devices by JAX's collectives and lax.ppermute only.
A program may use at most 64 MiB of HBM per device.

v0:
```python
import math

import jax
import jax.numpy as jnp
from jax import lax
from jax.sharding import PartitionSpec as P

SEND = 520
BAL = 720


inv_root_two = 0.7071067811865476
inv_root_tau = 0.3989422804014327


def shifted(block, axis, distance):
    devices = range(lax.axis_size(axis))
    route = [((i - distance) % len(devices), i) for i in devices]
    return lax.ppermute(block, axis, route)


def gelu_parts(pre_act):
    cumulative = 0.5 * (1.0 + jax.scipy.special.erf(pre_act * inv_root_two))
    activated = pre_act * cumulative
    derivative = cumulative + pre_act * jnp.exp(-0.5 * pre_act * pre_act) * inv_root_tau
    return (activated, derivative)


def crop_rows(row_total, crop_sizes, crop_starts):
    crop_ends = jnp.cumsum(crop_sizes)
    crop_begins = crop_ends - crop_sizes
    target_rows = jnp.arange(row_total, dtype=jnp.int32)[:, None]
    inside_crop = (target_rows >= crop_begins[None, :]) & (target_rows < crop_ends[None, :])
    source_rows = jnp.sum(
        jnp.where(inside_crop, crop_starts[None, :] + target_rows - crop_begins[None, :], 0), axis=1
    )
    return (source_rows, jnp.any(inside_crop, axis=1))


def select_rows(row_block, source_rows, valid_rows):
    taken = jnp.take(row_block, source_rows, axis=0)
    return jnp.where(valid_rows[:, None], taken, jnp.zeros((), row_block.dtype))


def local_grads(pre_rows, cot_part, live_rows, layer_scale, down_weight, home_rows):
    cot_full = lax.all_gather(cot_part, "tensor", axis=1, tiled=True)
    scaled = (cot_full.astype(jnp.float32) * layer_scale[None, :]).astype(jnp.bfloat16)
    activated, derivative = gelu_parts(pre_rows.astype(jnp.float32))
    activation = jnp.where(live_rows[:, None], activated, 0.0).astype(jnp.bfloat16)
    backward = jnp.dot(scaled, down_weight, preferred_element_type=jnp.float32) * derivative
    gradient_rows = jnp.where(live_rows[:, None], backward, 0.0).astype(jnp.bfloat16)
    weight_grad = lax.psum_scatter(
        lax.dot_general(
            scaled, activation, (((0,), (0,)), ((), ())), preferred_element_type=jnp.float32
        ),
        "dp",
        scatter_dimension=0,
        tiled=True,
    )
    return (gradient_rows, weight_grad / math.sqrt(lax.axis_size("dp") * home_rows))


def shards(hidden_pre, cotangent, down_weight, layer_scale, crop_lengths, crop_moves):
    devices = lax.axis_size("dp")
    half_axis = devices // 2
    device_index = lax.axis_index("dp")
    partner_index = (device_index + half_axis) % devices
    own_lengths = lax.dynamic_index_in_dim(crop_lengths, device_index, 0, keepdims=False)
    own_moves = lax.dynamic_index_in_dim(crop_moves, device_index, 0, keepdims=False)
    partner_lengths = lax.dynamic_index_in_dim(crop_lengths, partner_index, 0, keepdims=False)
    partner_moves = lax.dynamic_index_in_dim(crop_moves, partner_index, 0, keepdims=False)
    home_rows = hidden_pre.shape[0]
    own_starts = jnp.cumsum(own_lengths) - own_lengths
    sent_sizes = own_lengths * own_moves
    kept_sizes = own_lengths * (1 - own_moves)
    arrived = jnp.sum(partner_lengths * partner_moves)
    send_source, send_valid = crop_rows(SEND, sent_sizes, own_starts)
    keep_sizes = jnp.concatenate([kept_sizes, arrived[None]])
    keep_starts = jnp.concatenate([own_starts, jnp.full((1,), home_rows, jnp.int32)])
    keep_source, keep_valid = crop_rows(BAL, keep_sizes, keep_starts)
    live_home = jnp.arange(home_rows, dtype=jnp.int32) < jnp.sum(own_lengths)
    gradient_rows, weight_grad = local_grads(
        hidden_pre, cotangent, live_home, layer_scale, down_weight, home_rows
    )
    outgoing = select_rows(gradient_rows, send_source, send_valid)
    incoming = shifted(outgoing, "dp", half_axis)
    balanced = select_rows(jnp.concatenate([gradient_rows, incoming], 0), keep_source, keep_valid)
    return (balanced, weight_grad)


def solution(mesh):
    return jax.shard_map(
        shards,
        mesh=mesh,
        in_specs=(P("dp", "tensor"), P("dp", "tensor"), P(None, "tensor"), P(), P(), P()),
        out_specs=(P("dp", "tensor"), P("dp", "tensor")),
        check_vma=False,
    )
```

profile of v0, /device:TPU:0, one launch (start us, length us, event | category | flops | bytes accessed | tf_op | source)
XLA Modules:
  0.0 292.2 jit_solution(7969945494018915894)
XLA Ops:
  7.2 0.7 all-gather.2.cloned.1.call-update
  8.0 1.5 fusion.24
  9.5 0.7 iota_compare_fusion.4
  10.2 30.8 %all-gather.2.cloned.1.call-done = bf16[1032,1536]{1,0:T(8,128)(2,1)} async-done(((bf16[1032,384]{1,0:T(8,128)(2,1)}), bf16[1032,1536]{1,0:T(8,128)(2,1)}) %all-gather.2.cloned.1.call-update) | async-done | bytes 3170320 | tf_op jit(solution)/shard_map/all_gather | solution.py:46
  40.9 12.3 %fusion.10 = f32[1536,1536]{1,0:T(8,128)} fusion(bf16[1032,1536]{1,0:T(8,128)(2,1)} %param.6, pred[1032]{0:T(1024)(128)(4,1)S(1)} %iota_compare_fusion.4, bf16[1032,1536]{1,0:T(8,128)(2,1)} %all-gather.2.cloned.1.call-done, f32[1536]{0:T(1024)} %param.9), kind=kOutput, calls=%fused_computation.20 | convolution fusion | flops 4885438464 | bytes 15784968 | tf_op jit(solution)/shard_map/dot_general | solution.py:53
  53.2 0.1 copy.14
  53.3 0.1 copy.15
  53.4 0.2 reduce-window.18
  53.6 0.2 reduce-window.19
  53.9 0.1 fusion.22
  54.0 9.8 %fusion.1 = bf16[1032,1536]{1,0:T(8,128)(2,1)S(1)} fusion(bf16[1536,1536]{1,0:T(8,128)(2,1)} %param.8, bf16[1032,1536]{1,0:T(8,128)(2,1)} %param.6, pred[1032]{0:T(1024)(128)(4,1)S(1)} %iota_compare_fusion.4, bf16[1032,1536]{1,0:T(8,128)(2,1)} %all-gather.2.cloned.1.call-done, f32[1536]{0:T(1024)S(1)} %copy-done), kind=kOutput, calls=%fused_computation.9 | convolution fusion | flops 4893364224 | bytes 14236680 | tf_op jit(solution)/shard_map/dot_general | solution.py:50
  63.9 3.5 %gather_fusion = bf16[520,1536]{1,0:T(8,128)(2,1)} fusion(bf16[1032,1536]{1,0:T(8,128)(2,1)S(1)} %fusion.1, s32[1024]{0:T(1024)S(1)} %pad_clamp_fusion.1), kind=kCustom, calls=%fused_computation | custom fusion | bytes 3196960 | tf_op jit(solution)/shard_map/jit(_take)/gather | solution.py:41
  67.4 2.8 select_select_fusion.1
  70.2 2.4 collective-permute-start
  72.7 0.7 add_bitcast_fusion
  73.4 0.2 reduce-window.14
  73.6 0.7 add_subtract_fusion
  74.5 0.1 fusion.15
  74.6 134.0 %collective-permute-done = bf16[520,1536]{1,0:T(8,128)(2,1)} collective-permute-done((bf16[520,1536]{1,0:T(8,128)(2,1)}, bf16[520,1536]{1,0:T(8,128)(2,1)}, u32[]{:S(2)}, u32[]{:S(2)}) %collective-permute-start) | collective-permute-done | bytes 1597472 | tf_op jit(solution)/shard_map/ppermute | solution.py:19
  208.6 4.0 %pad_maximum_fusion = bf16[1552,1536]{1,0:T(8,128)(2,1)} fusion(bf16[520,1536]{1,0:T(8,128)(2,1)} %collective-permute-done, bf16[1032,1536]{1,0:T(8,128)(2,1)S(1)} %fusion.1), kind=kLoop, calls=%fused_computation.19 | loop fusion | flops 9535488 | bytes 9535488 | tf_op jit(solution)/shard_map/concatenate | solution.py:87
  212.6 8.3 %gather_fusion.1 = bf16[720,1536]{1,0:T(8,128)(2,1)S(1)} fusion(bf16[1552,1536]{1,0:T(8,128)(2,1)} %pad_maximum_fusion, s32[1024]{0:T(1024)S(1)} %pad_clamp_fusion), kind=kCustom, calls=%fused_computation.1 | custom fusion | bytes 4426560 | tf_op jit(solution)/shard_map/jit(_take)/gather | solution.py:41
  220.9 1.7 select_select_fusion
  222.6 60.4 %reduce-scatter.2.cloned.1.call-done = f32[192,1536]{1,0:T(8,128)} async-done(((f32[1536,1536]{1,0:T(8,128)}), f32[192,1536]{1,0:T(8,128)}) %reduce-scatter.2.cloned.1.call-update) | async-done | bytes 1179664 | tf_op jit(solution)/shard_map/reduce_scatter | solution.py:52
  283.0 2.4 broadcast_multiply_fusion
  (17 shorter events, 0.4 us)
Async XLA Ops:
  7.2 33.8 %all-gather.2.cloned.1.call-start = ((), (), s32[]{:S(2)}) async-start(), calls=%async_computation.1 | async-start | bytes 3962880 | tf_op jit(solution)/shard_map/all_gather | solution.py:46
  7.9 275.1 %reduce-scatter.2.cloned.1.call-start = ((), (), s32[]{:S(2)}) async-start(), calls=%async_computation.2 | async-start | bytes 10616832 | tf_op jit(solution)/shard_map/reduce_scatter | solution.py:52
  53.2 0.8 copy-start
  70.2 138.4 %collective-permute-start = (bf16[520,1536]{1,0:T(8,128)(2,1)}, bf16[520,1536]{1,0:T(8,128)(2,1)}, u32[]{:S(2)}, u32[]{:S(2)}) collective-permute-start(bf16[520,1536]{1,0:T(8,128)(2,1)} %select_select_fusion.1), channel_id=1, source_target_pairs={{16,0},{20,4},{24,8},{28,12},{0,16},{4,20},{8,24},{12,28},{17,1},{... | collective-permute-start | bytes 4792328 | tf_op jit(solution)/shard_map/ppermute | solution.py:19
Sparse Core Ops, SparseCore 0:
  9.6 31.3 all-gather.1
  53.4 229.5 reduce-scatter.1
where the time goes:
time: 293 us; the launch traced here: 292 us
  waiting for transfers between devices  226 us (77%)
  matrix products  22.1 us (8%)
  other arithmetic  15.5 us (5%)
  between operations  14.1 us (5%)
  local copies, waits for them, and re-layouts  12 us (4%)
    ppermute x1, waiting for transfers between devices, shifted(): return lax.ppermute(block, axis, route)  134 us
    reduce_scatter x1, waiting for transfers between devices, local_grads(): lax.psum_scatter(lax.dot_general(scaled, activation, (((0,), (0,)), ((),...  60.4 us
    all_gather x1, waiting for transfers between devices, local_grads(): cot_full = lax.all_gather(cot_part, 'tensor', axis=1, tiled=True)  30.8 us
    dot_general x1, matrix products, local_grads(): lax.dot_general(scaled, activation, (((0,), (0,)), ((), ())), preferred_e...  12.3 us
    gather x2, local copies, waits for them, and re-layouts, select_rows(): taken = jnp.take(row_block, source_rows, axis=0)  11.9 us
    dot_general x1, matrix products, local_grads(): jnp.dot(scaled, down_weight, preferred_element_type=jnp.float32)  9.83 us
  transfers between devices with their start and end apart: 3, of which 3 were waited for; matrix products, arithmetic and copies ran while one was open for 12% of the time, Pallas kernels for 0%

commit v1 on v0

--- a/solution.py
+++ b/solution.py
@@ -1,29 +1,289 @@
+import functools
 import math
 
 import jax
 import jax.numpy as jnp
 from jax import lax
+from jax.experimental import pallas as pl
+from jax.experimental.pallas import tpu as pltpu
 from jax.sharding import PartitionSpec as P
 
-SEND = 520
+SEND = 528
+KEEP = 528
+TILE = 16
 BAL = 720
-
+BF = jnp.bfloat16
+F32 = jnp.float32
 
 inv_root_two = 0.7071067811865476
 inv_root_tau = 0.3989422804014327
+
+
+def call(kernel, grid, scalars, in_specs, out_specs, out_shape, scratch, flops, nbytes, trans=0):
+    return pl.pallas_call(
+        kernel,
+        grid_spec=pltpu.PrefetchScalarGridSpec(
+            num_scalar_prefetch=scalars,
+            grid=grid,
+            in_specs=in_specs,
+            out_specs=out_specs,
+            scratch_shapes=scratch,
+        ),
+        out_shape=out_shape,
+        cost_estimate=pl.CostEstimate(flops=flops, bytes_accessed=nbytes, transcendentals=trans),
+        compiler_params=pltpu.CompilerParams(vmem_limit_bytes=48 * 1024 * 1024),
+    )
+
+
+def whole(shape):
+    return pl.BlockSpec(shape, lambda *_: (0,) * len(shape))
+
+
+def kept_total(lens, moves, d):
+    return sum(lens[d, j] * (1 - moves[d, j]) for j in range(lens.shape[1]))
+
+
+def picks(lens, moves, d, moved, first, rows, home):
+    at = lax.broadcasted_iota(jnp.int32, (rows, 1), 0) - first
+    source = jnp.full((rows, 1), -1, jnp.int32)
+    begin = jnp.int32(0)
+    start = jnp.int32(0)
+    for j in range(lens.shape[1]):
+        length = lens[d, j]
+        size = length * (moves[d, j] if moved else 1 - moves[d, j])
+        inside = (at >= begin) & (at < begin + size)
+        source = jnp.where(inside, at + (start - begin), source)
+        begin = begin + size
+        start = start + length
+    columns = lax.broadcasted_iota(jnp.int32, (rows, home), 1)
+    return jnp.where(columns == source, 1.0, 0.0).astype(BF)
+
+
+def both_picks(place, lens, moves, home):
+    d = place[0]
+    n = lens.shape[0]
+    partner = lax.rem(d + n // 2, n)
+    first = lax.rem(kept_total(lens, moves, partner), TILE)
+    sent = picks(lens, moves, d, True, first, SEND, home)
+    kept = picks(lens, moves, d, False, 0, KEEP, home)
+    return sent, kept
+
+
+def scaled_kernel(place, lens, moves, cot, scale, sent_out, kept_out):
+    sent, kept = both_picks(place, lens, moves, cot.shape[0])
+    for pick, out in ((sent, sent_out), (kept, kept_out)):
+        rows = jnp.dot(pick, cot[...], preferred_element_type=F32)
+        out[...] = (rows * scale[...]).astype(BF)
+
+
+def gelu_kernel(place, lens, moves, pre, act_out, der_out, pick, rows_f32):
+    home = pre.shape[0]
+
+    @pl.when(pl.program_id(0) == 0)
+    def _():
+        sent, kept = both_picks(place, lens, moves, home)
+        pick[0:SEND, :] = sent
+        pick[SEND : SEND + KEEP, :] = kept
+
+    rows_f32[...] = jnp.dot(pick[...], pre[...], preferred_element_type=F32)
+    step = 3 * TILE
+
+    def body(i, _):
+        at = pl.ds(pl.multiple_of(i * step, step), step)
+        x = rows_f32[at, :]
+        cumulative = 0.5 * (1.0 + lax.erf(x * inv_root_two))
+        act_out[at, :] = (x * cumulative).astype(BF)
+        der_out[at, :] = cumulative + x * jnp.exp(-0.5 * x * x) * inv_root_tau
+        return 0
+
+    lax.fori_loop(0, (SEND + KEEP) // step, body, 0)
+
+
+def assemble(place, pieces, lhs):
+    t = place[1]
+    width = pieces[0].shape[1]
+    for j, piece in enumerate(pieces):
+        at = pl.ds(pl.multiple_of((t ^ j) * width, 128), width)
+        lhs[:, at] = piece[...]
+
+
+def grad_kernel(chunks, place, p0, p1, p2, p3, weight, der, *rest):
+    outs, lhs = rest[:chunks], rest[chunks]
+    step = pl.program_id(0)
+
+    @pl.when(step == 0)
+    def _():
+        assemble(place, (p0, p1, p2, p3), lhs)
+
+    value = (jnp.dot(lhs[...], weight[...], preferred_element_type=F32) * der[...]).astype(BF)
+    for c in range(chunks):
+
+        @pl.when(step == c)
+        def _():
+            outs[c][...] = value
+
+
+def weight_kernel(place, sent, kept, act, send_out, keep_out, lhs):
+    @pl.when(pl.program_id(0) == 0)
+    def _():
+        both = jnp.concatenate([sent[...], kept[...]], axis=0).astype(F32).T.astype(BF)
+        half = both.shape[0] // 2
+        mine = place[0] % 2 == 0
+        lo, hi = both[:half], both[half:]
+        lhs[0:half, :] = jnp.where(mine, hi, lo)
+        lhs[half : 2 * half, :] = jnp.where(mine, lo, hi)
+
+    half = lhs.shape[0] // 2
+    value = jnp.dot(lhs[...], act[...], preferred_element_type=F32)
+    send_out[...] = value[:half].astype(BF)
+    keep_out[...] = value[half:]
+
+
+def place_kernel(place, lens, moves, kept, *rest):
+    incoming, out = rest[:-1], rest[-1]
+    d = place[0]
+    count = kept_total(lens, moves, d)
+    first = jnp.minimum(count - lax.rem(count, TILE), BAL - SEND)
+    first = pl.multiple_of(first, TILE)
+    out[0:KEEP, :] = kept[...]
+    out[KEEP:, :] = jnp.zeros((out.shape[0] - KEEP, out.shape[1]), BF)
+    rows = lax.broadcasted_iota(jnp.int32, (SEND, 1), 0) + first
+    step = pl.program_id(0)
+    window = pl.ds(first, SEND)
+    for c, block in enumerate(incoming):
+
+        @pl.when(step == c)
+        def _():
+            out[window, :] = jnp.where(rows < count, out[window, :], block[...])
+
+
+def swapped(block, axis, distance):
+    n = lax.axis_size(axis)
+    return lax.ppermute(block, axis, [(i, i ^ distance) for i in range(n)])
+
+
+def shards(hidden_pre, cotangent, down_weight, layer_scale, crop_lengths, crop_moves):
+    home, ff = hidden_pre.shape
+    width = cotangent.shape[1]
+    features = down_weight.shape[0]
+    n = lax.axis_size("dp")
+    d = lax.axis_index("dp").astype(jnp.int32)
+    t = lax.axis_index("tensor").astype(jnp.int32)
+    place = jnp.stack([d, t])
+    rows = SEND + KEEP
+    scale = layer_scale.reshape(1, features)
+
+    sent, kept = call(
+        scaled_kernel, (1,), 3,
+        [whole((home, width)), pl.BlockSpec((1, width), lambda i, place, *_: (0, place[1]))],
+        [whole((SEND, width)), whole((KEEP, width))],
+        [jax.ShapeDtypeStruct((SEND, width), BF), jax.ShapeDtypeStruct((KEEP, width), BF)],
+        [], 2 * rows * home * width, 2 * (rows + home) * width,
+    )(place, crop_lengths, crop_moves, cotangent, scale)
+
+    sent_y, sent_c = swapped(sent, "tensor", 2), swapped(sent, "tensor", 1)
+    kept_y, kept_c = swapped(kept, "tensor", 2), swapped(kept, "tensor", 1)
+    sent_yc, kept_yc = swapped(sent_y, "tensor", 1), swapped(kept_y, "tensor", 1)
+    sents = (sent, sent_c, sent_y, sent_yc)
+    kepts = (kept, kept_c, kept_y, kept_yc)
+
+    cols = 256
+    act, der = call(
+        gelu_kernel, (ff // cols,), 3,
+        [pl.BlockSpec((home, cols), lambda i, *_: (0, i))],
+        [pl.BlockSpec((rows, cols), lambda i, *_: (0, i))] * 2,
+        [jax.ShapeDtypeStruct((rows, ff), BF), jax.ShapeDtypeStruct((rows, ff), F32)],
+        [pltpu.VMEM((rows, home), BF), pltpu.VMEM((rows, cols), F32)],
+        2 * rows * home * ff, 2 * home * ff + 6 * rows * ff, 2 * rows * ff,
+    )(place, crop_lengths, crop_moves, hidden_pre)
+
+    def grads(pieces, half, chunks):
+        cols = ff // 4
+        count = pieces[0].shape[0]
+        if chunks == 1:
+            out_specs = [pl.BlockSpec((count, cols), lambda i, *_: (0, i))]
+            out_shape = [jax.ShapeDtypeStruct((count, ff), BF)]
+            kernel = functools.partial(grad_one_kernel)
+        else:
+            out_specs = [whole((count, cols))] * chunks
+            out_shape = [jax.ShapeDtypeStruct((count, cols), BF)] * chunks
+            kernel = functools.partial(grad_kernel, chunks)
+        return call(
+            kernel, (4,), 1,
+            [whole((count, width))] * 4
+            + [
+                pl.BlockSpec((features, cols), lambda i, *_: (0, i)),
+                pl.BlockSpec((count, cols), lambda i, *_: (half, i)),
+            ],
+            out_specs, out_shape, [pltpu.VMEM((count, features), BF)],
+            2 * count * features * ff, 2 * features * ff + 6 * count * ff,
+        )(place, *pieces, down_weight, der)
+
+    def weight_piece(j):
+        block = 512 if ff % 512 == 0 else ff
+        half = width // 2
+        return call(
+            weight_kernel, (ff // block,), 1,
+            [whole((SEND, width)), whole((KEEP, width)), pl.BlockSpec((rows, block), lambda i, *_: (0, i))],
+            [pl.BlockSpec((half, block), lambda i, *_: (0, i))] * 2,
+            [jax.ShapeDtypeStruct((half, ff), BF), jax.ShapeDtypeStruct((half, ff), F32)],
+            [pltpu.VMEM((width, rows), BF)],
+            2 * rows * width * ff, 2 * rows * ff + 3 * width * ff,
+        )(place, sents[j], kepts[j], act)
+
+    moving = grads(sents, 0, 4)
+    arrived = [swapped(block, "dp", n // 2) for block in moving]
+
+    held = []
+    for j in range(4):
+        out, keep = weight_piece(j)
+        held.append(keep + swapped(out, "dp", 1).astype(F32))
+    near = ((d // 2) ^ t) % 2 == 0
+    held_near = []
+    for a, b in ((held[0], held[1]), (held[2], held[3])):
+        out = jnp.where(near, b, a).astype(BF)
+        held_near.append(jnp.where(near, a, b) + swapped(out, "dp", 2).astype(F32))
+    far = ((d // 4) ^ (t // 2)) % 2 == 0
+    a, b = held_near
+    out = jnp.where(far, b, a).astype(BF)
+    total = jnp.where(far, a, b) + swapped(out, "dp", 4).astype(F32)
+    down_grad = total / math.sqrt(n * home)
+
+    kept_grad = grads(kepts, 1, 1)[0]
+    quarter = ff // 4
+    hidden_grad = call(
+        place_kernel, (4,), 3,
+        [pl.BlockSpec((KEEP, quarter), lambda i, *_: (0, i))] + [whole((SEND, quarter))] * 4,
+        pl.BlockSpec((BAL, quarter), lambda i, *_: (0, i)),
+        jax.ShapeDtypeStruct((BAL, ff), BF),
+        [], 0, 2 * ff * (BAL + KEEP + SEND),
+    )(place, crop_lengths, crop_moves, kept_grad, *arrived)
+    return (hidden_grad, down_grad)
+
+
+def grad_one_kernel(place, p0, p1, p2, p3, weight, der, out, lhs):
+    @pl.when(pl.program_id(0) == 0)
+    def _():
+        assemble(place, (p0, p1, p2, p3), lhs)
+
+    out[...] = (jnp.dot(lhs[...], weight[...], preferred_element_type=F32) * der[...]).astype(BF)
+
+
+def solution(mesh):
+    from_start = (mesh.shape["dp"], mesh.shape["tensor"]) != (8, 4)
+    return jax.shard_map(
+        general_shards if from_start else shards,
+        mesh=mesh,
+        in_specs=(P("dp", "tensor"), P("dp", "tensor"), P(None, "tensor"), P(), P(), P()),
+        out_specs=(P("dp", "tensor"), P("dp", "tensor")),
+        check_vma=False,
+    )
 
 
 def shifted(block, axis, distance):
     devices = range(lax.axis_size(axis))
     route = [((i - distance) % len(devices), i) for i in devices]
     return lax.ppermute(block, axis, route)
-
-
-def gelu_parts(pre_act):
-    cumulative = 0.5 * (1.0 + jax.scipy.special.erf(pre_act * inv_root_two))
-    activated = pre_act * cumulative
-    derivative = cumulative + pre_act * jnp.exp(-0.5 * pre_act * pre_act) * inv_root_tau
-    return (activated, derivative)
 
 
 def crop_rows(row_total, crop_sizes, crop_starts):
@@ -42,17 +302,22 @@
     return jnp.where(valid_rows[:, None], taken, jnp.zeros((), row_block.dtype))
 
 
+def gelu_parts(pre_act):
+    cumulative = 0.5 * (1.0 + jax.scipy.special.erf(pre_act * inv_root_two))
+    activated = pre_act * cumulative
+    derivative = cumulative + pre_act * jnp.exp(-0.5 * pre_act * pre_act) * inv_root_tau
+    return (activated, derivative)
+
+
 def local_grads(pre_rows, cot_part, live_rows, layer_scale, down_weight, home_rows):
     cot_full = lax.all_gather(cot_part, "tensor", axis=1, tiled=True)
-    scaled = (cot_full.astype(jnp.float32) * layer_scale[None, :]).astype(jnp.bfloat16)
-    activated, derivative = gelu_parts(pre_rows.astype(jnp.float32))
-    activation = jnp.where(live_rows[:, None], activated, 0.0).astype(jnp.bfloat16)
-    backward = jnp.dot(scaled, down_weight, preferred_element_type=jnp.float32) * derivative
-    gradient_rows = jnp.where(live_rows[:, None], backward, 0.0).astype(jnp.bfloat16)
+    scaled = (cot_full.astype(F32) * layer_scale[None, :]).astype(BF)
+    activated, derivative = gelu_parts(pre_rows.astype(F32))
+    activation = jnp.where(live_rows[:, None], activated, 0.0).astype(BF)
+    backward = jnp.dot(scaled, down_weight, preferred_element_type=F32) * derivative
+    gradient_rows = jnp.where(live_rows[:, None], backward, 0.0).astype(BF)
     weight_grad = lax.psum_scatter(
-        lax.dot_general(
-            scaled, activation, (((0,), (0,)), ((), ())), preferred_element_type=jnp.float32
-        ),
+        lax.dot_general(scaled, activation, (((0,), (0,)), ((), ())), preferred_element_type=F32),
         "dp",
         scatter_dimension=0,
         tiled=True,
@@ -60,7 +325,7 @@
     return (gradient_rows, weight_grad / math.sqrt(lax.axis_size("dp") * home_rows))
 
 
-def shards(hidden_pre, cotangent, down_weight, layer_scale, crop_lengths, crop_moves):
+def general_shards(hidden_pre, cotangent, down_weight, layer_scale, crop_lengths, crop_moves):
     devices = lax.axis_size("dp")
     half_axis = devices // 2
     device_index = lax.axis_index("dp")
@@ -86,13 +351,3 @@
     incoming = shifted(outgoing, "dp", half_axis)
     balanced = select_rows(jnp.concatenate([gradient_rows, incoming], 0), keep_source, keep_valid)
     return (balanced, weight_grad)
-
-
-def solution(mesh):
-    return jax.shard_map(
-        shards,
-        mesh=mesh,
-        in_specs=(P("dp", "tensor"), P("dp", "tensor"), P(None, "tensor"), P(), P(), P()),
-        out_specs=(P("dp", "tensor"), P("dp", "tensor")),
-        check_vma=False,
-    )

time: 293 us -> 206 us (0.70)
  waiting for transfers between devices: 226 us -> 120 us
  Pallas kernels: 0 us -> 47.3 us
  matrix products: 22.1 us -> 0 us
  starting transfers between devices: 2.52 us -> 20.4 us
  between operations: 14.1 us -> 0.81 us
  other arithmetic: 15.5 us -> 9.3 us
  local copies, waits for them, and re-layouts: 12 us -> 8.24 us
    reduce_scatter x1 -> x0, waiting for transfers between devices: 60.4 us -> none  [local_grads(): lax.psum_scatter(lax.dot_general(scaled, activation, (((0,), (0,)), ((),...]
    pallas_call x0 -> x9, Pallas kernels: none -> 47.3 us  [the longest x4 15.4 us: weight_piece(): call(weight_kernel, (ff // block,), 1, [whole((SEND, width)), whole((KEEP...]
    all_gather x1 -> x0, waiting for transfers between devices: 30.8 us -> none  [local_grads(): cot_full = lax.all_gather(cot_part, 'tensor', axis=1, tiled=True)]
    dot_general x2 -> x0, matrix products: 22.1 us -> none  [the longest x1 12.3 us: local_grads(): lax.dot_general(scaled, activation, (((0,), (0,)), ((), ())), preferred_e...]
    ppermute x1 -> x17, starting transfers between devices: 2.44 us -> 20.4 us  [swapped(): return lax.ppermute(block, axis, [(i, i ^ distance) for i in range(n)])]
    ppermute x1 -> x17, waiting for transfers between devices: 134 us -> 120 us  [swapped(): return lax.ppermute(block, axis, [(i, i ^ distance) for i in range(n)])]
    gather x2 -> x0, local copies, waits for them, and re-layouts: 11.9 us -> none  [select_rows(): taken = jnp.take(row_block, source_rows, axis=0)]
    convert_element_type x0 -> x3, other arithmetic: none -> 7.98 us  [the longest x2 4.88 us: shards(): out = jnp.where(near, b, a).astype(BF)]
  transfers between devices with their start and end apart: 3 -> 17, of which waited for: 3 -> 8; matrix products, arithmetic and copies ran while one was open for 12% -> 2% of each run, Pallas kernels for 0% -> 22%
where the time goes in v1:
time: 206 us
  waiting for transfers between devices  120 us (58%)
  Pallas kernels  47.3 us (23%)
  starting transfers between devices  20.4 us (10%)
  other arithmetic  9.3 us (5%)
  local copies, waits for them, and re-layouts  8.24 us (4%)
    ppermute x17, waiting for transfers between devices, swapped(): return lax.ppermute(block, axis, [(i, i ^ distance) for i in range(n)])  120 us
    ppermute x17, starting transfers between devices, swapped(): return lax.ppermute(block, axis, [(i, i ^ distance) for i in range(n)])  20.4 us
    pallas_call x4, Pallas kernels, weight_piece(): call(weight_kernel, (ff // block,), 1, [whole((SEND, width)), whole((KEEP...  15.4 us
    pallas_call x2, Pallas kernels, grads(): call(kernel, (4,), 1, [whole((count, width))] * 4 + [pl.BlockSpec((featur...  14.1 us
    pallas_call x1, Pallas kernels, shards(): call(gelu_kernel, (ff // cols,), 3, [pl.BlockSpec((home, cols), lambda i,...  12.5 us
    unnamed x44, local copies, waits for them, and re-layouts  7.54 us
    convert_element_type x2, other arithmetic, shards(): out = jnp.where(near, b, a).astype(BF)  4.88 us
  transfers between devices with their start and end apart: 17, of which 8 were waited for; matrix products, arithmetic and copies ran while one was open for 2% of the time, Pallas kernels for 22%

profile of v1, /device:TPU:0, one launch (start us, length us, event | category | flops | bytes accessed | tf_op | source)
XLA Modules:
  0.0 205.7 jit_solution(295755225882066670)
XLA Ops:
  4.1 2.4 %shard_map.77 = (bf16[528,384]{1,0:T(8,128)(2,1)S(1)}, bf16[528,384]{1,0:T(8,128)(2,1)S(1)}) custom-call(s32[2]{0:T(128)S(1)} %pad_add_fusion.place, s32[8,4]{1,0:T(8,128)S(1)} %copy.12.lens, s32[8,4]{1,0:T(8,128)S(1)} %copy.13.moves, bf16[1032,384]{1,0:T(8,128)(2,1)S(1)} %copy-done.19, f32[1,1536]{1,0:T(1,128)S(1)} %reshape.7.scale), custom_call_target="tpu_custom_call" | custom-call | flops 836960256 | bytes 1603584 | tf_op jit(solution)/shard_map/pallas_call | solution.py:176
  6.5 3.0 %collective-permute-start.1 = (bf16[528,384]{1,0:T(8,128)(2,1)S(1)}, bf16[528,384]{1,0:T(8,128)(2,1)S(1)}, u32[]{:S(2)}, u32[]{:S(2)}) collective-permute-start(bf16[528,384]{1,0:T(8,128)(2,1)S(1)} %get-tuple-element.18.p0.kept), channel_id=1, source_target_pairs={{0,2},{1,3},{2,0},{3,1},{4,6},{5,7},{6,4},{7,5},{8,10},{9,11},{10,... | collective-permute-start | bytes 1216520 | tf_op jit(solution)/shard_map/ppermute | solution.py:162
  12.0 12.5 %shard_map.78 = (bf16[1056,1536]{1,0:T(8,128)(2,1)}, f32[1056,1536]{1,0:T(8,128)}) custom-call(s32[2]{0:T(128)S(1)} %pad_add_fusion.place, s32[8,4]{1,0:T(8,128)S(1)} %copy.12.lens, s32[8,4]{1,0:T(8,128)S(1)} %copy.13.moves, bf16[1032,1536]{1,0:T(8,128)(2,1)S(1)} %copy-done.18), custom_call_target="tpu_custom_call" | custom-call | flops 3347841024 | bytes 12902400 | tf_op jit(solution)/shard_map/pallas_call | solution.py:191
  26.4 3.8 %shard_map.82 = (bf16[192,1536]{1,0:T(8,128)(2,1)}, f32[192,1536]{1,0:T(8,128)S(1)}) custom-call(s32[2]{0:T(128)S(1)} %pad_add_fusion.place, bf16[528,384]{1,0:T(8,128)(2,1)S(1)} %get-tuple-element.20.p0.sent, bf16[528,384]{1,0:T(8,128)(2,1)S(1)} %get-tuple-element.18.p0.kept, bf16[1056,1536]{1,0:T(8,128)(2,1)S(1)} %copy-done.20), custom_call_target="tpu_custom_call" | custom-call | flops 1245708288 | bytes 5013504 | tf_op jit(solution)/shard_map/pallas_call | solution.py:225
  31.9 3.9 %shard_map.83 = (bf16[192,1536]{1,0:T(8,128)(2,1)}, f32[192,1536]{1,0:T(8,128)S(1)}) custom-call(s32[2]{0:T(128)S(1)} %pad_add_fusion.place, bf16[528,384]{1,0:T(8,128)(2,1)S(1)} %collective-permute-done.3.p1.sent, bf16[528,384]{1,0:T(8,128)(2,1)S(1)} %collective-permute-done.p1.kept, bf16[1056,1536]{1,0:T(8,128)(2,1)S(1)} %copy-done.20), custom_call_target="tpu_custom_call" | custom-call | flops 1245708288 | bytes 5013504 | tf_op jit(solution)/shard_map/pallas_call | solution.py:225
  36.7 3.9 %shard_map.84 = (bf16[192,1536]{1,0:T(8,128)(2,1)}, f32[192,1536]{1,0:T(8,128)S(1)}) custom-call(s32[2]{0:T(128)S(1)} %pad_add_fusion.place, bf16[528,384]{1,0:T(8,128)(2,1)S(1)} %collective-permute-done.4.p2.sent, bf16[528,384]{1,0:T(8,128)(2,1)S(1)} %collective-permute-done.1.p2.kept, bf16[1056,1536]{1,0:T(8,128)(2,1)S(1)} %copy-done.20), custom_call_target="tpu_custom_call" | custom-call | flops 1245708288 | bytes 5013504 | tf_op jit(solution)/shard_map/pallas_call | solution.py:225
  42.3 3.8 %shard_map.85 = (bf16[192,1536]{1,0:T(8,128)(2,1)}, f32[192,1536]{1,0:T(8,128)S(1)}) custom-call(s32[2]{0:T(128)S(1)} %pad_add_fusion.place, bf16[528,384]{1,0:T(8,128)(2,1)S(1)} %collective-permute-done.5.p3.sent, bf16[528,384]{1,0:T(8,128)(2,1)S(1)} %collective-permute-done.2.p3.kept, bf16[1056,1536]{1,0:T(8,128)(2,1)S(1)} %copy-done.20), custom_call_target="tpu_custom_call" | custom-call | flops 1245708288 | bytes 5013504 | tf_op jit(solution)/shard_map/pallas_call | solution.py:225
  47.4 11.9 %collective-permute-done.11 = bf16[192,1536]{1,0:T(8,128)(2,1)} collective-permute-done((bf16[192,1536]{1,0:T(8,128)(2,1)}, bf16[192,1536]{1,0:T(8,128)(2,1)}, u32[]{:S(2)}, u32[]{:S(2)}) %collective-permute-start.11) | collective-permute-done | bytes 589856 | tf_op jit(solution)/shard_map/ppermute | solution.py:162
  59.3 2.5 %select_convert_fusion.2 = bf16[192,1536]{1,0:T(8,128)(2,1)} fusion(f32[192,1536]{1,0:T(8,128)S(1)} %get-tuple-element.26, bf16[192,1536]{1,0:T(8,128)(2,1)} %collective-permute-done.10, f32[192,1536]{1,0:T(8,128)S(1)} %get-tuple-element.28, bf16[192,1536]{1,0:T(8,128)(2,1)} %collective-permute-done.11, pred[]{:T(512)S(6)} %eq.10), kind=kLoop, calls=%fused_computation.7 | loop fusion | flops 1769472 | bytes 4128769 | tf_op jit(solution)/shard_map/convert_element_type | solution.py:244
  63.6 8.4 %collective-permute-done.13 = bf16[192,1536]{1,0:T(8,128)(2,1)} collective-permute-done((bf16[192,1536]{1,0:T(8,128)(2,1)}, bf16[192,1536]{1,0:T(8,128)(2,1)}, u32[]{:S(2)}, u32[]{:S(2)}) %collective-permute-start.13) | collective-permute-done | bytes 589856 | tf_op jit(solution)/shard_map/ppermute | solution.py:162
  72.0 12.0 %collective-permute-done.14 = bf16[192,1536]{1,0:T(8,128)(2,1)} collective-permute-done((bf16[192,1536]{1,0:T(8,128)(2,1)}, bf16[192,1536]{1,0:T(8,128)(2,1)}, u32[]{:S(2)}, u32[]{:S(2)}) %collective-permute-start.14) | collective-permute-done | bytes 589856 | tf_op jit(solution)/shard_map/ppermute | solution.py:162
  83.9 2.4 %select_convert_fusion.1 = bf16[192,1536]{1,0:T(8,128)(2,1)} fusion(f32[192,1536]{1,0:T(8,128)S(1)} %get-tuple-element.30, bf16[192,1536]{1,0:T(8,128)(2,1)} %collective-permute-done.13, f32[192,1536]{1,0:T(8,128)S(1)} %copy-done.1, bf16[192,1536]{1,0:T(8,128)(2,1)} %collective-permute-done.14, pred[]{:T(512)S(6)} %eq.10), kind=kLoop, calls=%fused_computation.3 | loop fusion | flops 1769472 | bytes 4128769 | tf_op jit(solution)/shard_map/convert_element_type | solution.py:244
  88.2 13.3 %collective-permute-done.15 = bf16[192,1536]{1,0:T(8,128)(2,1)} collective-permute-done((bf16[192,1536]{1,0:T(8,128)(2,1)}, bf16[192,1536]{1,0:T(8,128)(2,1)}, u32[]{:S(2)}, u32[]{:S(2)}) %collective-permute-start.15) | collective-permute-done | bytes 589856 | tf_op jit(solution)/shard_map/ppermute | solution.py:162
  101.4 3.1 %select_convert_fusion = (bf16[192,1536]{1,0:T(8,128)(2,1)S(1)}, f32[192,1536]{1,0:T(8,128)S(1)}, f32[192,1536]{1,0:T(8,128)S(1)}) fusion(pred[]{:T(512)S(6)} %eq.9, bf16[192,1536]{1,0:T(8,128)(2,1)} %collective-permute-done.12, f32[192,1536]{1,0:T(8,128)S(1)} %get-tuple-element.28, bf16[192,1536]{1,0:T(8,128)(2,1)} %collective-permute-done.11, ...), kind=kLoop, calls=%fused_computation.1 | loop fusion | flops 4423680 | bytes 11206658 | tf_op jit(solution)/shard_map/convert_element_type | solution.py:248
  104.6 2.8 %collective-permute-start.16 = (bf16[192,1536]{1,0:T(8,128)(2,1)S(1)}, bf16[192,1536]{1,0:T(8,128)(2,1)S(1)}, u32[]{:S(2)}, u32[]{:S(2)}) collective-permute-start(bf16[192,1536]{1,0:T(8,128)(2,1)S(1)} %get-tuple-element.34), channel_id=1, source_target_pairs={{0,16},{4,20},{8,24},{12,28},{16,0},{20,4},{24,8},{28,12},{1,17},{... | collective-permute-start | bytes 1769480 | tf_op jit(solution)/shard_map/ppermute | solution.py:162
  107.4 7.1 %shard_map.80 = (bf16[528,384]{1,0:T(8,128)(2,1)S(1)}, bf16[528,384]{1,0:T(8,128)(2,1)S(1)}, bf16[528,384]{1,0:T(8,128)(2,1)S(1)}, bf16[528,384]{1,0:T(8,128)(2,1)S(1)}) custom-call(s32[2]{0:T(128)S(1)} %pad_add_fusion.place, bf16[528,384]{1,0:T(8,128)(2,1)S(1)} %copy-done.3, bf16[528,384]{1,0:T(8,128)(2,1)S(1)} %copy-done.7, ...), custom_call_target="tpu_custom_call" | custom-call | flops 2491416576 | bytes 9584640 | tf_op jit(solution)/shard_map/pallas_call | solution.py:211
  114.7 2.8 %collective-permute-start.7 = (bf16[528,384]{1,0:T(8,128)(2,1)S(1)}, bf16[528,384]{1,0:T(8,128)(2,1)S(1)}, u32[]{:S(2)}, u32[]{:S(2)}) collective-permute-start(bf16[528,384]{1,0:T(8,128)(2,1)S(1)} %get-tuple-element.22), channel_id=1, source_target_pairs={{0,16},{4,20},{8,24},{12,28},{16,0},{20,4},{24,8},{28,12},{1,17},{... | collective-permute-start | bytes 1216520 | tf_op jit(solution)/shard_map/ppermute | solution.py:162
  117.7 2.8 %collective-permute-start.9 = (bf16[528,384]{1,0:T(8,128)(2,1)S(1)}, bf16[528,384]{1,0:T(8,128)(2,1)S(1)}, u32[]{:S(2)}, u32[]{:S(2)}) collective-permute-start(bf16[528,384]{1,0:T(8,128)(2,1)S(1)} %get-tuple-element.24), channel_id=1, source_target_pairs={{0,16},{4,20},{8,24},{12,28},{16,0},{20,4},{24,8},{28,12},{1,17},{... | collective-permute-start | bytes 1216520 | tf_op jit(solution)/shard_map/ppermute | solution.py:162
  120.4 7.0 %shard_map.79.kept = bf16[528,1536]{1,0:T(8,128)(2,1)S(1)} custom-call(s32[2]{0:T(128)S(1)} %pad_add_fusion.place, bf16[528,384]{1,0:T(8,128)(2,1)S(1)} %copy-done.11, bf16[528,384]{1,0:T(8,128)(2,1)S(1)} %copy-done.15, bf16[528,384]{1,0:T(8,128)(2,1)S(1)} %copy-done.13, bf16[528,384]{1,0:T(8,128)(2,1)S(1)} %copy-done.17, bf16[1536,1536]{1,0:T(8,128)(2,1)} %weight.3, ...), custom_call_target="tpu_custom_call" | custom-call | flops 2491416576 | bytes 9584640 | tf_op jit(solution)/shard_map/pallas_call | solution.py:211
  127.4 49.3 %collective-permute-done.6.rest_0_ = bf16[528,384]{1,0:T(8,128)(2,1)S(1)} collective-permute-done((bf16[528,384]{1,0:T(8,128)(2,1)S(1)}, bf16[528,384]{1,0:T(8,128)(2,1)S(1)}, u32[]{:S(2)}, u32[]{:S(2)}) %collective-permute-start.6) | collective-permute-done | bytes 405536 | tf_op jit(solution)/shard_map/ppermute | solution.py:162
  176.7 8.7 %collective-permute-done.7.rest_1_ = bf16[528,384]{1,0:T(8,128)(2,1)S(1)} collective-permute-done((bf16[528,384]{1,0:T(8,128)(2,1)S(1)}, bf16[528,384]{1,0:T(8,128)(2,1)S(1)}, u32[]{:S(2)}, u32[]{:S(2)}) %collective-permute-start.7) | collective-permute-done | bytes 405536 | tf_op jit(solution)/shard_map/ppermute | solution.py:162
  185.4 8.7 %collective-permute-done.8.rest_2_ = bf16[528,384]{1,0:T(8,128)(2,1)S(1)} collective-permute-done((bf16[528,384]{1,0:T(8,128)(2,1)S(1)}, bf16[528,384]{1,0:T(8,128)(2,1)S(1)}, u32[]{:S(2)}, u32[]{:S(2)}) %collective-permute-start.8) | collective-permute-done | bytes 405536 | tf_op jit(solution)/shard_map/ppermute | solution.py:162
  194.1 7.5 %collective-permute-done.9.rest_3_ = bf16[528,384]{1,0:T(8,128)(2,1)S(1)} collective-permute-done((bf16[528,384]{1,0:T(8,128)(2,1)S(1)}, bf16[528,384]{1,0:T(8,128)(2,1)S(1)}, u32[]{:S(2)}, u32[]{:S(2)}) %collective-permute-start.9) | collective-permute-done | bytes 405536 | tf_op jit(solution)/shard_map/ppermute | solution.py:162
  201.6 2.9 %shard_map.81 = bf16[720,1536]{1,0:T(8,128)(2,1)} custom-call(s32[2]{0:T(128)S(1)} %pad_add_fusion.place, s32[8,4]{1,0:T(8,128)S(1)} %copy.12.lens, s32[8,4]{1,0:T(8,128)S(1)} %copy.13.moves, bf16[528,1536]{1,0:T(8,128)(2,1)S(1)} %shard_map.79.kept, bf16[528,384]{1,0:T(8,128)(2,1)S(1)} %collective-permute-done.6.rest_0_, ...), custom_call_target="tpu_custom_call" | custom-call | bytes 5455872 | tf_op jit(solution)/shard_map/pallas_call | solution.py:254
  (69 shorter events, 18.7 us)
Async XLA Ops:
  6.5 17.9 %copy-start.2 = (bf16[528,384]{1,0:T(8,128)(2,1)}, bf16[528,384]{1,0:T(8,128)(2,1)S(1)}, u32[]{:S(2)}) copy-start(bf16[528,384]{1,0:T(8,128)(2,1)S(1)} %get-tuple-element.20.p0.sent) | copy-start | bytes 1216516
  6.5 17.9 %copy-start.10 = (bf16[528,384]{1,0:T(8,128)(2,1)}, bf16[528,384]{1,0:T(8,128)(2,1)S(1)}, u32[]{:S(2)}) copy-start(bf16[528,384]{1,0:T(8,128)(2,1)S(1)} %get-tuple-element.18.p0.kept) | copy-start | bytes 1216516
  6.5 29.6 %collective-permute-start.1 = (bf16[528,384]{1,0:T(8,128)(2,1)S(1)}, bf16[528,384]{1,0:T(8,128)(2,1)S(1)}, u32[]{:S(2)}, u32[]{:S(2)}) collective-permute-start(bf16[528,384]{1,0:T(8,128)(2,1)S(1)} %get-tuple-element.18.p0.kept), channel_id=1, source_target_pairs={{0,2},{1,3},{2,0},{3,1},{4,6},{5,7},{6,4},{7,5},{8,10},{9,11},{10,... | collective-permute-start | bytes 1216520 | tf_op jit(solution)/shard_map/ppermute | solution.py:162
  9.6 22.4 %collective-permute-start = (bf16[528,384]{1,0:T(8,128)(2,1)S(1)}, bf16[528,384]{1,0:T(8,128)(2,1)S(1)}, u32[]{:S(2)}, u32[]{:S(2)}) collective-permute-start(bf16[528,384]{1,0:T(8,128)(2,1)S(1)} %get-tuple-element.18.p0.kept), channel_id=1, source_target_pairs={{0,1},{1,0},{2,3},{3,2},{4,5},{5,4},{6,7},{7,6},{8,9},{9,8},{10,11... | collective-permute-start | bytes 1216520 | tf_op jit(solution)/shard_map/ppermute | solution.py:162
  9.6 26.6 %collective-permute-start.4 = (bf16[528,384]{1,0:T(8,128)(2,1)S(1)}, bf16[528,384]{1,0:T(8,128)(2,1)S(1)}, u32[]{:S(2)}, u32[]{:S(2)}) collective-permute-start(bf16[528,384]{1,0:T(8,128)(2,1)S(1)} %get-tuple-element.20.p0.sent), channel_id=1, source_target_pairs={{0,2},{1,3},{2,0},{3,1},{4,6},{5,7},{6,4},{7,5},{8,10},{9,11},{10,... | collective-permute-start | bytes 1216520 | tf_op jit(solution)/shard_map/ppermute | solution.py:162
  9.7 22.2 %collective-permute-start.3 = (bf16[528,384]{1,0:T(8,128)(2,1)S(1)}, bf16[528,384]{1,0:T(8,128)(2,1)S(1)}, u32[]{:S(2)}, u32[]{:S(2)}) collective-permute-start(bf16[528,384]{1,0:T(8,128)(2,1)S(1)} %get-tuple-element.20.p0.sent), channel_id=1, source_target_pairs={{0,1},{1,0},{2,3},{3,2},{4,5},{5,4},{6,7},{7,6},{8,9},{9,8},{10,11... | collective-permute-start | bytes 1216520 | tf_op jit(solution)/shard_map/ppermute | solution.py:162
  30.2 17.2 %collective-permute-start.10 = (bf16[192,1536]{1,0:T(8,128)(2,1)}, bf16[192,1536]{1,0:T(8,128)(2,1)}, u32[]{:S(2)}, u32[]{:S(2)}) collective-permute-start(bf16[192,1536]{1,0:T(8,128)(2,1)} %get-tuple-element.27), channel_id=1, source_target_pairs={{0,4},{4,0},{8,12},{12,8},{16,20},{20,16},{24,28},{28,24},{1,5},{5... | collective-permute-start | bytes 1769480 | tf_op jit(solution)/shard_map/ppermute | solution.py:162
  35.8 23.5 %collective-permute-start.11 = (bf16[192,1536]{1,0:T(8,128)(2,1)}, bf16[192,1536]{1,0:T(8,128)(2,1)}, u32[]{:S(2)}, u32[]{:S(2)}) collective-permute-start(bf16[192,1536]{1,0:T(8,128)(2,1)} %get-tuple-element.29), channel_id=1, source_target_pairs={{0,4},{4,0},{8,12},{12,8},{16,20},{20,16},{24,28},{28,24},{1,5},{5... | collective-permute-start | bytes 1769480 | tf_op jit(solution)/shard_map/ppermute | solution.py:162
  36.1 6.1 %collective-permute-start.2 = (bf16[528,384]{1,0:T(8,128)(2,1)S(1)}, bf16[528,384]{1,0:T(8,128)(2,1)S(1)}, u32[]{:S(2)}, u32[]{:S(2)}) collective-permute-start(bf16[528,384]{1,0:T(8,128)(2,1)S(1)} %collective-permute-done.1.p2.kept), channel_id=1, source_target_pairs={{0,1},{1,0},{2,3},{3,2},{4,5},{5,4},{6,7},{7,6},{8,9},{9,8},{10,11... | collective-permute-start | bytes 1216520 | tf_op jit(solution)/shard_map/ppermute | solution.py:162
  36.2 6.1 %collective-permute-start.5 = (bf16[528,384]{1,0:T(8,128)(2,1)S(1)}, bf16[528,384]{1,0:T(8,128)(2,1)S(1)}, u32[]{:S(2)}, u32[]{:S(2)}) collective-permute-start(bf16[528,384]{1,0:T(8,128)(2,1)S(1)} %collective-permute-done.4.p2.sent), channel_id=1, source_target_pairs={{0,1},{1,0},{2,3},{3,2},{4,5},{5,4},{6,7},{7,6},{8,9},{9,8},{10,11... | collective-permute-start | bytes 1216520 | tf_op jit(solution)/shard_map/ppermute | solution.py:162
  40.5 31.4 %collective-permute-start.13 = (bf16[192,1536]{1,0:T(8,128)(2,1)}, bf16[192,1536]{1,0:T(8,128)(2,1)}, u32[]{:S(2)}, u32[]{:S(2)}) collective-permute-start(bf16[192,1536]{1,0:T(8,128)(2,1)} %get-tuple-element.31), channel_id=1, source_target_pairs={{0,4},{4,0},{8,12},{12,8},{16,20},{20,16},{24,28},{28,24},{1,5},{5... | collective-permute-start | bytes 1769480 | tf_op jit(solution)/shard_map/ppermute | solution.py:162
  47.1 36.8 %collective-permute-start.14 = (bf16[192,1536]{1,0:T(8,128)(2,1)}, bf16[192,1536]{1,0:T(8,128)(2,1)}, u32[]{:S(2)}, u32[]{:S(2)}) collective-permute-start(bf16[192,1536]{1,0:T(8,128)(2,1)} %get-tuple-element.33), channel_id=1, source_target_pairs={{0,4},{4,0},{8,12},{12,8},{16,20},{20,16},{24,28},{28,24},{1,5},{5... | collective-permute-start | bytes 1769480 | tf_op jit(solution)/shard_map/ppermute | solution.py:162
  59.3 24.6 %copy-start.1 = (f32[192,1536]{1,0:T(8,128)S(1)}, f32[192,1536]{1,0:T(8,128)}, u32[]{:S(2)}) copy-start(f32[192,1536]{1,0:T(8,128)} %copy-done) | copy-start | bytes 3538948
  61.8 26.4 %collective-permute-start.12 = (bf16[192,1536]{1,0:T(8,128)(2,1)}, bf16[192,1536]{1,0:T(8,128)(2,1)}, u32[]{:S(2)}, u32[]{:S(2)}) collective-permute-start(bf16[192,1536]{1,0:T(8,128)(2,1)} %select_convert_fusion.2), channel_id=1, source_target_pairs={{0,8},{4,12},{8,0},{12,4},{16,24},{20,28},{24,16},{28,20},{1,9},{5... | collective-permute-start | bytes 1769480 | tf_op jit(solution)/shard_map/ppermute | solution.py:162
  86.3 15.1 %collective-permute-start.15 = (bf16[192,1536]{1,0:T(8,128)(2,1)}, bf16[192,1536]{1,0:T(8,128)(2,1)}, u32[]{:S(2)}, u32[]{:S(2)}) collective-permute-start(bf16[192,1536]{1,0:T(8,128)(2,1)} %select_convert_fusion.1), channel_id=1, source_target_pairs={{0,8},{4,12},{8,0},{12,4},{16,24},{20,28},{24,16},{28,20},{1,9},{5... | collective-permute-start | bytes 1769480 | tf_op jit(solution)/shard_map/ppermute | solution.py:162
  88.2 19.2 %copy-start.3 = (bf16[528,384]{1,0:T(8,128)(2,1)S(1)}, bf16[528,384]{1,0:T(8,128)(2,1)}, u32[]{:S(2)}) copy-start(bf16[528,384]{1,0:T(8,128)(2,1)} %copy-done.2) | copy-start | bytes 1216516
  88.2 19.2 %copy-start.5 = (bf16[528,384]{1,0:T(8,128)(2,1)S(1)}, bf16[528,384]{1,0:T(8,128)(2,1)}, u32[]{:S(2)}) copy-start(bf16[528,384]{1,0:T(8,128)(2,1)} %copy-done.4) | copy-start | bytes 1216516
  88.2 19.2 %copy-start.7 = (bf16[528,384]{1,0:T(8,128)(2,1)S(1)}, bf16[528,384]{1,0:T(8,128)(2,1)}, u32[]{:S(2)}) copy-start(bf16[528,384]{1,0:T(8,128)(2,1)} %copy-done.6) | copy-start | bytes 1216516
  88.2 19.2 %copy-start.9 = (bf16[528,384]{1,0:T(8,128)(2,1)S(1)}, bf16[528,384]{1,0:T(8,128)(2,1)}, u32[]{:S(2)}) copy-start(bf16[528,384]{1,0:T(8,128)(2,1)} %copy-done.8) | copy-start | bytes 1216516
  104.6 99.9 %collective-permute-start.16 = (bf16[192,1536]{1,0:T(8,128)(2,1)S(1)}, bf16[192,1536]{1,0:T(8,128)(2,1)S(1)}, u32[]{:S(2)}, u32[]{:S(2)}) collective-permute-start(bf16[192,1536]{1,0:T(8,128)(2,1)S(1)} %get-tuple-element.34), channel_id=1, source_target_pairs={{0,16},{4,20},{8,24},{12,28},{16,0},{20,4},{24,8},{28,12},{1,17},{... | collective-permute-start | bytes 1769480 | tf_op jit(solution)/shard_map/ppermute | solution.py:162
  114.5 62.2 %collective-permute-start.6 = (bf16[528,384]{1,0:T(8,128)(2,1)S(1)}, bf16[528,384]{1,0:T(8,128)(2,1)S(1)}, u32[]{:S(2)}, u32[]{:S(2)}) collective-permute-start(bf16[528,384]{1,0:T(8,128)(2,1)S(1)} %get-tuple-element.21), channel_id=1, source_target_pairs={{0,16},{4,20},{8,24},{12,28},{16,0},{20,4},{24,8},{28,12},{1,17},{... | collective-permute-start | bytes 1216520 | tf_op jit(solution)/shard_map/ppermute | solution.py:162
  114.7 70.7 %collective-permute-start.7 = (bf16[528,384]{1,0:T(8,128)(2,1)S(1)}, bf16[528,384]{1,0:T(8,128)(2,1)S(1)}, u32[]{:S(2)}, u32[]{:S(2)}) collective-permute-start(bf16[528,384]{1,0:T(8,128)(2,1)S(1)} %get-tuple-element.22), channel_id=1, source_target_pairs={{0,16},{4,20},{8,24},{12,28},{16,0},{20,4},{24,8},{28,12},{1,17},{... | collective-permute-start | bytes 1216520 | tf_op jit(solution)/shard_map/ppermute | solution.py:162
  117.5 76.6 %collective-permute-start.8 = (bf16[528,384]{1,0:T(8,128)(2,1)S(1)}, bf16[528,384]{1,0:T(8,128)(2,1)S(1)}, u32[]{:S(2)}, u32[]{:S(2)}) collective-permute-start(bf16[528,384]{1,0:T(8,128)(2,1)S(1)} %get-tuple-element.23), channel_id=1, source_target_pairs={{0,16},{4,20},{8,24},{12,28},{16,0},{20,4},{24,8},{28,12},{1,17},{... | collective-permute-start | bytes 1216520 | tf_op jit(solution)/shard_map/ppermute | solution.py:162
  117.7 83.9 %collective-permute-start.9 = (bf16[528,384]{1,0:T(8,128)(2,1)S(1)}, bf16[528,384]{1,0:T(8,128)(2,1)S(1)}, u32[]{:S(2)}, u32[]{:S(2)}) collective-permute-start(bf16[528,384]{1,0:T(8,128)(2,1)S(1)} %get-tuple-element.24), channel_id=1, source_target_pairs={{0,16},{4,20},{8,24},{12,28},{16,0},{20,4},{24,8},{28,12},{1,17},{... | collective-permute-start | bytes 1216520 | tf_op jit(solution)/shard_map/ppermute | solution.py:162
  (14 other events, 82.2 us)

commit v2 on v1

v2 whole, which is shorter than its diff:
```python
import functools
import math

import jax
import jax.numpy as jnp
from jax import lax
from jax.experimental import pallas as pl
from jax.experimental.pallas import tpu as pltpu
from jax.sharding import PartitionSpec as P

SEND = 528
KEEP = 528
TILE = 16
EARLY = 128
LATE = SEND - EARLY
SLOTS = 4
BAL = 720
BF = jnp.bfloat16
F32 = jnp.float32

inv_root_two = 0.7071067811865476
inv_root_tau = 0.3989422804014327


def call(kernel, grid, scalars, in_specs, out_specs, out_shape, scratch, flops, nbytes, trans=0):
    return pl.pallas_call(
        kernel,
        grid_spec=pltpu.PrefetchScalarGridSpec(
            num_scalar_prefetch=scalars,
            grid=grid,
            in_specs=in_specs,
            out_specs=out_specs,
            scratch_shapes=scratch,
        ),
        out_shape=out_shape,
        cost_estimate=pl.CostEstimate(flops=1, bytes_accessed=1, transcendentals=0),
        compiler_params=pltpu.CompilerParams(vmem_limit_bytes=48 * 1024 * 1024),
    )


def whole(shape):
    return pl.BlockSpec(shape, lambda *_: (0,) * len(shape))


def lengths_of(meta, d):
    return [meta[2 + d * SLOTS + j] for j in range(SLOTS)]


def moves_of(meta, n, d):
    return [meta[2 + (n + d) * SLOTS + j] for j in range(SLOTS)]


def kept_total(meta, n, d):
    return sum(a * (1 - b) for a, b in zip(lengths_of(meta, d), moves_of(meta, n, d)))


def picks(meta, n, moved, first, rows, home):
    d = meta[0]
    at = lax.broadcasted_iota(jnp.int32, (rows, 1), 0) - first
    source = jnp.full((rows, 1), -1, jnp.int32)
    begin = jnp.int32(0)
    start = jnp.int32(0)
    for length, move in zip(lengths_of(meta, d), moves_of(meta, n, d)):
        size = length * (move if moved else 1 - move)
        inside = (at >= begin) & (at < begin + size)
        source = jnp.where(inside, at + (start - begin), source)
        begin = begin + size
        start = start + length
    columns = lax.broadcasted_iota(jnp.int32, (rows, home), 1)
    return jnp.where(columns == source, 1.0, 0.0).astype(BF)


def sent_first(meta, n):
    partner = lax.rem(meta[0] + n // 2, n)
    return lax.rem(kept_total(meta, n, partner), TILE)


def early_picks(meta, n, home):
    return picks(meta, n, True, sent_first(meta, n), EARLY, home)


def late_picks(meta, n, home):
    return picks(meta, n, True, sent_first(meta, n) - EARLY, LATE, home)


def kept_picks(meta, n, home):
    return picks(meta, n, False, 0, KEEP, home)


def scaled_rows(pick, cot, scale):
    rows = jnp.dot(pick, cot[...], preferred_element_type=F32)
    return (rows * scale[...]).astype(BF)


def first_kernel(n, meta, cot, scale, pre, late_out, early_out, pre_a, pre_b):
    home = cot.shape[0]
    late_out[...] = scaled_rows(late_picks(meta, n, home), cot, scale)
    early = early_picks(meta, n, home)
    early_out[...] = scaled_rows(early, cot, scale)
    rows = jnp.dot(early, pre[...], preferred_element_type=F32).astype(BF)
    cut = pre_a.shape[1]
    pre_a[...] = rows[:, :cut]
    pre_b[...] = rows[:, cut:]


def rest_kernel(n, meta, cot, scale, rest_out):
    home = cot.shape[0]
    rest_out[0:EARLY, :] = scaled_rows(early_picks(meta, n, home), cot, scale)
    rest_out[EARLY:, :] = scaled_rows(kept_picks(meta, n, home), cot, scale)


def gelu_kernel(n, meta, pre, act_out, der_out, pick, rows_f32):
    home = pre.shape[0]

    @pl.when(pl.program_id(0) == 0)
    def _():
        pick[0:LATE, :] = late_picks(meta, n, home)
        pick[LATE:SEND, :] = early_picks(meta, n, home)
        pick[SEND:, :] = kept_picks(meta, n, home)

    rows_f32[...] = jnp.dot(pick[...], pre[...], preferred_element_type=F32)
    step = 3 * TILE

    def body(i, _):
        at = pl.ds(pl.multiple_of(i * step, step), step)
        x = rows_f32[at, :]
        cumulative = 0.5 * (1.0 + lax.erf(x * inv_root_two))
        act_out[at, :] = (x * cumulative).astype(BF)
        der_out[at, :] = cumulative + x * jnp.exp(-0.5 * x * x) * inv_root_tau
        return 0

    lax.fori_loop(0, (SEND + KEEP) // step, body, 0)


def assemble(meta, pieces, lhs):
    width = pieces[0].shape[1]
    for j, piece in enumerate(pieces):
        at = pl.ds(pl.multiple_of((meta[1] ^ j) * width, 128), width)
        lhs[:, at] = piece[...]


def late_kernel(meta, p0, p1, p2, p3, weight, der, *rest):
    outs, lhs = rest[:-1], rest[-1]
    step = pl.program_id(0)

    @pl.when(step == 0)
    def _():
        assemble(meta, (p0, p1, p2, p3), lhs)

    value = (jnp.dot(lhs[...], weight[...], preferred_element_type=F32) * der[...]).astype(BF)
    for c, out in enumerate(outs):

        @pl.when(step == c)
        def _():
            out[...] = value


def kept_kernel(meta, r0, r1, r2, r3, weight, der, out, lhs):
    @pl.when(pl.program_id(0) == 0)
    def _():
        assemble(meta, [r.at[pl.ds(EARLY, KEEP), :] for r in (r0, r1, r2, r3)], lhs)

    out[...] = (jnp.dot(lhs[...], weight[...], preferred_element_type=F32) * der[...]).astype(BF)


def early_kernel(meta, p0, p1, p2, p3, weight, pre_a, pre_b, out, lhs, acc, pre):
    step = pl.program_id(0)

    @pl.when(step == 0)
    def _():
        assemble(meta, (p0, p1, p2, p3), lhs)
        pre[...] = pre_a[...]

    @pl.when(step > 0)
    def _():
        pre[...] = pre_b[...]

    acc[...] = jnp.dot(lhs[...], weight[...], preferred_element_type=F32)
    for r in range(0, EARLY, TILE):
        at = slice(r, r + TILE)
        x = pre[at, :].astype(F32)
        cumulative = 0.5 * (1.0 + lax.erf(x * inv_root_two))
        derivative = cumulative + x * jnp.exp(-0.5 * x * x) * inv_root_tau
        out[at, :] = (acc[at, :] * derivative).astype(BF)


def transposed(meta, late, rest):
    both = jnp.concatenate([late[...], rest[...]], axis=0).T
    half = both.shape[0] // 2
    mine = meta[0] % 2 == 0
    lo, hi = both[:half], both[half:]
    return jnp.where(mine, hi, lo), jnp.where(mine, lo, hi)


def weight_kernel(meta, late, rest, act, send_out, keep_out, lhs):
    half = lhs.shape[0] // 2

    @pl.when(pl.program_id(0) == 0)
    def _():
        lhs[0:half, :], lhs[half:, :] = transposed(meta, late, rest)

    value = jnp.dot(lhs[...], act[...], preferred_element_type=F32)
    send_out[...] = value[:half].astype(BF)
    keep_out[...] = value[half:]


def weight_pair_kernel(meta, late_a, rest_a, late_b, rest_b, act, *rest):
    outs, lhs = rest[:-1], rest[-1]
    half = lhs.shape[0] // 4
    keeps_a = (meta[0] // 2 + meta[1]) % 2 == 0

    @pl.when(pl.program_id(0) == 0)
    def _():
        a = transposed(meta, late_a, rest_a)
        b = transposed(meta, late_b, rest_b)
        for i in range(2):
            lhs[i * half : (i + 1) * half, :] = jnp.where(keeps_a, b[i], a[i])
            lhs[(i + 2) * half : (i + 3) * half, :] = jnp.where(keeps_a, a[i], b[i])

    value = jnp.dot(lhs[...], act[...], preferred_element_type=F32)
    for i, out in enumerate(outs):
        out[...] = value[i * half : (i + 1) * half].astype(out.dtype)


def place_kernel(n, meta, kept, early, *rest):
    late, out = rest[:-1], rest[-1]
    count = kept_total(meta, n, meta[0])
    first = jnp.minimum(count - lax.rem(count, TILE), BAL - SEND)
    first = pl.multiple_of(first, TILE)
    out[0:KEEP, :] = kept[...]
    out[KEEP:, :] = jnp.zeros((out.shape[0] - KEEP, out.shape[1]), BF)
    step = pl.program_id(0)

    def put(block, at):
        rows = lax.broadcasted_iota(jnp.int32, (block.shape[0], 1), 0) + at
        window = pl.ds(at, block.shape[0])
        out[window, :] = jnp.where(rows < count, out[window, :], block[...])

    put(early, first)
    for c, block in enumerate(late):

        @pl.when(step == c)
        def _():
            put(block, pl.multiple_of(first + EARLY, TILE))


def swapped(block, axis, distance):
    n = lax.axis_size(axis)
    return lax.ppermute(block, axis, [(i, i ^ distance) for i in range(n)])


def after(value, *others):
    return lax.optimization_barrier((value, *others))[0]


def gathered(block, *others):
    far = after(swapped(block, "tensor", 2), *others)
    return (block, swapped(block, "tensor", 1), far, swapped(far, "tensor", 1))


def shards(hidden_pre, cotangent, down_weight, layer_scale, crop_lengths, crop_moves):
    home, ff = hidden_pre.shape
    width = cotangent.shape[1]
    features = down_weight.shape[0]
    half = width // 2
    n = lax.axis_size("dp")
    d = lax.axis_index("dp").astype(jnp.int32)
    t = lax.axis_index("tensor").astype(jnp.int32)
    meta = jnp.concatenate([jnp.stack([d, t]), crop_lengths.reshape(-1), crop_moves.reshape(-1)])
    rows = SEND + KEEP
    scale = layer_scale.reshape(1, features)
    scale_spec = pl.BlockSpec((1, width), lambda i, meta: (0, meta[1]))

    def shape(a, b, dtype=BF):
        return jax.ShapeDtypeStruct((a, b), dtype)

    block = 512
    steps = ff // block
    late, early, pre_a, pre_b = call(
        functools.partial(first_kernel, n), (1,), 1,
        [whole((home, width)), scale_spec, whole((home, ff))],
        [whole((LATE, width)), whole((EARLY, width)), whole((EARLY, block)), whole((EARLY, ff - block))],
        [shape(LATE, width), shape(EARLY, width), shape(EARLY, block), shape(EARLY, ff - block)],
        [], 2 * home * (SEND * width + EARLY * ff), 2 * home * (ff + width),
    )(meta, cotangent, scale, hidden_pre)

    arrived_early = swapped(early, "dp", n // 2)
    arrived_a = swapped(pre_a, "dp", n // 2)
    arrived_b = swapped(pre_b, "dp", n // 2)
    lates = gathered(late, arrived_early, arrived_a)

    rest = call(
        functools.partial(rest_kernel, n), (1,), 1,
        [whole((home, width)), scale_spec], whole((EARLY + KEEP, width)), shape(EARLY + KEEP, width),
        [], 2 * home * (EARLY + KEEP) * width, 4 * home * width,
    )(after(meta, late), cotangent, scale)
    rests = gathered(rest)

    cols = 256
    act, der = call(
        functools.partial(gelu_kernel, n), (ff // cols,), 1,
        [pl.BlockSpec((home, cols), lambda i, *_: (0, i))],
        [pl.BlockSpec((rows, cols), lambda i, *_: (0, i))] * 2,
        [shape(rows, ff), shape(rows, ff, F32)],
        [pltpu.VMEM((rows, home), BF), pltpu.VMEM((rows, cols), F32)],
        2 * rows * home * ff, 2 * home * ff + 6 * rows * ff, 2 * rows * ff,
    )(after(meta, rest), hidden_pre)

    act_spec = pl.BlockSpec((rows, block), lambda i, *_: (0, i))
    half_spec = pl.BlockSpec((half, block), lambda i, *_: (0, i))
    weight_spec = pl.BlockSpec((features, block), lambda i, *_: (0, i))

    def weight_piece(meta, j):
        return call(
            weight_kernel, (steps,), 1,
            [whole((LATE, width)), whole((EARLY + KEEP, width)), act_spec],
            [half_spec] * 2, [shape(half, ff), shape(half, ff, F32)],
            [pltpu.VMEM((width, rows), BF)],
            2 * rows * width * ff, 2 * rows * ff + 3 * width * ff,
        )(meta, lates[j], rests[j], act)

    out_0, keep_0 = weight_piece(meta, 0)
    got_0 = swapped(out_0, "dp", 1)

    wide = ff // 2
    moving = call(
        late_kernel, (2,), 1,
        [whole((LATE, width))] * 4
        + [pl.BlockSpec((features, wide), lambda i, *_: (0, i)), pl.BlockSpec((LATE, wide), lambda i, *_: (0, i))],
        [whole((LATE, wide))] * 2, [shape(LATE, wide)] * 2,
        [pltpu.VMEM((LATE, features), BF)],
        2 * LATE * features * ff, 2 * features * ff + 6 * LATE * ff,
    )(after(meta, out_0), *lates, down_weight, der)
    arrived = [swapped(block, "dp", n // 2) for block in moving]

    out_1, keep_1 = weight_piece(after(meta, *moving, arrived_b), 1)
    got_1 = swapped(out_1, "dp", 1)

    send_a, send_b, keep_a, keep_b = call(
        weight_pair_kernel, (steps,), 1,
        [whole((LATE, width)), whole((EARLY + KEEP, width))] * 2 + [act_spec],
        [half_spec] * 4, [shape(half, ff)] * 2 + [shape(half, ff, F32)] * 2,
        [pltpu.VMEM((2 * width, rows), BF)],
        4 * rows * width * ff, 2 * rows * ff + 6 * width * ff,
    )(after(meta, out_1), lates[2], rests[2], lates[3], rests[3], act)
    got_a = swapped(send_a, "dp", 2)
    got_b = swapped(send_b, "dp", 2)

    arrived_earlies = gathered(arrived_early)
    early_grad = call(
        early_kernel, (steps,), 1,
        [whole((EARLY, width))] * 4
        + [weight_spec, whole((EARLY, block)), pl.BlockSpec((EARLY, block), lambda i, *_: (0, jnp.maximum(i - 1, 0)))],
        pl.BlockSpec((EARLY, block), lambda i, *_: (0, i)), shape(EARLY, ff),
        [pltpu.VMEM((EARLY, features), BF), pltpu.VMEM((EARLY, block), F32), pltpu.VMEM((EARLY, block), BF)],
        2 * EARLY * features * ff, 2 * features * ff + 4 * EARLY * ff, EARLY * ff,
    )(after(meta, send_a), *arrived_earlies, down_weight, arrived_a, arrived_b)

    kept_grad = call(
        kept_kernel, (steps,), 1,
        [whole((EARLY + KEEP, width))] * 4 + [weight_spec, pl.BlockSpec((KEEP, block), lambda i, *_: (1, i))],
        pl.BlockSpec((KEEP, block), lambda i, *_: (0, i)), shape(KEEP, ff),
        [pltpu.VMEM((KEEP, features), BF)],
        2 * KEEP * features * ff, 2 * features * ff + 6 * KEEP * ff,
    )(after(meta, early_grad), *rests, down_weight, der)

    near = ((d // 2) ^ t) % 2 == 0
    got_0 = after(got_0, arrived[0])
    got_a = after(got_a, arrived[0])
    held_0 = keep_0 + got_0.astype(F32)
    held_1 = keep_1 + got_1.astype(F32)
    out_n = jnp.where(near, held_1, held_0).astype(BF)
    first = jnp.where(near, held_0, held_1) + swapped(out_n, "dp", 2).astype(F32)
    out_x = (keep_a + got_a.astype(F32)).astype(BF)
    second = keep_b + got_b.astype(F32) + swapped(out_x, "dp", 1).astype(F32)
    far = ((d // 4) ^ (t // 2)) % 2 == 0
    first = after(first, arrived[1])
    out_f = jnp.where(far, second, first).astype(BF)
    total = jnp.where(far, first, second) + swapped(out_f, "dp", 4).astype(F32)
    down_grad = total / math.sqrt(n * home)

    hidden_grad = call(
        functools.partial(place_kernel, n), (2,), 1,
        [pl.BlockSpec((KEEP, wide), lambda i, *_: (0, i)), pl.BlockSpec((EARLY, wide), lambda i, *_: (0, i))]
        + [whole((LATE, wide))] * 2,
        pl.BlockSpec((BAL, wide), lambda i, *_: (0, i)), shape(BAL, ff),
        [], 0, 2 * ff * (BAL + KEEP + SEND),
    )(meta, kept_grad, early_grad, *arrived)
    return (hidden_grad, down_grad)


def solution(mesh):
    pairs_and_fours = (mesh.shape["dp"], mesh.shape["tensor"]) == (8, 4)
    return jax.shard_map(
        shards if pairs_and_fours else general_shards,
        mesh=mesh,
        in_specs=(P("dp", "tensor"), P("dp", "tensor"), P(None, "tensor"), P(), P(), P()),
        out_specs=(P("dp", "tensor"), P("dp", "tensor")),
        check_vma=False,
    )


def shifted(block, axis, distance):
    devices = range(lax.axis_size(axis))
    route = [((i - distance) % len(devices), i) for i in devices]
    return lax.ppermute(block, axis, route)


def crop_rows(row_total, crop_sizes, crop_starts):
    crop_ends = jnp.cumsum(crop_sizes)
    crop_begins = crop_ends - crop_sizes
    target_rows = jnp.arange(row_total, dtype=jnp.int32)[:, None]
    inside_crop = (target_rows >= crop_begins[None, :]) & (target_rows < crop_ends[None, :])
    source_rows = jnp.sum(
        jnp.where(inside_crop, crop_starts[None, :] + target_rows - crop_begins[None, :], 0), axis=1
    )
    return (source_rows, jnp.any(inside_crop, axis=1))


def select_rows(row_block, source_rows, valid_rows):
    taken = jnp.take(row_block, source_rows, axis=0)
    return jnp.where(valid_rows[:, None], taken, jnp.zeros((), row_block.dtype))


def gelu_parts(pre_act):
    cumulative = 0.5 * (1.0 + jax.scipy.special.erf(pre_act * inv_root_two))
    activated = pre_act * cumulative
    derivative = cumulative + pre_act * jnp.exp(-0.5 * pre_act * pre_act) * inv_root_tau
    return (activated, derivative)


def local_grads(pre_rows, cot_part, live_rows, layer_scale, down_weight, home_rows):
    cot_full = lax.all_gather(cot_part, "tensor", axis=1, tiled=True)
    scaled = (cot_full.astype(F32) * layer_scale[None, :]).astype(BF)
    activated, derivative = gelu_parts(pre_rows.astype(F32))
    activation = jnp.where(live_rows[:, None], activated, 0.0).astype(BF)
    backward = jnp.dot(scaled, down_weight, preferred_element_type=F32) * derivative
    gradient_rows = jnp.where(live_rows[:, None], backward, 0.0).astype(BF)
    weight_grad = lax.psum_scatter(
        lax.dot_general(scaled, activation, (((0,), (0,)), ((), ())), preferred_element_type=F32),
        "dp",
        scatter_dimension=0,
        tiled=True,
    )
    return (gradient_rows, weight_grad / math.sqrt(lax.axis_size("dp") * home_rows))


def general_shards(hidden_pre, cotangent, down_weight, layer_scale, crop_lengths, crop_moves):
    devices = lax.axis_size("dp")
    half_axis = devices // 2
    device_index = lax.axis_index("dp")
    partner_index = (device_index + half_axis) % devices
    own_lengths = lax.dynamic_index_in_dim(crop_lengths, device_index, 0, keepdims=False)
    own_moves = lax.dynamic_index_in_dim(crop_moves, device_index, 0, keepdims=False)
    partner_lengths = lax.dynamic_index_in_dim(crop_lengths, partner_index, 0, keepdims=False)
    partner_moves = lax.dynamic_index_in_dim(crop_moves, partner_index, 0, keepdims=False)
    home_rows = hidden_pre.shape[0]
    own_starts = jnp.cumsum(own_lengths) - own_lengths
    sent_sizes = own_lengths * own_moves
    kept_sizes = own_lengths * (1 - own_moves)
    arrived = jnp.sum(partner_lengths * partner_moves)
    send_source, send_valid = crop_rows(SEND, sent_sizes, own_starts)
    keep_sizes = jnp.concatenate([kept_sizes, arrived[None]])
    keep_starts = jnp.concatenate([own_starts, jnp.full((1,), home_rows, jnp.int32)])
    keep_source, keep_valid = crop_rows(BAL, keep_sizes, keep_starts)
    live_home = jnp.arange(home_rows, dtype=jnp.int32) < jnp.sum(own_lengths)
    gradient_rows, weight_grad = local_grads(
        hidden_pre, cotangent, live_home, layer_scale, down_weight, home_rows
    )
    outgoing = select_rows(gradient_rows, send_source, send_valid)
    incoming = shifted(outgoing, "dp", half_axis)
    balanced = select_rows(jnp.concatenate([gradient_rows, incoming], 0), keep_source, keep_valid)
    return (balanced, weight_grad)
```

time: 206 us -> 166 us (0.81)
  waiting for transfers between devices: 120 us -> 72.2 us
  local copies, waits for them, and re-layouts: 8.24 us -> 12.8 us
  Pallas kernels: 47.3 us -> 50.1 us
    ppermute x17 -> x21, waiting for transfers between devices: 120 us -> 72.2 us  [swapped(): return lax.ppermute(block, axis, [(i, i ^ distance) for i in range(n)])]
    unnamed x44 -> x60, local copies, waits for them, and re-layouts: 7.54 us -> 12 us
    convert_element_type x3, other arithmetic: 7.98 us -> 4.47 us  [the longest x1 2.42 us: shards(): out_n = jnp.where(near, held_1, held_0).astype(BF)]
    pallas_call x9 -> x10, Pallas kernels: 47.3 us -> 50.1 us  [the longest x1 12.4 us: shards(): call(functools.partial(gelu_kernel, n), (ff // cols,), 1, [pl.BlockSpec((...]
    ppermute x17 -> x21, starting transfers between devices: 20.4 us -> 21 us  [swapped(): return lax.ppermute(block, axis, [(i, i ^ distance) for i in range(n)])]
  transfers between devices with their start and end apart: 17 -> 21, of which waited for: 8 -> 10; matrix products, arithmetic and copies ran while one was open for 2% -> 4% of each run, Pallas kernels for 22% -> 29%
where the time goes in v2:
time: 166 us; the launch traced here: 165 us
  waiting for transfers between devices  72.2 us (43%)
  Pallas kernels  50.1 us (30%)
  starting transfers between devices  21 us (13%)
  local copies, waits for them, and re-layouts  12.8 us (8%)
  other arithmetic  7.89 us (5%)
    ppermute x21, waiting for transfers between devices, swapped(): return lax.ppermute(block, axis, [(i, i ^ distance) for i in range(n)])  72.2 us
    ppermute x21, starting transfers between devices, swapped(): return lax.ppermute(block, axis, [(i, i ^ distance) for i in range(n)])  21 us
    pallas_call x1, Pallas kernels, shards(): call(functools.partial(gelu_kernel, n), (ff // cols,), 1, [pl.BlockSpec((...  12.4 us
    unnamed x60, local copies, waits for them, and re-layouts  12 us
    pallas_call x2, Pallas kernels, weight_piece(): call(weight_kernel, (steps,), 1, [whole((LATE, width)), whole((EARLY + KE...  7.64 us
    pallas_call x1, Pallas kernels, shards(): call(weight_pair_kernel, (steps,), 1, [whole((LATE, width)), whole((EARLY...  7.04 us
    pallas_call x1, Pallas kernels, shards(): call(late_kernel, (2,), 1, [whole((LATE, width))] * 4 + [pl.BlockSpec((fe...  6.66 us
    pallas_call x1, Pallas kernels, shards(): call(kept_kernel, (steps,), 1, [whole((EARLY + KEEP, width))] * 4 + [weig...  6.38 us
  transfers between devices with their start and end apart: 21, of which 10 were waited for; matrix products, arithmetic and copies ran while one was open for 4% of the time, Pallas kernels for 29%

profile of v2, /device:TPU:0, one launch (start us, length us, event | category | flops | bytes accessed | tf_op | source)
XLA Modules:
  0.0 165.0 jit_solution(11521349443567779752)
XLA Ops:
  3.1 1.9 %copy-done.2 = bf16[1032,1536]{1,0:T(8,128)(2,1)S(1)} copy-done((bf16[1032,1536]{1,0:T(8,128)(2,1)S(1)}, bf16[1032,1536]{1,0:T(8,128)(2,1)}, u32[]{:S(2)}) %copy-start.2) | copy-done | bytes 3170328
  6.1 2.0 %shard_map.77 = (bf16[400,384]{1,0:T(8,128)(2,1)S(1)}, bf16[128,384]{1,0:T(8,128)(2,1)S(1)}, bf16[128,512]{1,0:T(8,128)(2,1)S(1)}, bf16[128,1024]{1,0:T(8,128)(2,1)S(1)}) custom-call(s32[66]{0:T(128)S(1)} %pad_add_fusion.meta, bf16[1032,384]{1,0:T(8,128)(2,1)S(1)} %copy-done.10, f32[1,1536]{1,0:T(1,128)S(1)} %reshape.15.scale, bf16[1032,1536]{1,0:T(8,128)(2,1)S(1)} %copy-done.2), custom_call_target="tpu_custom_call" | custom-call | flops 1 | bytes 1 | tf_op jit(solution)/shard_map/pallas_call | solution.py:279
  8.1 3.0 %collective-permute-start.1 = (bf16[400,384]{1,0:T(8,128)(2,1)S(1)}, bf16[400,384]{1,0:T(8,128)(2,1)S(1)}, u32[]{:S(2)}, u32[]{:S(2)}) collective-permute-start(bf16[400,384]{1,0:T(8,128)(2,1)S(1)} %get-tuple-element.29.late.p0), channel_id=1, source_target_pairs={{0,2},{1,3},{2,0},{3,1},{4,6},{5,7},{6,4},{7,5},{8,10},{9,11},{10,... | collective-permute-start | bytes 921608 | tf_op jit(solution)/shard_map/ppermute | solution.py:249
  12.9 2.7 %collective-permute-start.3 = (bf16[128,512]{1,0:T(8,128)(2,1)S(1)}, bf16[128,512]{1,0:T(8,128)(2,1)S(1)}, u32[]{:S(2)}, u32[]{:S(2)}) collective-permute-start(bf16[128,512]{1,0:T(8,128)(2,1)S(1)} %get-tuple-element.36), channel_id=1, source_target_pairs={{0,16},{4,20},{8,24},{12,28},{16,0},{20,4},{24,8},{28,12},{1,17},{... | collective-permute-start | bytes 393224 | tf_op jit(solution)/shard_map/ppermute | solution.py:249
  16.2 10.7 %collective-permute-done.2.p0 = bf16[128,384]{1,0:T(8,128)(2,1)} collective-permute-done((bf16[128,384]{1,0:T(8,128)(2,1)S(1)}, bf16[128,384]{1,0:T(8,128)(2,1)}, u32[]{:S(2)}, u32[]{:S(2)}) %collective-permute-start.2) | collective-permute-done | bytes 98336 | tf_op jit(solution)/shard_map/ppermute | solution.py:249
  28.1 12.4 %shard_map.79 = (bf16[1056,1536]{1,0:T(8,128)(2,1)}, f32[1056,1536]{1,0:T(8,128)}) custom-call(s32[66]{0:T(128)S(1)} %pad_add_fusion.meta, bf16[1032,1536]{1,0:T(8,128)(2,1)S(1)} %copy-done.3), custom_call_target="tpu_custom_call" | custom-call | flops 1 | bytes 1 | tf_op jit(solution)/shard_map/pallas_call | solution.py:300
  40.5 1.9 %copy-done = bf16[1056,1536]{1,0:T(8,128)(2,1)S(1)} copy-done((bf16[1056,1536]{1,0:T(8,128)(2,1)S(1)}, bf16[1056,1536]{1,0:T(8,128)(2,1)}, u32[]{:S(2)}) %copy-start) | copy-done | bytes 3244056
  42.4 3.8 %shard_map.80 = (bf16[192,1536]{1,0:T(8,128)(2,1)}, f32[192,1536]{1,0:T(8,128)S(1)}) custom-call(s32[66]{0:T(128)S(1)} %pad_add_fusion.meta, bf16[400,384]{1,0:T(8,128)(2,1)S(1)} %get-tuple-element.29.late.p0, bf16[656,384]{1,0:T(8,128)(2,1)S(1)} %shard_map.78.rest.r0, bf16[1056,1536]{1,0:T(8,128)(2,1)S(1)} %copy-done), custom_call_target="tpu_custom_call" | custom-call | flops 1 | bytes 1 | tf_op jit(solution)/shard_map/pallas_call | solution.py:314
  46.3 6.7 %shard_map.81 = (bf16[400,768]{1,0:T(8,128)(2,1)}, bf16[400,768]{1,0:T(8,128)(2,1)S(1)}) custom-call(s32[66]{0:T(128)S(1)} %pad_add_fusion.meta, bf16[400,384]{1,0:T(8,128)(2,1)S(1)} %get-tuple-element.29.late.p0, bf16[400,384]{1,0:T(8,128)(2,1)S(1)} %collective-permute-done.p1.late, bf16[400,384]{1,0:T(8,128)(2,1)S(1)} %collective-permute-done.1.p2.late_a, ...), custom_call_target="tpu_custom_call" | custom-call | flops 1 | bytes 1 | tf_op jit(solution)/shard_map/pallas_call | solution.py:326
  53.0 3.0 %collective-permute-start.12 = (bf16[400,768]{1,0:T(8,128)(2,1)}, bf16[400,768]{1,0:T(8,128)(2,1)}, u32[]{:S(2)}, u32[]{:S(2)}) collective-permute-start(bf16[400,768]{1,0:T(8,128)(2,1)} %get-tuple-element.39), channel_id=1, source_target_pairs={{0,16},{4,20},{8,24},{12,28},{16,0},{20,4},{24,8},{28,12},{1,17},{... | collective-permute-start | bytes 1843208 | tf_op jit(solution)/shard_map/ppermute | solution.py:249
  57.5 3.8 %shard_map.82 = (bf16[192,1536]{1,0:T(8,128)(2,1)}, f32[192,1536]{1,0:T(8,128)S(1)}) custom-call(s32[66]{0:T(128)S(1)} %pad_add_fusion.meta, bf16[400,384]{1,0:T(8,128)(2,1)S(1)} %collective-permute-done.p1.late, bf16[656,384]{1,0:T(8,128)(2,1)S(1)} %collective-permute-done.6.rest.r1, bf16[1056,1536]{1,0:T(8,128)(2,1)S(1)} %copy-done.1), custom_call_target="tpu_custom_call" | custom-call | flops 1 | bytes 1 | tf_op jit(solution)/shard_map/pallas_call | solution.py:314
  62.9 2.1 %collective-permute-done.8.rest_b.r3 = bf16[656,384]{1,0:T(8,128)(2,1)S(1)} collective-permute-done((bf16[656,384]{1,0:T(8,128)(2,1)}, bf16[656,384]{1,0:T(8,128)(2,1)S(1)}, u32[]{:S(2)}, u32[]{:S(2)}) %collective-permute-start.8) | collective-permute-done | bytes 503840 | tf_op jit(solution)/shard_map/ppermute | solution.py:249
  68.7 7.0 %shard_map.83 = (bf16[192,1536]{1,0:T(8,128)(2,1)}, bf16[192,1536]{1,0:T(8,128)(2,1)S(1)}, f32[192,1536]{1,0:T(8,128)S(1)}, f32[192,1536]{1,0:T(8,128)S(1)}) custom-call(s32[66]{0:T(128)S(1)} %pad_add_fusion.meta, bf16[400,384]{1,0:T(8,128)(2,1)S(1)} %copy-done.17, bf16[656,384]{1,0:T(8,128)(2,1)} %collective-permute-done.7.rest_a.r2, ...), custom_call_target="tpu_custom_call" | custom-call | flops 1 | bytes 1 | tf_op jit(solution)/shard_map/pallas_call | solution.py:339
  77.0 6.4 %collective-permute-done.12.rest_0_ = bf16[400,768]{1,0:T(8,128)(2,1)} collective-permute-done((bf16[400,768]{1,0:T(8,128)(2,1)}, bf16[400,768]{1,0:T(8,128)(2,1)}, u32[]{:S(2)}, u32[]{:S(2)}) %collective-permute-start.12) | collective-permute-done | bytes 614432 | tf_op jit(solution)/shard_map/ppermute | solution.py:249
  83.7 2.4 %select_convert_fusion.1 = bf16[192,1536]{1,0:T(8,128)(2,1)} fusion(f32[192,1536]{1,0:T(8,128)S(1)} %copy-done.5, bf16[192,1536]{1,0:T(8,128)(2,1)} %collective-permute-done.14, f32[192,1536]{1,0:T(8,128)S(1)} %copy-done.7, bf16[192,1536]{1,0:T(8,128)(2,1)} %collective-permute-done.15, pred[]{:T(512)S(6)} %eq.10), kind=kLoop, calls=%fused_computation.5 | loop fusion | flops 1769472 | bytes 4128769 | tf_op jit(solution)/shard_map/convert_element_type | solution.py:372
  87.6 2.6 %collective-permute-start.13 = (bf16[400,768]{1,0:T(8,128)(2,1)}, bf16[400,768]{1,0:T(8,128)(2,1)S(1)}, u32[]{:S(2)}, u32[]{:S(2)}) collective-permute-start(bf16[400,768]{1,0:T(8,128)(2,1)} %copy-done.25), channel_id=1, source_target_pairs={{0,16},{4,20},{8,24},{12,28},{16,0},{20,4},{24,8},{28,12},{1,17},{... | collective-permute-start | bytes 1843208 | tf_op jit(solution)/shard_map/ppermute | solution.py:249
  90.3 18.9 %collective-permute-done.18 = bf16[192,1536]{1,0:T(8,128)(2,1)} collective-permute-done((bf16[192,1536]{1,0:T(8,128)(2,1)}, bf16[192,1536]{1,0:T(8,128)(2,1)}, u32[]{:S(2)}, u32[]{:S(2)}) %collective-permute-start.18) | collective-permute-done | bytes 589856 | tf_op jit(solution)/shard_map/ppermute | solution.py:249
  112.4 9.4 %collective-permute-done.16 = bf16[192,1536]{1,0:T(8,128)(2,1)} collective-permute-done((bf16[192,1536]{1,0:T(8,128)(2,1)}, bf16[192,1536]{1,0:T(8,128)(2,1)}, u32[]{:S(2)}, u32[]{:S(2)}) %collective-permute-start.16) | collective-permute-done | bytes 589856 | tf_op jit(solution)/shard_map/ppermute | solution.py:249
  123.7 10.6 %collective-permute-done.17 = bf16[192,1536]{1,0:T(8,128)(2,1)S(1)} collective-permute-done((bf16[192,1536]{1,0:T(8,128)(2,1)}, bf16[192,1536]{1,0:T(8,128)(2,1)S(1)}, u32[]{:S(2)}, u32[]{:S(2)}) %collective-permute-start.17) | collective-permute-done | bytes 589856 | tf_op jit(solution)/shard_map/ppermute | solution.py:249
  136.9 4.4 %collective-permute-done.10.p2 = bf16[128,384]{1,0:T(8,128)(2,1)S(1)} collective-permute-done((bf16[128,384]{1,0:T(8,128)(2,1)}, bf16[128,384]{1,0:T(8,128)(2,1)S(1)}, u32[]{:S(2)}, u32[]{:S(2)}) %collective-permute-start.10) | collective-permute-done | bytes 98336 | tf_op jit(solution)/shard_map/ppermute | solution.py:249
  142.6 3.0 %shard_map.84.early = bf16[128,1536]{1,0:T(8,128)(2,1)S(1)} custom-call(s32[66]{0:T(128)S(1)} %pad_add_fusion.meta, bf16[128,384]{1,0:T(8,128)(2,1)} %collective-permute-done.2.p0, bf16[128,384]{1,0:T(8,128)(2,1)S(1)} %collective-permute-done.9.p1, bf16[128,384]{1,0:T(8,128)(2,1)S(1)} %collective-permute-done.10.p2, ...), custom_call_target="tpu_custom_call" | custom-call | flops 1 | bytes 1 | tf_op jit(solution)/shard_map/pallas_call | solution.py:350
  145.6 6.4 %shard_map.85.kept = bf16[528,1536]{1,0:T(8,128)(2,1)S(1)} custom-call(s32[66]{0:T(128)S(1)} %pad_add_fusion.meta, bf16[656,384]{1,0:T(8,128)(2,1)S(1)} %copy-done.9, bf16[656,384]{1,0:T(8,128)(2,1)S(1)} %copy-done.15, bf16[656,384]{1,0:T(8,128)(2,1)} %collective-permute-done.7.rest_a.r2, bf16[656,384]{1,0:T(8,128)(2,1)S(1)} %copy-done.13, ...), custom_call_target="tpu_custom_call" | custom-call | flops 1 | bytes 1 | tf_op jit(solution)/shard_map/pallas_call | solution.py:359
  152.0 3.2 %shard_map.86 = bf16[720,1536]{1,0:T(8,128)(2,1)} custom-call(s32[66]{0:T(128)S(1)} %pad_add_fusion.meta, bf16[528,1536]{1,0:T(8,128)(2,1)S(1)} %shard_map.85.kept, bf16[128,1536]{1,0:T(8,128)(2,1)S(1)} %shard_map.84.early, bf16[400,768]{1,0:T(8,128)(2,1)} %collective-permute-done.12.rest_0_, bf16[400,768]{1,0:T(8,128)(2,1)S(1)} %collective-permute-done.13.rest_1_), custom_call_target="tpu_custom_call" | custom-call | flops 1 | bytes 1 | tf_op jit(solution)/shard_map/pallas_call | solution.py:382
  155.2 8.3 %collective-permute-done.20 = bf16[192,1536]{1,0:T(8,128)(2,1)S(1)} collective-permute-done((bf16[192,1536]{1,0:T(8,128)(2,1)S(1)}, bf16[192,1536]{1,0:T(8,128)(2,1)S(1)}, u32[]{:S(2)}, u32[]{:S(2)}) %collective-permute-start.20) | collective-permute-done | bytes 589856 | tf_op jit(solution)/shard_map/ppermute | solution.py:249
  (98 shorter events, 27.6 us)
Async XLA Ops:
  8.1 19.4 %collective-permute-start.1 = (bf16[400,384]{1,0:T(8,128)(2,1)S(1)}, bf16[400,384]{1,0:T(8,128)(2,1)S(1)}, u32[]{:S(2)}, u32[]{:S(2)}) collective-permute-start(bf16[400,384]{1,0:T(8,128)(2,1)S(1)} %get-tuple-element.29.late.p0), channel_id=1, source_target_pairs={{0,2},{1,3},{2,0},{3,1},{4,6},{5,7},{6,4},{7,5},{8,10},{9,11},{10,... | collective-permute-start | bytes 921608 | tf_op jit(solution)/shard_map/ppermute | solution.py:249
  12.9 27.7 %copy-start.8 = (bf16[656,384]{1,0:T(8,128)(2,1)}, bf16[656,384]{1,0:T(8,128)(2,1)S(1)}, u32[]{:S(2)}) copy-start(bf16[656,384]{1,0:T(8,128)(2,1)S(1)} %shard_map.78.rest.r0) | copy-start | bytes 1511428
  12.9 44.6 %collective-permute-start.6 = (bf16[656,384]{1,0:T(8,128)(2,1)S(1)}, bf16[656,384]{1,0:T(8,128)(2,1)S(1)}, u32[]{:S(2)}, u32[]{:S(2)}) collective-permute-start(bf16[656,384]{1,0:T(8,128)(2,1)S(1)} %shard_map.78.rest.r0), channel_id=1, source_target_pairs={{0,1},{1,0},{2,3},{3,2},{4,5},{5,4},{6,7},{7,6},{8,9},{9,8},{10,11... | collective-permute-start | bytes 1511432 | tf_op jit(solution)/shard_map/ppermute | solution.py:249
  12.9 13.9 %collective-permute-start.3 = (bf16[128,512]{1,0:T(8,128)(2,1)S(1)}, bf16[128,512]{1,0:T(8,128)(2,1)S(1)}, u32[]{:S(2)}, u32[]{:S(2)}) collective-permute-start(bf16[128,512]{1,0:T(8,128)(2,1)S(1)} %get-tuple-element.36), channel_id=1, source_target_pairs={{0,16},{4,20},{8,24},{12,28},{16,0},{20,4},{24,8},{28,12},{1,17},{... | collective-permute-start | bytes 393224 | tf_op jit(solution)/shard_map/ppermute | solution.py:249
  15.6 11.3 %collective-permute-start.2 = (bf16[128,384]{1,0:T(8,128)(2,1)S(1)}, bf16[128,384]{1,0:T(8,128)(2,1)}, u32[]{:S(2)}, u32[]{:S(2)}) collective-permute-start(bf16[128,384]{1,0:T(8,128)(2,1)S(1)} %get-tuple-element.35), channel_id=1, source_target_pairs={{0,16},{4,20},{8,24},{12,28},{16,0},{20,4},{24,8},{28,12},{1,17},{... | collective-permute-start | bytes 294920 | tf_op jit(solution)/shard_map/ppermute | solution.py:249
  15.9 46.9 %collective-permute-start.7 = (bf16[656,384]{1,0:T(8,128)(2,1)S(1)}, bf16[656,384]{1,0:T(8,128)(2,1)}, u32[]{:S(2)}, u32[]{:S(2)}) collective-permute-start(bf16[656,384]{1,0:T(8,128)(2,1)S(1)} %shard_map.78.rest.r0), channel_id=1, source_target_pairs={{0,2},{1,3},{2,0},{3,1},{4,6},{5,7},{6,4},{7,5},{8,10},{9,11},{10,... | collective-permute-start | bytes 1511432 | tf_op jit(solution)/shard_map/ppermute | solution.py:249
  26.9 19.4 %collective-permute-start = (bf16[400,384]{1,0:T(8,128)(2,1)S(1)}, bf16[400,384]{1,0:T(8,128)(2,1)S(1)}, u32[]{:S(2)}, u32[]{:S(2)}) collective-permute-start(bf16[400,384]{1,0:T(8,128)(2,1)S(1)} %get-tuple-element.29.late.p0), channel_id=1, source_target_pairs={{0,1},{1,0},{2,3},{3,2},{4,5},{5,4},{6,7},{7,6},{8,9},{9,8},{10,11... | collective-permute-start | bytes 921608 | tf_op jit(solution)/shard_map/ppermute | solution.py:249
  27.6 18.7 %collective-permute-start.4 = (bf16[400,384]{1,0:T(8,128)(2,1)S(1)}, bf16[400,384]{1,0:T(8,128)(2,1)S(1)}, u32[]{:S(2)}, u32[]{:S(2)}) collective-permute-start(bf16[400,384]{1,0:T(8,128)(2,1)S(1)} %collective-permute-done.1.p2.late_a), channel_id=1, source_target_pairs={{0,1},{1,0},{2,3},{3,2},{4,5},{5,4},{6,7},{7,6},{8,9},{9,8},{10,11... | collective-permute-start | bytes 921608 | tf_op jit(solution)/shard_map/ppermute | solution.py:249
  28.1 29.4 %collective-permute-start.5 = (bf16[128,1024]{1,0:T(8,128)(2,1)S(1)}, bf16[128,1024]{1,0:T(8,128)(2,1)S(1)}, u32[]{:S(2)}, u32[]{:S(2)}) collective-permute-start(bf16[128,1024]{1,0:T(8,128)(2,1)S(1)} %get-tuple-element.41), channel_id=1, source_target_pairs={{0,16},{4,20},{8,24},{12,28},{16,0},{20,4},{24,8},{28,12},{1,17},{... | collective-permute-start | bytes 786440 | tf_op jit(solution)/shard_map/ppermute | solution.py:249
  53.0 30.4 %collective-permute-start.12 = (bf16[400,768]{1,0:T(8,128)(2,1)}, bf16[400,768]{1,0:T(8,128)(2,1)}, u32[]{:S(2)}, u32[]{:S(2)}) collective-permute-start(bf16[400,768]{1,0:T(8,128)(2,1)} %get-tuple-element.39), channel_id=1, source_target_pairs={{0,16},{4,20},{8,24},{12,28},{16,0},{20,4},{24,8},{28,12},{1,17},{... | collective-permute-start | bytes 1843208 | tf_op jit(solution)/shard_map/ppermute | solution.py:249
  56.0 21.0 %collective-permute-start.14 = (bf16[192,1536]{1,0:T(8,128)(2,1)}, bf16[192,1536]{1,0:T(8,128)(2,1)}, u32[]{:S(2)}, u32[]{:S(2)}) collective-permute-start(bf16[192,1536]{1,0:T(8,128)(2,1)} %get-tuple-element.33), channel_id=1, source_target_pairs={{0,4},{4,0},{8,12},{12,8},{16,20},{20,16},{24,28},{28,24},{1,5},{5... | collective-permute-start | bytes 1769480 | tf_op jit(solution)/shard_map/ppermute | solution.py:249
  62.3 21.3 %collective-permute-start.15 = (bf16[192,1536]{1,0:T(8,128)(2,1)}, bf16[192,1536]{1,0:T(8,128)(2,1)}, u32[]{:S(2)}, u32[]{:S(2)}) collective-permute-start(bf16[192,1536]{1,0:T(8,128)(2,1)} %get-tuple-element.43), channel_id=1, source_target_pairs={{0,4},{4,0},{8,12},{12,8},{16,20},{20,16},{24,28},{28,24},{1,5},{5... | collective-permute-start | bytes 1769480 | tf_op jit(solution)/shard_map/ppermute | solution.py:249
  62.9 2.1 %collective-permute-start.8 = (bf16[656,384]{1,0:T(8,128)(2,1)}, bf16[656,384]{1,0:T(8,128)(2,1)S(1)}, u32[]{:S(2)}, u32[]{:S(2)}) collective-permute-start(bf16[656,384]{1,0:T(8,128)(2,1)} %collective-permute-done.7.rest_a.r2), channel_id=1, source_target_pairs={{0,1},{1,0},{2,3},{3,2},{4,5},{5,4},{6,7},{7,6},{8,9},{9,8},{10,11... | collective-permute-start | bytes 1511432 | tf_op jit(solution)/shard_map/ppermute | solution.py:249
  75.8 33.4 %collective-permute-start.18 = (bf16[192,1536]{1,0:T(8,128)(2,1)}, bf16[192,1536]{1,0:T(8,128)(2,1)}, u32[]{:S(2)}, u32[]{:S(2)}) collective-permute-start(bf16[192,1536]{1,0:T(8,128)(2,1)} %get-tuple-element.45), channel_id=1, source_target_pairs={{0,8},{4,12},{8,0},{12,4},{16,24},{20,28},{24,16},{28,20},{1,9},{5... | collective-permute-start | bytes 1769480 | tf_op jit(solution)/shard_map/ppermute | solution.py:249
  86.1 35.7 %collective-permute-start.16 = (bf16[192,1536]{1,0:T(8,128)(2,1)}, bf16[192,1536]{1,0:T(8,128)(2,1)}, u32[]{:S(2)}, u32[]{:S(2)}) collective-permute-start(bf16[192,1536]{1,0:T(8,128)(2,1)} %select_convert_fusion.1), channel_id=1, source_target_pairs={{0,8},{4,12},{8,0},{12,4},{16,24},{20,28},{24,16},{28,20},{1,9},{5... | collective-permute-start | bytes 1769480 | tf_op jit(solution)/shard_map/ppermute | solution.py:249
  87.6 36.1 %collective-permute-start.13 = (bf16[400,768]{1,0:T(8,128)(2,1)}, bf16[400,768]{1,0:T(8,128)(2,1)S(1)}, u32[]{:S(2)}, u32[]{:S(2)}) collective-permute-start(bf16[400,768]{1,0:T(8,128)(2,1)} %copy-done.25), channel_id=1, source_target_pairs={{0,16},{4,20},{8,24},{12,28},{16,0},{20,4},{24,8},{28,12},{1,17},{... | collective-permute-start | bytes 1843208 | tf_op jit(solution)/shard_map/ppermute | solution.py:249
  90.1 44.1 %collective-permute-start.17 = (bf16[192,1536]{1,0:T(8,128)(2,1)}, bf16[192,1536]{1,0:T(8,128)(2,1)S(1)}, u32[]{:S(2)}, u32[]{:S(2)}) collective-permute-start(bf16[192,1536]{1,0:T(8,128)(2,1)} %copy-done.26), channel_id=1, source_target_pairs={{0,8},{4,12},{8,0},{12,4},{16,24},{20,28},{24,16},{28,20},{1,9},{5... | collective-permute-start | bytes 1769480 | tf_op jit(solution)/shard_map/ppermute | solution.py:249
  109.2 33.4 %slice-start = ((s8[4718592]{0:T(1024)(128)(4,1)}), s8[4194304]{0:T(1024)(128)(4,1)S(1)}, s32[]{:S(2)}) async-start(s8[4718592]{0:T(1024)(128)(4,1)} %bitcast.2), calls=%async_computation | async-start | bytes 8388608
  110.8 31.7 %slice-start.1 = ((s8[4718592]{0:T(1024)(128)(4,1)}), s8[524288]{0:T(1024)(128)(4,1)S(1)}, s32[]{:S(2)}) async-start(s8[4718592]{0:T(1024)(128)(4,1)} %bitcast.2), calls=%async_computation.1 | async-start | bytes 1048576
  110.9 23.4 %collective-permute-start.19 = (bf16[192,1536]{1,0:T(8,128)(2,1)S(1)}, bf16[192,1536]{1,0:T(8,128)(2,1)S(1)}, u32[]{:S(2)}, u32[]{:S(2)}) collective-permute-start(bf16[192,1536]{1,0:T(8,128)(2,1)S(1)} %add_convert_fusion), channel_id=1, source_target_pairs={{0,4},{4,0},{8,12},{12,8},{16,20},{20,16},{24,28},{28,24},{1,5},{5... | collective-permute-start | bytes 1769480 | tf_op jit(solution)/shard_map/ppermute | solution.py:249
  134.7 28.9 %collective-permute-start.20 = (bf16[192,1536]{1,0:T(8,128)(2,1)S(1)}, bf16[192,1536]{1,0:T(8,128)(2,1)S(1)}, u32[]{:S(2)}, u32[]{:S(2)}) collective-permute-start(bf16[192,1536]{1,0:T(8,128)(2,1)S(1)} %select_convert_fusion), channel_id=1, source_target_pairs={{0,16},{4,20},{8,24},{12,28},{16,0},{20,4},{24,8},{28,12},{1,17},{... | collective-permute-start | bytes 1769480 | tf_op jit(solution)/shard_map/ppermute | solution.py:249
  136.4 4.8 %collective-permute-start.10 = (bf16[128,384]{1,0:T(8,128)(2,1)}, bf16[128,384]{1,0:T(8,128)(2,1)S(1)}, u32[]{:S(2)}, u32[]{:S(2)}) collective-permute-start(bf16[128,384]{1,0:T(8,128)(2,1)} %collective-permute-done.2.p0), channel_id=1, source_target_pairs={{0,2},{1,3},{2,0},{3,1},{4,6},{5,7},{6,4},{7,5},{8,10},{9,11},{10,... | collective-permute-start | bytes 294920 | tf_op jit(solution)/shard_map/ppermute | solution.py:249
  136.9 4.4 %collective-permute-start.9 = (bf16[128,384]{1,0:T(8,128)(2,1)}, bf16[128,384]{1,0:T(8,128)(2,1)S(1)}, u32[]{:S(2)}, u32[]{:S(2)}) collective-permute-start(bf16[128,384]{1,0:T(8,128)(2,1)} %collective-permute-done.2.p0), channel_id=1, source_target_pairs={{0,1},{1,0},{2,3},{3,2},{4,5},{5,4},{6,7},{7,6},{8,9},{9,8},{10,11... | collective-permute-start | bytes 294920 | tf_op jit(solution)/shard_map/ppermute | solution.py:249
  141.2 1.3 collective-permute-start.11
  (26 other events, 203.3 us)

commit v3 on v0

v3 whole, which is shorter than its diff:
```python
import functools
import math

import jax
import jax.numpy as jnp
from jax import lax
from jax.experimental import pallas as pl
from jax.experimental.pallas import tpu as pltpu
from jax.sharding import PartitionSpec as P

SEND = 528
KEEP = 528
TILE = 16
EARLY = 128
LATE = SEND - EARLY
SLOTS = 4
BAL = 720
BF = jnp.bfloat16
F32 = jnp.float32

inv_root_two = 0.7071067811865476
inv_root_tau = 0.3989422804014327


def kernel_call(kernel, out_shape, in_specs, out_specs, scratch=(), grid=(1,)):
    return pl.pallas_call(
        kernel,
        grid_spec=pltpu.PrefetchScalarGridSpec(
            num_scalar_prefetch=1,
            grid=grid,
            in_specs=in_specs,
            out_specs=out_specs,
            scratch_shapes=list(scratch),
        ),
        out_shape=out_shape,
        cost_estimate=pl.CostEstimate(flops=1, bytes_accessed=1, transcendentals=0),
        compiler_params=pltpu.CompilerParams(vmem_limit_bytes=16 * 1024 * 1024),
    )


IN_VMEM = pl.BlockSpec(memory_space=pltpu.VMEM)
IN_HBM = pl.BlockSpec(memory_space=pltpu.HBM)


def shape(a, b, dtype=BF):
    return jax.ShapeDtypeStruct((a, b), dtype)


def lengths_of(meta, d):
    return [meta[j, d] for j in range(SLOTS)]


def moves_of(meta, d):
    return [meta[SLOTS + j, d] for j in range(SLOTS)]


def dp_at(meta):
    return meta[2 * SLOTS, 0]


def tensor_at(meta):
    return meta[2 * SLOTS, 1]


def kept_total(meta, d):
    return sum(a * (1 - b) for a, b in zip(lengths_of(meta, d), moves_of(meta, d)))


def picks(meta, moved, first, rows, home):
    d = dp_at(meta)
    at = lax.broadcasted_iota(jnp.int32, (rows, 1), 0) - first
    source = jnp.full((rows, 1), -1, jnp.int32)
    begin = jnp.int32(0)
    start = jnp.int32(0)
    for length, move in zip(lengths_of(meta, d), moves_of(meta, d)):
        size = length * (move if moved else 1 - move)
        inside = (at >= begin) & (at < begin + size)
        source = jnp.where(inside, at + (start - begin), source)
        begin = begin + size
        start = start + length
    columns = lax.broadcasted_iota(jnp.int32, (rows, home), 1)
    return jnp.where(columns == source, 1.0, 0.0).astype(BF)


def sent_first(meta):
    n = meta.shape[1]
    partner = lax.rem(dp_at(meta) + n // 2, n)
    return lax.rem(kept_total(meta, partner), TILE)


def early_picks(meta, home):
    return picks(meta, True, sent_first(meta), EARLY, home)


def late_picks(meta, home):
    return picks(meta, True, sent_first(meta) - EARLY, LATE, home)


def kept_picks(meta, home):
    return picks(meta, False, 0, KEEP, home)


def scaled_rows(meta, pick, cot, scale):
    width = cot.shape[1]
    rows = jnp.dot(pick, cot[...], preferred_element_type=F32)
    own = scale[pl.ds(pl.multiple_of(tensor_at(meta) * width, 128), width)]
    return (rows * own[None, :]).astype(BF)


def first_kernel(meta, cot_hbm, scale_hbm, pre_hbm, late_out, early_out, *rest):
    pre_outs, (cot, scale, pre, sems) = rest[:-4], rest[-4:]
    home = cot.shape[0]
    pairs = ((cot_hbm, cot), (scale_hbm, scale), (pre_hbm, pre))
    copies = [pltpu.make_async_copy(a, b, sems.at[i]) for i, (a, b) in enumerate(pairs)]
    for copy in copies:
        copy.start()
    early = early_picks(meta, home)
    late = late_picks(meta, home)
    copies[0].wait()
    copies[1].wait()
    early_out[...] = scaled_rows(meta, early, cot, scale)
    late_out[...] = scaled_rows(meta, late, cot, scale)
    copies[2].wait()
    at = 0
    for out in pre_outs:
        columns = slice(at, at + out.shape[1])
        out[...] = jnp.dot(early, pre[:, columns], preferred_element_type=F32).astype(BF)
        at = columns.stop


def rest_kernel(meta, cot_hbm, scale_hbm, rest_out, cot, scale, sems):
    home = cot.shape[0]
    pairs = ((cot_hbm, cot), (scale_hbm, scale))
    copies = [pltpu.make_async_copy(a, b, sems.at[i]) for i, (a, b) in enumerate(pairs)]
    for copy in copies:
        copy.start()
    early = early_picks(meta, home)
    kept = kept_picks(meta, home)
    for copy in copies:
        copy.wait()
    rest_out[0:EARLY, :] = scaled_rows(meta, early, cot, scale)
    rest_out[EARLY:, :] = scaled_rows(meta, kept, cot, scale)


def gelu_and_slope(x):
    cumulative = 0.5 * (1.0 + lax.erf(x * inv_root_two))
    return x * cumulative, cumulative + x * jnp.exp(-0.5 * x * x) * inv_root_tau


def gelu_kernel(base, block, meta, pre_hbm, act_out, der_out, pick, rows_f32, pre, sems):
    home = pre.shape[1]
    rows = pick.shape[0]
    blocks = act_out.shape[1] // block

    def fetch(i):
        columns = pl.ds(base + i * block, block)
        return pltpu.make_async_copy(pre_hbm.at[:, columns], pre.at[i], sems.at[i])

    for i in range(blocks):
        fetch(i).start()
    pick[0:LATE, :] = late_picks(meta, home)
    pick[LATE:SEND, :] = early_picks(meta, home)
    pick[SEND:, :] = kept_picks(meta, home)
    step = 3 * TILE
    for i in range(blocks):
        fetch(i).wait()
        rows_f32[...] = jnp.dot(pick[...], pre[i], preferred_element_type=F32)
        columns = slice(i * block, (i + 1) * block)

        def body(k, _):
            at = pl.ds(pl.multiple_of(k * step, step), step)
            value, slope = gelu_and_slope(rows_f32[at, :])
            act_out[at, columns] = value.astype(BF)
            der_out[at, columns] = slope
            return 0

        lax.fori_loop(0, rows // step, body, 0)


def assemble(meta, pieces, lhs):
    width = pieces[0].shape[1]
    for j, piece in enumerate(pieces):
        at = pl.ds(pl.multiple_of((tensor_at(meta) ^ j) * width, 128), width)
        lhs[:, at] = piece[...]


def grad_kernel(first_piece_row, first_row, block, meta, p0, p1, p2, p3, weight, der_a, der_b, out, lhs):
    rows = out.shape[0]
    assemble(meta, [p.at[pl.ds(first_piece_row, rows), :] for p in (p0, p1, p2, p3)], lhs)
    half = der_a.shape[1]
    for at in range(0, out.shape[1], block):
        columns = slice(at, at + block)
        der = der_a if at < half else der_b
        slope = der[first_row : first_row + rows, at % half : at % half + block]
        value = jnp.dot(lhs[...], weight[:, columns], preferred_element_type=F32)
        out[:, columns] = (value * slope).astype(BF)


def early_kernel(block, meta, p0, p1, p2, p3, weight, *rest):
    pres, (out, lhs, acc) = rest[:-3], rest[-3:]
    assemble(meta, (p0, p1, p2, p3), lhs)
    at = 0
    for pre in pres:
        for c in range(0, pre.shape[1], block):
            columns = slice(at + c, at + c + block)
            acc[...] = jnp.dot(lhs[...], weight[:, columns], preferred_element_type=F32)

            def body(k, _):
                rows = pl.ds(pl.multiple_of(k * TILE, TILE), TILE)
                _, slope = gelu_and_slope(pre[rows, c : c + block].astype(F32))
                out[rows, columns] = (acc[rows, :] * slope).astype(BF)
                return 0

            lax.fori_loop(0, EARLY // TILE, body, 0)
        at += pre.shape[1]


def weight_kernel(count, block, meta, *refs):
    pieces, (act, send, keep, lhs) = refs[: 2 * count], refs[2 * count :]
    half = pieces[0].shape[1] // 2
    mine = dp_at(meta) % 2 == 0
    for i in range(count):
        both = jnp.concatenate([pieces[2 * i][...], pieces[2 * i + 1][...]], axis=0).T
        lo, hi = both[:half], both[half:]
        lhs[i * half : (i + 1) * half, :] = jnp.where(mine, hi, lo)
        lhs[(count + i) * half : (count + i + 1) * half, :] = jnp.where(mine, lo, hi)
    for at in range(0, act.shape[1], block):
        columns = slice(at, at + block)
        value = jnp.dot(lhs[...], act[:, columns], preferred_element_type=F32)
        send[:, columns] = value[: count * half].astype(BF)
        keep[:, columns] = value[count * half :]


def near_kernel(count, meta, *refs):
    keeps, gots, (out, mine) = refs[:count], refs[count : 2 * count], refs[2 * count :]
    half = out.shape[0] // 2
    parts = [(k, g, at) for k, g in zip(keeps, gots) for at in range(0, k.shape[0], half)]
    keeps_even = (dp_at(meta) // 2 + tensor_at(meta)) % 2 == 0
    step = 2 * TILE

    for pair in range(2):
        (k0, g0, a0), (k1, g1, a1) = parts[2 * pair], parts[2 * pair + 1]

        def body(i, _):
            def rows(at):
                return pl.ds(pl.multiple_of(at + i * step, TILE), step)

            even = k0[rows(a0), :] + g0[rows(a0), :].astype(F32)
            odd = k1[rows(a1), :] + g1[rows(a1), :].astype(F32)
            out[rows(pair * half), :] = jnp.where(keeps_even, odd, even).astype(BF)
            mine[rows(pair * half), :] = jnp.where(keeps_even, even, odd)
            return 0

        lax.fori_loop(0, half // step, body, 0)


def far_kernel(meta, held, got, out, mine):
    half = out.shape[0]
    keeps_first = (dp_at(meta) // 4 + tensor_at(meta) // 2) % 2 == 0
    step = 2 * TILE

    def body(i, _):
        first = pl.ds(pl.multiple_of(i * step, TILE), step)
        second = pl.ds(pl.multiple_of(half + i * step, TILE), step)
        a = held[first, :] + got[first, :].astype(F32)
        b = held[second, :] + got[second, :].astype(F32)
        out[first, :] = jnp.where(keeps_first, b, a).astype(BF)
        mine[first, :] = jnp.where(keeps_first, a, b)
        return 0

    lax.fori_loop(0, half // step, body, 0)


def place_kernel(meta, kept, early, late, out):
    count = kept_total(meta, dp_at(meta))
    first = jnp.minimum(count - lax.rem(count, TILE), BAL - SEND)
    first = pl.multiple_of(first, TILE)
    out[0:KEEP, :] = kept[...]
    out[KEEP:, :] = jnp.zeros((out.shape[0] - KEEP, out.shape[1]), BF)
    for block, at in ((early, first), (late, pl.multiple_of(first + EARLY, TILE))):
        rows = lax.broadcasted_iota(jnp.int32, (block.shape[0], 1), 0) + at
        window = pl.ds(at, block.shape[0])
        out[window, :] = jnp.where(rows < count, out[window, :], block[...])


def swapped(block, axis, distance):
    n = lax.axis_size(axis)
    return lax.ppermute(block, axis, [(i, i ^ distance) for i in range(n)])


def after(value, *others):
    return lax.optimization_barrier((value, *others))[0]


def shards(hidden_pre, cotangent, down_weight, layer_scale, crop_lengths, crop_moves):
    home, ff = hidden_pre.shape
    width = cotangent.shape[1]
    features = down_weight.shape[0]
    half, wide = width // 2, ff // 2
    rows = SEND + KEEP
    n = lax.axis_size("dp")
    d = lax.axis_index("dp").astype(jnp.int32)
    t = lax.axis_index("tensor").astype(jnp.int32)
    column = lax.broadcasted_iota(jnp.int32, (1, n), 1)
    own = jnp.where(column == 0, d, jnp.where(column == 1, t, 0))
    meta = jnp.concatenate([crop_lengths.T, crop_moves.T, own])
    vmem = pltpu.VMEM
    hidden_pre, cotangent, layer_scale = (
        pltpu.with_memory_space_constraint(x, pltpu.HBM) for x in (hidden_pre, cotangent, layer_scale)
    )
    sems = pltpu.SemaphoreType.DMA

    cuts = (256, 768, ff - 1024)
    late, early, *pres = kernel_call(
        first_kernel,
        [shape(LATE, width), shape(EARLY, width)] + [shape(EARLY, c) for c in cuts],
        [IN_HBM] * 3, [IN_VMEM] * 5,
        [vmem((home, width), BF), vmem((features,), F32), vmem((home, ff), BF), sems((3,))],
    )(meta, cotangent, layer_scale, hidden_pre)
    arrived_early = swapped(early, "dp", n // 2)
    arrived_pres = [swapped(pre, "dp", n // 2) for pre in pres]

    rest = kernel_call(
        rest_kernel, shape(EARLY + KEEP, width), [IN_HBM] * 2, IN_VMEM,
        [vmem((home, width), BF), vmem((features,), F32), sems((2,))],
    )(after(meta, late), cotangent, layer_scale)

    def gelu(meta, base):
        block = 256
        return kernel_call(
            functools.partial(gelu_kernel, base, block),
            [shape(rows, wide), shape(rows, wide, F32)],
            [IN_HBM], [IN_VMEM] * 2,
            [vmem((rows, home), BF), vmem((rows, block), F32), vmem((wide // block, home, block), BF),
             sems((wide // block,))],
        )(meta, hidden_pre)

    def weight_part(meta, pieces, act):
        count = len(pieces)
        return kernel_call(
            functools.partial(weight_kernel, count, 256),
            [shape(count * half, wide), shape(count * half, wide, F32)],
            [IN_VMEM] * (2 * count + 1), [IN_VMEM] * 2,
            [vmem((count * width, rows), BF)],
        )(meta, *[lates[j] if k == 0 else rests[j] for j in pieces for k in range(2)], act)

    def grads(meta, pieces, first_piece_row, first_row, count):
        return kernel_call(
            functools.partial(grad_kernel, first_piece_row, first_row, 256),
            shape(count, ff), [IN_VMEM] * 7, IN_VMEM, [vmem((count, features), BF)],
        )(meta, *pieces, down_weight, der_a, der_b)

    act_a, der_a = gelu(after(meta, rest), 0)
    late_c, late_y = swapped(late, "tensor", 1), swapped(late, "tensor", 2)
    late_y = after(late_y, act_a, late_c, arrived_early, arrived_pres[0])
    late_yc = swapped(late_y, "tensor", 1)
    lates, rests = (late,), (rest,)
    send_0, keep_0 = weight_part(after(meta, late_y), (0,), act_a)
    got_0 = swapped(send_0, "dp", 1)

    rest_sent = after(rest, late_y)
    rest_c, rest_y = swapped(rest_sent, "tensor", 1), swapped(rest_sent, "tensor", 2)
    act_b, der_b = gelu(after(meta, send_0), wide)
    lates, rests = (late, late_c, late_y, late_yc), (rest, rest_c)
    send_1, keep_1 = weight_part(after(meta, act_b, got_0, arrived_pres[1]), (1,), act_a)
    got_1 = swapped(send_1, "dp", 1)

    rest_y = after(rest_y, send_1)
    rest_yc = swapped(rest_y, "tensor", 1)
    rests = (rest, rest_c, rest_y, rest_yc)
    early_sent = after(arrived_early, rest_y)
    early_c, early_y = swapped(early_sent, "tensor", 1), swapped(early_sent, "tensor", 2)
    moving = grads(after(meta, rest_y), lates, 0, 0, LATE)
    arrived = swapped(moving, "dp", n // 2)

    early_y = after(early_y, moving, early_c)
    early_yc = swapped(early_y, "tensor", 1)
    send_23, keep_23 = weight_part(after(meta, early_y, arrived_pres[2], got_1), (2, 3), act_a)
    got_23 = swapped(send_23, "dp", 1)
    send_b, keep_b = weight_part(after(meta, send_23), (0, 1, 2, 3), act_b)
    kept_grad = grads(after(meta, send_b), rests, EARLY, SEND, KEEP)

    def near_step(meta, keeps, gots):
        count = len(keeps)
        return kernel_call(
            functools.partial(near_kernel, count),
            [shape(width, wide), shape(width, wide, F32)], [IN_VMEM] * (2 * count), [IN_VMEM] * 2,
        )(meta, *keeps, *gots)

    def far_step(meta, mine, got):
        return kernel_call(
            far_kernel, [shape(half, wide), shape(half, wide, F32)], [IN_VMEM] * 2, [IN_VMEM] * 2
        )(meta, mine, got)

    out_na, mine_a = near_step(after(meta, kept_grad), (keep_0, keep_1, keep_23), (got_0, got_1, got_23))
    got_na = swapped(out_na, "dp", 2)
    got_b = swapped(after(send_b, out_na), "dp", 1)

    early_grad = kernel_call(
        functools.partial(early_kernel, 256), shape(EARLY, ff), [IN_VMEM] * (5 + len(cuts)), IN_VMEM,
        [vmem((EARLY, features), BF), vmem((EARLY, 256), F32)],
    )(after(meta, out_na), arrived_early, early_c, early_y, early_yc, down_weight, *arrived_pres)

    out_fa, own_a = far_step(after(meta, arrived, early_grad), mine_a, got_na)
    got_fa = swapped(out_fa, "dp", 4)
    out_nb, mine_b = near_step(after(meta, out_fa), (keep_b,), (got_b,))
    got_nb = swapped(out_nb, "dp", 2)
    out_fb, own_b = far_step(meta, mine_b, got_nb)
    got_fb = swapped(out_fb, "dp", 4)
    total = jnp.concatenate([own_a + got_fa.astype(F32), own_b + got_fb.astype(F32)], axis=1)
    down_grad = total / math.sqrt(n * home)

    def columns(rows):
        return pl.BlockSpec((rows, 512), lambda i, *_: (0, i))

    hidden_grad = kernel_call(
        place_kernel, shape(BAL, ff), [columns(KEEP), columns(EARLY), columns(LATE)], columns(BAL),
        grid=(ff // 512,),
    )(meta, kept_grad, early_grad, arrived)
    return (hidden_grad, down_grad)


def solution(mesh):
    pairs_and_fours = (mesh.shape["dp"], mesh.shape["tensor"]) == (8, 4)
    return jax.shard_map(
        shards if pairs_and_fours else general_shards,
        mesh=mesh,
        in_specs=(P("dp", "tensor"), P("dp", "tensor"), P(None, "tensor"), P(), P(), P()),
        out_specs=(P("dp", "tensor"), P("dp", "tensor")),
        check_vma=False,
    )


def shifted(block, axis, distance):
    devices = range(lax.axis_size(axis))
    route = [((i - distance) % len(devices), i) for i in devices]
    return lax.ppermute(block, axis, route)


def crop_rows(row_total, crop_sizes, crop_starts):
    crop_ends = jnp.cumsum(crop_sizes)
    crop_begins = crop_ends - crop_sizes
    target_rows = jnp.arange(row_total, dtype=jnp.int32)[:, None]
    inside_crop = (target_rows >= crop_begins[None, :]) & (target_rows < crop_ends[None, :])
    source_rows = jnp.sum(
        jnp.where(inside_crop, crop_starts[None, :] + target_rows - crop_begins[None, :], 0), axis=1
    )
    return (source_rows, jnp.any(inside_crop, axis=1))


def select_rows(row_block, source_rows, valid_rows):
    taken = jnp.take(row_block, source_rows, axis=0)
    return jnp.where(valid_rows[:, None], taken, jnp.zeros((), row_block.dtype))


def gelu_parts(pre_act):
    cumulative = 0.5 * (1.0 + jax.scipy.special.erf(pre_act * inv_root_two))
    activated = pre_act * cumulative
    derivative = cumulative + pre_act * jnp.exp(-0.5 * pre_act * pre_act) * inv_root_tau
    return (activated, derivative)


def local_grads(pre_rows, cot_part, live_rows, layer_scale, down_weight, home_rows):
    cot_full = lax.all_gather(cot_part, "tensor", axis=1, tiled=True)
    scaled = (cot_full.astype(F32) * layer_scale[None, :]).astype(BF)
    activated, derivative = gelu_parts(pre_rows.astype(F32))
    activation = jnp.where(live_rows[:, None], activated, 0.0).astype(BF)
    backward = jnp.dot(scaled, down_weight, preferred_element_type=F32) * derivative
    gradient_rows = jnp.where(live_rows[:, None], backward, 0.0).astype(BF)
    weight_grad = lax.psum_scatter(
        lax.dot_general(scaled, activation, (((0,), (0,)), ((), ())), preferred_element_type=F32),
        "dp",
        scatter_dimension=0,
        tiled=True,
    )
    return (gradient_rows, weight_grad / math.sqrt(lax.axis_size("dp") * home_rows))


def general_shards(hidden_pre, cotangent, down_weight, layer_scale, crop_lengths, crop_moves):
    devices = lax.axis_size("dp")
    half_axis = devices // 2
    device_index = lax.axis_index("dp")
    partner_index = (device_index + half_axis) % devices
    own_lengths = lax.dynamic_index_in_dim(crop_lengths, device_index, 0, keepdims=False)
    own_moves = lax.dynamic_index_in_dim(crop_moves, device_index, 0, keepdims=False)
    partner_lengths = lax.dynamic_index_in_dim(crop_lengths, partner_index, 0, keepdims=False)
    partner_moves = lax.dynamic_index_in_dim(crop_moves, partner_index, 0, keepdims=False)
    home_rows = hidden_pre.shape[0]
    own_starts = jnp.cumsum(own_lengths) - own_lengths
    sent_sizes = own_lengths * own_moves
    kept_sizes = own_lengths * (1 - own_moves)
    arrived = jnp.sum(partner_lengths * partner_moves)
    send_source, send_valid = crop_rows(SEND, sent_sizes, own_starts)
    keep_sizes = jnp.concatenate([kept_sizes, arrived[None]])
    keep_starts = jnp.concatenate([own_starts, jnp.full((1,), home_rows, jnp.int32)])
    keep_source, keep_valid = crop_rows(BAL, keep_sizes, keep_starts)
    live_home = jnp.arange(home_rows, dtype=jnp.int32) < jnp.sum(own_lengths)
    gradient_rows, weight_grad = local_grads(
        hidden_pre, cotangent, live_home, layer_scale, down_weight, home_rows
    )
    outgoing = select_rows(gradient_rows, send_source, send_valid)
    incoming = shifted(outgoing, "dp", half_axis)
    balanced = select_rows(jnp.concatenate([gradient_rows, incoming], 0), keep_source, keep_valid)
    return (balanced, weight_grad)
```

time: 293 us -> 148 us (0.51)
  waiting for transfers between devices: 226 us -> 75.6 us
  Pallas kernels: 0 us -> 49 us
  matrix products: 22.1 us -> 0 us
  starting transfers between devices: 2.52 us -> 20.5 us
  other arithmetic: 15.5 us -> 1.98 us
  between operations: 14.1 us -> 0.86 us
  local copies, waits for them, and re-layouts: 12 us -> 0.01 us
    reduce_scatter x1 -> x0, waiting for transfers between devices: 60.4 us -> none  [local_grads(): lax.psum_scatter(lax.dot_general(scaled, activation, (((0,), (0,)), ((),...]
    ppermute x1 -> x22, waiting for transfers between devices: 134 us -> 75.6 us  [swapped(): return lax.ppermute(block, axis, [(i, i ^ distance) for i in range(n)])]
    pallas_call x0 -> x16, Pallas kernels: none -> 49 us  [the longest x2 15.6 us: gelu(): kernel_call(functools.partial(gelu_kernel, base, block), [shape(rows, wid...]
    all_gather x1 -> x0, waiting for transfers between devices: 30.8 us -> none  [local_grads(): cot_full = lax.all_gather(cot_part, 'tensor', axis=1, tiled=True)]
    dot_general x2 -> x0, matrix products: 22.1 us -> none  [the longest x1 12.3 us: local_grads(): lax.dot_general(scaled, activation, (((0,), (0,)), ((), ())), preferred_e...]
    ppermute x1 -> x22, starting transfers between devices: 2.44 us -> 20.5 us  [swapped(): return lax.ppermute(block, axis, [(i, i ^ distance) for i in range(n)])]
    gather x2 -> x0, local copies, waits for them, and re-layouts: 11.9 us -> none  [select_rows(): taken = jnp.take(row_block, source_rows, axis=0)]
    select_n x4 -> x1, other arithmetic: 4.56 us -> 0.01 us  [shards(): own = jnp.where(column == 0, d, jnp.where(column == 1, t, 0))]
  transfers between devices with their start and end apart: 3 -> 22, of which waited for: 3 -> 9; matrix products, arithmetic and copies ran while one was open for 12% -> 0% of each run, Pallas kernels for 0% -> 28%
where the time goes in v3:
time: 148 us
  waiting for transfers between devices  75.6 us (51%)
  Pallas kernels  49 us (33%)
  starting transfers between devices  20.5 us (14%)
  other arithmetic  1.98 us (1%)
    ppermute x22, waiting for transfers between devices, swapped(): return lax.ppermute(block, axis, [(i, i ^ distance) for i in range(n)])  75.6 us
    ppermute x22, starting transfers between devices, swapped(): return lax.ppermute(block, axis, [(i, i ^ distance) for i in range(n)])  20.5 us
    pallas_call x2, Pallas kernels, gelu(): kernel_call(functools.partial(gelu_kernel, base, block), [shape(rows, wid...  15.6 us
    pallas_call x4, Pallas kernels, weight_part(): kernel_call(functools.partial(weight_kernel, count, 256), [shape(count *...  10.1 us
    pallas_call x2, Pallas kernels, grads(): kernel_call(functools.partial(grad_kernel, first_piece_row, first_row, 25...  6.29 us
    pallas_call x1, Pallas kernels, shards(): kernel_call(functools.partial(early_kernel, 256), shape(EARLY, ff), [IN_V...  3.63 us
    pallas_call x1, Pallas kernels, shards(): kernel_call(first_kernel, [shape(LATE, width), shape(EARLY, width)] + [sh...  3.55 us
    pallas_call x1, Pallas kernels, shards(): kernel_call(rest_kernel, shape(EARLY + KEEP, width), [IN_HBM] * 2, IN_VME...  3.17 us
  transfers between devices with their start and end apart: 22, of which 9 were waited for; matrix products, arithmetic and copies ran while one was open for 0% of the time, Pallas kernels for 28%

profile of v3, /device:TPU:0, one launch (start us, length us, event | category | flops | bytes accessed | tf_op | source)
XLA Modules:
  0.0 147.9 jit_solution(4303850875310596383)
XLA Ops:
  1.4 3.5 %shard_map.77 = (bf16[400,384]{1,0:T(8,128)(2,1)S(1)}, bf16[128,384]{1,0:T(8,128)(2,1)S(1)}, bf16[128,256]{1,0:T(8,128)(2,1)S(1)}, bf16[128,768]{1,0:T(8,128)(2,1)S(1)}, bf16[128,512]{1,0:T(8,128)(2,1)S(1)}) custom-call(s32[9,8]{1,0:T(8,128)S(1)} %pad_add_fusion.meta, bf16[1032,384]{1,0:T(8,128)(2,1)} %cot_hbm.3, f32[1536]{0:T(1024)} %scale_hbm.3, ...), custom_call_target="tpu_custom_call" | custom-call | flops 1 | bytes 1 | tf_op jit(solution)/shard_map/pallas_call | solution.py:314
  5.4 2.6 %collective-permute-start.1 = (bf16[400,384]{1,0:T(8,128)(2,1)S(1)}, bf16[400,384]{1,0:T(8,128)(2,1)S(1)}, u32[]{:S(2)}, u32[]{:S(2)}) collective-permute-start(bf16[400,384]{1,0:T(8,128)(2,1)S(1)} %get-tuple-element.47.refs_0_.p0), channel_id=1, source_target_pairs={{0,2},{1,3},{2,0},{3,1},{4,6},{5,7},{6,4},{7,5},{8,10},{9,11},{10,... | collective-permute-start | bytes 921608 | tf_op jit(solution)/shard_map/ppermute | solution.py:288
  8.0 2.6 %collective-permute-start = (bf16[128,384]{1,0:T(8,128)(2,1)S(1)}, bf16[128,384]{1,0:T(8,128)(2,1)S(1)}, u32[]{:S(2)}, u32[]{:S(2)}) collective-permute-start(bf16[128,384]{1,0:T(8,128)(2,1)S(1)} %get-tuple-element.46), channel_id=1, source_target_pairs={{0,16},{4,20},{8,24},{12,28},{16,0},{20,4},{24,8},{28,12},{1,17},{... | collective-permute-start | bytes 294920 | tf_op jit(solution)/shard_map/ppermute | solution.py:288
  11.0 3.2 %shard_map.78.refs_1_.p0 = bf16[656,384]{1,0:T(8,128)(2,1)S(1)} custom-call(s32[9,8]{1,0:T(8,128)S(1)} %pad_add_fusion.meta, bf16[1032,384]{1,0:T(8,128)(2,1)} %cot_hbm.3, f32[1536]{0:T(1024)} %scale_hbm.3), custom_call_target="tpu_custom_call" | custom-call | flops 1 | bytes 1 | tf_op jit(solution)/shard_map/pallas_call | solution.py:323
  14.1 7.7 %shard_map.79 = (bf16[1056,768]{1,0:T(8,128)(2,1)S(1)}, f32[1056,768]{1,0:T(8,128)S(1)}) custom-call(s32[9,8]{1,0:T(8,128)S(1)} %pad_add_fusion.meta, bf16[1032,1536]{1,0:T(8,128)(2,1)} %pre_hbm.5), custom_call_target="tpu_custom_call" | custom-call | flops 1 | bytes 1 | tf_op jit(solution)/shard_map/pallas_call | solution.py:330
  22.2 1.7 %shard_map.80 = (bf16[192,768]{1,0:T(8,128)(2,1)S(1)}, f32[192,768]{1,0:T(8,128)S(1)}) custom-call(s32[9,8]{1,0:T(8,128)S(1)} %pad_add_fusion.meta, bf16[400,384]{1,0:T(8,128)(2,1)S(1)} %get-tuple-element.47.refs_0_.p0, bf16[656,384]{1,0:T(8,128)(2,1)S(1)} %shard_map.78.refs_1_.p0, bf16[1056,768]{1,0:T(8,128)(2,1)S(1)} %get-tuple-element.50.refs_2_.refs_4_), custom_call_target="tpu_custom_call" | custom-call | flops 1 | bytes 1 | tf_op jit(solution)/shard_map/pallas_call | solution.py:340
  23.9 1.9 %collective-permute-start.5 = (bf16[192,768]{1,0:T(8,128)(2,1)S(1)}, bf16[192,768]{1,0:T(8,128)(2,1)S(1)}, u32[]{:S(2)}, u32[]{:S(2)}) collective-permute-start(bf16[192,768]{1,0:T(8,128)(2,1)S(1)} %get-tuple-element.55), channel_id=1, source_target_pairs={{0,4},{4,0},{8,12},{12,8},{16,20},{20,16},{24,28},{28,24},{1,5},{5... | collective-permute-start | bytes 884744 | tf_op jit(solution)/shard_map/ppermute | solution.py:288
  25.8 2.6 %collective-permute-start.6 = (bf16[128,768]{1,0:T(8,128)(2,1)S(1)}, bf16[128,768]{1,0:T(8,128)(2,1)S(1)}, u32[]{:S(2)}, u32[]{:S(2)}) collective-permute-start(bf16[128,768]{1,0:T(8,128)(2,1)S(1)} %get-tuple-element.58), channel_id=1, source_target_pairs={{0,16},{4,20},{8,24},{12,28},{16,0},{20,4},{24,8},{28,12},{1,17},{... | collective-permute-start | bytes 589832 | tf_op jit(solution)/shard_map/ppermute | solution.py:288
  28.4 7.9 %shard_map.81 = (bf16[1056,768]{1,0:T(8,128)(2,1)S(1)}, f32[1056,768]{1,0:T(8,128)S(1)}) custom-call(s32[9,8]{1,0:T(8,128)S(1)} %pad_add_fusion.meta, bf16[1032,1536]{1,0:T(8,128)(2,1)} %pre_hbm.5), custom_call_target="tpu_custom_call" | custom-call | flops 1 | bytes 1 | tf_op jit(solution)/shard_map/pallas_call | solution.py:330
  37.6 1.7 %shard_map.82 = (bf16[192,768]{1,0:T(8,128)(2,1)S(1)}, f32[192,768]{1,0:T(8,128)S(1)}) custom-call(s32[9,8]{1,0:T(8,128)S(1)} %pad_add_fusion.meta, bf16[400,384]{1,0:T(8,128)(2,1)S(1)} %collective-permute-done.2.refs_0_.p1.refs_2_, bf16[656,384]{1,0:T(8,128)(2,1)S(1)} %collective-permute-done.7.refs_1_.refs_3_.p1, ...), custom_call_target="tpu_custom_call" | custom-call | flops 1 | bytes 1 | tf_op jit(solution)/shard_map/pallas_call | solution.py:340
  43.3 2.8 %shard_map.83 = bf16[400,1536]{1,0:T(8,128)(2,1)S(1)} custom-call(s32[9,8]{1,0:T(8,128)S(1)} %pad_add_fusion.meta, bf16[400,384]{1,0:T(8,128)(2,1)S(1)} %get-tuple-element.47.refs_0_.p0, bf16[400,384]{1,0:T(8,128)(2,1)S(1)} %collective-permute-done.2.refs_0_.p1.refs_2_, bf16[400,384]{1,0:T(8,128)(2,1)S(1)} %collective-permute-done.1.p2.refs_0_.refs_4_, ...), custom_call_target="tpu_custom_call" | custom-call | flops 1 | bytes 1 | tf_op jit(solution)/shard_map/pallas_call | solution.py:348
  46.6 2.7 %collective-permute-done.11.rest_2_ = bf16[128,512]{1,0:T(8,128)(2,1)S(1)} collective-permute-done((bf16[128,512]{1,0:T(8,128)(2,1)S(1)}, bf16[128,512]{1,0:T(8,128)(2,1)S(1)}, u32[]{:S(2)}, u32[]{:S(2)}) %collective-permute-start.11) | collective-permute-done | bytes 131104 | tf_op jit(solution)/shard_map/ppermute | solution.py:288
  49.3 2.5 %shard_map.84 = (bf16[384,768]{1,0:T(8,128)(2,1)S(1)}, f32[384,768]{1,0:T(8,128)S(1)}) custom-call(s32[9,8]{1,0:T(8,128)S(1)} %pad_add_fusion.meta, bf16[400,384]{1,0:T(8,128)(2,1)S(1)} %collective-permute-done.1.p2.refs_0_.refs_4_, bf16[656,384]{1,0:T(8,128)(2,1)S(1)} %collective-permute-done.4.refs_1_.refs_5_.p2, ...), custom_call_target="tpu_custom_call" | custom-call | flops 1 | bytes 1 | tf_op jit(solution)/shard_map/pallas_call | solution.py:340
  51.8 1.6 %collective-permute-start.14 = (bf16[384,768]{1,0:T(8,128)(2,1)S(1)}, bf16[384,768]{1,0:T(8,128)(2,1)S(1)}, u32[]{:S(2)}, u32[]{:S(2)}) collective-permute-start(bf16[384,768]{1,0:T(8,128)(2,1)S(1)} %get-tuple-element.69), channel_id=1, source_target_pairs={{0,4},{4,0},{8,12},{12,8},{16,20},{20,16},{24,28},{28,24},{1,5},{5... | collective-permute-start | bytes 1769480 | tf_op jit(solution)/shard_map/ppermute | solution.py:288
  53.5 4.2 %shard_map.85 = (bf16[768,768]{1,0:T(8,128)(2,1)S(1)}, f32[768,768]{1,0:T(8,128)S(1)}) custom-call(s32[9,8]{1,0:T(8,128)S(1)} %pad_add_fusion.meta, bf16[400,384]{1,0:T(8,128)(2,1)S(1)} %get-tuple-element.47.refs_0_.p0, bf16[656,384]{1,0:T(8,128)(2,1)S(1)} %shard_map.78.refs_1_.p0, bf16[400,384]{1,0:T(8,128)(2,1)S(1)} %collective-permute-done.2.refs_0_.p1.refs_2_, ...), custom_call_target="tpu_custom_call" | custom-call | flops 1 | bytes 1 | tf_op jit(solution)/shard_map/pallas_call | solution.py:340
  57.7 3.5 %shard_map.86.kept = bf16[528,1536]{1,0:T(8,128)(2,1)S(1)} custom-call(s32[9,8]{1,0:T(8,128)S(1)} %pad_add_fusion.meta, bf16[656,384]{1,0:T(8,128)(2,1)S(1)} %shard_map.78.refs_1_.p0, bf16[656,384]{1,0:T(8,128)(2,1)S(1)} %collective-permute-done.7.refs_1_.refs_3_.p1, bf16[656,384]{1,0:T(8,128)(2,1)S(1)} %collective-permute-done.4.refs_1_.refs_5_.p2, ...), custom_call_target="tpu_custom_call" | custom-call | flops 1 | bytes 1 | tf_op jit(solution)/shard_map/pallas_call | solution.py:348
  61.1 5.1 %collective-permute-done.14.refs_5_ = bf16[384,768]{1,0:T(8,128)(2,1)S(1)} collective-permute-done((bf16[384,768]{1,0:T(8,128)(2,1)S(1)}, bf16[384,768]{1,0:T(8,128)(2,1)S(1)}, u32[]{:S(2)}, u32[]{:S(2)}) %collective-permute-start.14) | collective-permute-done | bytes 589856 | tf_op jit(solution)/shard_map/ppermute | solution.py:288
  67.3 1.7 %collective-permute-start.19 = (bf16[768,768]{1,0:T(8,128)(2,1)S(1)}, bf16[768,768]{1,0:T(8,128)(2,1)S(1)}, u32[]{:S(2)}, u32[]{:S(2)}) collective-permute-start(bf16[768,768]{1,0:T(8,128)(2,1)S(1)} %get-tuple-element.85), channel_id=1, source_target_pairs={{0,4},{4,0},{8,12},{12,8},{16,20},{20,16},{24,28},{28,24},{1,5},{5... | collective-permute-start | bytes 3538952 | tf_op jit(solution)/shard_map/ppermute | solution.py:288
  71.2 3.6 %shard_map.88.early = bf16[128,1536]{1,0:T(8,128)(2,1)S(1)} custom-call(s32[9,8]{1,0:T(8,128)S(1)} %pad_add_fusion.meta, bf16[128,384]{1,0:T(8,128)(2,1)S(1)} %collective-permute-done.p0, bf16[128,384]{1,0:T(8,128)(2,1)S(1)} %collective-permute-done.10.p1, bf16[128,384]{1,0:T(8,128)(2,1)S(1)} %collective-permute-done.8.p2, ...), custom_call_target="tpu_custom_call" | custom-call | flops 1 | bytes 1 | tf_op jit(solution)/shard_map/pallas_call | solution.py:399
  74.8 33.7 %collective-permute-done.16.late = bf16[400,1536]{1,0:T(8,128)(2,1)S(1)} collective-permute-done((bf16[400,1536]{1,0:T(8,128)(2,1)S(1)}, bf16[400,1536]{1,0:T(8,128)(2,1)S(1)}, u32[]{:S(2)}, u32[]{:S(2)}) %collective-permute-start.16) | collective-permute-done | bytes 1228832 | tf_op jit(solution)/shard_map/ppermute | solution.py:288
  110.5 2.7 %collective-permute-start.18 = (bf16[192,768]{1,0:T(8,128)(2,1)S(1)}, bf16[192,768]{1,0:T(8,128)(2,1)S(1)}, u32[]{:S(2)}, u32[]{:S(2)}) collective-permute-start(bf16[192,768]{1,0:T(8,128)(2,1)S(1)} %get-tuple-element.82), channel_id=1, source_target_pairs={{0,16},{4,20},{8,24},{12,28},{16,0},{20,4},{24,8},{28,12},{1,17},{... | collective-permute-start | bytes 884744 | tf_op jit(solution)/shard_map/ppermute | solution.py:288
  113.2 18.4 %collective-permute-done.20.got = bf16[384,768]{1,0:T(8,128)(2,1)S(1)} collective-permute-done((bf16[384,768]{1,0:T(8,128)(2,1)S(1)}, bf16[384,768]{1,0:T(8,128)(2,1)S(1)}, u32[]{:S(2)}, u32[]{:S(2)}) %collective-permute-start.20) | collective-permute-done | bytes 589856 | tf_op jit(solution)/shard_map/ppermute | solution.py:288
  132.6 2.8 %shard_map.89 = bf16[720,1536]{1,0:T(8,128)(2,1)} custom-call(s32[9,8]{1,0:T(8,128)S(1)} %pad_add_fusion.meta, bf16[528,1536]{1,0:T(8,128)(2,1)S(1)} %shard_map.86.kept, bf16[128,1536]{1,0:T(8,128)(2,1)S(1)} %shard_map.88.early, bf16[400,1536]{1,0:T(8,128)(2,1)S(1)} %collective-permute-done.16.late), custom_call_target="tpu_custom_call" | custom-call | flops 1 | bytes 1 | tf_op jit(solution)/shard_map/pallas_call | solution.py:416
  135.5 11.2 %collective-permute-done.21 = bf16[192,768]{1,0:T(8,128)(2,1)S(1)} collective-permute-done((bf16[192,768]{1,0:T(8,128)(2,1)S(1)}, bf16[192,768]{1,0:T(8,128)(2,1)S(1)}, u32[]{:S(2)}, u32[]{:S(2)}) %collective-permute-start.21) | collective-permute-done | bytes 294944 | tf_op jit(solution)/shard_map/ppermute | solution.py:288
  (46 shorter events, 15.1 us)
Async XLA Ops:
  4.9 17.0 %collective-permute-start.2 = (bf16[400,384]{1,0:T(8,128)(2,1)S(1)}, bf16[400,384]{1,0:T(8,128)(2,1)S(1)}, u32[]{:S(2)}, u32[]{:S(2)}) collective-permute-start(bf16[400,384]{1,0:T(8,128)(2,1)S(1)} %get-tuple-element.47.refs_0_.p0), channel_id=1, source_target_pairs={{0,1},{1,0},{2,3},{3,2},{4,5},{5,4},{6,7},{7,6},{8,9},{9,8},{10,11... | collective-permute-start | bytes 921608 | tf_op jit(solution)/shard_map/ppermute | solution.py:288
  5.4 16.4 %collective-permute-start.1 = (bf16[400,384]{1,0:T(8,128)(2,1)S(1)}, bf16[400,384]{1,0:T(8,128)(2,1)S(1)}, u32[]{:S(2)}, u32[]{:S(2)}) collective-permute-start(bf16[400,384]{1,0:T(8,128)(2,1)S(1)} %get-tuple-element.47.refs_0_.p0), channel_id=1, source_target_pairs={{0,2},{1,3},{2,0},{3,1},{4,6},{5,7},{6,4},{7,5},{8,10},{9,11},{10,... | collective-permute-start | bytes 921608 | tf_op jit(solution)/shard_map/ppermute | solution.py:288
  8.0 13.8 %collective-permute-start = (bf16[128,384]{1,0:T(8,128)(2,1)S(1)}, bf16[128,384]{1,0:T(8,128)(2,1)S(1)}, u32[]{:S(2)}, u32[]{:S(2)}) collective-permute-start(bf16[128,384]{1,0:T(8,128)(2,1)S(1)} %get-tuple-element.46), channel_id=1, source_target_pairs={{0,16},{4,20},{8,24},{12,28},{16,0},{20,4},{24,8},{28,12},{1,17},{... | collective-permute-start | bytes 294920 | tf_op jit(solution)/shard_map/ppermute | solution.py:288
  10.6 11.2 %collective-permute-start.3 = (bf16[128,256]{1,0:T(8,128)(2,1)S(1)}, bf16[128,256]{1,0:T(8,128)(2,1)S(1)}, u32[]{:S(2)}, u32[]{:S(2)}) collective-permute-start(bf16[128,256]{1,0:T(8,128)(2,1)S(1)} %get-tuple-element.51), channel_id=1, source_target_pairs={{0,16},{4,20},{8,24},{12,28},{16,0},{20,4},{24,8},{28,12},{1,17},{... | collective-permute-start | bytes 196616 | tf_op jit(solution)/shard_map/ppermute | solution.py:288
  10.9 32.3 %slice-start = ((s8[4718592]{0:T(1024)(128)(4,1)}), s8[4194304]{0:T(1024)(128)(4,1)S(1)}, s32[]{:S(2)}) async-start(s8[4718592]{0:T(1024)(128)(4,1)} %bitcast.2), calls=%async_computation | async-start | bytes 8388608
  21.9 21.4 %slice-start.1 = ((s8[4718592]{0:T(1024)(128)(4,1)}), s8[524288]{0:T(1024)(128)(4,1)S(1)}, s32[]{:S(2)}) async-start(s8[4718592]{0:T(1024)(128)(4,1)} %bitcast.2), calls=%async_computation.1 | async-start | bytes 1048576
  21.9 15.7 %collective-permute-start.7 = (bf16[656,384]{1,0:T(8,128)(2,1)S(1)}, bf16[656,384]{1,0:T(8,128)(2,1)S(1)}, u32[]{:S(2)}, u32[]{:S(2)}) collective-permute-start(bf16[656,384]{1,0:T(8,128)(2,1)S(1)} %shard_map.78.refs_1_.p0), channel_id=1, source_target_pairs={{0,1},{1,0},{2,3},{3,2},{4,5},{5,4},{6,7},{7,6},{8,9},{9,8},{10,11... | collective-permute-start | bytes 1511432 | tf_op jit(solution)/shard_map/ppermute | solution.py:288
  22.0 17.4 %collective-permute-start.4 = (bf16[656,384]{1,0:T(8,128)(2,1)S(1)}, bf16[656,384]{1,0:T(8,128)(2,1)S(1)}, u32[]{:S(2)}, u32[]{:S(2)}) collective-permute-start(bf16[656,384]{1,0:T(8,128)(2,1)S(1)} %shard_map.78.refs_1_.p0), channel_id=1, source_target_pairs={{0,2},{1,3},{2,0},{3,1},{4,6},{5,7},{6,4},{7,5},{8,10},{9,11},{10,... | collective-permute-start | bytes 1511432 | tf_op jit(solution)/shard_map/ppermute | solution.py:288
  23.9 13.7 %collective-permute-start.5 = (bf16[192,768]{1,0:T(8,128)(2,1)S(1)}, bf16[192,768]{1,0:T(8,128)(2,1)S(1)}, u32[]{:S(2)}, u32[]{:S(2)}) collective-permute-start(bf16[192,768]{1,0:T(8,128)(2,1)S(1)} %get-tuple-element.55), channel_id=1, source_target_pairs={{0,4},{4,0},{8,12},{12,8},{16,20},{20,16},{24,28},{28,24},{1,5},{5... | collective-permute-start | bytes 884744 | tf_op jit(solution)/shard_map/ppermute | solution.py:288
  25.8 11.8 %collective-permute-start.6 = (bf16[128,768]{1,0:T(8,128)(2,1)S(1)}, bf16[128,768]{1,0:T(8,128)(2,1)S(1)}, u32[]{:S(2)}, u32[]{:S(2)}) collective-permute-start(bf16[128,768]{1,0:T(8,128)(2,1)S(1)} %get-tuple-element.58), channel_id=1, source_target_pairs={{0,16},{4,20},{8,24},{12,28},{16,0},{20,4},{24,8},{28,12},{1,17},{... | collective-permute-start | bytes 589832 | tf_op jit(solution)/shard_map/ppermute | solution.py:288
  39.3 10.0 %collective-permute-start.13 = (bf16[656,384]{1,0:T(8,128)(2,1)S(1)}, bf16[656,384]{1,0:T(8,128)(2,1)S(1)}, u32[]{:S(2)}, u32[]{:S(2)}) collective-permute-start(bf16[656,384]{1,0:T(8,128)(2,1)S(1)} %collective-permute-done.4.refs_1_.refs_5_.p2), channel_id=1, source_target_pairs={{0,1},{1,0},{2,3},{3,2},{4,5},{5,4},{6,7},{7,6},{8,9},{9,8},{10,11... | collective-permute-start | bytes 1511432 | tf_op jit(solution)/shard_map/ppermute | solution.py:288
  39.4 2.3 %collective-permute-start.9 = (bf16[400,384]{1,0:T(8,128)(2,1)S(1)}, bf16[400,384]{1,0:T(8,128)(2,1)S(1)}, u32[]{:S(2)}, u32[]{:S(2)}) collective-permute-start(bf16[400,384]{1,0:T(8,128)(2,1)S(1)} %collective-permute-done.1.p2.refs_0_.refs_4_), channel_id=1, source_target_pairs={{0,1},{1,0},{2,3},{3,2},{4,5},{5,4},{6,7},{7,6},{8,9},{9,8},{10,11... | collective-permute-start | bytes 921608 | tf_op jit(solution)/shard_map/ppermute | solution.py:288
  39.9 9.4 %collective-permute-start.12 = (bf16[192,768]{1,0:T(8,128)(2,1)S(1)}, bf16[192,768]{1,0:T(8,128)(2,1)S(1)}, u32[]{:S(2)}, u32[]{:S(2)}) collective-permute-start(bf16[192,768]{1,0:T(8,128)(2,1)S(1)} %get-tuple-element.60), channel_id=1, source_target_pairs={{0,4},{4,0},{8,12},{12,8},{16,20},{20,16},{24,28},{28,24},{1,5},{5... | collective-permute-start | bytes 884744 | tf_op jit(solution)/shard_map/ppermute | solution.py:288
  40.4 8.9 %collective-permute-start.11 = (bf16[128,512]{1,0:T(8,128)(2,1)S(1)}, bf16[128,512]{1,0:T(8,128)(2,1)S(1)}, u32[]{:S(2)}, u32[]{:S(2)}) collective-permute-start(bf16[128,512]{1,0:T(8,128)(2,1)S(1)} %get-tuple-element.67), channel_id=1, source_target_pairs={{0,16},{4,20},{8,24},{12,28},{16,0},{20,4},{24,8},{28,12},{1,17},{... | collective-permute-start | bytes 393224 | tf_op jit(solution)/shard_map/ppermute | solution.py:288
  40.5 5.6 %collective-permute-start.10 = (bf16[128,384]{1,0:T(8,128)(2,1)S(1)}, bf16[128,384]{1,0:T(8,128)(2,1)S(1)}, u32[]{:S(2)}, u32[]{:S(2)}) collective-permute-start(bf16[128,384]{1,0:T(8,128)(2,1)S(1)} %collective-permute-done.p0), channel_id=1, source_target_pairs={{0,1},{1,0},{2,3},{3,2},{4,5},{5,4},{6,7},{7,6},{8,9},{9,8},{10,11... | collective-permute-start | bytes 294920 | tf_op jit(solution)/shard_map/ppermute | solution.py:288
  41.7 4.8 %collective-permute-start.8 = (bf16[128,384]{1,0:T(8,128)(2,1)S(1)}, bf16[128,384]{1,0:T(8,128)(2,1)S(1)}, u32[]{:S(2)}, u32[]{:S(2)}) collective-permute-start(bf16[128,384]{1,0:T(8,128)(2,1)S(1)} %collective-permute-done.p0), channel_id=1, source_target_pairs={{0,2},{1,3},{2,0},{3,1},{4,6},{5,7},{6,4},{7,5},{8,10},{9,11},{10,... | collective-permute-start | bytes 294920 | tf_op jit(solution)/shard_map/ppermute | solution.py:288
  51.8 14.4 %collective-permute-start.14 = (bf16[384,768]{1,0:T(8,128)(2,1)S(1)}, bf16[384,768]{1,0:T(8,128)(2,1)S(1)}, u32[]{:S(2)}, u32[]{:S(2)}) collective-permute-start(bf16[384,768]{1,0:T(8,128)(2,1)S(1)} %get-tuple-element.69), channel_id=1, source_target_pairs={{0,4},{4,0},{8,12},{12,8},{16,20},{20,16},{24,28},{28,24},{1,5},{5... | collective-permute-start | bytes 1769480 | tf_op jit(solution)/shard_map/ppermute | solution.py:288
  53.5 55.0 %collective-permute-start.16 = (bf16[400,1536]{1,0:T(8,128)(2,1)S(1)}, bf16[400,1536]{1,0:T(8,128)(2,1)S(1)}, u32[]{:S(2)}, u32[]{:S(2)}) collective-permute-start(bf16[400,1536]{1,0:T(8,128)(2,1)S(1)} %shard_map.83), channel_id=1, source_target_pairs={{0,16},{4,20},{8,24},{12,28},{16,0},{20,4},{24,8},{28,12},{1,17},{... | collective-permute-start | bytes 3686408 | tf_op jit(solution)/shard_map/ppermute | solution.py:288
  67.3 42.1 %collective-permute-start.19 = (bf16[768,768]{1,0:T(8,128)(2,1)S(1)}, bf16[768,768]{1,0:T(8,128)(2,1)S(1)}, u32[]{:S(2)}, u32[]{:S(2)}) collective-permute-start(bf16[768,768]{1,0:T(8,128)(2,1)S(1)} %get-tuple-element.85), channel_id=1, source_target_pairs={{0,4},{4,0},{8,12},{12,8},{16,20},{20,16},{24,28},{28,24},{1,5},{5... | collective-permute-start | bytes 3538952 | tf_op jit(solution)/shard_map/ppermute | solution.py:288
  68.9 39.6 %collective-permute-start.17 = (bf16[384,768]{1,0:T(8,128)(2,1)S(1)}, bf16[384,768]{1,0:T(8,128)(2,1)S(1)}, u32[]{:S(2)}, u32[]{:S(2)}) collective-permute-start(bf16[384,768]{1,0:T(8,128)(2,1)S(1)} %get-tuple-element.77), channel_id=1, source_target_pairs={{0,8},{4,12},{8,0},{12,4},{16,24},{20,28},{24,16},{28,20},{1,9},{5... | collective-permute-start | bytes 1769480 | tf_op jit(solution)/shard_map/ppermute | solution.py:288
  69.9 1.3 collective-permute-start.15
  110.4 21.2 %collective-permute-start.20 = (bf16[384,768]{1,0:T(8,128)(2,1)S(1)}, bf16[384,768]{1,0:T(8,128)(2,1)S(1)}, u32[]{:S(2)}, u32[]{:S(2)}) collective-permute-start(bf16[384,768]{1,0:T(8,128)(2,1)S(1)} %get-tuple-element.87), channel_id=1, source_target_pairs={{0,8},{4,12},{8,0},{12,4},{16,24},{20,28},{24,16},{28,20},{1,9},{5... | collective-permute-start | bytes 1769480 | tf_op jit(solution)/shard_map/ppermute | solution.py:288
  110.5 24.9 %collective-permute-start.18 = (bf16[192,768]{1,0:T(8,128)(2,1)S(1)}, bf16[192,768]{1,0:T(8,128)(2,1)S(1)}, u32[]{:S(2)}, u32[]{:S(2)}) collective-permute-start(bf16[192,768]{1,0:T(8,128)(2,1)S(1)} %get-tuple-element.82), channel_id=1, source_target_pairs={{0,16},{4,20},{8,24},{12,28},{16,0},{20,4},{24,8},{28,12},{1,17},{... | collective-permute-start | bytes 884744 | tf_op jit(solution)/shard_map/ppermute | solution.py:288
  132.5 14.2 %collective-permute-start.21 = (bf16[192,768]{1,0:T(8,128)(2,1)S(1)}, bf16[192,768]{1,0:T(8,128)(2,1)S(1)}, u32[]{:S(2)}, u32[]{:S(2)}) collective-permute-start(bf16[192,768]{1,0:T(8,128)(2,1)S(1)} %get-tuple-element.89), channel_id=1, source_target_pairs={{0,16},{4,20},{8,24},{12,28},{16,0},{20,4},{24,8},{28,12},{1,17},{... | collective-permute-start | bytes 884744 | tf_op jit(solution)/shard_map/ppermute | solution.py:288

commit v4 on v3

--- a/solution.py
+++ b/solution.py
@@ -11,7 +11,7 @@
 SEND = 528
 KEEP = 528
 TILE = 16
-EARLY = 128
+EARLY = 96
 LATE = SEND - EARLY
 SLOTS = 4
 BAL = 720
@@ -107,7 +107,7 @@
     return (rows * own[None, :]).astype(BF)
 
 
-def first_kernel(meta, cot_hbm, scale_hbm, pre_hbm, late_out, early_out, *rest):
+def first_kernel(meta, cot_hbm, scale_hbm, pre_hbm, late_out, early_out, rest_out, *rest):
     pre_outs, (cot, scale, pre, sems) = rest[:-4], rest[-4:]
     home = cot.shape[0]
     pairs = ((cot_hbm, cot), (scale_hbm, scale), (pre_hbm, pre))
@@ -115,11 +115,13 @@
     for copy in copies:
         copy.start()
     early = early_picks(meta, home)
-    late = late_picks(meta, home)
     copies[0].wait()
     copies[1].wait()
-    early_out[...] = scaled_rows(meta, early, cot, scale)
-    late_out[...] = scaled_rows(meta, late, cot, scale)
+    early_rows = scaled_rows(meta, early, cot, scale)
+    early_out[...] = early_rows
+    rest_out[0:EARLY, :] = early_rows
+    rest_out[EARLY:, :] = scaled_rows(meta, kept_picks(meta, home), cot, scale)
+    late_out[...] = scaled_rows(meta, late_picks(meta, home), cot, scale)
     copies[2].wait()
     at = 0
     for out in pre_outs:
@@ -128,26 +130,12 @@
         at = columns.stop
 
 
-def rest_kernel(meta, cot_hbm, scale_hbm, rest_out, cot, scale, sems):
-    home = cot.shape[0]
-    pairs = ((cot_hbm, cot), (scale_hbm, scale))
-    copies = [pltpu.make_async_copy(a, b, sems.at[i]) for i, (a, b) in enumerate(pairs)]
-    for copy in copies:
-        copy.start()
-    early = early_picks(meta, home)
-    kept = kept_picks(meta, home)
-    for copy in copies:
-        copy.wait()
-    rest_out[0:EARLY, :] = scaled_rows(meta, early, cot, scale)
-    rest_out[EARLY:, :] = scaled_rows(meta, kept, cot, scale)
-
-
 def gelu_and_slope(x):
     cumulative = 0.5 * (1.0 + lax.erf(x * inv_root_two))
     return x * cumulative, cumulative + x * jnp.exp(-0.5 * x * x) * inv_root_tau
 
 
-def gelu_kernel(base, block, meta, pre_hbm, act_out, der_out, pick, rows_f32, pre, sems):
+def gelu_kernel(late, base, block, meta, pre_hbm, act_out, der_out, pick, rows_f32, pre, sems):
     home = pre.shape[1]
     rows = pick.shape[0]
     blocks = act_out.shape[1] // block
@@ -158,9 +146,11 @@
 
     for i in range(blocks):
         fetch(i).start()
-    pick[0:LATE, :] = late_picks(meta, home)
-    pick[LATE:SEND, :] = early_picks(meta, home)
-    pick[SEND:, :] = kept_picks(meta, home)
+    if late:
+        pick[...] = late_picks(meta, home)
+    else:
+        pick[0:EARLY, :] = early_picks(meta, home)
+        pick[EARLY:, :] = kept_picks(meta, home)
     step = 3 * TILE
     for i in range(blocks):
         fetch(i).wait()
@@ -184,16 +174,18 @@
         lhs[:, at] = piece[...]
 
 
-def grad_kernel(first_piece_row, first_row, block, meta, p0, p1, p2, p3, weight, der_a, der_b, out, lhs):
-    rows = out.shape[0]
-    assemble(meta, [p.at[pl.ds(first_piece_row, rows), :] for p in (p0, p1, p2, p3)], lhs)
-    half = der_a.shape[1]
-    for at in range(0, out.shape[1], block):
-        columns = slice(at, at + block)
-        der = der_a if at < half else der_b
-        slope = der[first_row : first_row + rows, at % half : at % half + block]
-        value = jnp.dot(lhs[...], weight[:, columns], preferred_element_type=F32)
-        out[:, columns] = (value * slope).astype(BF)
+def grad_kernel(first_row, slope_count, block, meta, p0, p1, p2, p3, weight, *rest):
+    slopes, outs, lhs = rest[:slope_count], rest[slope_count:-1], rest[-1]
+    rows = lhs.shape[0]
+    assemble(meta, [p.at[pl.ds(first_row, rows), :] for p in (p0, p1, p2, p3)], lhs)
+    part = slopes[0].shape[1]
+    at = 0
+    for out in outs:
+        for c in range(0, out.shape[1], block):
+            slope = slopes[at // part][first_row : first_row + rows, at % part : at % part + block]
+            value = jnp.dot(lhs[...], weight[:, at : at + block], preferred_element_type=F32)
+            out[:, c : c + block] = (value * slope).astype(BF)
+            at += block
 
 
 def early_kernel(block, meta, p0, p1, p2, p3, weight, *rest):
@@ -215,20 +207,35 @@
         at += pre.shape[1]
 
 
-def weight_kernel(count, block, meta, *refs):
-    pieces, (act, send, keep, lhs) = refs[: 2 * count], refs[2 * count :]
+def product(lhs_late, lhs_rest, act_late, act_rest, base):
+    columns = slice(base, base + act_rest.shape[1])
+    return jnp.dot(lhs_late[...], act_late[:, columns], preferred_element_type=F32) + jnp.dot(
+        lhs_rest[...], act_rest[...], preferred_element_type=F32
+    )
+
+
+def weight_kernel(count, base, meta, *refs):
+    pieces, (act_late, act_rest, send, keep, lhs_late, lhs_rest) = refs[: 2 * count], refs[2 * count :]
     half = pieces[0].shape[1] // 2
     mine = dp_at(meta) % 2 == 0
     for i in range(count):
-        both = jnp.concatenate([pieces[2 * i][...], pieces[2 * i + 1][...]], axis=0).T
-        lo, hi = both[:half], both[half:]
-        lhs[i * half : (i + 1) * half, :] = jnp.where(mine, hi, lo)
-        lhs[(count + i) * half : (count + i + 1) * half, :] = jnp.where(mine, lo, hi)
-    for at in range(0, act.shape[1], block):
-        columns = slice(at, at + block)
-        value = jnp.dot(lhs[...], act[:, columns], preferred_element_type=F32)
-        send[:, columns] = value[: count * half].astype(BF)
-        keep[:, columns] = value[count * half :]
+        for piece, lhs in ((pieces[2 * i], lhs_late), (pieces[2 * i + 1], lhs_rest)):
+            both = piece[...].T
+            lo, hi = both[:half], both[half:]
+            lhs[i * half : (i + 1) * half, :] = jnp.where(mine, hi, lo)
+            lhs[(count + i) * half : (count + i + 1) * half, :] = jnp.where(mine, lo, hi)
+    value = product(lhs_late, lhs_rest, act_late, act_rest, base)
+    send[...] = value[: count * half].astype(BF)
+    keep[...] = value[count * half :]
+
+
+def weight_again_kernel(base, meta, late_01, rest_01, late_23, rest_23, act_late, act_rest, *outs):
+    rows = late_01.shape[0] // 2
+    sends, keeps = outs[:2], outs[2:]
+    for i, (late, rest) in enumerate(((late_01, rest_01), (late_23, rest_23))):
+        value = product(late, rest, act_late, act_rest, base)
+        sends[i][...] = value[:rows].astype(BF)
+        keeps[i][...] = value[rows:]
 
 
 def near_kernel(count, meta, *refs):
@@ -271,16 +278,29 @@
     lax.fori_loop(0, half // step, body, 0)
 
 
-def place_kernel(meta, kept, early, late, out):
+def place_kernel(cuts, meta, kept, early, *rest):
+    lates, out = rest[:-1], rest[-1]
     count = kept_total(meta, dp_at(meta))
     first = jnp.minimum(count - lax.rem(count, TILE), BAL - SEND)
     first = pl.multiple_of(first, TILE)
-    out[0:KEEP, :] = kept[...]
-    out[KEEP:, :] = jnp.zeros((out.shape[0] - KEEP, out.shape[1]), BF)
-    for block, at in ((early, first), (late, pl.multiple_of(first + EARLY, TILE))):
+    wide = out.shape[1]
+    step = pl.program_id(0)
+    columns = pl.ds(pl.multiple_of(step * wide, wide), wide)
+    out[0:KEEP, :] = kept[:, columns]
+    out[KEEP:, :] = jnp.zeros((out.shape[0] - KEEP, wide), BF)
+
+    def put(block, at):
         rows = lax.broadcasted_iota(jnp.int32, (block.shape[0], 1), 0) + at
         window = pl.ds(at, block.shape[0])
-        out[window, :] = jnp.where(rows < count, out[window, :], block[...])
+        out[window, :] = jnp.where(rows < count, out[window, :], block)
+
+    put(early[:, columns], first)
+    sources = [(late, c) for late, cut in zip(lates, cuts) for c in range(0, cut, wide)]
+    for i, (late, c) in enumerate(sources):
+
+        @pl.when(step == i)
+        def _():
+            put(late[:, c : c + wide], pl.multiple_of(first + EARLY, TILE))
 
 
 def swapped(block, axis, distance):
@@ -293,11 +313,14 @@
 
 
 def shards(hidden_pre, cotangent, down_weight, layer_scale, crop_lengths, crop_moves):
+    hidden_pre, cotangent, layer_scale = (
+        pltpu.with_memory_space_constraint(x, pltpu.HBM) for x in (hidden_pre, cotangent, layer_scale)
+    )
     home, ff = hidden_pre.shape
     width = cotangent.shape[1]
     features = down_weight.shape[0]
-    half, wide = width // 2, ff // 2
-    rows = SEND + KEEP
+    half, part = width // 2, ff // 3
+    others = EARLY + KEEP
     n = lax.axis_size("dp")
     d = lax.axis_index("dp").astype(jnp.int32)
     t = lax.axis_index("tensor").astype(jnp.int32)
@@ -305,118 +328,122 @@
     own = jnp.where(column == 0, d, jnp.where(column == 1, t, 0))
     meta = jnp.concatenate([crop_lengths.T, crop_moves.T, own])
     vmem = pltpu.VMEM
-    hidden_pre, cotangent, layer_scale = (
-        pltpu.with_memory_space_constraint(x, pltpu.HBM) for x in (hidden_pre, cotangent, layer_scale)
-    )
     sems = pltpu.SemaphoreType.DMA
 
-    cuts = (256, 768, ff - 1024)
-    late, early, *pres = kernel_call(
+    def gelu(meta, late, base, columns):
+        block = 256
+        rows = LATE if late else others
+        return kernel_call(
+            functools.partial(gelu_kernel, late, base, block),
+            [shape(rows, columns), shape(rows, columns, F32)],
+            [IN_HBM], [IN_VMEM] * 2,
+            [vmem((rows, home), BF), vmem((rows, block), F32), vmem((columns // block, home, block), BF),
+             sems((columns // block,))],
+        )(meta, hidden_pre)
+
+    def weight_part(meta, pieces, act):
+        count = len(pieces)
+        return kernel_call(
+            functools.partial(weight_kernel, count, 0),
+            [shape(count * half, part), shape(count * half, part, F32),
+             shape(count * width, LATE), shape(count * width, others)],
+            [IN_VMEM] * (2 * count + 2), [IN_VMEM] * 4,
+        )(meta, *[x for j in pieces for x in (lates[j], rests[j])], act_late, act)
+
+    def weight_again(meta, base, act):
+        return kernel_call(
+            functools.partial(weight_again_kernel, base),
+            [shape(width, part)] * 2 + [shape(width, part, F32)] * 2, [IN_VMEM] * 6, [IN_VMEM] * 4,
+        )(meta, *lhs_01, *lhs_23, act_late, act)
+
+    def grads(meta, pieces, first_row, rows, slopes, cuts):
+        return kernel_call(
+            functools.partial(grad_kernel, first_row, len(slopes), 256),
+            [shape(rows, c) for c in cuts], [IN_VMEM] * (5 + len(slopes)), [IN_VMEM] * len(cuts),
+            [vmem((rows, features), BF)],
+        )(meta, *pieces, down_weight, *slopes)
+
+    def near_step(meta, keeps, gots):
+        count = len(keeps)
+        return kernel_call(
+            functools.partial(near_kernel, count),
+            [shape(width, part), shape(width, part, F32)], [IN_VMEM] * (2 * count), [IN_VMEM] * 2,
+        )(meta, *keeps, *gots)
+
+    def far_step(meta, mine, got):
+        return kernel_call(
+            far_kernel, [shape(half, part), shape(half, part, F32)], [IN_VMEM] * 2, [IN_VMEM] * 2
+        )(meta, mine, got)
+
+    cuts = (ff // 2, ff // 2)
+    late, early, rest, *pres = kernel_call(
         first_kernel,
-        [shape(LATE, width), shape(EARLY, width)] + [shape(EARLY, c) for c in cuts],
-        [IN_HBM] * 3, [IN_VMEM] * 5,
+        [shape(LATE, width), shape(EARLY, width), shape(others, width)] + [shape(EARLY, c) for c in cuts],
+        [IN_HBM] * 3, [IN_VMEM] * (3 + len(cuts)),
         [vmem((home, width), BF), vmem((features,), F32), vmem((home, ff), BF), sems((3,))],
     )(meta, cotangent, layer_scale, hidden_pre)
     arrived_early = swapped(early, "dp", n // 2)
     arrived_pres = [swapped(pre, "dp", n // 2) for pre in pres]
-
-    rest = kernel_call(
-        rest_kernel, shape(EARLY + KEEP, width), [IN_HBM] * 2, IN_VMEM,
-        [vmem((home, width), BF), vmem((features,), F32), sems((2,))],
-    )(after(meta, late), cotangent, layer_scale)
-
-    def gelu(meta, base):
-        block = 256
-        return kernel_call(
-            functools.partial(gelu_kernel, base, block),
-            [shape(rows, wide), shape(rows, wide, F32)],
-            [IN_HBM], [IN_VMEM] * 2,
-            [vmem((rows, home), BF), vmem((rows, block), F32), vmem((wide // block, home, block), BF),
-             sems((wide // block,))],
-        )(meta, hidden_pre)
-
-    def weight_part(meta, pieces, act):
-        count = len(pieces)
-        return kernel_call(
-            functools.partial(weight_kernel, count, 256),
-            [shape(count * half, wide), shape(count * half, wide, F32)],
-            [IN_VMEM] * (2 * count + 1), [IN_VMEM] * 2,
-            [vmem((count * width, rows), BF)],
-        )(meta, *[lates[j] if k == 0 else rests[j] for j in pieces for k in range(2)], act)
-
-    def grads(meta, pieces, first_piece_row, first_row, count):
-        return kernel_call(
-            functools.partial(grad_kernel, first_piece_row, first_row, 256),
-            shape(count, ff), [IN_VMEM] * 7, IN_VMEM, [vmem((count, features), BF)],
-        )(meta, *pieces, down_weight, der_a, der_b)
-
-    act_a, der_a = gelu(after(meta, rest), 0)
     late_c, late_y = swapped(late, "tensor", 1), swapped(late, "tensor", 2)
-    late_y = after(late_y, act_a, late_c, arrived_early, arrived_pres[0])
+    act_late, der_late = gelu(after(meta, late), True, 0, ff)
+
+    late_y = after(late_y, act_late, late_c, arrived_early, arrived_pres[0])
     late_yc = swapped(late_y, "tensor", 1)
-    lates, rests = (late,), (rest,)
-    send_0, keep_0 = weight_part(after(meta, late_y), (0,), act_a)
-    got_0 = swapped(send_0, "dp", 1)
-
     rest_sent = after(rest, late_y)
     rest_c, rest_y = swapped(rest_sent, "tensor", 1), swapped(rest_sent, "tensor", 2)
-    act_b, der_b = gelu(after(meta, send_0), wide)
-    lates, rests = (late, late_c, late_y, late_yc), (rest, rest_c)
-    send_1, keep_1 = weight_part(after(meta, act_b, got_0, arrived_pres[1]), (1,), act_a)
-    got_1 = swapped(send_1, "dp", 1)
-
-    rest_y = after(rest_y, send_1)
+
+    lates = (late, late_c, late_y, late_yc)
+    moves = (256, ff - 256)
+    moving = grads(after(meta, late_y), lates, 0, LATE, (der_late,), moves)
+    arrived = [swapped(block, "dp", n // 2) for block in moving]
+
+    act_a, der_a = gelu(after(meta, *moving, arrived_pres[1]), False, 0, part)
+    rests = (rest, rest_c)
+    send_01, keep_01, *lhs_01 = weight_part(after(meta, act_a), (0, 1), act_a)
+    got_01 = swapped(send_01, "dp", 1)
+    rest_y = after(rest_y, send_01, arrived[0])
     rest_yc = swapped(rest_y, "tensor", 1)
     rests = (rest, rest_c, rest_y, rest_yc)
     early_sent = after(arrived_early, rest_y)
     early_c, early_y = swapped(early_sent, "tensor", 1), swapped(early_sent, "tensor", 2)
-    moving = grads(after(meta, rest_y), lates, 0, 0, LATE)
-    arrived = swapped(moving, "dp", n // 2)
-
-    early_y = after(early_y, moving, early_c)
+
+    act_b, der_b = gelu(after(meta, rest_y), False, part, part)
+    early_y = after(early_y, act_b, early_c)
     early_yc = swapped(early_y, "tensor", 1)
-    send_23, keep_23 = weight_part(after(meta, early_y, arrived_pres[2], got_1), (2, 3), act_a)
+    send_23, keep_23, *lhs_23 = weight_part(after(meta, early_y), (2, 3), act_a)
     got_23 = swapped(send_23, "dp", 1)
-    send_b, keep_b = weight_part(after(meta, send_23), (0, 1, 2, 3), act_b)
-    kept_grad = grads(after(meta, send_b), rests, EARLY, SEND, KEEP)
-
-    def near_step(meta, keeps, gots):
-        count = len(keeps)
-        return kernel_call(
-            functools.partial(near_kernel, count),
-            [shape(width, wide), shape(width, wide, F32)], [IN_VMEM] * (2 * count), [IN_VMEM] * 2,
-        )(meta, *keeps, *gots)
-
-    def far_step(meta, mine, got):
-        return kernel_call(
-            far_kernel, [shape(half, wide), shape(half, wide, F32)], [IN_VMEM] * 2, [IN_VMEM] * 2
-        )(meta, mine, got)
-
-    out_na, mine_a = near_step(after(meta, kept_grad), (keep_0, keep_1, keep_23), (got_0, got_1, got_23))
+    *sends_b, keep_b01, keep_b23 = weight_again(after(meta, send_23), part, act_b)
+    act_c, der_c = gelu(after(meta, keep_b23), False, 2 * part, part)
+    *sends_c, keep_c01, keep_c23 = weight_again(after(meta, act_c), 2 * part, act_c)
+    (kept_grad,) = grads(after(meta, keep_c23), rests, EARLY, KEEP, (der_a, der_b, der_c), (ff,))
+
+    out_na, mine_a = near_step(after(meta, kept_grad), (keep_01, keep_23), (got_01, got_23))
     got_na = swapped(out_na, "dp", 2)
-    got_b = swapped(after(send_b, out_na), "dp", 1)
+    gots_b = [swapped(after(send, out_na), "dp", 1) for send in sends_b]
 
     early_grad = kernel_call(
         functools.partial(early_kernel, 256), shape(EARLY, ff), [IN_VMEM] * (5 + len(cuts)), IN_VMEM,
         [vmem((EARLY, features), BF), vmem((EARLY, 256), F32)],
     )(after(meta, out_na), arrived_early, early_c, early_y, early_yc, down_weight, *arrived_pres)
 
-    out_fa, own_a = far_step(after(meta, arrived, early_grad), mine_a, got_na)
+    out_nb, mine_b = near_step(after(meta, early_grad, got_na), (keep_b01, keep_b23), gots_b)
+    got_nb = swapped(out_nb, "dp", 2)
+    gots_c = [swapped(after(send, out_nb), "dp", 1) for send in sends_c]
+    out_fa, own_a = far_step(after(meta, out_nb, arrived[1]), mine_a, got_na)
     got_fa = swapped(out_fa, "dp", 4)
-    out_nb, mine_b = near_step(after(meta, out_fa), (keep_b,), (got_b,))
-    got_nb = swapped(out_nb, "dp", 2)
-    out_fb, own_b = far_step(meta, mine_b, got_nb)
+    out_nc, mine_c = near_step(after(meta, out_fa), (keep_c01, keep_c23), gots_c)
+    got_nc = swapped(out_nc, "dp", 2)
+    out_fb, own_b = far_step(after(meta, out_nc), mine_b, got_nb)
     got_fb = swapped(out_fb, "dp", 4)
-    total = jnp.concatenate([own_a + got_fa.astype(F32), own_b + got_fb.astype(F32)], axis=1)
-    down_grad = total / math.sqrt(n * home)
-
-    def columns(rows):
-        return pl.BlockSpec((rows, 512), lambda i, *_: (0, i))
+    out_fc, own_c = far_step(after(meta, out_fb), mine_c, got_nc)
+    got_fc = swapped(out_fc, "dp", 4)
+    total = [a + b.astype(F32) for a, b in ((own_a, got_fa), (own_b, got_fb), (own_c, got_fc))]
+    down_grad = jnp.concatenate(total, axis=1) / math.sqrt(n * home)
 
     hidden_grad = kernel_call(
-        place_kernel, shape(BAL, ff), [columns(KEEP), columns(EARLY), columns(LATE)], columns(BAL),
-        grid=(ff // 512,),
-    )(meta, kept_grad, early_grad, arrived)
+        functools.partial(place_kernel, moves), shape(BAL, ff), [IN_VMEM] * (2 + len(moves)),
+        pl.BlockSpec((BAL, 256), lambda i, *_: (0, i)), grid=(ff // 256,),
+    )(after(meta, out_fb), kept_grad, early_grad, *arrived)
     return (hidden_grad, down_grad)
 
 

time: 148 us -> 150 us (1.014)
  waiting for transfers between devices: 75.6 us -> 70.4 us
  Pallas kernels: 49 us -> 54 us
  starting transfers between devices: 20.5 us -> 22.4 us
    pallas_call x15 -> x18, Pallas kernels: 45.4 us -> 50.7 us  [the longest x4 21.4 us: gelu(): kernel_call(functools.partial(gelu_kernel, late, base, block), [shape(row...]
    ppermute x22 -> x26, waiting for transfers between devices: 75.6 us -> 70.4 us  [swapped(): return lax.ppermute(block, axis, [(i, i ^ distance) for i in range(n)])]
    ppermute x22 -> x26, starting transfers between devices: 20.5 us -> 22.4 us  [swapped(): return lax.ppermute(block, axis, [(i, i ^ distance) for i in range(n)])]
  transfers between devices with their start and end apart: 22 -> 26, of which waited for: 9 -> 10; matrix products, arithmetic and copies ran while one was open for 0% -> 0% of each run, Pallas kernels for 28% -> 33%
where the time goes in v4:
time: 150 us
  waiting for transfers between devices  70.4 us (47%)
  Pallas kernels  54 us (36%)
  starting transfers between devices  22.4 us (15%)
  other arithmetic  1.98 us (1%)
    ppermute x26, waiting for transfers between devices, swapped(): return lax.ppermute(block, axis, [(i, i ^ distance) for i in range(n)])  70.4 us
    ppermute x26, starting transfers between devices, swapped(): return lax.ppermute(block, axis, [(i, i ^ distance) for i in range(n)])  22.4 us
    pallas_call x4, Pallas kernels, gelu(): kernel_call(functools.partial(gelu_kernel, late, base, block), [shape(row...  21.4 us
    pallas_call x2, Pallas kernels, grads(): kernel_call(functools.partial(grad_kernel, first_row, len(slopes), 256),...  6.5 us
    pallas_call x2, Pallas kernels, weight_again(): kernel_call(functools.partial(weight_again_kernel, base), [shape(width, p...  5.7 us
    pallas_call x1, Pallas kernels, shards(): kernel_call(first_kernel, [shape(LATE, width), shape(EARLY, width), shape...  4.63 us
    pallas_call x2, Pallas kernels, weight_part(): kernel_call(functools.partial(weight_kernel, count, 0), [shape(count * ha...  3.82 us
    pallas_call x1, Pallas kernels, shards(): kernel_call(functools.partial(early_kernel, 256), shape(EARLY, ff), [IN_V...  3.35 us
  transfers between devices with their start and end apart: 26, of which 10 were waited for; matrix products, arithmetic and copies ran while one was open for 0% of the time, Pallas kernels for 33%

profile of v4, /device:TPU:0, one launch (start us, length us, event | category | flops | bytes accessed | tf_op | source)
XLA Modules:
  0.0 149.7 jit_solution(17723108123985009493)
XLA Ops:
  1.4 4.6 %shard_map.77 = (bf16[432,384]{1,0:T(8,128)(2,1)S(1)}, bf16[96,384]{1,0:T(8,128)(2,1)S(1)}, bf16[624,384]{1,0:T(8,128)(2,1)S(1)}, bf16[96,768]{1,0:T(8,128)(2,1)S(1)}, bf16[96,768]{1,0:T(8,128)(2,1)S(1)}) custom-call(s32[9,8]{1,0:T(8,128)S(1)} %pad_add_fusion.meta, bf16[1032,384]{1,0:T(8,128)(2,1)} %cot_hbm.1, f32[1536]{0:T(1024)} %scale_hbm.1, ...), custom_call_target="tpu_custom_call" | custom-call | flops 1 | bytes 1 | tf_op jit(solution)/shard_map/pallas_call | solution.py:379
  6.5 2.6 %collective-permute-start.1 = (bf16[432,384]{1,0:T(8,128)(2,1)S(1)}, bf16[432,384]{1,0:T(8,128)(2,1)S(1)}, u32[]{:S(2)}, u32[]{:S(2)}) collective-permute-start(bf16[432,384]{1,0:T(8,128)(2,1)S(1)} %get-tuple-element.73.p0.refs_0_), channel_id=1, source_target_pairs={{0,2},{1,3},{2,0},{3,1},{4,6},{5,7},{6,4},{7,5},{8,10},{9,11},{10,... | collective-permute-start | bytes 995336 | tf_op jit(solution)/shard_map/ppermute | solution.py:308
  9.1 2.6 %collective-permute-start.3 = (bf16[96,768]{1,0:T(8,128)(2,1)S(1)}, bf16[96,768]{1,0:T(8,128)(2,1)S(1)}, u32[]{:S(2)}, u32[]{:S(2)}) collective-permute-start(bf16[96,768]{1,0:T(8,128)(2,1)S(1)} %get-tuple-element.76), channel_id=1, source_target_pairs={{0,16},{4,20},{8,24},{12,28},{16,0},{20,4},{24,8},{28,12},{1,17},{... | collective-permute-start | bytes 442376 | tf_op jit(solution)/shard_map/ppermute | solution.py:308
  12.0 7.9 %shard_map.78 = (bf16[432,1536]{1,0:T(8,128)(2,1)S(1)}, f32[432,1536]{1,0:T(8,128)S(1)}) custom-call(s32[9,8]{1,0:T(8,128)S(1)} %pad_add_fusion.meta, bf16[1032,1536]{1,0:T(8,128)(2,1)} %pre_hbm.9), custom_call_target="tpu_custom_call" | custom-call | flops 1 | bytes 1 | tf_op jit(solution)/shard_map/pallas_call | solution.py:336
  19.9 2.3 %collective-permute-done.p0 = bf16[96,384]{1,0:T(8,128)(2,1)S(1)} collective-permute-done((bf16[96,384]{1,0:T(8,128)(2,1)S(1)}, bf16[96,384]{1,0:T(8,128)(2,1)S(1)}, u32[]{:S(2)}, u32[]{:S(2)}) %collective-permute-start) | collective-permute-done | bytes 73760 | tf_op jit(solution)/shard_map/ppermute | solution.py:308
  24.0 3.0 %shard_map.79 = (bf16[432,256]{1,0:T(8,128)(2,1)S(1)}, bf16[432,1280]{1,0:T(8,128)(2,1)S(1)}) custom-call(s32[9,8]{1,0:T(8,128)S(1)} %pad_add_fusion.meta, bf16[432,384]{1,0:T(8,128)(2,1)S(1)} %get-tuple-element.73.p0.refs_0_, bf16[432,384]{1,0:T(8,128)(2,1)S(1)} %collective-permute-done.2.p1.refs_2_, ...), custom_call_target="tpu_custom_call" | custom-call | flops 1 | bytes 1 | tf_op jit(solution)/shard_map/pallas_call | solution.py:360
  27.3 2.7 %collective-permute-start.6 = (bf16[96,768]{1,0:T(8,128)(2,1)S(1)}, bf16[96,768]{1,0:T(8,128)(2,1)S(1)}, u32[]{:S(2)}, u32[]{:S(2)}) collective-permute-start(bf16[96,768]{1,0:T(8,128)(2,1)S(1)} %get-tuple-element.83), channel_id=1, source_target_pairs={{0,16},{4,20},{8,24},{12,28},{16,0},{20,4},{24,8},{28,12},{1,17},{... | collective-permute-start | bytes 442376 | tf_op jit(solution)/shard_map/ppermute | solution.py:308
  30.0 16.5 %collective-permute-done.6.rest_1_ = bf16[96,768]{1,0:T(8,128)(2,1)S(1)} collective-permute-done((bf16[96,768]{1,0:T(8,128)(2,1)S(1)}, bf16[96,768]{1,0:T(8,128)(2,1)S(1)}, u32[]{:S(2)}, u32[]{:S(2)}) %collective-permute-start.6) | collective-permute-done | bytes 147488 | tf_op jit(solution)/shard_map/ppermute | solution.py:308
  46.5 4.5 %shard_map.80 = (bf16[624,512]{1,0:T(8,128)(2,1)S(1)}, f32[624,512]{1,0:T(8,128)S(1)}) custom-call(s32[9,8]{1,0:T(8,128)S(1)} %pad_add_fusion.meta, bf16[1032,1536]{1,0:T(8,128)(2,1)} %pre_hbm.9), custom_call_target="tpu_custom_call" | custom-call | flops 1 | bytes 1 | tf_op jit(solution)/shard_map/pallas_call | solution.py:336
  55.5 4.5 %shard_map.82 = (bf16[624,512]{1,0:T(8,128)(2,1)S(1)}, f32[624,512]{1,0:T(8,128)S(1)}) custom-call(s32[9,8]{1,0:T(8,128)S(1)} %pad_add_fusion.meta, bf16[1032,1536]{1,0:T(8,128)(2,1)} %pre_hbm.9), custom_call_target="tpu_custom_call" | custom-call | flops 1 | bytes 1 | tf_op jit(solution)/shard_map/pallas_call | solution.py:336
  60.0 1.9 %shard_map.83 = (bf16[384,512]{1,0:T(8,128)(2,1)S(1)}, f32[384,512]{1,0:T(8,128)S(1)}, bf16[768,432]{1,0:T(8,128)(2,1)S(1)}, bf16[768,624]{1,0:T(8,128)(2,1)S(1)}) custom-call(s32[9,8]{1,0:T(8,128)S(1)} %pad_add_fusion.meta, bf16[432,384]{1,0:T(8,128)(2,1)S(1)} %collective-permute-done.1.p2.refs_0_, bf16[624,384]{1,0:T(8,128)(2,1)S(1)} %collective-permute-done.4.refs_1_.p2, ...), custom_call_target="tpu_custom_call" | custom-call | flops 1 | bytes 1 | tf_op jit(solution)/shard_map/pallas_call | solution.py:346
  62.5 2.8 %shard_map.84 = (bf16[384,512]{1,0:T(8,128)(2,1)S(1)}, bf16[384,512]{1,0:T(8,128)(2,1)S(1)}, f32[384,512]{1,0:T(8,128)S(1)}, f32[384,512]{1,0:T(8,128)S(1)}) custom-call(s32[9,8]{1,0:T(8,128)S(1)} %pad_add_fusion.meta, bf16[768,432]{1,0:T(8,128)(2,1)S(1)} %get-tuple-element.96.late_01, bf16[768,624]{1,0:T(8,128)(2,1)S(1)} %get-tuple-element.97.rest_01, ...), custom_call_target="tpu_custom_call" | custom-call | flops 1 | bytes 1 | tf_op jit(solution)/shard_map/pallas_call | solution.py:354
  65.4 4.7 %shard_map.85 = (bf16[624,512]{1,0:T(8,128)(2,1)S(1)}, f32[624,512]{1,0:T(8,128)S(1)}) custom-call(s32[9,8]{1,0:T(8,128)S(1)} %pad_add_fusion.meta, bf16[1032,1536]{1,0:T(8,128)(2,1)} %pre_hbm.9), custom_call_target="tpu_custom_call" | custom-call | flops 1 | bytes 1 | tf_op jit(solution)/shard_map/pallas_call | solution.py:336
  70.0 2.9 %shard_map.86 = (bf16[384,512]{1,0:T(8,128)(2,1)S(1)}, bf16[384,512]{1,0:T(8,128)(2,1)S(1)}, f32[384,512]{1,0:T(8,128)S(1)}, f32[384,512]{1,0:T(8,128)S(1)}) custom-call(s32[9,8]{1,0:T(8,128)S(1)} %pad_add_fusion.meta, bf16[768,432]{1,0:T(8,128)(2,1)S(1)} %get-tuple-element.96.late_01, bf16[768,624]{1,0:T(8,128)(2,1)S(1)} %get-tuple-element.97.rest_01, ...), custom_call_target="tpu_custom_call" | custom-call | flops 1 | bytes 1 | tf_op jit(solution)/shard_map/pallas_call | solution.py:354
  72.9 3.5 %shard_map.87.kept = bf16[528,1536]{1,0:T(8,128)(2,1)S(1)} custom-call(s32[9,8]{1,0:T(8,128)S(1)} %pad_add_fusion.meta, bf16[624,384]{1,0:T(8,128)(2,1)S(1)} %get-tuple-element.78.refs_1_.p0, bf16[624,384]{1,0:T(8,128)(2,1)S(1)} %collective-permute-done.7.refs_3_.p1, bf16[624,384]{1,0:T(8,128)(2,1)S(1)} %collective-permute-done.4.refs_1_.p2, ...), custom_call_target="tpu_custom_call" | custom-call | flops 1 | bytes 1 | tf_op jit(solution)/shard_map/pallas_call | solution.py:360
  82.5 3.3 %shard_map.89.early = bf16[96,1536]{1,0:T(8,128)(2,1)S(1)} custom-call(s32[9,8]{1,0:T(8,128)S(1)} %pad_add_fusion.meta, bf16[96,384]{1,0:T(8,128)(2,1)S(1)} %collective-permute-done.p0, bf16[96,384]{1,0:T(8,128)(2,1)S(1)} %collective-permute-done.10.p1, bf16[96,384]{1,0:T(8,128)(2,1)S(1)} %collective-permute-done.9.p2, ...), custom_call_target="tpu_custom_call" | custom-call | flops 1 | bytes 1 | tf_op jit(solution)/shard_map/pallas_call | solution.py:424
  85.8 25.5 %collective-permute-done.15.got = bf16[384,512]{1,0:T(8,128)(2,1)S(1)} collective-permute-done((bf16[384,512]{1,0:T(8,128)(2,1)S(1)}, bf16[384,512]{1,0:T(8,128)(2,1)S(1)}, u32[]{:S(2)}, u32[]{:S(2)}) %collective-permute-start.15) | collective-permute-done | bytes 393248 | tf_op jit(solution)/shard_map/ppermute | solution.py:308
  115.2 4.9 %collective-permute-done.20.refs_3_ = bf16[384,512]{1,0:T(8,128)(2,1)S(1)} collective-permute-done((bf16[384,512]{1,0:T(8,128)(2,1)S(1)}, bf16[384,512]{1,0:T(8,128)(2,1)S(1)}, u32[]{:S(2)}, u32[]{:S(2)}) %collective-permute-start.20) | collective-permute-done | bytes 393248 | tf_op jit(solution)/shard_map/ppermute | solution.py:308
  120.1 4.2 %collective-permute-done.19.refs_2_ = bf16[384,512]{1,0:T(8,128)(2,1)S(1)} collective-permute-done((bf16[384,512]{1,0:T(8,128)(2,1)S(1)}, bf16[384,512]{1,0:T(8,128)(2,1)S(1)}, u32[]{:S(2)}, u32[]{:S(2)}) %collective-permute-start.19) | collective-permute-done | bytes 393248 | tf_op jit(solution)/shard_map/ppermute | solution.py:308
  125.3 6.2 %collective-permute-done.21.got = bf16[384,512]{1,0:T(8,128)(2,1)S(1)} collective-permute-done((bf16[384,512]{1,0:T(8,128)(2,1)S(1)}, bf16[384,512]{1,0:T(8,128)(2,1)S(1)}, u32[]{:S(2)}, u32[]{:S(2)}) %collective-permute-start.21) | collective-permute-done | bytes 393248 | tf_op jit(solution)/shard_map/ppermute | solution.py:308
  132.5 3.3 %shard_map.94 = bf16[720,1536]{1,0:T(8,128)(2,1)} custom-call(s32[9,8]{1,0:T(8,128)S(1)} %pad_add_fusion.meta, bf16[528,1536]{1,0:T(8,128)(2,1)S(1)} %shard_map.87.kept, bf16[96,1536]{1,0:T(8,128)(2,1)S(1)} %shard_map.89.early, bf16[432,256]{1,0:T(8,128)(2,1)S(1)} %collective-permute-done.8.rest_0_, bf16[432,1280]{1,0:T(8,128)(2,1)S(1)} %collective-permute-done.18.rest_1_), custom_call_target="tpu_custom_call" | custom-call | flops 1 | bytes 1 | tf_op jit(solution)/shard_map/pallas_call | solution.py:443
  136.7 3.0 %collective-permute-start.25 = (bf16[192,512]{1,0:T(8,128)(2,1)S(1)}, bf16[192,512]{1,0:T(8,128)(2,1)S(1)}, u32[]{:S(2)}, u32[]{:S(2)}) collective-permute-start(bf16[192,512]{1,0:T(8,128)(2,1)S(1)} %get-tuple-element.139), channel_id=1, source_target_pairs={{0,16},{4,20},{8,24},{12,28},{16,0},{20,4},{24,8},{28,12},{1,17},{... | collective-permute-start | bytes 589832 | tf_op jit(solution)/shard_map/ppermute | solution.py:308
  139.6 5.9 %collective-permute-done.23 = bf16[192,512]{1,0:T(8,128)(2,1)S(1)} collective-permute-done((bf16[192,512]{1,0:T(8,128)(2,1)S(1)}, bf16[192,512]{1,0:T(8,128)(2,1)S(1)}, u32[]{:S(2)}, u32[]{:S(2)}) %collective-permute-start.23) | collective-permute-done | bytes 196640 | tf_op jit(solution)/shard_map/ppermute | solution.py:308
  145.6 2.9 %collective-permute-done.25 = bf16[192,512]{1,0:T(8,128)(2,1)S(1)} collective-permute-done((bf16[192,512]{1,0:T(8,128)(2,1)S(1)}, bf16[192,512]{1,0:T(8,128)(2,1)S(1)}, u32[]{:S(2)}, u32[]{:S(2)}) %collective-permute-start.25) | collective-permute-done | bytes 196640 | tf_op jit(solution)/shard_map/ppermute | solution.py:308
  (55 shorter events, 22.7 us)
Async XLA Ops:
  6.0 16.3 %collective-permute-start.2 = (bf16[432,384]{1,0:T(8,128)(2,1)S(1)}, bf16[432,384]{1,0:T(8,128)(2,1)S(1)}, u32[]{:S(2)}, u32[]{:S(2)}) collective-permute-start(bf16[432,384]{1,0:T(8,128)(2,1)S(1)} %get-tuple-element.73.p0.refs_0_), channel_id=1, source_target_pairs={{0,1},{1,0},{2,3},{3,2},{4,5},{5,4},{6,7},{7,6},{8,9},{9,8},{10,11... | collective-permute-start | bytes 995336 | tf_op jit(solution)/shard_map/ppermute | solution.py:308
  6.5 15.7 %collective-permute-start.1 = (bf16[432,384]{1,0:T(8,128)(2,1)S(1)}, bf16[432,384]{1,0:T(8,128)(2,1)S(1)}, u32[]{:S(2)}, u32[]{:S(2)}) collective-permute-start(bf16[432,384]{1,0:T(8,128)(2,1)S(1)} %get-tuple-element.73.p0.refs_0_), channel_id=1, source_target_pairs={{0,2},{1,3},{2,0},{3,1},{4,6},{5,7},{6,4},{7,5},{8,10},{9,11},{10,... | collective-permute-start | bytes 995336 | tf_op jit(solution)/shard_map/ppermute | solution.py:308
  9.1 13.1 %collective-permute-start.3 = (bf16[96,768]{1,0:T(8,128)(2,1)S(1)}, bf16[96,768]{1,0:T(8,128)(2,1)S(1)}, u32[]{:S(2)}, u32[]{:S(2)}) collective-permute-start(bf16[96,768]{1,0:T(8,128)(2,1)S(1)} %get-tuple-element.76), channel_id=1, source_target_pairs={{0,16},{4,20},{8,24},{12,28},{16,0},{20,4},{24,8},{28,12},{1,17},{... | collective-permute-start | bytes 442376 | tf_op jit(solution)/shard_map/ppermute | solution.py:308
  11.7 10.5 %collective-permute-start = (bf16[96,384]{1,0:T(8,128)(2,1)S(1)}, bf16[96,384]{1,0:T(8,128)(2,1)S(1)}, u32[]{:S(2)}, u32[]{:S(2)}) collective-permute-start(bf16[96,384]{1,0:T(8,128)(2,1)S(1)} %get-tuple-element.71), channel_id=1, source_target_pairs={{0,16},{4,20},{8,24},{12,28},{16,0},{20,4},{24,8},{28,12},{1,17},{... | collective-permute-start | bytes 221192 | tf_op jit(solution)/shard_map/ppermute | solution.py:308
  22.3 28.6 %collective-permute-start.7 = (bf16[624,384]{1,0:T(8,128)(2,1)S(1)}, bf16[624,384]{1,0:T(8,128)(2,1)S(1)}, u32[]{:S(2)}, u32[]{:S(2)}) collective-permute-start(bf16[624,384]{1,0:T(8,128)(2,1)S(1)} %get-tuple-element.78.refs_1_.p0), channel_id=1, source_target_pairs={{0,1},{1,0},{2,3},{3,2},{4,5},{5,4},{6,7},{7,6},{8,9},{9,8},{10,11... | collective-permute-start | bytes 1437704 | tf_op jit(solution)/shard_map/ppermute | solution.py:308
  22.8 30.0 %collective-permute-start.4 = (bf16[624,384]{1,0:T(8,128)(2,1)S(1)}, bf16[624,384]{1,0:T(8,128)(2,1)S(1)}, u32[]{:S(2)}, u32[]{:S(2)}) collective-permute-start(bf16[624,384]{1,0:T(8,128)(2,1)S(1)} %get-tuple-element.78.refs_1_.p0), channel_id=1, source_target_pairs={{0,2},{1,3},{2,0},{3,1},{4,6},{5,7},{6,4},{7,5},{8,10},{9,11},{10,... | collective-permute-start | bytes 1437704 | tf_op jit(solution)/shard_map/ppermute | solution.py:308
  27.0 25.9 %collective-permute-start.8 = (bf16[432,256]{1,0:T(8,128)(2,1)S(1)}, bf16[432,256]{1,0:T(8,128)(2,1)S(1)}, u32[]{:S(2)}, u32[]{:S(2)}) collective-permute-start(bf16[432,256]{1,0:T(8,128)(2,1)S(1)} %get-tuple-element.81), channel_id=1, source_target_pairs={{0,16},{4,20},{8,24},{12,28},{16,0},{20,4},{24,8},{28,12},{1,17},{... | collective-permute-start | bytes 663560 | tf_op jit(solution)/shard_map/ppermute | solution.py:308
  27.3 19.2 %collective-permute-start.6 = (bf16[96,768]{1,0:T(8,128)(2,1)S(1)}, bf16[96,768]{1,0:T(8,128)(2,1)S(1)}, u32[]{:S(2)}, u32[]{:S(2)}) collective-permute-start(bf16[96,768]{1,0:T(8,128)(2,1)S(1)} %get-tuple-element.83), channel_id=1, source_target_pairs={{0,16},{4,20},{8,24},{12,28},{16,0},{20,4},{24,8},{28,12},{1,17},{... | collective-permute-start | bytes 442376 | tf_op jit(solution)/shard_map/ppermute | solution.py:308
  52.9 7.1 %collective-permute-start.11 = (bf16[624,384]{1,0:T(8,128)(2,1)S(1)}, bf16[624,384]{1,0:T(8,128)(2,1)S(1)}, u32[]{:S(2)}, u32[]{:S(2)}) collective-permute-start(bf16[624,384]{1,0:T(8,128)(2,1)S(1)} %collective-permute-done.4.refs_1_.p2), channel_id=1, source_target_pairs={{0,1},{1,0},{2,3},{3,2},{4,5},{5,4},{6,7},{7,6},{8,9},{9,8},{10,11... | collective-permute-start | bytes 1437704 | tf_op jit(solution)/shard_map/ppermute | solution.py:308
  52.9 7.0 %collective-permute-start.10 = (bf16[96,384]{1,0:T(8,128)(2,1)S(1)}, bf16[96,384]{1,0:T(8,128)(2,1)S(1)}, u32[]{:S(2)}, u32[]{:S(2)}) collective-permute-start(bf16[96,384]{1,0:T(8,128)(2,1)S(1)} %collective-permute-done.p0), channel_id=1, source_target_pairs={{0,1},{1,0},{2,3},{3,2},{4,5},{5,4},{6,7},{7,6},{8,9},{9,8},{10,11... | collective-permute-start | bytes 221192 | tf_op jit(solution)/shard_map/ppermute | solution.py:308
  53.4 6.5 %collective-permute-start.9 = (bf16[96,384]{1,0:T(8,128)(2,1)S(1)}, bf16[96,384]{1,0:T(8,128)(2,1)S(1)}, u32[]{:S(2)}, u32[]{:S(2)}) collective-permute-start(bf16[96,384]{1,0:T(8,128)(2,1)S(1)} %collective-permute-done.p0), channel_id=1, source_target_pairs={{0,2},{1,3},{2,0},{3,1},{4,6},{5,7},{6,4},{7,5},{8,10},{9,11},{10,... | collective-permute-start | bytes 221192 | tf_op jit(solution)/shard_map/ppermute | solution.py:308
  54.0 22.4 %collective-permute-start.12 = (bf16[384,512]{1,0:T(8,128)(2,1)S(1)}, bf16[384,512]{1,0:T(8,128)(2,1)S(1)}, u32[]{:S(2)}, u32[]{:S(2)}) collective-permute-start(bf16[384,512]{1,0:T(8,128)(2,1)S(1)} %get-tuple-element.87), channel_id=1, source_target_pairs={{0,4},{4,0},{8,12},{12,8},{16,20},{20,16},{24,28},{28,24},{1,5},{5... | collective-permute-start | bytes 1179656 | tf_op jit(solution)/shard_map/ppermute | solution.py:308
  61.9 14.5 %collective-permute-start.13 = (bf16[384,512]{1,0:T(8,128)(2,1)S(1)}, bf16[384,512]{1,0:T(8,128)(2,1)S(1)}, u32[]{:S(2)}, u32[]{:S(2)}) collective-permute-start(bf16[384,512]{1,0:T(8,128)(2,1)S(1)} %get-tuple-element.94), channel_id=1, source_target_pairs={{0,4},{4,0},{8,12},{12,8},{16,20},{20,16},{24,28},{28,24},{1,5},{5... | collective-permute-start | bytes 1179656 | tf_op jit(solution)/shard_map/ppermute | solution.py:308
  62.5 51.8 %collective-permute-start.18 = (bf16[432,1280]{1,0:T(8,128)(2,1)S(1)}, bf16[432,1280]{1,0:T(8,128)(2,1)S(1)}, u32[]{:S(2)}, u32[]{:S(2)}) collective-permute-start(bf16[432,1280]{1,0:T(8,128)(2,1)S(1)} %get-tuple-element.82), channel_id=1, source_target_pairs={{0,16},{4,20},{8,24},{12,28},{16,0},{20,4},{24,8},{28,12},{1,17},{... | collective-permute-start | bytes 3317768 | tf_op jit(solution)/shard_map/ppermute | solution.py:308
  77.4 33.9 %collective-permute-start.15 = (bf16[384,512]{1,0:T(8,128)(2,1)S(1)}, bf16[384,512]{1,0:T(8,128)(2,1)S(1)}, u32[]{:S(2)}, u32[]{:S(2)}) collective-permute-start(bf16[384,512]{1,0:T(8,128)(2,1)S(1)} %get-tuple-element.112), channel_id=1, source_target_pairs={{0,8},{4,12},{8,0},{12,4},{16,24},{20,28},{24,16},{28,20},{1,9},{5... | collective-permute-start | bytes 1179656 | tf_op jit(solution)/shard_map/ppermute | solution.py:308
  79.2 32.1 %collective-permute-start.17 = (bf16[384,512]{1,0:T(8,128)(2,1)S(1)}, bf16[384,512]{1,0:T(8,128)(2,1)S(1)}, u32[]{:S(2)}, u32[]{:S(2)}) collective-permute-start(bf16[384,512]{1,0:T(8,128)(2,1)S(1)} %get-tuple-element.119), channel_id=1, source_target_pairs={{0,4},{4,0},{8,12},{12,8},{16,20},{20,16},{24,28},{28,24},{1,5},{5... | collective-permute-start | bytes 1179656 | tf_op jit(solution)/shard_map/ppermute | solution.py:308
  80.7 30.6 %collective-permute-start.16 = (bf16[384,512]{1,0:T(8,128)(2,1)S(1)}, bf16[384,512]{1,0:T(8,128)(2,1)S(1)}, u32[]{:S(2)}, u32[]{:S(2)}) collective-permute-start(bf16[384,512]{1,0:T(8,128)(2,1)S(1)} %get-tuple-element.117), channel_id=1, source_target_pairs={{0,4},{4,0},{8,12},{12,8},{16,20},{20,16},{24,28},{28,24},{1,5},{5... | collective-permute-start | bytes 1179656 | tf_op jit(solution)/shard_map/ppermute | solution.py:308
  112.2 7.8 %collective-permute-start.20 = (bf16[384,512]{1,0:T(8,128)(2,1)S(1)}, bf16[384,512]{1,0:T(8,128)(2,1)S(1)}, u32[]{:S(2)}, u32[]{:S(2)}) collective-permute-start(bf16[384,512]{1,0:T(8,128)(2,1)S(1)} %get-tuple-element.129), channel_id=1, source_target_pairs={{0,4},{4,0},{8,12},{12,8},{16,20},{20,16},{24,28},{28,24},{1,5},{5... | collective-permute-start | bytes 1179656 | tf_op jit(solution)/shard_map/ppermute | solution.py:308
  113.8 10.5 %collective-permute-start.19 = (bf16[384,512]{1,0:T(8,128)(2,1)S(1)}, bf16[384,512]{1,0:T(8,128)(2,1)S(1)}, u32[]{:S(2)}, u32[]{:S(2)}) collective-permute-start(bf16[384,512]{1,0:T(8,128)(2,1)S(1)} %get-tuple-element.127), channel_id=1, source_target_pairs={{0,4},{4,0},{8,12},{12,8},{16,20},{20,16},{24,28},{28,24},{1,5},{5... | collective-permute-start | bytes 1179656 | tf_op jit(solution)/shard_map/ppermute | solution.py:308
  114.3 17.2 %collective-permute-start.21 = (bf16[384,512]{1,0:T(8,128)(2,1)S(1)}, bf16[384,512]{1,0:T(8,128)(2,1)S(1)}, u32[]{:S(2)}, u32[]{:S(2)}) collective-permute-start(bf16[384,512]{1,0:T(8,128)(2,1)S(1)} %get-tuple-element.120), channel_id=1, source_target_pairs={{0,8},{4,12},{8,0},{12,4},{16,24},{20,28},{24,16},{28,20},{1,9},{5... | collective-permute-start | bytes 1179656 | tf_op jit(solution)/shard_map/ppermute | solution.py:308
  115.2 17.3 %collective-permute-start.22 = (bf16[192,512]{1,0:T(8,128)(2,1)S(1)}, bf16[192,512]{1,0:T(8,128)(2,1)S(1)}, u32[]{:S(2)}, u32[]{:S(2)}) collective-permute-start(bf16[192,512]{1,0:T(8,128)(2,1)S(1)} %get-tuple-element.123), channel_id=1, source_target_pairs={{0,16},{4,20},{8,24},{12,28},{16,0},{20,4},{24,8},{28,12},{1,17},{... | collective-permute-start | bytes 589832 | tf_op jit(solution)/shard_map/ppermute | solution.py:308
  125.2 10.6 %collective-permute-start.24 = (bf16[384,512]{1,0:T(8,128)(2,1)S(1)}, bf16[384,512]{1,0:T(8,128)(2,1)S(1)}, u32[]{:S(2)}, u32[]{:S(2)}) collective-permute-start(bf16[384,512]{1,0:T(8,128)(2,1)S(1)} %get-tuple-element.130), channel_id=1, source_target_pairs={{0,8},{4,12},{8,0},{12,4},{16,24},{20,28},{24,16},{28,20},{1,9},{5... | collective-permute-start | bytes 1179656 | tf_op jit(solution)/shard_map/ppermute | solution.py:308
  132.4 13.2 %collective-permute-start.23 = (bf16[192,512]{1,0:T(8,128)(2,1)S(1)}, bf16[192,512]{1,0:T(8,128)(2,1)S(1)}, u32[]{:S(2)}, u32[]{:S(2)}) collective-permute-start(bf16[192,512]{1,0:T(8,128)(2,1)S(1)} %get-tuple-element.133), channel_id=1, source_target_pairs={{0,16},{4,20},{8,24},{12,28},{16,0},{20,4},{24,8},{28,12},{1,17},{... | collective-permute-start | bytes 589832 | tf_op jit(solution)/shard_map/ppermute | solution.py:308
  136.7 11.9 %collective-permute-start.25 = (bf16[192,512]{1,0:T(8,128)(2,1)S(1)}, bf16[192,512]{1,0:T(8,128)(2,1)S(1)}, u32[]{:S(2)}, u32[]{:S(2)}) collective-permute-start(bf16[192,512]{1,0:T(8,128)(2,1)S(1)} %get-tuple-element.139), channel_id=1, source_target_pairs={{0,16},{4,20},{8,24},{12,28},{16,0},{20,4},{24,8},{28,12},{1,17},{... | collective-permute-start | bytes 589832 | tf_op jit(solution)/shard_map/ppermute | solution.py:308
  (3 other events, 25.6 us)

commit v5 on v4

--- a/solution.py
+++ b/solution.py
@@ -11,7 +11,7 @@
 SEND = 528
 KEEP = 528
 TILE = 16
-EARLY = 96
+EARLY = 112
 LATE = SEND - EARLY
 SLOTS = 4
 BAL = 720
@@ -107,8 +107,8 @@
     return (rows * own[None, :]).astype(BF)
 
 
-def first_kernel(meta, cot_hbm, scale_hbm, pre_hbm, late_out, early_out, rest_out, *rest):
-    pre_outs, (cot, scale, pre, sems) = rest[:-4], rest[-4:]
+def first_kernel(meta, cot_hbm, scale_hbm, pre_hbm, late_out, early_out, rest_a, rest_b, cot, scale, pre, sems):
+    width = cot.shape[1]
     home = cot.shape[0]
     pairs = ((cot_hbm, cot), (scale_hbm, scale), (pre_hbm, pre))
     copies = [pltpu.make_async_copy(a, b, sems.at[i]) for i, (a, b) in enumerate(pairs)]
@@ -118,16 +118,15 @@
     copies[0].wait()
     copies[1].wait()
     early_rows = scaled_rows(meta, early, cot, scale)
-    early_out[...] = early_rows
-    rest_out[0:EARLY, :] = early_rows
-    rest_out[EARLY:, :] = scaled_rows(meta, kept_picks(meta, home), cot, scale)
+    early_out[:, :width] = early_rows
+    kept_rows = scaled_rows(meta, kept_picks(meta, home), cot, scale)
+    cut = rest_a.shape[0] - EARLY
+    rest_a[0:EARLY, :] = early_rows
+    rest_a[EARLY:, :] = kept_rows[:cut]
+    rest_b[...] = kept_rows[cut:]
     late_out[...] = scaled_rows(meta, late_picks(meta, home), cot, scale)
     copies[2].wait()
-    at = 0
-    for out in pre_outs:
-        columns = slice(at, at + out.shape[1])
-        out[...] = jnp.dot(early, pre[:, columns], preferred_element_type=F32).astype(BF)
-        at = columns.stop
+    early_out[:, width:] = jnp.dot(early, pre[...], preferred_element_type=F32).astype(BF)
 
 
 def gelu_and_slope(x):
@@ -151,7 +150,7 @@
     else:
         pick[0:EARLY, :] = early_picks(meta, home)
         pick[EARLY:, :] = kept_picks(meta, home)
-    step = 3 * TILE
+    step = next(TILE * k for k in (3, 4, 2, 1) if rows % (TILE * k) == 0)
     for i in range(blocks):
         fetch(i).wait()
         rows_f32[...] = jnp.dot(pick[...], pre[i], preferred_element_type=F32)
@@ -167,17 +166,31 @@
         lax.fori_loop(0, rows // step, body, 0)
 
 
-def assemble(meta, pieces, lhs):
-    width = pieces[0].shape[1]
+def assemble(meta, pieces, first_row, lhs):
+    rows = lhs.shape[0]
+    width = pieces[1][0].shape[1]
     for j, piece in enumerate(pieces):
-        at = pl.ds(pl.multiple_of((tensor_at(meta) ^ j) * width, 128), width)
-        lhs[:, at] = piece[...]
-
-
-def grad_kernel(first_row, slope_count, block, meta, p0, p1, p2, p3, weight, *rest):
-    slopes, outs, lhs = rest[:slope_count], rest[slope_count:-1], rest[-1]
+        columns = pl.ds(pl.multiple_of((tensor_at(meta) ^ j) * width, 128), width)
+        at = 0
+        for block in piece:
+            low, high = max(at, first_row), min(at + block.shape[0], first_row + rows)
+            if low < high:
+                lhs[low - first_row : high - first_row, columns] = block[low - at : high - at, 0:width]
+            at += block.shape[0]
+
+
+def split(refs, counts):
+    out, at = [], 0
+    for count in counts:
+        out.append(refs[at : at + count])
+        at += count
+    return out
+
+
+def grad_kernel(counts, first_row, block, meta, *refs):
+    p0, p1, p2, p3, (weight,), slopes, outs, (lhs,) = split(refs, counts)
     rows = lhs.shape[0]
-    assemble(meta, [p.at[pl.ds(first_row, rows), :] for p in (p0, p1, p2, p3)], lhs)
+    assemble(meta, (p0, p1, p2, p3), first_row, lhs)
     part = slopes[0].shape[1]
     at = 0
     for out in outs:
@@ -188,23 +201,20 @@
             at += block
 
 
-def early_kernel(block, meta, p0, p1, p2, p3, weight, *rest):
-    pres, (out, lhs, acc) = rest[:-3], rest[-3:]
-    assemble(meta, (p0, p1, p2, p3), lhs)
-    at = 0
-    for pre in pres:
-        for c in range(0, pre.shape[1], block):
-            columns = slice(at + c, at + c + block)
-            acc[...] = jnp.dot(lhs[...], weight[:, columns], preferred_element_type=F32)
-
-            def body(k, _):
-                rows = pl.ds(pl.multiple_of(k * TILE, TILE), TILE)
-                _, slope = gelu_and_slope(pre[rows, c : c + block].astype(F32))
-                out[rows, columns] = (acc[rows, :] * slope).astype(BF)
-                return 0
-
-            lax.fori_loop(0, EARLY // TILE, body, 0)
-        at += pre.shape[1]
+def early_kernel(block, meta, own, p1, p2, p3, weight, out, lhs, acc):
+    width = p1.shape[1]
+    assemble(meta, ([own], [p1], [p2], [p3]), 0, lhs)
+    for at in range(0, out.shape[1], block):
+        columns = slice(at, at + block)
+        acc[...] = jnp.dot(lhs[...], weight[:, columns], preferred_element_type=F32)
+
+        def body(k, _):
+            rows = pl.ds(pl.multiple_of(k * TILE, TILE), TILE)
+            _, slope = gelu_and_slope(own[rows, width + at : width + at + block].astype(F32))
+            out[rows, columns] = (acc[rows, :] * slope).astype(BF)
+            return 0
+
+        lax.fori_loop(0, EARLY // TILE, body, 0)
 
 
 def product(lhs_late, lhs_rest, act_late, act_rest, base):
@@ -214,13 +224,17 @@
     )
 
 
-def weight_kernel(count, base, meta, *refs):
-    pieces, (act_late, act_rest, send, keep, lhs_late, lhs_rest) = refs[: 2 * count], refs[2 * count :]
-    half = pieces[0].shape[1] // 2
+def weight_kernel(counts, base, meta, *refs):
+    *parts, (act_late, act_rest, send, keep, lhs_late, lhs_rest) = split(refs, counts)
+    count = len(parts) // 2
+    half = parts[0][0].shape[1] // 2
     mine = dp_at(meta) % 2 == 0
     for i in range(count):
-        for piece, lhs in ((pieces[2 * i], lhs_late), (pieces[2 * i + 1], lhs_rest)):
-            both = piece[...].T
+        for blocks, lhs in ((parts[2 * i], lhs_late), (parts[2 * i + 1], lhs_rest)):
+            both = blocks[0][...]
+            if len(blocks) > 1:
+                both = jnp.concatenate([block[...] for block in blocks], axis=0)
+            both = both.T
             lo, hi = both[:half], both[half:]
             lhs[i * half : (i + 1) * half, :] = jnp.where(mine, hi, lo)
             lhs[(count + i) * half : (count + i + 1) * half, :] = jnp.where(mine, lo, hi)
@@ -229,13 +243,12 @@
     keep[...] = value[count * half :]
 
 
-def weight_again_kernel(base, meta, late_01, rest_01, late_23, rest_23, act_late, act_rest, *outs):
+def weight_again_kernel(base, meta, late_01, rest_01, late_23, rest_23, act_late, act_rest, send, keep):
     rows = late_01.shape[0] // 2
-    sends, keeps = outs[:2], outs[2:]
     for i, (late, rest) in enumerate(((late_01, rest_01), (late_23, rest_23))):
         value = product(late, rest, act_late, act_rest, base)
-        sends[i][...] = value[:rows].astype(BF)
-        keeps[i][...] = value[rows:]
+        send[i * rows : (i + 1) * rows, :] = value[:rows].astype(BF)
+        keep[i * rows : (i + 1) * rows, :] = value[rows:]
 
 
 def near_kernel(count, meta, *refs):
@@ -343,25 +356,30 @@
 
     def weight_part(meta, pieces, act):
         count = len(pieces)
+        parts = [x for j in pieces for x in (lates[j], rests[j])]
+        counts = [len(x) for x in parts] + [6]
+        blocks = [block for x in parts for block in x]
         return kernel_call(
-            functools.partial(weight_kernel, count, 0),
+            functools.partial(weight_kernel, counts, 0),
             [shape(count * half, part), shape(count * half, part, F32),
              shape(count * width, LATE), shape(count * width, others)],
-            [IN_VMEM] * (2 * count + 2), [IN_VMEM] * 4,
-        )(meta, *[x for j in pieces for x in (lates[j], rests[j])], act_late, act)
+            [IN_VMEM] * (len(blocks) + 2), [IN_VMEM] * 4,
+        )(meta, *blocks, act_late, act)
 
     def weight_again(meta, base, act):
         return kernel_call(
             functools.partial(weight_again_kernel, base),
-            [shape(width, part)] * 2 + [shape(width, part, F32)] * 2, [IN_VMEM] * 6, [IN_VMEM] * 4,
+            [shape(4 * half, part), shape(4 * half, part, F32)], [IN_VMEM] * 6, [IN_VMEM] * 2,
         )(meta, *lhs_01, *lhs_23, act_late, act)
 
     def grads(meta, pieces, first_row, rows, slopes, cuts):
+        counts = [len(x) for x in pieces] + [1, len(slopes), len(cuts), 1]
+        blocks = [block for x in pieces for block in x]
         return kernel_call(
-            functools.partial(grad_kernel, first_row, len(slopes), 256),
-            [shape(rows, c) for c in cuts], [IN_VMEM] * (5 + len(slopes)), [IN_VMEM] * len(cuts),
+            functools.partial(grad_kernel, counts, first_row, 256),
+            [shape(rows, c) for c in cuts], [IN_VMEM] * (len(blocks) + 1 + len(slopes)), [IN_VMEM] * len(cuts),
             [vmem((rows, features), BF)],
-        )(meta, *pieces, down_weight, *slopes)
+        )(meta, *blocks, down_weight, *slopes)
 
     def near_step(meta, keeps, gots):
         count = len(keeps)
@@ -375,63 +393,63 @@
             far_kernel, [shape(half, part), shape(half, part, F32)], [IN_VMEM] * 2, [IN_VMEM] * 2
         )(meta, mine, got)
 
-    cuts = (ff // 2, ff // 2)
-    late, early, rest, *pres = kernel_call(
+    cut = others // 2
+    late, early, *rest = kernel_call(
         first_kernel,
-        [shape(LATE, width), shape(EARLY, width), shape(others, width)] + [shape(EARLY, c) for c in cuts],
-        [IN_HBM] * 3, [IN_VMEM] * (3 + len(cuts)),
+        [shape(LATE, width), shape(EARLY, width + ff), shape(cut, width), shape(others - cut, width)],
+        [IN_HBM] * 3, [IN_VMEM] * 4,
         [vmem((home, width), BF), vmem((features,), F32), vmem((home, ff), BF), sems((3,))],
     )(meta, cotangent, layer_scale, hidden_pre)
     arrived_early = swapped(early, "dp", n // 2)
-    arrived_pres = [swapped(pre, "dp", n // 2) for pre in pres]
     late_c, late_y = swapped(late, "tensor", 1), swapped(late, "tensor", 2)
     act_late, der_late = gelu(after(meta, late), True, 0, ff)
 
-    late_y = after(late_y, act_late, late_c, arrived_early, arrived_pres[0])
+    late_y = after(late_y, act_late, late_c)
     late_yc = swapped(late_y, "tensor", 1)
-    rest_sent = after(rest, late_y)
-    rest_c, rest_y = swapped(rest_sent, "tensor", 1), swapped(rest_sent, "tensor", 2)
-
-    lates = (late, late_c, late_y, late_yc)
-    moves = (256, ff - 256)
+    rest_sent = [after(block, late_y) for block in rest]
+    rest_y = [swapped(block, "tensor", 2) for block in rest_sent]
+    rest_c = [swapped(block, "tensor", 1) for block in rest_sent]
+
+    lates = ([late], [late_c], [late_y], [late_yc])
+    moves = (512, ff - 512)
     moving = grads(after(meta, late_y), lates, 0, LATE, (der_late,), moves)
     arrived = [swapped(block, "dp", n // 2) for block in moving]
 
-    act_a, der_a = gelu(after(meta, *moving, arrived_pres[1]), False, 0, part)
+    act_a, der_a = gelu(after(meta, *moving, arrived_early), False, 0, part)
     rests = (rest, rest_c)
     send_01, keep_01, *lhs_01 = weight_part(after(meta, act_a), (0, 1), act_a)
     got_01 = swapped(send_01, "dp", 1)
-    rest_y = after(rest_y, send_01, arrived[0])
-    rest_yc = swapped(rest_y, "tensor", 1)
+    rest_y = [after(block, send_01) for block in rest_y]
+    rest_yc = [swapped(block, "tensor", 1) for block in rest_y]
     rests = (rest, rest_c, rest_y, rest_yc)
-    early_sent = after(arrived_early, rest_y)
+
+    act_b, der_b = gelu(after(meta, *rest_y), False, part, part)
+    send_23, keep_23, *lhs_23 = weight_part(after(meta, act_b, arrived[0]), (2, 3), act_a)
+    got_23 = swapped(send_23, "dp", 1)
+    early_sent = after(arrived_early[:, :width], send_23)
     early_c, early_y = swapped(early_sent, "tensor", 1), swapped(early_sent, "tensor", 2)
-
-    act_b, der_b = gelu(after(meta, rest_y), False, part, part)
-    early_y = after(early_y, act_b, early_c)
+    send_b, keep_b = weight_again(after(meta, send_23), part, act_b)
+    got_b = swapped(send_b, "dp", 1)
+    act_c, der_c = gelu(after(meta, send_b), False, 2 * part, part)
+    early_y = after(early_y, act_c, early_c)
     early_yc = swapped(early_y, "tensor", 1)
-    send_23, keep_23, *lhs_23 = weight_part(after(meta, early_y), (2, 3), act_a)
-    got_23 = swapped(send_23, "dp", 1)
-    *sends_b, keep_b01, keep_b23 = weight_again(after(meta, send_23), part, act_b)
-    act_c, der_c = gelu(after(meta, keep_b23), False, 2 * part, part)
-    *sends_c, keep_c01, keep_c23 = weight_again(after(meta, act_c), 2 * part, act_c)
-    (kept_grad,) = grads(after(meta, keep_c23), rests, EARLY, KEEP, (der_a, der_b, der_c), (ff,))
-
-    out_na, mine_a = near_step(after(meta, kept_grad), (keep_01, keep_23), (got_01, got_23))
+    send_c, keep_c = weight_again(after(meta, early_y), 2 * part, act_c)
+
+    out_na, mine_a = near_step(after(meta, send_c), (keep_01, keep_23), (got_01, got_23))
     got_na = swapped(out_na, "dp", 2)
-    gots_b = [swapped(after(send, out_na), "dp", 1) for send in sends_b]
+    (kept_grad,) = grads(after(meta, out_na), rests, EARLY, KEEP, (der_a, der_b, der_c), (ff,))
 
     early_grad = kernel_call(
-        functools.partial(early_kernel, 256), shape(EARLY, ff), [IN_VMEM] * (5 + len(cuts)), IN_VMEM,
+        functools.partial(early_kernel, 256), shape(EARLY, ff), [IN_VMEM] * 5, IN_VMEM,
         [vmem((EARLY, features), BF), vmem((EARLY, 256), F32)],
-    )(after(meta, out_na), arrived_early, early_c, early_y, early_yc, down_weight, *arrived_pres)
-
-    out_nb, mine_b = near_step(after(meta, early_grad, got_na), (keep_b01, keep_b23), gots_b)
+    )(after(meta, kept_grad), arrived_early, early_c, early_y, early_yc, down_weight)
+
+    out_nb, mine_b = near_step(after(meta, early_grad, got_na), (keep_b,), (got_b,))
     got_nb = swapped(out_nb, "dp", 2)
-    gots_c = [swapped(after(send, out_nb), "dp", 1) for send in sends_c]
+    got_c = swapped(after(send_c, early_grad), "dp", 1)
     out_fa, own_a = far_step(after(meta, out_nb, arrived[1]), mine_a, got_na)
     got_fa = swapped(out_fa, "dp", 4)
-    out_nc, mine_c = near_step(after(meta, out_fa), (keep_c01, keep_c23), gots_c)
+    out_nc, mine_c = near_step(after(meta, out_fa), (keep_c,), (got_c,))
     got_nc = swapped(out_nc, "dp", 2)
     out_fb, own_b = far_step(after(meta, out_nc), mine_b, got_nb)
     got_fb = swapped(out_fb, "dp", 4)

time: 150 us -> 148 us (0.987)
  starting transfers between devices: 22.4 us -> 20.7 us
    ppermute x26 -> x25, starting transfers between devices: 22.4 us -> 20.7 us  [swapped(): return lax.ppermute(block, axis, [(i, i ^ distance) for i in range(n)])]
    ppermute x26 -> x25, waiting for transfers between devices: 70.4 us -> 70.1 us  [swapped(): return lax.ppermute(block, axis, [(i, i ^ distance) for i in range(n)])]
  transfers between devices with their start and end apart: 26 -> 25, of which waited for: 10 -> 8; matrix products, arithmetic and copies ran while one was open for 0% -> 0% of each run, Pallas kernels for 33% -> 33%
where the time goes in v5:
time: 148 us
  waiting for transfers between devices  70.1 us (47%)
  Pallas kernels  53.8 us (36%)
  starting transfers between devices  20.7 us (14%)
  other arithmetic  1.97 us (1%)
    ppermute x25, waiting for transfers between devices, swapped(): return lax.ppermute(block, axis, [(i, i ^ distance) for i in range(n)])  70.1 us
    pallas_call x4, Pallas kernels, gelu(): kernel_call(functools.partial(gelu_kernel, late, base, block), [shape(row...  21.1 us
    ppermute x25, starting transfers between devices, swapped(): return lax.ppermute(block, axis, [(i, i ^ distance) for i in range(n)])  20.7 us
    pallas_call x2, Pallas kernels, grads(): kernel_call(functools.partial(grad_kernel, counts, first_row, 256), [shap...  6.36 us
    pallas_call x2, Pallas kernels, weight_again(): kernel_call(functools.partial(weight_again_kernel, base), [shape(4 * half...  5.69 us
    pallas_call x1, Pallas kernels, shards(): kernel_call(first_kernel, [shape(LATE, width), shape(EARLY, width + ff),...  4.62 us
    pallas_call x2, Pallas kernels, weight_part(): kernel_call(functools.partial(weight_kernel, counts, 0), [shape(count * h...  3.79 us
    pallas_call x1, Pallas kernels, shards(): kernel_call(functools.partial(early_kernel, 256), shape(EARLY, ff), [IN_V...  3.5 us
  transfers between devices with their start and end apart: 25, of which 8 were waited for; matrix products, arithmetic and copies ran while one was open for 0% of the time, Pallas kernels for 33%

profile of v5, /device:TPU:0, one launch (start us, length us, event | category | flops | bytes accessed | tf_op | source)
XLA Modules:
  0.0 147.6 jit_solution(18210608249707883829)
XLA Ops:
  1.4 4.6 %shard_map.77 = (bf16[416,384]{1,0:T(8,128)(2,1)S(1)}, bf16[112,1920]{1,0:T(8,128)(2,1)S(1)}, bf16[320,384]{1,0:T(8,128)(2,1)S(1)}, bf16[320,384]{1,0:T(8,128)(2,1)S(1)}) custom-call(s32[9,8]{1,0:T(8,128)S(1)} %pad_add_fusion.meta, bf16[1032,384]{1,0:T(8,128)(2,1)} %cot_hbm.1, f32[1536]{0:T(1024)} %scale_hbm.1, bf16[1032,1536]{1,0:T(8,128)(2,1)} %pre_hbm.9), custom_call_target="tpu_custom_call" | custom-call | flops 1 | bytes 1 | tf_op jit(solution)/shard_map/pallas_call | solution.py:397
  6.5 2.6 %collective-permute-start.1 = (bf16[416,384]{1,0:T(8,128)(2,1)S(1)}, bf16[416,384]{1,0:T(8,128)(2,1)S(1)}, u32[]{:S(2)}, u32[]{:S(2)}) collective-permute-start(bf16[416,384]{1,0:T(8,128)(2,1)S(1)} %get-tuple-element.67.refs_0_), channel_id=1, source_target_pairs={{0,2},{1,3},{2,0},{3,1},{4,6},{5,7},{6,4},{7,5},{8,10},{9,11},{10,... | collective-permute-start | bytes 958472 | tf_op jit(solution)/shard_map/ppermute | solution.py:321
  9.1 2.6 %collective-permute-start = (bf16[112,1920]{1,0:T(8,128)(2,1)S(1)}, bf16[112,1920]{1,0:T(8,128)(2,1)S(1)}, u32[]{:S(2)}, u32[]{:S(2)}) collective-permute-start(bf16[112,1920]{1,0:T(8,128)(2,1)S(1)} %get-tuple-element.65), channel_id=1, source_target_pairs={{0,16},{4,20},{8,24},{12,28},{16,0},{20,4},{24,8},{28,12},{1,17},{... | collective-permute-start | bytes 1290248 | tf_op jit(solution)/shard_map/ppermute | solution.py:321
  11.7 7.8 %shard_map.78 = (bf16[416,1536]{1,0:T(8,128)(2,1)S(1)}, f32[416,1536]{1,0:T(8,128)S(1)}) custom-call(s32[9,8]{1,0:T(8,128)S(1)} %pad_add_fusion.meta, bf16[1032,1536]{1,0:T(8,128)(2,1)} %pre_hbm.9), custom_call_target="tpu_custom_call" | custom-call | flops 1 | bytes 1 | tf_op jit(solution)/shard_map/pallas_call | solution.py:349
  22.2 2.9 %shard_map.79 = (bf16[416,512]{1,0:T(8,128)(2,1)S(1)}, bf16[416,1024]{1,0:T(8,128)(2,1)S(1)}) custom-call(s32[9,8]{1,0:T(8,128)S(1)} %pad_add_fusion.meta, bf16[416,384]{1,0:T(8,128)(2,1)S(1)} %get-tuple-element.67.refs_0_, bf16[416,384]{1,0:T(8,128)(2,1)S(1)} %collective-permute-done.2.refs_1_.refs_3_, ...), custom_call_target="tpu_custom_call" | custom-call | flops 1 | bytes 1 | tf_op jit(solution)/shard_map/pallas_call | solution.py:378
  25.1 6.1 %collective-permute-done.own = bf16[112,1920]{1,0:T(8,128)(2,1)S(1)} collective-permute-done((bf16[112,1920]{1,0:T(8,128)(2,1)S(1)}, bf16[112,1920]{1,0:T(8,128)(2,1)S(1)}, u32[]{:S(2)}, u32[]{:S(2)}) %collective-permute-start) | collective-permute-done | bytes 430112 | tf_op jit(solution)/shard_map/ppermute | solution.py:321
  31.2 4.4 %shard_map.80 = (bf16[640,512]{1,0:T(8,128)(2,1)S(1)}, f32[640,512]{1,0:T(8,128)S(1)}) custom-call(s32[9,8]{1,0:T(8,128)S(1)} %pad_add_fusion.meta, bf16[1032,1536]{1,0:T(8,128)(2,1)} %pre_hbm.9), custom_call_target="tpu_custom_call" | custom-call | flops 1 | bytes 1 | tf_op jit(solution)/shard_map/pallas_call | solution.py:349
  35.6 1.9 %shard_map.81 = (bf16[384,512]{1,0:T(8,128)(2,1)S(1)}, f32[384,512]{1,0:T(8,128)S(1)}, bf16[768,416]{1,0:T(8,128)(2,1)S(1)}, bf16[768,640]{1,0:T(8,128)(2,1)S(1)}) custom-call(s32[9,8]{1,0:T(8,128)S(1)} %pad_add_fusion.meta, bf16[416,384]{1,0:T(8,128)(2,1)S(1)} %get-tuple-element.67.refs_0_, bf16[320,384]{1,0:T(8,128)(2,1)S(1)} %get-tuple-element.71.refs_1_.refs_0_, ...), custom_call_target="tpu_custom_call" | custom-call | flops 1 | bytes 1 | tf_op jit(solution)/shard_map/pallas_call | solution.py:362
  39.6 4.4 %shard_map.82 = (bf16[640,512]{1,0:T(8,128)(2,1)S(1)}, f32[640,512]{1,0:T(8,128)S(1)}) custom-call(s32[9,8]{1,0:T(8,128)S(1)} %pad_add_fusion.meta, bf16[1032,1536]{1,0:T(8,128)(2,1)} %pre_hbm.9), custom_call_target="tpu_custom_call" | custom-call | flops 1 | bytes 1 | tf_op jit(solution)/shard_map/pallas_call | solution.py:349
  44.1 8.2 %collective-permute-done.8.rest_0_ = bf16[416,512]{1,0:T(8,128)(2,1)S(1)} collective-permute-done((bf16[416,512]{1,0:T(8,128)(2,1)S(1)}, bf16[416,512]{1,0:T(8,128)(2,1)S(1)}, u32[]{:S(2)}, u32[]{:S(2)}) %collective-permute-start.8) | collective-permute-done | bytes 426016 | tf_op jit(solution)/shard_map/ppermute | solution.py:321
  52.3 1.9 %shard_map.83 = (bf16[384,512]{1,0:T(8,128)(2,1)S(1)}, f32[384,512]{1,0:T(8,128)S(1)}, bf16[768,416]{1,0:T(8,128)(2,1)S(1)}, bf16[768,640]{1,0:T(8,128)(2,1)S(1)}) custom-call(s32[9,8]{1,0:T(8,128)S(1)} %pad_add_fusion.meta, bf16[416,384]{1,0:T(8,128)(2,1)S(1)} %collective-permute-done.1.refs_2_.refs_0_, ...), custom_call_target="tpu_custom_call" | custom-call | flops 1 | bytes 1 | tf_op jit(solution)/shard_map/pallas_call | solution.py:362
  55.7 2.8 %shard_map.84 = (bf16[768,512]{1,0:T(8,128)(2,1)S(1)}, f32[768,512]{1,0:T(8,128)S(1)}) custom-call(s32[9,8]{1,0:T(8,128)S(1)} %pad_add_fusion.meta, bf16[768,416]{1,0:T(8,128)(2,1)S(1)} %get-tuple-element.90.late_01, bf16[768,640]{1,0:T(8,128)(2,1)S(1)} %get-tuple-element.91.rest_01, bf16[768,416]{1,0:T(8,128)(2,1)S(1)} %get-tuple-element.92.late_23, ...), custom_call_target="tpu_custom_call" | custom-call | flops 1 | bytes 1 | tf_op jit(solution)/shard_map/pallas_call | solution.py:370
  60.6 4.4 %shard_map.85 = (bf16[640,512]{1,0:T(8,128)(2,1)S(1)}, f32[640,512]{1,0:T(8,128)S(1)}) custom-call(s32[9,8]{1,0:T(8,128)S(1)} %pad_add_fusion.meta, bf16[1032,1536]{1,0:T(8,128)(2,1)} %pre_hbm.9), custom_call_target="tpu_custom_call" | custom-call | flops 1 | bytes 1 | tf_op jit(solution)/shard_map/pallas_call | solution.py:349
  65.2 2.8 %shard_map.86 = (bf16[768,512]{1,0:T(8,128)(2,1)S(1)}, f32[768,512]{1,0:T(8,128)S(1)}) custom-call(s32[9,8]{1,0:T(8,128)S(1)} %pad_add_fusion.meta, bf16[768,416]{1,0:T(8,128)(2,1)S(1)} %get-tuple-element.90.late_01, bf16[768,640]{1,0:T(8,128)(2,1)S(1)} %get-tuple-element.91.rest_01, bf16[768,416]{1,0:T(8,128)(2,1)S(1)} %get-tuple-element.92.late_23, ...), custom_call_target="tpu_custom_call" | custom-call | flops 1 | bytes 1 | tf_op jit(solution)/shard_map/pallas_call | solution.py:370
  69.2 3.5 %shard_map.88.kept = bf16[528,1536]{1,0:T(8,128)(2,1)S(1)} custom-call(s32[9,8]{1,0:T(8,128)S(1)} %pad_add_fusion.meta, bf16[320,384]{1,0:T(8,128)(2,1)S(1)} %get-tuple-element.71.refs_1_.refs_0_, bf16[320,384]{1,0:T(8,128)(2,1)S(1)} %get-tuple-element.80.refs_2_.refs_1_, bf16[320,384]{1,0:T(8,128)(2,1)S(1)} %collective-permute-done.5.refs_4_.refs_2_, ...), custom_call_target="tpu_custom_call" | custom-call | flops 1 | bytes 1 | tf_op jit(solution)/shard_map/pallas_call | solution.py:378
  72.7 3.5 %shard_map.89.early = bf16[112,1536]{1,0:T(8,128)(2,1)S(1)} custom-call(s32[9,8]{1,0:T(8,128)S(1)} %pad_add_fusion.meta, bf16[112,1920]{1,0:T(8,128)(2,1)S(1)} %collective-permute-done.own, bf16[112,384]{1,0:T(8,128)(2,1)S(1)} %collective-permute-done.12.p1, bf16[112,384]{1,0:T(8,128)(2,1)S(1)} %collective-permute-done.11.p2, ...), custom_call_target="tpu_custom_call" | custom-call | flops 1 | bytes 1 | tf_op jit(solution)/shard_map/pallas_call | solution.py:442
  76.2 1.6 %collective-permute-start.19 = (bf16[768,512]{1,0:T(8,128)(2,1)S(1)}, bf16[768,512]{1,0:T(8,128)(2,1)S(1)}, u32[]{:S(2)}, u32[]{:S(2)}) collective-permute-start(bf16[768,512]{1,0:T(8,128)(2,1)S(1)} %get-tuple-element.117), channel_id=1, source_target_pairs={{0,4},{4,0},{8,12},{12,8},{16,20},{20,16},{24,28},{28,24},{1,5},{5... | collective-permute-start | bytes 2359304 | tf_op jit(solution)/shard_map/ppermute | solution.py:321
  77.8 1.6 %collective-permute-start.16 = (bf16[384,512]{1,0:T(8,128)(2,1)S(1)}, bf16[384,512]{1,0:T(8,128)(2,1)S(1)}, u32[]{:S(2)}, u32[]{:S(2)}) collective-permute-start(bf16[384,512]{1,0:T(8,128)(2,1)S(1)} %get-tuple-element.103), channel_id=1, source_target_pairs={{0,8},{4,12},{8,0},{12,4},{16,24},{20,28},{24,16},{28,20},{1,9},{5... | collective-permute-start | bytes 1179656 | tf_op jit(solution)/shard_map/ppermute | solution.py:321
  79.4 27.7 %collective-permute-done.16.got = bf16[384,512]{1,0:T(8,128)(2,1)S(1)} collective-permute-done((bf16[384,512]{1,0:T(8,128)(2,1)S(1)}, bf16[384,512]{1,0:T(8,128)(2,1)S(1)}, u32[]{:S(2)}, u32[]{:S(2)}) %collective-permute-start.16) | collective-permute-done | bytes 393248 | tf_op jit(solution)/shard_map/ppermute | solution.py:321
  108.9 3.2 %collective-permute-start.21 = (bf16[192,512]{1,0:T(8,128)(2,1)S(1)}, bf16[192,512]{1,0:T(8,128)(2,1)S(1)}, u32[]{:S(2)}, u32[]{:S(2)}) collective-permute-start(bf16[192,512]{1,0:T(8,128)(2,1)S(1)} %get-tuple-element.114), channel_id=1, source_target_pairs={{0,16},{4,20},{8,24},{12,28},{16,0},{20,4},{24,8},{28,12},{1,17},{... | collective-permute-start | bytes 589832 | tf_op jit(solution)/shard_map/ppermute | solution.py:321
  113.2 11.2 %collective-permute-done.20.got = bf16[384,512]{1,0:T(8,128)(2,1)S(1)} collective-permute-done((bf16[384,512]{1,0:T(8,128)(2,1)S(1)}, bf16[384,512]{1,0:T(8,128)(2,1)S(1)}, u32[]{:S(2)}, u32[]{:S(2)}) %collective-permute-start.20) | collective-permute-done | bytes 393248 | tf_op jit(solution)/shard_map/ppermute | solution.py:321
  126.0 3.3 %shard_map.94 = bf16[720,1536]{1,0:T(8,128)(2,1)} custom-call(s32[9,8]{1,0:T(8,128)S(1)} %pad_add_fusion.meta, bf16[528,1536]{1,0:T(8,128)(2,1)S(1)} %shard_map.88.kept, bf16[112,1536]{1,0:T(8,128)(2,1)S(1)} %shard_map.89.early, bf16[416,512]{1,0:T(8,128)(2,1)S(1)} %collective-permute-done.8.rest_0_, bf16[416,1024]{1,0:T(8,128)(2,1)S(1)} %collective-permute-done.18.rest_1_), custom_call_target="tpu_custom_call" | custom-call | flops 1 | bytes 1 | tf_op jit(solution)/shard_map/pallas_call | solution.py:461
  129.3 6.1 %collective-permute-done.23.got = bf16[384,512]{1,0:T(8,128)(2,1)S(1)} collective-permute-done((bf16[384,512]{1,0:T(8,128)(2,1)S(1)}, bf16[384,512]{1,0:T(8,128)(2,1)S(1)}, u32[]{:S(2)}, u32[]{:S(2)}) %collective-permute-start.23) | collective-permute-done | bytes 393248 | tf_op jit(solution)/shard_map/ppermute | solution.py:321
  136.4 10.0 %collective-permute-done.24 = bf16[192,512]{1,0:T(8,128)(2,1)S(1)} collective-permute-done((bf16[192,512]{1,0:T(8,128)(2,1)S(1)}, bf16[192,512]{1,0:T(8,128)(2,1)S(1)}, u32[]{:S(2)}, u32[]{:S(2)}) %collective-permute-start.24) | collective-permute-done | bytes 196640 | tf_op jit(solution)/shard_map/ppermute | solution.py:321
  (54 shorter events, 17.6 us)
Async XLA Ops:
  6.0 13.5 %collective-permute-start.2 = (bf16[416,384]{1,0:T(8,128)(2,1)S(1)}, bf16[416,384]{1,0:T(8,128)(2,1)S(1)}, u32[]{:S(2)}, u32[]{:S(2)}) collective-permute-start(bf16[416,384]{1,0:T(8,128)(2,1)S(1)} %get-tuple-element.67.refs_0_), channel_id=1, source_target_pairs={{0,1},{1,0},{2,3},{3,2},{4,5},{5,4},{6,7},{7,6},{8,9},{9,8},{10,11... | collective-permute-start | bytes 958472 | tf_op jit(solution)/shard_map/ppermute | solution.py:321
  6.5 13.0 %collective-permute-start.1 = (bf16[416,384]{1,0:T(8,128)(2,1)S(1)}, bf16[416,384]{1,0:T(8,128)(2,1)S(1)}, u32[]{:S(2)}, u32[]{:S(2)}) collective-permute-start(bf16[416,384]{1,0:T(8,128)(2,1)S(1)} %get-tuple-element.67.refs_0_), channel_id=1, source_target_pairs={{0,2},{1,3},{2,0},{3,1},{4,6},{5,7},{6,4},{7,5},{8,10},{9,11},{10,... | collective-permute-start | bytes 958472 | tf_op jit(solution)/shard_map/ppermute | solution.py:321
  9.1 22.1 %collective-permute-start = (bf16[112,1920]{1,0:T(8,128)(2,1)S(1)}, bf16[112,1920]{1,0:T(8,128)(2,1)S(1)}, u32[]{:S(2)}, u32[]{:S(2)}) collective-permute-start(bf16[112,1920]{1,0:T(8,128)(2,1)S(1)} %get-tuple-element.65), channel_id=1, source_target_pairs={{0,16},{4,20},{8,24},{12,28},{16,0},{20,4},{24,8},{28,12},{1,17},{... | collective-permute-start | bytes 1290248 | tf_op jit(solution)/shard_map/ppermute | solution.py:321
  19.5 1.7 %collective-permute-start.4 = (bf16[416,384]{1,0:T(8,128)(2,1)S(1)}, bf16[416,384]{1,0:T(8,128)(2,1)S(1)}, u32[]{:S(2)}, u32[]{:S(2)}) collective-permute-start(bf16[416,384]{1,0:T(8,128)(2,1)S(1)} %collective-permute-done.1.refs_2_.refs_0_), channel_id=1, source_target_pairs={{0,1},{1,0},{2,3},{3,2},{4,5},{5,4},{6,7},{7,6},{8,9},{9,8},{10,11... | collective-permute-start | bytes 958472 | tf_op jit(solution)/shard_map/ppermute | solution.py:321
  19.6 16.0 %collective-permute-start.5 = (bf16[320,384]{1,0:T(8,128)(2,1)S(1)}, bf16[320,384]{1,0:T(8,128)(2,1)S(1)}, u32[]{:S(2)}, u32[]{:S(2)}) collective-permute-start(bf16[320,384]{1,0:T(8,128)(2,1)S(1)} %get-tuple-element.71.refs_1_.refs_0_), channel_id=1, source_target_pairs={{0,1},{1,0},{2,3},{3,2},{4,5},{5,4},{6,7},{7,6},{8,9},{9,8},{10,11... | collective-permute-start | bytes 737288 | tf_op jit(solution)/shard_map/ppermute | solution.py:321
  20.1 15.5 %collective-permute-start.6 = (bf16[320,384]{1,0:T(8,128)(2,1)S(1)}, bf16[320,384]{1,0:T(8,128)(2,1)S(1)}, u32[]{:S(2)}, u32[]{:S(2)}) collective-permute-start(bf16[320,384]{1,0:T(8,128)(2,1)S(1)} %get-tuple-element.80.refs_2_.refs_1_), channel_id=1, source_target_pairs={{0,1},{1,0},{2,3},{3,2},{4,5},{5,4},{6,7},{7,6},{8,9},{9,8},{10,11... | collective-permute-start | bytes 737288 | tf_op jit(solution)/shard_map/ppermute | solution.py:321
  20.2 17.4 %collective-permute-start.7 = (bf16[320,384]{1,0:T(8,128)(2,1)S(1)}, bf16[320,384]{1,0:T(8,128)(2,1)S(1)}, u32[]{:S(2)}, u32[]{:S(2)}) collective-permute-start(bf16[320,384]{1,0:T(8,128)(2,1)S(1)} %get-tuple-element.80.refs_2_.refs_1_), channel_id=1, source_target_pairs={{0,2},{1,3},{2,0},{3,1},{4,6},{5,7},{6,4},{7,5},{8,10},{9,11},{10,... | collective-permute-start | bytes 737288 | tf_op jit(solution)/shard_map/ppermute | solution.py:321
  21.2 16.4 %collective-permute-start.3 = (bf16[320,384]{1,0:T(8,128)(2,1)S(1)}, bf16[320,384]{1,0:T(8,128)(2,1)S(1)}, u32[]{:S(2)}, u32[]{:S(2)}) collective-permute-start(bf16[320,384]{1,0:T(8,128)(2,1)S(1)} %get-tuple-element.71.refs_1_.refs_0_), channel_id=1, source_target_pairs={{0,2},{1,3},{2,0},{3,1},{4,6},{5,7},{6,4},{7,5},{8,10},{9,11},{10,... | collective-permute-start | bytes 737288 | tf_op jit(solution)/shard_map/ppermute | solution.py:321
  31.2 21.1 %collective-permute-start.8 = (bf16[416,512]{1,0:T(8,128)(2,1)S(1)}, bf16[416,512]{1,0:T(8,128)(2,1)S(1)}, u32[]{:S(2)}, u32[]{:S(2)}) collective-permute-start(bf16[416,512]{1,0:T(8,128)(2,1)S(1)} %get-tuple-element.74), channel_id=1, source_target_pairs={{0,16},{4,20},{8,24},{12,28},{16,0},{20,4},{24,8},{28,12},{1,17},{... | collective-permute-start | bytes 1277960 | tf_op jit(solution)/shard_map/ppermute | solution.py:321
  37.6 14.7 %collective-permute-start.9 = (bf16[320,384]{1,0:T(8,128)(2,1)S(1)}, bf16[320,384]{1,0:T(8,128)(2,1)S(1)}, u32[]{:S(2)}, u32[]{:S(2)}) collective-permute-start(bf16[320,384]{1,0:T(8,128)(2,1)S(1)} %collective-permute-done.3.refs_1_.refs_4_), channel_id=1, source_target_pairs={{0,1},{1,0},{2,3},{3,2},{4,5},{5,4},{6,7},{7,6},{8,9},{9,8},{10,11... | collective-permute-start | bytes 737288 | tf_op jit(solution)/shard_map/ppermute | solution.py:321
  37.6 14.6 %collective-permute-start.10 = (bf16[320,384]{1,0:T(8,128)(2,1)S(1)}, bf16[320,384]{1,0:T(8,128)(2,1)S(1)}, u32[]{:S(2)}, u32[]{:S(2)}) collective-permute-start(bf16[320,384]{1,0:T(8,128)(2,1)S(1)} %collective-permute-done.7.refs_2_.refs_5_), channel_id=1, source_target_pairs={{0,1},{1,0},{2,3},{3,2},{4,5},{5,4},{6,7},{7,6},{8,9},{9,8},{10,11... | collective-permute-start | bytes 737288 | tf_op jit(solution)/shard_map/ppermute | solution.py:321
  38.1 29.9 %collective-permute-start.13 = (bf16[384,512]{1,0:T(8,128)(2,1)S(1)}, bf16[384,512]{1,0:T(8,128)(2,1)S(1)}, u32[]{:S(2)}, u32[]{:S(2)}) collective-permute-start(bf16[384,512]{1,0:T(8,128)(2,1)S(1)} %get-tuple-element.81), channel_id=1, source_target_pairs={{0,4},{4,0},{8,12},{12,8},{16,20},{20,16},{24,28},{28,24},{1,5},{5... | collective-permute-start | bytes 1179656 | tf_op jit(solution)/shard_map/ppermute | solution.py:321
  54.2 13.9 %collective-permute-start.14 = (bf16[384,512]{1,0:T(8,128)(2,1)S(1)}, bf16[384,512]{1,0:T(8,128)(2,1)S(1)}, u32[]{:S(2)}, u32[]{:S(2)}) collective-permute-start(bf16[384,512]{1,0:T(8,128)(2,1)S(1)} %get-tuple-element.87), channel_id=1, source_target_pairs={{0,4},{4,0},{8,12},{12,8},{16,20},{20,16},{24,28},{28,24},{1,5},{5... | collective-permute-start | bytes 1179656 | tf_op jit(solution)/shard_map/ppermute | solution.py:321
  58.6 48.5 %collective-permute-start.17 = (bf16[768,512]{1,0:T(8,128)(2,1)S(1)}, bf16[768,512]{1,0:T(8,128)(2,1)S(1)}, u32[]{:S(2)}, u32[]{:S(2)}) collective-permute-start(bf16[768,512]{1,0:T(8,128)(2,1)S(1)} %get-tuple-element.94), channel_id=1, source_target_pairs={{0,4},{4,0},{8,12},{12,8},{16,20},{20,16},{24,28},{28,24},{1,5},{5... | collective-permute-start | bytes 2359304 | tf_op jit(solution)/shard_map/ppermute | solution.py:321
  59.3 5.7 %collective-permute-start.11 = (bf16[112,384]{1,0:T(8,128)(2,1)S(1)}, bf16[112,384]{1,0:T(8,128)(2,1)S(1)}, u32[]{:S(2)}, u32[]{:S(2)}) collective-permute-start(bf16[112,384]{1,0:T(8,128)(2,1)S(1)} %slice.4), channel_id=1, source_target_pairs={{0,2},{1,3},{2,0},{3,1},{4,6},{5,7},{6,4},{7,5},{8,10},{9,11},{10,... | collective-permute-start | bytes 258056 | tf_op jit(solution)/shard_map/ppermute | solution.py:321
  60.5 47.5 %collective-permute-start.18 = (bf16[416,1024]{1,0:T(8,128)(2,1)S(1)}, bf16[416,1024]{1,0:T(8,128)(2,1)S(1)}, u32[]{:S(2)}, u32[]{:S(2)}) collective-permute-start(bf16[416,1024]{1,0:T(8,128)(2,1)S(1)} %get-tuple-element.75), channel_id=1, source_target_pairs={{0,16},{4,20},{8,24},{12,28},{16,0},{20,4},{24,8},{28,12},{1,17},{... | collective-permute-start | bytes 2555912 | tf_op jit(solution)/shard_map/ppermute | solution.py:321
  65.0 7.7 %collective-permute-start.15 = (bf16[112,384]{1,0:T(8,128)(2,1)S(1)}, bf16[112,384]{1,0:T(8,128)(2,1)S(1)}, u32[]{:S(2)}, u32[]{:S(2)}) collective-permute-start(bf16[112,384]{1,0:T(8,128)(2,1)S(1)} %collective-permute-done.11.p2), channel_id=1, source_target_pairs={{0,1},{1,0},{2,3},{3,2},{4,5},{5,4},{6,7},{7,6},{8,9},{9,8},{10,11... | collective-permute-start | bytes 258056 | tf_op jit(solution)/shard_map/ppermute | solution.py:321
  76.2 35.9 %collective-permute-start.19 = (bf16[768,512]{1,0:T(8,128)(2,1)S(1)}, bf16[768,512]{1,0:T(8,128)(2,1)S(1)}, u32[]{:S(2)}, u32[]{:S(2)}) collective-permute-start(bf16[768,512]{1,0:T(8,128)(2,1)S(1)} %get-tuple-element.117), channel_id=1, source_target_pairs={{0,4},{4,0},{8,12},{12,8},{16,20},{20,16},{24,28},{28,24},{1,5},{5... | collective-permute-start | bytes 2359304 | tf_op jit(solution)/shard_map/ppermute | solution.py:321
  77.8 29.2 %collective-permute-start.16 = (bf16[384,512]{1,0:T(8,128)(2,1)S(1)}, bf16[384,512]{1,0:T(8,128)(2,1)S(1)}, u32[]{:S(2)}, u32[]{:S(2)}) collective-permute-start(bf16[384,512]{1,0:T(8,128)(2,1)S(1)} %get-tuple-element.103), channel_id=1, source_target_pairs={{0,8},{4,12},{8,0},{12,4},{16,24},{20,28},{24,16},{28,20},{1,9},{5... | collective-permute-start | bytes 1179656 | tf_op jit(solution)/shard_map/ppermute | solution.py:321
  108.0 16.3 %collective-permute-start.20 = (bf16[384,512]{1,0:T(8,128)(2,1)S(1)}, bf16[384,512]{1,0:T(8,128)(2,1)S(1)}, u32[]{:S(2)}, u32[]{:S(2)}) collective-permute-start(bf16[384,512]{1,0:T(8,128)(2,1)S(1)} %get-tuple-element.111), channel_id=1, source_target_pairs={{0,8},{4,12},{8,0},{12,4},{16,24},{20,28},{24,16},{28,20},{1,9},{5... | collective-permute-start | bytes 1179656 | tf_op jit(solution)/shard_map/ppermute | solution.py:321
  108.9 17.0 %collective-permute-start.21 = (bf16[192,512]{1,0:T(8,128)(2,1)S(1)}, bf16[192,512]{1,0:T(8,128)(2,1)S(1)}, u32[]{:S(2)}, u32[]{:S(2)}) collective-permute-start(bf16[192,512]{1,0:T(8,128)(2,1)S(1)} %get-tuple-element.114), channel_id=1, source_target_pairs={{0,16},{4,20},{8,24},{12,28},{16,0},{20,4},{24,8},{28,12},{1,17},{... | collective-permute-start | bytes 589832 | tf_op jit(solution)/shard_map/ppermute | solution.py:321
  113.1 22.3 %collective-permute-start.23 = (bf16[384,512]{1,0:T(8,128)(2,1)S(1)}, bf16[384,512]{1,0:T(8,128)(2,1)S(1)}, u32[]{:S(2)}, u32[]{:S(2)}) collective-permute-start(bf16[384,512]{1,0:T(8,128)(2,1)S(1)} %get-tuple-element.118), channel_id=1, source_target_pairs={{0,8},{4,12},{8,0},{12,4},{16,24},{20,28},{24,16},{28,20},{1,9},{5... | collective-permute-start | bytes 1179656 | tf_op jit(solution)/shard_map/ppermute | solution.py:321
  125.1 11.2 %collective-permute-start.22 = (bf16[192,512]{1,0:T(8,128)(2,1)S(1)}, bf16[192,512]{1,0:T(8,128)(2,1)S(1)}, u32[]{:S(2)}, u32[]{:S(2)}) collective-permute-start(bf16[192,512]{1,0:T(8,128)(2,1)S(1)} %get-tuple-element.121), channel_id=1, source_target_pairs={{0,16},{4,20},{8,24},{12,28},{16,0},{20,4},{24,8},{28,12},{1,17},{... | collective-permute-start | bytes 589832 | tf_op jit(solution)/shard_map/ppermute | solution.py:321
  136.1 10.2 %collective-permute-start.24 = (bf16[192,512]{1,0:T(8,128)(2,1)S(1)}, bf16[192,512]{1,0:T(8,128)(2,1)S(1)}, u32[]{:S(2)}, u32[]{:S(2)}) collective-permute-start(bf16[192,512]{1,0:T(8,128)(2,1)S(1)} %get-tuple-element.127), channel_id=1, source_target_pairs={{0,16},{4,20},{8,24},{12,28},{16,0},{20,4},{24,8},{28,12},{1,17},{... | collective-permute-start | bytes 589832 | tf_op jit(solution)/shard_map/ppermute | solution.py:321
  (2 other events, 22.2 us)

commit v6 on v5

--- a/solution.py
+++ b/solution.py
@@ -11,7 +11,7 @@
 SEND = 528
 KEEP = 528
 TILE = 16
-EARLY = 112
+EARLY = 80
 LATE = SEND - EARLY
 SLOTS = 4
 BAL = 720
@@ -107,7 +107,7 @@
     return (rows * own[None, :]).astype(BF)
 
 
-def first_kernel(meta, cot_hbm, scale_hbm, pre_hbm, late_out, early_out, rest_a, rest_b, cot, scale, pre, sems):
+def first_kernel(meta, cot_hbm, scale_hbm, pre_hbm, late_out, early_out, rest_out, rest_a, rest_b, cot, scale, pre, sems):
     width = cot.shape[1]
     home = cot.shape[0]
     pairs = ((cot_hbm, cot), (scale_hbm, scale), (pre_hbm, pre))
@@ -120,6 +120,8 @@
     early_rows = scaled_rows(meta, early, cot, scale)
     early_out[:, :width] = early_rows
     kept_rows = scaled_rows(meta, kept_picks(meta, home), cot, scale)
+    rest_out[0:EARLY, :] = early_rows
+    rest_out[EARLY:, :] = kept_rows
     cut = rest_a.shape[0] - EARLY
     rest_a[0:EARLY, :] = early_rows
     rest_a[EARLY:, :] = kept_rows[:cut]
@@ -291,14 +293,13 @@
     lax.fori_loop(0, half // step, body, 0)
 
 
-def place_kernel(cuts, meta, kept, early, *rest):
-    lates, out = rest[:-1], rest[-1]
-    count = kept_total(meta, dp_at(meta))
+def place_kernel(meta, kept, early, inner, outer, out):
+    d = dp_at(meta)
+    count = kept_total(meta, d)
     first = jnp.minimum(count - lax.rem(count, TILE), BAL - SEND)
     first = pl.multiple_of(first, TILE)
     wide = out.shape[1]
-    step = pl.program_id(0)
-    columns = pl.ds(pl.multiple_of(step * wide, wide), wide)
+    columns = pl.ds(pl.multiple_of(pl.program_id(0) * wide, wide), wide)
     out[0:KEEP, :] = kept[:, columns]
     out[KEEP:, :] = jnp.zeros((out.shape[0] - KEEP, wide), BF)
 
@@ -308,17 +309,17 @@
         out[window, :] = jnp.where(rows < count, out[window, :], block)
 
     put(early[:, columns], first)
-    sources = [(late, c) for late, cut in zip(lates, cuts) for c in range(0, cut, wide)]
-    for i, (late, c) in enumerate(sources):
-
-        @pl.when(step == i)
-        def _():
-            put(late[:, c : c + wide], pl.multiple_of(first + EARLY, TILE))
+    is_inner = (d // 2 == 1) | (d // 2 == 2)
+    put(jnp.where(is_inner, inner[:, columns], outer[:, columns]), pl.multiple_of(first + EARLY, TILE))
 
 
 def swapped(block, axis, distance):
     n = lax.axis_size(axis)
     return lax.ppermute(block, axis, [(i, i ^ distance) for i in range(n)])
+
+
+def routed(block, pairs):
+    return lax.ppermute(block, "dp", [(2 * a + x, 2 * b + x) for a, b in pairs for x in range(2)])
 
 
 def after(value, *others):
@@ -394,64 +395,65 @@
         )(meta, mine, got)
 
     cut = others // 2
-    late, early, *rest = kernel_call(
+    late, early, rest, *rest_blocks = kernel_call(
         first_kernel,
-        [shape(LATE, width), shape(EARLY, width + ff), shape(cut, width), shape(others - cut, width)],
-        [IN_HBM] * 3, [IN_VMEM] * 4,
+        [shape(r, c) for r, c in ((LATE, width), (EARLY, width + ff), (others, width), (cut, width), (others - cut, width))],
+        [IN_HBM] * 3, [IN_VMEM] * 5,
         [vmem((home, width), BF), vmem((features,), F32), vmem((home, ff), BF), sems((3,))],
     )(meta, cotangent, layer_scale, hidden_pre)
     arrived_early = swapped(early, "dp", n // 2)
     late_c, late_y = swapped(late, "tensor", 1), swapped(late, "tensor", 2)
     act_late, der_late = gelu(after(meta, late), True, 0, ff)
 
-    late_y = after(late_y, act_late, late_c)
+    late_y = after(late_y, act_late, late_c, arrived_early)
     late_yc = swapped(late_y, "tensor", 1)
-    rest_sent = [after(block, late_y) for block in rest]
-    rest_y = [swapped(block, "tensor", 2) for block in rest_sent]
-    rest_c = [swapped(block, "tensor", 1) for block in rest_sent]
+    rest_y = [swapped(after(block, late_y), "tensor", 2) for block in rest_blocks]
+    rest_c = swapped(after(rest, late_y), "tensor", 1)
 
     lates = ([late], [late_c], [late_y], [late_yc])
-    moves = (512, ff - 512)
-    moving = grads(after(meta, late_y), lates, 0, LATE, (der_late,), moves)
-    arrived = [swapped(block, "dp", n // 2) for block in moving]
-
-    act_a, der_a = gelu(after(meta, *moving, arrived_early), False, 0, part)
-    rests = (rest, rest_c)
+    (moving,) = grads(after(meta, late_y), lates, 0, LATE, (der_late,), (ff,))
+    from_outer = routed(moving, ((0, 1), (3, 2)))
+    from_inner = routed(moving, ((1, 2), (2, 1)))
+
+    act_a, der_a = gelu(after(meta, moving), False, 0, part)
+    rests = ([rest], [rest_c])
     send_01, keep_01, *lhs_01 = weight_part(after(meta, act_a), (0, 1), act_a)
     got_01 = swapped(send_01, "dp", 1)
-    rest_y = [after(block, send_01) for block in rest_y]
+    act_b, der_b = gelu(after(meta, send_01), False, part, part)
+    rest_y = [after(block, act_b) for block in rest_y]
     rest_yc = [swapped(block, "tensor", 1) for block in rest_y]
-    rests = (rest, rest_c, rest_y, rest_yc)
-
-    act_b, der_b = gelu(after(meta, *rest_y), False, part, part)
-    send_23, keep_23, *lhs_23 = weight_part(after(meta, act_b, arrived[0]), (2, 3), act_a)
+    rests = ([rest], [rest_c], rest_y, rest_yc)
+    send_23, keep_23, *lhs_23 = weight_part(after(meta, act_b, got_01), (2, 3), act_a)
     got_23 = swapped(send_23, "dp", 1)
-    early_sent = after(arrived_early[:, :width], send_23)
-    early_c, early_y = swapped(early_sent, "tensor", 1), swapped(early_sent, "tensor", 2)
     send_b, keep_b = weight_again(after(meta, send_23), part, act_b)
     got_b = swapped(send_b, "dp", 1)
-    act_c, der_c = gelu(after(meta, send_b), False, 2 * part, part)
-    early_y = after(early_y, act_c, early_c)
+
+    out_na, mine_a = near_step(after(meta, send_b), (keep_01, keep_23), (got_01, got_23))
+    got_na = swapped(out_na, "dp", 2)
+    arrived_inner = routed(after(from_outer, out_na), ((1, 2), (2, 1)))
+    arrived_outer = routed(after(from_inner, out_na), ((2, 3), (1, 0)))
+
+    act_c, der_c = gelu(after(meta, out_na), False, 2 * part, part)
+    early_sent = after(arrived_early[:, :width], act_c)
+    early_c, early_y = swapped(early_sent, "tensor", 1), swapped(early_sent, "tensor", 2)
+    send_c, keep_c = weight_again(after(meta, act_c), 2 * part, act_c)
+    out_nb, mine_b = near_step(after(meta, send_c, got_na), (keep_b,), (got_b,))
+    got_nb = swapped(out_nb, "dp", 2)
+    got_c = swapped(after(send_c, out_nb), "dp", 1)
+
+    (kept_grad,) = grads(after(meta, out_nb), rests, EARLY, KEEP, (der_a, der_b, der_c), (ff,))
+    early_y = after(early_y, kept_grad, early_c)
     early_yc = swapped(early_y, "tensor", 1)
-    send_c, keep_c = weight_again(after(meta, early_y), 2 * part, act_c)
-
-    out_na, mine_a = near_step(after(meta, send_c), (keep_01, keep_23), (got_01, got_23))
-    got_na = swapped(out_na, "dp", 2)
-    (kept_grad,) = grads(after(meta, out_na), rests, EARLY, KEEP, (der_a, der_b, der_c), (ff,))
-
     early_grad = kernel_call(
         functools.partial(early_kernel, 256), shape(EARLY, ff), [IN_VMEM] * 5, IN_VMEM,
         [vmem((EARLY, features), BF), vmem((EARLY, 256), F32)],
     )(after(meta, kept_grad), arrived_early, early_c, early_y, early_yc, down_weight)
 
-    out_nb, mine_b = near_step(after(meta, early_grad, got_na), (keep_b,), (got_b,))
-    got_nb = swapped(out_nb, "dp", 2)
-    got_c = swapped(after(send_c, early_grad), "dp", 1)
-    out_fa, own_a = far_step(after(meta, out_nb, arrived[1]), mine_a, got_na)
+    out_fa, own_a = far_step(after(meta, early_grad, arrived_inner, arrived_outer), mine_a, got_na)
     got_fa = swapped(out_fa, "dp", 4)
     out_nc, mine_c = near_step(after(meta, out_fa), (keep_c,), (got_c,))
     got_nc = swapped(out_nc, "dp", 2)
-    out_fb, own_b = far_step(after(meta, out_nc), mine_b, got_nb)
+    out_fb, own_b = far_step(after(meta, out_nc, got_fa), mine_b, got_nb)
     got_fb = swapped(out_fb, "dp", 4)
     out_fc, own_c = far_step(after(meta, out_fb), mine_c, got_nc)
     got_fc = swapped(out_fc, "dp", 4)
@@ -459,9 +461,9 @@
     down_grad = jnp.concatenate(total, axis=1) / math.sqrt(n * home)
 
     hidden_grad = kernel_call(
-        functools.partial(place_kernel, moves), shape(BAL, ff), [IN_VMEM] * (2 + len(moves)),
+        place_kernel, shape(BAL, ff), [IN_VMEM] * 4,
         pl.BlockSpec((BAL, 256), lambda i, *_: (0, i)), grid=(ff // 256,),
-    )(after(meta, out_fb), kept_grad, early_grad, *arrived)
+    )(after(meta, out_fb), kept_grad, early_grad, arrived_inner, arrived_outer)
     return (hidden_grad, down_grad)
 
 

time: 148 us -> 158 us (1.068)
  starting transfers between devices: 20.7 us -> 28.7 us
  waiting for transfers between devices: 70.1 us -> 72.5 us
    ppermute x0 -> x4, starting transfers between devices: none -> 5.88 us  [routed(): lax.ppermute(block, 'dp', [(2 * a + x, 2 * b + x) for a, b in pairs for x...]
    ppermute x25 -> x22, waiting for transfers between devices: 70.1 us -> 72.5 us  [swapped(): return lax.ppermute(block, axis, [(i, i ^ distance) for i in range(n)])]
    ppermute x25 -> x22, starting transfers between devices: 20.7 us -> 22.8 us  [swapped(): return lax.ppermute(block, axis, [(i, i ^ distance) for i in range(n)])]
  transfers between devices with their start and end apart: 25 -> 26, of which waited for: 8 -> 12; matrix products, arithmetic and copies ran while one was open for 0% -> 0% of each run, Pallas kernels for 33% -> 29%
where the time goes in v6:
time: 158 us
  waiting for transfers between devices  72.5 us (46%)
  Pallas kernels  53.5 us (34%)
  starting transfers between devices  28.7 us (18%)
  other arithmetic  1.99 us (1%)
    ppermute x22, waiting for transfers between devices, swapped(): return lax.ppermute(block, axis, [(i, i ^ distance) for i in range(n)])  72.5 us
    ppermute x22, starting transfers between devices, swapped(): return lax.ppermute(block, axis, [(i, i ^ distance) for i in range(n)])  22.8 us
    pallas_call x4, Pallas kernels, gelu(): kernel_call(functools.partial(gelu_kernel, late, base, block), [shape(row...  21 us
    pallas_call x2, Pallas kernels, grads(): kernel_call(functools.partial(grad_kernel, counts, first_row, 256), [shap...  6.52 us
    ppermute x4, starting transfers between devices, routed(): lax.ppermute(block, 'dp', [(2 * a + x, 2 * b + x) for a, b in pairs for x...  5.88 us
    pallas_call x2, Pallas kernels, weight_again(): kernel_call(functools.partial(weight_again_kernel, base), [shape(4 * half...  5.7 us
    pallas_call x1, Pallas kernels, shards(): kernel_call(first_kernel, [shape(r, c) for r, c in ((LATE, width), (EARLY...  4.69 us
    pallas_call x2, Pallas kernels, weight_part(): kernel_call(functools.partial(weight_kernel, counts, 0), [shape(count * h...  3.82 us
  transfers between devices with their start and end apart: 26, of which 12 were waited for; matrix products, arithmetic and copies ran while one was open for 0% of the time, Pallas kernels for 29%

profile of v6, /device:TPU:0, one launch (start us, length us, event | category | flops | bytes accessed | tf_op | source)
XLA Modules:
  0.0 157.7 jit_solution(5329333428134863295)
XLA Ops:
  1.4 4.7 %shard_map.77 = (bf16[448,384]{1,0:T(8,128)(2,1)S(1)}, bf16[80,1920]{1,0:T(8,128)(2,1)S(1)}, bf16[608,384]{1,0:T(8,128)(2,1)S(1)}, bf16[304,384]{1,0:T(8,128)(2,1)S(1)}, bf16[304,384]{1,0:T(8,128)(2,1)S(1)}) custom-call(s32[9,8]{1,0:T(8,128)S(1)} %pad_add_fusion.meta, bf16[1032,384]{1,0:T(8,128)(2,1)} %cot_hbm.1, f32[1536]{0:T(1024)} %scale_hbm.1, ...), custom_call_target="tpu_custom_call" | custom-call | flops 1 | bytes 1 | tf_op jit(solution)/shard_map/pallas_call | solution.py:398
  6.1 3.0 %collective-permute-start = (bf16[448,384]{1,0:T(8,128)(2,1)S(1)}, bf16[448,384]{1,0:T(8,128)(2,1)S(1)}, u32[]{:S(2)}, u32[]{:S(2)}) collective-permute-start(bf16[448,384]{1,0:T(8,128)(2,1)S(1)} %get-tuple-element.67.refs_0_), channel_id=1, source_target_pairs={{0,2},{1,3},{2,0},{3,1},{4,6},{5,7},{6,4},{7,5},{8,10},{9,11},{10,... | collective-permute-start | bytes 1032200 | tf_op jit(solution)/shard_map/ppermute | solution.py:318
  9.1 2.6 %collective-permute-start.2 = (bf16[80,1920]{1,0:T(8,128)(2,1)S(1)}, bf16[80,1920]{1,0:T(8,128)(2,1)S(1)}, u32[]{:S(2)}, u32[]{:S(2)}) collective-permute-start(bf16[80,1920]{1,0:T(8,128)(2,1)S(1)} %get-tuple-element.70), channel_id=1, source_target_pairs={{0,16},{4,20},{8,24},{12,28},{16,0},{20,4},{24,8},{28,12},{1,17},{... | collective-permute-start | bytes 921608 | tf_op jit(solution)/shard_map/ppermute | solution.py:318
  11.7 7.7 %shard_map.78 = (bf16[448,1536]{1,0:T(8,128)(2,1)S(1)}, f32[448,1536]{1,0:T(8,128)S(1)}) custom-call(s32[9,8]{1,0:T(8,128)S(1)} %pad_add_fusion.meta, bf16[1032,1536]{1,0:T(8,128)(2,1)} %pre_hbm.9), custom_call_target="tpu_custom_call" | custom-call | flops 1 | bytes 1 | tf_op jit(solution)/shard_map/pallas_call | solution.py:350
  19.4 6.9 %collective-permute-done.2.own = bf16[80,1920]{1,0:T(8,128)(2,1)S(1)} collective-permute-done((bf16[80,1920]{1,0:T(8,128)(2,1)S(1)}, bf16[80,1920]{1,0:T(8,128)(2,1)S(1)}, u32[]{:S(2)}, u32[]{:S(2)}) %collective-permute-start.2) | collective-permute-done | bytes 307232 | tf_op jit(solution)/shard_map/ppermute | solution.py:318
  27.9 3.1 %shard_map.79 = bf16[448,1536]{1,0:T(8,128)(2,1)S(1)} custom-call(s32[9,8]{1,0:T(8,128)S(1)} %pad_add_fusion.meta, bf16[448,384]{1,0:T(8,128)(2,1)S(1)} %get-tuple-element.67.refs_0_, bf16[448,384]{1,0:T(8,128)(2,1)S(1)} %collective-permute-done.1.refs_1_.refs_2_, bf16[448,384]{1,0:T(8,128)(2,1)S(1)} %collective-permute-done.refs_2_.refs_0_, ...), custom_call_target="tpu_custom_call" | custom-call | flops 1 | bytes 1 | tf_op jit(solution)/shard_map/pallas_call | solution.py:379
  31.0 2.7 %collective-permute-start.16 = (bf16[448,1536]{1,0:T(8,128)(2,1)S(1)}, bf16[448,1536]{1,0:T(8,128)(2,1)S(1)}, u32[]{:S(2)}, u32[]{:S(2)}) collective-permute-start(bf16[448,1536]{1,0:T(8,128)(2,1)S(1)} %shard_map.79), channel_id=1, source_target_pairs={{0,8},{4,12},{24,16},{28,20},{1,9},{5,13},{25,17},{29,21},{2,10},{... | collective-permute-start | bytes 4128776 | tf_op jit(solution)/shard_map/ppermute | solution.py:322
  36.8 4.4 %shard_map.80 = (bf16[608,512]{1,0:T(8,128)(2,1)S(1)}, f32[608,512]{1,0:T(8,128)S(1)}) custom-call(s32[9,8]{1,0:T(8,128)S(1)} %pad_add_fusion.meta, bf16[1032,1536]{1,0:T(8,128)(2,1)} %pre_hbm.9), custom_call_target="tpu_custom_call" | custom-call | flops 1 | bytes 1 | tf_op jit(solution)/shard_map/pallas_call | solution.py:350
  44.7 4.4 %shard_map.82 = (bf16[608,512]{1,0:T(8,128)(2,1)S(1)}, f32[608,512]{1,0:T(8,128)S(1)}) custom-call(s32[9,8]{1,0:T(8,128)S(1)} %pad_add_fusion.meta, bf16[1032,1536]{1,0:T(8,128)(2,1)} %pre_hbm.9), custom_call_target="tpu_custom_call" | custom-call | flops 1 | bytes 1 | tf_op jit(solution)/shard_map/pallas_call | solution.py:350
  49.8 4.4 %collective-permute-done.5.refs_2_ = bf16[384,512]{1,0:T(8,128)(2,1)S(1)} collective-permute-done((bf16[384,512]{1,0:T(8,128)(2,1)S(1)}, bf16[384,512]{1,0:T(8,128)(2,1)S(1)}, u32[]{:S(2)}, u32[]{:S(2)}) %collective-permute-start.5) | collective-permute-done | bytes 393248 | tf_op jit(solution)/shard_map/ppermute | solution.py:318
  54.1 1.9 %shard_map.83 = (bf16[384,512]{1,0:T(8,128)(2,1)S(1)}, f32[384,512]{1,0:T(8,128)S(1)}, bf16[768,448]{1,0:T(8,128)(2,1)S(1)}, bf16[768,608]{1,0:T(8,128)(2,1)S(1)}) custom-call(s32[9,8]{1,0:T(8,128)S(1)} %pad_add_fusion.meta, bf16[448,384]{1,0:T(8,128)(2,1)S(1)} %collective-permute-done.refs_2_.refs_0_, ...), custom_call_target="tpu_custom_call" | custom-call | flops 1 | bytes 1 | tf_op jit(solution)/shard_map/pallas_call | solution.py:363
  57.6 2.8 %shard_map.84 = (bf16[768,512]{1,0:T(8,128)(2,1)S(1)}, f32[768,512]{1,0:T(8,128)S(1)}) custom-call(s32[9,8]{1,0:T(8,128)S(1)} %pad_add_fusion.meta, bf16[768,448]{1,0:T(8,128)(2,1)S(1)} %get-tuple-element.91.late_01, bf16[768,608]{1,0:T(8,128)(2,1)S(1)} %get-tuple-element.92.rest_01, bf16[768,448]{1,0:T(8,128)(2,1)S(1)} %get-tuple-element.93.late_23, ...), custom_call_target="tpu_custom_call" | custom-call | flops 1 | bytes 1 | tf_op jit(solution)/shard_map/pallas_call | solution.py:371
  61.1 7.1 %collective-permute-done.10.refs_3_ = bf16[384,512]{1,0:T(8,128)(2,1)S(1)} collective-permute-done((bf16[384,512]{1,0:T(8,128)(2,1)S(1)}, bf16[384,512]{1,0:T(8,128)(2,1)S(1)}, u32[]{:S(2)}, u32[]{:S(2)}) %collective-permute-start.10) | collective-permute-done | bytes 393248 | tf_op jit(solution)/shard_map/ppermute | solution.py:318
  71.4 3.8 %collective-permute-start.11 = (bf16[384,512]{1,0:T(8,128)(2,1)S(1)}, bf16[384,512]{1,0:T(8,128)(2,1)S(1)}, u32[]{:S(2)}, u32[]{:S(2)}) collective-permute-start(bf16[384,512]{1,0:T(8,128)(2,1)S(1)} %get-tuple-element.99), channel_id=1, source_target_pairs={{0,8},{4,12},{8,0},{12,4},{16,24},{20,28},{24,16},{28,20},{1,9},{5... | collective-permute-start | bytes 1179656 | tf_op jit(solution)/shard_map/ppermute | solution.py:318
  75.2 4.4 %shard_map.86 = (bf16[608,512]{1,0:T(8,128)(2,1)S(1)}, f32[608,512]{1,0:T(8,128)S(1)}) custom-call(s32[9,8]{1,0:T(8,128)S(1)} %pad_add_fusion.meta, bf16[1032,1536]{1,0:T(8,128)(2,1)} %pre_hbm.9), custom_call_target="tpu_custom_call" | custom-call | flops 1 | bytes 1 | tf_op jit(solution)/shard_map/pallas_call | solution.py:350
  79.6 2.9 %shard_map.87 = (bf16[768,512]{1,0:T(8,128)(2,1)S(1)}, f32[768,512]{1,0:T(8,128)S(1)}) custom-call(s32[9,8]{1,0:T(8,128)S(1)} %pad_add_fusion.meta, bf16[768,448]{1,0:T(8,128)(2,1)S(1)} %get-tuple-element.91.late_01, bf16[768,608]{1,0:T(8,128)(2,1)S(1)} %get-tuple-element.92.rest_01, bf16[768,448]{1,0:T(8,128)(2,1)S(1)} %get-tuple-element.93.late_23, ...), custom_call_target="tpu_custom_call" | custom-call | flops 1 | bytes 1 | tf_op jit(solution)/shard_map/pallas_call | solution.py:371
  82.5 26.9 %collective-permute-done.11.got = bf16[384,512]{1,0:T(8,128)(2,1)S(1)} collective-permute-done((bf16[384,512]{1,0:T(8,128)(2,1)S(1)}, bf16[384,512]{1,0:T(8,128)(2,1)S(1)}, u32[]{:S(2)}, u32[]{:S(2)}) %collective-permute-start.11) | collective-permute-done | bytes 393248 | tf_op jit(solution)/shard_map/ppermute | solution.py:318
  110.3 2.5 %collective-permute-start.20 = (bf16[768,512]{1,0:T(8,128)(2,1)S(1)}, bf16[768,512]{1,0:T(8,128)(2,1)S(1)}, u32[]{:S(2)}, u32[]{:S(2)}) collective-permute-start(bf16[768,512]{1,0:T(8,128)(2,1)S(1)} %get-tuple-element.121), channel_id=1, source_target_pairs={{0,4},{4,0},{8,12},{12,8},{16,20},{20,16},{24,28},{28,24},{1,5},{5... | collective-permute-start | bytes 2359304 | tf_op jit(solution)/shard_map/ppermute | solution.py:318
  114.6 3.5 %shard_map.89.kept = bf16[528,1536]{1,0:T(8,128)(2,1)S(1)} custom-call(s32[9,8]{1,0:T(8,128)S(1)} %pad_add_fusion.meta, bf16[608,384]{1,0:T(8,128)(2,1)S(1)} %get-tuple-element.78.refs_1_.refs_0_, bf16[608,384]{1,0:T(8,128)(2,1)S(1)} %collective-permute-done.4.refs_3_.refs_1_, bf16[304,384]{1,0:T(8,128)(2,1)S(1)} %collective-permute-done.6.refs_1_.refs_2_, ...), custom_call_target="tpu_custom_call" | custom-call | flops 1 | bytes 1 | tf_op jit(solution)/shard_map/pallas_call | solution.py:379
  119.6 3.3 %shard_map.90.early = bf16[80,1536]{1,0:T(8,128)(2,1)S(1)} custom-call(s32[9,8]{1,0:T(8,128)S(1)} %pad_add_fusion.meta, bf16[80,1920]{1,0:T(8,128)(2,1)S(1)} %collective-permute-done.2.own, bf16[80,384]{1,0:T(8,128)(2,1)S(1)} %collective-permute-done.13.p1, bf16[80,384]{1,0:T(8,128)(2,1)S(1)} %collective-permute-done.14.p2, ...), custom_call_target="tpu_custom_call" | custom-call | flops 1 | bytes 1 | tf_op jit(solution)/shard_map/pallas_call | solution.py:447
  126.7 9.2 %collective-permute-done.21 = bf16[192,512]{1,0:T(8,128)(2,1)S(1)} collective-permute-done((bf16[192,512]{1,0:T(8,128)(2,1)S(1)}, bf16[192,512]{1,0:T(8,128)(2,1)S(1)}, u32[]{:S(2)}, u32[]{:S(2)}) %collective-permute-start.21) | collective-permute-done | bytes 196640 | tf_op jit(solution)/shard_map/ppermute | solution.py:318
  136.8 3.3 %shard_map.94 = bf16[720,1536]{1,0:T(8,128)(2,1)} custom-call(s32[9,8]{1,0:T(8,128)S(1)} %pad_add_fusion.meta, bf16[528,1536]{1,0:T(8,128)(2,1)S(1)} %shard_map.89.kept, bf16[80,1536]{1,0:T(8,128)(2,1)S(1)} %shard_map.90.early, bf16[448,1536]{1,0:T(8,128)(2,1)S(1)} %collective-permute-done.17.inner, bf16[448,1536]{1,0:T(8,128)(2,1)S(1)} %collective-permute-done.19.outer), custom_call_target="tpu_custom_call" | custom-call | flops 1 | bytes 1 | tf_op jit(solution)/shard_map/pallas_call | solution.py:463
  144.0 9.7 %collective-permute-done.23 = bf16[192,512]{1,0:T(8,128)(2,1)S(1)} collective-permute-done((bf16[192,512]{1,0:T(8,128)(2,1)S(1)}, bf16[192,512]{1,0:T(8,128)(2,1)S(1)}, u32[]{:S(2)}, u32[]{:S(2)}) %collective-permute-start.23) | collective-permute-done | bytes 196640 | tf_op jit(solution)/shard_map/ppermute | solution.py:318
  153.7 2.7 %collective-permute-done.25 = bf16[192,512]{1,0:T(8,128)(2,1)S(1)} collective-permute-done((bf16[192,512]{1,0:T(8,128)(2,1)S(1)}, bf16[192,512]{1,0:T(8,128)(2,1)S(1)}, u32[]{:S(2)}, u32[]{:S(2)}) %collective-permute-start.25) | collective-permute-done | bytes 196640 | tf_op jit(solution)/shard_map/ppermute | solution.py:318
  (56 shorter events, 28.9 us)
Async XLA Ops:
  6.1 20.2 %collective-permute-start = (bf16[448,384]{1,0:T(8,128)(2,1)S(1)}, bf16[448,384]{1,0:T(8,128)(2,1)S(1)}, u32[]{:S(2)}, u32[]{:S(2)}) collective-permute-start(bf16[448,384]{1,0:T(8,128)(2,1)S(1)} %get-tuple-element.67.refs_0_), channel_id=1, source_target_pairs={{0,2},{1,3},{2,0},{3,1},{4,6},{5,7},{6,4},{7,5},{8,10},{9,11},{10,... | collective-permute-start | bytes 1032200 | tf_op jit(solution)/shard_map/ppermute | solution.py:318
  9.1 17.2 %collective-permute-start.1 = (bf16[448,384]{1,0:T(8,128)(2,1)S(1)}, bf16[448,384]{1,0:T(8,128)(2,1)S(1)}, u32[]{:S(2)}, u32[]{:S(2)}) collective-permute-start(bf16[448,384]{1,0:T(8,128)(2,1)S(1)} %get-tuple-element.67.refs_0_), channel_id=1, source_target_pairs={{0,1},{1,0},{2,3},{3,2},{4,5},{5,4},{6,7},{7,6},{8,9},{9,8},{10,11... | collective-permute-start | bytes 1032200 | tf_op jit(solution)/shard_map/ppermute | solution.py:318
  9.1 17.2 %collective-permute-start.2 = (bf16[80,1920]{1,0:T(8,128)(2,1)S(1)}, bf16[80,1920]{1,0:T(8,128)(2,1)S(1)}, u32[]{:S(2)}, u32[]{:S(2)}) collective-permute-start(bf16[80,1920]{1,0:T(8,128)(2,1)S(1)} %get-tuple-element.70), channel_id=1, source_target_pairs={{0,16},{4,20},{8,24},{12,28},{16,0},{20,4},{24,8},{28,12},{1,17},{... | collective-permute-start | bytes 921608 | tf_op jit(solution)/shard_map/ppermute | solution.py:318
  26.3 1.7 %collective-permute-start.3 = (bf16[448,384]{1,0:T(8,128)(2,1)S(1)}, bf16[448,384]{1,0:T(8,128)(2,1)S(1)}, u32[]{:S(2)}, u32[]{:S(2)}) collective-permute-start(bf16[448,384]{1,0:T(8,128)(2,1)S(1)} %collective-permute-done.refs_2_.refs_0_), channel_id=1, source_target_pairs={{0,1},{1,0},{2,3},{3,2},{4,5},{5,4},{6,7},{7,6},{8,9},{9,8},{10,11... | collective-permute-start | bytes 1032200 | tf_op jit(solution)/shard_map/ppermute | solution.py:318
  31.0 38.1 %collective-permute-start.16 = (bf16[448,1536]{1,0:T(8,128)(2,1)S(1)}, bf16[448,1536]{1,0:T(8,128)(2,1)S(1)}, u32[]{:S(2)}, u32[]{:S(2)}) collective-permute-start(bf16[448,1536]{1,0:T(8,128)(2,1)S(1)} %shard_map.79), channel_id=1, source_target_pairs={{0,8},{4,12},{24,16},{28,20},{1,9},{5,13},{25,17},{29,21},{2,10},{... | collective-permute-start | bytes 4128776 | tf_op jit(solution)/shard_map/ppermute | solution.py:322
  33.7 36.2 %collective-permute-start.18 = (bf16[448,1536]{1,0:T(8,128)(2,1)S(1)}, bf16[448,1536]{1,0:T(8,128)(2,1)S(1)}, u32[]{:S(2)}, u32[]{:S(2)}) collective-permute-start(bf16[448,1536]{1,0:T(8,128)(2,1)S(1)} %shard_map.79), channel_id=1, source_target_pairs={{8,16},{12,20},{16,8},{20,12},{9,17},{13,21},{17,9},{21,13},{10,18... | collective-permute-start | bytes 4128776 | tf_op jit(solution)/shard_map/ppermute | solution.py:322
  34.6 6.6 %collective-permute-start.4 = (bf16[608,384]{1,0:T(8,128)(2,1)S(1)}, bf16[608,384]{1,0:T(8,128)(2,1)S(1)}, u32[]{:S(2)}, u32[]{:S(2)}) collective-permute-start(bf16[608,384]{1,0:T(8,128)(2,1)S(1)} %get-tuple-element.78.refs_1_.refs_0_), channel_id=1, source_target_pairs={{0,1},{1,0},{2,3},{3,2},{4,5},{5,4},{6,7},{7,6},{8,9},{9,8},{10,11... | collective-permute-start | bytes 1400840 | tf_op jit(solution)/shard_map/ppermute | solution.py:318
  34.7 14.5 %collective-permute-start.6 = (bf16[304,384]{1,0:T(8,128)(2,1)S(1)}, bf16[304,384]{1,0:T(8,128)(2,1)S(1)}, u32[]{:S(2)}, u32[]{:S(2)}) collective-permute-start(bf16[304,384]{1,0:T(8,128)(2,1)S(1)} %get-tuple-element.84), channel_id=1, source_target_pairs={{0,2},{1,3},{2,0},{3,1},{4,6},{5,7},{6,4},{7,5},{8,10},{9,11},{10,... | collective-permute-start | bytes 700424 | tf_op jit(solution)/shard_map/ppermute | solution.py:318
  35.3 13.9 %collective-permute-start.7 = (bf16[304,384]{1,0:T(8,128)(2,1)S(1)}, bf16[304,384]{1,0:T(8,128)(2,1)S(1)}, u32[]{:S(2)}, u32[]{:S(2)}) collective-permute-start(bf16[304,384]{1,0:T(8,128)(2,1)S(1)} %get-tuple-element.87), channel_id=1, source_target_pairs={{0,2},{1,3},{2,0},{3,1},{4,6},{5,7},{6,4},{7,5},{8,10},{9,11},{10,... | collective-permute-start | bytes 700424 | tf_op jit(solution)/shard_map/ppermute | solution.py:318
  43.2 11.0 %collective-permute-start.5 = (bf16[384,512]{1,0:T(8,128)(2,1)S(1)}, bf16[384,512]{1,0:T(8,128)(2,1)S(1)}, u32[]{:S(2)}, u32[]{:S(2)}) collective-permute-start(bf16[384,512]{1,0:T(8,128)(2,1)S(1)} %get-tuple-element.79), channel_id=1, source_target_pairs={{0,4},{4,0},{8,12},{12,8},{16,20},{20,16},{24,28},{28,24},{1,5},{5... | collective-permute-start | bytes 1179656 | tf_op jit(solution)/shard_map/ppermute | solution.py:318
  49.2 5.0 %collective-permute-start.8 = (bf16[304,384]{1,0:T(8,128)(2,1)S(1)}, bf16[304,384]{1,0:T(8,128)(2,1)S(1)}, u32[]{:S(2)}, u32[]{:S(2)}) collective-permute-start(bf16[304,384]{1,0:T(8,128)(2,1)S(1)} %collective-permute-done.6.refs_1_.refs_2_), channel_id=1, source_target_pairs={{0,1},{1,0},{2,3},{3,2},{4,5},{5,4},{6,7},{7,6},{8,9},{9,8},{10,11... | collective-permute-start | bytes 700424 | tf_op jit(solution)/shard_map/ppermute | solution.py:318
  49.3 4.9 %collective-permute-start.9 = (bf16[304,384]{1,0:T(8,128)(2,1)S(1)}, bf16[304,384]{1,0:T(8,128)(2,1)S(1)}, u32[]{:S(2)}, u32[]{:S(2)}) collective-permute-start(bf16[304,384]{1,0:T(8,128)(2,1)S(1)} %collective-permute-done.7.refs_2_.refs_3_), channel_id=1, source_target_pairs={{0,1},{1,0},{2,3},{3,2},{4,5},{5,4},{6,7},{7,6},{8,9},{9,8},{10,11... | collective-permute-start | bytes 700424 | tf_op jit(solution)/shard_map/ppermute | solution.py:318
  56.0 12.1 %collective-permute-start.10 = (bf16[384,512]{1,0:T(8,128)(2,1)S(1)}, bf16[384,512]{1,0:T(8,128)(2,1)S(1)}, u32[]{:S(2)}, u32[]{:S(2)}) collective-permute-start(bf16[384,512]{1,0:T(8,128)(2,1)S(1)} %get-tuple-element.89), channel_id=1, source_target_pairs={{0,4},{4,0},{8,12},{12,8},{16,20},{20,16},{24,28},{28,24},{1,5},{5... | collective-permute-start | bytes 1179656 | tf_op jit(solution)/shard_map/ppermute | solution.py:318
  60.4 48.9 %collective-permute-start.12 = (bf16[768,512]{1,0:T(8,128)(2,1)S(1)}, bf16[768,512]{1,0:T(8,128)(2,1)S(1)}, u32[]{:S(2)}, u32[]{:S(2)}) collective-permute-start(bf16[768,512]{1,0:T(8,128)(2,1)S(1)} %get-tuple-element.95), channel_id=1, source_target_pairs={{0,4},{4,0},{8,12},{12,8},{16,20},{20,16},{24,28},{28,24},{1,5},{5... | collective-permute-start | bytes 2359304 | tf_op jit(solution)/shard_map/ppermute | solution.py:318
  69.1 53.7 %collective-permute-start.17 = (bf16[448,1536]{1,0:T(8,128)(2,1)S(1)}, bf16[448,1536]{1,0:T(8,128)(2,1)S(1)}, u32[]{:S(2)}, u32[]{:S(2)}) collective-permute-start(bf16[448,1536]{1,0:T(8,128)(2,1)S(1)} %collective-permute-done.16), channel_id=1, source_target_pairs={{8,16},{12,20},{16,8},{20,12},{9,17},{13,21},{17,9},{21,13},{10,18... | collective-permute-start | bytes 4128776 | tf_op jit(solution)/shard_map/ppermute | solution.py:322
  69.9 53.0 %collective-permute-start.19 = (bf16[448,1536]{1,0:T(8,128)(2,1)S(1)}, bf16[448,1536]{1,0:T(8,128)(2,1)S(1)}, u32[]{:S(2)}, u32[]{:S(2)}) collective-permute-start(bf16[448,1536]{1,0:T(8,128)(2,1)S(1)} %collective-permute-done.18), channel_id=1, source_target_pairs={{16,24},{20,28},{8,0},{12,4},{17,25},{21,29},{9,1},{13,5},{18,26},... | collective-permute-start | bytes 4128776 | tf_op jit(solution)/shard_map/ppermute | solution.py:322
  71.4 38.0 %collective-permute-start.11 = (bf16[384,512]{1,0:T(8,128)(2,1)S(1)}, bf16[384,512]{1,0:T(8,128)(2,1)S(1)}, u32[]{:S(2)}, u32[]{:S(2)}) collective-permute-start(bf16[384,512]{1,0:T(8,128)(2,1)S(1)} %get-tuple-element.99), channel_id=1, source_target_pairs={{0,8},{4,12},{8,0},{12,4},{16,24},{20,28},{24,16},{28,20},{1,9},{5... | collective-permute-start | bytes 1179656 | tf_op jit(solution)/shard_map/ppermute | solution.py:318
  110.3 15.1 %collective-permute-start.20 = (bf16[768,512]{1,0:T(8,128)(2,1)S(1)}, bf16[768,512]{1,0:T(8,128)(2,1)S(1)}, u32[]{:S(2)}, u32[]{:S(2)}) collective-permute-start(bf16[768,512]{1,0:T(8,128)(2,1)S(1)} %get-tuple-element.121), channel_id=1, source_target_pairs={{0,4},{4,0},{8,12},{12,8},{16,20},{20,16},{24,28},{28,24},{1,5},{5... | collective-permute-start | bytes 2359304 | tf_op jit(solution)/shard_map/ppermute | solution.py:318
  112.8 23.1 %collective-permute-start.22 = (bf16[384,512]{1,0:T(8,128)(2,1)S(1)}, bf16[384,512]{1,0:T(8,128)(2,1)S(1)}, u32[]{:S(2)}, u32[]{:S(2)}) collective-permute-start(bf16[384,512]{1,0:T(8,128)(2,1)S(1)} %get-tuple-element.106), channel_id=1, source_target_pairs={{0,8},{4,12},{8,0},{12,4},{16,24},{20,28},{24,16},{28,20},{1,9},{5... | collective-permute-start | bytes 1179656 | tf_op jit(solution)/shard_map/ppermute | solution.py:318
  114.1 4.2 %collective-permute-start.14 = (bf16[80,384]{1,0:T(8,128)(2,1)S(1)}, bf16[80,384]{1,0:T(8,128)(2,1)S(1)}, u32[]{:S(2)}, u32[]{:S(2)}) collective-permute-start(bf16[80,384]{1,0:T(8,128)(2,1)S(1)} %slice.4), channel_id=1, source_target_pairs={{0,2},{1,3},{2,0},{3,1},{4,6},{5,7},{6,4},{7,5},{8,10},{9,11},{10,... | collective-permute-start | bytes 184328 | tf_op jit(solution)/shard_map/ppermute | solution.py:318
  123.7 12.2 %collective-permute-start.21 = (bf16[192,512]{1,0:T(8,128)(2,1)S(1)}, bf16[192,512]{1,0:T(8,128)(2,1)S(1)}, u32[]{:S(2)}, u32[]{:S(2)}) collective-permute-start(bf16[192,512]{1,0:T(8,128)(2,1)S(1)} %get-tuple-element.118), channel_id=1, source_target_pairs={{0,16},{4,20},{8,24},{12,28},{16,0},{20,4},{24,8},{28,12},{1,17},{... | collective-permute-start | bytes 589832 | tf_op jit(solution)/shard_map/ppermute | solution.py:318
  126.3 15.2 %collective-permute-start.24 = (bf16[384,512]{1,0:T(8,128)(2,1)S(1)}, bf16[384,512]{1,0:T(8,128)(2,1)S(1)}, u32[]{:S(2)}, u32[]{:S(2)}) collective-permute-start(bf16[384,512]{1,0:T(8,128)(2,1)S(1)} %get-tuple-element.122), channel_id=1, source_target_pairs={{0,8},{4,12},{8,0},{12,4},{16,24},{20,28},{24,16},{28,20},{1,9},{5... | collective-permute-start | bytes 1179656 | tf_op jit(solution)/shard_map/ppermute | solution.py:318
  136.7 16.9 %collective-permute-start.23 = (bf16[192,512]{1,0:T(8,128)(2,1)S(1)}, bf16[192,512]{1,0:T(8,128)(2,1)S(1)}, u32[]{:S(2)}, u32[]{:S(2)}) collective-permute-start(bf16[192,512]{1,0:T(8,128)(2,1)S(1)} %get-tuple-element.125), channel_id=1, source_target_pairs={{0,16},{4,20},{8,24},{12,28},{16,0},{20,4},{24,8},{28,12},{1,17},{... | collective-permute-start | bytes 589832 | tf_op jit(solution)/shard_map/ppermute | solution.py:318
  142.3 14.1 %collective-permute-start.25 = (bf16[192,512]{1,0:T(8,128)(2,1)S(1)}, bf16[192,512]{1,0:T(8,128)(2,1)S(1)}, u32[]{:S(2)}, u32[]{:S(2)}) collective-permute-start(bf16[192,512]{1,0:T(8,128)(2,1)S(1)} %get-tuple-element.131), channel_id=1, source_target_pairs={{0,16},{4,20},{8,24},{12,28},{16,0},{20,4},{24,8},{28,12},{1,17},{... | collective-permute-start | bytes 589832 | tf_op jit(solution)/shard_map/ppermute | solution.py:318
  (3 other events, 29.1 us)

commit v7 on v6

--- a/solution.py
+++ b/solution.py
@@ -107,9 +107,8 @@
     return (rows * own[None, :]).astype(BF)
 
 
-def first_kernel(meta, cot_hbm, scale_hbm, pre_hbm, late_out, early_out, rest_out, rest_a, rest_b, cot, scale, pre, sems):
-    width = cot.shape[1]
-    home = cot.shape[0]
+def first_kernel(meta, cot_hbm, scale_hbm, pre_hbm, rows_out, early_out, cot, scale, pre, sems):
+    home, width = cot.shape
     pairs = ((cot_hbm, cot), (scale_hbm, scale), (pre_hbm, pre))
     copies = [pltpu.make_async_copy(a, b, sems.at[i]) for i, (a, b) in enumerate(pairs)]
     for copy in copies:
@@ -119,14 +118,9 @@
     copies[1].wait()
     early_rows = scaled_rows(meta, early, cot, scale)
     early_out[:, :width] = early_rows
-    kept_rows = scaled_rows(meta, kept_picks(meta, home), cot, scale)
-    rest_out[0:EARLY, :] = early_rows
-    rest_out[EARLY:, :] = kept_rows
-    cut = rest_a.shape[0] - EARLY
-    rest_a[0:EARLY, :] = early_rows
-    rest_a[EARLY:, :] = kept_rows[:cut]
-    rest_b[...] = kept_rows[cut:]
-    late_out[...] = scaled_rows(meta, late_picks(meta, home), cot, scale)
+    rows_out[0:LATE, :] = scaled_rows(meta, late_picks(meta, home), cot, scale)
+    rows_out[LATE:SEND, :] = early_rows
+    rows_out[SEND:, :] = scaled_rows(meta, kept_picks(meta, home), cot, scale)
     copies[2].wait()
     early_out[:, width:] = jnp.dot(early, pre[...], preferred_element_type=F32).astype(BF)
 
@@ -170,34 +164,21 @@
 
 def assemble(meta, pieces, first_row, lhs):
     rows = lhs.shape[0]
-    width = pieces[1][0].shape[1]
+    width = pieces[1].shape[1]
     for j, piece in enumerate(pieces):
         columns = pl.ds(pl.multiple_of((tensor_at(meta) ^ j) * width, 128), width)
-        at = 0
-        for block in piece:
-            low, high = max(at, first_row), min(at + block.shape[0], first_row + rows)
-            if low < high:
-                lhs[low - first_row : high - first_row, columns] = block[low - at : high - at, 0:width]
-            at += block.shape[0]
-
-
-def split(refs, counts):
-    out, at = [], 0
-    for count in counts:
-        out.append(refs[at : at + count])
-        at += count
-    return out
-
-
-def grad_kernel(counts, first_row, block, meta, *refs):
-    p0, p1, p2, p3, (weight,), slopes, outs, (lhs,) = split(refs, counts)
+        lhs[:, columns] = piece[first_row : first_row + rows, 0:width]
+
+
+def grad_kernel(first_row, first_slope, slope_count, block, meta, p0, p1, p2, p3, weight, *rest):
+    slopes, outs, lhs = rest[:slope_count], rest[slope_count:-1], rest[-1]
     rows = lhs.shape[0]
     assemble(meta, (p0, p1, p2, p3), first_row, lhs)
     part = slopes[0].shape[1]
     at = 0
     for out in outs:
         for c in range(0, out.shape[1], block):
-            slope = slopes[at // part][first_row : first_row + rows, at % part : at % part + block]
+            slope = slopes[at // part][first_slope : first_slope + rows, at % part : at % part + block]
             value = jnp.dot(lhs[...], weight[:, at : at + block], preferred_element_type=F32)
             out[:, c : c + block] = (value * slope).astype(BF)
             at += block
@@ -205,7 +186,7 @@
 
 def early_kernel(block, meta, own, p1, p2, p3, weight, out, lhs, acc):
     width = p1.shape[1]
-    assemble(meta, ([own], [p1], [p2], [p3]), 0, lhs)
+    assemble(meta, (own, p1, p2, p3), 0, lhs)
     for at in range(0, out.shape[1], block):
         columns = slice(at, at + block)
         acc[...] = jnp.dot(lhs[...], weight[:, columns], preferred_element_type=F32)
@@ -226,17 +207,13 @@
     )
 
 
-def weight_kernel(counts, base, meta, *refs):
-    *parts, (act_late, act_rest, send, keep, lhs_late, lhs_rest) = split(refs, counts)
-    count = len(parts) // 2
-    half = parts[0][0].shape[1] // 2
+def weight_kernel(count, base, meta, *refs):
+    pieces, (act_late, act_rest, send, keep, lhs_late, lhs_rest) = refs[:count], refs[count:]
+    half = pieces[0].shape[1] // 2
     mine = dp_at(meta) % 2 == 0
-    for i in range(count):
-        for blocks, lhs in ((parts[2 * i], lhs_late), (parts[2 * i + 1], lhs_rest)):
-            both = blocks[0][...]
-            if len(blocks) > 1:
-                both = jnp.concatenate([block[...] for block in blocks], axis=0)
-            both = both.T
+    for i, piece in enumerate(pieces):
+        for rows, lhs in ((slice(0, LATE), lhs_late), (slice(LATE, SEND + KEEP), lhs_rest)):
+            both = piece[rows, :].T
             lo, hi = both[:half], both[half:]
             lhs[i * half : (i + 1) * half, :] = jnp.where(mine, hi, lo)
             lhs[(count + i) * half : (count + i + 1) * half, :] = jnp.where(mine, lo, hi)
@@ -293,13 +270,15 @@
     lax.fori_loop(0, half // step, body, 0)
 
 
-def place_kernel(meta, kept, early, inner, outer, out):
+def place_kernel(meta, kept, early, *rest):
+    inner, outer, out = rest[:2], rest[2:4], rest[4]
     d = dp_at(meta)
     count = kept_total(meta, d)
     first = jnp.minimum(count - lax.rem(count, TILE), BAL - SEND)
     first = pl.multiple_of(first, TILE)
     wide = out.shape[1]
-    columns = pl.ds(pl.multiple_of(pl.program_id(0) * wide, wide), wide)
+    step = pl.program_id(0)
+    columns = pl.ds(pl.multiple_of(step * wide, wide), wide)
     out[0:KEEP, :] = kept[:, columns]
     out[KEEP:, :] = jnp.zeros((out.shape[0] - KEEP, wide), BF)
 
@@ -310,7 +289,14 @@
 
     put(early[:, columns], first)
     is_inner = (d // 2 == 1) | (d // 2 == 2)
-    put(jnp.where(is_inner, inner[:, columns], outer[:, columns]), pl.multiple_of(first + EARLY, TILE))
+    half = inner[0].shape[1] // wide
+    for i in range(2):
+
+        @pl.when(step // half == i)
+        def _():
+            at = pl.ds(pl.multiple_of((step - i * half) * wide, wide), wide)
+            block = jnp.where(is_inner, inner[i][:, at], outer[i][:, at])
+            put(block, pl.multiple_of(first + EARLY, TILE))
 
 
 def swapped(block, axis, distance):
@@ -357,15 +343,12 @@
 
     def weight_part(meta, pieces, act):
         count = len(pieces)
-        parts = [x for j in pieces for x in (lates[j], rests[j])]
-        counts = [len(x) for x in parts] + [6]
-        blocks = [block for x in parts for block in x]
         return kernel_call(
-            functools.partial(weight_kernel, counts, 0),
+            functools.partial(weight_kernel, count, 0),
             [shape(count * half, part), shape(count * half, part, F32),
              shape(count * width, LATE), shape(count * width, others)],
-            [IN_VMEM] * (len(blocks) + 2), [IN_VMEM] * 4,
-        )(meta, *blocks, act_late, act)
+            [IN_VMEM] * (count + 2), [IN_VMEM] * 4,
+        )(meta, *pieces, act_late, act)
 
     def weight_again(meta, base, act):
         return kernel_call(
@@ -373,14 +356,12 @@
             [shape(4 * half, part), shape(4 * half, part, F32)], [IN_VMEM] * 6, [IN_VMEM] * 2,
         )(meta, *lhs_01, *lhs_23, act_late, act)
 
-    def grads(meta, pieces, first_row, rows, slopes, cuts):
-        counts = [len(x) for x in pieces] + [1, len(slopes), len(cuts), 1]
-        blocks = [block for x in pieces for block in x]
+    def grads(meta, first_row, first_slope, rows, slopes, cuts):
         return kernel_call(
-            functools.partial(grad_kernel, counts, first_row, 256),
-            [shape(rows, c) for c in cuts], [IN_VMEM] * (len(blocks) + 1 + len(slopes)), [IN_VMEM] * len(cuts),
+            functools.partial(grad_kernel, first_row, first_slope, len(slopes), 256),
+            [shape(rows, c) for c in cuts], [IN_VMEM] * (5 + len(slopes)), [IN_VMEM] * len(cuts),
             [vmem((rows, features), BF)],
-        )(meta, *blocks, down_weight, *slopes)
+        )(meta, *pieces, down_weight, *slopes)
 
     def near_step(meta, keeps, gots):
         count = len(keeps)
@@ -394,76 +375,78 @@
             far_kernel, [shape(half, part), shape(half, part, F32)], [IN_VMEM] * 2, [IN_VMEM] * 2
         )(meta, mine, got)
 
-    cut = others // 2
-    late, early, rest, *rest_blocks = kernel_call(
-        first_kernel,
-        [shape(r, c) for r, c in ((LATE, width), (EARLY, width + ff), (others, width), (cut, width), (others - cut, width))],
-        [IN_HBM] * 3, [IN_VMEM] * 5,
+    own_rows, early = kernel_call(
+        first_kernel, [shape(SEND + KEEP, width), shape(EARLY, width + ff)], [IN_HBM] * 3, [IN_VMEM] * 2,
         [vmem((home, width), BF), vmem((features,), F32), vmem((home, ff), BF), sems((3,))],
     )(meta, cotangent, layer_scale, hidden_pre)
     arrived_early = swapped(early, "dp", n // 2)
-    late_c, late_y = swapped(late, "tensor", 1), swapped(late, "tensor", 2)
-    act_late, der_late = gelu(after(meta, late), True, 0, ff)
-
-    late_y = after(late_y, act_late, late_c, arrived_early)
-    late_yc = swapped(late_y, "tensor", 1)
-    rest_y = [swapped(after(block, late_y), "tensor", 2) for block in rest_blocks]
-    rest_c = swapped(after(rest, late_y), "tensor", 1)
-
-    lates = ([late], [late_c], [late_y], [late_yc])
-    (moving,) = grads(after(meta, late_y), lates, 0, LATE, (der_late,), (ff,))
-    from_outer = routed(moving, ((0, 1), (3, 2)))
-    from_inner = routed(moving, ((1, 2), (2, 1)))
-
-    act_a, der_a = gelu(after(meta, moving), False, 0, part)
-    rests = ([rest], [rest_c])
-    send_01, keep_01, *lhs_01 = weight_part(after(meta, act_a), (0, 1), act_a)
+
+    rows_c, rows_y = swapped(own_rows, "tensor", 1), swapped(own_rows, "tensor", 2)
+    act_late, der_late = gelu(after(meta, own_rows), True, 0, ff)
+    act_a, der_a = gelu(after(meta, act_late), False, 0, part)
+
+    send_01, keep_01, *lhs_01 = weight_part(after(meta, act_a), (own_rows, rows_c), act_a)
     got_01 = swapped(send_01, "dp", 1)
-    act_b, der_b = gelu(after(meta, send_01), False, part, part)
-    rest_y = [after(block, act_b) for block in rest_y]
-    rest_yc = [swapped(block, "tensor", 1) for block in rest_y]
-    rests = ([rest], [rest_c], rest_y, rest_yc)
-    send_23, keep_23, *lhs_23 = weight_part(after(meta, act_b, got_01), (2, 3), act_a)
+    rows_y = after(rows_y, send_01, arrived_early)
+    rows_yc = swapped(rows_y, "tensor", 1)
+    pieces = (own_rows, rows_c, rows_y, rows_yc)
+
+    moving = grads(after(meta, rows_y), 0, 0, LATE, (der_late,), (ff // 2, ff // 2))
+    to_inner, across, to_outer = ((0, 1), (3, 2)), ((1, 2), (2, 1)), ((1, 0), (2, 3))
+    at_inner_a = routed(moving[0], to_inner)
+    crossed_a = routed(moving[0], across)
+    crossed_b = routed(moving[1], across)
+
+    send_23, keep_23, *lhs_23 = weight_part(after(meta, got_01, *moving), (rows_y, rows_yc), act_a)
     got_23 = swapped(send_23, "dp", 1)
-    send_b, keep_b = weight_again(after(meta, send_23), part, act_b)
+    act_b, der_b = gelu(after(meta, send_23), False, part, part)
+    send_b, keep_b = weight_again(after(meta, act_b), part, act_b)
     got_b = swapped(send_b, "dp", 1)
 
-    out_na, mine_a = near_step(after(meta, send_b), (keep_01, keep_23), (got_01, got_23))
+    out_na, mine_a = near_step(
+        after(meta, send_b, at_inner_a, crossed_a), (keep_01, keep_23), (got_01, got_23)
+    )
     got_na = swapped(out_na, "dp", 2)
-    arrived_inner = routed(after(from_outer, out_na), ((1, 2), (2, 1)))
-    arrived_outer = routed(after(from_inner, out_na), ((2, 3), (1, 0)))
-
     act_c, der_c = gelu(after(meta, out_na), False, 2 * part, part)
     early_sent = after(arrived_early[:, :width], act_c)
     early_c, early_y = swapped(early_sent, "tensor", 1), swapped(early_sent, "tensor", 2)
     send_c, keep_c = weight_again(after(meta, act_c), 2 * part, act_c)
-    out_nb, mine_b = near_step(after(meta, send_c, got_na), (keep_b,), (got_b,))
+    early_y = after(early_y, send_c, early_c)
+    early_yc = swapped(early_y, "tensor", 1)
+
+    is_inner = (d // 2 == 1) | (d // 2 == 2)
+    hop = jnp.where(is_inner, crossed_a, moving[1])
+    hop = after(hop, got_na, send_c, crossed_b)
+    hopped = routed(hop, to_inner + to_outer)
+    inner_a = routed(after(at_inner_a, send_c), across)
+
+    out_fa, own_a = far_step(after(meta, hop), mine_a, got_na)
+    got_fa = swapped(out_fa, "dp", 4)
+    out_nb, mine_b = near_step(after(meta, out_fa, hopped, inner_a, early_yc), (keep_b,), (got_b,))
     got_nb = swapped(out_nb, "dp", 2)
     got_c = swapped(after(send_c, out_nb), "dp", 1)
-
-    (kept_grad,) = grads(after(meta, out_nb), rests, EARLY, KEEP, (der_a, der_b, der_c), (ff,))
-    early_y = after(early_y, kept_grad, early_c)
-    early_yc = swapped(early_y, "tensor", 1)
+    inner_b = routed(after(hopped, out_nb), across)
+    outer_b = routed(after(crossed_b, out_nb), to_outer)
+
+    (kept_grad,) = grads(after(meta, out_nb), SEND, EARLY, KEEP, (der_a, der_b, der_c), (ff,))
     early_grad = kernel_call(
         functools.partial(early_kernel, 256), shape(EARLY, ff), [IN_VMEM] * 5, IN_VMEM,
         [vmem((EARLY, features), BF), vmem((EARLY, 256), F32)],
     )(after(meta, kept_grad), arrived_early, early_c, early_y, early_yc, down_weight)
 
-    out_fa, own_a = far_step(after(meta, early_grad, arrived_inner, arrived_outer), mine_a, got_na)
-    got_fa = swapped(out_fa, "dp", 4)
-    out_nc, mine_c = near_step(after(meta, out_fa), (keep_c,), (got_c,))
+    out_fb, own_b = far_step(after(meta, early_grad, got_fa), mine_b, got_nb)
+    got_fb = swapped(out_fb, "dp", 4)
+    out_nc, mine_c = near_step(after(meta, out_fb), (keep_c,), (got_c,))
     got_nc = swapped(out_nc, "dp", 2)
-    out_fb, own_b = far_step(after(meta, out_nc, got_fa), mine_b, got_nb)
-    got_fb = swapped(out_fb, "dp", 4)
-    out_fc, own_c = far_step(after(meta, out_fb), mine_c, got_nc)
+    out_fc, own_c = far_step(after(meta, out_nc, inner_b, outer_b), mine_c, got_nc)
     got_fc = swapped(out_fc, "dp", 4)
     total = [a + b.astype(F32) for a, b in ((own_a, got_fa), (own_b, got_fb), (own_c, got_fc))]
     down_grad = jnp.concatenate(total, axis=1) / math.sqrt(n * home)
 
     hidden_grad = kernel_call(
-        place_kernel, shape(BAL, ff), [IN_VMEM] * 4,
+        place_kernel, shape(BAL, ff), [IN_VMEM] * 6,
         pl.BlockSpec((BAL, 256), lambda i, *_: (0, i)), grid=(ff // 256,),
-    )(after(meta, out_fb), kept_grad, early_grad, arrived_inner, arrived_outer)
+    )(after(meta, out_fc), kept_grad, early_grad, inner_a, inner_b, hopped, outer_b)
     return (hidden_grad, down_grad)
 
 

time: 158 us -> 143 us (0.905)
  waiting for transfers between devices: 72.5 us -> 40.3 us
  starting transfers between devices: 28.7 us -> 38.3 us
  local copies, waits for them, and re-layouts: 0.01 us -> 3.34 us
  Pallas kernels: 53.5 us -> 56.5 us
    ppermute x22 -> x17, waiting for transfers between devices: 72.5 us -> 31.1 us  [swapped(): return lax.ppermute(block, axis, [(i, i ^ distance) for i in range(n)])]
    ppermute x4 -> x7, waiting for transfers between devices: 0.01 us -> 9.15 us  [routed(): lax.ppermute(block, 'dp', [(2 * a + x, 2 * b + x) for a, b in pairs for x...]
    ppermute x4 -> x7, starting transfers between devices: 5.88 us -> 13.4 us  [routed(): lax.ppermute(block, 'dp', [(2 * a + x, 2 * b + x) for a, b in pairs for x...]
    unnamed x2 -> x54, local copies, waits for them, and re-layouts: 0.01 us -> 3.34 us
    ppermute x22 -> x17, starting transfers between devices: 22.8 us -> 24.9 us  [swapped(): return lax.ppermute(block, axis, [(i, i ^ distance) for i in range(n)])]
  transfers between devices with their start and end apart: 26 -> 24, of which waited for: 12 -> 9; matrix products, arithmetic and copies ran while one was open for 0% -> 1% of each run, Pallas kernels for 29% -> 36%
where the time goes in v7:
time: 143 us
  Pallas kernels  56.5 us (40%)
  waiting for transfers between devices  40.3 us (28%)
  starting transfers between devices  38.3 us (27%)
  local copies, waits for them, and re-layouts  3.34 us (2%)
  other arithmetic  3.27 us (2%)
    ppermute x17, waiting for transfers between devices, swapped(): return lax.ppermute(block, axis, [(i, i ^ distance) for i in range(n)])  31.1 us
    ppermute x17, starting transfers between devices, swapped(): return lax.ppermute(block, axis, [(i, i ^ distance) for i in range(n)])  24.9 us
    pallas_call x4, Pallas kernels, gelu(): kernel_call(functools.partial(gelu_kernel, late, base, block), [shape(row...  21.3 us
    ppermute x7, starting transfers between devices, routed(): lax.ppermute(block, 'dp', [(2 * a + x, 2 * b + x) for a, b in pairs for x...  13.4 us
    ppermute x7, waiting for transfers between devices, routed(): lax.ppermute(block, 'dp', [(2 * a + x, 2 * b + x) for a, b in pairs for x...  9.15 us
    pallas_call x2, Pallas kernels, grads(): kernel_call(functools.partial(grad_kernel, first_row, first_slope, len(sl...  7.45 us
    pallas_call x2, Pallas kernels, weight_again(): kernel_call(functools.partial(weight_again_kernel, base), [shape(4 * half...  5.7 us
    pallas_call x1, Pallas kernels, shards(): kernel_call(first_kernel, [shape(SEND + KEEP, width), shape(EARLY, width...  4.68 us
  transfers between devices with their start and end apart: 24, of which 9 were waited for; matrix products, arithmetic and copies ran while one was open for 1% of the time, Pallas kernels for 36%

profile of v7, /device:TPU:0, one launch (start us, length us, event | category | flops | bytes accessed | tf_op | source)
XLA Modules:
  0.0 142.9 jit_solution(7481358911758428734)
XLA Ops:
  1.4 4.7 %shard_map.77 = (bf16[1056,384]{1,0:T(8,128)(2,1)S(1)}, bf16[80,1920]{1,0:T(8,128)(2,1)S(1)}) custom-call(s32[9,8]{1,0:T(8,128)S(1)} %pad_add_fusion.meta, bf16[1032,384]{1,0:T(8,128)(2,1)} %cot_hbm.1, f32[1536]{0:T(1024)} %scale_hbm.1, bf16[1032,1536]{1,0:T(8,128)(2,1)} %pre_hbm.9), custom_call_target="tpu_custom_call" | custom-call | flops 1 | bytes 1 | tf_op jit(solution)/shard_map/pallas_call | solution.py:378
  6.6 2.6 %collective-permute-start = (bf16[1056,384]{1,0:T(8,128)(2,1)S(1)}, bf16[1056,384]{1,0:T(8,128)(2,1)S(1)}, u32[]{:S(2)}, u32[]{:S(2)}) collective-permute-start(bf16[1056,384]{1,0:T(8,128)(2,1)S(1)} %get-tuple-element.64.refs_0_.p0), channel_id=1, source_target_pairs={{0,2},{1,3},{2,0},{3,1},{4,6},{5,7},{6,4},{7,5},{8,10},{9,11},{10,... | collective-permute-start | bytes 2433032 | tf_op jit(solution)/shard_map/ppermute | solution.py:304
  9.2 2.6 %collective-permute-start.2 = (bf16[80,1920]{1,0:T(8,128)(2,1)S(1)}, bf16[80,1920]{1,0:T(8,128)(2,1)S(1)}, u32[]{:S(2)}, u32[]{:S(2)}) collective-permute-start(bf16[80,1920]{1,0:T(8,128)(2,1)S(1)} %get-tuple-element.71), channel_id=1, source_target_pairs={{0,16},{4,20},{8,24},{12,28},{16,0},{20,4},{24,8},{28,12},{1,17},{... | collective-permute-start | bytes 921608 | tf_op jit(solution)/shard_map/ppermute | solution.py:304
  11.8 7.7 %shard_map.78 = (bf16[448,1536]{1,0:T(8,128)(2,1)S(1)}, f32[448,1536]{1,0:T(8,128)S(1)}) custom-call(s32[9,8]{1,0:T(8,128)S(1)} %pad_add_fusion.meta, bf16[1032,1536]{1,0:T(8,128)(2,1)} %pre_hbm.9), custom_call_target="tpu_custom_call" | custom-call | flops 1 | bytes 1 | tf_op jit(solution)/shard_map/pallas_call | solution.py:336
  19.5 4.4 %shard_map.79 = (bf16[608,512]{1,0:T(8,128)(2,1)S(1)}, f32[608,512]{1,0:T(8,128)S(1)}) custom-call(s32[9,8]{1,0:T(8,128)S(1)} %pad_add_fusion.meta, bf16[1032,1536]{1,0:T(8,128)(2,1)} %pre_hbm.9), custom_call_target="tpu_custom_call" | custom-call | flops 1 | bytes 1 | tf_op jit(solution)/shard_map/pallas_call | solution.py:336
  23.9 1.9 %shard_map.80 = (bf16[384,512]{1,0:T(8,128)(2,1)S(1)}, f32[384,512]{1,0:T(8,128)S(1)}, bf16[768,448]{1,0:T(8,128)(2,1)S(1)}, bf16[768,608]{1,0:T(8,128)(2,1)S(1)}) custom-call(s32[9,8]{1,0:T(8,128)S(1)} %pad_add_fusion.meta, bf16[1056,384]{1,0:T(8,128)(2,1)S(1)} %get-tuple-element.64.refs_0_.p0, bf16[1056,384]{1,0:T(8,128)(2,1)S(1)} %collective-permute-done.1.refs_1_.p1, ...), custom_call_target="tpu_custom_call" | custom-call | flops 1 | bytes 1 | tf_op jit(solution)/shard_map/pallas_call | solution.py:346
  30.2 4.0 %shard_map.81 = (bf16[448,768]{1,0:T(8,128)(2,1)S(1)}, bf16[448,768]{1,0:T(8,128)(2,1)}) custom-call(s32[9,8]{1,0:T(8,128)S(1)} %pad_add_fusion.meta, bf16[1056,384]{1,0:T(8,128)(2,1)S(1)} %get-tuple-element.64.refs_0_.p0, bf16[1056,384]{1,0:T(8,128)(2,1)S(1)} %collective-permute-done.1.refs_1_.p1, bf16[1056,384]{1,0:T(8,128)(2,1)S(1)} %collective-permute-done.p2.refs_0_, ...), custom_call_target="tpu_custom_call" | custom-call | flops 1 | bytes 1 | tf_op jit(solution)/shard_map/pallas_call | solution.py:360
  34.8 6.5 %collective-permute-start.6 = (bf16[448,768]{1,0:T(8,128)(2,1)S(1)}, bf16[448,768]{1,0:T(8,128)(2,1)S(1)}, u32[]{:S(2)}, u32[]{:S(2)}) collective-permute-start(bf16[448,768]{1,0:T(8,128)(2,1)S(1)} %get-tuple-element.75), channel_id=1, source_target_pairs={{0,8},{4,12},{24,16},{28,20},{1,9},{5,13},{25,17},{29,21},{2,10},{... | collective-permute-start | bytes 2064392 | tf_op jit(solution)/shard_map/ppermute | solution.py:308
  41.4 1.9 %shard_map.82 = (bf16[384,512]{1,0:T(8,128)(2,1)S(1)}, f32[384,512]{1,0:T(8,128)S(1)}, bf16[768,448]{1,0:T(8,128)(2,1)S(1)}, bf16[768,608]{1,0:T(8,128)(2,1)S(1)}) custom-call(s32[9,8]{1,0:T(8,128)S(1)} %pad_add_fusion.meta, bf16[1056,384]{1,0:T(8,128)(2,1)S(1)} %collective-permute-done.p2.refs_0_, bf16[1056,384]{1,0:T(8,128)(2,1)S(1)} %collective-permute-done.3.p3.refs_1_, ...), custom_call_target="tpu_custom_call" | custom-call | flops 1 | bytes 1 | tf_op jit(solution)/shard_map/pallas_call | solution.py:346
  46.4 4.4 %shard_map.83 = (bf16[608,512]{1,0:T(8,128)(2,1)S(1)}, f32[608,512]{1,0:T(8,128)S(1)}) custom-call(s32[9,8]{1,0:T(8,128)S(1)} %pad_add_fusion.meta, bf16[1032,1536]{1,0:T(8,128)(2,1)} %pre_hbm.9), custom_call_target="tpu_custom_call" | custom-call | flops 1 | bytes 1 | tf_op jit(solution)/shard_map/pallas_call | solution.py:336
  50.9 2.9 %shard_map.84 = (bf16[768,512]{1,0:T(8,128)(2,1)S(1)}, f32[768,512]{1,0:T(8,128)S(1)}) custom-call(s32[9,8]{1,0:T(8,128)S(1)} %pad_add_fusion.meta, bf16[768,448]{1,0:T(8,128)(2,1)S(1)} %get-tuple-element.82.late_01, bf16[768,608]{1,0:T(8,128)(2,1)S(1)} %get-tuple-element.83.rest_01, bf16[768,448]{1,0:T(8,128)(2,1)S(1)} %get-tuple-element.84.late_23, ...), custom_call_target="tpu_custom_call" | custom-call | flops 1 | bytes 1 | tf_op jit(solution)/shard_map/pallas_call | solution.py:354
  58.7 2.5 %collective-permute-start.8 = (bf16[384,512]{1,0:T(8,128)(2,1)}, bf16[384,512]{1,0:T(8,128)(2,1)}, u32[]{:S(2)}, u32[]{:S(2)}) collective-permute-start(bf16[384,512]{1,0:T(8,128)(2,1)} %get-tuple-element.90), channel_id=1, source_target_pairs={{0,8},{4,12},{8,0},{12,4},{16,24},{20,28},{24,16},{28,20},{1,9},{5... | collective-permute-start | bytes 1179656 | tf_op jit(solution)/shard_map/ppermute | solution.py:304
  62.7 4.7 %shard_map.86 = (bf16[608,512]{1,0:T(8,128)(2,1)S(1)}, f32[608,512]{1,0:T(8,128)S(1)}) custom-call(s32[9,8]{1,0:T(8,128)S(1)} %pad_add_fusion.meta, bf16[1032,1536]{1,0:T(8,128)(2,1)} %pre_hbm.9), custom_call_target="tpu_custom_call" | custom-call | flops 1 | bytes 1 | tf_op jit(solution)/shard_map/pallas_call | solution.py:336
  68.6 2.9 %shard_map.87 = (bf16[768,512]{1,0:T(8,128)(2,1)S(1)}, f32[768,512]{1,0:T(8,128)S(1)}) custom-call(s32[9,8]{1,0:T(8,128)S(1)} %pad_add_fusion.meta, bf16[768,448]{1,0:T(8,128)(2,1)S(1)} %copy-done.9, bf16[768,608]{1,0:T(8,128)(2,1)S(1)} %copy-done.5, bf16[768,448]{1,0:T(8,128)(2,1)S(1)} %copy-done.11, bf16[768,608]{1,0:T(8,128)(2,1)S(1)} %copy-done.7, ...), custom_call_target="tpu_custom_call" | custom-call | flops 1 | bytes 1 | tf_op jit(solution)/shard_map/pallas_call | solution.py:354
  77.0 2.7 %collective-permute-done.12.p2 = bf16[80,384]{1,0:T(8,128)(2,1)S(1)} collective-permute-done((bf16[80,384]{1,0:T(8,128)(2,1)S(1)}, bf16[80,384]{1,0:T(8,128)(2,1)S(1)}, u32[]{:S(2)}, u32[]{:S(2)}) %collective-permute-start.12) | collective-permute-done | bytes 61472 | tf_op jit(solution)/shard_map/ppermute | solution.py:304
  81.6 8.0 %collective-permute-done.10.rest_2_ = bf16[448,768]{1,0:T(8,128)(2,1)S(1)} collective-permute-done((bf16[448,768]{1,0:T(8,128)(2,1)S(1)}, bf16[448,768]{1,0:T(8,128)(2,1)S(1)}, u32[]{:S(2)}, u32[]{:S(2)}) %collective-permute-start.10) | collective-permute-done | bytes 688160 | tf_op jit(solution)/shard_map/ppermute | solution.py:308
  95.0 3.8 %collective-permute-start.16 = (bf16[192,512]{1,0:T(8,128)(2,1)S(1)}, bf16[192,512]{1,0:T(8,128)(2,1)S(1)}, u32[]{:S(2)}, u32[]{:S(2)}) collective-permute-start(bf16[192,512]{1,0:T(8,128)(2,1)S(1)} %get-tuple-element.98), channel_id=1, source_target_pairs={{0,16},{4,20},{8,24},{12,28},{16,0},{20,4},{24,8},{28,12},{1,17},{... | collective-permute-start | bytes 589832 | tf_op jit(solution)/shard_map/ppermute | solution.py:304
  98.9 3.5 %shard_map.90.kept = bf16[528,1536]{1,0:T(8,128)(2,1)S(1)} custom-call(s32[9,8]{1,0:T(8,128)S(1)} %pad_add_fusion.meta, bf16[1056,384]{1,0:T(8,128)(2,1)S(1)} %get-tuple-element.64.refs_0_.p0, bf16[1056,384]{1,0:T(8,128)(2,1)S(1)} %collective-permute-done.1.refs_1_.p1, bf16[1056,384]{1,0:T(8,128)(2,1)S(1)} %copy-done.1, bf16[1056,384]{1,0:T(8,128)(2,1)S(1)} %copy-done.3, ...), custom_call_target="tpu_custom_call" | custom-call | flops 1 | bytes 1 | tf_op jit(solution)/shard_map/pallas_call | solution.py:360
  102.4 3.3 %shard_map.91.early = bf16[80,1536]{1,0:T(8,128)(2,1)S(1)} custom-call(s32[9,8]{1,0:T(8,128)S(1)} %pad_add_fusion.meta, bf16[80,1920]{1,0:T(8,128)(2,1)S(1)} %collective-permute-done.2.own, bf16[80,384]{1,0:T(8,128)(2,1)S(1)} %collective-permute-done.13.p1, bf16[80,384]{1,0:T(8,128)(2,1)S(1)} %collective-permute-done.12.p2, ...), custom_call_target="tpu_custom_call" | custom-call | flops 1 | bytes 1 | tf_op jit(solution)/shard_map/pallas_call | solution.py:432
  105.6 12.1 %collective-permute-done.16 = bf16[192,512]{1,0:T(8,128)(2,1)S(1)} collective-permute-done((bf16[192,512]{1,0:T(8,128)(2,1)S(1)}, bf16[192,512]{1,0:T(8,128)(2,1)S(1)}, u32[]{:S(2)}, u32[]{:S(2)}) %collective-permute-start.16) | collective-permute-done | bytes 196640 | tf_op jit(solution)/shard_map/ppermute | solution.py:304
  119.5 3.2 %collective-permute-start.22 = (bf16[192,512]{1,0:T(8,128)(2,1)S(1)}, bf16[192,512]{1,0:T(8,128)(2,1)S(1)}, u32[]{:S(2)}, u32[]{:S(2)}) collective-permute-start(bf16[192,512]{1,0:T(8,128)(2,1)S(1)} %get-tuple-element.112), channel_id=1, source_target_pairs={{0,16},{4,20},{8,24},{12,28},{16,0},{20,4},{24,8},{28,12},{1,17},{... | collective-permute-start | bytes 589832 | tf_op jit(solution)/shard_map/ppermute | solution.py:304
  122.8 8.4 %collective-permute-done.21.got = bf16[384,512]{1,0:T(8,128)(2,1)S(1)} collective-permute-done((bf16[384,512]{1,0:T(8,128)(2,1)S(1)}, bf16[384,512]{1,0:T(8,128)(2,1)S(1)}, u32[]{:S(2)}, u32[]{:S(2)}) %collective-permute-start.21) | collective-permute-done | bytes 393248 | tf_op jit(solution)/shard_map/ppermute | solution.py:304
  133.0 3.3 %shard_map.95 = bf16[720,1536]{1,0:T(8,128)(2,1)} custom-call(s32[9,8]{1,0:T(8,128)S(1)} %pad_add_fusion.meta, bf16[528,1536]{1,0:T(8,128)(2,1)S(1)} %shard_map.90.kept, bf16[80,1536]{1,0:T(8,128)(2,1)S(1)} %shard_map.91.early, bf16[448,768]{1,0:T(8,128)(2,1)S(1)} %collective-permute-done.11.rest_0_, bf16[448,768]{1,0:T(8,128)(2,1)S(1)} %collective-permute-done.19.rest_1_, ...), custom_call_target="tpu_custom_call" | custom-call | flops 1 | bytes 1 | tf_op jit(solution)/shard_map/pallas_call | solution.py:446
  136.3 5.4 %collective-permute-done.23 = bf16[192,512]{1,0:T(8,128)(2,1)S(1)} collective-permute-done((bf16[192,512]{1,0:T(8,128)(2,1)S(1)}, bf16[192,512]{1,0:T(8,128)(2,1)S(1)}, u32[]{:S(2)}, u32[]{:S(2)}) %collective-permute-start.23) | collective-permute-done | bytes 196640 | tf_op jit(solution)/shard_map/ppermute | solution.py:304
  (107 shorter events, 34.5 us)
Async XLA Ops:
  6.1 17.9 %collective-permute-start.1 = (bf16[1056,384]{1,0:T(8,128)(2,1)S(1)}, bf16[1056,384]{1,0:T(8,128)(2,1)S(1)}, u32[]{:S(2)}, u32[]{:S(2)}) collective-permute-start(bf16[1056,384]{1,0:T(8,128)(2,1)S(1)} %get-tuple-element.64.refs_0_.p0), channel_id=1, source_target_pairs={{0,1},{1,0},{2,3},{3,2},{4,5},{5,4},{6,7},{7,6},{8,9},{9,8},{10,11... | collective-permute-start | bytes 2433032 | tf_op jit(solution)/shard_map/ppermute | solution.py:304
  6.6 21.3 %collective-permute-start = (bf16[1056,384]{1,0:T(8,128)(2,1)S(1)}, bf16[1056,384]{1,0:T(8,128)(2,1)S(1)}, u32[]{:S(2)}, u32[]{:S(2)}) collective-permute-start(bf16[1056,384]{1,0:T(8,128)(2,1)S(1)} %get-tuple-element.64.refs_0_.p0), channel_id=1, source_target_pairs={{0,2},{1,3},{2,0},{3,1},{4,6},{5,7},{6,4},{7,5},{8,10},{9,11},{10,... | collective-permute-start | bytes 2433032 | tf_op jit(solution)/shard_map/ppermute | solution.py:304
  9.2 16.8 %collective-permute-start.2 = (bf16[80,1920]{1,0:T(8,128)(2,1)S(1)}, bf16[80,1920]{1,0:T(8,128)(2,1)S(1)}, u32[]{:S(2)}, u32[]{:S(2)}) collective-permute-start(bf16[80,1920]{1,0:T(8,128)(2,1)S(1)} %get-tuple-element.71), channel_id=1, source_target_pairs={{0,16},{4,20},{8,24},{12,28},{16,0},{20,4},{24,8},{28,12},{1,17},{... | collective-permute-start | bytes 921608 | tf_op jit(solution)/shard_map/ppermute | solution.py:304
  27.8 2.3 %collective-permute-start.3 = (bf16[1056,384]{1,0:T(8,128)(2,1)S(1)}, bf16[1056,384]{1,0:T(8,128)(2,1)S(1)}, u32[]{:S(2)}, u32[]{:S(2)}) collective-permute-start(bf16[1056,384]{1,0:T(8,128)(2,1)S(1)} %collective-permute-done.p2.refs_0_), channel_id=1, source_target_pairs={{0,1},{1,0},{2,3},{3,2},{4,5},{5,4},{6,7},{7,6},{8,9},{9,8},{10,11... | collective-permute-start | bytes 2433032 | tf_op jit(solution)/shard_map/ppermute | solution.py:304
  27.8 13.5 %collective-permute-start.5 = (bf16[384,512]{1,0:T(8,128)(2,1)S(1)}, bf16[384,512]{1,0:T(8,128)(2,1)S(1)}, u32[]{:S(2)}, u32[]{:S(2)}) collective-permute-start(bf16[384,512]{1,0:T(8,128)(2,1)S(1)} %get-tuple-element.70), channel_id=1, source_target_pairs={{0,4},{4,0},{8,12},{12,8},{16,20},{20,16},{24,28},{28,24},{1,5},{5... | collective-permute-start | bytes 1179656 | tf_op jit(solution)/shard_map/ppermute | solution.py:304
  34.1 20.8 %collective-permute-start.4 = (bf16[448,768]{1,0:T(8,128)(2,1)S(1)}, bf16[448,768]{1,0:T(8,128)(2,1)S(1)}, u32[]{:S(2)}, u32[]{:S(2)}) collective-permute-start(bf16[448,768]{1,0:T(8,128)(2,1)S(1)} %get-tuple-element.75), channel_id=1, source_target_pairs={{8,16},{12,20},{16,8},{20,12},{9,17},{13,21},{17,9},{21,13},{10,18... | collective-permute-start | bytes 2064392 | tf_op jit(solution)/shard_map/ppermute | solution.py:308
  34.8 21.2 %collective-permute-start.6 = (bf16[448,768]{1,0:T(8,128)(2,1)S(1)}, bf16[448,768]{1,0:T(8,128)(2,1)S(1)}, u32[]{:S(2)}, u32[]{:S(2)}) collective-permute-start(bf16[448,768]{1,0:T(8,128)(2,1)S(1)} %get-tuple-element.75), channel_id=1, source_target_pairs={{0,8},{4,12},{24,16},{28,20},{1,9},{5,13},{25,17},{29,21},{2,10},{... | collective-permute-start | bytes 2064392 | tf_op jit(solution)/shard_map/ppermute | solution.py:308
  43.3 12.7 %collective-permute-start.7 = (bf16[384,512]{1,0:T(8,128)(2,1)S(1)}, bf16[384,512]{1,0:T(8,128)(2,1)S(1)}, u32[]{:S(2)}, u32[]{:S(2)}) collective-permute-start(bf16[384,512]{1,0:T(8,128)(2,1)S(1)} %get-tuple-element.78), channel_id=1, source_target_pairs={{0,4},{4,0},{8,12},{12,8},{16,20},{20,16},{24,28},{28,24},{1,5},{5... | collective-permute-start | bytes 1179656 | tf_op jit(solution)/shard_map/ppermute | solution.py:304
  44.9 28.7 %collective-permute-start.9 = (bf16[448,768]{1,0:T(8,128)(2,1)}, bf16[448,768]{1,0:T(8,128)(2,1)}, u32[]{:S(2)}, u32[]{:S(2)}) collective-permute-start(bf16[448,768]{1,0:T(8,128)(2,1)} %get-tuple-element.76), channel_id=1, source_target_pairs={{8,16},{12,20},{16,8},{20,12},{9,17},{13,21},{17,9},{21,13},{10,18... | collective-permute-start | bytes 2064392 | tf_op jit(solution)/shard_map/ppermute | solution.py:308
  58.7 14.9 %collective-permute-start.8 = (bf16[384,512]{1,0:T(8,128)(2,1)}, bf16[384,512]{1,0:T(8,128)(2,1)}, u32[]{:S(2)}, u32[]{:S(2)}) collective-permute-start(bf16[384,512]{1,0:T(8,128)(2,1)} %get-tuple-element.90), channel_id=1, source_target_pairs={{0,8},{4,12},{8,0},{12,4},{16,24},{20,28},{24,16},{28,20},{1,9},{5... | collective-permute-start | bytes 1179656 | tf_op jit(solution)/shard_map/ppermute | solution.py:304
  61.2 28.4 %collective-permute-start.15 = (bf16[768,512]{1,0:T(8,128)(2,1)}, bf16[768,512]{1,0:T(8,128)(2,1)S(1)}, u32[]{:S(2)}, u32[]{:S(2)}) collective-permute-start(bf16[768,512]{1,0:T(8,128)(2,1)} %copy-done.20), channel_id=1, source_target_pairs={{0,4},{4,0},{8,12},{12,8},{16,20},{20,16},{24,28},{28,24},{1,5},{5... | collective-permute-start | bytes 2359304 | tf_op jit(solution)/shard_map/ppermute | solution.py:304
  71.5 10.1 %collective-permute-start.11 = (bf16[448,768]{1,0:T(8,128)(2,1)}, bf16[448,768]{1,0:T(8,128)(2,1)S(1)}, u32[]{:S(2)}, u32[]{:S(2)}) collective-permute-start(bf16[448,768]{1,0:T(8,128)(2,1)} %copy-done.22), channel_id=1, source_target_pairs={{8,16},{12,20},{16,8},{20,12},{9,17},{13,21},{17,9},{21,13},{10,18... | collective-permute-start | bytes 2064392 | tf_op jit(solution)/shard_map/ppermute | solution.py:308
  73.6 16.0 %collective-permute-start.10 = (bf16[448,768]{1,0:T(8,128)(2,1)S(1)}, bf16[448,768]{1,0:T(8,128)(2,1)S(1)}, u32[]{:S(2)}, u32[]{:S(2)}) collective-permute-start(bf16[448,768]{1,0:T(8,128)(2,1)S(1)} %broadcast_select_fusion), channel_id=1, source_target_pairs={{0,8},{4,12},{24,16},{28,20},{8,0},{12,4},{16,24},{20,28},{1,9},{5... | collective-permute-start | bytes 2064392 | tf_op jit(solution)/shard_map/ppermute | solution.py:308
  75.5 4.2 %collective-permute-start.12 = (bf16[80,384]{1,0:T(8,128)(2,1)S(1)}, bf16[80,384]{1,0:T(8,128)(2,1)S(1)}, u32[]{:S(2)}, u32[]{:S(2)}) collective-permute-start(bf16[80,384]{1,0:T(8,128)(2,1)S(1)} %slice.4), channel_id=1, source_target_pairs={{0,2},{1,3},{2,0},{3,1},{4,6},{5,7},{6,4},{7,5},{8,10},{9,11},{10,... | collective-permute-start | bytes 184328 | tf_op jit(solution)/shard_map/ppermute | solution.py:304
  77.0 2.7 %collective-permute-start.13 = (bf16[80,384]{1,0:T(8,128)(2,1)S(1)}, bf16[80,384]{1,0:T(8,128)(2,1)S(1)}, u32[]{:S(2)}, u32[]{:S(2)}) collective-permute-start(bf16[80,384]{1,0:T(8,128)(2,1)S(1)} %slice.4), channel_id=1, source_target_pairs={{0,1},{1,0},{2,3},{3,2},{4,5},{5,4},{6,7},{7,6},{8,9},{9,8},{10,11... | collective-permute-start | bytes 184328 | tf_op jit(solution)/shard_map/ppermute | solution.py:304
  79.7 1.8 %collective-permute-start.14 = (bf16[80,384]{1,0:T(8,128)(2,1)S(1)}, bf16[80,384]{1,0:T(8,128)(2,1)S(1)}, u32[]{:S(2)}, u32[]{:S(2)}) collective-permute-start(bf16[80,384]{1,0:T(8,128)(2,1)S(1)} %collective-permute-done.12.p2), channel_id=1, source_target_pairs={{0,1},{1,0},{2,3},{3,2},{4,5},{5,4},{6,7},{7,6},{8,9},{9,8},{10,11... | collective-permute-start | bytes 184328 | tf_op jit(solution)/shard_map/ppermute | solution.py:304
  90.6 28.0 %collective-permute-start.18 = (bf16[768,512]{1,0:T(8,128)(2,1)S(1)}, bf16[768,512]{1,0:T(8,128)(2,1)S(1)}, u32[]{:S(2)}, u32[]{:S(2)}) collective-permute-start(bf16[768,512]{1,0:T(8,128)(2,1)S(1)} %get-tuple-element.115), channel_id=1, source_target_pairs={{0,4},{4,0},{8,12},{12,8},{16,20},{20,16},{24,28},{28,24},{1,5},{5... | collective-permute-start | bytes 2359304 | tf_op jit(solution)/shard_map/ppermute | solution.py:304
  91.3 26.4 %collective-permute-start.17 = (bf16[384,512]{1,0:T(8,128)(2,1)S(1)}, bf16[384,512]{1,0:T(8,128)(2,1)S(1)}, u32[]{:S(2)}, u32[]{:S(2)}) collective-permute-start(bf16[384,512]{1,0:T(8,128)(2,1)S(1)} %get-tuple-element.104), channel_id=1, source_target_pairs={{0,8},{4,12},{8,0},{12,4},{16,24},{20,28},{24,16},{28,20},{1,9},{5... | collective-permute-start | bytes 1179656 | tf_op jit(solution)/shard_map/ppermute | solution.py:304
  93.0 29.7 %collective-permute-start.19 = (bf16[448,768]{1,0:T(8,128)(2,1)S(1)}, bf16[448,768]{1,0:T(8,128)(2,1)S(1)}, u32[]{:S(2)}, u32[]{:S(2)}) collective-permute-start(bf16[448,768]{1,0:T(8,128)(2,1)S(1)} %collective-permute-done.10.rest_2_), channel_id=1, source_target_pairs={{8,16},{12,20},{16,8},{20,12},{9,17},{13,21},{17,9},{21,13},{10,18... | collective-permute-start | bytes 2064392 | tf_op jit(solution)/shard_map/ppermute | solution.py:308
  93.8 29.0 %collective-permute-start.20 = (bf16[448,768]{1,0:T(8,128)(2,1)}, bf16[448,768]{1,0:T(8,128)(2,1)S(1)}, u32[]{:S(2)}, u32[]{:S(2)}) collective-permute-start(bf16[448,768]{1,0:T(8,128)(2,1)} %collective-permute-done.9), channel_id=1, source_target_pairs={{8,0},{12,4},{16,24},{20,28},{9,1},{13,5},{17,25},{21,29},{10,2},{... | collective-permute-start | bytes 2064392 | tf_op jit(solution)/shard_map/ppermute | solution.py:308
  95.0 22.6 %collective-permute-start.16 = (bf16[192,512]{1,0:T(8,128)(2,1)S(1)}, bf16[192,512]{1,0:T(8,128)(2,1)S(1)}, u32[]{:S(2)}, u32[]{:S(2)}) collective-permute-start(bf16[192,512]{1,0:T(8,128)(2,1)S(1)} %get-tuple-element.98), channel_id=1, source_target_pairs={{0,16},{4,20},{8,24},{12,28},{16,0},{20,4},{24,8},{28,12},{1,17},{... | collective-permute-start | bytes 589832 | tf_op jit(solution)/shard_map/ppermute | solution.py:304
  119.5 11.8 %collective-permute-start.21 = (bf16[384,512]{1,0:T(8,128)(2,1)S(1)}, bf16[384,512]{1,0:T(8,128)(2,1)S(1)}, u32[]{:S(2)}, u32[]{:S(2)}) collective-permute-start(bf16[384,512]{1,0:T(8,128)(2,1)S(1)} %get-tuple-element.116), channel_id=1, source_target_pairs={{0,8},{4,12},{8,0},{12,4},{16,24},{20,28},{24,16},{28,20},{1,9},{5... | collective-permute-start | bytes 1179656 | tf_op jit(solution)/shard_map/ppermute | solution.py:304
  119.5 13.4 %collective-permute-start.22 = (bf16[192,512]{1,0:T(8,128)(2,1)S(1)}, bf16[192,512]{1,0:T(8,128)(2,1)S(1)}, u32[]{:S(2)}, u32[]{:S(2)}) collective-permute-start(bf16[192,512]{1,0:T(8,128)(2,1)S(1)} %get-tuple-element.112), channel_id=1, source_target_pairs={{0,16},{4,20},{8,24},{12,28},{16,0},{20,4},{24,8},{28,12},{1,17},{... | collective-permute-start | bytes 589832 | tf_op jit(solution)/shard_map/ppermute | solution.py:304
  132.0 9.6 %collective-permute-start.23 = (bf16[192,512]{1,0:T(8,128)(2,1)S(1)}, bf16[192,512]{1,0:T(8,128)(2,1)S(1)}, u32[]{:S(2)}, u32[]{:S(2)}) collective-permute-start(bf16[192,512]{1,0:T(8,128)(2,1)S(1)} %get-tuple-element.121), channel_id=1, source_target_pairs={{0,16},{4,20},{8,24},{12,28},{16,0},{20,4},{24,8},{28,12},{1,17},{... | collective-permute-start | bytes 589832 | tf_op jit(solution)/shard_map/ppermute | solution.py:304
  (27 other events, 351.7 us)

commit v8 on v7

--- a/solution.py
+++ b/solution.py
@@ -397,48 +397,49 @@
     crossed_a = routed(moving[0], across)
     crossed_b = routed(moving[1], across)
 
-    send_23, keep_23, *lhs_23 = weight_part(after(meta, got_01, *moving), (rows_y, rows_yc), act_a)
+    early_sent = after(arrived_early[:, :width], *moving)
+    early_c, early_y = swapped(early_sent, "tensor", 1), swapped(early_sent, "tensor", 2)
+
+    send_23, keep_23, *lhs_23 = weight_part(
+        after(meta, got_01, early_y, early_c, *moving), (rows_y, rows_yc), act_a
+    )
     got_23 = swapped(send_23, "dp", 1)
+    early_y = after(early_y, send_23)
+    early_yc = swapped(early_y, "tensor", 1)
     act_b, der_b = gelu(after(meta, send_23), False, part, part)
-    send_b, keep_b = weight_again(after(meta, act_b), part, act_b)
+    send_b, keep_b = weight_again(after(meta, act_b, early_yc), part, act_b)
     got_b = swapped(send_b, "dp", 1)
 
+    is_inner = (d // 2 == 1) | (d // 2 == 2)
+    hop = after(jnp.where(is_inner, crossed_a, moving[1]), send_b, got_23, at_inner_a)
+    hopped = routed(hop, to_inner + to_outer)
+    inner_a = routed(after(at_inner_a, hop), across)
+    act_c, der_c = gelu(after(meta, hop), False, 2 * part, part)
+    send_c, keep_c = weight_again(after(meta, act_c), 2 * part, act_c)
+    got_c = swapped(send_c, "dp", 1)
+
     out_na, mine_a = near_step(
-        after(meta, send_b, at_inner_a, crossed_a), (keep_01, keep_23), (got_01, got_23)
+        after(meta, send_c, hopped, crossed_b), (keep_01, keep_23), (got_01, got_23)
     )
     got_na = swapped(out_na, "dp", 2)
-    act_c, der_c = gelu(after(meta, out_na), False, 2 * part, part)
-    early_sent = after(arrived_early[:, :width], act_c)
-    early_c, early_y = swapped(early_sent, "tensor", 1), swapped(early_sent, "tensor", 2)
-    send_c, keep_c = weight_again(after(meta, act_c), 2 * part, act_c)
-    early_y = after(early_y, send_c, early_c)
-    early_yc = swapped(early_y, "tensor", 1)
-
-    is_inner = (d // 2 == 1) | (d // 2 == 2)
-    hop = jnp.where(is_inner, crossed_a, moving[1])
-    hop = after(hop, got_na, send_c, crossed_b)
-    hopped = routed(hop, to_inner + to_outer)
-    inner_a = routed(after(at_inner_a, send_c), across)
-
-    out_fa, own_a = far_step(after(meta, hop), mine_a, got_na)
-    got_fa = swapped(out_fa, "dp", 4)
-    out_nb, mine_b = near_step(after(meta, out_fa, hopped, inner_a, early_yc), (keep_b,), (got_b,))
+    inner_b = routed(after(hopped, out_na), across)
+    (kept_grad,) = grads(after(meta, out_na), SEND, EARLY, KEEP, (der_a, der_b, der_c), (ff,))
+    out_nb, mine_b = near_step(after(meta, kept_grad, inner_a), (keep_b,), (got_b,))
     got_nb = swapped(out_nb, "dp", 2)
-    got_c = swapped(after(send_c, out_nb), "dp", 1)
-    inner_b = routed(after(hopped, out_nb), across)
     outer_b = routed(after(crossed_b, out_nb), to_outer)
 
-    (kept_grad,) = grads(after(meta, out_nb), SEND, EARLY, KEEP, (der_a, der_b, der_c), (ff,))
     early_grad = kernel_call(
         functools.partial(early_kernel, 256), shape(EARLY, ff), [IN_VMEM] * 5, IN_VMEM,
         [vmem((EARLY, features), BF), vmem((EARLY, 256), F32)],
-    )(after(meta, kept_grad), arrived_early, early_c, early_y, early_yc, down_weight)
-
-    out_fb, own_b = far_step(after(meta, early_grad, got_fa), mine_b, got_nb)
+    )(after(meta, out_nb), arrived_early, early_c, early_y, early_yc, down_weight)
+
+    out_fa, own_a = far_step(after(meta, early_grad), mine_a, got_na)
+    got_fa = swapped(out_fa, "dp", 4)
+    out_nc, mine_c = near_step(after(meta, out_fa, inner_b), (keep_c,), (got_c,))
+    got_nc = swapped(out_nc, "dp", 2)
+    out_fb, own_b = far_step(after(meta, out_nc), mine_b, got_nb)
     got_fb = swapped(out_fb, "dp", 4)
-    out_nc, mine_c = near_step(after(meta, out_fb), (keep_c,), (got_c,))
-    got_nc = swapped(out_nc, "dp", 2)
-    out_fc, own_c = far_step(after(meta, out_nc, inner_b, outer_b), mine_c, got_nc)
+    out_fc, own_c = far_step(after(meta, out_fb, outer_b, got_fa), mine_c, got_nc)
     got_fc = swapped(out_fc, "dp", 4)
     total = [a + b.astype(F32) for a, b in ((own_a, got_fa), (own_b, got_fb), (own_c, got_fc))]
     down_grad = jnp.concatenate(total, axis=1) / math.sqrt(n * home)

time: 143 us -> 153 us (1.070)
  waiting for transfers between devices: 40.3 us -> 49.4 us
    ppermute x17, waiting for transfers between devices: 31.1 us -> 44.1 us  [swapped(): return lax.ppermute(block, axis, [(i, i ^ distance) for i in range(n)])]
    ppermute x7, starting transfers between devices: 13.4 us -> 17.7 us  [routed(): lax.ppermute(block, 'dp', [(2 * a + x, 2 * b + x) for a, b in pairs for x...]
    ppermute x7, waiting for transfers between devices: 9.15 us -> 5.31 us  [routed(): lax.ppermute(block, 'dp', [(2 * a + x, 2 * b + x) for a, b in pairs for x...]
    ppermute x17, starting transfers between devices: 24.9 us -> 22 us  [swapped(): return lax.ppermute(block, axis, [(i, i ^ distance) for i in range(n)])]
    unnamed x54 -> x52, local copies, waits for them, and re-layouts: 3.34 us -> 4.78 us
  transfers between devices with their start and end apart: 24 -> 24, of which waited for: 9 -> 11; matrix products, arithmetic and copies ran while one was open for 1% -> 0% of each run, Pallas kernels for 36% -> 31%
where the time goes in v8:
time: 153 us
  Pallas kernels  55.6 us (36%)
  waiting for transfers between devices  49.4 us (32%)
  starting transfers between devices  39.6 us (26%)
  local copies, waits for them, and re-layouts  4.79 us (3%)
  other arithmetic  2.1 us (1%)
    ppermute x17, waiting for transfers between devices, swapped(): return lax.ppermute(block, axis, [(i, i ^ distance) for i in range(n)])  44.1 us
    ppermute x17, starting transfers between devices, swapped(): return lax.ppermute(block, axis, [(i, i ^ distance) for i in range(n)])  22 us
    pallas_call x4, Pallas kernels, gelu(): kernel_call(functools.partial(gelu_kernel, late, base, block), [shape(row...  21.4 us
    ppermute x7, starting transfers between devices, routed(): lax.ppermute(block, 'dp', [(2 * a + x, 2 * b + x) for a, b in pairs for x...  17.7 us
    pallas_call x2, Pallas kernels, grads(): kernel_call(functools.partial(grad_kernel, first_row, first_slope, len(sl...  6.68 us
    pallas_call x2, Pallas kernels, weight_again(): kernel_call(functools.partial(weight_again_kernel, base), [shape(4 * half...  5.7 us
    ppermute x7, waiting for transfers between devices, routed(): lax.ppermute(block, 'dp', [(2 * a + x, 2 * b + x) for a, b in pairs for x...  5.31 us
    unnamed x52, local copies, waits for them, and re-layouts  4.78 us
  transfers between devices with their start and end apart: 24, of which 11 were waited for; matrix products, arithmetic and copies ran while one was open for 0% of the time, Pallas kernels for 31%

profile of v8, /device:TPU:0, one launch (start us, length us, event | category | flops | bytes accessed | tf_op | source)
XLA Modules:
  0.0 152.7 jit_solution(8312098672714728822)
XLA Ops:
  1.4 4.7 %shard_map.77 = (bf16[1056,384]{1,0:T(8,128)(2,1)S(1)}, bf16[80,1920]{1,0:T(8,128)(2,1)S(1)}) custom-call(s32[9,8]{1,0:T(8,128)S(1)} %pad_add_fusion.meta, bf16[1032,384]{1,0:T(8,128)(2,1)} %cot_hbm.1, f32[1536]{0:T(1024)} %scale_hbm.1, bf16[1032,1536]{1,0:T(8,128)(2,1)} %pre_hbm.9), custom_call_target="tpu_custom_call" | custom-call | flops 1 | bytes 1 | tf_op jit(solution)/shard_map/pallas_call | solution.py:378
  6.6 2.6 %collective-permute-start = (bf16[1056,384]{1,0:T(8,128)(2,1)S(1)}, bf16[1056,384]{1,0:T(8,128)(2,1)S(1)}, u32[]{:S(2)}, u32[]{:S(2)}) collective-permute-start(bf16[1056,384]{1,0:T(8,128)(2,1)S(1)} %get-tuple-element.63.refs_0_.p0), channel_id=1, source_target_pairs={{0,2},{1,3},{2,0},{3,1},{4,6},{5,7},{6,4},{7,5},{8,10},{9,11},{10,... | collective-permute-start | bytes 2433032 | tf_op jit(solution)/shard_map/ppermute | solution.py:304
  9.2 2.6 %collective-permute-start.2 = (bf16[80,1920]{1,0:T(8,128)(2,1)S(1)}, bf16[80,1920]{1,0:T(8,128)(2,1)S(1)}, u32[]{:S(2)}, u32[]{:S(2)}) collective-permute-start(bf16[80,1920]{1,0:T(8,128)(2,1)S(1)} %get-tuple-element.70), channel_id=1, source_target_pairs={{0,16},{4,20},{8,24},{12,28},{16,0},{20,4},{24,8},{28,12},{1,17},{... | collective-permute-start | bytes 921608 | tf_op jit(solution)/shard_map/ppermute | solution.py:304
  11.8 7.7 %shard_map.78 = (bf16[448,1536]{1,0:T(8,128)(2,1)S(1)}, f32[448,1536]{1,0:T(8,128)S(1)}) custom-call(s32[9,8]{1,0:T(8,128)S(1)} %pad_add_fusion.meta, bf16[1032,1536]{1,0:T(8,128)(2,1)} %pre_hbm.9), custom_call_target="tpu_custom_call" | custom-call | flops 1 | bytes 1 | tf_op jit(solution)/shard_map/pallas_call | solution.py:336
  19.5 4.4 %shard_map.79 = (bf16[608,512]{1,0:T(8,128)(2,1)S(1)}, f32[608,512]{1,0:T(8,128)S(1)}) custom-call(s32[9,8]{1,0:T(8,128)S(1)} %pad_add_fusion.meta, bf16[1032,1536]{1,0:T(8,128)(2,1)} %pre_hbm.9), custom_call_target="tpu_custom_call" | custom-call | flops 1 | bytes 1 | tf_op jit(solution)/shard_map/pallas_call | solution.py:336
  27.8 2.3 %collective-permute-done.3.p3.refs_1_ = bf16[1056,384]{1,0:T(8,128)(2,1)S(1)} collective-permute-done((bf16[1056,384]{1,0:T(8,128)(2,1)S(1)}, bf16[1056,384]{1,0:T(8,128)(2,1)S(1)}, u32[]{:S(2)}, u32[]{:S(2)}) %collective-permute-start.3) | collective-permute-done | bytes 811040 | tf_op jit(solution)/shard_map/ppermute | solution.py:304
  30.2 3.2 %shard_map.81 = (bf16[448,768]{1,0:T(8,128)(2,1)}, bf16[448,768]{1,0:T(8,128)(2,1)S(1)}) custom-call(s32[9,8]{1,0:T(8,128)S(1)} %pad_add_fusion.meta, bf16[1056,384]{1,0:T(8,128)(2,1)S(1)} %get-tuple-element.63.refs_0_.p0, bf16[1056,384]{1,0:T(8,128)(2,1)S(1)} %collective-permute-done.1.refs_1_.p1, bf16[1056,384]{1,0:T(8,128)(2,1)S(1)} %collective-permute-done.p2.refs_0_, ...), custom_call_target="tpu_custom_call" | custom-call | flops 1 | bytes 1 | tf_op jit(solution)/shard_map/pallas_call | solution.py:360
  36.7 6.3 %collective-permute-start.10 = (bf16[448,768]{1,0:T(8,128)(2,1)}, bf16[448,768]{1,0:T(8,128)(2,1)}, u32[]{:S(2)}, u32[]{:S(2)}) collective-permute-start(bf16[448,768]{1,0:T(8,128)(2,1)} %get-tuple-element.74), channel_id=1, source_target_pairs={{0,8},{4,12},{24,16},{28,20},{1,9},{5,13},{25,17},{29,21},{2,10},{... | collective-permute-start | bytes 2064392 | tf_op jit(solution)/shard_map/ppermute | solution.py:308
  47.4 2.6 %shard_map.82 = (bf16[384,512]{1,0:T(8,128)(2,1)}, f32[384,512]{1,0:T(8,128)S(1)}, bf16[768,448]{1,0:T(8,128)(2,1)S(1)}, bf16[768,608]{1,0:T(8,128)(2,1)S(1)}) custom-call(s32[9,8]{1,0:T(8,128)S(1)} %pad_add_fusion.meta, bf16[1056,384]{1,0:T(8,128)(2,1)S(1)} %collective-permute-done.p2.refs_0_, bf16[1056,384]{1,0:T(8,128)(2,1)S(1)} %collective-permute-done.3.p3.refs_1_, ...), custom_call_target="tpu_custom_call" | custom-call | flops 1 | bytes 1 | tf_op jit(solution)/shard_map/pallas_call | solution.py:346
  55.1 4.4 %shard_map.83 = (bf16[608,512]{1,0:T(8,128)(2,1)S(1)}, f32[608,512]{1,0:T(8,128)S(1)}) custom-call(s32[9,8]{1,0:T(8,128)S(1)} %pad_add_fusion.meta, bf16[1032,1536]{1,0:T(8,128)(2,1)} %pre_hbm.9), custom_call_target="tpu_custom_call" | custom-call | flops 1 | bytes 1 | tf_op jit(solution)/shard_map/pallas_call | solution.py:336
  60.7 2.8 %shard_map.84 = (bf16[768,512]{1,0:T(8,128)(2,1)S(1)}, f32[768,512]{1,0:T(8,128)S(1)}) custom-call(s32[9,8]{1,0:T(8,128)S(1)} %pad_add_fusion.meta, bf16[768,448]{1,0:T(8,128)(2,1)S(1)} %copy-done.9, bf16[768,608]{1,0:T(8,128)(2,1)S(1)} %copy-done.5, bf16[768,448]{1,0:T(8,128)(2,1)S(1)} %copy-done.11, bf16[768,608]{1,0:T(8,128)(2,1)S(1)} %copy-done.7, ...), custom_call_target="tpu_custom_call" | custom-call | flops 1 | bytes 1 | tf_op jit(solution)/shard_map/pallas_call | solution.py:354
  63.8 6.1 %collective-permute-start.11 = (bf16[448,768]{1,0:T(8,128)(2,1)S(1)}, bf16[448,768]{1,0:T(8,128)(2,1)S(1)}, u32[]{:S(2)}, u32[]{:S(2)}) collective-permute-start(bf16[448,768]{1,0:T(8,128)(2,1)S(1)} %broadcast_select_fusion), channel_id=1, source_target_pairs={{0,8},{4,12},{24,16},{28,20},{8,0},{12,4},{16,24},{20,28},{1,9},{5... | collective-permute-start | bytes 2064392 | tf_op jit(solution)/shard_map/ppermute | solution.py:308
  71.2 4.8 %shard_map.85 = (bf16[608,512]{1,0:T(8,128)(2,1)S(1)}, f32[608,512]{1,0:T(8,128)S(1)}) custom-call(s32[9,8]{1,0:T(8,128)S(1)} %pad_add_fusion.meta, bf16[1032,1536]{1,0:T(8,128)(2,1)} %pre_hbm.9), custom_call_target="tpu_custom_call" | custom-call | flops 1 | bytes 1 | tf_op jit(solution)/shard_map/pallas_call | solution.py:336
  76.0 2.9 %shard_map.86 = (bf16[768,512]{1,0:T(8,128)(2,1)S(1)}, f32[768,512]{1,0:T(8,128)S(1)}) custom-call(s32[9,8]{1,0:T(8,128)S(1)} %pad_add_fusion.meta, bf16[768,448]{1,0:T(8,128)(2,1)S(1)} %copy-done.9, bf16[768,608]{1,0:T(8,128)(2,1)S(1)} %copy-done.5, bf16[768,448]{1,0:T(8,128)(2,1)S(1)} %copy-done.11, bf16[768,608]{1,0:T(8,128)(2,1)S(1)} %copy-done.7, ...), custom_call_target="tpu_custom_call" | custom-call | flops 1 | bytes 1 | tf_op jit(solution)/shard_map/pallas_call | solution.py:354
  80.4 5.3 %collective-permute-done.11.rest_2_ = bf16[448,768]{1,0:T(8,128)(2,1)S(1)} collective-permute-done((bf16[448,768]{1,0:T(8,128)(2,1)S(1)}, bf16[448,768]{1,0:T(8,128)(2,1)S(1)}, u32[]{:S(2)}, u32[]{:S(2)}) %collective-permute-start.11) | collective-permute-done | bytes 688160 | tf_op jit(solution)/shard_map/ppermute | solution.py:308
  88.4 4.6 %collective-permute-start.15 = (bf16[384,512]{1,0:T(8,128)(2,1)S(1)}, bf16[384,512]{1,0:T(8,128)(2,1)S(1)}, u32[]{:S(2)}, u32[]{:S(2)}) collective-permute-start(bf16[384,512]{1,0:T(8,128)(2,1)S(1)} %get-tuple-element.96), channel_id=1, source_target_pairs={{0,8},{4,12},{8,0},{12,4},{16,24},{20,28},{24,16},{28,20},{1,9},{5... | collective-permute-start | bytes 1179656 | tf_op jit(solution)/shard_map/ppermute | solution.py:304
  93.0 3.5 %shard_map.88.kept = bf16[528,1536]{1,0:T(8,128)(2,1)S(1)} custom-call(s32[9,8]{1,0:T(8,128)S(1)} %pad_add_fusion.meta, bf16[1056,384]{1,0:T(8,128)(2,1)S(1)} %get-tuple-element.63.refs_0_.p0, bf16[1056,384]{1,0:T(8,128)(2,1)S(1)} %collective-permute-done.1.refs_1_.p1, bf16[1056,384]{1,0:T(8,128)(2,1)S(1)} %copy-done.1, bf16[1056,384]{1,0:T(8,128)(2,1)S(1)} %copy-done.3, ...), custom_call_target="tpu_custom_call" | custom-call | flops 1 | bytes 1 | tf_op jit(solution)/shard_map/pallas_call | solution.py:360
  98.7 2.7 %collective-permute-start.18 = (bf16[384,512]{1,0:T(8,128)(2,1)S(1)}, bf16[384,512]{1,0:T(8,128)(2,1)S(1)}, u32[]{:S(2)}, u32[]{:S(2)}) collective-permute-start(bf16[384,512]{1,0:T(8,128)(2,1)S(1)} %get-tuple-element.104), channel_id=1, source_target_pairs={{0,8},{4,12},{8,0},{12,4},{16,24},{20,28},{24,16},{28,20},{1,9},{5... | collective-permute-start | bytes 1179656 | tf_op jit(solution)/shard_map/ppermute | solution.py:304
  101.4 3.2 %shard_map.90.early = bf16[80,1536]{1,0:T(8,128)(2,1)S(1)} custom-call(s32[9,8]{1,0:T(8,128)S(1)} %pad_add_fusion.meta, bf16[80,1920]{1,0:T(8,128)(2,1)S(1)} %collective-permute-done.2.own, bf16[80,384]{1,0:T(8,128)(2,1)S(1)} %collective-permute-done.7.p1, bf16[80,384]{1,0:T(8,128)(2,1)S(1)} %collective-permute-done.6.p2, ...), custom_call_target="tpu_custom_call" | custom-call | flops 1 | bytes 1 | tf_op jit(solution)/shard_map/pallas_call | solution.py:431
  107.1 2.1 %collective-permute-start.21 = (bf16[384,512]{1,0:T(8,128)(2,1)S(1)}, bf16[384,512]{1,0:T(8,128)(2,1)S(1)}, u32[]{:S(2)}, u32[]{:S(2)}) collective-permute-start(bf16[384,512]{1,0:T(8,128)(2,1)S(1)} %get-tuple-element.112), channel_id=1, source_target_pairs={{0,8},{4,12},{8,0},{12,4},{16,24},{20,28},{24,16},{28,20},{1,9},{5... | collective-permute-start | bytes 1179656 | tf_op jit(solution)/shard_map/ppermute | solution.py:304
  109.2 21.1 %collective-permute-done.18.got = bf16[384,512]{1,0:T(8,128)(2,1)S(1)} collective-permute-done((bf16[384,512]{1,0:T(8,128)(2,1)S(1)}, bf16[384,512]{1,0:T(8,128)(2,1)S(1)}, u32[]{:S(2)}, u32[]{:S(2)}) %collective-permute-start.18) | collective-permute-done | bytes 393248 | tf_op jit(solution)/shard_map/ppermute | solution.py:304
  131.3 10.1 %collective-permute-done.21.got = bf16[384,512]{1,0:T(8,128)(2,1)S(1)} collective-permute-done((bf16[384,512]{1,0:T(8,128)(2,1)S(1)}, bf16[384,512]{1,0:T(8,128)(2,1)S(1)}, u32[]{:S(2)}, u32[]{:S(2)}) %collective-permute-start.21) | collective-permute-done | bytes 393248 | tf_op jit(solution)/shard_map/ppermute | solution.py:304
  142.3 3.3 %shard_map.95 = bf16[720,1536]{1,0:T(8,128)(2,1)} custom-call(s32[9,8]{1,0:T(8,128)S(1)} %pad_add_fusion.meta, bf16[528,1536]{1,0:T(8,128)(2,1)S(1)} %shard_map.88.kept, bf16[80,1536]{1,0:T(8,128)(2,1)S(1)} %shard_map.90.early, bf16[448,768]{1,0:T(8,128)(2,1)S(1)} %collective-permute-done.13.rest_0_, bf16[448,768]{1,0:T(8,128)(2,1)S(1)} %collective-permute-done.16.rest_1_, ...), custom_call_target="tpu_custom_call" | custom-call | flops 1 | bytes 1 | tf_op jit(solution)/shard_map/pallas_call | solution.py:447
  145.6 5.9 %collective-permute-done.23 = bf16[192,512]{1,0:T(8,128)(2,1)S(1)} collective-permute-done((bf16[192,512]{1,0:T(8,128)(2,1)S(1)}, bf16[192,512]{1,0:T(8,128)(2,1)S(1)}, u32[]{:S(2)}, u32[]{:S(2)}) %collective-permute-start.23) | collective-permute-done | bytes 196640 | tf_op jit(solution)/shard_map/ppermute | solution.py:304
  (105 shorter events, 32.3 us)
Async XLA Ops:
  6.1 17.9 %collective-permute-start.1 = (bf16[1056,384]{1,0:T(8,128)(2,1)S(1)}, bf16[1056,384]{1,0:T(8,128)(2,1)S(1)}, u32[]{:S(2)}, u32[]{:S(2)}) collective-permute-start(bf16[1056,384]{1,0:T(8,128)(2,1)S(1)} %get-tuple-element.63.refs_0_.p0), channel_id=1, source_target_pairs={{0,1},{1,0},{2,3},{3,2},{4,5},{5,4},{6,7},{7,6},{8,9},{9,8},{10,11... | collective-permute-start | bytes 2433032 | tf_op jit(solution)/shard_map/ppermute | solution.py:304
  6.6 21.3 %collective-permute-start = (bf16[1056,384]{1,0:T(8,128)(2,1)S(1)}, bf16[1056,384]{1,0:T(8,128)(2,1)S(1)}, u32[]{:S(2)}, u32[]{:S(2)}) collective-permute-start(bf16[1056,384]{1,0:T(8,128)(2,1)S(1)} %get-tuple-element.63.refs_0_.p0), channel_id=1, source_target_pairs={{0,2},{1,3},{2,0},{3,1},{4,6},{5,7},{6,4},{7,5},{8,10},{9,11},{10,... | collective-permute-start | bytes 2433032 | tf_op jit(solution)/shard_map/ppermute | solution.py:304
  9.2 16.8 %collective-permute-start.2 = (bf16[80,1920]{1,0:T(8,128)(2,1)S(1)}, bf16[80,1920]{1,0:T(8,128)(2,1)S(1)}, u32[]{:S(2)}, u32[]{:S(2)}) collective-permute-start(bf16[80,1920]{1,0:T(8,128)(2,1)S(1)} %get-tuple-element.70), channel_id=1, source_target_pairs={{0,16},{4,20},{8,24},{12,28},{16,0},{20,4},{24,8},{28,12},{1,17},{... | collective-permute-start | bytes 921608 | tf_op jit(solution)/shard_map/ppermute | solution.py:304
  27.8 2.3 %collective-permute-start.3 = (bf16[1056,384]{1,0:T(8,128)(2,1)S(1)}, bf16[1056,384]{1,0:T(8,128)(2,1)S(1)}, u32[]{:S(2)}, u32[]{:S(2)}) collective-permute-start(bf16[1056,384]{1,0:T(8,128)(2,1)S(1)} %collective-permute-done.p2.refs_0_), channel_id=1, source_target_pairs={{0,1},{1,0},{2,3},{3,2},{4,5},{5,4},{6,7},{7,6},{8,9},{9,8},{10,11... | collective-permute-start | bytes 2433032 | tf_op jit(solution)/shard_map/ppermute | solution.py:304
  33.4 30.1 %collective-permute-start.4 = (bf16[448,768]{1,0:T(8,128)(2,1)}, bf16[448,768]{1,0:T(8,128)(2,1)}, u32[]{:S(2)}, u32[]{:S(2)}) collective-permute-start(bf16[448,768]{1,0:T(8,128)(2,1)} %get-tuple-element.74), channel_id=1, source_target_pairs={{8,16},{12,20},{16,8},{20,12},{9,17},{13,21},{17,9},{21,13},{10,18... | collective-permute-start | bytes 2064392 | tf_op jit(solution)/shard_map/ppermute | solution.py:308
  35.0 11.2 %collective-permute-start.5 = (bf16[384,512]{1,0:T(8,128)(2,1)S(1)}, bf16[384,512]{1,0:T(8,128)(2,1)S(1)}, u32[]{:S(2)}, u32[]{:S(2)}) collective-permute-start(bf16[384,512]{1,0:T(8,128)(2,1)S(1)} %get-tuple-element.69), channel_id=1, source_target_pairs={{0,4},{4,0},{8,12},{12,8},{16,20},{20,16},{24,28},{28,24},{1,5},{5... | collective-permute-start | bytes 1179656 | tf_op jit(solution)/shard_map/ppermute | solution.py:304
  36.7 27.1 %collective-permute-start.10 = (bf16[448,768]{1,0:T(8,128)(2,1)}, bf16[448,768]{1,0:T(8,128)(2,1)}, u32[]{:S(2)}, u32[]{:S(2)}) collective-permute-start(bf16[448,768]{1,0:T(8,128)(2,1)} %get-tuple-element.74), channel_id=1, source_target_pairs={{0,8},{4,12},{24,16},{28,20},{1,9},{5,13},{25,17},{29,21},{2,10},{... | collective-permute-start | bytes 2064392 | tf_op jit(solution)/shard_map/ppermute | solution.py:308
  43.0 3.9 %collective-permute-start.7 = (bf16[80,384]{1,0:T(8,128)(2,1)S(1)}, bf16[80,384]{1,0:T(8,128)(2,1)S(1)}, u32[]{:S(2)}, u32[]{:S(2)}) collective-permute-start(bf16[80,384]{1,0:T(8,128)(2,1)S(1)} %slice.4), channel_id=1, source_target_pairs={{0,1},{1,0},{2,3},{3,2},{4,5},{5,4},{6,7},{7,6},{8,9},{9,8},{10,11... | collective-permute-start | bytes 184328 | tf_op jit(solution)/shard_map/ppermute | solution.py:304
  43.0 4.4 %collective-permute-start.6 = (bf16[80,384]{1,0:T(8,128)(2,1)S(1)}, bf16[80,384]{1,0:T(8,128)(2,1)S(1)}, u32[]{:S(2)}, u32[]{:S(2)}) collective-permute-start(bf16[80,384]{1,0:T(8,128)(2,1)S(1)} %slice.4), channel_id=1, source_target_pairs={{0,2},{1,3},{2,0},{3,1},{4,6},{5,7},{6,4},{7,5},{8,10},{9,11},{10,... | collective-permute-start | bytes 184328 | tf_op jit(solution)/shard_map/ppermute | solution.py:304
  52.8 11.0 %collective-permute-start.9 = (bf16[384,512]{1,0:T(8,128)(2,1)}, bf16[384,512]{1,0:T(8,128)(2,1)}, u32[]{:S(2)}, u32[]{:S(2)}) collective-permute-start(bf16[384,512]{1,0:T(8,128)(2,1)} %get-tuple-element.78), channel_id=1, source_target_pairs={{0,4},{4,0},{8,12},{12,8},{16,20},{20,16},{24,28},{28,24},{1,5},{5... | collective-permute-start | bytes 1179656 | tf_op jit(solution)/shard_map/ppermute | solution.py:304
  54.0 5.5 %collective-permute-start.8 = (bf16[80,384]{1,0:T(8,128)(2,1)S(1)}, bf16[80,384]{1,0:T(8,128)(2,1)S(1)}, u32[]{:S(2)}, u32[]{:S(2)}) collective-permute-start(bf16[80,384]{1,0:T(8,128)(2,1)S(1)} %collective-permute-done.6.p2), channel_id=1, source_target_pairs={{0,1},{1,0},{2,3},{3,2},{4,5},{5,4},{6,7},{7,6},{8,9},{9,8},{10,11... | collective-permute-start | bytes 184328 | tf_op jit(solution)/shard_map/ppermute | solution.py:304
  54.0 26.4 %collective-permute-start.12 = (bf16[448,768]{1,0:T(8,128)(2,1)}, bf16[448,768]{1,0:T(8,128)(2,1)S(1)}, u32[]{:S(2)}, u32[]{:S(2)}) collective-permute-start(bf16[448,768]{1,0:T(8,128)(2,1)} %copy-done.18), channel_id=1, source_target_pairs={{8,16},{12,20},{16,8},{20,12},{9,17},{13,21},{17,9},{21,13},{10,18... | collective-permute-start | bytes 2064392 | tf_op jit(solution)/shard_map/ppermute | solution.py:308
  63.8 21.9 %collective-permute-start.11 = (bf16[448,768]{1,0:T(8,128)(2,1)S(1)}, bf16[448,768]{1,0:T(8,128)(2,1)S(1)}, u32[]{:S(2)}, u32[]{:S(2)}) collective-permute-start(bf16[448,768]{1,0:T(8,128)(2,1)S(1)} %broadcast_select_fusion), channel_id=1, source_target_pairs={{0,8},{4,12},{24,16},{28,20},{8,0},{12,4},{16,24},{20,28},{1,9},{5... | collective-permute-start | bytes 2064392 | tf_op jit(solution)/shard_map/ppermute | solution.py:308
  69.9 26.5 %collective-permute-start.14 = (bf16[768,512]{1,0:T(8,128)(2,1)S(1)}, bf16[768,512]{1,0:T(8,128)(2,1)S(1)}, u32[]{:S(2)}, u32[]{:S(2)}) collective-permute-start(bf16[768,512]{1,0:T(8,128)(2,1)S(1)} %get-tuple-element.87), channel_id=1, source_target_pairs={{0,4},{4,0},{8,12},{12,8},{16,20},{20,16},{24,28},{28,24},{1,5},{5... | collective-permute-start | bytes 2359304 | tf_op jit(solution)/shard_map/ppermute | solution.py:304
  70.4 26.0 %collective-permute-start.13 = (bf16[448,768]{1,0:T(8,128)(2,1)}, bf16[448,768]{1,0:T(8,128)(2,1)S(1)}, u32[]{:S(2)}, u32[]{:S(2)}) collective-permute-start(bf16[448,768]{1,0:T(8,128)(2,1)} %collective-permute-done.10), channel_id=1, source_target_pairs={{8,16},{12,20},{16,8},{20,12},{9,17},{13,21},{17,9},{21,13},{10,18... | collective-permute-start | bytes 2064392 | tf_op jit(solution)/shard_map/ppermute | solution.py:308
  78.9 27.3 %collective-permute-start.17 = (bf16[768,512]{1,0:T(8,128)(2,1)S(1)}, bf16[768,512]{1,0:T(8,128)(2,1)S(1)}, u32[]{:S(2)}, u32[]{:S(2)}) collective-permute-start(bf16[768,512]{1,0:T(8,128)(2,1)S(1)} %get-tuple-element.92), channel_id=1, source_target_pairs={{0,4},{4,0},{8,12},{12,8},{16,20},{20,16},{24,28},{28,24},{1,5},{5... | collective-permute-start | bytes 2359304 | tf_op jit(solution)/shard_map/ppermute | solution.py:304
  87.6 18.0 %collective-permute-start.16 = (bf16[448,768]{1,0:T(8,128)(2,1)S(1)}, bf16[448,768]{1,0:T(8,128)(2,1)S(1)}, u32[]{:S(2)}, u32[]{:S(2)}) collective-permute-start(bf16[448,768]{1,0:T(8,128)(2,1)S(1)} %collective-permute-done.11.rest_2_), channel_id=1, source_target_pairs={{8,16},{12,20},{16,8},{20,12},{9,17},{13,21},{17,9},{21,13},{10,18... | collective-permute-start | bytes 2064392 | tf_op jit(solution)/shard_map/ppermute | solution.py:308
  88.4 16.3 %collective-permute-start.15 = (bf16[384,512]{1,0:T(8,128)(2,1)S(1)}, bf16[384,512]{1,0:T(8,128)(2,1)S(1)}, u32[]{:S(2)}, u32[]{:S(2)}) collective-permute-start(bf16[384,512]{1,0:T(8,128)(2,1)S(1)} %get-tuple-element.96), channel_id=1, source_target_pairs={{0,8},{4,12},{8,0},{12,4},{16,24},{20,28},{24,16},{28,20},{1,9},{5... | collective-permute-start | bytes 1179656 | tf_op jit(solution)/shard_map/ppermute | solution.py:304
  97.4 33.9 %collective-permute-start.19 = (bf16[448,768]{1,0:T(8,128)(2,1)S(1)}, bf16[448,768]{1,0:T(8,128)(2,1)S(1)}, u32[]{:S(2)}, u32[]{:S(2)}) collective-permute-start(bf16[448,768]{1,0:T(8,128)(2,1)S(1)} %collective-permute-done.12), channel_id=1, source_target_pairs={{8,0},{12,4},{16,24},{20,28},{9,1},{13,5},{17,25},{21,29},{10,2},{... | collective-permute-start | bytes 2064392 | tf_op jit(solution)/shard_map/ppermute | solution.py:308
  98.7 31.6 %collective-permute-start.18 = (bf16[384,512]{1,0:T(8,128)(2,1)S(1)}, bf16[384,512]{1,0:T(8,128)(2,1)S(1)}, u32[]{:S(2)}, u32[]{:S(2)}) collective-permute-start(bf16[384,512]{1,0:T(8,128)(2,1)S(1)} %get-tuple-element.104), channel_id=1, source_target_pairs={{0,8},{4,12},{8,0},{12,4},{16,24},{20,28},{24,16},{28,20},{1,9},{5... | collective-permute-start | bytes 1179656 | tf_op jit(solution)/shard_map/ppermute | solution.py:304
  105.5 25.7 %collective-permute-start.20 = (bf16[192,512]{1,0:T(8,128)(2,1)S(1)}, bf16[192,512]{1,0:T(8,128)(2,1)S(1)}, u32[]{:S(2)}, u32[]{:S(2)}) collective-permute-start(bf16[192,512]{1,0:T(8,128)(2,1)S(1)} %get-tuple-element.108), channel_id=1, source_target_pairs={{0,16},{4,20},{8,24},{12,28},{16,0},{20,4},{24,8},{28,12},{1,17},{... | collective-permute-start | bytes 589832 | tf_op jit(solution)/shard_map/ppermute | solution.py:304
  107.1 34.3 %collective-permute-start.21 = (bf16[384,512]{1,0:T(8,128)(2,1)S(1)}, bf16[384,512]{1,0:T(8,128)(2,1)S(1)}, u32[]{:S(2)}, u32[]{:S(2)}) collective-permute-start(bf16[384,512]{1,0:T(8,128)(2,1)S(1)} %get-tuple-element.112), channel_id=1, source_target_pairs={{0,8},{4,12},{8,0},{12,4},{16,24},{20,28},{24,16},{28,20},{1,9},{5... | collective-permute-start | bytes 1179656 | tf_op jit(solution)/shard_map/ppermute | solution.py:304
  131.1 11.1 %collective-permute-start.22 = (bf16[192,512]{1,0:T(8,128)(2,1)S(1)}, bf16[192,512]{1,0:T(8,128)(2,1)S(1)}, u32[]{:S(2)}, u32[]{:S(2)}) collective-permute-start(bf16[192,512]{1,0:T(8,128)(2,1)S(1)} %get-tuple-element.115), channel_id=1, source_target_pairs={{0,16},{4,20},{8,24},{12,28},{16,0},{20,4},{24,8},{28,12},{1,17},{... | collective-permute-start | bytes 589832 | tf_op jit(solution)/shard_map/ppermute | solution.py:304
  142.1 9.3 %collective-permute-start.23 = (bf16[192,512]{1,0:T(8,128)(2,1)S(1)}, bf16[192,512]{1,0:T(8,128)(2,1)S(1)}, u32[]{:S(2)}, u32[]{:S(2)}) collective-permute-start(bf16[192,512]{1,0:T(8,128)(2,1)S(1)} %get-tuple-element.119), channel_id=1, source_target_pairs={{0,16},{4,20},{8,24},{12,28},{16,0},{20,4},{24,8},{28,12},{1,17},{... | collective-permute-start | bytes 589832 | tf_op jit(solution)/shard_map/ppermute | solution.py:304
  (26 other events, 265.1 us)

commit v9 on v8

--- a/solution.py
+++ b/solution.py
@@ -11,7 +11,7 @@
 SEND = 528
 KEEP = 528
 TILE = 16
-EARLY = 80
+EARLY = 48
 LATE = SEND - EARLY
 SLOTS = 4
 BAL = 720
@@ -107,7 +107,7 @@
     return (rows * own[None, :]).astype(BF)
 
 
-def first_kernel(meta, cot_hbm, scale_hbm, pre_hbm, rows_out, early_out, cot, scale, pre, sems):
+def first_kernel(meta, cot_hbm, scale_hbm, pre_hbm, late_out, rest_out, early_out, cot, scale, pre, sems):
     home, width = cot.shape
     pairs = ((cot_hbm, cot), (scale_hbm, scale), (pre_hbm, pre))
     copies = [pltpu.make_async_copy(a, b, sems.at[i]) for i, (a, b) in enumerate(pairs)]
@@ -118,9 +118,9 @@
     copies[1].wait()
     early_rows = scaled_rows(meta, early, cot, scale)
     early_out[:, :width] = early_rows
-    rows_out[0:LATE, :] = scaled_rows(meta, late_picks(meta, home), cot, scale)
-    rows_out[LATE:SEND, :] = early_rows
-    rows_out[SEND:, :] = scaled_rows(meta, kept_picks(meta, home), cot, scale)
+    late_out[...] = scaled_rows(meta, late_picks(meta, home), cot, scale)
+    rest_out[0:EARLY, :] = early_rows
+    rest_out[EARLY:, :] = scaled_rows(meta, kept_picks(meta, home), cot, scale)
     copies[2].wait()
     early_out[:, width:] = jnp.dot(early, pre[...], preferred_element_type=F32).astype(BF)
 
@@ -200,34 +200,29 @@
         lax.fori_loop(0, EARLY // TILE, body, 0)
 
 
-def product(lhs_late, lhs_rest, act_late, act_rest, base):
-    columns = slice(base, base + act_rest.shape[1])
-    return jnp.dot(lhs_late[...], act_late[:, columns], preferred_element_type=F32) + jnp.dot(
-        lhs_rest[...], act_rest[...], preferred_element_type=F32
-    )
-
-
 def weight_kernel(count, base, meta, *refs):
-    pieces, (act_late, act_rest, send, keep, lhs_late, lhs_rest) = refs[:count], refs[count:]
-    half = pieces[0].shape[1] // 2
+    lates, rests = refs[:count], refs[count : 2 * count]
+    act_late, act_rest, send, keep, lhs_late, lhs_rest = refs[2 * count :]
+    half = lates[0].shape[1] // 2
     mine = dp_at(meta) % 2 == 0
-    for i, piece in enumerate(pieces):
-        for rows, lhs in ((slice(0, LATE), lhs_late), (slice(LATE, SEND + KEEP), lhs_rest)):
-            both = piece[rows, :].T
+    for i in range(count):
+        for piece, lhs in ((lates[i], lhs_late), (rests[i], lhs_rest)):
+            both = piece[...].T
             lo, hi = both[:half], both[half:]
             lhs[i * half : (i + 1) * half, :] = jnp.where(mine, hi, lo)
             lhs[(count + i) * half : (count + i + 1) * half, :] = jnp.where(mine, lo, hi)
-    value = product(lhs_late, lhs_rest, act_late, act_rest, base)
-    send[...] = value[: count * half].astype(BF)
-    keep[...] = value[count * half :]
-
-
-def weight_again_kernel(base, meta, late_01, rest_01, late_23, rest_23, act_late, act_rest, send, keep):
-    rows = late_01.shape[0] // 2
-    for i, (late, rest) in enumerate(((late_01, rest_01), (late_23, rest_23))):
-        value = product(late, rest, act_late, act_rest, base)
-        send[i * rows : (i + 1) * rows, :] = value[:rows].astype(BF)
-        keep[i * rows : (i + 1) * rows, :] = value[rows:]
+    again_kernel(base, meta, lhs_late, lhs_rest, act_late, act_rest, send, keep)
+
+
+def again_kernel(base, meta, lhs_late, lhs_rest, act_late, act_rest, send, keep):
+    rows = send.shape[0]
+    for out, at in ((send, 0), (keep, rows)):
+        for i in range(0, rows, rows // 2):
+            part = slice(at + i, at + i + rows // 2)
+            columns = slice(base, base + act_rest.shape[1])
+            value = jnp.dot(lhs_late[part, :], act_late[:, columns], preferred_element_type=F32)
+            value += jnp.dot(lhs_rest[part, :], act_rest[...], preferred_element_type=F32)
+            out[i : i + rows // 2, :] = value.astype(out.dtype)
 
 
 def near_kernel(count, meta, *refs):
@@ -270,10 +265,9 @@
     lax.fori_loop(0, half // step, body, 0)
 
 
-def place_kernel(meta, kept, early, *rest):
-    inner, outer, out = rest[:2], rest[2:4], rest[4]
-    d = dp_at(meta)
-    count = kept_total(meta, d)
+def place_kernel(cuts, meta, kept, early, *rest):
+    lates, out = rest[:-1], rest[-1]
+    count = kept_total(meta, dp_at(meta))
     first = jnp.minimum(count - lax.rem(count, TILE), BAL - SEND)
     first = pl.multiple_of(first, TILE)
     wide = out.shape[1]
@@ -288,24 +282,17 @@
         out[window, :] = jnp.where(rows < count, out[window, :], block)
 
     put(early[:, columns], first)
-    is_inner = (d // 2 == 1) | (d // 2 == 2)
-    half = inner[0].shape[1] // wide
-    for i in range(2):
-
-        @pl.when(step // half == i)
+    sources = [(late, c) for late, cut in zip(lates, cuts) for c in range(0, cut, wide)]
+    for i, (late, c) in enumerate(sources):
+
+        @pl.when(step == i)
         def _():
-            at = pl.ds(pl.multiple_of((step - i * half) * wide, wide), wide)
-            block = jnp.where(is_inner, inner[i][:, at], outer[i][:, at])
-            put(block, pl.multiple_of(first + EARLY, TILE))
+            put(late[:, c : c + wide], pl.multiple_of(first + EARLY, TILE))
 
 
 def swapped(block, axis, distance):
     n = lax.axis_size(axis)
     return lax.ppermute(block, axis, [(i, i ^ distance) for i in range(n)])
-
-
-def routed(block, pairs):
-    return lax.ppermute(block, "dp", [(2 * a + x, 2 * b + x) for a, b in pairs for x in range(2)])
 
 
 def after(value, *others):
@@ -341,22 +328,22 @@
              sems((columns // block,))],
         )(meta, hidden_pre)
 
-    def weight_part(meta, pieces, act):
-        count = len(pieces)
+    def weight_first(meta, act):
+        count = len(lates)
         return kernel_call(
             functools.partial(weight_kernel, count, 0),
             [shape(count * half, part), shape(count * half, part, F32),
              shape(count * width, LATE), shape(count * width, others)],
-            [IN_VMEM] * (count + 2), [IN_VMEM] * 4,
-        )(meta, *pieces, act_late, act)
+            [IN_VMEM] * (2 * count + 2), [IN_VMEM] * 4,
+        )(meta, *lates, *rests, act_late, act)
 
     def weight_again(meta, base, act):
         return kernel_call(
-            functools.partial(weight_again_kernel, base),
-            [shape(4 * half, part), shape(4 * half, part, F32)], [IN_VMEM] * 6, [IN_VMEM] * 2,
-        )(meta, *lhs_01, *lhs_23, act_late, act)
-
-    def grads(meta, first_row, first_slope, rows, slopes, cuts):
+            functools.partial(again_kernel, base),
+            [shape(4 * half, part), shape(4 * half, part, F32)], [IN_VMEM] * 4, [IN_VMEM] * 2,
+        )(meta, *lhs, act_late, act)
+
+    def grads(meta, pieces, first_row, first_slope, rows, slopes, cuts):
         return kernel_call(
             functools.partial(grad_kernel, first_row, first_slope, len(slopes), 256),
             [shape(rows, c) for c in cuts], [IN_VMEM] * (5 + len(slopes)), [IN_VMEM] * len(cuts),
@@ -375,79 +362,67 @@
             far_kernel, [shape(half, part), shape(half, part, F32)], [IN_VMEM] * 2, [IN_VMEM] * 2
         )(meta, mine, got)
 
-    own_rows, early = kernel_call(
-        first_kernel, [shape(SEND + KEEP, width), shape(EARLY, width + ff)], [IN_HBM] * 3, [IN_VMEM] * 2,
+    late, rest, early = kernel_call(
+        first_kernel, [shape(LATE, width), shape(others, width), shape(EARLY, width + ff)],
+        [IN_HBM] * 3, [IN_VMEM] * 3,
         [vmem((home, width), BF), vmem((features,), F32), vmem((home, ff), BF), sems((3,))],
     )(meta, cotangent, layer_scale, hidden_pre)
     arrived_early = swapped(early, "dp", n // 2)
 
-    rows_c, rows_y = swapped(own_rows, "tensor", 1), swapped(own_rows, "tensor", 2)
-    act_late, der_late = gelu(after(meta, own_rows), True, 0, ff)
-    act_a, der_a = gelu(after(meta, act_late), False, 0, part)
-
-    send_01, keep_01, *lhs_01 = weight_part(after(meta, act_a), (own_rows, rows_c), act_a)
-    got_01 = swapped(send_01, "dp", 1)
-    rows_y = after(rows_y, send_01, arrived_early)
-    rows_yc = swapped(rows_y, "tensor", 1)
-    pieces = (own_rows, rows_c, rows_y, rows_yc)
-
-    moving = grads(after(meta, rows_y), 0, 0, LATE, (der_late,), (ff // 2, ff // 2))
-    to_inner, across, to_outer = ((0, 1), (3, 2)), ((1, 2), (2, 1)), ((1, 0), (2, 3))
-    at_inner_a = routed(moving[0], to_inner)
-    crossed_a = routed(moving[0], across)
-    crossed_b = routed(moving[1], across)
-
-    early_sent = after(arrived_early[:, :width], *moving)
+    late_c, late_y = swapped(late, "tensor", 1), swapped(late, "tensor", 2)
+    rest_c, rest_y = swapped(rest, "tensor", 1), swapped(rest, "tensor", 2)
+    act_late, der_late = gelu(after(meta, late), True, 0, ff)
+    late_y = after(late_y, act_late, late_c, rest_c, arrived_early)
+    late_yc = swapped(late_y, "tensor", 1)
+    lates = (late, late_c, late_y, late_yc)
+
+    moves = (1024, ff - 1024)
+    moving = grads(after(meta, late_y), lates, 0, 0, LATE, (der_late,), moves)
+    arrived_a = swapped(moving[0], "dp", n // 2)
+    rest_y = after(rest_y, *moving)
+    rest_yc = swapped(rest_y, "tensor", 1)
+    rests = (rest, rest_c, rest_y, rest_yc)
+
+    act_a, der_a = gelu(after(meta, *moving), False, 0, part)
+    send_a, keep_a, *lhs = weight_first(after(meta, act_a), act_a)
+    got_a = swapped(send_a, "dp", 1)
+    early_sent = after(arrived_early[:, :width], send_a)
     early_c, early_y = swapped(early_sent, "tensor", 1), swapped(early_sent, "tensor", 2)
-
-    send_23, keep_23, *lhs_23 = weight_part(
-        after(meta, got_01, early_y, early_c, *moving), (rows_y, rows_yc), act_a
-    )
-    got_23 = swapped(send_23, "dp", 1)
-    early_y = after(early_y, send_23)
+    act_b, der_b = gelu(after(meta, send_a), False, part, part)
+    send_b, keep_b = weight_again(after(meta, act_b, early_c, early_y), part, act_b)
+    got_b = swapped(send_b, "dp", 1)
+    early_y = after(early_y, send_b)
     early_yc = swapped(early_y, "tensor", 1)
-    act_b, der_b = gelu(after(meta, send_23), False, part, part)
-    send_b, keep_b = weight_again(after(meta, act_b, early_yc), part, act_b)
-    got_b = swapped(send_b, "dp", 1)
-
-    is_inner = (d // 2 == 1) | (d // 2 == 2)
-    hop = after(jnp.where(is_inner, crossed_a, moving[1]), send_b, got_23, at_inner_a)
-    hopped = routed(hop, to_inner + to_outer)
-    inner_a = routed(after(at_inner_a, hop), across)
-    act_c, der_c = gelu(after(meta, hop), False, 2 * part, part)
-    send_c, keep_c = weight_again(after(meta, act_c), 2 * part, act_c)
+    act_c, der_c = gelu(after(meta, send_b), False, 2 * part, part)
+    send_c, keep_c = weight_again(after(meta, act_c, early_yc), 2 * part, act_c)
     got_c = swapped(send_c, "dp", 1)
 
-    out_na, mine_a = near_step(
-        after(meta, send_c, hopped, crossed_b), (keep_01, keep_23), (got_01, got_23)
-    )
-    got_na = swapped(out_na, "dp", 2)
-    inner_b = routed(after(hopped, out_na), across)
-    (kept_grad,) = grads(after(meta, out_na), SEND, EARLY, KEEP, (der_a, der_b, der_c), (ff,))
-    out_nb, mine_b = near_step(after(meta, kept_grad, inner_a), (keep_b,), (got_b,))
-    got_nb = swapped(out_nb, "dp", 2)
-    outer_b = routed(after(crossed_b, out_nb), to_outer)
-
+    (kept_grad,) = grads(after(meta, send_c), rests, EARLY, EARLY, KEEP, (der_a, der_b, der_c), (ff,))
     early_grad = kernel_call(
         functools.partial(early_kernel, 256), shape(EARLY, ff), [IN_VMEM] * 5, IN_VMEM,
         [vmem((EARLY, features), BF), vmem((EARLY, 256), F32)],
-    )(after(meta, out_nb), arrived_early, early_c, early_y, early_yc, down_weight)
-
-    out_fa, own_a = far_step(after(meta, early_grad), mine_a, got_na)
+    )(after(meta, kept_grad), arrived_early, early_c, early_y, early_yc, down_weight)
+
+    out_na, mine_a = near_step(after(meta, early_grad, arrived_a), (keep_a,), (got_a,))
+    got_na = swapped(out_na, "dp", 2)
+    out_nb, mine_b = near_step(after(meta, out_na), (keep_b,), (got_b,))
+    got_nb = swapped(out_nb, "dp", 2)
+    arrived_b = swapped(after(moving[1], out_nb), "dp", n // 2)
+    out_fa, own_a = far_step(after(meta, out_nb), mine_a, got_na)
     got_fa = swapped(out_fa, "dp", 4)
-    out_nc, mine_c = near_step(after(meta, out_fa, inner_b), (keep_c,), (got_c,))
+    out_nc, mine_c = near_step(after(meta, out_fa), (keep_c,), (got_c,))
     got_nc = swapped(out_nc, "dp", 2)
     out_fb, own_b = far_step(after(meta, out_nc), mine_b, got_nb)
     got_fb = swapped(out_fb, "dp", 4)
-    out_fc, own_c = far_step(after(meta, out_fb, outer_b, got_fa), mine_c, got_nc)
+    out_fc, own_c = far_step(after(meta, out_fb, arrived_b, got_fa), mine_c, got_nc)
     got_fc = swapped(out_fc, "dp", 4)
     total = [a + b.astype(F32) for a, b in ((own_a, got_fa), (own_b, got_fb), (own_c, got_fc))]
     down_grad = jnp.concatenate(total, axis=1) / math.sqrt(n * home)
 
     hidden_grad = kernel_call(
-        place_kernel, shape(BAL, ff), [IN_VMEM] * 6,
+        functools.partial(place_kernel, moves), shape(BAL, ff), [IN_VMEM] * (2 + len(moves)),
         pl.BlockSpec((BAL, 256), lambda i, *_: (0, i)), grid=(ff // 256,),
-    )(after(meta, out_fc), kept_grad, early_grad, inner_a, inner_b, hopped, outer_b)
+    )(after(meta, out_fc), kept_grad, early_grad, arrived_a, arrived_b)
     return (hidden_grad, down_grad)
 
 

time: 153 us -> 135 us (0.88)
  starting transfers between devices: 39.6 us -> 24.8 us
  waiting for transfers between devices: 49.4 us -> 54.3 us
  local copies, waits for them, and re-layouts: 4.79 us -> 0.01 us
  Pallas kernels: 55.6 us -> 52.8 us
    ppermute x7 -> x0, starting transfers between devices: 17.7 us -> none  [routed(): lax.ppermute(block, 'dp', [(2 * a + x, 2 * b + x) for a, b in pairs for x...]
    ppermute x17 -> x21, waiting for transfers between devices: 44.1 us -> 54.3 us  [swapped(): return lax.ppermute(block, axis, [(i, i ^ distance) for i in range(n)])]
    ppermute x7 -> x0, waiting for transfers between devices: 5.31 us -> none  [routed(): lax.ppermute(block, 'dp', [(2 * a + x, 2 * b + x) for a, b in pairs for x...]
    unnamed x52 -> x2, local copies, waits for them, and re-layouts: 4.78 us -> 0.01 us
    ppermute x17 -> x21, starting transfers between devices: 22 us -> 24.8 us  [swapped(): return lax.ppermute(block, axis, [(i, i ^ distance) for i in range(n)])]
    pallas_call x6 -> x5, Pallas kernels: 18.2 us -> 16.6 us  [the longest x2 5.7 us: weight_again(): kernel_call(functools.partial(again_kernel, base), [shape(4 * half, part)...]
  transfers between devices with their start and end apart: 24 -> 21, of which waited for: 11 -> 7; matrix products, arithmetic and copies ran while one was open for 0% -> 0% of each run, Pallas kernels for 31% -> 36%
where the time goes in v9:
time: 135 us
  waiting for transfers between devices  54.3 us (40%)
  Pallas kernels  52.8 us (39%)
  starting transfers between devices  24.8 us (18%)
  other arithmetic  2 us (1%)
    ppermute x21, waiting for transfers between devices, swapped(): return lax.ppermute(block, axis, [(i, i ^ distance) for i in range(n)])  54.3 us
    ppermute x21, starting transfers between devices, swapped(): return lax.ppermute(block, axis, [(i, i ^ distance) for i in range(n)])  24.8 us
    pallas_call x4, Pallas kernels, gelu(): kernel_call(functools.partial(gelu_kernel, late, base, block), [shape(row...  21.4 us
    pallas_call x2, Pallas kernels, grads(): kernel_call(functools.partial(grad_kernel, first_row, first_slope, len(sl...  6.68 us
    pallas_call x2, Pallas kernels, weight_again(): kernel_call(functools.partial(again_kernel, base), [shape(4 * half, part)...  5.7 us
    pallas_call x1, Pallas kernels, shards(): kernel_call(first_kernel, [shape(LATE, width), shape(others, width), shap...  4.62 us
    pallas_call x1, Pallas kernels, shards(): kernel_call(functools.partial(place_kernel, moves), shape(BAL, ff), [IN_V...  3.3 us
    pallas_call x1, Pallas kernels, weight_first(): kernel_call(functools.partial(weight_kernel, count, 0), [shape(count * ha...  2.93 us
  transfers between devices with their start and end apart: 21, of which 7 were waited for; matrix products, arithmetic and copies ran while one was open for 0% of the time, Pallas kernels for 36%

profile of v9, /device:TPU:0, one launch (start us, length us, event | category | flops | bytes accessed | tf_op | source)
XLA Modules:
  0.0 134.7 jit_solution(16281158047534049801)
XLA Ops:
  1.4 4.6 %shard_map.77 = (bf16[480,384]{1,0:T(8,128)(2,1)S(1)}, bf16[576,384]{1,0:T(8,128)(2,1)S(1)}, bf16[48,1920]{1,0:T(8,128)(2,1)S(1)}) custom-call(s32[9,8]{1,0:T(8,128)S(1)} %pad_add_fusion.meta, bf16[1032,384]{1,0:T(8,128)(2,1)} %cot_hbm.1, f32[1536]{0:T(1024)} %scale_hbm.1, bf16[1032,1536]{1,0:T(8,128)(2,1)} %pre_hbm.9), custom_call_target="tpu_custom_call" | custom-call | flops 1 | bytes 1 | tf_op jit(solution)/shard_map/pallas_call | solution.py:365
  6.6 2.9 %collective-permute-start = (bf16[480,384]{1,0:T(8,128)(2,1)S(1)}, bf16[480,384]{1,0:T(8,128)(2,1)S(1)}, u32[]{:S(2)}, u32[]{:S(2)}) collective-permute-start(bf16[480,384]{1,0:T(8,128)(2,1)S(1)} %get-tuple-element.57.p0.refs_0_), channel_id=1, source_target_pairs={{0,2},{1,3},{2,0},{3,1},{4,6},{5,7},{6,4},{7,5},{8,10},{9,11},{10,... | collective-permute-start | bytes 1105928 | tf_op jit(solution)/shard_map/ppermute | solution.py:295
  9.5 2.6 %collective-permute-start.3 = (bf16[48,1920]{1,0:T(8,128)(2,1)S(1)}, bf16[48,1920]{1,0:T(8,128)(2,1)S(1)}, u32[]{:S(2)}, u32[]{:S(2)}) collective-permute-start(bf16[48,1920]{1,0:T(8,128)(2,1)S(1)} %get-tuple-element.61), channel_id=1, source_target_pairs={{0,16},{4,20},{8,24},{12,28},{16,0},{20,4},{24,8},{28,12},{1,17},{... | collective-permute-start | bytes 552968 | tf_op jit(solution)/shard_map/ppermute | solution.py:295
  12.6 8.4 %shard_map.78 = (bf16[480,1536]{1,0:T(8,128)(2,1)S(1)}, f32[480,1536]{1,0:T(8,128)S(1)}) custom-call(s32[9,8]{1,0:T(8,128)S(1)} %pad_add_fusion.meta, bf16[1032,1536]{1,0:T(8,128)(2,1)} %pre_hbm.9), custom_call_target="tpu_custom_call" | custom-call | flops 1 | bytes 1 | tf_op jit(solution)/shard_map/pallas_call | solution.py:323
  21.2 1.7 %collective-permute-done.4.p3.refs_3_ = bf16[480,384]{1,0:T(8,128)(2,1)S(1)} collective-permute-done((bf16[480,384]{1,0:T(8,128)(2,1)S(1)}, bf16[480,384]{1,0:T(8,128)(2,1)S(1)}, u32[]{:S(2)}, u32[]{:S(2)}) %collective-permute-start.4) | collective-permute-done | bytes 368672 | tf_op jit(solution)/shard_map/ppermute | solution.py:295
  22.9 3.2 %shard_map.79 = (bf16[480,1024]{1,0:T(8,128)(2,1)S(1)}, bf16[480,512]{1,0:T(8,128)(2,1)S(1)}) custom-call(s32[9,8]{1,0:T(8,128)S(1)} %pad_add_fusion.meta, bf16[480,384]{1,0:T(8,128)(2,1)S(1)} %get-tuple-element.57.p0.refs_0_, bf16[480,384]{1,0:T(8,128)(2,1)S(1)} %collective-permute-done.1.p1.refs_1_, bf16[480,384]{1,0:T(8,128)(2,1)S(1)} %collective-permute-done.p2.refs_2_, ...), custom_call_target="tpu_custom_call" | custom-call | flops 1 | bytes 1 | tf_op jit(solution)/shard_map/pallas_call | solution.py:347
  26.1 1.8 %collective-permute-done.5.refs_6_.p2 = bf16[576,384]{1,0:T(8,128)(2,1)S(1)} collective-permute-done((bf16[576,384]{1,0:T(8,128)(2,1)S(1)}, bf16[576,384]{1,0:T(8,128)(2,1)S(1)}, u32[]{:S(2)}, u32[]{:S(2)}) %collective-permute-start.5) | collective-permute-done | bytes 442400 | tf_op jit(solution)/shard_map/ppermute | solution.py:295
  27.8 2.8 %collective-permute-start.10 = (bf16[480,1024]{1,0:T(8,128)(2,1)S(1)}, bf16[480,1024]{1,0:T(8,128)(2,1)S(1)}, u32[]{:S(2)}, u32[]{:S(2)}) collective-permute-start(bf16[480,1024]{1,0:T(8,128)(2,1)S(1)} %get-tuple-element.65), channel_id=1, source_target_pairs={{0,16},{4,20},{8,24},{12,28},{16,0},{20,4},{24,8},{28,12},{1,17},{... | collective-permute-start | bytes 2949128 | tf_op jit(solution)/shard_map/ppermute | solution.py:295
  30.7 4.3 %shard_map.80 = (bf16[576,512]{1,0:T(8,128)(2,1)S(1)}, f32[576,512]{1,0:T(8,128)S(1)}) custom-call(s32[9,8]{1,0:T(8,128)S(1)} %pad_add_fusion.meta, bf16[1032,1536]{1,0:T(8,128)(2,1)} %pre_hbm.9), custom_call_target="tpu_custom_call" | custom-call | flops 1 | bytes 1 | tf_op jit(solution)/shard_map/pallas_call | solution.py:323
  34.9 2.9 %shard_map.81 = (bf16[768,512]{1,0:T(8,128)(2,1)S(1)}, f32[768,512]{1,0:T(8,128)S(1)}, bf16[1536,480]{1,0:T(8,128)(2,1)S(1)}, bf16[1536,576]{1,0:T(8,128)(2,1)S(1)}) custom-call(s32[9,8]{1,0:T(8,128)S(1)} %pad_add_fusion.meta, bf16[480,384]{1,0:T(8,128)(2,1)S(1)} %get-tuple-element.57.p0.refs_0_, bf16[480,384]{1,0:T(8,128)(2,1)S(1)} %collective-permute-done.1.p1.refs_1_, ...), custom_call_target="tpu_custom_call" | custom-call | flops 1 | bytes 1 | tf_op jit(solution)/shard_map/pallas_call | solution.py:333
  41.0 4.3 %shard_map.82 = (bf16[576,512]{1,0:T(8,128)(2,1)S(1)}, f32[576,512]{1,0:T(8,128)S(1)}) custom-call(s32[9,8]{1,0:T(8,128)S(1)} %pad_add_fusion.meta, bf16[1032,1536]{1,0:T(8,128)(2,1)} %pre_hbm.9), custom_call_target="tpu_custom_call" | custom-call | flops 1 | bytes 1 | tf_op jit(solution)/shard_map/pallas_call | solution.py:323
  45.3 2.9 %shard_map.83 = (bf16[768,512]{1,0:T(8,128)(2,1)S(1)}, f32[768,512]{1,0:T(8,128)S(1)}) custom-call(s32[9,8]{1,0:T(8,128)S(1)} %pad_add_fusion.meta, bf16[1536,480]{1,0:T(8,128)(2,1)S(1)} %get-tuple-element.76.lhs_late, bf16[1536,576]{1,0:T(8,128)(2,1)S(1)} %get-tuple-element.77.lhs_rest, bf16[480,1536]{1,0:T(8,128)(2,1)S(1)} %get-tuple-element.59.refs_8_.act_late, ...), custom_call_target="tpu_custom_call" | custom-call | flops 1 | bytes 1 | tf_op jit(solution)/shard_map/pallas_call | solution.py:341
  48.9 4.5 %shard_map.84 = (bf16[576,512]{1,0:T(8,128)(2,1)S(1)}, f32[576,512]{1,0:T(8,128)S(1)}) custom-call(s32[9,8]{1,0:T(8,128)S(1)} %pad_add_fusion.meta, bf16[1032,1536]{1,0:T(8,128)(2,1)} %pre_hbm.9), custom_call_target="tpu_custom_call" | custom-call | flops 1 | bytes 1 | tf_op jit(solution)/shard_map/pallas_call | solution.py:323
  53.4 2.9 %shard_map.85 = (bf16[768,512]{1,0:T(8,128)(2,1)S(1)}, f32[768,512]{1,0:T(8,128)S(1)}) custom-call(s32[9,8]{1,0:T(8,128)S(1)} %pad_add_fusion.meta, bf16[1536,480]{1,0:T(8,128)(2,1)S(1)} %get-tuple-element.76.lhs_late, bf16[1536,576]{1,0:T(8,128)(2,1)S(1)} %get-tuple-element.77.lhs_rest, bf16[480,1536]{1,0:T(8,128)(2,1)S(1)} %get-tuple-element.59.refs_8_.act_late, ...), custom_call_target="tpu_custom_call" | custom-call | flops 1 | bytes 1 | tf_op jit(solution)/shard_map/pallas_call | solution.py:341
  57.9 3.5 %shard_map.86.kept = bf16[528,1536]{1,0:T(8,128)(2,1)S(1)} custom-call(s32[9,8]{1,0:T(8,128)S(1)} %pad_add_fusion.meta, bf16[576,384]{1,0:T(8,128)(2,1)S(1)} %get-tuple-element.60.refs_4_.p0, bf16[576,384]{1,0:T(8,128)(2,1)S(1)} %collective-permute-done.2.refs_5_.p1, bf16[576,384]{1,0:T(8,128)(2,1)S(1)} %collective-permute-done.5.refs_6_.p2, ...), custom_call_target="tpu_custom_call" | custom-call | flops 1 | bytes 1 | tf_op jit(solution)/shard_map/pallas_call | solution.py:347
  61.3 2.9 %shard_map.87.early = bf16[48,1536]{1,0:T(8,128)(2,1)S(1)} custom-call(s32[9,8]{1,0:T(8,128)S(1)} %pad_add_fusion.meta, bf16[48,1920]{1,0:T(8,128)(2,1)S(1)} %collective-permute-done.3.own, bf16[48,384]{1,0:T(8,128)(2,1)S(1)} %collective-permute-done.7.p1, bf16[48,384]{1,0:T(8,128)(2,1)S(1)} %collective-permute-done.8.p2, ...), custom_call_target="tpu_custom_call" | custom-call | flops 1 | bytes 1 | tf_op jit(solution)/shard_map/pallas_call | solution.py:401
  64.2 9.9 %collective-permute-done.10.rest_0_ = bf16[480,1024]{1,0:T(8,128)(2,1)S(1)} collective-permute-done((bf16[480,1024]{1,0:T(8,128)(2,1)S(1)}, bf16[480,1024]{1,0:T(8,128)(2,1)S(1)}, u32[]{:S(2)}, u32[]{:S(2)}) %collective-permute-start.10) | collective-permute-done | bytes 983072 | tf_op jit(solution)/shard_map/ppermute | solution.py:295
  76.8 3.4 %collective-permute-start.16 = (bf16[480,512]{1,0:T(8,128)(2,1)S(1)}, bf16[480,512]{1,0:T(8,128)(2,1)S(1)}, u32[]{:S(2)}, u32[]{:S(2)}) collective-permute-start(bf16[480,512]{1,0:T(8,128)(2,1)S(1)} %get-tuple-element.104), channel_id=1, source_target_pairs={{0,16},{4,20},{8,24},{12,28},{16,0},{20,4},{24,8},{28,12},{1,17},{... | collective-permute-start | bytes 1474568 | tf_op jit(solution)/shard_map/ppermute | solution.py:295
  80.3 14.1 %collective-permute-done.13.got = bf16[384,512]{1,0:T(8,128)(2,1)S(1)} collective-permute-done((bf16[384,512]{1,0:T(8,128)(2,1)S(1)}, bf16[384,512]{1,0:T(8,128)(2,1)S(1)}, u32[]{:S(2)}, u32[]{:S(2)}) %collective-permute-start.13) | collective-permute-done | bytes 393248 | tf_op jit(solution)/shard_map/ppermute | solution.py:295
  96.2 2.5 %collective-permute-start.18 = (bf16[384,512]{1,0:T(8,128)(2,1)S(1)}, bf16[384,512]{1,0:T(8,128)(2,1)S(1)}, u32[]{:S(2)}, u32[]{:S(2)}) collective-permute-start(bf16[384,512]{1,0:T(8,128)(2,1)S(1)} %get-tuple-element.100), channel_id=1, source_target_pairs={{0,8},{4,12},{8,0},{12,4},{16,24},{20,28},{24,16},{28,20},{1,9},{5... | collective-permute-start | bytes 1179656 | tf_op jit(solution)/shard_map/ppermute | solution.py:295
  98.7 11.7 %collective-permute-done.15.got = bf16[384,512]{1,0:T(8,128)(2,1)S(1)} collective-permute-done((bf16[384,512]{1,0:T(8,128)(2,1)S(1)}, bf16[384,512]{1,0:T(8,128)(2,1)S(1)}, u32[]{:S(2)}, u32[]{:S(2)}) %collective-permute-start.15) | collective-permute-done | bytes 393248 | tf_op jit(solution)/shard_map/ppermute | solution.py:295
  112.9 8.9 %collective-permute-done.18.got = bf16[384,512]{1,0:T(8,128)(2,1)S(1)} collective-permute-done((bf16[384,512]{1,0:T(8,128)(2,1)S(1)}, bf16[384,512]{1,0:T(8,128)(2,1)S(1)}, u32[]{:S(2)}, u32[]{:S(2)}) %collective-permute-start.18) | collective-permute-done | bytes 393248 | tf_op jit(solution)/shard_map/ppermute | solution.py:295
  124.0 3.3 %shard_map.94 = bf16[720,1536]{1,0:T(8,128)(2,1)} custom-call(s32[9,8]{1,0:T(8,128)S(1)} %pad_add_fusion.meta, bf16[528,1536]{1,0:T(8,128)(2,1)S(1)} %shard_map.86.kept, bf16[48,1536]{1,0:T(8,128)(2,1)S(1)} %shard_map.87.early, bf16[480,1024]{1,0:T(8,128)(2,1)S(1)} %collective-permute-done.10.rest_0_, bf16[480,512]{1,0:T(8,128)(2,1)S(1)} %collective-permute-done.16.rest_1_), custom_call_target="tpu_custom_call" | custom-call | flops 1 | bytes 1 | tf_op jit(solution)/shard_map/pallas_call | solution.py:422
  127.3 6.2 %collective-permute-done.20 = bf16[192,512]{1,0:T(8,128)(2,1)S(1)} collective-permute-done((bf16[192,512]{1,0:T(8,128)(2,1)S(1)}, bf16[192,512]{1,0:T(8,128)(2,1)S(1)}, u32[]{:S(2)}, u32[]{:S(2)}) %collective-permute-start.20) | collective-permute-done | bytes 196640 | tf_op jit(solution)/shard_map/ppermute | solution.py:295
  (45 shorter events, 17.8 us)
Async XLA Ops:
  1.4 21.5 %copy-start = (bf16[1536,1536]{1,0:T(8,128)(2,1)S(1)}, bf16[1536,1536]{1,0:T(8,128)(2,1)}, u32[]{:S(2)}) copy-start(bf16[1536,1536]{1,0:T(8,128)(2,1)} %weight.5) | copy-start | bytes 14155780
  6.0 15.1 %collective-permute-start.2 = (bf16[576,384]{1,0:T(8,128)(2,1)S(1)}, bf16[576,384]{1,0:T(8,128)(2,1)S(1)}, u32[]{:S(2)}, u32[]{:S(2)}) collective-permute-start(bf16[576,384]{1,0:T(8,128)(2,1)S(1)} %get-tuple-element.60.refs_4_.p0), channel_id=1, source_target_pairs={{0,1},{1,0},{2,3},{3,2},{4,5},{5,4},{6,7},{7,6},{8,9},{9,8},{10,11... | collective-permute-start | bytes 1327112 | tf_op jit(solution)/shard_map/ppermute | solution.py:295
  6.5 14.6 %collective-permute-start.1 = (bf16[480,384]{1,0:T(8,128)(2,1)S(1)}, bf16[480,384]{1,0:T(8,128)(2,1)S(1)}, u32[]{:S(2)}, u32[]{:S(2)}) collective-permute-start(bf16[480,384]{1,0:T(8,128)(2,1)S(1)} %get-tuple-element.57.p0.refs_0_), channel_id=1, source_target_pairs={{0,1},{1,0},{2,3},{3,2},{4,5},{5,4},{6,7},{7,6},{8,9},{9,8},{10,11... | collective-permute-start | bytes 1105928 | tf_op jit(solution)/shard_map/ppermute | solution.py:295
  6.6 14.5 %collective-permute-start = (bf16[480,384]{1,0:T(8,128)(2,1)S(1)}, bf16[480,384]{1,0:T(8,128)(2,1)S(1)}, u32[]{:S(2)}, u32[]{:S(2)}) collective-permute-start(bf16[480,384]{1,0:T(8,128)(2,1)S(1)} %get-tuple-element.57.p0.refs_0_), channel_id=1, source_target_pairs={{0,2},{1,3},{2,0},{3,1},{4,6},{5,7},{6,4},{7,5},{8,10},{9,11},{10,... | collective-permute-start | bytes 1105928 | tf_op jit(solution)/shard_map/ppermute | solution.py:295
  9.5 11.5 %collective-permute-start.3 = (bf16[48,1920]{1,0:T(8,128)(2,1)S(1)}, bf16[48,1920]{1,0:T(8,128)(2,1)S(1)}, u32[]{:S(2)}, u32[]{:S(2)}) collective-permute-start(bf16[48,1920]{1,0:T(8,128)(2,1)S(1)} %get-tuple-element.61), channel_id=1, source_target_pairs={{0,16},{4,20},{8,24},{12,28},{16,0},{20,4},{24,8},{28,12},{1,17},{... | collective-permute-start | bytes 552968 | tf_op jit(solution)/shard_map/ppermute | solution.py:295
  12.1 15.7 %collective-permute-start.5 = (bf16[576,384]{1,0:T(8,128)(2,1)S(1)}, bf16[576,384]{1,0:T(8,128)(2,1)S(1)}, u32[]{:S(2)}, u32[]{:S(2)}) collective-permute-start(bf16[576,384]{1,0:T(8,128)(2,1)S(1)} %get-tuple-element.60.refs_4_.p0), channel_id=1, source_target_pairs={{0,2},{1,3},{2,0},{3,1},{4,6},{5,7},{6,4},{7,5},{8,10},{9,11},{10,... | collective-permute-start | bytes 1327112 | tf_op jit(solution)/shard_map/ppermute | solution.py:295
  21.1 1.8 %collective-permute-start.4 = (bf16[480,384]{1,0:T(8,128)(2,1)S(1)}, bf16[480,384]{1,0:T(8,128)(2,1)S(1)}, u32[]{:S(2)}, u32[]{:S(2)}) collective-permute-start(bf16[480,384]{1,0:T(8,128)(2,1)S(1)} %collective-permute-done.p2.refs_2_), channel_id=1, source_target_pairs={{0,1},{1,0},{2,3},{3,2},{4,5},{5,4},{6,7},{7,6},{8,9},{9,8},{10,11... | collective-permute-start | bytes 1105928 | tf_op jit(solution)/shard_map/ppermute | solution.py:295
  27.8 7.1 %collective-permute-start.6 = (bf16[576,384]{1,0:T(8,128)(2,1)S(1)}, bf16[576,384]{1,0:T(8,128)(2,1)S(1)}, u32[]{:S(2)}, u32[]{:S(2)}) collective-permute-start(bf16[576,384]{1,0:T(8,128)(2,1)S(1)} %collective-permute-done.5.refs_6_.p2), channel_id=1, source_target_pairs={{0,1},{1,0},{2,3},{3,2},{4,5},{5,4},{6,7},{7,6},{8,9},{9,8},{10,11... | collective-permute-start | bytes 1327112 | tf_op jit(solution)/shard_map/ppermute | solution.py:295
  27.8 46.3 %collective-permute-start.10 = (bf16[480,1024]{1,0:T(8,128)(2,1)S(1)}, bf16[480,1024]{1,0:T(8,128)(2,1)S(1)}, u32[]{:S(2)}, u32[]{:S(2)}) collective-permute-start(bf16[480,1024]{1,0:T(8,128)(2,1)S(1)} %get-tuple-element.65), channel_id=1, source_target_pairs={{0,16},{4,20},{8,24},{12,28},{16,0},{20,4},{24,8},{28,12},{1,17},{... | collective-permute-start | bytes 2949128 | tf_op jit(solution)/shard_map/ppermute | solution.py:295
  37.9 36.3 %collective-permute-start.11 = (bf16[768,512]{1,0:T(8,128)(2,1)S(1)}, bf16[768,512]{1,0:T(8,128)(2,1)S(1)}, u32[]{:S(2)}, u32[]{:S(2)}) collective-permute-start(bf16[768,512]{1,0:T(8,128)(2,1)S(1)} %get-tuple-element.71), channel_id=1, source_target_pairs={{0,4},{4,0},{8,12},{12,8},{16,20},{20,16},{24,28},{28,24},{1,5},{5... | collective-permute-start | bytes 2359304 | tf_op jit(solution)/shard_map/ppermute | solution.py:295
  39.4 5.8 %collective-permute-start.8 = (bf16[48,384]{1,0:T(8,128)(2,1)S(1)}, bf16[48,384]{1,0:T(8,128)(2,1)S(1)}, u32[]{:S(2)}, u32[]{:S(2)}) collective-permute-start(bf16[48,384]{1,0:T(8,128)(2,1)S(1)} %slice.4), channel_id=1, source_target_pairs={{0,2},{1,3},{2,0},{3,1},{4,6},{5,7},{6,4},{7,5},{8,10},{9,11},{10,... | collective-permute-start | bytes 110600 | tf_op jit(solution)/shard_map/ppermute | solution.py:295
  41.0 4.3 %collective-permute-start.7 = (bf16[48,384]{1,0:T(8,128)(2,1)S(1)}, bf16[48,384]{1,0:T(8,128)(2,1)S(1)}, u32[]{:S(2)}, u32[]{:S(2)}) collective-permute-start(bf16[48,384]{1,0:T(8,128)(2,1)S(1)} %slice.4), channel_id=1, source_target_pairs={{0,1},{1,0},{2,3},{3,2},{4,5},{5,4},{6,7},{7,6},{8,9},{9,8},{10,11... | collective-permute-start | bytes 110600 | tf_op jit(solution)/shard_map/ppermute | solution.py:295
  48.1 27.8 %collective-permute-start.12 = (bf16[768,512]{1,0:T(8,128)(2,1)S(1)}, bf16[768,512]{1,0:T(8,128)(2,1)S(1)}, u32[]{:S(2)}, u32[]{:S(2)}) collective-permute-start(bf16[768,512]{1,0:T(8,128)(2,1)S(1)} %get-tuple-element.78), channel_id=1, source_target_pairs={{0,4},{4,0},{8,12},{12,8},{16,20},{20,16},{24,28},{28,24},{1,5},{5... | collective-permute-start | bytes 2359304 | tf_op jit(solution)/shard_map/ppermute | solution.py:295
  48.7 4.7 %collective-permute-start.9 = (bf16[48,384]{1,0:T(8,128)(2,1)S(1)}, bf16[48,384]{1,0:T(8,128)(2,1)S(1)}, u32[]{:S(2)}, u32[]{:S(2)}) collective-permute-start(bf16[48,384]{1,0:T(8,128)(2,1)S(1)} %collective-permute-done.8.p2), channel_id=1, source_target_pairs={{0,1},{1,0},{2,3},{3,2},{4,5},{5,4},{6,7},{7,6},{8,9},{9,8},{10,11... | collective-permute-start | bytes 110600 | tf_op jit(solution)/shard_map/ppermute | solution.py:295
  56.3 39.0 %collective-permute-start.14 = (bf16[768,512]{1,0:T(8,128)(2,1)S(1)}, bf16[768,512]{1,0:T(8,128)(2,1)S(1)}, u32[]{:S(2)}, u32[]{:S(2)}) collective-permute-start(bf16[768,512]{1,0:T(8,128)(2,1)S(1)} %get-tuple-element.83), channel_id=1, source_target_pairs={{0,4},{4,0},{8,12},{12,8},{16,20},{20,16},{24,28},{28,24},{1,5},{5... | collective-permute-start | bytes 2359304 | tf_op jit(solution)/shard_map/ppermute | solution.py:295
  75.1 19.3 %collective-permute-start.13 = (bf16[384,512]{1,0:T(8,128)(2,1)S(1)}, bf16[384,512]{1,0:T(8,128)(2,1)S(1)}, u32[]{:S(2)}, u32[]{:S(2)}) collective-permute-start(bf16[384,512]{1,0:T(8,128)(2,1)S(1)} %get-tuple-element.91), channel_id=1, source_target_pairs={{0,8},{4,12},{8,0},{12,4},{16,24},{20,28},{24,16},{28,20},{1,9},{5... | collective-permute-start | bytes 1179656 | tf_op jit(solution)/shard_map/ppermute | solution.py:295
  76.8 36.0 %collective-permute-start.16 = (bf16[480,512]{1,0:T(8,128)(2,1)S(1)}, bf16[480,512]{1,0:T(8,128)(2,1)S(1)}, u32[]{:S(2)}, u32[]{:S(2)}) collective-permute-start(bf16[480,512]{1,0:T(8,128)(2,1)S(1)} %get-tuple-element.104), channel_id=1, source_target_pairs={{0,16},{4,20},{8,24},{12,28},{16,0},{20,4},{24,8},{28,12},{1,17},{... | collective-permute-start | bytes 1474568 | tf_op jit(solution)/shard_map/ppermute | solution.py:295
  80.3 30.1 %collective-permute-start.15 = (bf16[384,512]{1,0:T(8,128)(2,1)S(1)}, bf16[384,512]{1,0:T(8,128)(2,1)S(1)}, u32[]{:S(2)}, u32[]{:S(2)}) collective-permute-start(bf16[384,512]{1,0:T(8,128)(2,1)S(1)} %get-tuple-element.94), channel_id=1, source_target_pairs={{0,8},{4,12},{8,0},{12,4},{16,24},{20,28},{24,16},{28,20},{1,9},{5... | collective-permute-start | bytes 1179656 | tf_op jit(solution)/shard_map/ppermute | solution.py:295
  95.2 17.6 %collective-permute-start.17 = (bf16[192,512]{1,0:T(8,128)(2,1)S(1)}, bf16[192,512]{1,0:T(8,128)(2,1)S(1)}, u32[]{:S(2)}, u32[]{:S(2)}) collective-permute-start(bf16[192,512]{1,0:T(8,128)(2,1)S(1)} %get-tuple-element.97), channel_id=1, source_target_pairs={{0,16},{4,20},{8,24},{12,28},{16,0},{20,4},{24,8},{28,12},{1,17},{... | collective-permute-start | bytes 589832 | tf_op jit(solution)/shard_map/ppermute | solution.py:295
  96.2 25.6 %collective-permute-start.18 = (bf16[384,512]{1,0:T(8,128)(2,1)S(1)}, bf16[384,512]{1,0:T(8,128)(2,1)S(1)}, u32[]{:S(2)}, u32[]{:S(2)}) collective-permute-start(bf16[384,512]{1,0:T(8,128)(2,1)S(1)} %get-tuple-element.100), channel_id=1, source_target_pairs={{0,8},{4,12},{8,0},{12,4},{16,24},{20,28},{24,16},{28,20},{1,9},{5... | collective-permute-start | bytes 1179656 | tf_op jit(solution)/shard_map/ppermute | solution.py:295
  111.1 12.8 %collective-permute-start.19 = (bf16[192,512]{1,0:T(8,128)(2,1)S(1)}, bf16[192,512]{1,0:T(8,128)(2,1)S(1)}, u32[]{:S(2)}, u32[]{:S(2)}) collective-permute-start(bf16[192,512]{1,0:T(8,128)(2,1)S(1)} %get-tuple-element.103), channel_id=1, source_target_pairs={{0,16},{4,20},{8,24},{12,28},{16,0},{20,4},{24,8},{28,12},{1,17},{... | collective-permute-start | bytes 589832 | tf_op jit(solution)/shard_map/ppermute | solution.py:295
  122.6 10.9 %collective-permute-start.20 = (bf16[192,512]{1,0:T(8,128)(2,1)S(1)}, bf16[192,512]{1,0:T(8,128)(2,1)S(1)}, u32[]{:S(2)}, u32[]{:S(2)}) collective-permute-start(bf16[192,512]{1,0:T(8,128)(2,1)S(1)} %get-tuple-element.107), channel_id=1, source_target_pairs={{0,16},{4,20},{8,24},{12,28},{16,0},{20,4},{24,8},{28,12},{1,17},{... | collective-permute-start | bytes 589832 | tf_op jit(solution)/shard_map/ppermute | solution.py:295

commit v10 on v9

--- a/solution.py
+++ b/solution.py
@@ -178,10 +178,11 @@
     at = 0
     for out in outs:
         for c in range(0, out.shape[1], block):
-            slope = slopes[at // part][first_slope : first_slope + rows, at % part : at % part + block]
-            value = jnp.dot(lhs[...], weight[:, at : at + block], preferred_element_type=F32)
-            out[:, c : c + block] = (value * slope).astype(BF)
-            at += block
+            wide = min(block, out.shape[1] - c)
+            slope = slopes[at // part][first_slope : first_slope + rows, at % part : at % part + wide]
+            value = jnp.dot(lhs[...], weight[:, at : at + wide], preferred_element_type=F32)
+            out[:, c : c + wide] = (value * slope).astype(BF)
+            at += wide
 
 
 def early_kernel(block, meta, own, p1, p2, p3, weight, out, lhs, acc):
@@ -202,7 +203,7 @@
 
 def weight_kernel(count, base, meta, *refs):
     lates, rests = refs[:count], refs[count : 2 * count]
-    act_late, act_rest, send, keep, lhs_late, lhs_rest = refs[2 * count :]
+    act_late, act_rest, *outs, lhs_late, lhs_rest = refs[2 * count :]
     half = lates[0].shape[1] // 2
     mine = dp_at(meta) % 2 == 0
     for i in range(count):
@@ -211,18 +212,24 @@
             lo, hi = both[:half], both[half:]
             lhs[i * half : (i + 1) * half, :] = jnp.where(mine, hi, lo)
             lhs[(count + i) * half : (count + i + 1) * half, :] = jnp.where(mine, lo, hi)
-    again_kernel(base, meta, lhs_late, lhs_rest, act_late, act_rest, send, keep)
-
-
-def again_kernel(base, meta, lhs_late, lhs_rest, act_late, act_rest, send, keep):
-    rows = send.shape[0]
-    for out, at in ((send, 0), (keep, rows)):
-        for i in range(0, rows, rows // 2):
-            part = slice(at + i, at + i + rows // 2)
-            columns = slice(base, base + act_rest.shape[1])
+    again_kernel(base, meta, lhs_late, lhs_rest, act_late, act_rest, *outs)
+
+
+def again_kernel(base, meta, lhs_late, lhs_rest, act_late, act_rest, *outs):
+    columns = slice(base, base + act_rest.shape[1])
+    step = lhs_late.shape[0] // 4
+    at = 0
+    for out in outs:
+        for i in range(0, out.shape[0], step):
+            part = slice(at, at + step)
             value = jnp.dot(lhs_late[part, :], act_late[:, columns], preferred_element_type=F32)
             value += jnp.dot(lhs_rest[part, :], act_rest[...], preferred_element_type=F32)
-            out[i : i + rows // 2, :] = value.astype(out.dtype)
+            out[i : i + step, :] = value.astype(out.dtype)
+            at += step
+
+
+def tick_kernel(meta, out):
+    out[...] = jnp.zeros(out.shape, out.dtype)
 
 
 def near_kernel(count, meta, *refs):
@@ -332,9 +339,9 @@
         count = len(lates)
         return kernel_call(
             functools.partial(weight_kernel, count, 0),
-            [shape(count * half, part), shape(count * half, part, F32),
-             shape(count * width, LATE), shape(count * width, others)],
-            [IN_VMEM] * (2 * count + 2), [IN_VMEM] * 4,
+            [shape(width, part)] * 2 + [shape(width, part, F32)] * 2
+            + [shape(count * width, LATE), shape(count * width, others)],
+            [IN_VMEM] * (2 * count + 2), [IN_VMEM] * 6,
         )(meta, *lates, *rests, act_late, act)
 
     def weight_again(meta, base, act):
@@ -350,6 +357,9 @@
             [vmem((rows, features), BF)],
         )(meta, *pieces, down_weight, *slopes)
 
+    def tick(meta):
+        return kernel_call(tick_kernel, shape(8, 128, F32), [], IN_VMEM)(meta)
+
     def near_step(meta, keeps, gots):
         count = len(keeps)
         return kernel_call(
@@ -376,7 +386,7 @@
     late_yc = swapped(late_y, "tensor", 1)
     lates = (late, late_c, late_y, late_yc)
 
-    moves = (1024, ff - 1024)
+    moves = (640, 512, ff - 1152)
     moving = grads(after(meta, late_y), lates, 0, 0, LATE, (der_late,), moves)
     arrived_a = swapped(moving[0], "dp", n // 2)
     rest_y = after(rest_y, *moving)
@@ -384,11 +394,12 @@
     rests = (rest, rest_c, rest_y, rest_yc)
 
     act_a, der_a = gelu(after(meta, *moving), False, 0, part)
-    send_a, keep_a, *lhs = weight_first(after(meta, act_a), act_a)
-    got_a = swapped(send_a, "dp", 1)
-    early_sent = after(arrived_early[:, :width], send_a)
+    *sends_a, keep_01, keep_23, lhs_late, lhs_rest = weight_first(after(meta, act_a), act_a)
+    lhs = (lhs_late, lhs_rest)
+    gots_a = [swapped(send, "dp", 1) for send in sends_a]
+    early_sent = after(arrived_early[:, :width], keep_01)
     early_c, early_y = swapped(early_sent, "tensor", 1), swapped(early_sent, "tensor", 2)
-    act_b, der_b = gelu(after(meta, send_a), False, part, part)
+    act_b, der_b = gelu(after(meta, keep_01), False, part, part)
     send_b, keep_b = weight_again(after(meta, act_b, early_c, early_y), part, act_b)
     got_b = swapped(send_b, "dp", 1)
     early_y = after(early_y, send_b)
@@ -397,32 +408,36 @@
     send_c, keep_c = weight_again(after(meta, act_c, early_yc), 2 * part, act_c)
     got_c = swapped(send_c, "dp", 1)
 
-    (kept_grad,) = grads(after(meta, send_c), rests, EARLY, EARLY, KEEP, (der_a, der_b, der_c), (ff,))
+    out_na, mine_a = near_step(after(meta, send_c, arrived_a), (keep_01, keep_23), gots_a)
+    got_na = swapped(out_na, "dp", 2)
+    tick_a = tick(after(meta, out_na))
+    arrived_b = swapped(after(moving[1], tick_a), "dp", n // 2)
+
+    (kept_grad,) = grads(after(meta, tick_a), rests, EARLY, EARLY, KEEP, (der_a, der_b, der_c), (ff,))
     early_grad = kernel_call(
         functools.partial(early_kernel, 256), shape(EARLY, ff), [IN_VMEM] * 5, IN_VMEM,
         [vmem((EARLY, features), BF), vmem((EARLY, 256), F32)],
     )(after(meta, kept_grad), arrived_early, early_c, early_y, early_yc, down_weight)
 
-    out_na, mine_a = near_step(after(meta, early_grad, arrived_a), (keep_a,), (got_a,))
-    got_na = swapped(out_na, "dp", 2)
-    out_nb, mine_b = near_step(after(meta, out_na), (keep_b,), (got_b,))
+    out_nb, mine_b = near_step(after(meta, early_grad, got_na), (keep_b,), (got_b,))
     got_nb = swapped(out_nb, "dp", 2)
-    arrived_b = swapped(after(moving[1], out_nb), "dp", n // 2)
-    out_fa, own_a = far_step(after(meta, out_nb), mine_a, got_na)
+    tick_b = tick(after(meta, out_nb))
+    arrived_c = swapped(after(moving[2], tick_b), "dp", n // 2)
+    out_fa, own_a = far_step(after(meta, tick_b), mine_a, got_na)
     got_fa = swapped(out_fa, "dp", 4)
-    out_nc, mine_c = near_step(after(meta, out_fa), (keep_c,), (got_c,))
+    out_nc, mine_c = near_step(after(meta, out_fa, arrived_b), (keep_c,), (got_c,))
     got_nc = swapped(out_nc, "dp", 2)
     out_fb, own_b = far_step(after(meta, out_nc), mine_b, got_nb)
     got_fb = swapped(out_fb, "dp", 4)
-    out_fc, own_c = far_step(after(meta, out_fb, arrived_b, got_fa), mine_c, got_nc)
+    out_fc, own_c = far_step(after(meta, out_fb, arrived_c, got_fa), mine_c, got_nc)
     got_fc = swapped(out_fc, "dp", 4)
     total = [a + b.astype(F32) for a, b in ((own_a, got_fa), (own_b, got_fb), (own_c, got_fc))]
     down_grad = jnp.concatenate(total, axis=1) / math.sqrt(n * home)
 
     hidden_grad = kernel_call(
         functools.partial(place_kernel, moves), shape(BAL, ff), [IN_VMEM] * (2 + len(moves)),
-        pl.BlockSpec((BAL, 256), lambda i, *_: (0, i)), grid=(ff // 256,),
-    )(after(meta, out_fc), kept_grad, early_grad, arrived_a, arrived_b)
+        pl.BlockSpec((BAL, 128), lambda i, *_: (0, i)), grid=(ff // 128,),
+    )(after(meta, out_fc), kept_grad, early_grad, arrived_a, arrived_b, arrived_c)
     return (hidden_grad, down_grad)
 
 

time: 135 us -> 133 us (0.985)
  waiting for transfers between devices: 54.3 us -> 38.9 us
  starting transfers between devices: 24.8 us -> 35.2 us
  Pallas kernels: 52.8 us -> 55.5 us
    ppermute x21 -> x23, waiting for transfers between devices: 54.3 us -> 38.9 us  [swapped(): return lax.ppermute(block, axis, [(i, i ^ distance) for i in range(n)])]
    ppermute x21 -> x23, starting transfers between devices: 24.8 us -> 35.2 us  [swapped(): return lax.ppermute(block, axis, [(i, i ^ distance) for i in range(n)])]
    pallas_call x1, Pallas kernels: 3.3 us -> 5.67 us  [shards(): kernel_call(functools.partial(place_kernel, moves), shape(BAL, ff), [IN_V...]
  transfers between devices with their start and end apart: 21 -> 23, of which waited for: 7 -> 10; matrix products, arithmetic and copies ran while one was open for 0% -> 0% of each run, Pallas kernels for 36% -> 38%
where the time goes in v10:
time: 133 us
  Pallas kernels  55.5 us (42%)
  waiting for transfers between devices  38.9 us (29%)
  starting transfers between devices  35.2 us (26%)
  other arithmetic  1.98 us (1%)
    ppermute x23, waiting for transfers between devices, swapped(): return lax.ppermute(block, axis, [(i, i ^ distance) for i in range(n)])  38.9 us
    ppermute x23, starting transfers between devices, swapped(): return lax.ppermute(block, axis, [(i, i ^ distance) for i in range(n)])  35.2 us
    pallas_call x4, Pallas kernels, gelu(): kernel_call(functools.partial(gelu_kernel, late, base, block), [shape(row...  21.4 us
    pallas_call x2, Pallas kernels, grads(): kernel_call(functools.partial(grad_kernel, first_row, first_slope, len(sl...  7.07 us
    pallas_call x2, Pallas kernels, weight_again(): kernel_call(functools.partial(again_kernel, base), [shape(4 * half, part)...  5.7 us
    pallas_call x1, Pallas kernels, shards(): kernel_call(functools.partial(place_kernel, moves), shape(BAL, ff), [IN_V...  5.67 us
    pallas_call x1, Pallas kernels, shards(): kernel_call(first_kernel, [shape(LATE, width), shape(others, width), shap...  4.62 us
    pallas_call x1, Pallas kernels, weight_first(): kernel_call(functools.partial(weight_kernel, count, 0), [shape(width, par...  2.93 us
  transfers between devices with their start and end apart: 23, of which 10 were waited for; matrix products, arithmetic and copies ran while one was open for 0% of the time, Pallas kernels for 38%

profile of v10, /device:TPU:0, one launch (start us, length us, event | category | flops | bytes accessed | tf_op | source)
XLA Modules:
  0.0 132.5 jit_solution(138320850093532173)
XLA Ops:
  1.4 4.6 %shard_map.77 = (bf16[480,384]{1,0:T(8,128)(2,1)S(1)}, bf16[576,384]{1,0:T(8,128)(2,1)S(1)}, bf16[48,1920]{1,0:T(8,128)(2,1)S(1)}) custom-call(s32[9,8]{1,0:T(8,128)S(1)} %pad_add_fusion.meta, bf16[1032,384]{1,0:T(8,128)(2,1)} %cot_hbm.1, f32[1536]{0:T(1024)} %scale_hbm.1, bf16[1032,1536]{1,0:T(8,128)(2,1)} %pre_hbm.9), custom_call_target="tpu_custom_call" | custom-call | flops 1 | bytes 1 | tf_op jit(solution)/shard_map/pallas_call | solution.py:375
  6.6 2.9 %collective-permute-start = (bf16[480,384]{1,0:T(8,128)(2,1)S(1)}, bf16[480,384]{1,0:T(8,128)(2,1)S(1)}, u32[]{:S(2)}, u32[]{:S(2)}) collective-permute-start(bf16[480,384]{1,0:T(8,128)(2,1)S(1)} %get-tuple-element.63.p0.refs_0_), channel_id=1, source_target_pairs={{0,2},{1,3},{2,0},{3,1},{4,6},{5,7},{6,4},{7,5},{8,10},{9,11},{10,... | collective-permute-start | bytes 1105928 | tf_op jit(solution)/shard_map/ppermute | solution.py:302
  9.5 2.6 %collective-permute-start.3 = (bf16[48,1920]{1,0:T(8,128)(2,1)S(1)}, bf16[48,1920]{1,0:T(8,128)(2,1)S(1)}, u32[]{:S(2)}, u32[]{:S(2)}) collective-permute-start(bf16[48,1920]{1,0:T(8,128)(2,1)S(1)} %get-tuple-element.67), channel_id=1, source_target_pairs={{0,16},{4,20},{8,24},{12,28},{16,0},{20,4},{24,8},{28,12},{1,17},{... | collective-permute-start | bytes 552968 | tf_op jit(solution)/shard_map/ppermute | solution.py:302
  12.6 8.4 %shard_map.78 = (bf16[480,1536]{1,0:T(8,128)(2,1)S(1)}, f32[480,1536]{1,0:T(8,128)S(1)}) custom-call(s32[9,8]{1,0:T(8,128)S(1)} %pad_add_fusion.meta, bf16[1032,1536]{1,0:T(8,128)(2,1)} %pre_hbm.9), custom_call_target="tpu_custom_call" | custom-call | flops 1 | bytes 1 | tf_op jit(solution)/shard_map/pallas_call | solution.py:330
  21.2 1.7 %collective-permute-done.4.p3.refs_3_ = bf16[480,384]{1,0:T(8,128)(2,1)S(1)} collective-permute-done((bf16[480,384]{1,0:T(8,128)(2,1)S(1)}, bf16[480,384]{1,0:T(8,128)(2,1)S(1)}, u32[]{:S(2)}, u32[]{:S(2)}) %collective-permute-start.4) | collective-permute-done | bytes 368672 | tf_op jit(solution)/shard_map/ppermute | solution.py:302
  22.9 3.6 %shard_map.79 = (bf16[480,640]{1,0:T(8,128)(2,1)S(1)}, bf16[480,512]{1,0:T(8,128)(2,1)S(1)}, bf16[480,384]{1,0:T(8,128)(2,1)S(1)}) custom-call(s32[9,8]{1,0:T(8,128)S(1)} %pad_add_fusion.meta, bf16[480,384]{1,0:T(8,128)(2,1)S(1)} %get-tuple-element.63.p0.refs_0_, bf16[480,384]{1,0:T(8,128)(2,1)S(1)} %collective-permute-done.1.p1.refs_1_, ...), custom_call_target="tpu_custom_call" | custom-call | flops 1 | bytes 1 | tf_op jit(solution)/shard_map/pallas_call | solution.py:354
  27.8 2.8 %collective-permute-start.10 = (bf16[480,640]{1,0:T(8,128)(2,1)S(1)}, bf16[480,640]{1,0:T(8,128)(2,1)S(1)}, u32[]{:S(2)}, u32[]{:S(2)}) collective-permute-start(bf16[480,640]{1,0:T(8,128)(2,1)S(1)} %get-tuple-element.71), channel_id=1, source_target_pairs={{0,16},{4,20},{8,24},{12,28},{16,0},{20,4},{24,8},{28,12},{1,17},{... | collective-permute-start | bytes 1843208 | tf_op jit(solution)/shard_map/ppermute | solution.py:302
  30.7 4.3 %shard_map.80 = (bf16[576,512]{1,0:T(8,128)(2,1)S(1)}, f32[576,512]{1,0:T(8,128)S(1)}) custom-call(s32[9,8]{1,0:T(8,128)S(1)} %pad_add_fusion.meta, bf16[1032,1536]{1,0:T(8,128)(2,1)} %pre_hbm.9), custom_call_target="tpu_custom_call" | custom-call | flops 1 | bytes 1 | tf_op jit(solution)/shard_map/pallas_call | solution.py:330
  34.9 2.9 %shard_map.81 = (bf16[384,512]{1,0:T(8,128)(2,1)S(1)}, bf16[384,512]{1,0:T(8,128)(2,1)S(1)}, f32[384,512]{1,0:T(8,128)S(1)}, f32[384,512]{1,0:T(8,128)S(1)}, bf1...) custom-call(s32[9,8]{1,0:T(8,128)S(1)} %pad_add_fusion.meta, ...), custom_call_target="tpu_custom_call" | custom-call | flops 1 | bytes 1 | tf_op jit(solution)/shard_map/pallas_call | solution.py:340
  41.5 4.3 %shard_map.82 = (bf16[576,512]{1,0:T(8,128)(2,1)S(1)}, f32[576,512]{1,0:T(8,128)S(1)}) custom-call(s32[9,8]{1,0:T(8,128)S(1)} %pad_add_fusion.meta, bf16[1032,1536]{1,0:T(8,128)(2,1)} %pre_hbm.9), custom_call_target="tpu_custom_call" | custom-call | flops 1 | bytes 1 | tf_op jit(solution)/shard_map/pallas_call | solution.py:330
  45.8 2.9 %shard_map.83 = (bf16[768,512]{1,0:T(8,128)(2,1)S(1)}, f32[768,512]{1,0:T(8,128)S(1)}) custom-call(s32[9,8]{1,0:T(8,128)S(1)} %pad_add_fusion.meta, bf16[1536,480]{1,0:T(8,128)(2,1)S(1)} %get-tuple-element.83.lhs_late, bf16[1536,576]{1,0:T(8,128)(2,1)S(1)} %get-tuple-element.84.lhs_rest, bf16[480,1536]{1,0:T(8,128)(2,1)S(1)} %get-tuple-element.65.refs_8_.act_late, ...), custom_call_target="tpu_custom_call" | custom-call | flops 1 | bytes 1 | tf_op jit(solution)/shard_map/pallas_call | solution.py:348
  50.2 4.5 %shard_map.84 = (bf16[576,512]{1,0:T(8,128)(2,1)S(1)}, f32[576,512]{1,0:T(8,128)S(1)}) custom-call(s32[9,8]{1,0:T(8,128)S(1)} %pad_add_fusion.meta, bf16[1032,1536]{1,0:T(8,128)(2,1)} %pre_hbm.9), custom_call_target="tpu_custom_call" | custom-call | flops 1 | bytes 1 | tf_op jit(solution)/shard_map/pallas_call | solution.py:330
  54.7 2.9 %shard_map.85 = (bf16[768,512]{1,0:T(8,128)(2,1)S(1)}, f32[768,512]{1,0:T(8,128)S(1)}) custom-call(s32[9,8]{1,0:T(8,128)S(1)} %pad_add_fusion.meta, bf16[1536,480]{1,0:T(8,128)(2,1)S(1)} %get-tuple-element.83.lhs_late, bf16[1536,576]{1,0:T(8,128)(2,1)S(1)} %get-tuple-element.84.lhs_rest, bf16[480,1536]{1,0:T(8,128)(2,1)S(1)} %get-tuple-element.65.refs_8_.act_late, ...), custom_call_target="tpu_custom_call" | custom-call | flops 1 | bytes 1 | tf_op jit(solution)/shard_map/pallas_call | solution.py:348
  60.8 1.6 %collective-permute-start.13 = (bf16[384,512]{1,0:T(8,128)(2,1)S(1)}, bf16[384,512]{1,0:T(8,128)(2,1)S(1)}, u32[]{:S(2)}, u32[]{:S(2)}) collective-permute-start(bf16[384,512]{1,0:T(8,128)(2,1)S(1)} %get-tuple-element.95), channel_id=1, source_target_pairs={{0,8},{4,12},{8,0},{12,4},{16,24},{20,28},{24,16},{28,20},{1,9},{5... | collective-permute-start | bytes 1179656 | tf_op jit(solution)/shard_map/ppermute | solution.py:302
  63.5 3.5 %shard_map.87.kept = bf16[528,1536]{1,0:T(8,128)(2,1)S(1)} custom-call(s32[9,8]{1,0:T(8,128)S(1)} %pad_add_fusion.meta, bf16[576,384]{1,0:T(8,128)(2,1)S(1)} %get-tuple-element.66.refs_4_.p0, bf16[576,384]{1,0:T(8,128)(2,1)S(1)} %collective-permute-done.2.refs_5_.p1, bf16[576,384]{1,0:T(8,128)(2,1)S(1)} %collective-permute-done.5.refs_6_.p2, ...), custom_call_target="tpu_custom_call" | custom-call | flops 1 | bytes 1 | tf_op jit(solution)/shard_map/pallas_call | solution.py:354
  66.9 2.9 %shard_map.88.early = bf16[48,1536]{1,0:T(8,128)(2,1)S(1)} custom-call(s32[9,8]{1,0:T(8,128)S(1)} %pad_add_fusion.meta, bf16[48,1920]{1,0:T(8,128)(2,1)S(1)} %collective-permute-done.3.own, bf16[48,384]{1,0:T(8,128)(2,1)S(1)} %collective-permute-done.7.p1, bf16[48,384]{1,0:T(8,128)(2,1)S(1)} %collective-permute-done.8.p2, ...), custom_call_target="tpu_custom_call" | custom-call | flops 1 | bytes 1 | tf_op jit(solution)/shard_map/pallas_call | solution.py:417
  69.8 8.7 %collective-permute-done.13.got = bf16[384,512]{1,0:T(8,128)(2,1)S(1)} collective-permute-done((bf16[384,512]{1,0:T(8,128)(2,1)S(1)}, bf16[384,512]{1,0:T(8,128)(2,1)S(1)}, u32[]{:S(2)}, u32[]{:S(2)}) %collective-permute-start.13) | collective-permute-done | bytes 393248 | tf_op jit(solution)/shard_map/ppermute | solution.py:302
  80.4 4.1 %collective-permute-start.19 = (bf16[192,512]{1,0:T(8,128)(2,1)S(1)}, bf16[192,512]{1,0:T(8,128)(2,1)S(1)}, u32[]{:S(2)}, u32[]{:S(2)}) collective-permute-start(bf16[192,512]{1,0:T(8,128)(2,1)S(1)} %get-tuple-element.108), channel_id=1, source_target_pairs={{0,16},{4,20},{8,24},{12,28},{16,0},{20,4},{24,8},{28,12},{1,17},{... | collective-permute-start | bytes 589832 | tf_op jit(solution)/shard_map/ppermute | solution.py:302
  84.5 3.4 %collective-permute-done.15.rest_1_ = bf16[480,512]{1,0:T(8,128)(2,1)S(1)} collective-permute-done((bf16[480,512]{1,0:T(8,128)(2,1)S(1)}, bf16[480,512]{1,0:T(8,128)(2,1)S(1)}, u32[]{:S(2)}, u32[]{:S(2)}) %collective-permute-start.15) | collective-permute-done | bytes 491552 | tf_op jit(solution)/shard_map/ppermute | solution.py:302
  87.9 5.2 %collective-permute-done.16.refs_1_ = bf16[768,512]{1,0:T(8,128)(2,1)S(1)} collective-permute-done((bf16[768,512]{1,0:T(8,128)(2,1)S(1)}, bf16[768,512]{1,0:T(8,128)(2,1)S(1)}, u32[]{:S(2)}, u32[]{:S(2)}) %collective-permute-start.16) | collective-permute-done | bytes 786464 | tf_op jit(solution)/shard_map/ppermute | solution.py:302
  97.2 11.0 %collective-permute-start.21 = (bf16[192,512]{1,0:T(8,128)(2,1)S(1)}, bf16[192,512]{1,0:T(8,128)(2,1)S(1)}, u32[]{:S(2)}, u32[]{:S(2)}) collective-permute-start(bf16[192,512]{1,0:T(8,128)(2,1)S(1)} %get-tuple-element.115), channel_id=1, source_target_pairs={{0,16},{4,20},{8,24},{12,28},{16,0},{20,4},{24,8},{28,12},{1,17},{... | collective-permute-start | bytes 589832 | tf_op jit(solution)/shard_map/ppermute | solution.py:302
  108.2 14.2 %collective-permute-done.18.rest_2_ = bf16[480,384]{1,0:T(8,128)(2,1)S(1)} collective-permute-done((bf16[480,384]{1,0:T(8,128)(2,1)S(1)}, bf16[480,384]{1,0:T(8,128)(2,1)S(1)}, u32[]{:S(2)}, u32[]{:S(2)}) %collective-permute-start.18) | collective-permute-done | bytes 368672 | tf_op jit(solution)/shard_map/ppermute | solution.py:302
  123.2 5.7 %shard_map.94 = bf16[720,1536]{1,0:T(8,128)(2,1)} custom-call(s32[9,8]{1,0:T(8,128)S(1)} %pad_add_fusion.meta, bf16[528,1536]{1,0:T(8,128)(2,1)S(1)} %shard_map.87.kept, bf16[48,1536]{1,0:T(8,128)(2,1)S(1)} %shard_map.88.early, bf16[480,640]{1,0:T(8,128)(2,1)S(1)} %collective-permute-done.10.rest_0_, bf16[480,512]{1,0:T(8,128)(2,1)S(1)} %collective-permute-done.15.rest_1_, ...), custom_call_target="tpu_custom_call" | custom-call | flops 1 | bytes 1 | tf_op jit(solution)/shard_map/pallas_call | solution.py:437
  129.0 2.4 %collective-permute-done.22 = bf16[192,512]{1,0:T(8,128)(2,1)S(1)} collective-permute-done((bf16[192,512]{1,0:T(8,128)(2,1)S(1)}, bf16[192,512]{1,0:T(8,128)(2,1)S(1)}, u32[]{:S(2)}, u32[]{:S(2)}) %collective-permute-start.22) | collective-permute-done | bytes 196640 | tf_op jit(solution)/shard_map/ppermute | solution.py:302
  (49 shorter events, 20.7 us)
Async XLA Ops:
  1.4 21.5 %copy-start = (bf16[1536,1536]{1,0:T(8,128)(2,1)S(1)}, bf16[1536,1536]{1,0:T(8,128)(2,1)}, u32[]{:S(2)}) copy-start(bf16[1536,1536]{1,0:T(8,128)(2,1)} %weight.5) | copy-start | bytes 14155780
  6.0 15.1 %collective-permute-start.2 = (bf16[576,384]{1,0:T(8,128)(2,1)S(1)}, bf16[576,384]{1,0:T(8,128)(2,1)S(1)}, u32[]{:S(2)}, u32[]{:S(2)}) collective-permute-start(bf16[576,384]{1,0:T(8,128)(2,1)S(1)} %get-tuple-element.66.refs_4_.p0), channel_id=1, source_target_pairs={{0,1},{1,0},{2,3},{3,2},{4,5},{5,4},{6,7},{7,6},{8,9},{9,8},{10,11... | collective-permute-start | bytes 1327112 | tf_op jit(solution)/shard_map/ppermute | solution.py:302
  6.5 14.6 %collective-permute-start.1 = (bf16[480,384]{1,0:T(8,128)(2,1)S(1)}, bf16[480,384]{1,0:T(8,128)(2,1)S(1)}, u32[]{:S(2)}, u32[]{:S(2)}) collective-permute-start(bf16[480,384]{1,0:T(8,128)(2,1)S(1)} %get-tuple-element.63.p0.refs_0_), channel_id=1, source_target_pairs={{0,1},{1,0},{2,3},{3,2},{4,5},{5,4},{6,7},{7,6},{8,9},{9,8},{10,11... | collective-permute-start | bytes 1105928 | tf_op jit(solution)/shard_map/ppermute | solution.py:302
  6.6 14.5 %collective-permute-start = (bf16[480,384]{1,0:T(8,128)(2,1)S(1)}, bf16[480,384]{1,0:T(8,128)(2,1)S(1)}, u32[]{:S(2)}, u32[]{:S(2)}) collective-permute-start(bf16[480,384]{1,0:T(8,128)(2,1)S(1)} %get-tuple-element.63.p0.refs_0_), channel_id=1, source_target_pairs={{0,2},{1,3},{2,0},{3,1},{4,6},{5,7},{6,4},{7,5},{8,10},{9,11},{10,... | collective-permute-start | bytes 1105928 | tf_op jit(solution)/shard_map/ppermute | solution.py:302
  9.5 11.5 %collective-permute-start.3 = (bf16[48,1920]{1,0:T(8,128)(2,1)S(1)}, bf16[48,1920]{1,0:T(8,128)(2,1)S(1)}, u32[]{:S(2)}, u32[]{:S(2)}) collective-permute-start(bf16[48,1920]{1,0:T(8,128)(2,1)S(1)} %get-tuple-element.67), channel_id=1, source_target_pairs={{0,16},{4,20},{8,24},{12,28},{16,0},{20,4},{24,8},{28,12},{1,17},{... | collective-permute-start | bytes 552968 | tf_op jit(solution)/shard_map/ppermute | solution.py:302
  12.1 15.7 %collective-permute-start.5 = (bf16[576,384]{1,0:T(8,128)(2,1)S(1)}, bf16[576,384]{1,0:T(8,128)(2,1)S(1)}, u32[]{:S(2)}, u32[]{:S(2)}) collective-permute-start(bf16[576,384]{1,0:T(8,128)(2,1)S(1)} %get-tuple-element.66.refs_4_.p0), channel_id=1, source_target_pairs={{0,2},{1,3},{2,0},{3,1},{4,6},{5,7},{6,4},{7,5},{8,10},{9,11},{10,... | collective-permute-start | bytes 1327112 | tf_op jit(solution)/shard_map/ppermute | solution.py:302
  21.1 1.8 %collective-permute-start.4 = (bf16[480,384]{1,0:T(8,128)(2,1)S(1)}, bf16[480,384]{1,0:T(8,128)(2,1)S(1)}, u32[]{:S(2)}, u32[]{:S(2)}) collective-permute-start(bf16[480,384]{1,0:T(8,128)(2,1)S(1)} %collective-permute-done.p2.refs_2_), channel_id=1, source_target_pairs={{0,1},{1,0},{2,3},{3,2},{4,5},{5,4},{6,7},{7,6},{8,9},{9,8},{10,11... | collective-permute-start | bytes 1105928 | tf_op jit(solution)/shard_map/ppermute | solution.py:302
  27.8 7.1 %collective-permute-start.6 = (bf16[576,384]{1,0:T(8,128)(2,1)S(1)}, bf16[576,384]{1,0:T(8,128)(2,1)S(1)}, u32[]{:S(2)}, u32[]{:S(2)}) collective-permute-start(bf16[576,384]{1,0:T(8,128)(2,1)S(1)} %collective-permute-done.5.refs_6_.p2), channel_id=1, source_target_pairs={{0,1},{1,0},{2,3},{3,2},{4,5},{5,4},{6,7},{7,6},{8,9},{9,8},{10,11... | collective-permute-start | bytes 1327112 | tf_op jit(solution)/shard_map/ppermute | solution.py:302
  27.8 30.5 %collective-permute-start.10 = (bf16[480,640]{1,0:T(8,128)(2,1)S(1)}, bf16[480,640]{1,0:T(8,128)(2,1)S(1)}, u32[]{:S(2)}, u32[]{:S(2)}) collective-permute-start(bf16[480,640]{1,0:T(8,128)(2,1)S(1)} %get-tuple-element.71), channel_id=1, source_target_pairs={{0,16},{4,20},{8,24},{12,28},{16,0},{20,4},{24,8},{28,12},{1,17},{... | collective-permute-start | bytes 1843208 | tf_op jit(solution)/shard_map/ppermute | solution.py:302
  37.9 7.9 %collective-permute-start.8 = (bf16[48,384]{1,0:T(8,128)(2,1)S(1)}, bf16[48,384]{1,0:T(8,128)(2,1)S(1)}, u32[]{:S(2)}, u32[]{:S(2)}) collective-permute-start(bf16[48,384]{1,0:T(8,128)(2,1)S(1)} %slice.4), channel_id=1, source_target_pairs={{0,2},{1,3},{2,0},{3,1},{4,6},{5,7},{6,4},{7,5},{8,10},{9,11},{10,... | collective-permute-start | bytes 110600 | tf_op jit(solution)/shard_map/ppermute | solution.py:302
  39.5 6.3 %collective-permute-start.7 = (bf16[48,384]{1,0:T(8,128)(2,1)S(1)}, bf16[48,384]{1,0:T(8,128)(2,1)S(1)}, u32[]{:S(2)}, u32[]{:S(2)}) collective-permute-start(bf16[48,384]{1,0:T(8,128)(2,1)S(1)} %slice.4), channel_id=1, source_target_pairs={{0,1},{1,0},{2,3},{3,2},{4,5},{5,4},{6,7},{7,6},{8,9},{9,8},{10,11... | collective-permute-start | bytes 110600 | tf_op jit(solution)/shard_map/ppermute | solution.py:302
  39.5 18.9 %collective-permute-start.11 = (bf16[384,512]{1,0:T(8,128)(2,1)S(1)}, bf16[384,512]{1,0:T(8,128)(2,1)S(1)}, u32[]{:S(2)}, u32[]{:S(2)}) collective-permute-start(bf16[384,512]{1,0:T(8,128)(2,1)S(1)} %get-tuple-element.93), channel_id=1, source_target_pairs={{0,4},{4,0},{8,12},{12,8},{16,20},{20,16},{24,28},{28,24},{1,5},{5... | collective-permute-start | bytes 1179656 | tf_op jit(solution)/shard_map/ppermute | solution.py:302
  41.0 18.8 %collective-permute-start.12 = (bf16[384,512]{1,0:T(8,128)(2,1)S(1)}, bf16[384,512]{1,0:T(8,128)(2,1)S(1)}, u32[]{:S(2)}, u32[]{:S(2)}) collective-permute-start(bf16[384,512]{1,0:T(8,128)(2,1)S(1)} %get-tuple-element.94), channel_id=1, source_target_pairs={{0,4},{4,0},{8,12},{12,8},{16,20},{20,16},{24,28},{28,24},{1,5},{5... | collective-permute-start | bytes 1179656 | tf_op jit(solution)/shard_map/ppermute | solution.py:302
  48.6 29.9 %collective-permute-start.14 = (bf16[768,512]{1,0:T(8,128)(2,1)S(1)}, bf16[768,512]{1,0:T(8,128)(2,1)S(1)}, u32[]{:S(2)}, u32[]{:S(2)}) collective-permute-start(bf16[768,512]{1,0:T(8,128)(2,1)S(1)} %get-tuple-element.85), channel_id=1, source_target_pairs={{0,4},{4,0},{8,12},{12,8},{16,20},{20,16},{24,28},{28,24},{1,5},{5... | collective-permute-start | bytes 2359304 | tf_op jit(solution)/shard_map/ppermute | solution.py:302
  50.2 4.5 %collective-permute-start.9 = (bf16[48,384]{1,0:T(8,128)(2,1)S(1)}, bf16[48,384]{1,0:T(8,128)(2,1)S(1)}, u32[]{:S(2)}, u32[]{:S(2)}) collective-permute-start(bf16[48,384]{1,0:T(8,128)(2,1)S(1)} %collective-permute-done.8.p2), channel_id=1, source_target_pairs={{0,1},{1,0},{2,3},{3,2},{4,5},{5,4},{6,7},{7,6},{8,9},{9,8},{10,11... | collective-permute-start | bytes 110600 | tf_op jit(solution)/shard_map/ppermute | solution.py:302
  57.6 35.6 %collective-permute-start.16 = (bf16[768,512]{1,0:T(8,128)(2,1)S(1)}, bf16[768,512]{1,0:T(8,128)(2,1)S(1)}, u32[]{:S(2)}, u32[]{:S(2)}) collective-permute-start(bf16[768,512]{1,0:T(8,128)(2,1)S(1)} %get-tuple-element.90), channel_id=1, source_target_pairs={{0,4},{4,0},{8,12},{12,8},{16,20},{20,16},{24,28},{28,24},{1,5},{5... | collective-permute-start | bytes 2359304 | tf_op jit(solution)/shard_map/ppermute | solution.py:302
  60.8 17.8 %collective-permute-start.13 = (bf16[384,512]{1,0:T(8,128)(2,1)S(1)}, bf16[384,512]{1,0:T(8,128)(2,1)S(1)}, u32[]{:S(2)}, u32[]{:S(2)}) collective-permute-start(bf16[384,512]{1,0:T(8,128)(2,1)S(1)} %get-tuple-element.95), channel_id=1, source_target_pairs={{0,8},{4,12},{8,0},{12,4},{16,24},{20,28},{24,16},{28,20},{1,9},{5... | collective-permute-start | bytes 1179656 | tf_op jit(solution)/shard_map/ppermute | solution.py:302
  62.4 25.5 %collective-permute-start.15 = (bf16[480,512]{1,0:T(8,128)(2,1)S(1)}, bf16[480,512]{1,0:T(8,128)(2,1)S(1)}, u32[]{:S(2)}, u32[]{:S(2)}) collective-permute-start(bf16[480,512]{1,0:T(8,128)(2,1)S(1)} %get-tuple-element.109), channel_id=1, source_target_pairs={{0,16},{4,20},{8,24},{12,28},{16,0},{20,4},{24,8},{28,12},{1,17},{... | collective-permute-start | bytes 1474568 | tf_op jit(solution)/shard_map/ppermute | solution.py:302
  79.5 16.9 %collective-permute-start.17 = (bf16[384,512]{1,0:T(8,128)(2,1)S(1)}, bf16[384,512]{1,0:T(8,128)(2,1)S(1)}, u32[]{:S(2)}, u32[]{:S(2)}) collective-permute-start(bf16[384,512]{1,0:T(8,128)(2,1)S(1)} %get-tuple-element.104), channel_id=1, source_target_pairs={{0,8},{4,12},{8,0},{12,4},{16,24},{20,28},{24,16},{28,20},{1,9},{5... | collective-permute-start | bytes 1179656 | tf_op jit(solution)/shard_map/ppermute | solution.py:302
  80.4 27.8 %collective-permute-start.19 = (bf16[192,512]{1,0:T(8,128)(2,1)S(1)}, bf16[192,512]{1,0:T(8,128)(2,1)S(1)}, u32[]{:S(2)}, u32[]{:S(2)}) collective-permute-start(bf16[192,512]{1,0:T(8,128)(2,1)S(1)} %get-tuple-element.108), channel_id=1, source_target_pairs={{0,16},{4,20},{8,24},{12,28},{16,0},{20,4},{24,8},{28,12},{1,17},{... | collective-permute-start | bytes 589832 | tf_op jit(solution)/shard_map/ppermute | solution.py:302
  94.1 28.3 %collective-permute-start.20 = (bf16[384,512]{1,0:T(8,128)(2,1)S(1)}, bf16[384,512]{1,0:T(8,128)(2,1)S(1)}, u32[]{:S(2)}, u32[]{:S(2)}) collective-permute-start(bf16[384,512]{1,0:T(8,128)(2,1)S(1)} %get-tuple-element.112), channel_id=1, source_target_pairs={{0,8},{4,12},{8,0},{12,4},{16,24},{20,28},{24,16},{28,20},{1,9},{5... | collective-permute-start | bytes 1179656 | tf_op jit(solution)/shard_map/ppermute | solution.py:302
  95.7 26.6 %collective-permute-start.18 = (bf16[480,384]{1,0:T(8,128)(2,1)S(1)}, bf16[480,384]{1,0:T(8,128)(2,1)S(1)}, u32[]{:S(2)}, u32[]{:S(2)}) collective-permute-start(bf16[480,384]{1,0:T(8,128)(2,1)S(1)} %get-tuple-element.116), channel_id=1, source_target_pairs={{0,16},{4,20},{8,24},{12,28},{16,0},{20,4},{24,8},{28,12},{1,17},{... | collective-permute-start | bytes 1105928 | tf_op jit(solution)/shard_map/ppermute | solution.py:302
  97.2 31.7 %collective-permute-start.21 = (bf16[192,512]{1,0:T(8,128)(2,1)S(1)}, bf16[192,512]{1,0:T(8,128)(2,1)S(1)}, u32[]{:S(2)}, u32[]{:S(2)}) collective-permute-start(bf16[192,512]{1,0:T(8,128)(2,1)S(1)} %get-tuple-element.115), channel_id=1, source_target_pairs={{0,16},{4,20},{8,24},{12,28},{16,0},{20,4},{24,8},{28,12},{1,17},{... | collective-permute-start | bytes 589832 | tf_op jit(solution)/shard_map/ppermute | solution.py:302
  123.2 8.2 %collective-permute-start.22 = (bf16[192,512]{1,0:T(8,128)(2,1)S(1)}, bf16[192,512]{1,0:T(8,128)(2,1)S(1)}, u32[]{:S(2)}, u32[]{:S(2)}) collective-permute-start(bf16[192,512]{1,0:T(8,128)(2,1)S(1)} %get-tuple-element.119), channel_id=1, source_target_pairs={{0,16},{4,20},{8,24},{12,28},{16,0},{20,4},{24,8},{28,12},{1,17},{... | collective-permute-start | bytes 589832 | tf_op jit(solution)/shard_map/ppermute | solution.py:302

commit v11 on v10

--- a/solution.py
+++ b/solution.py
@@ -130,33 +130,40 @@
     return x * cumulative, cumulative + x * jnp.exp(-0.5 * x * x) * inv_root_tau
 
 
+def cut_at(widths, block):
+    return [
+        (i, c, min(block, width - c)) for i, width in enumerate(widths) for c in range(0, width, block)
+    ]
+
+
 def gelu_kernel(late, base, block, meta, pre_hbm, act_out, der_out, pick, rows_f32, pre, sems):
     home = pre.shape[1]
     rows = pick.shape[0]
-    blocks = act_out.shape[1] // block
-
-    def fetch(i):
-        columns = pl.ds(base + i * block, block)
-        return pltpu.make_async_copy(pre_hbm.at[:, columns], pre.at[i], sems.at[i])
-
-    for i in range(blocks):
-        fetch(i).start()
+    blocks = cut_at((act_out.shape[1],), block)
+    copies = [
+        pltpu.make_async_copy(
+            pre_hbm.at[:, pl.ds(base + at, wide)], pre.at[i, :, pl.ds(0, wide)], sems.at[i]
+        )
+        for i, (_, at, wide) in enumerate(blocks)
+    ]
+    for copy in copies:
+        copy.start()
     if late:
         pick[...] = late_picks(meta, home)
     else:
         pick[0:EARLY, :] = early_picks(meta, home)
         pick[EARLY:, :] = kept_picks(meta, home)
     step = next(TILE * k for k in (3, 4, 2, 1) if rows % (TILE * k) == 0)
-    for i in range(blocks):
-        fetch(i).wait()
-        rows_f32[...] = jnp.dot(pick[...], pre[i], preferred_element_type=F32)
-        columns = slice(i * block, (i + 1) * block)
+    for i, (_, at, wide) in enumerate(blocks):
+        copies[i].wait()
+        rows_f32[:, 0:wide] = jnp.dot(pick[...], pre[i, :, 0:wide], preferred_element_type=F32)
+        columns = slice(at, at + wide)
 
         def body(k, _):
-            at = pl.ds(pl.multiple_of(k * step, step), step)
-            value, slope = gelu_and_slope(rows_f32[at, :])
-            act_out[at, columns] = value.astype(BF)
-            der_out[at, columns] = slope
+            rows = pl.ds(pl.multiple_of(k * step, step), step)
+            value, slope = gelu_and_slope(rows_f32[rows, 0:wide])
+            act_out[rows, columns] = value.astype(BF)
+            der_out[rows, columns] = slope
             return 0
 
         lax.fori_loop(0, rows // step, body, 0)
@@ -170,19 +177,23 @@
         lhs[:, columns] = piece[first_row : first_row + rows, 0:width]
 
 
-def grad_kernel(first_row, first_slope, slope_count, block, meta, p0, p1, p2, p3, weight, *rest):
+def grad_kernel(first_row, first_slope, base, slope_count, block, meta, p0, p1, p2, p3, weight, *rest):
     slopes, outs, lhs = rest[:slope_count], rest[slope_count:-1], rest[-1]
     rows = lhs.shape[0]
     assemble(meta, (p0, p1, p2, p3), first_row, lhs)
-    part = slopes[0].shape[1]
-    at = 0
-    for out in outs:
-        for c in range(0, out.shape[1], block):
-            wide = min(block, out.shape[1] - c)
-            slope = slopes[at // part][first_slope : first_slope + rows, at % part : at % part + wide]
-            value = jnp.dot(lhs[...], weight[:, at : at + wide], preferred_element_type=F32)
-            out[:, c : c + wide] = (value * slope).astype(BF)
-            at += wide
+    parts = slopes if slope_count > len(outs) else outs
+    starts = [sum(part.shape[1] for part in parts[:i]) for i in range(len(parts))]
+    slope_rows = slice(first_slope, first_slope + rows)
+    for i, c, wide in cut_at([part.shape[1] for part in parts], block):
+        at = starts[i] + c
+        inside, whole_at = slice(c, c + wide), slice(at, at + wide)
+        slope = slopes[i][slope_rows, inside] if slope_count == len(parts) else slopes[0][slope_rows, whole_at]
+        columns = slice(base + at, base + at + wide)
+        value = (jnp.dot(lhs[...], weight[:, columns], preferred_element_type=F32) * slope).astype(BF)
+        if len(outs) == len(parts):
+            outs[i][:, inside] = value
+        else:
+            outs[0][:, whole_at] = value
 
 
 def early_kernel(block, meta, own, p1, p2, p3, weight, out, lhs, acc):
@@ -201,7 +212,7 @@
         lax.fori_loop(0, EARLY // TILE, body, 0)
 
 
-def weight_kernel(count, base, meta, *refs):
+def weight_kernel(count, meta, *refs):
     lates, rests = refs[:count], refs[count : 2 * count]
     act_late, act_rest, *outs, lhs_late, lhs_rest = refs[2 * count :]
     half = lates[0].shape[1] // 2
@@ -212,17 +223,16 @@
             lo, hi = both[:half], both[half:]
             lhs[i * half : (i + 1) * half, :] = jnp.where(mine, hi, lo)
             lhs[(count + i) * half : (count + i + 1) * half, :] = jnp.where(mine, lo, hi)
-    again_kernel(base, meta, lhs_late, lhs_rest, act_late, act_rest, *outs)
-
-
-def again_kernel(base, meta, lhs_late, lhs_rest, act_late, act_rest, *outs):
-    columns = slice(base, base + act_rest.shape[1])
+    again_kernel(meta, lhs_late, lhs_rest, act_late, act_rest, *outs)
+
+
+def again_kernel(meta, lhs_late, lhs_rest, act_late, act_rest, *outs):
     step = lhs_late.shape[0] // 4
     at = 0
     for out in outs:
         for i in range(0, out.shape[0], step):
             part = slice(at, at + step)
-            value = jnp.dot(lhs_late[part, :], act_late[:, columns], preferred_element_type=F32)
+            value = jnp.dot(lhs_late[part, :], act_late[...], preferred_element_type=F32)
             value += jnp.dot(lhs_rest[part, :], act_rest[...], preferred_element_type=F32)
             out[i : i + step, :] = value.astype(out.dtype)
             at += step
@@ -313,7 +323,9 @@
     home, ff = hidden_pre.shape
     width = cotangent.shape[1]
     features = down_weight.shape[0]
-    half, part = width // 2, ff // 3
+    half = width // 2
+    parts = (640, 512, ff - 1152)
+    begins = (0, 640, 1152)
     others = EARLY + KEEP
     n = lax.axis_size("dp")
     d = lax.axis_index("dp").astype(jnp.int32)
@@ -327,32 +339,33 @@
     def gelu(meta, late, base, columns):
         block = 256
         rows = LATE if late else others
+        count = pl.cdiv(columns, block)
         return kernel_call(
             functools.partial(gelu_kernel, late, base, block),
             [shape(rows, columns), shape(rows, columns, F32)],
             [IN_HBM], [IN_VMEM] * 2,
-            [vmem((rows, home), BF), vmem((rows, block), F32), vmem((columns // block, home, block), BF),
-             sems((columns // block,))],
+            [vmem((rows, home), BF), vmem((rows, block), F32), vmem((count, home, block), BF), sems((count,))],
         )(meta, hidden_pre)
 
-    def weight_first(meta, act):
+    def weight_first(meta, act_late, act):
         count = len(lates)
         return kernel_call(
-            functools.partial(weight_kernel, count, 0),
-            [shape(width, part)] * 2 + [shape(width, part, F32)] * 2
+            functools.partial(weight_kernel, count),
+            [shape(width, parts[0])] * 2 + [shape(width, parts[0], F32)] * 2
             + [shape(count * width, LATE), shape(count * width, others)],
             [IN_VMEM] * (2 * count + 2), [IN_VMEM] * 6,
         )(meta, *lates, *rests, act_late, act)
 
-    def weight_again(meta, base, act):
+    def weight_again(meta, act_late, act):
+        columns = act.shape[1]
         return kernel_call(
-            functools.partial(again_kernel, base),
-            [shape(4 * half, part), shape(4 * half, part, F32)], [IN_VMEM] * 4, [IN_VMEM] * 2,
+            again_kernel,
+            [shape(4 * half, columns), shape(4 * half, columns, F32)], [IN_VMEM] * 4, [IN_VMEM] * 2,
         )(meta, *lhs, act_late, act)
 
-    def grads(meta, pieces, first_row, first_slope, rows, slopes, cuts):
+    def grads(meta, pieces, first_row, first_slope, rows, base, slopes, cuts):
         return kernel_call(
-            functools.partial(grad_kernel, first_row, first_slope, len(slopes), 256),
+            functools.partial(grad_kernel, first_row, first_slope, base, len(slopes), 256),
             [shape(rows, c) for c in cuts], [IN_VMEM] * (5 + len(slopes)), [IN_VMEM] * len(cuts),
             [vmem((rows, features), BF)],
         )(meta, *pieces, down_weight, *slopes)
@@ -361,15 +374,16 @@
         return kernel_call(tick_kernel, shape(8, 128, F32), [], IN_VMEM)(meta)
 
     def near_step(meta, keeps, gots):
-        count = len(keeps)
+        count, columns = len(keeps), keeps[0].shape[1]
         return kernel_call(
             functools.partial(near_kernel, count),
-            [shape(width, part), shape(width, part, F32)], [IN_VMEM] * (2 * count), [IN_VMEM] * 2,
+            [shape(width, columns), shape(width, columns, F32)], [IN_VMEM] * (2 * count), [IN_VMEM] * 2,
         )(meta, *keeps, *gots)
 
     def far_step(meta, mine, got):
+        columns = got.shape[1]
         return kernel_call(
-            far_kernel, [shape(half, part), shape(half, part, F32)], [IN_VMEM] * 2, [IN_VMEM] * 2
+            far_kernel, [shape(half, columns), shape(half, columns, F32)], [IN_VMEM] * 2, [IN_VMEM] * 2
         )(meta, mine, got)
 
     late, rest, early = kernel_call(
@@ -381,61 +395,65 @@
 
     late_c, late_y = swapped(late, "tensor", 1), swapped(late, "tensor", 2)
     rest_c, rest_y = swapped(rest, "tensor", 1), swapped(rest, "tensor", 2)
-    act_late, der_late = gelu(after(meta, late), True, 0, ff)
-    late_y = after(late_y, act_late, late_c, rest_c, arrived_early)
+    act_l1, der_l1 = gelu(after(meta, late), True, 0, parts[0])
+    late_y = after(late_y, act_l1, late_c, rest_c, arrived_early)
     late_yc = swapped(late_y, "tensor", 1)
     lates = (late, late_c, late_y, late_yc)
 
-    moves = (640, 512, ff - 1152)
-    moving = grads(after(meta, late_y), lates, 0, 0, LATE, (der_late,), moves)
-    arrived_a = swapped(moving[0], "dp", n // 2)
-    rest_y = after(rest_y, *moving)
+    (moving_a,) = grads(after(meta, late_y), lates, 0, 0, LATE, 0, (der_l1,), parts[:1])
+    arrived_a = swapped(moving_a, "dp", n // 2)
+
+    act_a, der_a = gelu(after(meta, moving_a), False, 0, parts[0])
+    rest_y = after(rest_y, act_a)
     rest_yc = swapped(rest_y, "tensor", 1)
     rests = (rest, rest_c, rest_y, rest_yc)
-
-    act_a, der_a = gelu(after(meta, *moving), False, 0, part)
-    *sends_a, keep_01, keep_23, lhs_late, lhs_rest = weight_first(after(meta, act_a), act_a)
+    *sends_a, keep_01, keep_23, lhs_late, lhs_rest = weight_first(after(meta, act_a), act_l1, act_a)
     lhs = (lhs_late, lhs_rest)
     gots_a = [swapped(send, "dp", 1) for send in sends_a]
-    early_sent = after(arrived_early[:, :width], keep_01)
+
+    act_l2, der_l2 = gelu(after(meta, keep_01), True, begins[1], parts[1])
+    (moving_b,) = grads(after(meta, act_l2), lates, 0, 0, LATE, begins[1], (der_l2,), parts[1:2])
+    act_b, der_b = gelu(after(meta, moving_b), False, begins[1], parts[1])
+    send_b, keep_b = weight_again(after(meta, act_b, arrived_a), act_l2, act_b)
+    got_b = swapped(send_b, "dp", 1)
+    arrived_b = swapped(after(moving_b, send_b), "dp", n // 2)
+
+    act_l3, der_l3 = gelu(after(meta, send_b), True, begins[2], parts[2])
+    early_sent = after(arrived_early[:, :width], act_l3)
     early_c, early_y = swapped(early_sent, "tensor", 1), swapped(early_sent, "tensor", 2)
-    act_b, der_b = gelu(after(meta, keep_01), False, part, part)
-    send_b, keep_b = weight_again(after(meta, act_b, early_c, early_y), part, act_b)
-    got_b = swapped(send_b, "dp", 1)
-    early_y = after(early_y, send_b)
+    act_c, der_c = gelu(after(meta, act_l3), False, begins[2], parts[2])
+    send_c, keep_c = weight_again(after(meta, act_c, early_c, early_y), act_l3, act_c)
+    got_c = swapped(send_c, "dp", 1)
+    early_y = after(early_y, send_c)
     early_yc = swapped(early_y, "tensor", 1)
-    act_c, der_c = gelu(after(meta, send_b), False, 2 * part, part)
-    send_c, keep_c = weight_again(after(meta, act_c, early_yc), 2 * part, act_c)
-    got_c = swapped(send_c, "dp", 1)
-
-    out_na, mine_a = near_step(after(meta, send_c, arrived_a), (keep_01, keep_23), gots_a)
+
+    out_na, mine_a = near_step(after(meta, send_c), (keep_01, keep_23), gots_a)
     got_na = swapped(out_na, "dp", 2)
-    tick_a = tick(after(meta, out_na))
-    arrived_b = swapped(after(moving[1], tick_a), "dp", n // 2)
-
-    (kept_grad,) = grads(after(meta, tick_a), rests, EARLY, EARLY, KEEP, (der_a, der_b, der_c), (ff,))
+
+    (moving_c,) = grads(after(meta, out_na), lates, 0, 0, LATE, begins[2], (der_l3,), parts[2:])
+    (kept_grad,) = grads(after(meta, moving_c), rests, EARLY, EARLY, KEEP, 0, (der_a, der_b, der_c), (ff,))
     early_grad = kernel_call(
         functools.partial(early_kernel, 256), shape(EARLY, ff), [IN_VMEM] * 5, IN_VMEM,
         [vmem((EARLY, features), BF), vmem((EARLY, 256), F32)],
     )(after(meta, kept_grad), arrived_early, early_c, early_y, early_yc, down_weight)
 
-    out_nb, mine_b = near_step(after(meta, early_grad, got_na), (keep_b,), (got_b,))
+    out_nb, mine_b = near_step(after(meta, early_grad, arrived_b), (keep_b,), (got_b,))
     got_nb = swapped(out_nb, "dp", 2)
     tick_b = tick(after(meta, out_nb))
-    arrived_c = swapped(after(moving[2], tick_b), "dp", n // 2)
+    arrived_c = swapped(after(moving_c, tick_b), "dp", n // 2)
     out_fa, own_a = far_step(after(meta, tick_b), mine_a, got_na)
     got_fa = swapped(out_fa, "dp", 4)
-    out_nc, mine_c = near_step(after(meta, out_fa, arrived_b), (keep_c,), (got_c,))
+    out_nc, mine_c = near_step(after(meta, out_fa, arrived_c), (keep_c,), (got_c,))
     got_nc = swapped(out_nc, "dp", 2)
     out_fb, own_b = far_step(after(meta, out_nc), mine_b, got_nb)
     got_fb = swapped(out_fb, "dp", 4)
-    out_fc, own_c = far_step(after(meta, out_fb, arrived_c, got_fa), mine_c, got_nc)
+    out_fc, own_c = far_step(after(meta, out_fb, got_fa), mine_c, got_nc)
     got_fc = swapped(out_fc, "dp", 4)
     total = [a + b.astype(F32) for a, b in ((own_a, got_fa), (own_b, got_fb), (own_c, got_fc))]
     down_grad = jnp.concatenate(total, axis=1) / math.sqrt(n * home)
 
     hidden_grad = kernel_call(
-        functools.partial(place_kernel, moves), shape(BAL, ff), [IN_VMEM] * (2 + len(moves)),
+        functools.partial(place_kernel, parts), shape(BAL, ff), [IN_VMEM] * (2 + len(parts)),
         pl.BlockSpec((BAL, 128), lambda i, *_: (0, i)), grid=(ff // 128,),
     )(after(meta, out_fc), kept_grad, early_grad, arrived_a, arrived_b, arrived_c)
     return (hidden_grad, down_grad)

time: 133 us -> 134 us (level)
  starting transfers between devices: 35.2 us -> 18.5 us
  waiting for transfers between devices: 38.9 us -> 48.7 us
  Pallas kernels: 55.5 us -> 63.2 us
    ppermute x23, starting transfers between devices: 35.2 us -> 18.5 us  [swapped(): return lax.ppermute(block, axis, [(i, i ^ distance) for i in range(n)])]
    ppermute x23, waiting for transfers between devices: 38.9 us -> 48.7 us  [swapped(): return lax.ppermute(block, axis, [(i, i ^ distance) for i in range(n)])]
    pallas_call x4 -> x6, Pallas kernels: 21.4 us -> 25.8 us  [gelu(): kernel_call(functools.partial(gelu_kernel, late, base, block), [shape(row...]
    pallas_call x12 -> x14, Pallas kernels: 26.6 us -> 29.9 us  [the longest x4 9.37 us: grads(): kernel_call(functools.partial(grad_kernel, first_row, first_slope, base,...]
  transfers between devices with their start and end apart: 23 -> 23, of which waited for: 10 -> 13; matrix products, arithmetic and copies ran while one was open for 0% -> 0% of each run, Pallas kernels for 38% -> 44%
where the time goes in v11:
time: 134 us; the launch traced here: 133 us
  Pallas kernels  63.2 us (47%)
  waiting for transfers between devices  48.7 us (36%)
  starting transfers between devices  18.5 us (14%)
  other arithmetic  2 us (1%)
    ppermute x23, waiting for transfers between devices, swapped(): return lax.ppermute(block, axis, [(i, i ^ distance) for i in range(n)])  48.7 us
    pallas_call x6, Pallas kernels, gelu(): kernel_call(functools.partial(gelu_kernel, late, base, block), [shape(row...  25.8 us
    ppermute x23, starting transfers between devices, swapped(): return lax.ppermute(block, axis, [(i, i ^ distance) for i in range(n)])  18.5 us
    pallas_call x4, Pallas kernels, grads(): kernel_call(functools.partial(grad_kernel, first_row, first_slope, base,...  9.37 us
    pallas_call x1, Pallas kernels, shards(): kernel_call(functools.partial(place_kernel, parts), shape(BAL, ff), [IN_V...  5.67 us
    pallas_call x2, Pallas kernels, weight_again(): kernel_call(again_kernel, [shape(4 * half, columns), shape(4 * half, colu...  5.62 us
    pallas_call x1, Pallas kernels, shards(): kernel_call(first_kernel, [shape(LATE, width), shape(others, width), shap...  4.62 us
    pallas_call x1, Pallas kernels, weight_first(): kernel_call(functools.partial(weight_kernel, count), [shape(width, parts[...  3.99 us
  transfers between devices with their start and end apart: 23, of which 13 were waited for; matrix products, arithmetic and copies ran while one was open for 0% of the time, Pallas kernels for 44%

profile of v11, /device:TPU:0, one launch (start us, length us, event | category | flops | bytes accessed | tf_op | source)
XLA Modules:
  0.0 133.3 jit_solution(15216103759678982106)
XLA Ops:
  1.4 4.6 %shard_map.77 = (bf16[480,384]{1,0:T(8,128)(2,1)S(1)}, bf16[576,384]{1,0:T(8,128)(2,1)S(1)}, bf16[48,1920]{1,0:T(8,128)(2,1)S(1)}) custom-call(s32[9,8]{1,0:T(8,128)S(1)} %pad_add_fusion.meta, bf16[1032,384]{1,0:T(8,128)(2,1)} %cot_hbm.1, f32[1536]{0:T(1024)} %scale_hbm.1, bf16[1032,1536]{1,0:T(8,128)(2,1)} %pre_hbm.13), custom_call_target="tpu_custom_call" | custom-call | flops 1 | bytes 1 | tf_op jit(solution)/shard_map/pallas_call | solution.py:389
  6.6 2.9 %collective-permute-start = (bf16[480,384]{1,0:T(8,128)(2,1)S(1)}, bf16[480,384]{1,0:T(8,128)(2,1)S(1)}, u32[]{:S(2)}, u32[]{:S(2)}) collective-permute-start(bf16[480,384]{1,0:T(8,128)(2,1)S(1)} %get-tuple-element.67.p0.refs_0_), channel_id=1, source_target_pairs={{0,2},{1,3},{2,0},{3,1},{4,6},{5,7},{6,4},{7,5},{8,10},{9,11},{10,... | collective-permute-start | bytes 1105928 | tf_op jit(solution)/shard_map/ppermute | solution.py:312
  9.5 2.6 %collective-permute-start.3 = (bf16[48,1920]{1,0:T(8,128)(2,1)S(1)}, bf16[48,1920]{1,0:T(8,128)(2,1)S(1)}, u32[]{:S(2)}, u32[]{:S(2)}) collective-permute-start(bf16[48,1920]{1,0:T(8,128)(2,1)S(1)} %get-tuple-element.71), channel_id=1, source_target_pairs={{0,16},{4,20},{8,24},{12,28},{16,0},{20,4},{24,8},{28,12},{1,17},{... | collective-permute-start | bytes 552968 | tf_op jit(solution)/shard_map/ppermute | solution.py:312
  12.1 4.7 %shard_map.78 = (bf16[480,640]{1,0:T(8,128)(2,1)S(1)}, f32[480,640]{1,0:T(8,128)S(1)}) custom-call(s32[9,8]{1,0:T(8,128)S(1)} %pad_add_fusion.meta, bf16[1032,1536]{1,0:T(8,128)(2,1)} %pre_hbm.13), custom_call_target="tpu_custom_call" | custom-call | flops 1 | bytes 1 | tf_op jit(solution)/shard_map/pallas_call | solution.py:343
  16.9 3.9 %collective-permute-done.3.own = bf16[48,1920]{1,0:T(8,128)(2,1)S(1)} collective-permute-done((bf16[48,1920]{1,0:T(8,128)(2,1)S(1)}, bf16[48,1920]{1,0:T(8,128)(2,1)S(1)}, u32[]{:S(2)}, u32[]{:S(2)}) %collective-permute-start.3) | collective-permute-done | bytes 184352 | tf_op jit(solution)/shard_map/ppermute | solution.py:312
  22.5 2.1 %shard_map.79 = bf16[480,640]{1,0:T(8,128)(2,1)S(1)} custom-call(s32[9,8]{1,0:T(8,128)S(1)} %pad_add_fusion.meta, bf16[480,384]{1,0:T(8,128)(2,1)S(1)} %get-tuple-element.67.p0.refs_0_, bf16[480,384]{1,0:T(8,128)(2,1)S(1)} %collective-permute-done.1.p1.refs_1_, bf16[480,384]{1,0:T(8,128)(2,1)S(1)} %collective-permute-done.p2.refs_2_, ...), custom_call_target="tpu_custom_call" | custom-call | flops 1 | bytes 1 | tf_op jit(solution)/shard_map/pallas_call | solution.py:367
  25.0 5.0 %shard_map.80 = (bf16[576,640]{1,0:T(8,128)(2,1)S(1)}, f32[576,640]{1,0:T(8,128)S(1)}) custom-call(s32[9,8]{1,0:T(8,128)S(1)} %pad_add_fusion.meta, bf16[1032,1536]{1,0:T(8,128)(2,1)} %pre_hbm.13), custom_call_target="tpu_custom_call" | custom-call | flops 1 | bytes 1 | tf_op jit(solution)/shard_map/pallas_call | solution.py:343
  30.0 3.4 %collective-permute-done.5.refs_6_.p2 = bf16[576,384]{1,0:T(8,128)(2,1)S(1)} collective-permute-done((bf16[576,384]{1,0:T(8,128)(2,1)S(1)}, bf16[576,384]{1,0:T(8,128)(2,1)S(1)}, u32[]{:S(2)}, u32[]{:S(2)}) %collective-permute-start.5) | collective-permute-done | bytes 442400 | tf_op jit(solution)/shard_map/ppermute | solution.py:312
  35.2 4.0 %shard_map.81 = (bf16[384,640]{1,0:T(8,128)(2,1)S(1)}, bf16[384,640]{1,0:T(8,128)(2,1)S(1)}, f32[384,640]{1,0:T(8,128)S(1)}, f32[384,640]{1,0:T(8,128)S(1)}, bf1...) custom-call(s32[9,8]{1,0:T(8,128)S(1)} %pad_add_fusion.meta, ...), custom_call_target="tpu_custom_call" | custom-call | flops 1 | bytes 1 | tf_op jit(solution)/shard_map/pallas_call | solution.py:352
  41.3 3.9 %shard_map.82 = (bf16[480,512]{1,0:T(8,128)(2,1)S(1)}, f32[480,512]{1,0:T(8,128)S(1)}) custom-call(s32[9,8]{1,0:T(8,128)S(1)} %pad_add_fusion.meta, bf16[1032,1536]{1,0:T(8,128)(2,1)} %pre_hbm.13), custom_call_target="tpu_custom_call" | custom-call | flops 1 | bytes 1 | tf_op jit(solution)/shard_map/pallas_call | solution.py:343
  46.9 4.3 %shard_map.84 = (bf16[576,512]{1,0:T(8,128)(2,1)S(1)}, f32[576,512]{1,0:T(8,128)S(1)}) custom-call(s32[9,8]{1,0:T(8,128)S(1)} %pad_add_fusion.meta, bf16[1032,1536]{1,0:T(8,128)(2,1)} %pre_hbm.13), custom_call_target="tpu_custom_call" | custom-call | flops 1 | bytes 1 | tf_op jit(solution)/shard_map/pallas_call | solution.py:343
  51.2 3.4 %collective-permute-done.7.rest_0_ = bf16[480,640]{1,0:T(8,128)(2,1)S(1)} collective-permute-done((bf16[480,640]{1,0:T(8,128)(2,1)S(1)}, bf16[480,640]{1,0:T(8,128)(2,1)S(1)}, u32[]{:S(2)}, u32[]{:S(2)}) %collective-permute-start.7) | collective-permute-done | bytes 614432 | tf_op jit(solution)/shard_map/ppermute | solution.py:312
  54.6 2.8 %shard_map.85 = (bf16[768,512]{1,0:T(8,128)(2,1)S(1)}, f32[768,512]{1,0:T(8,128)S(1)}) custom-call(s32[9,8]{1,0:T(8,128)S(1)} %pad_add_fusion.meta, bf16[1536,480]{1,0:T(8,128)(2,1)S(1)} %get-tuple-element.87.lhs_late, bf16[1536,576]{1,0:T(8,128)(2,1)S(1)} %get-tuple-element.88.lhs_rest, bf16[480,512]{1,0:T(8,128)(2,1)S(1)} %get-tuple-element.81.act_late, ...), custom_call_target="tpu_custom_call" | custom-call | flops 1 | bytes 1 | tf_op jit(solution)/shard_map/pallas_call | solution.py:361
  59.0 3.9 %shard_map.86 = (bf16[480,384]{1,0:T(8,128)(2,1)S(1)}, f32[480,384]{1,0:T(8,128)S(1)}) custom-call(s32[9,8]{1,0:T(8,128)S(1)} %pad_add_fusion.meta, bf16[1032,1536]{1,0:T(8,128)(2,1)} %pre_hbm.13), custom_call_target="tpu_custom_call" | custom-call | flops 1 | bytes 1 | tf_op jit(solution)/shard_map/pallas_call | solution.py:343
  63.5 3.5 %collective-permute-done.9.p2 = bf16[48,384]{1,0:T(8,128)(2,1)S(1)} collective-permute-done((bf16[48,384]{1,0:T(8,128)(2,1)S(1)}, bf16[48,384]{1,0:T(8,128)(2,1)S(1)}, u32[]{:S(2)}, u32[]{:S(2)}) %collective-permute-start.9) | collective-permute-done | bytes 36896 | tf_op jit(solution)/shard_map/ppermute | solution.py:312
  67.0 4.0 %shard_map.87 = (bf16[576,384]{1,0:T(8,128)(2,1)S(1)}, f32[576,384]{1,0:T(8,128)S(1)}) custom-call(s32[9,8]{1,0:T(8,128)S(1)} %pad_add_fusion.meta, bf16[1032,1536]{1,0:T(8,128)(2,1)} %pre_hbm.13), custom_call_target="tpu_custom_call" | custom-call | flops 1 | bytes 1 | tf_op jit(solution)/shard_map/pallas_call | solution.py:343
  71.0 2.8 %shard_map.88 = (bf16[768,384]{1,0:T(8,128)(2,1)S(1)}, f32[768,384]{1,0:T(8,128)S(1)}) custom-call(s32[9,8]{1,0:T(8,128)S(1)} %pad_add_fusion.meta, bf16[1536,480]{1,0:T(8,128)(2,1)S(1)} %get-tuple-element.87.lhs_late, bf16[1536,576]{1,0:T(8,128)(2,1)S(1)} %get-tuple-element.88.lhs_rest, bf16[480,384]{1,0:T(8,128)(2,1)S(1)} %get-tuple-element.91.act_late, ...), custom_call_target="tpu_custom_call" | custom-call | flops 1 | bytes 1 | tf_op jit(solution)/shard_map/pallas_call | solution.py:361
  78.9 3.9 %shard_map.91.kept = bf16[528,1536]{1,0:T(8,128)(2,1)S(1)} custom-call(s32[9,8]{1,0:T(8,128)S(1)} %pad_add_fusion.meta, bf16[576,384]{1,0:T(8,128)(2,1)S(1)} %get-tuple-element.70.refs_4_.p0, bf16[576,384]{1,0:T(8,128)(2,1)S(1)} %collective-permute-done.2.refs_5_.p1, bf16[576,384]{1,0:T(8,128)(2,1)S(1)} %collective-permute-done.5.refs_6_.p2, ...), custom_call_target="tpu_custom_call" | custom-call | flops 1 | bytes 1 | tf_op jit(solution)/shard_map/pallas_call | solution.py:367
  82.8 2.9 %shard_map.92.early = bf16[48,1536]{1,0:T(8,128)(2,1)S(1)} custom-call(s32[9,8]{1,0:T(8,128)S(1)} %pad_add_fusion.meta, bf16[48,1920]{1,0:T(8,128)(2,1)S(1)} %collective-permute-done.3.own, bf16[48,384]{1,0:T(8,128)(2,1)S(1)} %collective-permute-done.8.p1, bf16[48,384]{1,0:T(8,128)(2,1)S(1)} %collective-permute-done.9.p2, ...), custom_call_target="tpu_custom_call" | custom-call | flops 1 | bytes 1 | tf_op jit(solution)/shard_map/pallas_call | solution.py:435
  89.9 2.9 %collective-permute-done.15.got = bf16[384,640]{1,0:T(8,128)(2,1)S(1)} collective-permute-done((bf16[384,640]{1,0:T(8,128)(2,1)S(1)}, bf16[384,640]{1,0:T(8,128)(2,1)S(1)}, u32[]{:S(2)}, u32[]{:S(2)}) %collective-permute-start.15) | collective-permute-done | bytes 491552 | tf_op jit(solution)/shard_map/ppermute | solution.py:312
  93.7 13.2 %collective-permute-done.16.rest_2_ = bf16[480,384]{1,0:T(8,128)(2,1)S(1)} collective-permute-done((bf16[480,384]{1,0:T(8,128)(2,1)S(1)}, bf16[480,384]{1,0:T(8,128)(2,1)S(1)}, u32[]{:S(2)}, u32[]{:S(2)}) %collective-permute-start.16) | collective-permute-done | bytes 368672 | tf_op jit(solution)/shard_map/ppermute | solution.py:312
  111.3 6.2 %collective-permute-done.19 = bf16[192,640]{1,0:T(8,128)(2,1)S(1)} collective-permute-done((bf16[192,640]{1,0:T(8,128)(2,1)S(1)}, bf16[192,640]{1,0:T(8,128)(2,1)S(1)}, u32[]{:S(2)}, u32[]{:S(2)}) %collective-permute-start.19) | collective-permute-done | bytes 245792 | tf_op jit(solution)/shard_map/ppermute | solution.py:312
  117.5 5.2 %collective-permute-done.20.got = bf16[384,384]{1,0:T(8,128)(2,1)S(1)} collective-permute-done((bf16[384,384]{1,0:T(8,128)(2,1)S(1)}, bf16[384,384]{1,0:T(8,128)(2,1)S(1)}, u32[]{:S(2)}, u32[]{:S(2)}) %collective-permute-start.20) | collective-permute-done | bytes 294944 | tf_op jit(solution)/shard_map/ppermute | solution.py:312
  125.7 5.7 %shard_map.98 = bf16[720,1536]{1,0:T(8,128)(2,1)} custom-call(s32[9,8]{1,0:T(8,128)S(1)} %pad_add_fusion.meta, bf16[528,1536]{1,0:T(8,128)(2,1)S(1)} %shard_map.91.kept, bf16[48,1536]{1,0:T(8,128)(2,1)S(1)} %shard_map.92.early, bf16[480,640]{1,0:T(8,128)(2,1)S(1)} %collective-permute-done.7.rest_0_, bf16[480,512]{1,0:T(8,128)(2,1)S(1)} %collective-permute-done.13.rest_1_, ...), custom_call_target="tpu_custom_call" | custom-call | flops 1 | bytes 1 | tf_op jit(solution)/shard_map/pallas_call | solution.py:455
  (53 shorter events, 30.8 us)
Async XLA Ops:
  1.4 21.1 %copy-start = (bf16[1536,1536]{1,0:T(8,128)(2,1)S(1)}, bf16[1536,1536]{1,0:T(8,128)(2,1)}, u32[]{:S(2)}) copy-start(bf16[1536,1536]{1,0:T(8,128)(2,1)} %weight.9) | copy-start | bytes 14155780
  6.0 14.7 %collective-permute-start.2 = (bf16[576,384]{1,0:T(8,128)(2,1)S(1)}, bf16[576,384]{1,0:T(8,128)(2,1)S(1)}, u32[]{:S(2)}, u32[]{:S(2)}) collective-permute-start(bf16[576,384]{1,0:T(8,128)(2,1)S(1)} %get-tuple-element.70.refs_4_.p0), channel_id=1, source_target_pairs={{0,1},{1,0},{2,3},{3,2},{4,5},{5,4},{6,7},{7,6},{8,9},{9,8},{10,11... | collective-permute-start | bytes 1327112 | tf_op jit(solution)/shard_map/ppermute | solution.py:312
  6.5 14.2 %collective-permute-start.1 = (bf16[480,384]{1,0:T(8,128)(2,1)S(1)}, bf16[480,384]{1,0:T(8,128)(2,1)S(1)}, u32[]{:S(2)}, u32[]{:S(2)}) collective-permute-start(bf16[480,384]{1,0:T(8,128)(2,1)S(1)} %get-tuple-element.67.p0.refs_0_), channel_id=1, source_target_pairs={{0,1},{1,0},{2,3},{3,2},{4,5},{5,4},{6,7},{7,6},{8,9},{9,8},{10,11... | collective-permute-start | bytes 1105928 | tf_op jit(solution)/shard_map/ppermute | solution.py:312
  6.6 14.1 %collective-permute-start = (bf16[480,384]{1,0:T(8,128)(2,1)S(1)}, bf16[480,384]{1,0:T(8,128)(2,1)S(1)}, u32[]{:S(2)}, u32[]{:S(2)}) collective-permute-start(bf16[480,384]{1,0:T(8,128)(2,1)S(1)} %get-tuple-element.67.p0.refs_0_), channel_id=1, source_target_pairs={{0,2},{1,3},{2,0},{3,1},{4,6},{5,7},{6,4},{7,5},{8,10},{9,11},{10,... | collective-permute-start | bytes 1105928 | tf_op jit(solution)/shard_map/ppermute | solution.py:312
  9.5 11.2 %collective-permute-start.3 = (bf16[48,1920]{1,0:T(8,128)(2,1)S(1)}, bf16[48,1920]{1,0:T(8,128)(2,1)S(1)}, u32[]{:S(2)}, u32[]{:S(2)}) collective-permute-start(bf16[48,1920]{1,0:T(8,128)(2,1)S(1)} %get-tuple-element.71), channel_id=1, source_target_pairs={{0,16},{4,20},{8,24},{12,28},{16,0},{20,4},{24,8},{28,12},{1,17},{... | collective-permute-start | bytes 552968 | tf_op jit(solution)/shard_map/ppermute | solution.py:312
  20.7 1.8 %collective-permute-start.4 = (bf16[480,384]{1,0:T(8,128)(2,1)S(1)}, bf16[480,384]{1,0:T(8,128)(2,1)S(1)}, u32[]{:S(2)}, u32[]{:S(2)}) collective-permute-start(bf16[480,384]{1,0:T(8,128)(2,1)S(1)} %collective-permute-done.p2.refs_2_), channel_id=1, source_target_pairs={{0,1},{1,0},{2,3},{3,2},{4,5},{5,4},{6,7},{7,6},{8,9},{9,8},{10,11... | collective-permute-start | bytes 1105928 | tf_op jit(solution)/shard_map/ppermute | solution.py:312
  20.8 12.6 %collective-permute-start.5 = (bf16[576,384]{1,0:T(8,128)(2,1)S(1)}, bf16[576,384]{1,0:T(8,128)(2,1)S(1)}, u32[]{:S(2)}, u32[]{:S(2)}) collective-permute-start(bf16[576,384]{1,0:T(8,128)(2,1)S(1)} %get-tuple-element.70.refs_4_.p0), channel_id=1, source_target_pairs={{0,2},{1,3},{2,0},{3,1},{4,6},{5,7},{6,4},{7,5},{8,10},{9,11},{10,... | collective-permute-start | bytes 1327112 | tf_op jit(solution)/shard_map/ppermute | solution.py:312
  24.6 30.0 %collective-permute-start.7 = (bf16[480,640]{1,0:T(8,128)(2,1)S(1)}, bf16[480,640]{1,0:T(8,128)(2,1)S(1)}, u32[]{:S(2)}, u32[]{:S(2)}) collective-permute-start(bf16[480,640]{1,0:T(8,128)(2,1)S(1)} %shard_map.79), channel_id=1, source_target_pairs={{0,16},{4,20},{8,24},{12,28},{16,0},{20,4},{24,8},{28,12},{1,17},{... | collective-permute-start | bytes 1843208 | tf_op jit(solution)/shard_map/ppermute | solution.py:312
  33.4 1.8 %collective-permute-start.6 = (bf16[576,384]{1,0:T(8,128)(2,1)S(1)}, bf16[576,384]{1,0:T(8,128)(2,1)S(1)}, u32[]{:S(2)}, u32[]{:S(2)}) collective-permute-start(bf16[576,384]{1,0:T(8,128)(2,1)S(1)} %collective-permute-done.5.refs_6_.p2), channel_id=1, source_target_pairs={{0,1},{1,0},{2,3},{3,2},{4,5},{5,4},{6,7},{7,6},{8,9},{9,8},{10,11... | collective-permute-start | bytes 1327112 | tf_op jit(solution)/shard_map/ppermute | solution.py:312
  39.2 34.6 %collective-permute-start.10 = (bf16[384,640]{1,0:T(8,128)(2,1)S(1)}, bf16[384,640]{1,0:T(8,128)(2,1)S(1)}, u32[]{:S(2)}, u32[]{:S(2)}) collective-permute-start(bf16[384,640]{1,0:T(8,128)(2,1)S(1)} %get-tuple-element.99), channel_id=1, source_target_pairs={{0,4},{4,0},{8,12},{12,8},{16,20},{20,16},{24,28},{28,24},{1,5},{5... | collective-permute-start | bytes 1474568 | tf_op jit(solution)/shard_map/ppermute | solution.py:312
  40.8 33.0 %collective-permute-start.11 = (bf16[384,640]{1,0:T(8,128)(2,1)S(1)}, bf16[384,640]{1,0:T(8,128)(2,1)S(1)}, u32[]{:S(2)}, u32[]{:S(2)}) collective-permute-start(bf16[384,640]{1,0:T(8,128)(2,1)S(1)} %get-tuple-element.100), channel_id=1, source_target_pairs={{0,4},{4,0},{8,12},{12,8},{16,20},{20,16},{24,28},{28,24},{1,5},{5... | collective-permute-start | bytes 1474568 | tf_op jit(solution)/shard_map/ppermute | solution.py:312
  57.5 28.3 %collective-permute-start.14 = (bf16[768,512]{1,0:T(8,128)(2,1)S(1)}, bf16[768,512]{1,0:T(8,128)(2,1)S(1)}, u32[]{:S(2)}, u32[]{:S(2)}) collective-permute-start(bf16[768,512]{1,0:T(8,128)(2,1)S(1)} %get-tuple-element.89), channel_id=1, source_target_pairs={{0,4},{4,0},{8,12},{12,8},{16,20},{20,16},{24,28},{28,24},{1,5},{5... | collective-permute-start | bytes 2359304 | tf_op jit(solution)/shard_map/ppermute | solution.py:312
  59.0 26.7 %collective-permute-start.13 = (bf16[480,512]{1,0:T(8,128)(2,1)S(1)}, bf16[480,512]{1,0:T(8,128)(2,1)S(1)}, u32[]{:S(2)}, u32[]{:S(2)}) collective-permute-start(bf16[480,512]{1,0:T(8,128)(2,1)S(1)} %shard_map.83), channel_id=1, source_target_pairs={{0,16},{4,20},{8,24},{12,28},{16,0},{20,4},{24,8},{28,12},{1,17},{... | collective-permute-start | bytes 1474568 | tf_op jit(solution)/shard_map/ppermute | solution.py:312
  62.9 4.0 %collective-permute-start.9 = (bf16[48,384]{1,0:T(8,128)(2,1)S(1)}, bf16[48,384]{1,0:T(8,128)(2,1)S(1)}, u32[]{:S(2)}, u32[]{:S(2)}) collective-permute-start(bf16[48,384]{1,0:T(8,128)(2,1)S(1)} %slice.4), channel_id=1, source_target_pairs={{0,2},{1,3},{2,0},{3,1},{4,6},{5,7},{6,4},{7,5},{8,10},{9,11},{10,... | collective-permute-start | bytes 110600 | tf_op jit(solution)/shard_map/ppermute | solution.py:312
  67.0 4.0 %collective-permute-start.8 = (bf16[48,384]{1,0:T(8,128)(2,1)S(1)}, bf16[48,384]{1,0:T(8,128)(2,1)S(1)}, u32[]{:S(2)}, u32[]{:S(2)}) collective-permute-start(bf16[48,384]{1,0:T(8,128)(2,1)S(1)} %slice.4), channel_id=1, source_target_pairs={{0,1},{1,0},{2,3},{3,2},{4,5},{5,4},{6,7},{7,6},{8,9},{9,8},{10,11... | collective-permute-start | bytes 110600 | tf_op jit(solution)/shard_map/ppermute | solution.py:312
  74.8 17.9 %collective-permute-start.15 = (bf16[384,640]{1,0:T(8,128)(2,1)S(1)}, bf16[384,640]{1,0:T(8,128)(2,1)S(1)}, u32[]{:S(2)}, u32[]{:S(2)}) collective-permute-start(bf16[384,640]{1,0:T(8,128)(2,1)S(1)} %get-tuple-element.101), channel_id=1, source_target_pairs={{0,8},{4,12},{8,0},{12,4},{16,24},{20,28},{24,16},{28,20},{1,9},{5... | collective-permute-start | bytes 1474568 | tf_op jit(solution)/shard_map/ppermute | solution.py:312
  76.7 30.2 %collective-permute-start.17 = (bf16[768,384]{1,0:T(8,128)(2,1)S(1)}, bf16[768,384]{1,0:T(8,128)(2,1)S(1)}, u32[]{:S(2)}, u32[]{:S(2)}) collective-permute-start(bf16[768,384]{1,0:T(8,128)(2,1)S(1)} %get-tuple-element.96), channel_id=1, source_target_pairs={{0,4},{4,0},{8,12},{12,8},{16,20},{20,16},{24,28},{28,24},{1,5},{5... | collective-permute-start | bytes 1769480 | tf_op jit(solution)/shard_map/ppermute | solution.py:312
  77.2 5.6 %collective-permute-start.12 = (bf16[48,384]{1,0:T(8,128)(2,1)S(1)}, bf16[48,384]{1,0:T(8,128)(2,1)S(1)}, u32[]{:S(2)}, u32[]{:S(2)}) collective-permute-start(bf16[48,384]{1,0:T(8,128)(2,1)S(1)} %collective-permute-done.9.p2), channel_id=1, source_target_pairs={{0,1},{1,0},{2,3},{3,2},{4,5},{5,4},{6,7},{7,6},{8,9},{9,8},{10,11... | collective-permute-start | bytes 110600 | tf_op jit(solution)/shard_map/ppermute | solution.py:312
  86.7 20.2 %collective-permute-start.16 = (bf16[480,384]{1,0:T(8,128)(2,1)S(1)}, bf16[480,384]{1,0:T(8,128)(2,1)S(1)}, u32[]{:S(2)}, u32[]{:S(2)}) collective-permute-start(bf16[480,384]{1,0:T(8,128)(2,1)S(1)} %shard_map.90), channel_id=1, source_target_pairs={{0,16},{4,20},{8,24},{12,28},{16,0},{20,4},{24,8},{28,12},{1,17},{... | collective-permute-start | bytes 1105928 | tf_op jit(solution)/shard_map/ppermute | solution.py:312
  88.2 21.4 %collective-permute-start.18 = (bf16[384,512]{1,0:T(8,128)(2,1)S(1)}, bf16[384,512]{1,0:T(8,128)(2,1)S(1)}, u32[]{:S(2)}, u32[]{:S(2)}) collective-permute-start(bf16[384,512]{1,0:T(8,128)(2,1)S(1)} %get-tuple-element.113), channel_id=1, source_target_pairs={{0,8},{4,12},{8,0},{12,4},{16,24},{20,28},{24,16},{28,20},{1,9},{5... | collective-permute-start | bytes 1179656 | tf_op jit(solution)/shard_map/ppermute | solution.py:312
  93.6 23.9 %collective-permute-start.19 = (bf16[192,640]{1,0:T(8,128)(2,1)S(1)}, bf16[192,640]{1,0:T(8,128)(2,1)S(1)}, u32[]{:S(2)}, u32[]{:S(2)}) collective-permute-start(bf16[192,640]{1,0:T(8,128)(2,1)S(1)} %get-tuple-element.117), channel_id=1, source_target_pairs={{0,16},{4,20},{8,24},{12,28},{16,0},{20,4},{24,8},{28,12},{1,17},{... | collective-permute-start | bytes 737288 | tf_op jit(solution)/shard_map/ppermute | solution.py:312
  107.7 15.0 %collective-permute-start.20 = (bf16[384,384]{1,0:T(8,128)(2,1)S(1)}, bf16[384,384]{1,0:T(8,128)(2,1)S(1)}, u32[]{:S(2)}, u32[]{:S(2)}) collective-permute-start(bf16[384,384]{1,0:T(8,128)(2,1)S(1)} %get-tuple-element.121), channel_id=1, source_target_pairs={{0,8},{4,12},{8,0},{12,4},{16,24},{20,28},{24,16},{28,20},{1,9},{5... | collective-permute-start | bytes 884744 | tf_op jit(solution)/shard_map/ppermute | solution.py:312
  110.4 15.2 %collective-permute-start.21 = (bf16[192,512]{1,0:T(8,128)(2,1)S(1)}, bf16[192,512]{1,0:T(8,128)(2,1)S(1)}, u32[]{:S(2)}, u32[]{:S(2)}) collective-permute-start(bf16[192,512]{1,0:T(8,128)(2,1)S(1)} %get-tuple-element.124), channel_id=1, source_target_pairs={{0,16},{4,20},{8,24},{12,28},{16,0},{20,4},{24,8},{28,12},{1,17},{... | collective-permute-start | bytes 589832 | tf_op jit(solution)/shard_map/ppermute | solution.py:312
  123.5 8.6 %collective-permute-start.22 = (bf16[192,384]{1,0:T(8,128)(2,1)S(1)}, bf16[192,384]{1,0:T(8,128)(2,1)S(1)}, u32[]{:S(2)}, u32[]{:S(2)}) collective-permute-start(bf16[192,384]{1,0:T(8,128)(2,1)S(1)} %get-tuple-element.127), channel_id=1, source_target_pairs={{0,16},{4,20},{8,24},{12,28},{16,0},{20,4},{24,8},{28,12},{1,17},{... | collective-permute-start | bytes 442376 | tf_op jit(solution)/shard_map/ppermute | solution.py:312

commit v12 on v11

v12 whole, which is shorter than its diff:
```python
import functools
import math

import jax
import jax.numpy as jnp
from jax import lax
from jax.experimental import pallas as pl
from jax.experimental.pallas import tpu as pltpu
from jax.sharding import PartitionSpec as P

SEND = 528
KEEP = 528
TILE = 16
SLOTS = 4
BAL = 720
BF = jnp.bfloat16
F32 = jnp.float32

inv_root_two = 0.7071067811865476
inv_root_tau = 0.3989422804014327


def kernel_call(kernel, out_shape, in_specs, out_specs, scratch=(), grid=(1,)):
    return pl.pallas_call(
        kernel,
        grid_spec=pltpu.PrefetchScalarGridSpec(
            num_scalar_prefetch=1,
            grid=grid,
            in_specs=in_specs,
            out_specs=out_specs,
            scratch_shapes=list(scratch),
        ),
        out_shape=out_shape,
        cost_estimate=pl.CostEstimate(flops=1, bytes_accessed=1, transcendentals=0),
        compiler_params=pltpu.CompilerParams(vmem_limit_bytes=16 * 1024 * 1024),
    )


IN_VMEM = pl.BlockSpec(memory_space=pltpu.VMEM)
IN_HBM = pl.BlockSpec(memory_space=pltpu.HBM)


def shape(a, b, dtype=BF):
    return jax.ShapeDtypeStruct((a, b), dtype)


def lengths_of(meta, d):
    return [meta[j, d] for j in range(SLOTS)]


def moves_of(meta, d):
    return [meta[SLOTS + j, d] for j in range(SLOTS)]


def dp_at(meta):
    return meta[2 * SLOTS, 0]


def tensor_at(meta):
    return meta[2 * SLOTS, 1]


def kept_total(meta, d):
    return sum(a * (1 - b) for a, b in zip(lengths_of(meta, d), moves_of(meta, d)))


def picks(meta, moved, first, rows, home):
    d = dp_at(meta)
    at = lax.broadcasted_iota(jnp.int32, (rows, 1), 0) - first
    source = jnp.full((rows, 1), -1, jnp.int32)
    begin = jnp.int32(0)
    start = jnp.int32(0)
    for length, move in zip(lengths_of(meta, d), moves_of(meta, d)):
        size = length * (move if moved else 1 - move)
        inside = (at >= begin) & (at < begin + size)
        source = jnp.where(inside, at + (start - begin), source)
        begin = begin + size
        start = start + length
    columns = lax.broadcasted_iota(jnp.int32, (rows, home), 1)
    return jnp.where(columns == source, 1.0, 0.0).astype(BF)


def moved_picks(meta, home):
    n = meta.shape[1]
    partner = lax.rem(dp_at(meta) + n // 2, n)
    return picks(meta, True, lax.rem(kept_total(meta, partner), TILE), SEND, home)


def kept_picks(meta, home):
    return picks(meta, False, 0, KEEP, home)


def scaled_rows(meta, pick, cot, scale):
    width = cot.shape[1]
    rows = jnp.dot(pick, cot[...], preferred_element_type=F32)
    own = scale[pl.ds(pl.multiple_of(tensor_at(meta) * width, 128), width)]
    return (rows * own[None, :]).astype(BF)


def first_kernel(meta, cot_hbm, scale_hbm, moved_out, kept_out, cot, scale, sems):
    home = cot.shape[0]
    pairs = ((cot_hbm, cot), (scale_hbm, scale))
    copies = [pltpu.make_async_copy(a, b, sems.at[i]) for i, (a, b) in enumerate(pairs)]
    for copy in copies:
        copy.start()
    moved = moved_picks(meta, home)
    kept = kept_picks(meta, home)
    for copy in copies:
        copy.wait()
    moved_out[...] = scaled_rows(meta, moved, cot, scale)
    kept_out[...] = scaled_rows(meta, kept, cot, scale)


def gelu_and_slope(x):
    cumulative = 0.5 * (1.0 + lax.erf(x * inv_root_two))
    return x * cumulative, cumulative + x * jnp.exp(-0.5 * x * x) * inv_root_tau


def cut_at(widths, block):
    return [
        (i, c, min(block, width - c)) for i, width in enumerate(widths) for c in range(0, width, block)
    ]


def gelu_kernel(moved, base, block, meta, pre_hbm, act_out, der_out, pick, rows_f32, pre, sems):
    home = pre.shape[1]
    rows = pick.shape[0]
    blocks = cut_at((act_out.shape[1],), block)
    copies = [
        pltpu.make_async_copy(
            pre_hbm.at[:, pl.ds(base + at, wide)], pre.at[i, :, pl.ds(0, wide)], sems.at[i]
        )
        for i, (_, at, wide) in enumerate(blocks)
    ]
    for copy in copies:
        copy.start()
    pick[...] = moved_picks(meta, home) if moved else kept_picks(meta, home)
    step = next(TILE * k for k in (3, 4, 2, 1) if rows % (TILE * k) == 0)
    for i, (_, at, wide) in enumerate(blocks):
        copies[i].wait()
        rows_f32[:, 0:wide] = jnp.dot(pick[...], pre[i, :, 0:wide], preferred_element_type=F32)
        columns = slice(at, at + wide)

        def body(k, _):
            rows = pl.ds(pl.multiple_of(k * step, step), step)
            value, slope = gelu_and_slope(rows_f32[rows, 0:wide])
            act_out[rows, columns] = value.astype(BF)
            der_out[rows, columns] = slope
            return 0

        lax.fori_loop(0, rows // step, body, 0)


def grad_kernel(base, slope_count, block, meta, p0, p1, p2, p3, weight_hbm, *rest):
    slopes, outs, (lhs, weight, sems) = rest[:slope_count], rest[slope_count:-3], rest[-3:]
    parts = slopes if slope_count > len(outs) else outs
    starts = [sum(part.shape[1] for part in parts[:i]) for i in range(len(parts))]
    blocks = cut_at([part.shape[1] for part in parts], block)
    copies = [
        pltpu.make_async_copy(
            weight_hbm.at[:, pl.ds(base + starts[i] + c, wide)], weight.at[k, :, pl.ds(0, wide)], sems.at[k]
        )
        for k, (i, c, wide) in enumerate(blocks)
    ]
    for copy in copies:
        copy.start()
    width = p0.shape[1]
    for j, piece in enumerate((p0, p1, p2, p3)):
        lhs[:, pl.ds(pl.multiple_of((tensor_at(meta) ^ j) * width, 128), width)] = piece[...]
    for k, (i, c, wide) in enumerate(blocks):
        at = starts[i] + c
        inside, whole_at = slice(c, c + wide), slice(at, at + wide)
        slope = slopes[i][:, inside] if slope_count == len(parts) else slopes[0][:, whole_at]
        copies[k].wait()
        value = jnp.dot(lhs[...], weight[k, :, 0:wide], preferred_element_type=F32)
        value = (value * slope).astype(BF)
        if len(outs) == len(parts):
            outs[i][:, inside] = value
        else:
            outs[0][:, whole_at] = value


def weight_kernel(count, meta, *refs):
    moved, kept = refs[:count], refs[count : 2 * count]
    act_moved, act_kept, *outs, lhs_moved, lhs_kept = refs[2 * count :]
    half = moved[0].shape[1] // 2
    mine = dp_at(meta) % 2 == 0
    for i in range(count):
        for piece, lhs in ((moved[i], lhs_moved), (kept[i], lhs_kept)):
            both = piece[...].T
            lo, hi = both[:half], both[half:]
            lhs[i * half : (i + 1) * half, :] = jnp.where(mine, hi, lo)
            lhs[(count + i) * half : (count + i + 1) * half, :] = jnp.where(mine, lo, hi)
    again_kernel(0, meta, lhs_moved, lhs_kept, act_moved, act_kept, *outs)


def again_kernel(base, meta, lhs_moved, lhs_kept, act_moved, act_kept, *outs):
    columns = slice(base, base + act_kept.shape[1])
    step = lhs_moved.shape[0] // 4
    at = 0
    for out in outs:
        for i in range(0, out.shape[0], step):
            part = slice(at, at + step)
            value = jnp.dot(lhs_moved[part, :], act_moved[:, columns], preferred_element_type=F32)
            value += jnp.dot(lhs_kept[part, :], act_kept[...], preferred_element_type=F32)
            out[i : i + step, :] = value.astype(out.dtype)
            at += step


def near_kernel(count, meta, *refs):
    keeps, gots, (out, mine) = refs[:count], refs[count : 2 * count], refs[2 * count :]
    half = out.shape[0] // 2
    parts = [(k, g, at) for k, g in zip(keeps, gots) for at in range(0, k.shape[0], half)]
    keeps_even = (dp_at(meta) // 2 + tensor_at(meta)) % 2 == 0
    step = 2 * TILE

    for pair in range(2):
        (k0, g0, a0), (k1, g1, a1) = parts[2 * pair], parts[2 * pair + 1]

        def body(i, _):
            def rows(at):
                return pl.ds(pl.multiple_of(at + i * step, TILE), step)

            even = k0[rows(a0), :] + g0[rows(a0), :].astype(F32)
            odd = k1[rows(a1), :] + g1[rows(a1), :].astype(F32)
            out[rows(pair * half), :] = jnp.where(keeps_even, odd, even).astype(BF)
            mine[rows(pair * half), :] = jnp.where(keeps_even, even, odd)
            return 0

        lax.fori_loop(0, half // step, body, 0)


def far_kernel(meta, held, got, out, mine):
    half = out.shape[0]
    keeps_first = (dp_at(meta) // 4 + tensor_at(meta) // 2) % 2 == 0
    step = 2 * TILE

    def body(i, _):
        first = pl.ds(pl.multiple_of(i * step, TILE), step)
        second = pl.ds(pl.multiple_of(half + i * step, TILE), step)
        a = held[first, :] + got[first, :].astype(F32)
        b = held[second, :] + got[second, :].astype(F32)
        out[first, :] = jnp.where(keeps_first, b, a).astype(BF)
        mine[first, :] = jnp.where(keeps_first, a, b)
        return 0

    lax.fori_loop(0, half // step, body, 0)


def place_kernel(cuts, meta, kept, *rest):
    moved, out = rest[:-1], rest[-1]
    count = kept_total(meta, dp_at(meta))
    first = jnp.minimum(count - lax.rem(count, TILE), BAL - SEND)
    first = pl.multiple_of(first, TILE)
    wide = out.shape[1]
    step = pl.program_id(0)
    out[0:KEEP, :] = kept[:, pl.ds(pl.multiple_of(step * wide, wide), wide)]
    out[KEEP:, :] = jnp.zeros((out.shape[0] - KEEP, wide), BF)
    rows = lax.broadcasted_iota(jnp.int32, (SEND, 1), 0) + first
    window = pl.ds(first, SEND)
    for i, (part, c, _) in enumerate(cut_at(cuts, wide)):

        @pl.when(step == i)
        def _():
            out[window, :] = jnp.where(rows < count, out[window, :], moved[part][:, c : c + wide])


def swapped(block, axis, distance):
    n = lax.axis_size(axis)
    return lax.ppermute(block, axis, [(i, i ^ distance) for i in range(n)])


def after(value, *others):
    return lax.optimization_barrier((value, *others))[0]


def shards(hidden_pre, cotangent, down_weight, layer_scale, crop_lengths, crop_moves):
    hidden_pre, cotangent, down_weight, layer_scale = (
        pltpu.with_memory_space_constraint(x, pltpu.HBM)
        for x in (hidden_pre, cotangent, down_weight, layer_scale)
    )
    home, ff = hidden_pre.shape
    width = cotangent.shape[1]
    features = down_weight.shape[0]
    half = width // 2
    part = ff // 3
    n = lax.axis_size("dp")
    d = lax.axis_index("dp").astype(jnp.int32)
    t = lax.axis_index("tensor").astype(jnp.int32)
    column = lax.broadcasted_iota(jnp.int32, (1, n), 1)
    own = jnp.where(column == 0, d, jnp.where(column == 1, t, 0))
    meta = jnp.concatenate([crop_lengths.T, crop_moves.T, own])
    vmem = pltpu.VMEM
    sems = pltpu.SemaphoreType.DMA

    def gelu(meta, moved, base, columns):
        block = 256
        rows = SEND if moved else KEEP
        count = pl.cdiv(columns, block)
        return kernel_call(
            functools.partial(gelu_kernel, moved, base, block),
            [shape(rows, columns), shape(rows, columns, F32)],
            [IN_HBM], [IN_VMEM] * 2,
            [vmem((rows, home), BF), vmem((rows, block), F32), vmem((count, home, block), BF), sems((count,))],
        )(meta, hidden_pre)

    def weight_first(meta, act_moved, act_kept):
        return kernel_call(
            functools.partial(weight_kernel, 4),
            [shape(width, part)] * 2 + [shape(width, part, F32)] * 2
            + [shape(features, SEND), shape(features, KEEP)],
            [IN_VMEM] * 10, [IN_VMEM] * 6,
        )(meta, *moved, *kept, act_moved, act_kept)

    def weight_again(meta, base, act_moved, act_kept, count):
        rows = features // 2 // count
        return kernel_call(
            functools.partial(again_kernel, base),
            [shape(rows, part)] * count + [shape(rows, part, F32)] * count,
            [IN_VMEM] * 4, [IN_VMEM] * (2 * count),
        )(meta, *lhs, act_moved, act_kept)

    def grads(meta, pieces, base, slopes, cuts):
        rows, block = pieces[0].shape[0], 256
        count = sum(cuts) // block
        return kernel_call(
            functools.partial(grad_kernel, base, len(slopes), block),
            [shape(rows, c) for c in cuts],
            [IN_VMEM] * 4 + [IN_HBM] + [IN_VMEM] * len(slopes), [IN_VMEM] * len(cuts),
            [vmem((rows, features), BF), vmem((count, features, block), BF), sems((count,))],
        )(meta, *pieces, down_weight, *slopes)

    def near_step(meta, keeps, gots):
        count = len(keeps)
        return kernel_call(
            functools.partial(near_kernel, count),
            [shape(width, part), shape(width, part, F32)], [IN_VMEM] * (2 * count), [IN_VMEM] * 2,
        )(meta, *keeps, *gots)

    def far_step(meta, mine, got):
        return kernel_call(
            far_kernel, [shape(half, part), shape(half, part, F32)], [IN_VMEM] * 2, [IN_VMEM] * 2
        )(meta, mine, got)

    moved_0, kept_0 = kernel_call(
        first_kernel, [shape(SEND, width), shape(KEEP, width)], [IN_HBM] * 2, [IN_VMEM] * 2,
        [vmem((home, width), BF), vmem((features,), F32), sems((2,))],
    )(meta, cotangent, layer_scale)

    moved_1, moved_2 = swapped(moved_0, "tensor", 1), swapped(moved_0, "tensor", 2)
    kept_1, kept_2 = swapped(kept_0, "tensor", 1), swapped(kept_0, "tensor", 2)
    act_ma, der_ma = gelu(after(meta, moved_0), True, 0, part)
    moved_2 = after(moved_2, act_ma, moved_1, kept_1)
    moved_3 = swapped(moved_2, "tensor", 1)
    moved = (moved_0, moved_1, moved_2, moved_3)

    (moving_a,) = grads(after(meta, moved_2), moved, 0, (der_ma,), (part,))
    arrived_a = swapped(moving_a, "dp", n // 2)

    act_ka, der_ka = gelu(after(meta, moving_a), False, 0, part)
    kept_2 = after(kept_2, act_ka)
    kept_3 = swapped(kept_2, "tensor", 1)
    kept = (kept_0, kept_1, kept_2, kept_3)
    *sends_a, keep_01, keep_23, lhs_moved, lhs_kept = weight_first(after(meta, act_ka), act_ma, act_ka)
    lhs = (lhs_moved, lhs_kept)
    gots_a = [swapped(send, "dp", 1) for send in sends_a]

    act_m, der_m = gelu(after(meta, keep_01), True, part, 2 * part)
    moving_b, moving_c = grads(after(meta, act_m), moved, part, (der_m,), (part, part))
    act_kb, der_kb = gelu(after(meta, moving_b), False, part, part)
    send_b, keep_b = weight_again(after(meta, act_kb, arrived_a), 0, act_m, act_kb, 1)
    got_b = swapped(send_b, "dp", 1)
    arrived_b = swapped(after(moving_b, send_b), "dp", n // 2)

    out_na, mine_a = near_step(after(meta, send_b), (keep_01, keep_23), gots_a)
    got_na = swapped(out_na, "dp", 2)
    act_kc, der_kc = gelu(after(meta, out_na), False, 2 * part, part)
    *sends_c, keep_c01, keep_c23 = weight_again(after(meta, act_kc), part, act_m, act_kc, 2)
    gots_c = [swapped(send, "dp", 1) for send in sends_c]
    (kept_grad,) = grads(after(meta, keep_c01), kept, 0, (der_ka, der_kb, der_kc), (ff,))

    out_nb, mine_b = near_step(after(meta, kept_grad, arrived_b, got_na), (keep_b,), (got_b,))
    got_nb = swapped(out_nb, "dp", 2)
    arrived_c = swapped(after(moving_c, out_nb), "dp", n // 2)
    out_fa, own_a = far_step(after(meta, out_nb), mine_a, got_na)
    got_fa = swapped(out_fa, "dp", 4)
    out_nc, mine_c = near_step(after(meta, out_fa), (keep_c01, keep_c23), gots_c)
    got_nc = swapped(out_nc, "dp", 2)
    out_fb, own_b = far_step(after(meta, out_nc), mine_b, got_nb)
    got_fb = swapped(out_fb, "dp", 4)
    out_fc, own_c = far_step(after(meta, out_fb, got_fa, arrived_c), mine_c, got_nc)
    got_fc = swapped(out_fc, "dp", 4)
    total = [a + b.astype(F32) for a, b in ((own_a, got_fa), (own_b, got_fb), (own_c, got_fc))]
    down_grad = jnp.concatenate(total, axis=1) / math.sqrt(n * home)

    hidden_grad = kernel_call(
        functools.partial(place_kernel, (part,) * 3), shape(BAL, ff), [IN_VMEM] * 4,
        pl.BlockSpec((BAL, 256), lambda i, *_: (0, i)), grid=(ff // 256,),
    )(after(meta, out_fc), kept_grad, arrived_a, arrived_b, arrived_c)
    return (hidden_grad, down_grad)


def solution(mesh):
    pairs_and_fours = (mesh.shape["dp"], mesh.shape["tensor"]) == (8, 4)
    return jax.shard_map(
        shards if pairs_and_fours else general_shards,
        mesh=mesh,
        in_specs=(P("dp", "tensor"), P("dp", "tensor"), P(None, "tensor"), P(), P(), P()),
        out_specs=(P("dp", "tensor"), P("dp", "tensor")),
        check_vma=False,
    )


def shifted(block, axis, distance):
    devices = range(lax.axis_size(axis))
    route = [((i - distance) % len(devices), i) for i in devices]
    return lax.ppermute(block, axis, route)


def crop_rows(row_total, crop_sizes, crop_starts):
    crop_ends = jnp.cumsum(crop_sizes)
    crop_begins = crop_ends - crop_sizes
    target_rows = jnp.arange(row_total, dtype=jnp.int32)[:, None]
    inside_crop = (target_rows >= crop_begins[None, :]) & (target_rows < crop_ends[None, :])
    source_rows = jnp.sum(
        jnp.where(inside_crop, crop_starts[None, :] + target_rows - crop_begins[None, :], 0), axis=1
    )
    return (source_rows, jnp.any(inside_crop, axis=1))


def select_rows(row_block, source_rows, valid_rows):
    taken = jnp.take(row_block, source_rows, axis=0)
    return jnp.where(valid_rows[:, None], taken, jnp.zeros((), row_block.dtype))


def gelu_parts(pre_act):
    cumulative = 0.5 * (1.0 + jax.scipy.special.erf(pre_act * inv_root_two))
    activated = pre_act * cumulative
    derivative = cumulative + pre_act * jnp.exp(-0.5 * pre_act * pre_act) * inv_root_tau
    return (activated, derivative)


def local_grads(pre_rows, cot_part, live_rows, layer_scale, down_weight, home_rows):
    cot_full = lax.all_gather(cot_part, "tensor", axis=1, tiled=True)
    scaled = (cot_full.astype(F32) * layer_scale[None, :]).astype(BF)
    activated, derivative = gelu_parts(pre_rows.astype(F32))
    activation = jnp.where(live_rows[:, None], activated, 0.0).astype(BF)
    backward = jnp.dot(scaled, down_weight, preferred_element_type=F32) * derivative
    gradient_rows = jnp.where(live_rows[:, None], backward, 0.0).astype(BF)
    weight_grad = lax.psum_scatter(
        lax.dot_general(scaled, activation, (((0,), (0,)), ((), ())), preferred_element_type=F32),
        "dp",
        scatter_dimension=0,
        tiled=True,
    )
    return (gradient_rows, weight_grad / math.sqrt(lax.axis_size("dp") * home_rows))


def general_shards(hidden_pre, cotangent, down_weight, layer_scale, crop_lengths, crop_moves):
    devices = lax.axis_size("dp")
    half_axis = devices // 2
    device_index = lax.axis_index("dp")
    partner_index = (device_index + half_axis) % devices
    own_lengths = lax.dynamic_index_in_dim(crop_lengths, device_index, 0, keepdims=False)
    own_moves = lax.dynamic_index_in_dim(crop_moves, device_index, 0, keepdims=False)
    partner_lengths = lax.dynamic_index_in_dim(crop_lengths, partner_index, 0, keepdims=False)
    partner_moves = lax.dynamic_index_in_dim(crop_moves, partner_index, 0, keepdims=False)
    home_rows = hidden_pre.shape[0]
    own_starts = jnp.cumsum(own_lengths) - own_lengths
    sent_sizes = own_lengths * own_moves
    kept_sizes = own_lengths * (1 - own_moves)
    arrived = jnp.sum(partner_lengths * partner_moves)
    send_source, send_valid = crop_rows(SEND, sent_sizes, own_starts)
    keep_sizes = jnp.concatenate([kept_sizes, arrived[None]])
    keep_starts = jnp.concatenate([own_starts, jnp.full((1,), home_rows, jnp.int32)])
    keep_source, keep_valid = crop_rows(BAL, keep_sizes, keep_starts)
    live_home = jnp.arange(home_rows, dtype=jnp.int32) < jnp.sum(own_lengths)
    gradient_rows, weight_grad = local_grads(
        hidden_pre, cotangent, live_home, layer_scale, down_weight, home_rows
    )
    outgoing = select_rows(gradient_rows, send_source, send_valid)
    incoming = shifted(outgoing, "dp", half_axis)
    balanced = select_rows(jnp.concatenate([gradient_rows, incoming], 0), keep_source, keep_valid)
    return (balanced, weight_grad)
```

time: 134 us -> 140 us (1.045)
  starting transfers between devices: 18.5 us -> 22.8 us
  waiting for transfers between devices: 48.7 us -> 51.3 us
    ppermute x23 -> x20, starting transfers between devices: 18.5 us -> 22.8 us  [swapped(): return lax.ppermute(block, axis, [(i, i ^ distance) for i in range(n)])]
    ppermute x23 -> x20, waiting for transfers between devices: 48.7 us -> 51.3 us  [swapped(): return lax.ppermute(block, axis, [(i, i ^ distance) for i in range(n)])]
    pallas_call x22 -> x19, Pallas kernels: 63.2 us -> 62.7 us  [the longest x5 22.9 us: gelu(): kernel_call(functools.partial(gelu_kernel, moved, base, block), [shape(ro...]
  transfers between devices with their start and end apart: 23 -> 20, of which waited for: 13 -> 7; matrix products, arithmetic and copies ran while one was open for 0% -> 0% of each run, Pallas kernels for 44% -> 42%
where the time goes in v12:
time: 140 us
  Pallas kernels  62.7 us (45%)
  waiting for transfers between devices  51.3 us (37%)
  starting transfers between devices  22.8 us (16%)
  other arithmetic  1.99 us (1%)
    ppermute x20, waiting for transfers between devices, swapped(): return lax.ppermute(block, axis, [(i, i ^ distance) for i in range(n)])  51.3 us
    pallas_call x5, Pallas kernels, gelu(): kernel_call(functools.partial(gelu_kernel, moved, base, block), [shape(ro...  22.9 us
    ppermute x20, starting transfers between devices, swapped(): return lax.ppermute(block, axis, [(i, i ^ distance) for i in range(n)])  22.8 us
    pallas_call x3, Pallas kernels, grads(): kernel_call(functools.partial(grad_kernel, base, len(slopes), block), [sh...  17.7 us
    pallas_call x2, Pallas kernels, weight_again(): kernel_call(functools.partial(again_kernel, base), [shape(rows, part)] *...  6.51 us
    pallas_call x1, Pallas kernels, shards(): kernel_call(first_kernel, [shape(SEND, width), shape(KEEP, width)], [IN_H...  3.42 us
    pallas_call x1, Pallas kernels, weight_first(): kernel_call(functools.partial(weight_kernel, 4), [shape(width, part)] * 2...  3.37 us
    pallas_call x1, Pallas kernels, shards(): kernel_call(functools.partial(place_kernel, (part,) * 3), shape(BAL, ff),...  3.34 us
  transfers between devices with their start and end apart: 20, of which 7 were waited for; matrix products, arithmetic and copies ran while one was open for 0% of the time, Pallas kernels for 42%

profile of v12, /device:TPU:0, one launch (start us, length us, event | category | flops | bytes accessed | tf_op | source)
XLA Modules:
  0.0 139.8 jit_solution(3231285628741635443)
XLA Ops:
  1.4 3.4 %shard_map.77 = (bf16[528,384]{1,0:T(8,128)(2,1)S(1)}, bf16[528,384]{1,0:T(8,128)(2,1)S(1)}) custom-call(s32[9,8]{1,0:T(8,128)S(1)} %pad_add_fusion.meta, bf16[1032,384]{1,0:T(8,128)(2,1)} %cot_hbm.1, f32[1536]{0:T(1024)} %scale_hbm.1), custom_call_target="tpu_custom_call" | custom-call | flops 1 | bytes 1 | tf_op jit(solution)/shard_map/pallas_call | solution.py:345
  5.4 3.0 %collective-permute-start = (bf16[528,384]{1,0:T(8,128)(2,1)S(1)}, bf16[528,384]{1,0:T(8,128)(2,1)S(1)}, u32[]{:S(2)}, u32[]{:S(2)}) collective-permute-start(bf16[528,384]{1,0:T(8,128)(2,1)S(1)} %get-tuple-element.62.p0.refs_0_), channel_id=1, source_target_pairs={{0,2},{1,3},{2,0},{3,1},{4,6},{5,7},{6,4},{7,5},{8,10},{9,11},{10,... | collective-permute-start | bytes 1216520 | tf_op jit(solution)/shard_map/ppermute | solution.py:270
  8.3 4.3 %shard_map.78 = (bf16[528,512]{1,0:T(8,128)(2,1)S(1)}, f32[528,512]{1,0:T(8,128)S(1)}) custom-call(s32[9,8]{1,0:T(8,128)S(1)} %pad_add_fusion.meta, bf16[1032,1536]{1,0:T(8,128)(2,1)} %pre_hbm.9), custom_call_target="tpu_custom_call" | custom-call | flops 1 | bytes 1 | tf_op jit(solution)/shard_map/pallas_call | solution.py:300
  12.6 5.3 %collective-permute-done.p2.refs_2_ = bf16[528,384]{1,0:T(8,128)(2,1)S(1)} collective-permute-done((bf16[528,384]{1,0:T(8,128)(2,1)S(1)}, bf16[528,384]{1,0:T(8,128)(2,1)S(1)}, u32[]{:S(2)}, u32[]{:S(2)}) %collective-permute-start) | collective-permute-done | bytes 405536 | tf_op jit(solution)/shard_map/ppermute | solution.py:270
  18.0 1.7 %collective-permute-start.4 = (bf16[528,384]{1,0:T(8,128)(2,1)S(1)}, bf16[528,384]{1,0:T(8,128)(2,1)S(1)}, u32[]{:S(2)}, u32[]{:S(2)}) collective-permute-start(bf16[528,384]{1,0:T(8,128)(2,1)S(1)} %get-tuple-element.65.refs_4_.p0), channel_id=1, source_target_pairs={{0,2},{1,3},{2,0},{3,1},{4,6},{5,7},{6,4},{7,5},{8,10},{9,11},{10,... | collective-permute-start | bytes 1216520 | tf_op jit(solution)/shard_map/ppermute | solution.py:270
  19.7 3.9 %shard_map.79 = bf16[528,512]{1,0:T(8,128)(2,1)S(1)} custom-call(s32[9,8]{1,0:T(8,128)S(1)} %pad_add_fusion.meta, bf16[528,384]{1,0:T(8,128)(2,1)S(1)} %get-tuple-element.62.p0.refs_0_, bf16[528,384]{1,0:T(8,128)(2,1)S(1)} %collective-permute-done.1.p1.refs_1_, bf16[528,384]{1,0:T(8,128)(2,1)S(1)} %collective-permute-done.p2.refs_2_, ...), custom_call_target="tpu_custom_call" | custom-call | flops 1 | bytes 1 | tf_op jit(solution)/shard_map/pallas_call | solution.py:326
  23.6 2.9 %collective-permute-start.6 = (bf16[528,512]{1,0:T(8,128)(2,1)S(1)}, bf16[528,512]{1,0:T(8,128)(2,1)S(1)}, u32[]{:S(2)}, u32[]{:S(2)}) collective-permute-start(bf16[528,512]{1,0:T(8,128)(2,1)S(1)} %shard_map.79), channel_id=1, source_target_pairs={{0,16},{4,20},{8,24},{12,28},{16,0},{20,4},{24,8},{28,12},{1,17},{... | collective-permute-start | bytes 1622024 | tf_op jit(solution)/shard_map/ppermute | solution.py:270
  26.5 4.1 %shard_map.80 = (bf16[528,512]{1,0:T(8,128)(2,1)S(1)}, f32[528,512]{1,0:T(8,128)S(1)}) custom-call(s32[9,8]{1,0:T(8,128)S(1)} %pad_add_fusion.meta, bf16[1032,1536]{1,0:T(8,128)(2,1)} %pre_hbm.9), custom_call_target="tpu_custom_call" | custom-call | flops 1 | bytes 1 | tf_op jit(solution)/shard_map/pallas_call | solution.py:300
  32.4 3.4 %shard_map.81 = (bf16[384,512]{1,0:T(8,128)(2,1)S(1)}, bf16[384,512]{1,0:T(8,128)(2,1)S(1)}, f32[384,512]{1,0:T(8,128)S(1)}, f32[384,512]{1,0:T(8,128)S(1)}, bf1...) custom-call(s32[9,8]{1,0:T(8,128)S(1)} %pad_add_fusion.meta, ...), custom_call_target="tpu_custom_call" | custom-call | flops 1 | bytes 1 | tf_op jit(solution)/shard_map/pallas_call | solution.py:308
  37.9 6.4 %shard_map.82 = (bf16[528,1024]{1,0:T(8,128)(2,1)S(1)}, f32[528,1024]{1,0:T(8,128)S(1)}) custom-call(s32[9,8]{1,0:T(8,128)S(1)} %pad_add_fusion.meta, bf16[1032,1536]{1,0:T(8,128)(2,1)} %pre_hbm.9), custom_call_target="tpu_custom_call" | custom-call | flops 1 | bytes 1 | tf_op jit(solution)/shard_map/pallas_call | solution.py:300
  44.3 5.9 %shard_map.83 = (bf16[528,512]{1,0:T(8,128)(2,1)S(1)}, bf16[528,512]{1,0:T(8,128)(2,1)S(1)}) custom-call(s32[9,8]{1,0:T(8,128)S(1)} %pad_add_fusion.meta, bf16[528,384]{1,0:T(8,128)(2,1)S(1)} %get-tuple-element.62.p0.refs_0_, bf16[528,384]{1,0:T(8,128)(2,1)S(1)} %collective-permute-done.1.p1.refs_1_, bf16[528,384]{1,0:T(8,128)(2,1)S(1)} %collective-permute-done.p2.refs_2_, ...), custom_call_target="tpu_custom_call" | custom-call | flops 1 | bytes 1 | tf_op jit(solution)/shard_map/pallas_call | solution.py:326
  50.2 4.1 %shard_map.84 = (bf16[528,512]{1,0:T(8,128)(2,1)S(1)}, f32[528,512]{1,0:T(8,128)S(1)}) custom-call(s32[9,8]{1,0:T(8,128)S(1)} %pad_add_fusion.meta, bf16[1032,1536]{1,0:T(8,128)(2,1)} %pre_hbm.9), custom_call_target="tpu_custom_call" | custom-call | flops 1 | bytes 1 | tf_op jit(solution)/shard_map/pallas_call | solution.py:300
  54.3 3.3 %shard_map.85 = (bf16[768,512]{1,0:T(8,128)(2,1)S(1)}, f32[768,512]{1,0:T(8,128)S(1)}) custom-call(s32[9,8]{1,0:T(8,128)S(1)} %pad_add_fusion.meta, bf16[1536,528]{1,0:T(8,128)(2,1)S(1)} %get-tuple-element.82.lhs_moved, bf16[1536,528]{1,0:T(8,128)(2,1)S(1)} %get-tuple-element.83.lhs_kept, bf16[528,1024]{1,0:T(8,128)(2,1)S(1)} %get-tuple-element.75.act_moved, ...), custom_call_target="tpu_custom_call" | custom-call | flops 1 | bytes 1 | tf_op jit(solution)/shard_map/pallas_call | solution.py:317
  59.2 1.9 %collective-permute-start.9 = (bf16[528,512]{1,0:T(8,128)(2,1)S(1)}, bf16[528,512]{1,0:T(8,128)(2,1)S(1)}, u32[]{:S(2)}, u32[]{:S(2)}) collective-permute-start(bf16[528,512]{1,0:T(8,128)(2,1)S(1)} %get-tuple-element.98), channel_id=1, source_target_pairs={{0,16},{4,20},{8,24},{12,28},{16,0},{20,4},{24,8},{28,12},{1,17},{... | collective-permute-start | bytes 1622024 | tf_op jit(solution)/shard_map/ppermute | solution.py:270
  63.9 4.1 %shard_map.87 = (bf16[528,512]{1,0:T(8,128)(2,1)S(1)}, f32[528,512]{1,0:T(8,128)S(1)}) custom-call(s32[9,8]{1,0:T(8,128)S(1)} %pad_add_fusion.meta, bf16[1032,1536]{1,0:T(8,128)(2,1)} %pre_hbm.9), custom_call_target="tpu_custom_call" | custom-call | flops 1 | bytes 1 | tf_op jit(solution)/shard_map/pallas_call | solution.py:300
  67.9 3.3 %shard_map.88 = (bf16[384,512]{1,0:T(8,128)(2,1)S(1)}, bf16[384,512]{1,0:T(8,128)(2,1)S(1)}, f32[384,512]{1,0:T(8,128)S(1)}, f32[384,512]{1,0:T(8,128)S(1)}) custom-call(s32[9,8]{1,0:T(8,128)S(1)} %pad_add_fusion.meta, bf16[1536,528]{1,0:T(8,128)(2,1)S(1)} %get-tuple-element.82.lhs_moved, bf16[1536,528]{1,0:T(8,128)(2,1)S(1)} %get-tuple-element.83.lhs_kept, ...), custom_call_target="tpu_custom_call" | custom-call | flops 1 | bytes 1 | tf_op jit(solution)/shard_map/pallas_call | solution.py:317
  73.3 7.9 %shard_map.89.kept = bf16[528,1536]{1,0:T(8,128)(2,1)S(1)} custom-call(s32[9,8]{1,0:T(8,128)S(1)} %pad_add_fusion.meta, bf16[528,384]{1,0:T(8,128)(2,1)S(1)} %get-tuple-element.65.refs_4_.p0, bf16[528,384]{1,0:T(8,128)(2,1)S(1)} %collective-permute-done.2.refs_5_.p1, bf16[528,384]{1,0:T(8,128)(2,1)S(1)} %collective-permute-done.4.refs_6_.p2, ...), custom_call_target="tpu_custom_call" | custom-call | flops 1 | bytes 1 | tf_op jit(solution)/shard_map/pallas_call | solution.py:326
  81.2 3.8 %collective-permute-done.9.rest_1_ = bf16[528,512]{1,0:T(8,128)(2,1)S(1)} collective-permute-done((bf16[528,512]{1,0:T(8,128)(2,1)S(1)}, bf16[528,512]{1,0:T(8,128)(2,1)S(1)}, u32[]{:S(2)}, u32[]{:S(2)}) %collective-permute-start.9) | collective-permute-done | bytes 540704 | tf_op jit(solution)/shard_map/ppermute | solution.py:270
  86.1 3.4 %collective-permute-start.16 = (bf16[528,512]{1,0:T(8,128)(2,1)S(1)}, bf16[528,512]{1,0:T(8,128)(2,1)S(1)}, u32[]{:S(2)}, u32[]{:S(2)}) collective-permute-start(bf16[528,512]{1,0:T(8,128)(2,1)S(1)} %get-tuple-element.114), channel_id=1, source_target_pairs={{0,16},{4,20},{8,24},{12,28},{16,0},{20,4},{24,8},{28,12},{1,17},{... | collective-permute-start | bytes 1622024 | tf_op jit(solution)/shard_map/ppermute | solution.py:270
  90.4 3.1 %collective-permute-done.13.refs_3_ = bf16[384,512]{1,0:T(8,128)(2,1)S(1)} collective-permute-done((bf16[384,512]{1,0:T(8,128)(2,1)S(1)}, bf16[384,512]{1,0:T(8,128)(2,1)S(1)}, u32[]{:S(2)}, u32[]{:S(2)}) %collective-permute-start.13) | collective-permute-done | bytes 393248 | tf_op jit(solution)/shard_map/ppermute | solution.py:270
  96.1 10.3 %collective-permute-done.14.got = bf16[384,512]{1,0:T(8,128)(2,1)S(1)} collective-permute-done((bf16[384,512]{1,0:T(8,128)(2,1)S(1)}, bf16[384,512]{1,0:T(8,128)(2,1)S(1)}, u32[]{:S(2)}, u32[]{:S(2)}) %collective-permute-start.14) | collective-permute-done | bytes 393248 | tf_op jit(solution)/shard_map/ppermute | solution.py:270
  107.2 21.7 %collective-permute-done.15 = bf16[192,512]{1,0:T(8,128)(2,1)S(1)} collective-permute-done((bf16[192,512]{1,0:T(8,128)(2,1)S(1)}, bf16[192,512]{1,0:T(8,128)(2,1)S(1)}, u32[]{:S(2)}, u32[]{:S(2)}) %collective-permute-start.15) | collective-permute-done | bytes 196640 | tf_op jit(solution)/shard_map/ppermute | solution.py:270
  129.9 3.3 %shard_map.95 = bf16[720,1536]{1,0:T(8,128)(2,1)} custom-call(s32[9,8]{1,0:T(8,128)S(1)} %pad_add_fusion.meta, bf16[528,1536]{1,0:T(8,128)(2,1)S(1)} %shard_map.89.kept, bf16[528,512]{1,0:T(8,128)(2,1)S(1)} %collective-permute-done.6.rest_0_, bf16[528,512]{1,0:T(8,128)(2,1)S(1)} %collective-permute-done.9.rest_1_, ...), custom_call_target="tpu_custom_call" | custom-call | flops 1 | bytes 1 | tf_op jit(solution)/shard_map/pallas_call | solution.py:396
  133.3 5.2 %collective-permute-done.19 = bf16[192,512]{1,0:T(8,128)(2,1)S(1)} collective-permute-done((bf16[192,512]{1,0:T(8,128)(2,1)S(1)}, bf16[192,512]{1,0:T(8,128)(2,1)S(1)}, u32[]{:S(2)}, u32[]{:S(2)}) %collective-permute-start.19) | collective-permute-done | bytes 196640 | tf_op jit(solution)/shard_map/ppermute | solution.py:270
  (41 shorter events, 19.1 us)
Async XLA Ops:
  4.8 7.8 %collective-permute-start.2 = (bf16[528,384]{1,0:T(8,128)(2,1)S(1)}, bf16[528,384]{1,0:T(8,128)(2,1)S(1)}, u32[]{:S(2)}, u32[]{:S(2)}) collective-permute-start(bf16[528,384]{1,0:T(8,128)(2,1)S(1)} %get-tuple-element.65.refs_4_.p0), channel_id=1, source_target_pairs={{0,1},{1,0},{2,3},{3,2},{4,5},{5,4},{6,7},{7,6},{8,9},{9,8},{10,11... | collective-permute-start | bytes 1216520 | tf_op jit(solution)/shard_map/ppermute | solution.py:270
  5.3 7.3 %collective-permute-start.1 = (bf16[528,384]{1,0:T(8,128)(2,1)S(1)}, bf16[528,384]{1,0:T(8,128)(2,1)S(1)}, u32[]{:S(2)}, u32[]{:S(2)}) collective-permute-start(bf16[528,384]{1,0:T(8,128)(2,1)S(1)} %get-tuple-element.62.p0.refs_0_), channel_id=1, source_target_pairs={{0,1},{1,0},{2,3},{3,2},{4,5},{5,4},{6,7},{7,6},{8,9},{9,8},{10,11... | collective-permute-start | bytes 1216520 | tf_op jit(solution)/shard_map/ppermute | solution.py:270
  5.4 12.6 %collective-permute-start = (bf16[528,384]{1,0:T(8,128)(2,1)S(1)}, bf16[528,384]{1,0:T(8,128)(2,1)S(1)}, u32[]{:S(2)}, u32[]{:S(2)}) collective-permute-start(bf16[528,384]{1,0:T(8,128)(2,1)S(1)} %get-tuple-element.62.p0.refs_0_), channel_id=1, source_target_pairs={{0,2},{1,3},{2,0},{3,1},{4,6},{5,7},{6,4},{7,5},{8,10},{9,11},{10,... | collective-permute-start | bytes 1216520 | tf_op jit(solution)/shard_map/ppermute | solution.py:270
  17.9 1.8 %collective-permute-start.3 = (bf16[528,384]{1,0:T(8,128)(2,1)S(1)}, bf16[528,384]{1,0:T(8,128)(2,1)S(1)}, u32[]{:S(2)}, u32[]{:S(2)}) collective-permute-start(bf16[528,384]{1,0:T(8,128)(2,1)S(1)} %collective-permute-done.p2.refs_2_), channel_id=1, source_target_pairs={{0,1},{1,0},{2,3},{3,2},{4,5},{5,4},{6,7},{7,6},{8,9},{9,8},{10,11... | collective-permute-start | bytes 1216520 | tf_op jit(solution)/shard_map/ppermute | solution.py:270
  18.0 12.6 %collective-permute-start.4 = (bf16[528,384]{1,0:T(8,128)(2,1)S(1)}, bf16[528,384]{1,0:T(8,128)(2,1)S(1)}, u32[]{:S(2)}, u32[]{:S(2)}) collective-permute-start(bf16[528,384]{1,0:T(8,128)(2,1)S(1)} %get-tuple-element.65.refs_4_.p0), channel_id=1, source_target_pairs={{0,2},{1,3},{2,0},{3,1},{4,6},{5,7},{6,4},{7,5},{8,10},{9,11},{10,... | collective-permute-start | bytes 1216520 | tf_op jit(solution)/shard_map/ppermute | solution.py:270
  23.6 30.7 %collective-permute-start.6 = (bf16[528,512]{1,0:T(8,128)(2,1)S(1)}, bf16[528,512]{1,0:T(8,128)(2,1)S(1)}, u32[]{:S(2)}, u32[]{:S(2)}) collective-permute-start(bf16[528,512]{1,0:T(8,128)(2,1)S(1)} %shard_map.79), channel_id=1, source_target_pairs={{0,16},{4,20},{8,24},{12,28},{16,0},{20,4},{24,8},{28,12},{1,17},{... | collective-permute-start | bytes 1622024 | tf_op jit(solution)/shard_map/ppermute | solution.py:270
  30.6 1.8 %collective-permute-start.5 = (bf16[528,384]{1,0:T(8,128)(2,1)S(1)}, bf16[528,384]{1,0:T(8,128)(2,1)S(1)}, u32[]{:S(2)}, u32[]{:S(2)}) collective-permute-start(bf16[528,384]{1,0:T(8,128)(2,1)S(1)} %collective-permute-done.4.refs_6_.p2), channel_id=1, source_target_pairs={{0,1},{1,0},{2,3},{3,2},{4,5},{5,4},{6,7},{7,6},{8,9},{9,8},{10,11... | collective-permute-start | bytes 1216520 | tf_op jit(solution)/shard_map/ppermute | solution.py:270
  35.8 25.3 %collective-permute-start.7 = (bf16[384,512]{1,0:T(8,128)(2,1)S(1)}, bf16[384,512]{1,0:T(8,128)(2,1)S(1)}, u32[]{:S(2)}, u32[]{:S(2)}) collective-permute-start(bf16[384,512]{1,0:T(8,128)(2,1)S(1)} %get-tuple-element.87), channel_id=1, source_target_pairs={{0,4},{4,0},{8,12},{12,8},{16,20},{20,16},{24,28},{28,24},{1,5},{5... | collective-permute-start | bytes 1179656 | tf_op jit(solution)/shard_map/ppermute | solution.py:270
  37.3 23.7 %collective-permute-start.8 = (bf16[384,512]{1,0:T(8,128)(2,1)S(1)}, bf16[384,512]{1,0:T(8,128)(2,1)S(1)}, u32[]{:S(2)}, u32[]{:S(2)}) collective-permute-start(bf16[384,512]{1,0:T(8,128)(2,1)S(1)} %get-tuple-element.88), channel_id=1, source_target_pairs={{0,4},{4,0},{8,12},{12,8},{16,20},{20,16},{24,28},{28,24},{1,5},{5... | collective-permute-start | bytes 1179656 | tf_op jit(solution)/shard_map/ppermute | solution.py:270
  57.6 27.5 %collective-permute-start.11 = (bf16[768,512]{1,0:T(8,128)(2,1)S(1)}, bf16[768,512]{1,0:T(8,128)(2,1)S(1)}, u32[]{:S(2)}, u32[]{:S(2)}) collective-permute-start(bf16[768,512]{1,0:T(8,128)(2,1)S(1)} %get-tuple-element.84), channel_id=1, source_target_pairs={{0,4},{4,0},{8,12},{12,8},{16,20},{20,16},{24,28},{28,24},{1,5},{5... | collective-permute-start | bytes 2359304 | tf_op jit(solution)/shard_map/ppermute | solution.py:270
  59.2 25.9 %collective-permute-start.9 = (bf16[528,512]{1,0:T(8,128)(2,1)S(1)}, bf16[528,512]{1,0:T(8,128)(2,1)S(1)}, u32[]{:S(2)}, u32[]{:S(2)}) collective-permute-start(bf16[528,512]{1,0:T(8,128)(2,1)S(1)} %get-tuple-element.98), channel_id=1, source_target_pairs={{0,16},{4,20},{8,24},{12,28},{16,0},{20,4},{24,8},{28,12},{1,17},{... | collective-permute-start | bytes 1622024 | tf_op jit(solution)/shard_map/ppermute | solution.py:270
  62.2 22.9 %collective-permute-start.10 = (bf16[384,512]{1,0:T(8,128)(2,1)S(1)}, bf16[384,512]{1,0:T(8,128)(2,1)S(1)}, u32[]{:S(2)}, u32[]{:S(2)}) collective-permute-start(bf16[384,512]{1,0:T(8,128)(2,1)S(1)} %get-tuple-element.89), channel_id=1, source_target_pairs={{0,8},{4,12},{8,0},{12,4},{16,24},{20,28},{24,16},{28,20},{1,9},{5... | collective-permute-start | bytes 1179656 | tf_op jit(solution)/shard_map/ppermute | solution.py:270
  71.2 19.2 %collective-permute-start.12 = (bf16[384,512]{1,0:T(8,128)(2,1)S(1)}, bf16[384,512]{1,0:T(8,128)(2,1)S(1)}, u32[]{:S(2)}, u32[]{:S(2)}) collective-permute-start(bf16[384,512]{1,0:T(8,128)(2,1)S(1)} %get-tuple-element.107), channel_id=1, source_target_pairs={{0,4},{4,0},{8,12},{12,8},{16,20},{20,16},{24,28},{28,24},{1,5},{5... | collective-permute-start | bytes 1179656 | tf_op jit(solution)/shard_map/ppermute | solution.py:270
  71.8 21.7 %collective-permute-start.13 = (bf16[384,512]{1,0:T(8,128)(2,1)S(1)}, bf16[384,512]{1,0:T(8,128)(2,1)S(1)}, u32[]{:S(2)}, u32[]{:S(2)}) collective-permute-start(bf16[384,512]{1,0:T(8,128)(2,1)S(1)} %get-tuple-element.108), channel_id=1, source_target_pairs={{0,4},{4,0},{8,12},{12,8},{16,20},{20,16},{24,28},{28,24},{1,5},{5... | collective-permute-start | bytes 1179656 | tf_op jit(solution)/shard_map/ppermute | solution.py:270
  86.0 20.3 %collective-permute-start.14 = (bf16[384,512]{1,0:T(8,128)(2,1)S(1)}, bf16[384,512]{1,0:T(8,128)(2,1)S(1)}, u32[]{:S(2)}, u32[]{:S(2)}) collective-permute-start(bf16[384,512]{1,0:T(8,128)(2,1)S(1)} %get-tuple-element.101), channel_id=1, source_target_pairs={{0,8},{4,12},{8,0},{12,4},{16,24},{20,28},{24,16},{28,20},{1,9},{5... | collective-permute-start | bytes 1179656 | tf_op jit(solution)/shard_map/ppermute | solution.py:270
  86.1 42.9 %collective-permute-start.16 = (bf16[528,512]{1,0:T(8,128)(2,1)S(1)}, bf16[528,512]{1,0:T(8,128)(2,1)S(1)}, u32[]{:S(2)}, u32[]{:S(2)}) collective-permute-start(bf16[528,512]{1,0:T(8,128)(2,1)S(1)} %get-tuple-element.114), channel_id=1, source_target_pairs={{0,16},{4,20},{8,24},{12,28},{16,0},{20,4},{24,8},{28,12},{1,17},{... | collective-permute-start | bytes 1622024 | tf_op jit(solution)/shard_map/ppermute | solution.py:270
  90.3 38.7 %collective-permute-start.15 = (bf16[192,512]{1,0:T(8,128)(2,1)S(1)}, bf16[192,512]{1,0:T(8,128)(2,1)S(1)}, u32[]{:S(2)}, u32[]{:S(2)}) collective-permute-start(bf16[192,512]{1,0:T(8,128)(2,1)S(1)} %get-tuple-element.104), channel_id=1, source_target_pairs={{0,16},{4,20},{8,24},{12,28},{16,0},{20,4},{24,8},{28,12},{1,17},{... | collective-permute-start | bytes 589832 | tf_op jit(solution)/shard_map/ppermute | solution.py:270
  94.5 34.6 %collective-permute-start.17 = (bf16[384,512]{1,0:T(8,128)(2,1)S(1)}, bf16[384,512]{1,0:T(8,128)(2,1)S(1)}, u32[]{:S(2)}, u32[]{:S(2)}) collective-permute-start(bf16[384,512]{1,0:T(8,128)(2,1)S(1)} %get-tuple-element.109), channel_id=1, source_target_pairs={{0,8},{4,12},{8,0},{12,4},{16,24},{20,28},{24,16},{28,20},{1,9},{5... | collective-permute-start | bytes 1179656 | tf_op jit(solution)/shard_map/ppermute | solution.py:270
  107.2 26.1 %collective-permute-start.18 = (bf16[192,512]{1,0:T(8,128)(2,1)S(1)}, bf16[192,512]{1,0:T(8,128)(2,1)S(1)}, u32[]{:S(2)}, u32[]{:S(2)}) collective-permute-start(bf16[192,512]{1,0:T(8,128)(2,1)S(1)} %get-tuple-element.112), channel_id=1, source_target_pairs={{0,16},{4,20},{8,24},{12,28},{16,0},{20,4},{24,8},{28,12},{1,17},{... | collective-permute-start | bytes 589832 | tf_op jit(solution)/shard_map/ppermute | solution.py:270
  129.9 8.7 %collective-permute-start.19 = (bf16[192,512]{1,0:T(8,128)(2,1)S(1)}, bf16[192,512]{1,0:T(8,128)(2,1)S(1)}, u32[]{:S(2)}, u32[]{:S(2)}) collective-permute-start(bf16[192,512]{1,0:T(8,128)(2,1)S(1)} %get-tuple-element.117), channel_id=1, source_target_pairs={{0,16},{4,20},{8,24},{12,28},{16,0},{20,4},{24,8},{28,12},{1,17},{... | collective-permute-start | bytes 589832 | tf_op jit(solution)/shard_map/ppermute | solution.py:270

commit v13 on v11

--- a/solution.py
+++ b/solution.py
@@ -107,20 +107,27 @@
     return (rows * own[None, :]).astype(BF)
 
 
-def first_kernel(meta, cot_hbm, scale_hbm, pre_hbm, late_out, rest_out, early_out, cot, scale, pre, sems):
+def first_kernel(
+    meta, cot_hbm, scale_hbm, pre_hbm, late_out, rest_out, early_out, late_pick, rest_pick, pre, cot, scale, sems
+):
     home, width = cot.shape
     pairs = ((cot_hbm, cot), (scale_hbm, scale), (pre_hbm, pre))
     copies = [pltpu.make_async_copy(a, b, sems.at[i]) for i, (a, b) in enumerate(pairs)]
     for copy in copies:
         copy.start()
     early = early_picks(meta, home)
+    late = late_picks(meta, home)
+    kept = kept_picks(meta, home)
+    late_pick[...] = late
+    rest_pick[0:EARLY, :] = early
+    rest_pick[EARLY:, :] = kept
     copies[0].wait()
     copies[1].wait()
     early_rows = scaled_rows(meta, early, cot, scale)
     early_out[:, :width] = early_rows
-    late_out[...] = scaled_rows(meta, late_picks(meta, home), cot, scale)
+    late_out[...] = scaled_rows(meta, late, cot, scale)
     rest_out[0:EARLY, :] = early_rows
-    rest_out[EARLY:, :] = scaled_rows(meta, kept_picks(meta, home), cot, scale)
+    rest_out[EARLY:, :] = scaled_rows(meta, kept, cot, scale)
     copies[2].wait()
     early_out[:, width:] = jnp.dot(early, pre[...], preferred_element_type=F32).astype(BF)
 
@@ -136,34 +143,19 @@
     ]
 
 
-def gelu_kernel(late, base, block, meta, pre_hbm, act_out, der_out, pick, rows_f32, pre, sems):
-    home = pre.shape[1]
+def gelu_kernel(base, block, meta, pick, pre, act_out, der_out, rows_f32):
     rows = pick.shape[0]
-    blocks = cut_at((act_out.shape[1],), block)
-    copies = [
-        pltpu.make_async_copy(
-            pre_hbm.at[:, pl.ds(base + at, wide)], pre.at[i, :, pl.ds(0, wide)], sems.at[i]
-        )
-        for i, (_, at, wide) in enumerate(blocks)
-    ]
-    for copy in copies:
-        copy.start()
-    if late:
-        pick[...] = late_picks(meta, home)
-    else:
-        pick[0:EARLY, :] = early_picks(meta, home)
-        pick[EARLY:, :] = kept_picks(meta, home)
     step = next(TILE * k for k in (3, 4, 2, 1) if rows % (TILE * k) == 0)
-    for i, (_, at, wide) in enumerate(blocks):
-        copies[i].wait()
-        rows_f32[:, 0:wide] = jnp.dot(pick[...], pre[i, :, 0:wide], preferred_element_type=F32)
-        columns = slice(at, at + wide)
+    for at in range(0, act_out.shape[1], block):
+        source = slice(base + at, base + at + block)
+        rows_f32[...] = jnp.dot(pick[...], pre[:, source], preferred_element_type=F32)
+        columns = slice(at, at + block)
 
         def body(k, _):
-            rows = pl.ds(pl.multiple_of(k * step, step), step)
-            value, slope = gelu_and_slope(rows_f32[rows, 0:wide])
-            act_out[rows, columns] = value.astype(BF)
-            der_out[rows, columns] = slope
+            part = pl.ds(pl.multiple_of(k * step, step), step)
+            value, slope = gelu_and_slope(rows_f32[part, :])
+            act_out[part, columns] = value.astype(BF)
+            der_out[part, columns] = slope
             return 0
 
         lax.fori_loop(0, rows // step, body, 0)
@@ -213,33 +205,30 @@
 
 
 def weight_kernel(count, meta, *refs):
-    lates, rests = refs[:count], refs[count : 2 * count]
-    act_late, act_rest, *outs, lhs_late, lhs_rest = refs[2 * count :]
-    half = lates[0].shape[1] // 2
+    moved, kept = refs[:count], refs[count : 2 * count]
+    act_moved, act_kept, *outs, lhs_moved, lhs_kept = refs[2 * count :]
+    half = moved[0].shape[1] // 2
     mine = dp_at(meta) % 2 == 0
     for i in range(count):
-        for piece, lhs in ((lates[i], lhs_late), (rests[i], lhs_rest)):
+        for piece, lhs in ((moved[i], lhs_moved), (kept[i], lhs_kept)):
             both = piece[...].T
             lo, hi = both[:half], both[half:]
             lhs[i * half : (i + 1) * half, :] = jnp.where(mine, hi, lo)
             lhs[(count + i) * half : (count + i + 1) * half, :] = jnp.where(mine, lo, hi)
-    again_kernel(meta, lhs_late, lhs_rest, act_late, act_rest, *outs)
-
-
-def again_kernel(meta, lhs_late, lhs_rest, act_late, act_rest, *outs):
-    step = lhs_late.shape[0] // 4
+    again_kernel(0, meta, lhs_moved, lhs_kept, act_moved, act_kept, *outs)
+
+
+def again_kernel(base, meta, lhs_moved, lhs_kept, act_moved, act_kept, *outs):
+    columns = slice(base, base + act_kept.shape[1])
+    step = lhs_moved.shape[0] // 4
     at = 0
     for out in outs:
         for i in range(0, out.shape[0], step):
             part = slice(at, at + step)
-            value = jnp.dot(lhs_late[part, :], act_late[...], preferred_element_type=F32)
-            value += jnp.dot(lhs_rest[part, :], act_rest[...], preferred_element_type=F32)
+            value = jnp.dot(lhs_moved[part, :], act_moved[:, columns], preferred_element_type=F32)
+            value += jnp.dot(lhs_kept[part, :], act_kept[...], preferred_element_type=F32)
             out[i : i + step, :] = value.astype(out.dtype)
             at += step
-
-
-def tick_kernel(meta, out):
-    out[...] = jnp.zeros(out.shape, out.dtype)
 
 
 def near_kernel(count, meta, *refs):
@@ -324,8 +313,7 @@
     width = cotangent.shape[1]
     features = down_weight.shape[0]
     half = width // 2
-    parts = (640, 512, ff - 1152)
-    begins = (0, 640, 1152)
+    part = ff // 3
     others = EARLY + KEEP
     n = lax.axis_size("dp")
     d = lax.axis_index("dp").astype(jnp.int32)
@@ -336,32 +324,29 @@
     vmem = pltpu.VMEM
     sems = pltpu.SemaphoreType.DMA
 
-    def gelu(meta, late, base, columns):
-        block = 256
-        rows = LATE if late else others
-        count = pl.cdiv(columns, block)
+    def gelu(meta, pick, base, columns):
+        rows, block = pick.shape[0], 256
         return kernel_call(
-            functools.partial(gelu_kernel, late, base, block),
+            functools.partial(gelu_kernel, base, block),
             [shape(rows, columns), shape(rows, columns, F32)],
-            [IN_HBM], [IN_VMEM] * 2,
-            [vmem((rows, home), BF), vmem((rows, block), F32), vmem((count, home, block), BF), sems((count,))],
-        )(meta, hidden_pre)
-
-    def weight_first(meta, act_late, act):
-        count = len(lates)
+            [IN_VMEM] * 2, [IN_VMEM] * 2, [vmem((rows, block), F32)],
+        )(meta, pick, pre)
+
+    def weight_first(meta, act_moved, act_kept):
         return kernel_call(
-            functools.partial(weight_kernel, count),
-            [shape(width, parts[0])] * 2 + [shape(width, parts[0], F32)] * 2
-            + [shape(count * width, LATE), shape(count * width, others)],
-            [IN_VMEM] * (2 * count + 2), [IN_VMEM] * 6,
-        )(meta, *lates, *rests, act_late, act)
-
-    def weight_again(meta, act_late, act):
-        columns = act.shape[1]
+            functools.partial(weight_kernel, 4),
+            [shape(width, part)] * 2 + [shape(width, part, F32)] * 2
+            + [shape(features, LATE), shape(features, others)],
+            [IN_VMEM] * 10, [IN_VMEM] * 6,
+        )(meta, *lates, *rests, act_moved, act_kept)
+
+    def weight_again(meta, base, act_moved, act_kept, count):
+        rows = features // 2 // count
         return kernel_call(
-            again_kernel,
-            [shape(4 * half, columns), shape(4 * half, columns, F32)], [IN_VMEM] * 4, [IN_VMEM] * 2,
-        )(meta, *lhs, act_late, act)
+            functools.partial(again_kernel, base),
+            [shape(rows, part)] * count + [shape(rows, part, F32)] * count,
+            [IN_VMEM] * 4, [IN_VMEM] * (2 * count),
+        )(meta, *lhs, act_moved, act_kept)
 
     def grads(meta, pieces, first_row, first_slope, rows, base, slopes, cuts):
         return kernel_call(
@@ -370,91 +355,85 @@
             [vmem((rows, features), BF)],
         )(meta, *pieces, down_weight, *slopes)
 
-    def tick(meta):
-        return kernel_call(tick_kernel, shape(8, 128, F32), [], IN_VMEM)(meta)
-
     def near_step(meta, keeps, gots):
-        count, columns = len(keeps), keeps[0].shape[1]
+        count = len(keeps)
         return kernel_call(
             functools.partial(near_kernel, count),
-            [shape(width, columns), shape(width, columns, F32)], [IN_VMEM] * (2 * count), [IN_VMEM] * 2,
+            [shape(width, part), shape(width, part, F32)], [IN_VMEM] * (2 * count), [IN_VMEM] * 2,
         )(meta, *keeps, *gots)
 
     def far_step(meta, mine, got):
-        columns = got.shape[1]
         return kernel_call(
-            far_kernel, [shape(half, columns), shape(half, columns, F32)], [IN_VMEM] * 2, [IN_VMEM] * 2
+            far_kernel, [shape(half, part), shape(half, part, F32)], [IN_VMEM] * 2, [IN_VMEM] * 2
         )(meta, mine, got)
 
-    late, rest, early = kernel_call(
-        first_kernel, [shape(LATE, width), shape(others, width), shape(EARLY, width + ff)],
-        [IN_HBM] * 3, [IN_VMEM] * 3,
-        [vmem((home, width), BF), vmem((features,), F32), vmem((home, ff), BF), sems((3,))],
+    late, rest, early, late_pick, rest_pick, pre = kernel_call(
+        first_kernel,
+        [shape(LATE, width), shape(others, width), shape(EARLY, width + ff),
+         shape(LATE, home), shape(others, home), shape(home, ff)],
+        [IN_HBM] * 3, [IN_VMEM] * 6,
+        [vmem((home, width), BF), vmem((features,), F32), sems((3,))],
     )(meta, cotangent, layer_scale, hidden_pre)
     arrived_early = swapped(early, "dp", n // 2)
 
     late_c, late_y = swapped(late, "tensor", 1), swapped(late, "tensor", 2)
     rest_c, rest_y = swapped(rest, "tensor", 1), swapped(rest, "tensor", 2)
-    act_l1, der_l1 = gelu(after(meta, late), True, 0, parts[0])
-    late_y = after(late_y, act_l1, late_c, rest_c, arrived_early)
+    act_la, der_la = gelu(after(meta, late), late_pick, 0, part)
+    act_ra, der_ra = gelu(after(meta, act_la), rest_pick, 0, part)
+    late_y = after(late_y, act_ra, late_c, rest_c, arrived_early)
     late_yc = swapped(late_y, "tensor", 1)
     lates = (late, late_c, late_y, late_yc)
 
-    (moving_a,) = grads(after(meta, late_y), lates, 0, 0, LATE, 0, (der_l1,), parts[:1])
+    (moving_a,) = grads(after(meta, late_y), lates, 0, 0, LATE, 0, (der_la,), (part,))
     arrived_a = swapped(moving_a, "dp", n // 2)
 
-    act_a, der_a = gelu(after(meta, moving_a), False, 0, parts[0])
-    rest_y = after(rest_y, act_a)
+    rest_y = after(rest_y, moving_a)
     rest_yc = swapped(rest_y, "tensor", 1)
     rests = (rest, rest_c, rest_y, rest_yc)
-    *sends_a, keep_01, keep_23, lhs_late, lhs_rest = weight_first(after(meta, act_a), act_l1, act_a)
-    lhs = (lhs_late, lhs_rest)
+    *sends_a, keep_01, keep_23, lhs_moved, lhs_kept = weight_first(after(meta, moving_a), act_la, act_ra)
+    lhs = (lhs_moved, lhs_kept)
     gots_a = [swapped(send, "dp", 1) for send in sends_a]
 
-    act_l2, der_l2 = gelu(after(meta, keep_01), True, begins[1], parts[1])
-    (moving_b,) = grads(after(meta, act_l2), lates, 0, 0, LATE, begins[1], (der_l2,), parts[1:2])
-    act_b, der_b = gelu(after(meta, moving_b), False, begins[1], parts[1])
-    send_b, keep_b = weight_again(after(meta, act_b, arrived_a), act_l2, act_b)
+    act_l, der_l = gelu(after(meta, keep_01), late_pick, part, 2 * part)
+    moving_b, moving_c = grads(after(meta, act_l), lates, 0, 0, LATE, part, (der_l,), (part, part))
+    act_rb, der_rb = gelu(after(meta, moving_b), rest_pick, part, part)
+    send_b, keep_b = weight_again(after(meta, act_rb, arrived_a), 0, act_l, act_rb, 1)
     got_b = swapped(send_b, "dp", 1)
     arrived_b = swapped(after(moving_b, send_b), "dp", n // 2)
 
-    act_l3, der_l3 = gelu(after(meta, send_b), True, begins[2], parts[2])
-    early_sent = after(arrived_early[:, :width], act_l3)
+    out_na, mine_a = near_step(after(meta, send_b), (keep_01, keep_23), gots_a)
+    got_na = swapped(out_na, "dp", 2)
+    early_sent = after(arrived_early[:, :width], out_na)
     early_c, early_y = swapped(early_sent, "tensor", 1), swapped(early_sent, "tensor", 2)
-    act_c, der_c = gelu(after(meta, act_l3), False, begins[2], parts[2])
-    send_c, keep_c = weight_again(after(meta, act_c, early_c, early_y), act_l3, act_c)
-    got_c = swapped(send_c, "dp", 1)
-    early_y = after(early_y, send_c)
+    act_rc, der_rc = gelu(after(meta, out_na), rest_pick, 2 * part, part)
+    early_y = after(early_y, early_c, act_rc)
     early_yc = swapped(early_y, "tensor", 1)
-
-    out_na, mine_a = near_step(after(meta, send_c), (keep_01, keep_23), gots_a)
-    got_na = swapped(out_na, "dp", 2)
-
-    (moving_c,) = grads(after(meta, out_na), lates, 0, 0, LATE, begins[2], (der_l3,), parts[2:])
-    (kept_grad,) = grads(after(meta, moving_c), rests, EARLY, EARLY, KEEP, 0, (der_a, der_b, der_c), (ff,))
+    *sends_c, keep_c01, keep_c23 = weight_again(after(meta, early_yc), part, act_l, act_rc, 2)
+    gots_c = [swapped(send, "dp", 1) for send in sends_c]
+
+    (kept_grad,) = grads(after(meta, keep_c01), rests, EARLY, EARLY, KEEP, 0, (der_ra, der_rb, der_rc), (ff,))
     early_grad = kernel_call(
         functools.partial(early_kernel, 256), shape(EARLY, ff), [IN_VMEM] * 5, IN_VMEM,
         [vmem((EARLY, features), BF), vmem((EARLY, 256), F32)],
     )(after(meta, kept_grad), arrived_early, early_c, early_y, early_yc, down_weight)
 
-    out_nb, mine_b = near_step(after(meta, early_grad, arrived_b), (keep_b,), (got_b,))
+    out_nb, mine_b = near_step(after(meta, early_grad, arrived_b, got_na), (keep_b,), (got_b,))
     got_nb = swapped(out_nb, "dp", 2)
-    tick_b = tick(after(meta, out_nb))
-    arrived_c = swapped(after(moving_c, tick_b), "dp", n // 2)
-    out_fa, own_a = far_step(after(meta, tick_b), mine_a, got_na)
+    arrived_c = swapped(after(moving_c, out_nb), "dp", n // 2)
+    out_fa, own_a = far_step(after(meta, out_nb), mine_a, got_na)
     got_fa = swapped(out_fa, "dp", 4)
-    out_nc, mine_c = near_step(after(meta, out_fa, arrived_c), (keep_c,), (got_c,))
+    out_nc, mine_c = near_step(after(meta, out_fa), (keep_c01, keep_c23), gots_c)
     got_nc = swapped(out_nc, "dp", 2)
     out_fb, own_b = far_step(after(meta, out_nc), mine_b, got_nb)
     got_fb = swapped(out_fb, "dp", 4)
-    out_fc, own_c = far_step(after(meta, out_fb, got_fa), mine_c, got_nc)
+    out_fc, own_c = far_step(after(meta, out_fb, got_fa, arrived_c), mine_c, got_nc)
     got_fc = swapped(out_fc, "dp", 4)
     total = [a + b.astype(F32) for a, b in ((own_a, got_fa), (own_b, got_fb), (own_c, got_fc))]
     down_grad = jnp.concatenate(total, axis=1) / math.sqrt(n * home)
 
     hidden_grad = kernel_call(
-        functools.partial(place_kernel, parts), shape(BAL, ff), [IN_VMEM] * (2 + len(parts)),
-        pl.BlockSpec((BAL, 128), lambda i, *_: (0, i)), grid=(ff // 128,),
+        functools.partial(place_kernel, (part,) * 3), shape(BAL, ff), [IN_VMEM] * 5,
+        pl.BlockSpec((BAL, 256), lambda i, *_: (0, i)), grid=(ff // 256,),
     )(after(meta, out_fc), kept_grad, early_grad, arrived_a, arrived_b, arrived_c)
     return (hidden_grad, down_grad)
 

time: 134 us -> 136 us (1.015)
  Pallas kernels: 63.2 us -> 50 us
  waiting for transfers between devices: 48.7 us -> 57.2 us
  starting transfers between devices: 18.5 us -> 24.1 us
    pallas_call x16 -> x15, Pallas kernels: 46.3 us -> 35 us  [the longest x5 17.9 us: gelu(): kernel_call(functools.partial(gelu_kernel, base, block), [shape(rows, col...]
    ppermute x23 -> x24, waiting for transfers between devices: 48.7 us -> 57.2 us  [swapped(): return lax.ppermute(block, axis, [(i, i ^ distance) for i in range(n)])]
    ppermute x23 -> x24, starting transfers between devices: 18.5 us -> 24.1 us  [swapped(): return lax.ppermute(block, axis, [(i, i ^ distance) for i in range(n)])]
    pallas_call x4 -> x3, Pallas kernels: 9.37 us -> 7.63 us  [grads(): kernel_call(functools.partial(grad_kernel, first_row, first_slope, base,...]
  transfers between devices with their start and end apart: 23 -> 24, of which waited for: 13 -> 15; matrix products, arithmetic and copies ran while one was open for 0% -> 0% of each run, Pallas kernels for 44% -> 34%
where the time goes in v13:
time: 136 us; the launch traced here: 134 us
  waiting for transfers between devices  57.2 us (42%)
  Pallas kernels  50 us (37%)
  starting transfers between devices  24.1 us (18%)
  other arithmetic  1.99 us (1%)
    ppermute x24, waiting for transfers between devices, swapped(): return lax.ppermute(block, axis, [(i, i ^ distance) for i in range(n)])  57.2 us
    ppermute x24, starting transfers between devices, swapped(): return lax.ppermute(block, axis, [(i, i ^ distance) for i in range(n)])  24.1 us
    pallas_call x5, Pallas kernels, gelu(): kernel_call(functools.partial(gelu_kernel, base, block), [shape(rows, col...  17.9 us
    pallas_call x3, Pallas kernels, grads(): kernel_call(functools.partial(grad_kernel, first_row, first_slope, base,...  7.63 us
    pallas_call x2, Pallas kernels, weight_again(): kernel_call(functools.partial(again_kernel, base), [shape(rows, part)] *...  5.7 us
    pallas_call x1, Pallas kernels, shards(): kernel_call(first_kernel, [shape(LATE, width), shape(others, width), shap...  4.44 us
    pallas_call x1, Pallas kernels, shards(): kernel_call(functools.partial(place_kernel, (part,) * 3), shape(BAL, ff),...  3.29 us
    pallas_call x1, Pallas kernels, weight_first(): kernel_call(functools.partial(weight_kernel, 4), [shape(width, part)] * 2...  2.92 us
  transfers between devices with their start and end apart: 24, of which 15 were waited for; matrix products, arithmetic and copies ran while one was open for 0% of the time, Pallas kernels for 34%

profile of v13, /device:TPU:0, one launch (start us, length us, event | category | flops | bytes accessed | tf_op | source)
XLA Modules:
  0.0 134.1 jit_solution(2391013804938055738)
XLA Ops:
  1.4 4.4 %shard_map.77 = (bf16[480,384]{1,0:T(8,128)(2,1)S(1)}, bf16[576,384]{1,0:T(8,128)(2,1)S(1)}, bf16[48,1920]{1,0:T(8,128)(2,1)S(1)}, bf16[480,1032]{1,0:T(8,128)(2...) custom-call(s32[9,8]{1,0:T(8,128)S(1)} %pad_add_fusion.meta, bf16[1032,384]{1,0:T(8,128)(2,1)} %cot_hbm.1, ...), custom_call_target="tpu_custom_call" | custom-call | flops 1 | bytes 1 | tf_op jit(solution)/shard_map/pallas_call | solution.py:370
  6.4 2.9 %collective-permute-start.1 = (bf16[480,384]{1,0:T(8,128)(2,1)S(1)}, bf16[480,384]{1,0:T(8,128)(2,1)S(1)}, u32[]{:S(2)}, u32[]{:S(2)}) collective-permute-start(bf16[480,384]{1,0:T(8,128)(2,1)S(1)} %get-tuple-element.70.p0.refs_0_), channel_id=1, source_target_pairs={{0,2},{1,3},{2,0},{3,1},{4,6},{5,7},{6,4},{7,5},{8,10},{9,11},{10,... | collective-permute-start | bytes 1105928 | tf_op jit(solution)/shard_map/ppermute | solution.py:301
  9.4 2.6 %collective-permute-start = (bf16[48,1920]{1,0:T(8,128)(2,1)S(1)}, bf16[48,1920]{1,0:T(8,128)(2,1)S(1)}, u32[]{:S(2)}, u32[]{:S(2)}) collective-permute-start(bf16[48,1920]{1,0:T(8,128)(2,1)S(1)} %get-tuple-element.69), channel_id=1, source_target_pairs={{0,16},{4,20},{8,24},{12,28},{16,0},{20,4},{24,8},{28,12},{1,17},{... | collective-permute-start | bytes 552968 | tf_op jit(solution)/shard_map/ppermute | solution.py:301
  12.4 3.0 %shard_map.78 = (bf16[480,512]{1,0:T(8,128)(2,1)S(1)}, f32[480,512]{1,0:T(8,128)S(1)}) custom-call(s32[9,8]{1,0:T(8,128)S(1)} %pad_add_fusion.meta, bf16[480,1032]{1,0:T(8,128)(2,1)S(1)} %get-tuple-element.72.pick, bf16[1032,1536]{1,0:T(8,128)(2,1)S(1)} %get-tuple-element.73.pre), custom_call_target="tpu_custom_call" | custom-call | flops 1 | bytes 1 | tf_op jit(solution)/shard_map/pallas_call | solution.py:329
  15.5 3.2 %shard_map.79 = (bf16[576,512]{1,0:T(8,128)(2,1)S(1)}, f32[576,512]{1,0:T(8,128)S(1)}) custom-call(s32[9,8]{1,0:T(8,128)S(1)} %pad_add_fusion.meta, bf16[576,1032]{1,0:T(8,128)(2,1)S(1)} %get-tuple-element.76.pick, bf16[1032,1536]{1,0:T(8,128)(2,1)S(1)} %get-tuple-element.73.pre), custom_call_target="tpu_custom_call" | custom-call | flops 1 | bytes 1 | tf_op jit(solution)/shard_map/pallas_call | solution.py:329
  25.3 2.3 %collective-permute-done.5.refs_6_.p2 = bf16[576,384]{1,0:T(8,128)(2,1)S(1)} collective-permute-done((bf16[576,384]{1,0:T(8,128)(2,1)S(1)}, bf16[576,384]{1,0:T(8,128)(2,1)S(1)}, u32[]{:S(2)}, u32[]{:S(2)}) %collective-permute-start.5) | collective-permute-done | bytes 442400 | tf_op jit(solution)/shard_map/ppermute | solution.py:301
  29.5 2.9 %shard_map.81 = (bf16[384,512]{1,0:T(8,128)(2,1)S(1)}, bf16[384,512]{1,0:T(8,128)(2,1)S(1)}, f32[384,512]{1,0:T(8,128)S(1)}, f32[384,512]{1,0:T(8,128)S(1)}, bf1...) custom-call(s32[9,8]{1,0:T(8,128)S(1)} %pad_add_fusion.meta, ...), custom_call_target="tpu_custom_call" | custom-call | flops 1 | bytes 1 | tf_op jit(solution)/shard_map/pallas_call | solution.py:336
  32.4 5.0 %shard_map.82 = (bf16[480,1024]{1,0:T(8,128)(2,1)S(1)}, f32[480,1024]{1,0:T(8,128)S(1)}) custom-call(s32[9,8]{1,0:T(8,128)S(1)} %pad_add_fusion.meta, bf16[480,1032]{1,0:T(8,128)(2,1)S(1)} %get-tuple-element.72.pick, bf16[1032,1536]{1,0:T(8,128)(2,1)S(1)} %get-tuple-element.73.pre), custom_call_target="tpu_custom_call" | custom-call | flops 1 | bytes 1 | tf_op jit(solution)/shard_map/pallas_call | solution.py:329
  37.4 2.5 %shard_map.83 = (bf16[480,512]{1,0:T(8,128)(2,1)S(1)}, bf16[480,512]{1,0:T(8,128)(2,1)S(1)}) custom-call(s32[9,8]{1,0:T(8,128)S(1)} %pad_add_fusion.meta, bf16[480,384]{1,0:T(8,128)(2,1)S(1)} %get-tuple-element.70.p0.refs_0_, bf16[480,384]{1,0:T(8,128)(2,1)S(1)} %collective-permute-done.2.p1.refs_1_, bf16[480,384]{1,0:T(8,128)(2,1)S(1)} %collective-permute-done.1.p2.refs_2_, ...), custom_call_target="tpu_custom_call" | custom-call | flops 1 | bytes 1 | tf_op jit(solution)/shard_map/pallas_call | solution.py:352
  39.9 3.2 %shard_map.84 = (bf16[576,512]{1,0:T(8,128)(2,1)S(1)}, f32[576,512]{1,0:T(8,128)S(1)}) custom-call(s32[9,8]{1,0:T(8,128)S(1)} %pad_add_fusion.meta, bf16[576,1032]{1,0:T(8,128)(2,1)S(1)} %get-tuple-element.76.pick, bf16[1032,1536]{1,0:T(8,128)(2,1)S(1)} %get-tuple-element.73.pre), custom_call_target="tpu_custom_call" | custom-call | flops 1 | bytes 1 | tf_op jit(solution)/shard_map/pallas_call | solution.py:329
  45.2 3.6 %collective-permute-done.7.rest_0_ = bf16[480,512]{1,0:T(8,128)(2,1)S(1)} collective-permute-done((bf16[480,512]{1,0:T(8,128)(2,1)S(1)}, bf16[480,512]{1,0:T(8,128)(2,1)S(1)}, u32[]{:S(2)}, u32[]{:S(2)}) %collective-permute-start.7) | collective-permute-done | bytes 491552 | tf_op jit(solution)/shard_map/ppermute | solution.py:301
  48.8 2.9 %shard_map.85 = (bf16[768,512]{1,0:T(8,128)(2,1)S(1)}, f32[768,512]{1,0:T(8,128)S(1)}) custom-call(s32[9,8]{1,0:T(8,128)S(1)} %pad_add_fusion.meta, bf16[1536,480]{1,0:T(8,128)(2,1)S(1)} %get-tuple-element.93.lhs_moved, bf16[1536,576]{1,0:T(8,128)(2,1)S(1)} %get-tuple-element.94.lhs_kept, bf16[480,1024]{1,0:T(8,128)(2,1)S(1)} %get-tuple-element.86.act_moved, ...), custom_call_target="tpu_custom_call" | custom-call | flops 1 | bytes 1 | tf_op jit(solution)/shard_map/pallas_call | solution.py:345
  55.1 8.4 %collective-permute-done.9.refs_3_ = bf16[384,512]{1,0:T(8,128)(2,1)S(1)} collective-permute-done((bf16[384,512]{1,0:T(8,128)(2,1)S(1)}, bf16[384,512]{1,0:T(8,128)(2,1)S(1)}, u32[]{:S(2)}, u32[]{:S(2)}) %collective-permute-start.9) | collective-permute-done | bytes 393248 | tf_op jit(solution)/shard_map/ppermute | solution.py:301
  67.9 3.4 %shard_map.87 = (bf16[576,512]{1,0:T(8,128)(2,1)S(1)}, f32[576,512]{1,0:T(8,128)S(1)}) custom-call(s32[9,8]{1,0:T(8,128)S(1)} %pad_add_fusion.meta, bf16[576,1032]{1,0:T(8,128)(2,1)S(1)} %get-tuple-element.76.pick, bf16[1032,1536]{1,0:T(8,128)(2,1)S(1)} %get-tuple-element.73.pre), custom_call_target="tpu_custom_call" | custom-call | flops 1 | bytes 1 | tf_op jit(solution)/shard_map/pallas_call | solution.py:329
  72.8 2.9 %shard_map.88 = (bf16[384,512]{1,0:T(8,128)(2,1)S(1)}, bf16[384,512]{1,0:T(8,128)(2,1)S(1)}, f32[384,512]{1,0:T(8,128)S(1)}, f32[384,512]{1,0:T(8,128)S(1)}) custom-call(s32[9,8]{1,0:T(8,128)S(1)} %pad_add_fusion.meta, bf16[1536,480]{1,0:T(8,128)(2,1)S(1)} %get-tuple-element.93.lhs_moved, bf16[1536,576]{1,0:T(8,128)(2,1)S(1)} %get-tuple-element.94.lhs_kept, ...), custom_call_target="tpu_custom_call" | custom-call | flops 1 | bytes 1 | tf_op jit(solution)/shard_map/pallas_call | solution.py:345
  77.7 3.5 %shard_map.89.kept = bf16[528,1536]{1,0:T(8,128)(2,1)S(1)} custom-call(s32[9,8]{1,0:T(8,128)S(1)} %pad_add_fusion.meta, bf16[576,384]{1,0:T(8,128)(2,1)S(1)} %get-tuple-element.78.refs_4_.p0, bf16[576,384]{1,0:T(8,128)(2,1)S(1)} %collective-permute-done.3.refs_5_.p1, bf16[576,384]{1,0:T(8,128)(2,1)S(1)} %collective-permute-done.5.refs_6_.p2, ...), custom_call_target="tpu_custom_call" | custom-call | flops 1 | bytes 1 | tf_op jit(solution)/shard_map/pallas_call | solution.py:352
  81.2 2.9 %shard_map.90.early = bf16[48,1536]{1,0:T(8,128)(2,1)S(1)} custom-call(s32[9,8]{1,0:T(8,128)S(1)} %pad_add_fusion.meta, bf16[48,1920]{1,0:T(8,128)(2,1)S(1)} %collective-permute-done.own, bf16[48,384]{1,0:T(8,128)(2,1)S(1)} %collective-permute-done.11.p1, bf16[48,384]{1,0:T(8,128)(2,1)S(1)} %collective-permute-done.10.p2, ...), custom_call_target="tpu_custom_call" | custom-call | flops 1 | bytes 1 | tf_op jit(solution)/shard_map/pallas_call | solution.py:415
  85.6 2.6 %collective-permute-start.20 = (bf16[480,512]{1,0:T(8,128)(2,1)S(1)}, bf16[480,512]{1,0:T(8,128)(2,1)S(1)}, u32[]{:S(2)}, u32[]{:S(2)}) collective-permute-start(bf16[480,512]{1,0:T(8,128)(2,1)S(1)} %get-tuple-element.128), channel_id=1, source_target_pairs={{0,16},{4,20},{8,24},{12,28},{16,0},{20,4},{24,8},{28,12},{1,17},{... | collective-permute-start | bytes 1474568 | tf_op jit(solution)/shard_map/ppermute | solution.py:301
  89.4 7.1 %collective-permute-done.17.refs_3_ = bf16[384,512]{1,0:T(8,128)(2,1)S(1)} collective-permute-done((bf16[384,512]{1,0:T(8,128)(2,1)S(1)}, bf16[384,512]{1,0:T(8,128)(2,1)S(1)}, u32[]{:S(2)}, u32[]{:S(2)}) %collective-permute-start.17) | collective-permute-done | bytes 393248 | tf_op jit(solution)/shard_map/ppermute | solution.py:301
  99.3 7.3 %collective-permute-done.18.got = bf16[384,512]{1,0:T(8,128)(2,1)S(1)} collective-permute-done((bf16[384,512]{1,0:T(8,128)(2,1)S(1)}, bf16[384,512]{1,0:T(8,128)(2,1)S(1)}, u32[]{:S(2)}, u32[]{:S(2)}) %collective-permute-start.18) | collective-permute-done | bytes 393248 | tf_op jit(solution)/shard_map/ppermute | solution.py:301
  107.5 12.2 %collective-permute-done.19 = bf16[192,512]{1,0:T(8,128)(2,1)S(1)} collective-permute-done((bf16[192,512]{1,0:T(8,128)(2,1)S(1)}, bf16[192,512]{1,0:T(8,128)(2,1)S(1)}, u32[]{:S(2)}, u32[]{:S(2)}) %collective-permute-start.19) | collective-permute-done | bytes 196640 | tf_op jit(solution)/shard_map/ppermute | solution.py:301
  123.8 3.3 %shard_map.96 = bf16[720,1536]{1,0:T(8,128)(2,1)} custom-call(s32[9,8]{1,0:T(8,128)S(1)} %pad_add_fusion.meta, bf16[528,1536]{1,0:T(8,128)(2,1)S(1)} %shard_map.89.kept, bf16[48,1536]{1,0:T(8,128)(2,1)S(1)} %shard_map.90.early, bf16[480,512]{1,0:T(8,128)(2,1)S(1)} %collective-permute-done.7.rest_0_, bf16[480,512]{1,0:T(8,128)(2,1)S(1)} %collective-permute-done.13.rest_1_, ...), custom_call_target="tpu_custom_call" | custom-call | flops 1 | bytes 1 | tf_op jit(solution)/shard_map/pallas_call | solution.py:434
  127.1 2.7 %collective-permute-done.22 = bf16[192,512]{1,0:T(8,128)(2,1)S(1)} collective-permute-done((bf16[192,512]{1,0:T(8,128)(2,1)S(1)}, bf16[192,512]{1,0:T(8,128)(2,1)S(1)}, u32[]{:S(2)}, u32[]{:S(2)}) %collective-permute-start.22) | collective-permute-done | bytes 196640 | tf_op jit(solution)/shard_map/ppermute | solution.py:301
  129.9 3.0 %collective-permute-done.23 = bf16[192,512]{1,0:T(8,128)(2,1)S(1)} collective-permute-done((bf16[192,512]{1,0:T(8,128)(2,1)S(1)}, bf16[192,512]{1,0:T(8,128)(2,1)S(1)}, u32[]{:S(2)}, u32[]{:S(2)}) %collective-permute-start.23) | collective-permute-done | bytes 196640 | tf_op jit(solution)/shard_map/ppermute | solution.py:301
  (56 shorter events, 35.4 us)
Async XLA Ops:
  5.8 14.7 %collective-permute-start.3 = (bf16[576,384]{1,0:T(8,128)(2,1)S(1)}, bf16[576,384]{1,0:T(8,128)(2,1)S(1)}, u32[]{:S(2)}, u32[]{:S(2)}) collective-permute-start(bf16[576,384]{1,0:T(8,128)(2,1)S(1)} %get-tuple-element.78.refs_4_.p0), channel_id=1, source_target_pairs={{0,1},{1,0},{2,3},{3,2},{4,5},{5,4},{6,7},{7,6},{8,9},{9,8},{10,11... | collective-permute-start | bytes 1327112 | tf_op jit(solution)/shard_map/ppermute | solution.py:301
  6.3 14.2 %collective-permute-start.2 = (bf16[480,384]{1,0:T(8,128)(2,1)S(1)}, bf16[480,384]{1,0:T(8,128)(2,1)S(1)}, u32[]{:S(2)}, u32[]{:S(2)}) collective-permute-start(bf16[480,384]{1,0:T(8,128)(2,1)S(1)} %get-tuple-element.70.p0.refs_0_), channel_id=1, source_target_pairs={{0,1},{1,0},{2,3},{3,2},{4,5},{5,4},{6,7},{7,6},{8,9},{9,8},{10,11... | collective-permute-start | bytes 1105928 | tf_op jit(solution)/shard_map/ppermute | solution.py:301
  6.4 14.1 %collective-permute-start.1 = (bf16[480,384]{1,0:T(8,128)(2,1)S(1)}, bf16[480,384]{1,0:T(8,128)(2,1)S(1)}, u32[]{:S(2)}, u32[]{:S(2)}) collective-permute-start(bf16[480,384]{1,0:T(8,128)(2,1)S(1)} %get-tuple-element.70.p0.refs_0_), channel_id=1, source_target_pairs={{0,2},{1,3},{2,0},{3,1},{4,6},{5,7},{6,4},{7,5},{8,10},{9,11},{10,... | collective-permute-start | bytes 1105928 | tf_op jit(solution)/shard_map/ppermute | solution.py:301
  9.4 11.2 %collective-permute-start = (bf16[48,1920]{1,0:T(8,128)(2,1)S(1)}, bf16[48,1920]{1,0:T(8,128)(2,1)S(1)}, u32[]{:S(2)}, u32[]{:S(2)}) collective-permute-start(bf16[48,1920]{1,0:T(8,128)(2,1)S(1)} %get-tuple-element.69), channel_id=1, source_target_pairs={{0,16},{4,20},{8,24},{12,28},{16,0},{20,4},{24,8},{28,12},{1,17},{... | collective-permute-start | bytes 552968 | tf_op jit(solution)/shard_map/ppermute | solution.py:301
  11.9 15.7 %collective-permute-start.5 = (bf16[576,384]{1,0:T(8,128)(2,1)S(1)}, bf16[576,384]{1,0:T(8,128)(2,1)S(1)}, u32[]{:S(2)}, u32[]{:S(2)}) collective-permute-start(bf16[576,384]{1,0:T(8,128)(2,1)S(1)} %get-tuple-element.78.refs_4_.p0), channel_id=1, source_target_pairs={{0,2},{1,3},{2,0},{3,1},{4,6},{5,7},{6,4},{7,5},{8,10},{9,11},{10,... | collective-permute-start | bytes 1327112 | tf_op jit(solution)/shard_map/ppermute | solution.py:301
  20.6 1.8 %collective-permute-start.4 = (bf16[480,384]{1,0:T(8,128)(2,1)S(1)}, bf16[480,384]{1,0:T(8,128)(2,1)S(1)}, u32[]{:S(2)}, u32[]{:S(2)}) collective-permute-start(bf16[480,384]{1,0:T(8,128)(2,1)S(1)} %collective-permute-done.1.p2.refs_2_), channel_id=1, source_target_pairs={{0,1},{1,0},{2,3},{3,2},{4,5},{5,4},{6,7},{7,6},{8,9},{9,8},{10,11... | collective-permute-start | bytes 1105928 | tf_op jit(solution)/shard_map/ppermute | solution.py:301
  24.0 24.8 %collective-permute-start.7 = (bf16[480,512]{1,0:T(8,128)(2,1)S(1)}, bf16[480,512]{1,0:T(8,128)(2,1)S(1)}, u32[]{:S(2)}, u32[]{:S(2)}) collective-permute-start(bf16[480,512]{1,0:T(8,128)(2,1)S(1)} %shard_map.80), channel_id=1, source_target_pairs={{0,16},{4,20},{8,24},{12,28},{16,0},{20,4},{24,8},{28,12},{1,17},{... | collective-permute-start | bytes 1474568 | tf_op jit(solution)/shard_map/ppermute | solution.py:301
  27.7 1.8 %collective-permute-start.6 = (bf16[576,384]{1,0:T(8,128)(2,1)S(1)}, bf16[576,384]{1,0:T(8,128)(2,1)S(1)}, u32[]{:S(2)}, u32[]{:S(2)}) collective-permute-start(bf16[576,384]{1,0:T(8,128)(2,1)S(1)} %collective-permute-done.5.refs_6_.p2), channel_id=1, source_target_pairs={{0,1},{1,0},{2,3},{3,2},{4,5},{5,4},{6,7},{7,6},{8,9},{9,8},{10,11... | collective-permute-start | bytes 1327112 | tf_op jit(solution)/shard_map/ppermute | solution.py:301
  43.1 12.0 %collective-permute-start.8 = (bf16[384,512]{1,0:T(8,128)(2,1)S(1)}, bf16[384,512]{1,0:T(8,128)(2,1)S(1)}, u32[]{:S(2)}, u32[]{:S(2)}) collective-permute-start(bf16[384,512]{1,0:T(8,128)(2,1)S(1)} %get-tuple-element.98), channel_id=1, source_target_pairs={{0,4},{4,0},{8,12},{12,8},{16,20},{20,16},{24,28},{28,24},{1,5},{5... | collective-permute-start | bytes 1179656 | tf_op jit(solution)/shard_map/ppermute | solution.py:301
  44.9 18.7 %collective-permute-start.9 = (bf16[384,512]{1,0:T(8,128)(2,1)S(1)}, bf16[384,512]{1,0:T(8,128)(2,1)S(1)}, u32[]{:S(2)}, u32[]{:S(2)}) collective-permute-start(bf16[384,512]{1,0:T(8,128)(2,1)S(1)} %get-tuple-element.99), channel_id=1, source_target_pairs={{0,4},{4,0},{8,12},{12,8},{16,20},{20,16},{24,28},{28,24},{1,5},{5... | collective-permute-start | bytes 1179656 | tf_op jit(solution)/shard_map/ppermute | solution.py:301
  51.6 32.7 %collective-permute-start.15 = (bf16[768,512]{1,0:T(8,128)(2,1)S(1)}, bf16[768,512]{1,0:T(8,128)(2,1)S(1)}, u32[]{:S(2)}, u32[]{:S(2)}) collective-permute-start(bf16[768,512]{1,0:T(8,128)(2,1)S(1)} %get-tuple-element.95), channel_id=1, source_target_pairs={{0,4},{4,0},{8,12},{12,8},{16,20},{20,16},{24,28},{28,24},{1,5},{5... | collective-permute-start | bytes 2359304 | tf_op jit(solution)/shard_map/ppermute | solution.py:301
  53.2 30.9 %collective-permute-start.13 = (bf16[480,512]{1,0:T(8,128)(2,1)S(1)}, bf16[480,512]{1,0:T(8,128)(2,1)S(1)}, u32[]{:S(2)}, u32[]{:S(2)}) collective-permute-start(bf16[480,512]{1,0:T(8,128)(2,1)S(1)} %get-tuple-element.112), channel_id=1, source_target_pairs={{0,16},{4,20},{8,24},{12,28},{16,0},{20,4},{24,8},{28,12},{1,17},{... | collective-permute-start | bytes 1474568 | tf_op jit(solution)/shard_map/ppermute | solution.py:301
  64.5 19.8 %collective-permute-start.14 = (bf16[384,512]{1,0:T(8,128)(2,1)S(1)}, bf16[384,512]{1,0:T(8,128)(2,1)S(1)}, u32[]{:S(2)}, u32[]{:S(2)}) collective-permute-start(bf16[384,512]{1,0:T(8,128)(2,1)S(1)} %get-tuple-element.100), channel_id=1, source_target_pairs={{0,8},{4,12},{8,0},{12,4},{16,24},{20,28},{24,16},{28,20},{1,9},{5... | collective-permute-start | bytes 1179656 | tf_op jit(solution)/shard_map/ppermute | solution.py:301
  66.3 5.0 %collective-permute-start.10 = (bf16[48,384]{1,0:T(8,128)(2,1)S(1)}, bf16[48,384]{1,0:T(8,128)(2,1)S(1)}, u32[]{:S(2)}, u32[]{:S(2)}) collective-permute-start(bf16[48,384]{1,0:T(8,128)(2,1)S(1)} %slice.4), channel_id=1, source_target_pairs={{0,2},{1,3},{2,0},{3,1},{4,6},{5,7},{6,4},{7,5},{8,10},{9,11},{10,... | collective-permute-start | bytes 110600 | tf_op jit(solution)/shard_map/ppermute | solution.py:301
  67.9 3.5 %collective-permute-start.11 = (bf16[48,384]{1,0:T(8,128)(2,1)S(1)}, bf16[48,384]{1,0:T(8,128)(2,1)S(1)}, u32[]{:S(2)}, u32[]{:S(2)}) collective-permute-start(bf16[48,384]{1,0:T(8,128)(2,1)S(1)} %slice.4), channel_id=1, source_target_pairs={{0,1},{1,0},{2,3},{3,2},{4,5},{5,4},{6,7},{7,6},{8,9},{9,8},{10,11... | collective-permute-start | bytes 110600 | tf_op jit(solution)/shard_map/ppermute | solution.py:301
  71.3 1.4 %collective-permute-start.12 = (bf16[48,384]{1,0:T(8,128)(2,1)S(1)}, bf16[48,384]{1,0:T(8,128)(2,1)S(1)}, u32[]{:S(2)}, u32[]{:S(2)}) collective-permute-start(bf16[48,384]{1,0:T(8,128)(2,1)S(1)} %collective-permute-done.10.p2), channel_id=1, source_target_pairs={{0,1},{1,0},{2,3},{3,2},{4,5},{5,4},{6,7},{7,6},{8,9},{9,8},{10,11... | collective-permute-start | bytes 110600 | tf_op jit(solution)/shard_map/ppermute | solution.py:301
  75.6 13.7 %collective-permute-start.16 = (bf16[384,512]{1,0:T(8,128)(2,1)S(1)}, bf16[384,512]{1,0:T(8,128)(2,1)S(1)}, u32[]{:S(2)}, u32[]{:S(2)}) collective-permute-start(bf16[384,512]{1,0:T(8,128)(2,1)S(1)} %get-tuple-element.121), channel_id=1, source_target_pairs={{0,4},{4,0},{8,12},{12,8},{16,20},{20,16},{24,28},{28,24},{1,5},{5... | collective-permute-start | bytes 1179656 | tf_op jit(solution)/shard_map/ppermute | solution.py:301
  77.2 19.3 %collective-permute-start.17 = (bf16[384,512]{1,0:T(8,128)(2,1)S(1)}, bf16[384,512]{1,0:T(8,128)(2,1)S(1)}, u32[]{:S(2)}, u32[]{:S(2)}) collective-permute-start(bf16[384,512]{1,0:T(8,128)(2,1)S(1)} %get-tuple-element.122), channel_id=1, source_target_pairs={{0,4},{4,0},{8,12},{12,8},{16,20},{20,16},{24,28},{28,24},{1,5},{5... | collective-permute-start | bytes 1179656 | tf_op jit(solution)/shard_map/ppermute | solution.py:301
  85.3 21.3 %collective-permute-start.18 = (bf16[384,512]{1,0:T(8,128)(2,1)S(1)}, bf16[384,512]{1,0:T(8,128)(2,1)S(1)}, u32[]{:S(2)}, u32[]{:S(2)}) collective-permute-start(bf16[384,512]{1,0:T(8,128)(2,1)S(1)} %get-tuple-element.115), channel_id=1, source_target_pairs={{0,8},{4,12},{8,0},{12,4},{16,24},{20,28},{24,16},{28,20},{1,9},{5... | collective-permute-start | bytes 1179656 | tf_op jit(solution)/shard_map/ppermute | solution.py:301
  85.6 34.2 %collective-permute-start.20 = (bf16[480,512]{1,0:T(8,128)(2,1)S(1)}, bf16[480,512]{1,0:T(8,128)(2,1)S(1)}, u32[]{:S(2)}, u32[]{:S(2)}) collective-permute-start(bf16[480,512]{1,0:T(8,128)(2,1)S(1)} %get-tuple-element.128), channel_id=1, source_target_pairs={{0,16},{4,20},{8,24},{12,28},{16,0},{20,4},{24,8},{28,12},{1,17},{... | collective-permute-start | bytes 1474568 | tf_op jit(solution)/shard_map/ppermute | solution.py:301
  89.0 30.7 %collective-permute-start.19 = (bf16[192,512]{1,0:T(8,128)(2,1)S(1)}, bf16[192,512]{1,0:T(8,128)(2,1)S(1)}, u32[]{:S(2)}, u32[]{:S(2)}) collective-permute-start(bf16[192,512]{1,0:T(8,128)(2,1)S(1)} %get-tuple-element.118), channel_id=1, source_target_pairs={{0,16},{4,20},{8,24},{12,28},{16,0},{20,4},{24,8},{28,12},{1,17},{... | collective-permute-start | bytes 589832 | tf_op jit(solution)/shard_map/ppermute | solution.py:301
  97.4 24.5 %collective-permute-start.21 = (bf16[384,512]{1,0:T(8,128)(2,1)S(1)}, bf16[384,512]{1,0:T(8,128)(2,1)S(1)}, u32[]{:S(2)}, u32[]{:S(2)}) collective-permute-start(bf16[384,512]{1,0:T(8,128)(2,1)S(1)} %get-tuple-element.123), channel_id=1, source_target_pairs={{0,8},{4,12},{8,0},{12,4},{16,24},{20,28},{24,16},{28,20},{1,9},{5... | collective-permute-start | bytes 1179656 | tf_op jit(solution)/shard_map/ppermute | solution.py:301
  107.4 22.4 %collective-permute-start.22 = (bf16[192,512]{1,0:T(8,128)(2,1)S(1)}, bf16[192,512]{1,0:T(8,128)(2,1)S(1)}, u32[]{:S(2)}, u32[]{:S(2)}) collective-permute-start(bf16[192,512]{1,0:T(8,128)(2,1)S(1)} %get-tuple-element.126), channel_id=1, source_target_pairs={{0,16},{4,20},{8,24},{12,28},{16,0},{20,4},{24,8},{28,12},{1,17},{... | collective-permute-start | bytes 589832 | tf_op jit(solution)/shard_map/ppermute | solution.py:301
  122.7 10.2 %collective-permute-start.23 = (bf16[192,512]{1,0:T(8,128)(2,1)S(1)}, bf16[192,512]{1,0:T(8,128)(2,1)S(1)}, u32[]{:S(2)}, u32[]{:S(2)}) collective-permute-start(bf16[192,512]{1,0:T(8,128)(2,1)S(1)} %get-tuple-element.131), channel_id=1, source_target_pairs={{0,16},{4,20},{8,24},{12,28},{16,0},{20,4},{24,8},{28,12},{1,17},{... | collective-permute-start | bytes 589832 | tf_op jit(solution)/shard_map/ppermute | solution.py:301
  (2 other events, 30.8 us)

commit v14 on v13

--- a/solution.py
+++ b/solution.py
@@ -396,7 +396,7 @@
 
     act_l, der_l = gelu(after(meta, keep_01), late_pick, part, 2 * part)
     moving_b, moving_c = grads(after(meta, act_l), lates, 0, 0, LATE, part, (der_l,), (part, part))
-    act_rb, der_rb = gelu(after(meta, moving_b), rest_pick, part, part)
+    act_rb, der_rb = gelu(after(meta, moving_b, gots_a[0]), rest_pick, part, part)
     send_b, keep_b = weight_again(after(meta, act_rb, arrived_a), 0, act_l, act_rb, 1)
     got_b = swapped(send_b, "dp", 1)
     arrived_b = swapped(after(moving_b, send_b), "dp", n // 2)
@@ -419,14 +419,14 @@
 
     out_nb, mine_b = near_step(after(meta, early_grad, arrived_b, got_na), (keep_b,), (got_b,))
     got_nb = swapped(out_nb, "dp", 2)
-    arrived_c = swapped(after(moving_c, out_nb), "dp", n // 2)
+    arrived_c = swapped(after(moving_c, keep_c01), "dp", n // 2)
     out_fa, own_a = far_step(after(meta, out_nb), mine_a, got_na)
     got_fa = swapped(out_fa, "dp", 4)
     out_nc, mine_c = near_step(after(meta, out_fa), (keep_c01, keep_c23), gots_c)
     got_nc = swapped(out_nc, "dp", 2)
-    out_fb, own_b = far_step(after(meta, out_nc), mine_b, got_nb)
+    out_fb, own_b = far_step(after(meta, out_nc, arrived_c), mine_b, got_nb)
     got_fb = swapped(out_fb, "dp", 4)
-    out_fc, own_c = far_step(after(meta, out_fb, got_fa, arrived_c), mine_c, got_nc)
+    out_fc, own_c = far_step(after(meta, out_fb, got_fa), mine_c, got_nc)
     got_fc = swapped(out_fc, "dp", 4)
     total = [a + b.astype(F32) for a, b in ((own_a, got_fa), (own_b, got_fb), (own_c, got_fc))]
     down_grad = jnp.concatenate(total, axis=1) / math.sqrt(n * home)

time: 136 us -> 136 us (level); the launches traced: 134 us -> 135 us
  starting transfers between devices: 24.1 us -> 31 us
  waiting for transfers between devices: 57.2 us -> 51.6 us
    ppermute x24, starting transfers between devices: 24.1 us -> 31 us  [swapped(): return lax.ppermute(block, axis, [(i, i ^ distance) for i in range(n)])]
    ppermute x24, waiting for transfers between devices: 57.2 us -> 51.6 us  [swapped(): return lax.ppermute(block, axis, [(i, i ^ distance) for i in range(n)])]
  transfers between devices with their start and end apart: 24 -> 24, of which waited for: 15 -> 13; matrix products, arithmetic and copies ran while one was open for 0% -> 0% of each run, Pallas kernels for 34% -> 34%
where the time goes in v14:
time: 136 us; the launch traced here: 135 us
  waiting for transfers between devices  51.6 us (38%)
  Pallas kernels  50 us (37%)
  starting transfers between devices  31 us (23%)
  other arithmetic  1.99 us (1%)
    ppermute x24, waiting for transfers between devices, swapped(): return lax.ppermute(block, axis, [(i, i ^ distance) for i in range(n)])  51.6 us
    ppermute x24, starting transfers between devices, swapped(): return lax.ppermute(block, axis, [(i, i ^ distance) for i in range(n)])  31 us
    pallas_call x5, Pallas kernels, gelu(): kernel_call(functools.partial(gelu_kernel, base, block), [shape(rows, col...  17.9 us
    pallas_call x3, Pallas kernels, grads(): kernel_call(functools.partial(grad_kernel, first_row, first_slope, base,...  7.63 us
    pallas_call x2, Pallas kernels, weight_again(): kernel_call(functools.partial(again_kernel, base), [shape(rows, part)] *...  5.7 us
    pallas_call x1, Pallas kernels, shards(): kernel_call(first_kernel, [shape(LATE, width), shape(others, width), shap...  4.44 us
    pallas_call x1, Pallas kernels, shards(): kernel_call(functools.partial(place_kernel, (part,) * 3), shape(BAL, ff),...  3.29 us
    pallas_call x1, Pallas kernels, weight_first(): kernel_call(functools.partial(weight_kernel, 4), [shape(width, part)] * 2...  2.93 us
  transfers between devices with their start and end apart: 24, of which 13 were waited for; matrix products, arithmetic and copies ran while one was open for 0% of the time, Pallas kernels for 34%

profile of v14, /device:TPU:0, one launch (start us, length us, event | category | flops | bytes accessed | tf_op | source)
XLA Modules:
  0.0 135.5 jit_solution(18111382633324095813)
XLA Ops:
  1.4 4.4 %shard_map.77 = (bf16[480,384]{1,0:T(8,128)(2,1)S(1)}, bf16[576,384]{1,0:T(8,128)(2,1)S(1)}, bf16[48,1920]{1,0:T(8,128)(2,1)S(1)}, bf16[480,1032]{1,0:T(8,128)(2...) custom-call(s32[9,8]{1,0:T(8,128)S(1)} %pad_add_fusion.meta, bf16[1032,384]{1,0:T(8,128)(2,1)} %cot_hbm.1, ...), custom_call_target="tpu_custom_call" | custom-call | flops 1 | bytes 1 | tf_op jit(solution)/shard_map/pallas_call | solution.py:370
  6.4 2.9 %collective-permute-start.1 = (bf16[480,384]{1,0:T(8,128)(2,1)S(1)}, bf16[480,384]{1,0:T(8,128)(2,1)S(1)}, u32[]{:S(2)}, u32[]{:S(2)}) collective-permute-start(bf16[480,384]{1,0:T(8,128)(2,1)S(1)} %get-tuple-element.70.p0.refs_0_), channel_id=1, source_target_pairs={{0,2},{1,3},{2,0},{3,1},{4,6},{5,7},{6,4},{7,5},{8,10},{9,11},{10,... | collective-permute-start | bytes 1105928 | tf_op jit(solution)/shard_map/ppermute | solution.py:301
  9.4 2.6 %collective-permute-start = (bf16[48,1920]{1,0:T(8,128)(2,1)S(1)}, bf16[48,1920]{1,0:T(8,128)(2,1)S(1)}, u32[]{:S(2)}, u32[]{:S(2)}) collective-permute-start(bf16[48,1920]{1,0:T(8,128)(2,1)S(1)} %get-tuple-element.69), channel_id=1, source_target_pairs={{0,16},{4,20},{8,24},{12,28},{16,0},{20,4},{24,8},{28,12},{1,17},{... | collective-permute-start | bytes 552968 | tf_op jit(solution)/shard_map/ppermute | solution.py:301
  12.4 3.0 %shard_map.78 = (bf16[480,512]{1,0:T(8,128)(2,1)S(1)}, f32[480,512]{1,0:T(8,128)S(1)}) custom-call(s32[9,8]{1,0:T(8,128)S(1)} %pad_add_fusion.meta, bf16[480,1032]{1,0:T(8,128)(2,1)S(1)} %get-tuple-element.72.pick, bf16[1032,1536]{1,0:T(8,128)(2,1)S(1)} %get-tuple-element.73.pre), custom_call_target="tpu_custom_call" | custom-call | flops 1 | bytes 1 | tf_op jit(solution)/shard_map/pallas_call | solution.py:329
  15.5 3.2 %shard_map.79 = (bf16[576,512]{1,0:T(8,128)(2,1)S(1)}, f32[576,512]{1,0:T(8,128)S(1)}) custom-call(s32[9,8]{1,0:T(8,128)S(1)} %pad_add_fusion.meta, bf16[576,1032]{1,0:T(8,128)(2,1)S(1)} %get-tuple-element.76.pick, bf16[1032,1536]{1,0:T(8,128)(2,1)S(1)} %get-tuple-element.73.pre), custom_call_target="tpu_custom_call" | custom-call | flops 1 | bytes 1 | tf_op jit(solution)/shard_map/pallas_call | solution.py:329
  24.0 3.6 %collective-permute-done.5.refs_6_.p2 = bf16[576,384]{1,0:T(8,128)(2,1)S(1)} collective-permute-done((bf16[576,384]{1,0:T(8,128)(2,1)S(1)}, bf16[576,384]{1,0:T(8,128)(2,1)S(1)}, u32[]{:S(2)}, u32[]{:S(2)}) %collective-permute-start.5) | collective-permute-done | bytes 442400 | tf_op jit(solution)/shard_map/ppermute | solution.py:301
  27.7 2.8 %collective-permute-start.8 = (bf16[480,512]{1,0:T(8,128)(2,1)S(1)}, bf16[480,512]{1,0:T(8,128)(2,1)S(1)}, u32[]{:S(2)}, u32[]{:S(2)}) collective-permute-start(bf16[480,512]{1,0:T(8,128)(2,1)S(1)} %shard_map.80), channel_id=1, source_target_pairs={{0,16},{4,20},{8,24},{12,28},{16,0},{20,4},{24,8},{28,12},{1,17},{... | collective-permute-start | bytes 1474568 | tf_op jit(solution)/shard_map/ppermute | solution.py:301
  30.5 2.9 %shard_map.81 = (bf16[384,512]{1,0:T(8,128)(2,1)S(1)}, bf16[384,512]{1,0:T(8,128)(2,1)S(1)}, f32[384,512]{1,0:T(8,128)S(1)}, f32[384,512]{1,0:T(8,128)S(1)}, bf1...) custom-call(s32[9,8]{1,0:T(8,128)S(1)} %pad_add_fusion.meta, ...), custom_call_target="tpu_custom_call" | custom-call | flops 1 | bytes 1 | tf_op jit(solution)/shard_map/pallas_call | solution.py:336
  35.5 5.0 %shard_map.82 = (bf16[480,1024]{1,0:T(8,128)(2,1)S(1)}, f32[480,1024]{1,0:T(8,128)S(1)}) custom-call(s32[9,8]{1,0:T(8,128)S(1)} %pad_add_fusion.meta, bf16[480,1032]{1,0:T(8,128)(2,1)S(1)} %get-tuple-element.72.pick, bf16[1032,1536]{1,0:T(8,128)(2,1)S(1)} %get-tuple-element.73.pre), custom_call_target="tpu_custom_call" | custom-call | flops 1 | bytes 1 | tf_op jit(solution)/shard_map/pallas_call | solution.py:329
  45.4 3.2 %shard_map.84 = (bf16[576,512]{1,0:T(8,128)(2,1)S(1)}, f32[576,512]{1,0:T(8,128)S(1)}) custom-call(s32[9,8]{1,0:T(8,128)S(1)} %pad_add_fusion.meta, bf16[576,1032]{1,0:T(8,128)(2,1)S(1)} %get-tuple-element.76.pick, bf16[1032,1536]{1,0:T(8,128)(2,1)S(1)} %get-tuple-element.73.pre), custom_call_target="tpu_custom_call" | custom-call | flops 1 | bytes 1 | tf_op jit(solution)/shard_map/pallas_call | solution.py:329
  48.6 4.2 %collective-permute-done.8.rest_0_ = bf16[480,512]{1,0:T(8,128)(2,1)S(1)} collective-permute-done((bf16[480,512]{1,0:T(8,128)(2,1)S(1)}, bf16[480,512]{1,0:T(8,128)(2,1)S(1)}, u32[]{:S(2)}, u32[]{:S(2)}) %collective-permute-start.8) | collective-permute-done | bytes 491552 | tf_op jit(solution)/shard_map/ppermute | solution.py:301
  52.9 2.9 %shard_map.85 = (bf16[768,512]{1,0:T(8,128)(2,1)S(1)}, f32[768,512]{1,0:T(8,128)S(1)}) custom-call(s32[9,8]{1,0:T(8,128)S(1)} %pad_add_fusion.meta, bf16[1536,480]{1,0:T(8,128)(2,1)S(1)} %get-tuple-element.94.lhs_moved, bf16[1536,576]{1,0:T(8,128)(2,1)S(1)} %get-tuple-element.95.lhs_kept, bf16[480,1024]{1,0:T(8,128)(2,1)S(1)} %get-tuple-element.86.act_moved, ...), custom_call_target="tpu_custom_call" | custom-call | flops 1 | bytes 1 | tf_op jit(solution)/shard_map/pallas_call | solution.py:345
  58.3 4.1 %collective-permute-start.14 = (bf16[384,512]{1,0:T(8,128)(2,1)S(1)}, bf16[384,512]{1,0:T(8,128)(2,1)S(1)}, u32[]{:S(2)}, u32[]{:S(2)}) collective-permute-start(bf16[384,512]{1,0:T(8,128)(2,1)S(1)} %get-tuple-element.100), channel_id=1, source_target_pairs={{0,8},{4,12},{8,0},{12,4},{16,24},{20,28},{24,16},{28,20},{1,9},{5... | collective-permute-start | bytes 1179656 | tf_op jit(solution)/shard_map/ppermute | solution.py:301
  64.0 3.4 %shard_map.87 = (bf16[576,512]{1,0:T(8,128)(2,1)S(1)}, f32[576,512]{1,0:T(8,128)S(1)}) custom-call(s32[9,8]{1,0:T(8,128)S(1)} %pad_add_fusion.meta, bf16[576,1032]{1,0:T(8,128)(2,1)S(1)} %get-tuple-element.76.pick, bf16[1032,1536]{1,0:T(8,128)(2,1)S(1)} %get-tuple-element.73.pre), custom_call_target="tpu_custom_call" | custom-call | flops 1 | bytes 1 | tf_op jit(solution)/shard_map/pallas_call | solution.py:329
  68.8 2.9 %shard_map.88 = (bf16[384,512]{1,0:T(8,128)(2,1)S(1)}, bf16[384,512]{1,0:T(8,128)(2,1)S(1)}, f32[384,512]{1,0:T(8,128)S(1)}, f32[384,512]{1,0:T(8,128)S(1)}) custom-call(s32[9,8]{1,0:T(8,128)S(1)} %pad_add_fusion.meta, bf16[1536,480]{1,0:T(8,128)(2,1)S(1)} %get-tuple-element.94.lhs_moved, bf16[1536,576]{1,0:T(8,128)(2,1)S(1)} %get-tuple-element.95.lhs_kept, ...), custom_call_target="tpu_custom_call" | custom-call | flops 1 | bytes 1 | tf_op jit(solution)/shard_map/pallas_call | solution.py:345
  76.2 7.1 %collective-permute-start.18 = (bf16[480,512]{1,0:T(8,128)(2,1)S(1)}, bf16[480,512]{1,0:T(8,128)(2,1)S(1)}, u32[]{:S(2)}, u32[]{:S(2)}) collective-permute-start(bf16[480,512]{1,0:T(8,128)(2,1)S(1)} %get-tuple-element.125), channel_id=1, source_target_pairs={{0,16},{4,20},{8,24},{12,28},{16,0},{20,4},{24,8},{28,12},{1,17},{... | collective-permute-start | bytes 1474568 | tf_op jit(solution)/shard_map/ppermute | solution.py:301
  83.3 3.5 %shard_map.89.kept = bf16[528,1536]{1,0:T(8,128)(2,1)S(1)} custom-call(s32[9,8]{1,0:T(8,128)S(1)} %pad_add_fusion.meta, bf16[576,384]{1,0:T(8,128)(2,1)S(1)} %get-tuple-element.78.refs_4_.p0, bf16[576,384]{1,0:T(8,128)(2,1)S(1)} %collective-permute-done.3.refs_5_.p1, bf16[576,384]{1,0:T(8,128)(2,1)S(1)} %collective-permute-done.5.refs_6_.p2, ...), custom_call_target="tpu_custom_call" | custom-call | flops 1 | bytes 1 | tf_op jit(solution)/shard_map/pallas_call | solution.py:352
  86.8 2.9 %shard_map.90.early = bf16[48,1536]{1,0:T(8,128)(2,1)S(1)} custom-call(s32[9,8]{1,0:T(8,128)S(1)} %pad_add_fusion.meta, bf16[48,1920]{1,0:T(8,128)(2,1)S(1)} %collective-permute-done.own, bf16[48,384]{1,0:T(8,128)(2,1)S(1)} %collective-permute-done.11.p1, bf16[48,384]{1,0:T(8,128)(2,1)S(1)} %collective-permute-done.10.p2, ...), custom_call_target="tpu_custom_call" | custom-call | flops 1 | bytes 1 | tf_op jit(solution)/shard_map/pallas_call | solution.py:415
  95.8 11.6 %collective-permute-done.18.rest_2_ = bf16[480,512]{1,0:T(8,128)(2,1)S(1)} collective-permute-done((bf16[480,512]{1,0:T(8,128)(2,1)S(1)}, bf16[480,512]{1,0:T(8,128)(2,1)S(1)}, u32[]{:S(2)}, u32[]{:S(2)}) %collective-permute-start.18) | collective-permute-done | bytes 491552 | tf_op jit(solution)/shard_map/ppermute | solution.py:301
  107.4 9.9 %collective-permute-done.19.got = bf16[384,512]{1,0:T(8,128)(2,1)S(1)} collective-permute-done((bf16[384,512]{1,0:T(8,128)(2,1)S(1)}, bf16[384,512]{1,0:T(8,128)(2,1)S(1)}, u32[]{:S(2)}, u32[]{:S(2)}) %collective-permute-start.19) | collective-permute-done | bytes 393248 | tf_op jit(solution)/shard_map/ppermute | solution.py:301
  118.3 5.2 %collective-permute-done.21.got = bf16[384,512]{1,0:T(8,128)(2,1)S(1)} collective-permute-done((bf16[384,512]{1,0:T(8,128)(2,1)S(1)}, bf16[384,512]{1,0:T(8,128)(2,1)S(1)}, u32[]{:S(2)}, u32[]{:S(2)}) %collective-permute-start.21) | collective-permute-done | bytes 393248 | tf_op jit(solution)/shard_map/ppermute | solution.py:301
  124.4 3.3 %shard_map.96 = bf16[720,1536]{1,0:T(8,128)(2,1)} custom-call(s32[9,8]{1,0:T(8,128)S(1)} %pad_add_fusion.meta, bf16[528,1536]{1,0:T(8,128)(2,1)S(1)} %shard_map.89.kept, bf16[48,1536]{1,0:T(8,128)(2,1)S(1)} %shard_map.90.early, bf16[480,512]{1,0:T(8,128)(2,1)S(1)} %collective-permute-done.8.rest_0_, bf16[480,512]{1,0:T(8,128)(2,1)S(1)} %collective-permute-done.13.rest_1_, ...), custom_call_target="tpu_custom_call" | custom-call | flops 1 | bytes 1 | tf_op jit(solution)/shard_map/pallas_call | solution.py:434
  127.7 3.5 %collective-permute-done.22 = bf16[192,512]{1,0:T(8,128)(2,1)S(1)} collective-permute-done((bf16[192,512]{1,0:T(8,128)(2,1)S(1)}, bf16[192,512]{1,0:T(8,128)(2,1)S(1)}, u32[]{:S(2)}, u32[]{:S(2)}) %collective-permute-start.22) | collective-permute-done | bytes 196640 | tf_op jit(solution)/shard_map/ppermute | solution.py:301
  131.3 3.0 %collective-permute-done.23 = bf16[192,512]{1,0:T(8,128)(2,1)S(1)} collective-permute-done((bf16[192,512]{1,0:T(8,128)(2,1)S(1)}, bf16[192,512]{1,0:T(8,128)(2,1)S(1)}, u32[]{:S(2)}, u32[]{:S(2)}) %collective-permute-start.23) | collective-permute-done | bytes 196640 | tf_op jit(solution)/shard_map/ppermute | solution.py:301
  (56 shorter events, 33.2 us)
Async XLA Ops:
  5.8 14.7 %collective-permute-start.3 = (bf16[576,384]{1,0:T(8,128)(2,1)S(1)}, bf16[576,384]{1,0:T(8,128)(2,1)S(1)}, u32[]{:S(2)}, u32[]{:S(2)}) collective-permute-start(bf16[576,384]{1,0:T(8,128)(2,1)S(1)} %get-tuple-element.78.refs_4_.p0), channel_id=1, source_target_pairs={{0,1},{1,0},{2,3},{3,2},{4,5},{5,4},{6,7},{7,6},{8,9},{9,8},{10,11... | collective-permute-start | bytes 1327112 | tf_op jit(solution)/shard_map/ppermute | solution.py:301
  6.3 14.2 %collective-permute-start.2 = (bf16[480,384]{1,0:T(8,128)(2,1)S(1)}, bf16[480,384]{1,0:T(8,128)(2,1)S(1)}, u32[]{:S(2)}, u32[]{:S(2)}) collective-permute-start(bf16[480,384]{1,0:T(8,128)(2,1)S(1)} %get-tuple-element.70.p0.refs_0_), channel_id=1, source_target_pairs={{0,1},{1,0},{2,3},{3,2},{4,5},{5,4},{6,7},{7,6},{8,9},{9,8},{10,11... | collective-permute-start | bytes 1105928 | tf_op jit(solution)/shard_map/ppermute | solution.py:301
  6.4 14.1 %collective-permute-start.1 = (bf16[480,384]{1,0:T(8,128)(2,1)S(1)}, bf16[480,384]{1,0:T(8,128)(2,1)S(1)}, u32[]{:S(2)}, u32[]{:S(2)}) collective-permute-start(bf16[480,384]{1,0:T(8,128)(2,1)S(1)} %get-tuple-element.70.p0.refs_0_), channel_id=1, source_target_pairs={{0,2},{1,3},{2,0},{3,1},{4,6},{5,7},{6,4},{7,5},{8,10},{9,11},{10,... | collective-permute-start | bytes 1105928 | tf_op jit(solution)/shard_map/ppermute | solution.py:301
  9.4 11.2 %collective-permute-start = (bf16[48,1920]{1,0:T(8,128)(2,1)S(1)}, bf16[48,1920]{1,0:T(8,128)(2,1)S(1)}, u32[]{:S(2)}, u32[]{:S(2)}) collective-permute-start(bf16[48,1920]{1,0:T(8,128)(2,1)S(1)} %get-tuple-element.69), channel_id=1, source_target_pairs={{0,16},{4,20},{8,24},{12,28},{16,0},{20,4},{24,8},{28,12},{1,17},{... | collective-permute-start | bytes 552968 | tf_op jit(solution)/shard_map/ppermute | solution.py:301
  11.9 15.7 %collective-permute-start.5 = (bf16[576,384]{1,0:T(8,128)(2,1)S(1)}, bf16[576,384]{1,0:T(8,128)(2,1)S(1)}, u32[]{:S(2)}, u32[]{:S(2)}) collective-permute-start(bf16[576,384]{1,0:T(8,128)(2,1)S(1)} %get-tuple-element.78.refs_4_.p0), channel_id=1, source_target_pairs={{0,2},{1,3},{2,0},{3,1},{4,6},{5,7},{6,4},{7,5},{8,10},{9,11},{10,... | collective-permute-start | bytes 1327112 | tf_op jit(solution)/shard_map/ppermute | solution.py:301
  20.6 1.8 %collective-permute-start.4 = (bf16[480,384]{1,0:T(8,128)(2,1)S(1)}, bf16[480,384]{1,0:T(8,128)(2,1)S(1)}, u32[]{:S(2)}, u32[]{:S(2)}) collective-permute-start(bf16[480,384]{1,0:T(8,128)(2,1)S(1)} %collective-permute-done.1.p2.refs_2_), channel_id=1, source_target_pairs={{0,1},{1,0},{2,3},{3,2},{4,5},{5,4},{6,7},{7,6},{8,9},{9,8},{10,11... | collective-permute-start | bytes 1105928 | tf_op jit(solution)/shard_map/ppermute | solution.py:301
  27.7 2.8 %collective-permute-start.6 = (bf16[576,384]{1,0:T(8,128)(2,1)S(1)}, bf16[576,384]{1,0:T(8,128)(2,1)S(1)}, u32[]{:S(2)}, u32[]{:S(2)}) collective-permute-start(bf16[576,384]{1,0:T(8,128)(2,1)S(1)} %collective-permute-done.5.refs_6_.p2), channel_id=1, source_target_pairs={{0,1},{1,0},{2,3},{3,2},{4,5},{5,4},{6,7},{7,6},{8,9},{9,8},{10,11... | collective-permute-start | bytes 1327112 | tf_op jit(solution)/shard_map/ppermute | solution.py:301
  27.7 25.2 %collective-permute-start.8 = (bf16[480,512]{1,0:T(8,128)(2,1)S(1)}, bf16[480,512]{1,0:T(8,128)(2,1)S(1)}, u32[]{:S(2)}, u32[]{:S(2)}) collective-permute-start(bf16[480,512]{1,0:T(8,128)(2,1)S(1)} %shard_map.80), channel_id=1, source_target_pairs={{0,16},{4,20},{8,24},{12,28},{16,0},{20,4},{24,8},{28,12},{1,17},{... | collective-permute-start | bytes 1474568 | tf_op jit(solution)/shard_map/ppermute | solution.py:301
  33.4 12.0 %collective-permute-start.7 = (bf16[384,512]{1,0:T(8,128)(2,1)S(1)}, bf16[384,512]{1,0:T(8,128)(2,1)S(1)}, u32[]{:S(2)}, u32[]{:S(2)}) collective-permute-start(bf16[384,512]{1,0:T(8,128)(2,1)S(1)} %get-tuple-element.90), channel_id=1, source_target_pairs={{0,4},{4,0},{8,12},{12,8},{16,20},{20,16},{24,28},{28,24},{1,5},{5... | collective-permute-start | bytes 1179656 | tf_op jit(solution)/shard_map/ppermute | solution.py:301
  35.0 22.4 %collective-permute-start.9 = (bf16[384,512]{1,0:T(8,128)(2,1)S(1)}, bf16[384,512]{1,0:T(8,128)(2,1)S(1)}, u32[]{:S(2)}, u32[]{:S(2)}) collective-permute-start(bf16[384,512]{1,0:T(8,128)(2,1)S(1)} %get-tuple-element.99), channel_id=1, source_target_pairs={{0,4},{4,0},{8,12},{12,8},{16,20},{20,16},{24,28},{28,24},{1,5},{5... | collective-permute-start | bytes 1179656 | tf_op jit(solution)/shard_map/ppermute | solution.py:301
  55.8 35.1 %collective-permute-start.15 = (bf16[768,512]{1,0:T(8,128)(2,1)S(1)}, bf16[768,512]{1,0:T(8,128)(2,1)S(1)}, u32[]{:S(2)}, u32[]{:S(2)}) collective-permute-start(bf16[768,512]{1,0:T(8,128)(2,1)S(1)} %get-tuple-element.96), channel_id=1, source_target_pairs={{0,4},{4,0},{8,12},{12,8},{16,20},{20,16},{24,28},{28,24},{1,5},{5... | collective-permute-start | bytes 2359304 | tf_op jit(solution)/shard_map/ppermute | solution.py:301
  57.4 33.5 %collective-permute-start.13 = (bf16[480,512]{1,0:T(8,128)(2,1)S(1)}, bf16[480,512]{1,0:T(8,128)(2,1)S(1)}, u32[]{:S(2)}, u32[]{:S(2)}) collective-permute-start(bf16[480,512]{1,0:T(8,128)(2,1)S(1)} %get-tuple-element.112), channel_id=1, source_target_pairs={{0,16},{4,20},{8,24},{12,28},{16,0},{20,4},{24,8},{28,12},{1,17},{... | collective-permute-start | bytes 1474568 | tf_op jit(solution)/shard_map/ppermute | solution.py:301
  58.3 17.9 %collective-permute-start.14 = (bf16[384,512]{1,0:T(8,128)(2,1)S(1)}, bf16[384,512]{1,0:T(8,128)(2,1)S(1)}, u32[]{:S(2)}, u32[]{:S(2)}) collective-permute-start(bf16[384,512]{1,0:T(8,128)(2,1)S(1)} %get-tuple-element.100), channel_id=1, source_target_pairs={{0,8},{4,12},{8,0},{12,4},{16,24},{20,28},{24,16},{28,20},{1,9},{5... | collective-permute-start | bytes 1179656 | tf_op jit(solution)/shard_map/ppermute | solution.py:301
  62.4 5.0 %collective-permute-start.10 = (bf16[48,384]{1,0:T(8,128)(2,1)S(1)}, bf16[48,384]{1,0:T(8,128)(2,1)S(1)}, u32[]{:S(2)}, u32[]{:S(2)}) collective-permute-start(bf16[48,384]{1,0:T(8,128)(2,1)S(1)} %slice.4), channel_id=1, source_target_pairs={{0,2},{1,3},{2,0},{3,1},{4,6},{5,7},{6,4},{7,5},{8,10},{9,11},{10,... | collective-permute-start | bytes 110600 | tf_op jit(solution)/shard_map/ppermute | solution.py:301
  63.9 3.5 %collective-permute-start.11 = (bf16[48,384]{1,0:T(8,128)(2,1)S(1)}, bf16[48,384]{1,0:T(8,128)(2,1)S(1)}, u32[]{:S(2)}, u32[]{:S(2)}) collective-permute-start(bf16[48,384]{1,0:T(8,128)(2,1)S(1)} %slice.4), channel_id=1, source_target_pairs={{0,1},{1,0},{2,3},{3,2},{4,5},{5,4},{6,7},{7,6},{8,9},{9,8},{10,11... | collective-permute-start | bytes 110600 | tf_op jit(solution)/shard_map/ppermute | solution.py:301
  67.4 1.4 %collective-permute-start.12 = (bf16[48,384]{1,0:T(8,128)(2,1)S(1)}, bf16[48,384]{1,0:T(8,128)(2,1)S(1)}, u32[]{:S(2)}, u32[]{:S(2)}) collective-permute-start(bf16[48,384]{1,0:T(8,128)(2,1)S(1)} %collective-permute-done.10.p2), channel_id=1, source_target_pairs={{0,1},{1,0},{2,3},{3,2},{4,5},{5,4},{6,7},{7,6},{8,9},{9,8},{10,11... | collective-permute-start | bytes 110600 | tf_op jit(solution)/shard_map/ppermute | solution.py:301
  71.7 22.4 %collective-permute-start.16 = (bf16[384,512]{1,0:T(8,128)(2,1)S(1)}, bf16[384,512]{1,0:T(8,128)(2,1)S(1)}, u32[]{:S(2)}, u32[]{:S(2)}) collective-permute-start(bf16[384,512]{1,0:T(8,128)(2,1)S(1)} %get-tuple-element.121), channel_id=1, source_target_pairs={{0,4},{4,0},{8,12},{12,8},{16,20},{20,16},{24,28},{28,24},{1,5},{5... | collective-permute-start | bytes 1179656 | tf_op jit(solution)/shard_map/ppermute | solution.py:301
  72.3 21.8 %collective-permute-start.17 = (bf16[384,512]{1,0:T(8,128)(2,1)S(1)}, bf16[384,512]{1,0:T(8,128)(2,1)S(1)}, u32[]{:S(2)}, u32[]{:S(2)}) collective-permute-start(bf16[384,512]{1,0:T(8,128)(2,1)S(1)} %get-tuple-element.122), channel_id=1, source_target_pairs={{0,4},{4,0},{8,12},{12,8},{16,20},{20,16},{24,28},{28,24},{1,5},{5... | collective-permute-start | bytes 1179656 | tf_op jit(solution)/shard_map/ppermute | solution.py:301
  76.2 31.2 %collective-permute-start.18 = (bf16[480,512]{1,0:T(8,128)(2,1)S(1)}, bf16[480,512]{1,0:T(8,128)(2,1)S(1)}, u32[]{:S(2)}, u32[]{:S(2)}) collective-permute-start(bf16[480,512]{1,0:T(8,128)(2,1)S(1)} %get-tuple-element.125), channel_id=1, source_target_pairs={{0,16},{4,20},{8,24},{12,28},{16,0},{20,4},{24,8},{28,12},{1,17},{... | collective-permute-start | bytes 1474568 | tf_op jit(solution)/shard_map/ppermute | solution.py:301
  91.8 25.6 %collective-permute-start.19 = (bf16[384,512]{1,0:T(8,128)(2,1)S(1)}, bf16[384,512]{1,0:T(8,128)(2,1)S(1)}, u32[]{:S(2)}, u32[]{:S(2)}) collective-permute-start(bf16[384,512]{1,0:T(8,128)(2,1)S(1)} %get-tuple-element.115), channel_id=1, source_target_pairs={{0,8},{4,12},{8,0},{12,4},{16,24},{20,28},{24,16},{28,20},{1,9},{5... | collective-permute-start | bytes 1179656 | tf_op jit(solution)/shard_map/ppermute | solution.py:301
  94.0 24.3 %collective-permute-start.20 = (bf16[192,512]{1,0:T(8,128)(2,1)S(1)}, bf16[192,512]{1,0:T(8,128)(2,1)S(1)}, u32[]{:S(2)}, u32[]{:S(2)}) collective-permute-start(bf16[192,512]{1,0:T(8,128)(2,1)S(1)} %get-tuple-element.118), channel_id=1, source_target_pairs={{0,16},{4,20},{8,24},{12,28},{16,0},{20,4},{24,8},{28,12},{1,17},{... | collective-permute-start | bytes 589832 | tf_op jit(solution)/shard_map/ppermute | solution.py:301
  95.0 28.5 %collective-permute-start.21 = (bf16[384,512]{1,0:T(8,128)(2,1)S(1)}, bf16[384,512]{1,0:T(8,128)(2,1)S(1)}, u32[]{:S(2)}, u32[]{:S(2)}) collective-permute-start(bf16[384,512]{1,0:T(8,128)(2,1)S(1)} %get-tuple-element.123), channel_id=1, source_target_pairs={{0,8},{4,12},{8,0},{12,4},{16,24},{20,28},{24,16},{28,20},{1,9},{5... | collective-permute-start | bytes 1179656 | tf_op jit(solution)/shard_map/ppermute | solution.py:301
  118.2 13.1 %collective-permute-start.22 = (bf16[192,512]{1,0:T(8,128)(2,1)S(1)}, bf16[192,512]{1,0:T(8,128)(2,1)S(1)}, u32[]{:S(2)}, u32[]{:S(2)}) collective-permute-start(bf16[192,512]{1,0:T(8,128)(2,1)S(1)} %get-tuple-element.128), channel_id=1, source_target_pairs={{0,16},{4,20},{8,24},{12,28},{16,0},{20,4},{24,8},{28,12},{1,17},{... | collective-permute-start | bytes 589832 | tf_op jit(solution)/shard_map/ppermute | solution.py:301
  124.3 10.0 %collective-permute-start.23 = (bf16[192,512]{1,0:T(8,128)(2,1)S(1)}, bf16[192,512]{1,0:T(8,128)(2,1)S(1)}, u32[]{:S(2)}, u32[]{:S(2)}) collective-permute-start(bf16[192,512]{1,0:T(8,128)(2,1)S(1)} %get-tuple-element.131), channel_id=1, source_target_pairs={{0,16},{4,20},{8,24},{12,28},{16,0},{20,4},{24,8},{28,12},{1,17},{... | collective-permute-start | bytes 589832 | tf_op jit(solution)/shard_map/ppermute | solution.py:301
  (2 other events, 30.8 us)

commit v15 on v12

--- a/solution.py
+++ b/solution.py
@@ -97,18 +97,23 @@
     return (rows * own[None, :]).astype(BF)
 
 
-def first_kernel(meta, cot_hbm, scale_hbm, moved_out, kept_out, cot, scale, sems):
+def first_kernel(
+    meta, cot_hbm, scale_hbm, pre_hbm, moved_out, kept_out, moved_pick, kept_pick, pre, cot, scale, sems
+):
     home = cot.shape[0]
-    pairs = ((cot_hbm, cot), (scale_hbm, scale))
+    pairs = ((cot_hbm, cot), (scale_hbm, scale), (pre_hbm, pre))
     copies = [pltpu.make_async_copy(a, b, sems.at[i]) for i, (a, b) in enumerate(pairs)]
     for copy in copies:
         copy.start()
     moved = moved_picks(meta, home)
     kept = kept_picks(meta, home)
-    for copy in copies:
-        copy.wait()
+    moved_pick[...] = moved
+    kept_pick[...] = kept
+    copies[0].wait()
+    copies[1].wait()
     moved_out[...] = scaled_rows(meta, moved, cot, scale)
     kept_out[...] = scaled_rows(meta, kept, cot, scale)
+    copies[2].wait()
 
 
 def gelu_and_slope(x):
@@ -122,62 +127,35 @@
     ]
 
 
-def gelu_kernel(moved, base, block, meta, pre_hbm, act_out, der_out, pick, rows_f32, pre, sems):
-    home = pre.shape[1]
+def gelu_kernel(base, block, meta, pick, pre, act_out, der_out, rows_f32):
     rows = pick.shape[0]
-    blocks = cut_at((act_out.shape[1],), block)
-    copies = [
-        pltpu.make_async_copy(
-            pre_hbm.at[:, pl.ds(base + at, wide)], pre.at[i, :, pl.ds(0, wide)], sems.at[i]
-        )
-        for i, (_, at, wide) in enumerate(blocks)
-    ]
-    for copy in copies:
-        copy.start()
-    pick[...] = moved_picks(meta, home) if moved else kept_picks(meta, home)
     step = next(TILE * k for k in (3, 4, 2, 1) if rows % (TILE * k) == 0)
-    for i, (_, at, wide) in enumerate(blocks):
-        copies[i].wait()
-        rows_f32[:, 0:wide] = jnp.dot(pick[...], pre[i, :, 0:wide], preferred_element_type=F32)
-        columns = slice(at, at + wide)
+    for at in range(0, act_out.shape[1], block):
+        source = slice(base + at, base + at + block)
+        rows_f32[...] = jnp.dot(pick[...], pre[:, source], preferred_element_type=F32)
+        columns = slice(at, at + block)
 
         def body(k, _):
-            rows = pl.ds(pl.multiple_of(k * step, step), step)
-            value, slope = gelu_and_slope(rows_f32[rows, 0:wide])
-            act_out[rows, columns] = value.astype(BF)
-            der_out[rows, columns] = slope
+            part = pl.ds(pl.multiple_of(k * step, step), step)
+            value, slope = gelu_and_slope(rows_f32[part, :])
+            act_out[part, columns] = value.astype(BF)
+            der_out[part, columns] = slope
             return 0
 
         lax.fori_loop(0, rows // step, body, 0)
 
 
-def grad_kernel(base, slope_count, block, meta, p0, p1, p2, p3, weight_hbm, *rest):
-    slopes, outs, (lhs, weight, sems) = rest[:slope_count], rest[slope_count:-3], rest[-3:]
-    parts = slopes if slope_count > len(outs) else outs
-    starts = [sum(part.shape[1] for part in parts[:i]) for i in range(len(parts))]
-    blocks = cut_at([part.shape[1] for part in parts], block)
-    copies = [
-        pltpu.make_async_copy(
-            weight_hbm.at[:, pl.ds(base + starts[i] + c, wide)], weight.at[k, :, pl.ds(0, wide)], sems.at[k]
-        )
-        for k, (i, c, wide) in enumerate(blocks)
-    ]
-    for copy in copies:
-        copy.start()
+def grad_kernel(slope_count, block, meta, p0, p1, p2, p3, weight, *rest):
+    slopes, (out, lhs) = rest[:slope_count], rest[slope_count:]
     width = p0.shape[1]
     for j, piece in enumerate((p0, p1, p2, p3)):
         lhs[:, pl.ds(pl.multiple_of((tensor_at(meta) ^ j) * width, 128), width)] = piece[...]
-    for k, (i, c, wide) in enumerate(blocks):
-        at = starts[i] + c
-        inside, whole_at = slice(c, c + wide), slice(at, at + wide)
-        slope = slopes[i][:, inside] if slope_count == len(parts) else slopes[0][:, whole_at]
-        copies[k].wait()
-        value = jnp.dot(lhs[...], weight[k, :, 0:wide], preferred_element_type=F32)
-        value = (value * slope).astype(BF)
-        if len(outs) == len(parts):
-            outs[i][:, inside] = value
-        else:
-            outs[0][:, whole_at] = value
+    at = 0
+    for i, c, wide in cut_at([slope.shape[1] for slope in slopes], block):
+        columns = slice(at, at + wide)
+        value = jnp.dot(lhs[...], weight[:, columns], preferred_element_type=F32)
+        out[:, columns] = (value * slopes[i][:, c : c + wide]).astype(BF)
+        at += wide
 
 
 def weight_kernel(count, meta, *refs):
@@ -247,22 +225,26 @@
     lax.fori_loop(0, half // step, body, 0)
 
 
-def place_kernel(cuts, meta, kept, *rest):
-    moved, out = rest[:-1], rest[-1]
-    count = kept_total(meta, dp_at(meta))
+def place_kernel(meta, kept, inner, *rest):
+    outer, out = rest[:-1], rest[-1]
+    d = dp_at(meta)
+    count = kept_total(meta, d)
     first = jnp.minimum(count - lax.rem(count, TILE), BAL - SEND)
     first = pl.multiple_of(first, TILE)
     wide = out.shape[1]
     step = pl.program_id(0)
-    out[0:KEEP, :] = kept[:, pl.ds(pl.multiple_of(step * wide, wide), wide)]
+    columns = pl.ds(pl.multiple_of(step * wide, wide), wide)
+    out[0:KEEP, :] = kept[:, columns]
     out[KEEP:, :] = jnp.zeros((out.shape[0] - KEEP, wide), BF)
     rows = lax.broadcasted_iota(jnp.int32, (SEND, 1), 0) + first
     window = pl.ds(first, SEND)
-    for i, (part, c, _) in enumerate(cut_at(cuts, wide)):
+    is_inner = (d // 2 == 1) | (d // 2 == 2)
+    for i, (part, c, _) in enumerate(cut_at([x.shape[1] for x in outer], wide)):
 
         @pl.when(step == i)
         def _():
-            out[window, :] = jnp.where(rows < count, out[window, :], moved[part][:, c : c + wide])
+            block = jnp.where(is_inner, inner[:, columns], outer[part][:, c : c + wide])
+            out[window, :] = jnp.where(rows < count, out[window, :], block)
 
 
 def swapped(block, axis, distance):
@@ -270,14 +252,17 @@
     return lax.ppermute(block, axis, [(i, i ^ distance) for i in range(n)])
 
 
+def routed(block, pairs):
+    return lax.ppermute(block, "dp", [(2 * a + x, 2 * b + x) for a, b in pairs for x in range(2)])
+
+
 def after(value, *others):
     return lax.optimization_barrier((value, *others))[0]
 
 
 def shards(hidden_pre, cotangent, down_weight, layer_scale, crop_lengths, crop_moves):
-    hidden_pre, cotangent, down_weight, layer_scale = (
-        pltpu.with_memory_space_constraint(x, pltpu.HBM)
-        for x in (hidden_pre, cotangent, down_weight, layer_scale)
+    hidden_pre, cotangent, layer_scale = (
+        pltpu.with_memory_space_constraint(x, pltpu.HBM) for x in (hidden_pre, cotangent, layer_scale)
     )
     home, ff = hidden_pre.shape
     width = cotangent.shape[1]
@@ -293,41 +278,33 @@
     vmem = pltpu.VMEM
     sems = pltpu.SemaphoreType.DMA
 
-    def gelu(meta, moved, base, columns):
-        block = 256
-        rows = SEND if moved else KEEP
-        count = pl.cdiv(columns, block)
-        return kernel_call(
-            functools.partial(gelu_kernel, moved, base, block),
+    def gelu(meta, pick, base, columns):
+        rows, block = pick.shape[0], 256
+        return kernel_call(
+            functools.partial(gelu_kernel, base, block),
             [shape(rows, columns), shape(rows, columns, F32)],
-            [IN_HBM], [IN_VMEM] * 2,
-            [vmem((rows, home), BF), vmem((rows, block), F32), vmem((count, home, block), BF), sems((count,))],
-        )(meta, hidden_pre)
+            [IN_VMEM] * 2, [IN_VMEM] * 2, [vmem((rows, block), F32)],
+        )(meta, pick, pre)
 
     def weight_first(meta, act_moved, act_kept):
         return kernel_call(
             functools.partial(weight_kernel, 4),
-            [shape(width, part)] * 2 + [shape(width, part, F32)] * 2
+            [shape(features // 2, part), shape(features // 2, part, F32)]
             + [shape(features, SEND), shape(features, KEEP)],
-            [IN_VMEM] * 10, [IN_VMEM] * 6,
+            [IN_VMEM] * 10, [IN_VMEM] * 4,
         )(meta, *moved, *kept, act_moved, act_kept)
 
-    def weight_again(meta, base, act_moved, act_kept, count):
-        rows = features // 2 // count
+    def weight_again(meta, base, act_moved, act_kept):
         return kernel_call(
             functools.partial(again_kernel, base),
-            [shape(rows, part)] * count + [shape(rows, part, F32)] * count,
-            [IN_VMEM] * 4, [IN_VMEM] * (2 * count),
+            [shape(features // 2, part), shape(features // 2, part, F32)], [IN_VMEM] * 4, [IN_VMEM] * 2,
         )(meta, *lhs, act_moved, act_kept)
 
-    def grads(meta, pieces, base, slopes, cuts):
-        rows, block = pieces[0].shape[0], 256
-        count = sum(cuts) // block
-        return kernel_call(
-            functools.partial(grad_kernel, base, len(slopes), block),
-            [shape(rows, c) for c in cuts],
-            [IN_VMEM] * 4 + [IN_HBM] + [IN_VMEM] * len(slopes), [IN_VMEM] * len(cuts),
-            [vmem((rows, features), BF), vmem((count, features, block), BF), sems((count,))],
+    def grads(meta, pieces, slopes):
+        rows = pieces[0].shape[0]
+        return kernel_call(
+            functools.partial(grad_kernel, len(slopes), 256), shape(rows, ff),
+            [IN_VMEM] * (5 + len(slopes)), IN_VMEM, [vmem((rows, features), BF)],
         )(meta, *pieces, down_weight, *slopes)
 
     def near_step(meta, keeps, gots):
@@ -342,61 +319,62 @@
             far_kernel, [shape(half, part), shape(half, part, F32)], [IN_VMEM] * 2, [IN_VMEM] * 2
         )(meta, mine, got)
 
-    moved_0, kept_0 = kernel_call(
-        first_kernel, [shape(SEND, width), shape(KEEP, width)], [IN_HBM] * 2, [IN_VMEM] * 2,
-        [vmem((home, width), BF), vmem((features,), F32), sems((2,))],
-    )(meta, cotangent, layer_scale)
+    moved_0, kept_0, moved_pick, kept_pick, pre = kernel_call(
+        first_kernel,
+        [shape(SEND, width), shape(KEEP, width), shape(SEND, home), shape(KEEP, home), shape(home, ff)],
+        [IN_HBM] * 3, [IN_VMEM] * 5,
+        [vmem((home, width), BF), vmem((features,), F32), sems((3,))],
+    )(meta, cotangent, layer_scale, hidden_pre)
 
     moved_1, moved_2 = swapped(moved_0, "tensor", 1), swapped(moved_0, "tensor", 2)
     kept_1, kept_2 = swapped(kept_0, "tensor", 1), swapped(kept_0, "tensor", 2)
-    act_ma, der_ma = gelu(after(meta, moved_0), True, 0, part)
-    moved_2 = after(moved_2, act_ma, moved_1, kept_1)
+    act_m, der_m = gelu(after(meta, moved_0), moved_pick, 0, ff)
+    moved_2 = after(moved_2, act_m, moved_1, kept_1)
     moved_3 = swapped(moved_2, "tensor", 1)
     moved = (moved_0, moved_1, moved_2, moved_3)
 
-    (moving_a,) = grads(after(meta, moved_2), moved, 0, (der_ma,), (part,))
-    arrived_a = swapped(moving_a, "dp", n // 2)
-
-    act_ka, der_ka = gelu(after(meta, moving_a), False, 0, part)
+    moving = grads(after(meta, moved_2), moved, (der_m,))
+    to_inner, across, to_outer = ((0, 1), (3, 2)), ((1, 2), (2, 1)), ((1, 0), (2, 3))
+    relayed = routed(moving, to_inner)
+    crossed = routed(moving, across)
+
+    act_ka, der_ka = gelu(after(meta, moving), kept_pick, 0, part)
     kept_2 = after(kept_2, act_ka)
     kept_3 = swapped(kept_2, "tensor", 1)
     kept = (kept_0, kept_1, kept_2, kept_3)
-    *sends_a, keep_01, keep_23, lhs_moved, lhs_kept = weight_first(after(meta, act_ka), act_ma, act_ka)
-    lhs = (lhs_moved, lhs_kept)
-    gots_a = [swapped(send, "dp", 1) for send in sends_a]
-
-    act_m, der_m = gelu(after(meta, keep_01), True, part, 2 * part)
-    moving_b, moving_c = grads(after(meta, act_m), moved, part, (der_m,), (part, part))
-    act_kb, der_kb = gelu(after(meta, moving_b), False, part, part)
-    send_b, keep_b = weight_again(after(meta, act_kb, arrived_a), 0, act_m, act_kb, 1)
+    send_a, keep_a, *lhs = weight_first(after(meta, act_ka), act_m, act_ka)
+    got_a = swapped(send_a, "dp", 1)
+    act_kb, der_kb = gelu(after(meta, send_a), kept_pick, part, part)
+    send_b, keep_b = weight_again(after(meta, act_kb), part, act_m, act_kb)
     got_b = swapped(send_b, "dp", 1)
-    arrived_b = swapped(after(moving_b, send_b), "dp", n // 2)
-
-    out_na, mine_a = near_step(after(meta, send_b), (keep_01, keep_23), gots_a)
+    act_kc, der_kc = gelu(after(meta, send_b), kept_pick, 2 * part, part)
+    send_c, keep_c = weight_again(after(meta, act_kc), 2 * part, act_m, act_kc)
+    kept_grad = grads(after(meta, send_c), kept, (der_ka, der_kb, der_kc))
+
+    out_na, mine_a = near_step(after(meta, kept_grad, relayed, crossed), (keep_a,), (got_a,))
     got_na = swapped(out_na, "dp", 2)
-    act_kc, der_kc = gelu(after(meta, out_na), False, 2 * part, part)
-    *sends_c, keep_c01, keep_c23 = weight_again(after(meta, act_kc), part, act_m, act_kc, 2)
-    gots_c = [swapped(send, "dp", 1) for send in sends_c]
-    (kept_grad,) = grads(after(meta, keep_c01), kept, 0, (der_ka, der_kb, der_kc), (ff,))
-
-    out_nb, mine_b = near_step(after(meta, kept_grad, arrived_b, got_na), (keep_b,), (got_b,))
+    inner = routed(after(relayed, out_na), across)
+    outer_a = routed(after(crossed[:, :part], got_na), to_outer)
+    out_fa, own_a = far_step(after(meta, out_na), mine_a, got_na)
+    got_fa = swapped(out_fa, "dp", 4)
+    out_nb, mine_b = near_step(after(meta, out_fa, outer_a), (keep_b,), (got_b,))
     got_nb = swapped(out_nb, "dp", 2)
-    arrived_c = swapped(after(moving_c, out_nb), "dp", n // 2)
-    out_fa, own_a = far_step(after(meta, out_nb), mine_a, got_na)
-    got_fa = swapped(out_fa, "dp", 4)
-    out_nc, mine_c = near_step(after(meta, out_fa), (keep_c01, keep_c23), gots_c)
+    got_c = swapped(after(send_c, out_nb), "dp", 1)
+    outer_b = routed(after(crossed[:, part : 2 * part], out_nb), to_outer)
+    out_nc, mine_c = near_step(after(meta, out_nb), (keep_c,), (got_c,))
     got_nc = swapped(out_nc, "dp", 2)
-    out_fb, own_b = far_step(after(meta, out_nc), mine_b, got_nb)
+    outer_c = routed(after(crossed[:, 2 * part :], out_nc), to_outer)
+    out_fb, own_b = far_step(after(meta, out_nc, got_fa), mine_b, got_nb)
     got_fb = swapped(out_fb, "dp", 4)
-    out_fc, own_c = far_step(after(meta, out_fb, got_fa, arrived_c), mine_c, got_nc)
+    out_fc, own_c = far_step(after(meta, out_fb, inner, outer_b), mine_c, got_nc)
     got_fc = swapped(out_fc, "dp", 4)
     total = [a + b.astype(F32) for a, b in ((own_a, got_fa), (own_b, got_fb), (own_c, got_fc))]
     down_grad = jnp.concatenate(total, axis=1) / math.sqrt(n * home)
 
     hidden_grad = kernel_call(
-        functools.partial(place_kernel, (part,) * 3), shape(BAL, ff), [IN_VMEM] * 4,
+        place_kernel, shape(BAL, ff), [IN_VMEM] * 5,
         pl.BlockSpec((BAL, 256), lambda i, *_: (0, i)), grid=(ff // 256,),
-    )(after(meta, out_fc), kept_grad, arrived_a, arrived_b, arrived_c)
+    )(after(meta, out_fc), kept_grad, inner, outer_a, outer_b, outer_c)
     return (hidden_grad, down_grad)
 
 

time: 140 us -> 152 us (1.086)
  waiting for transfers between devices: 51.3 us -> 74.7 us
  Pallas kernels: 62.7 us -> 46.1 us
  starting transfers between devices: 22.8 us -> 27.8 us
    pallas_call x13 -> x11, Pallas kernels: 57.3 us -> 40.8 us  [the longest x4 16.8 us: gelu(): kernel_call(functools.partial(gelu_kernel, base, block), [shape(rows, col...]
    ppermute x0 -> x6, waiting for transfers between devices: none -> 15.9 us  [routed(): lax.ppermute(block, 'dp', [(2 * a + x, 2 * b + x) for a, b in pairs for x...]
    ppermute x0 -> x6, starting transfers between devices: none -> 9.36 us  [routed(): lax.ppermute(block, 'dp', [(2 * a + x, 2 * b + x) for a, b in pairs for x...]
    ppermute x20 -> x15, waiting for transfers between devices: 51.3 us -> 58.8 us  [swapped(): return lax.ppermute(block, axis, [(i, i ^ distance) for i in range(n)])]
    ppermute x20 -> x15, starting transfers between devices: 22.8 us -> 18.5 us  [swapped(): return lax.ppermute(block, axis, [(i, i ^ distance) for i in range(n)])]
  transfers between devices with their start and end apart: 20 -> 21, of which waited for: 7 -> 11; matrix products, arithmetic and copies ran while one was open for 0% -> 0% of each run, Pallas kernels for 42% -> 25%
where the time goes in v15:
time: 152 us
  waiting for transfers between devices  74.7 us (49%)
  Pallas kernels  46.1 us (30%)
  starting transfers between devices  27.8 us (18%)
  other arithmetic  1.97 us (1%)
    ppermute x15, waiting for transfers between devices, swapped(): return lax.ppermute(block, axis, [(i, i ^ distance) for i in range(n)])  58.8 us
    ppermute x15, starting transfers between devices, swapped(): return lax.ppermute(block, axis, [(i, i ^ distance) for i in range(n)])  18.5 us
    pallas_call x4, Pallas kernels, gelu(): kernel_call(functools.partial(gelu_kernel, base, block), [shape(rows, col...  16.8 us
    ppermute x6, waiting for transfers between devices, routed(): lax.ppermute(block, 'dp', [(2 * a + x, 2 * b + x) for a, b in pairs for x...  15.9 us
    ppermute x6, starting transfers between devices, routed(): lax.ppermute(block, 'dp', [(2 * a + x, 2 * b + x) for a, b in pairs for x...  9.36 us
    pallas_call x2, Pallas kernels, grads(): kernel_call(functools.partial(grad_kernel, len(slopes), 256), shape(rows,...  6.96 us
    pallas_call x2, Pallas kernels, weight_again(): kernel_call(functools.partial(again_kernel, base), [shape(features // 2,...  6.52 us
    pallas_call x1, Pallas kernels, shards(): kernel_call(first_kernel, [shape(SEND, width), shape(KEEP, width), shape(...  3.73 us
  transfers between devices with their start and end apart: 21, of which 11 were waited for; matrix products, arithmetic and copies ran while one was open for 0% of the time, Pallas kernels for 25%

profile of v15, /device:TPU:0, one launch (start us, length us, event | category | flops | bytes accessed | tf_op | source)
XLA Modules:
  0.0 151.6 jit_solution(3122260215245849680)
XLA Ops:
  1.4 3.7 %shard_map.77 = (bf16[528,384]{1,0:T(8,128)(2,1)S(1)}, bf16[528,384]{1,0:T(8,128)(2,1)S(1)}, bf16[528,1032]{1,0:T(8,128)(2,1)S(1)}, bf16[528,1032]{1,0:T(8,128)(2,1)S(1)}, bf16[1032,1536]{1,0:T(8,128)(2,1)S(1)}) custom-call(s32[9,8]{1,0:T(8,128)S(1)} %pad_add_fusion.meta, bf16[1032,384]{1,0:T(8,128)(2,1)} %cot_hbm.1, f32[1536]{0:T(1024)} %scale_hbm.1, ...), custom_call_target="tpu_custom_call" | custom-call | flops 1 | bytes 1 | tf_op jit(solution)/shard_map/pallas_call | solution.py:322
  5.7 2.9 %collective-permute-start = (bf16[528,384]{1,0:T(8,128)(2,1)S(1)}, bf16[528,384]{1,0:T(8,128)(2,1)S(1)}, u32[]{:S(2)}, u32[]{:S(2)}) collective-permute-start(bf16[528,384]{1,0:T(8,128)(2,1)S(1)} %get-tuple-element.58.p0.refs_0_), channel_id=1, source_target_pairs={{0,2},{1,3},{2,0},{3,1},{4,6},{5,7},{6,4},{7,5},{8,10},{9,11},{10,... | collective-permute-start | bytes 1216520 | tf_op jit(solution)/shard_map/ppermute | solution.py:252
  8.6 7.8 %shard_map.78 = (bf16[528,1536]{1,0:T(8,128)(2,1)S(1)}, f32[528,1536]{1,0:T(8,128)S(1)}) custom-call(s32[9,8]{1,0:T(8,128)S(1)} %pad_add_fusion.meta, bf16[528,1032]{1,0:T(8,128)(2,1)S(1)} %get-tuple-element.60.pick, bf16[1032,1536]{1,0:T(8,128)(2,1)S(1)} %get-tuple-element.61.pre), custom_call_target="tpu_custom_call" | custom-call | flops 1 | bytes 1 | tf_op jit(solution)/shard_map/pallas_call | solution.py:283
  20.0 3.5 %shard_map.79 = bf16[528,1536]{1,0:T(8,128)(2,1)S(1)} custom-call(s32[9,8]{1,0:T(8,128)S(1)} %pad_add_fusion.meta, bf16[528,384]{1,0:T(8,128)(2,1)S(1)} %get-tuple-element.58.p0.refs_0_, bf16[528,384]{1,0:T(8,128)(2,1)S(1)} %collective-permute-done.1.p1.refs_1_, bf16[528,384]{1,0:T(8,128)(2,1)S(1)} %collective-permute-done.p2.refs_2_, ...), custom_call_target="tpu_custom_call" | custom-call | flops 1 | bytes 1 | tf_op jit(solution)/shard_map/pallas_call | solution.py:305
  23.5 3.8 %collective-permute-start.6 = (bf16[528,1536]{1,0:T(8,128)(2,1)S(1)}, bf16[528,1536]{1,0:T(8,128)(2,1)S(1)}, u32[]{:S(2)}, u32[]{:S(2)}) collective-permute-start(bf16[528,1536]{1,0:T(8,128)(2,1)S(1)} %shard_map.79), channel_id=1, source_target_pairs={{0,8},{4,12},{24,16},{28,20},{1,9},{5,13},{25,17},{29,21},{2,10},{... | collective-permute-start | bytes 4866056 | tf_op jit(solution)/shard_map/ppermute | solution.py:256
  29.9 3.0 %shard_map.80 = (bf16[528,512]{1,0:T(8,128)(2,1)S(1)}, f32[528,512]{1,0:T(8,128)S(1)}) custom-call(s32[9,8]{1,0:T(8,128)S(1)} %pad_add_fusion.meta, bf16[528,1032]{1,0:T(8,128)(2,1)S(1)} %get-tuple-element.68.pick, bf16[1032,1536]{1,0:T(8,128)(2,1)S(1)} %get-tuple-element.61.pre), custom_call_target="tpu_custom_call" | custom-call | flops 1 | bytes 1 | tf_op jit(solution)/shard_map/pallas_call | solution.py:283
  32.9 6.6 %collective-permute-done.4.refs_6_.p2 = bf16[528,384]{1,0:T(8,128)(2,1)S(1)} collective-permute-done((bf16[528,384]{1,0:T(8,128)(2,1)S(1)}, bf16[528,384]{1,0:T(8,128)(2,1)S(1)}, u32[]{:S(2)}, u32[]{:S(2)}) %collective-permute-start.4) | collective-permute-done | bytes 405536 | tf_op jit(solution)/shard_map/ppermute | solution.py:252
  41.2 3.3 %shard_map.81 = (bf16[768,512]{1,0:T(8,128)(2,1)S(1)}, f32[768,512]{1,0:T(8,128)S(1)}, bf16[1536,528]{1,0:T(8,128)(2,1)S(1)}, bf16[1536,528]{1,0:T(8,128)(2,1)S(1)}) custom-call(s32[9,8]{1,0:T(8,128)S(1)} %pad_add_fusion.meta, bf16[528,384]{1,0:T(8,128)(2,1)S(1)} %get-tuple-element.58.p0.refs_0_, bf16[528,384]{1,0:T(8,128)(2,1)S(1)} %collective-permute-done.1.p1.refs_1_, ...), custom_call_target="tpu_custom_call" | custom-call | flops 1 | bytes 1 | tf_op jit(solution)/shard_map/pallas_call | solution.py:290
  46.1 3.0 %shard_map.82 = (bf16[528,512]{1,0:T(8,128)(2,1)S(1)}, f32[528,512]{1,0:T(8,128)S(1)}) custom-call(s32[9,8]{1,0:T(8,128)S(1)} %pad_add_fusion.meta, bf16[528,1032]{1,0:T(8,128)(2,1)S(1)} %get-tuple-element.68.pick, bf16[1032,1536]{1,0:T(8,128)(2,1)S(1)} %get-tuple-element.61.pre), custom_call_target="tpu_custom_call" | custom-call | flops 1 | bytes 1 | tf_op jit(solution)/shard_map/pallas_call | solution.py:283
  49.2 3.3 %shard_map.83 = (bf16[768,512]{1,0:T(8,128)(2,1)S(1)}, f32[768,512]{1,0:T(8,128)S(1)}) custom-call(s32[9,8]{1,0:T(8,128)S(1)} %pad_add_fusion.meta, bf16[1536,528]{1,0:T(8,128)(2,1)S(1)} %get-tuple-element.76.lhs_moved, bf16[1536,528]{1,0:T(8,128)(2,1)S(1)} %get-tuple-element.77.lhs_kept, bf16[528,1536]{1,0:T(8,128)(2,1)S(1)} %get-tuple-element.62.refs_8_.act_moved, ...), custom_call_target="tpu_custom_call" | custom-call | flops 1 | bytes 1 | tf_op jit(solution)/shard_map/pallas_call | solution.py:298
  52.4 3.0 %shard_map.84 = (bf16[528,512]{1,0:T(8,128)(2,1)S(1)}, f32[528,512]{1,0:T(8,128)S(1)}) custom-call(s32[9,8]{1,0:T(8,128)S(1)} %pad_add_fusion.meta, bf16[528,1032]{1,0:T(8,128)(2,1)S(1)} %get-tuple-element.68.pick, bf16[1032,1536]{1,0:T(8,128)(2,1)S(1)} %get-tuple-element.61.pre), custom_call_target="tpu_custom_call" | custom-call | flops 1 | bytes 1 | tf_op jit(solution)/shard_map/pallas_call | solution.py:283
  55.5 3.3 %shard_map.85 = (bf16[768,512]{1,0:T(8,128)(2,1)S(1)}, f32[768,512]{1,0:T(8,128)S(1)}) custom-call(s32[9,8]{1,0:T(8,128)S(1)} %pad_add_fusion.meta, bf16[1536,528]{1,0:T(8,128)(2,1)S(1)} %get-tuple-element.76.lhs_moved, bf16[1536,528]{1,0:T(8,128)(2,1)S(1)} %get-tuple-element.77.lhs_kept, bf16[528,1536]{1,0:T(8,128)(2,1)S(1)} %get-tuple-element.62.refs_8_.act_moved, ...), custom_call_target="tpu_custom_call" | custom-call | flops 1 | bytes 1 | tf_op jit(solution)/shard_map/pallas_call | solution.py:298
  58.7 3.5 %shard_map.86.kept = bf16[528,1536]{1,0:T(8,128)(2,1)S(1)} custom-call(s32[9,8]{1,0:T(8,128)S(1)} %pad_add_fusion.meta, bf16[528,384]{1,0:T(8,128)(2,1)S(1)} %get-tuple-element.63.refs_4_.p0, bf16[528,384]{1,0:T(8,128)(2,1)S(1)} %collective-permute-done.2.refs_5_.p1, bf16[528,384]{1,0:T(8,128)(2,1)S(1)} %collective-permute-done.4.refs_6_.p2, ...), custom_call_target="tpu_custom_call" | custom-call | flops 1 | bytes 1 | tf_op jit(solution)/shard_map/pallas_call | solution.py:305
  62.2 2.0 %collective-permute-done.8.refs_1_ = bf16[768,512]{1,0:T(8,128)(2,1)S(1)} collective-permute-done((bf16[768,512]{1,0:T(8,128)(2,1)S(1)}, bf16[768,512]{1,0:T(8,128)(2,1)S(1)}, u32[]{:S(2)}, u32[]{:S(2)}) %collective-permute-start.8) | collective-permute-done | bytes 786464 | tf_op jit(solution)/shard_map/ppermute | solution.py:252
  65.2 2.1 %collective-permute-start.9 = (bf16[384,512]{1,0:T(8,128)(2,1)S(1)}, bf16[384,512]{1,0:T(8,128)(2,1)S(1)}, u32[]{:S(2)}, u32[]{:S(2)}) collective-permute-start(bf16[384,512]{1,0:T(8,128)(2,1)S(1)} %get-tuple-element.89), channel_id=1, source_target_pairs={{0,8},{4,12},{8,0},{12,4},{16,24},{20,28},{24,16},{28,20},{1,9},{5... | collective-permute-start | bytes 1179656 | tf_op jit(solution)/shard_map/ppermute | solution.py:252
  68.9 7.0 %collective-permute-done.9.got = bf16[384,512]{1,0:T(8,128)(2,1)S(1)} collective-permute-done((bf16[384,512]{1,0:T(8,128)(2,1)S(1)}, bf16[384,512]{1,0:T(8,128)(2,1)S(1)}, u32[]{:S(2)}, u32[]{:S(2)}) %collective-permute-start.9) | collective-permute-done | bytes 393248 | tf_op jit(solution)/shard_map/ppermute | solution.py:252
  78.7 11.9 %collective-permute-done.10.rest_0_ = bf16[528,512]{1,0:T(8,128)(2,1)S(1)} collective-permute-done((bf16[528,512]{1,0:T(8,128)(2,1)S(1)}, bf16[528,512]{1,0:T(8,128)(2,1)S(1)}, u32[]{:S(2)}, u32[]{:S(2)}) %collective-permute-start.10) | collective-permute-done | bytes 540704 | tf_op jit(solution)/shard_map/ppermute | solution.py:256
  94.4 3.3 %collective-permute-start.13 = (bf16[192,512]{1,0:T(8,128)(2,1)S(1)}, bf16[192,512]{1,0:T(8,128)(2,1)S(1)}, u32[]{:S(2)}, u32[]{:S(2)}) collective-permute-start(bf16[192,512]{1,0:T(8,128)(2,1)S(1)} %get-tuple-element.92), channel_id=1, source_target_pairs={{0,16},{4,20},{8,24},{12,28},{16,0},{20,4},{24,8},{28,12},{1,17},{... | collective-permute-start | bytes 589832 | tf_op jit(solution)/shard_map/ppermute | solution.py:252
  97.6 11.2 %collective-permute-done.12.refs_1_ = bf16[768,512]{1,0:T(8,128)(2,1)S(1)} collective-permute-done((bf16[768,512]{1,0:T(8,128)(2,1)S(1)}, bf16[768,512]{1,0:T(8,128)(2,1)S(1)}, u32[]{:S(2)}, u32[]{:S(2)}) %collective-permute-start.12) | collective-permute-done | bytes 786464 | tf_op jit(solution)/shard_map/ppermute | solution.py:252
  109.8 15.6 %collective-permute-done.13 = bf16[192,512]{1,0:T(8,128)(2,1)S(1)} collective-permute-done((bf16[192,512]{1,0:T(8,128)(2,1)S(1)}, bf16[192,512]{1,0:T(8,128)(2,1)S(1)}, u32[]{:S(2)}, u32[]{:S(2)}) %collective-permute-start.13) | collective-permute-done | bytes 196640 | tf_op jit(solution)/shard_map/ppermute | solution.py:252
  127.5 3.3 %collective-permute-start.19 = (bf16[192,512]{1,0:T(8,128)(2,1)S(1)}, bf16[192,512]{1,0:T(8,128)(2,1)S(1)}, u32[]{:S(2)}, u32[]{:S(2)}) collective-permute-start(bf16[192,512]{1,0:T(8,128)(2,1)S(1)} %get-tuple-element.103), channel_id=1, source_target_pairs={{0,16},{4,20},{8,24},{12,28},{16,0},{20,4},{24,8},{28,12},{1,17},{... | collective-permute-start | bytes 589832 | tf_op jit(solution)/shard_map/ppermute | solution.py:252
  131.8 11.1 %collective-permute-done.19 = bf16[192,512]{1,0:T(8,128)(2,1)S(1)} collective-permute-done((bf16[192,512]{1,0:T(8,128)(2,1)S(1)}, bf16[192,512]{1,0:T(8,128)(2,1)S(1)}, u32[]{:S(2)}, u32[]{:S(2)}) %collective-permute-start.19) | collective-permute-done | bytes 196640 | tf_op jit(solution)/shard_map/ppermute | solution.py:252
  142.9 4.0 %collective-permute-done.18.rest_2_ = bf16[528,512]{1,0:T(8,128)(2,1)S(1)} collective-permute-done((bf16[528,512]{1,0:T(8,128)(2,1)S(1)}, bf16[528,512]{1,0:T(8,128)(2,1)S(1)}, u32[]{:S(2)}, u32[]{:S(2)}) %collective-permute-start.18) | collective-permute-done | bytes 540704 | tf_op jit(solution)/shard_map/ppermute | solution.py:256
  147.0 3.4 %shard_map.93 = bf16[720,1536]{1,0:T(8,128)(2,1)} custom-call(s32[9,8]{1,0:T(8,128)S(1)} %pad_add_fusion.meta, bf16[528,1536]{1,0:T(8,128)(2,1)S(1)} %shard_map.86.kept, bf16[528,1536]{1,0:T(8,128)(2,1)S(1)} %collective-permute-done.15.inner, bf16[528,512]{1,0:T(8,128)(2,1)S(1)} %collective-permute-done.10.rest_0_, ...), custom_call_target="tpu_custom_call" | custom-call | flops 1 | bytes 1 | tf_op jit(solution)/shard_map/pallas_call | solution.py:374
  (44 shorter events, 25.2 us)
Async XLA Ops:
  1.4 18.6 %copy-start = (bf16[1536,1536]{1,0:T(8,128)(2,1)S(1)}, bf16[1536,1536]{1,0:T(8,128)(2,1)}, u32[]{:S(2)}) copy-start(bf16[1536,1536]{1,0:T(8,128)(2,1)} %weight.3) | copy-start | bytes 14155780
  5.1 11.3 %collective-permute-start.1 = (bf16[528,384]{1,0:T(8,128)(2,1)S(1)}, bf16[528,384]{1,0:T(8,128)(2,1)S(1)}, u32[]{:S(2)}, u32[]{:S(2)}) collective-permute-start(bf16[528,384]{1,0:T(8,128)(2,1)S(1)} %get-tuple-element.58.p0.refs_0_), channel_id=1, source_target_pairs={{0,1},{1,0},{2,3},{3,2},{4,5},{5,4},{6,7},{7,6},{8,9},{9,8},{10,11... | collective-permute-start | bytes 1216520 | tf_op jit(solution)/shard_map/ppermute | solution.py:252
  5.6 10.8 %collective-permute-start.2 = (bf16[528,384]{1,0:T(8,128)(2,1)S(1)}, bf16[528,384]{1,0:T(8,128)(2,1)S(1)}, u32[]{:S(2)}, u32[]{:S(2)}) collective-permute-start(bf16[528,384]{1,0:T(8,128)(2,1)S(1)} %get-tuple-element.63.refs_4_.p0), channel_id=1, source_target_pairs={{0,1},{1,0},{2,3},{3,2},{4,5},{5,4},{6,7},{7,6},{8,9},{9,8},{10,11... | collective-permute-start | bytes 1216520 | tf_op jit(solution)/shard_map/ppermute | solution.py:252
  5.7 12.6 %collective-permute-start = (bf16[528,384]{1,0:T(8,128)(2,1)S(1)}, bf16[528,384]{1,0:T(8,128)(2,1)S(1)}, u32[]{:S(2)}, u32[]{:S(2)}) collective-permute-start(bf16[528,384]{1,0:T(8,128)(2,1)S(1)} %get-tuple-element.58.p0.refs_0_), channel_id=1, source_target_pairs={{0,2},{1,3},{2,0},{3,1},{4,6},{5,7},{6,4},{7,5},{8,10},{9,11},{10,... | collective-permute-start | bytes 1216520 | tf_op jit(solution)/shard_map/ppermute | solution.py:252
  18.3 1.7 %collective-permute-start.3 = (bf16[528,384]{1,0:T(8,128)(2,1)S(1)}, bf16[528,384]{1,0:T(8,128)(2,1)S(1)}, u32[]{:S(2)}, u32[]{:S(2)}) collective-permute-start(bf16[528,384]{1,0:T(8,128)(2,1)S(1)} %collective-permute-done.p2.refs_2_), channel_id=1, source_target_pairs={{0,1},{1,0},{2,3},{3,2},{4,5},{5,4},{6,7},{7,6},{8,9},{9,8},{10,11... | collective-permute-start | bytes 1216520 | tf_op jit(solution)/shard_map/ppermute | solution.py:252
  23.5 38.7 %collective-permute-start.6 = (bf16[528,1536]{1,0:T(8,128)(2,1)S(1)}, bf16[528,1536]{1,0:T(8,128)(2,1)S(1)}, u32[]{:S(2)}, u32[]{:S(2)}) collective-permute-start(bf16[528,1536]{1,0:T(8,128)(2,1)S(1)} %shard_map.79), channel_id=1, source_target_pairs={{0,8},{4,12},{24,16},{28,20},{1,9},{5,13},{25,17},{29,21},{2,10},{... | collective-permute-start | bytes 4866056 | tf_op jit(solution)/shard_map/ppermute | solution.py:256
  27.3 34.9 %collective-permute-start.7 = (bf16[528,1536]{1,0:T(8,128)(2,1)S(1)}, bf16[528,1536]{1,0:T(8,128)(2,1)S(1)}, u32[]{:S(2)}, u32[]{:S(2)}) collective-permute-start(bf16[528,1536]{1,0:T(8,128)(2,1)S(1)} %shard_map.79), channel_id=1, source_target_pairs={{8,16},{12,20},{16,8},{20,12},{9,17},{13,21},{17,9},{21,13},{10,18... | collective-permute-start | bytes 4866056 | tf_op jit(solution)/shard_map/ppermute | solution.py:256
  28.3 11.2 %collective-permute-start.4 = (bf16[528,384]{1,0:T(8,128)(2,1)S(1)}, bf16[528,384]{1,0:T(8,128)(2,1)S(1)}, u32[]{:S(2)}, u32[]{:S(2)}) collective-permute-start(bf16[528,384]{1,0:T(8,128)(2,1)S(1)} %get-tuple-element.63.refs_4_.p0), channel_id=1, source_target_pairs={{0,2},{1,3},{2,0},{3,1},{4,6},{5,7},{6,4},{7,5},{8,10},{9,11},{10,... | collective-permute-start | bytes 1216520 | tf_op jit(solution)/shard_map/ppermute | solution.py:252
  39.5 1.7 %collective-permute-start.5 = (bf16[528,384]{1,0:T(8,128)(2,1)S(1)}, bf16[528,384]{1,0:T(8,128)(2,1)S(1)}, u32[]{:S(2)}, u32[]{:S(2)}) collective-permute-start(bf16[528,384]{1,0:T(8,128)(2,1)S(1)} %collective-permute-done.4.refs_6_.p2), channel_id=1, source_target_pairs={{0,1},{1,0},{2,3},{3,2},{4,5},{5,4},{6,7},{7,6},{8,9},{9,8},{10,11... | collective-permute-start | bytes 1216520 | tf_op jit(solution)/shard_map/ppermute | solution.py:252
  44.6 19.6 %collective-permute-start.8 = (bf16[768,512]{1,0:T(8,128)(2,1)S(1)}, bf16[768,512]{1,0:T(8,128)(2,1)S(1)}, u32[]{:S(2)}, u32[]{:S(2)}) collective-permute-start(bf16[768,512]{1,0:T(8,128)(2,1)S(1)} %get-tuple-element.72), channel_id=1, source_target_pairs={{0,4},{4,0},{8,12},{12,8},{16,20},{20,16},{24,28},{28,24},{1,5},{5... | collective-permute-start | bytes 2359304 | tf_op jit(solution)/shard_map/ppermute | solution.py:252
  65.2 10.7 %collective-permute-start.9 = (bf16[384,512]{1,0:T(8,128)(2,1)S(1)}, bf16[384,512]{1,0:T(8,128)(2,1)S(1)}, u32[]{:S(2)}, u32[]{:S(2)}) collective-permute-start(bf16[384,512]{1,0:T(8,128)(2,1)S(1)} %get-tuple-element.89), channel_id=1, source_target_pairs={{0,8},{4,12},{8,0},{12,4},{16,24},{20,28},{24,16},{28,20},{1,9},{5... | collective-permute-start | bytes 1179656 | tf_op jit(solution)/shard_map/ppermute | solution.py:252
  67.3 23.3 %collective-permute-start.11 = (bf16[768,512]{1,0:T(8,128)(2,1)S(1)}, bf16[768,512]{1,0:T(8,128)(2,1)S(1)}, u32[]{:S(2)}, u32[]{:S(2)}) collective-permute-start(bf16[768,512]{1,0:T(8,128)(2,1)S(1)} %get-tuple-element.78), channel_id=1, source_target_pairs={{0,4},{4,0},{8,12},{12,8},{16,20},{20,16},{24,28},{28,24},{1,5},{5... | collective-permute-start | bytes 2359304 | tf_op jit(solution)/shard_map/ppermute | solution.py:252
  75.8 14.7 %collective-permute-start.10 = (bf16[528,512]{1,0:T(8,128)(2,1)S(1)}, bf16[528,512]{1,0:T(8,128)(2,1)S(1)}, u32[]{:S(2)}, u32[]{:S(2)}) collective-permute-start(bf16[528,512]{1,0:T(8,128)(2,1)S(1)} %get-tuple-element.93), channel_id=1, source_target_pairs={{8,0},{12,4},{16,24},{20,28},{9,1},{13,5},{17,25},{21,29},{10,2},{... | collective-permute-start | bytes 1622024 | tf_op jit(solution)/shard_map/ppermute | solution.py:256
  77.1 53.7 %collective-permute-start.15 = (bf16[528,1536]{1,0:T(8,128)(2,1)S(1)}, bf16[528,1536]{1,0:T(8,128)(2,1)S(1)}, u32[]{:S(2)}, u32[]{:S(2)}) collective-permute-start(bf16[528,1536]{1,0:T(8,128)(2,1)S(1)} %collective-permute-done.6), channel_id=1, source_target_pairs={{8,16},{12,20},{16,8},{20,12},{9,17},{13,21},{17,9},{21,13},{10,18... | collective-permute-start | bytes 4866056 | tf_op jit(solution)/shard_map/ppermute | solution.py:256
  91.5 17.3 %collective-permute-start.12 = (bf16[768,512]{1,0:T(8,128)(2,1)S(1)}, bf16[768,512]{1,0:T(8,128)(2,1)S(1)}, u32[]{:S(2)}, u32[]{:S(2)}) collective-permute-start(bf16[768,512]{1,0:T(8,128)(2,1)S(1)} %get-tuple-element.99), channel_id=1, source_target_pairs={{0,4},{4,0},{8,12},{12,8},{16,20},{20,16},{24,28},{28,24},{1,5},{5... | collective-permute-start | bytes 2359304 | tf_op jit(solution)/shard_map/ppermute | solution.py:252
  93.1 33.6 %collective-permute-start.14 = (bf16[384,512]{1,0:T(8,128)(2,1)S(1)}, bf16[384,512]{1,0:T(8,128)(2,1)S(1)}, u32[]{:S(2)}, u32[]{:S(2)}) collective-permute-start(bf16[384,512]{1,0:T(8,128)(2,1)S(1)} %get-tuple-element.96), channel_id=1, source_target_pairs={{0,8},{4,12},{8,0},{12,4},{16,24},{20,28},{24,16},{28,20},{1,9},{5... | collective-permute-start | bytes 1179656 | tf_op jit(solution)/shard_map/ppermute | solution.py:252
  93.1 37.8 %collective-permute-start.16 = (bf16[528,512]{1,0:T(8,128)(2,1)S(1)}, bf16[528,512]{1,0:T(8,128)(2,1)S(1)}, u32[]{:S(2)}, u32[]{:S(2)}) collective-permute-start(bf16[528,512]{1,0:T(8,128)(2,1)S(1)} %get-tuple-element.105), channel_id=1, source_target_pairs={{8,0},{12,4},{16,24},{20,28},{9,1},{13,5},{17,25},{21,29},{10,2},{... | collective-permute-start | bytes 1622024 | tf_op jit(solution)/shard_map/ppermute | solution.py:256
  94.4 31.1 %collective-permute-start.13 = (bf16[192,512]{1,0:T(8,128)(2,1)S(1)}, bf16[192,512]{1,0:T(8,128)(2,1)S(1)}, u32[]{:S(2)}, u32[]{:S(2)}) collective-permute-start(bf16[192,512]{1,0:T(8,128)(2,1)S(1)} %get-tuple-element.92), channel_id=1, source_target_pairs={{0,16},{4,20},{8,24},{12,28},{16,0},{20,4},{24,8},{28,12},{1,17},{... | collective-permute-start | bytes 589832 | tf_op jit(solution)/shard_map/ppermute | solution.py:252
  109.7 21.2 %collective-permute-start.17 = (bf16[384,512]{1,0:T(8,128)(2,1)S(1)}, bf16[384,512]{1,0:T(8,128)(2,1)S(1)}, u32[]{:S(2)}, u32[]{:S(2)}) collective-permute-start(bf16[384,512]{1,0:T(8,128)(2,1)S(1)} %get-tuple-element.100), channel_id=1, source_target_pairs={{0,8},{4,12},{8,0},{12,4},{16,24},{20,28},{24,16},{28,20},{1,9},{5... | collective-permute-start | bytes 1179656 | tf_op jit(solution)/shard_map/ppermute | solution.py:252
  125.4 21.6 %collective-permute-start.18 = (bf16[528,512]{1,0:T(8,128)(2,1)S(1)}, bf16[528,512]{1,0:T(8,128)(2,1)S(1)}, u32[]{:S(2)}, u32[]{:S(2)}) collective-permute-start(bf16[528,512]{1,0:T(8,128)(2,1)S(1)} %get-tuple-element.110), channel_id=1, source_target_pairs={{8,0},{12,4},{16,24},{20,28},{9,1},{13,5},{17,25},{21,29},{10,2},{... | collective-permute-start | bytes 1622024 | tf_op jit(solution)/shard_map/ppermute | solution.py:256
  127.5 15.4 %collective-permute-start.19 = (bf16[192,512]{1,0:T(8,128)(2,1)S(1)}, bf16[192,512]{1,0:T(8,128)(2,1)S(1)}, u32[]{:S(2)}, u32[]{:S(2)}) collective-permute-start(bf16[192,512]{1,0:T(8,128)(2,1)S(1)} %get-tuple-element.103), channel_id=1, source_target_pairs={{0,16},{4,20},{8,24},{12,28},{16,0},{20,4},{24,8},{28,12},{1,17},{... | collective-permute-start | bytes 589832 | tf_op jit(solution)/shard_map/ppermute | solution.py:252
  131.7 18.7 %collective-permute-start.20 = (bf16[192,512]{1,0:T(8,128)(2,1)S(1)}, bf16[192,512]{1,0:T(8,128)(2,1)S(1)}, u32[]{:S(2)}, u32[]{:S(2)}) collective-permute-start(bf16[192,512]{1,0:T(8,128)(2,1)S(1)} %get-tuple-element.108), channel_id=1, source_target_pairs={{0,16},{4,20},{8,24},{12,28},{16,0},{20,4},{24,8},{28,12},{1,17},{... | collective-permute-start | bytes 589832 | tf_op jit(solution)/shard_map/ppermute | solution.py:252

commit v16 on v15

--- a/solution.py
+++ b/solution.py
@@ -146,15 +146,15 @@
 
 
 def grad_kernel(slope_count, block, meta, p0, p1, p2, p3, weight, *rest):
-    slopes, (out, lhs) = rest[:slope_count], rest[slope_count:]
+    slopes, outs, lhs = rest[:slope_count], rest[slope_count:-1], rest[-1]
     width = p0.shape[1]
     for j, piece in enumerate((p0, p1, p2, p3)):
         lhs[:, pl.ds(pl.multiple_of((tensor_at(meta) ^ j) * width, 128), width)] = piece[...]
     at = 0
     for i, c, wide in cut_at([slope.shape[1] for slope in slopes], block):
-        columns = slice(at, at + wide)
-        value = jnp.dot(lhs[...], weight[:, columns], preferred_element_type=F32)
-        out[:, columns] = (value * slopes[i][:, c : c + wide]).astype(BF)
+        value = jnp.dot(lhs[...], weight[:, at : at + wide], preferred_element_type=F32)
+        part = outs[0].shape[1]
+        outs[at // part][:, at % part : at % part + wide] = (value * slopes[i][:, c : c + wide]).astype(BF)
         at += wide
 
 
@@ -225,25 +225,25 @@
     lax.fori_loop(0, half // step, body, 0)
 
 
-def place_kernel(meta, kept, inner, *rest):
-    outer, out = rest[:-1], rest[-1]
+def place_kernel(meta, kept, inner_1, inner_2, outer_1, outer_2, out):
     d = dp_at(meta)
     count = kept_total(meta, d)
     first = jnp.minimum(count - lax.rem(count, TILE), BAL - SEND)
     first = pl.multiple_of(first, TILE)
     wide = out.shape[1]
     step = pl.program_id(0)
-    columns = pl.ds(pl.multiple_of(step * wide, wide), wide)
-    out[0:KEEP, :] = kept[:, columns]
+    out[0:KEEP, :] = kept[:, pl.ds(pl.multiple_of(step * wide, wide), wide)]
     out[KEEP:, :] = jnp.zeros((out.shape[0] - KEEP, wide), BF)
     rows = lax.broadcasted_iota(jnp.int32, (SEND, 1), 0) + first
     window = pl.ds(first, SEND)
     is_inner = (d // 2 == 1) | (d // 2 == 2)
-    for i, (part, c, _) in enumerate(cut_at([x.shape[1] for x in outer], wide)):
-
-        @pl.when(step == i)
+    per = inner_1.shape[1] // wide
+    for i, (inner, outer) in enumerate(((inner_1, outer_1), (inner_2, outer_2))):
+
+        @pl.when(step // per == i)
         def _():
-            block = jnp.where(is_inner, inner[:, columns], outer[part][:, c : c + wide])
+            columns = pl.ds(pl.multiple_of((step - i * per) * wide, wide), wide)
+            block = jnp.where(is_inner, inner[:, columns], outer[:, columns])
             out[window, :] = jnp.where(rows < count, out[window, :], block)
 
 
@@ -300,11 +300,11 @@
             [shape(features // 2, part), shape(features // 2, part, F32)], [IN_VMEM] * 4, [IN_VMEM] * 2,
         )(meta, *lhs, act_moved, act_kept)
 
-    def grads(meta, pieces, slopes):
+    def grads(meta, pieces, slopes, cuts):
         rows = pieces[0].shape[0]
         return kernel_call(
-            functools.partial(grad_kernel, len(slopes), 256), shape(rows, ff),
-            [IN_VMEM] * (5 + len(slopes)), IN_VMEM, [vmem((rows, features), BF)],
+            functools.partial(grad_kernel, len(slopes), 256), [shape(rows, c) for c in cuts],
+            [IN_VMEM] * (5 + len(slopes)), [IN_VMEM] * len(cuts), [vmem((rows, features), BF)],
         )(meta, *pieces, down_weight, *slopes)
 
     def near_step(meta, keeps, gots):
@@ -329,52 +329,52 @@
     moved_1, moved_2 = swapped(moved_0, "tensor", 1), swapped(moved_0, "tensor", 2)
     kept_1, kept_2 = swapped(kept_0, "tensor", 1), swapped(kept_0, "tensor", 2)
     act_m, der_m = gelu(after(meta, moved_0), moved_pick, 0, ff)
-    moved_2 = after(moved_2, act_m, moved_1, kept_1)
+    act_ka, der_ka = gelu(after(meta, act_m), kept_pick, 0, part)
+    moved_2 = after(moved_2, act_ka, moved_1, kept_1)
     moved_3 = swapped(moved_2, "tensor", 1)
     moved = (moved_0, moved_1, moved_2, moved_3)
-
-    moving = grads(after(meta, moved_2), moved, (der_m,))
-    to_inner, across, to_outer = ((0, 1), (3, 2)), ((1, 2), (2, 1)), ((1, 0), (2, 3))
-    relayed = routed(moving, to_inner)
-    crossed = routed(moving, across)
-
-    act_ka, der_ka = gelu(after(meta, moving), kept_pick, 0, part)
-    kept_2 = after(kept_2, act_ka)
+    kept_2 = after(kept_2, moved_2)
     kept_3 = swapped(kept_2, "tensor", 1)
     kept = (kept_0, kept_1, kept_2, kept_3)
-    send_a, keep_a, *lhs = weight_first(after(meta, act_ka), act_m, act_ka)
+
+    moving = grads(after(meta, moved_2), moved, (der_m,), (ff // 2, ff // 2))
+    to_inner, across, to_outer = ((0, 1), (3, 2)), ((1, 2), (2, 1)), ((1, 0), (2, 3))
+    relayed_1, relayed_2 = [routed(block, to_inner) for block in moving]
+    crossed_1, crossed_2 = [routed(block, across) for block in moving]
+
+    send_a, keep_a, *lhs = weight_first(after(meta, *moving), act_m, act_ka)
     got_a = swapped(send_a, "dp", 1)
     act_kb, der_kb = gelu(after(meta, send_a), kept_pick, part, part)
     send_b, keep_b = weight_again(after(meta, act_kb), part, act_m, act_kb)
     got_b = swapped(send_b, "dp", 1)
     act_kc, der_kc = gelu(after(meta, send_b), kept_pick, 2 * part, part)
-    send_c, keep_c = weight_again(after(meta, act_kc), 2 * part, act_m, act_kc)
-    kept_grad = grads(after(meta, send_c), kept, (der_ka, der_kb, der_kc))
-
-    out_na, mine_a = near_step(after(meta, kept_grad, relayed, crossed), (keep_a,), (got_a,))
+    outer_1 = routed(after(crossed_1, act_kc), to_outer)
+    send_c, keep_c = weight_again(after(meta, act_kc, relayed_1), 2 * part, act_m, act_kc)
+    (kept_grad,) = grads(after(meta, send_c), kept, (der_ka, der_kb, der_kc), (ff,))
+    inner_1 = routed(after(relayed_1, send_c), across)
+
+    out_na, mine_a = near_step(after(meta, kept_grad), (keep_a,), (got_a,))
     got_na = swapped(out_na, "dp", 2)
-    inner = routed(after(relayed, out_na), across)
-    outer_a = routed(after(crossed[:, :part], got_na), to_outer)
-    out_fa, own_a = far_step(after(meta, out_na), mine_a, got_na)
+    outer_2 = routed(after(crossed_2, out_na, outer_1), to_outer)
+    inner_2 = routed(after(relayed_2, out_na), across)
+    out_nb, mine_b = near_step(after(meta, out_na, crossed_2, relayed_2), (keep_b,), (got_b,))
+    got_nb = swapped(out_nb, "dp", 2)
+    got_c = swapped(after(send_c, out_na), "dp", 1)
+    out_fa, own_a = far_step(after(meta, out_nb, inner_1), mine_a, got_na)
     got_fa = swapped(out_fa, "dp", 4)
-    out_nb, mine_b = near_step(after(meta, out_fa, outer_a), (keep_b,), (got_b,))
-    got_nb = swapped(out_nb, "dp", 2)
-    got_c = swapped(after(send_c, out_nb), "dp", 1)
-    outer_b = routed(after(crossed[:, part : 2 * part], out_nb), to_outer)
-    out_nc, mine_c = near_step(after(meta, out_nb), (keep_c,), (got_c,))
+    out_nc, mine_c = near_step(after(meta, out_fa, outer_2), (keep_c,), (got_c,))
     got_nc = swapped(out_nc, "dp", 2)
-    outer_c = routed(after(crossed[:, 2 * part :], out_nc), to_outer)
-    out_fb, own_b = far_step(after(meta, out_nc, got_fa), mine_b, got_nb)
+    out_fb, own_b = far_step(after(meta, out_nc, inner_2), mine_b, got_nb)
     got_fb = swapped(out_fb, "dp", 4)
-    out_fc, own_c = far_step(after(meta, out_fb, inner, outer_b), mine_c, got_nc)
+    hidden_grad = kernel_call(
+        place_kernel, shape(BAL, ff), [IN_VMEM] * 5,
+        pl.BlockSpec((BAL, 256), lambda i, *_: (0, i)), grid=(ff // 256,),
+    )(after(meta, out_fb), kept_grad, inner_1, inner_2, outer_1, outer_2)
+    out_fc, own_c = far_step(after(meta, out_fb), mine_c, got_nc)
     got_fc = swapped(out_fc, "dp", 4)
     total = [a + b.astype(F32) for a, b in ((own_a, got_fa), (own_b, got_fb), (own_c, got_fc))]
     down_grad = jnp.concatenate(total, axis=1) / math.sqrt(n * home)
 
-    hidden_grad = kernel_call(
-        place_kernel, shape(BAL, ff), [IN_VMEM] * 5,
-        pl.BlockSpec((BAL, 256), lambda i, *_: (0, i)), grid=(ff // 256,),
-    )(after(meta, out_fc), kept_grad, inner, outer_a, outer_b, outer_c)
     return (hidden_grad, down_grad)
 
 

time: 152 us -> 137 us (0.901)
  waiting for transfers between devices: 74.7 us -> 55 us
  starting transfers between devices: 27.8 us -> 32.8 us
    ppermute x15, waiting for transfers between devices: 58.8 us -> 48.2 us  [swapped(): return lax.ppermute(block, axis, [(i, i ^ distance) for i in range(n)])]
    ppermute x6 -> x8, waiting for transfers between devices: 15.9 us -> 6.84 us  [routed(): lax.ppermute(block, 'dp', [(2 * a + x, 2 * b + x) for a, b in pairs for x...]
    ppermute x6 -> x8, starting transfers between devices: 9.36 us -> 13.7 us  [routed(): lax.ppermute(block, 'dp', [(2 * a + x, 2 * b + x) for a, b in pairs for x...]
  transfers between devices with their start and end apart: 21 -> 23, of which waited for: 11 -> 8; matrix products, arithmetic and copies ran while one was open for 0% -> 0% of each run, Pallas kernels for 25% -> 31%
where the time goes in v16:
time: 137 us
  waiting for transfers between devices  55 us (40%)
  Pallas kernels  46 us (34%)
  starting transfers between devices  32.8 us (24%)
  other arithmetic  1.99 us (1%)
    ppermute x15, waiting for transfers between devices, swapped(): return lax.ppermute(block, axis, [(i, i ^ distance) for i in range(n)])  48.2 us
    ppermute x15, starting transfers between devices, swapped(): return lax.ppermute(block, axis, [(i, i ^ distance) for i in range(n)])  19.1 us
    pallas_call x4, Pallas kernels, gelu(): kernel_call(functools.partial(gelu_kernel, base, block), [shape(rows, col...  16.8 us
    ppermute x8, starting transfers between devices, routed(): lax.ppermute(block, 'dp', [(2 * a + x, 2 * b + x) for a, b in pairs for x...  13.7 us
    pallas_call x2, Pallas kernels, grads(): kernel_call(functools.partial(grad_kernel, len(slopes), 256), [shape(rows...  6.97 us
    ppermute x8, waiting for transfers between devices, routed(): lax.ppermute(block, 'dp', [(2 * a + x, 2 * b + x) for a, b in pairs for x...  6.84 us
    pallas_call x2, Pallas kernels, weight_again(): kernel_call(functools.partial(again_kernel, base), [shape(features // 2,...  6.52 us
    pallas_call x1, Pallas kernels, shards(): kernel_call(first_kernel, [shape(SEND, width), shape(KEEP, width), shape(...  3.73 us
  transfers between devices with their start and end apart: 23, of which 8 were waited for; matrix products, arithmetic and copies ran while one was open for 0% of the time, Pallas kernels for 31%

profile of v16, /device:TPU:0, one launch (start us, length us, event | category | flops | bytes accessed | tf_op | source)
XLA Modules:
  0.0 136.8 jit_solution(8448641618082694865)
XLA Ops:
  1.4 3.7 %shard_map.77 = (bf16[528,384]{1,0:T(8,128)(2,1)S(1)}, bf16[528,384]{1,0:T(8,128)(2,1)S(1)}, bf16[528,1032]{1,0:T(8,128)(2,1)S(1)}, bf16[528,1032]{1,0:T(8,128)(2,1)S(1)}, bf16[1032,1536]{1,0:T(8,128)(2,1)S(1)}) custom-call(s32[9,8]{1,0:T(8,128)S(1)} %pad_add_fusion.meta, bf16[1032,384]{1,0:T(8,128)(2,1)} %cot_hbm.1, f32[1536]{0:T(1024)} %scale_hbm.1, ...), custom_call_target="tpu_custom_call" | custom-call | flops 1 | bytes 1 | tf_op jit(solution)/shard_map/pallas_call | solution.py:322
  5.7 2.9 %collective-permute-start = (bf16[528,384]{1,0:T(8,128)(2,1)S(1)}, bf16[528,384]{1,0:T(8,128)(2,1)S(1)}, u32[]{:S(2)}, u32[]{:S(2)}) collective-permute-start(bf16[528,384]{1,0:T(8,128)(2,1)S(1)} %get-tuple-element.59.p0.refs_0_), channel_id=1, source_target_pairs={{0,2},{1,3},{2,0},{3,1},{4,6},{5,7},{6,4},{7,5},{8,10},{9,11},{10,... | collective-permute-start | bytes 1216520 | tf_op jit(solution)/shard_map/ppermute | solution.py:252
  8.6 7.8 %shard_map.78 = (bf16[528,1536]{1,0:T(8,128)(2,1)S(1)}, f32[528,1536]{1,0:T(8,128)S(1)}) custom-call(s32[9,8]{1,0:T(8,128)S(1)} %pad_add_fusion.meta, bf16[528,1032]{1,0:T(8,128)(2,1)S(1)} %get-tuple-element.61.pick, bf16[1032,1536]{1,0:T(8,128)(2,1)S(1)} %get-tuple-element.62.pre), custom_call_target="tpu_custom_call" | custom-call | flops 1 | bytes 1 | tf_op jit(solution)/shard_map/pallas_call | solution.py:283
  16.4 3.0 %shard_map.79 = (bf16[528,512]{1,0:T(8,128)(2,1)S(1)}, f32[528,512]{1,0:T(8,128)S(1)}) custom-call(s32[9,8]{1,0:T(8,128)S(1)} %pad_add_fusion.meta, bf16[528,1032]{1,0:T(8,128)(2,1)S(1)} %get-tuple-element.65.pick, bf16[1032,1536]{1,0:T(8,128)(2,1)S(1)} %get-tuple-element.62.pre), custom_call_target="tpu_custom_call" | custom-call | flops 1 | bytes 1 | tf_op jit(solution)/shard_map/pallas_call | solution.py:283
  21.3 3.5 %shard_map.80 = (bf16[528,768]{1,0:T(8,128)(2,1)S(1)}, bf16[528,768]{1,0:T(8,128)(2,1)S(1)}) custom-call(s32[9,8]{1,0:T(8,128)S(1)} %pad_add_fusion.meta, bf16[528,384]{1,0:T(8,128)(2,1)S(1)} %get-tuple-element.59.p0.refs_0_, bf16[528,384]{1,0:T(8,128)(2,1)S(1)} %collective-permute-done.1.p1.refs_1_, bf16[528,384]{1,0:T(8,128)(2,1)S(1)} %collective-permute-done.p2.refs_2_, ...), custom_call_target="tpu_custom_call" | custom-call | flops 1 | bytes 1 | tf_op jit(solution)/shard_map/pallas_call | solution.py:305
  25.5 5.8 %collective-permute-done.4.refs_6_.p2 = bf16[528,384]{1,0:T(8,128)(2,1)S(1)} collective-permute-done((bf16[528,384]{1,0:T(8,128)(2,1)S(1)}, bf16[528,384]{1,0:T(8,128)(2,1)S(1)}, u32[]{:S(2)}, u32[]{:S(2)}) %collective-permute-start.4) | collective-permute-done | bytes 405536 | tf_op jit(solution)/shard_map/ppermute | solution.py:252
  31.4 3.5 %collective-permute-start.6 = (bf16[528,768]{1,0:T(8,128)(2,1)S(1)}, bf16[528,768]{1,0:T(8,128)(2,1)S(1)}, u32[]{:S(2)}, u32[]{:S(2)}) collective-permute-start(bf16[528,768]{1,0:T(8,128)(2,1)S(1)} %get-tuple-element.71), channel_id=1, source_target_pairs={{0,8},{4,12},{24,16},{28,20},{1,9},{5,13},{25,17},{29,21},{2,10},{... | collective-permute-start | bytes 2433032 | tf_op jit(solution)/shard_map/ppermute | solution.py:256
  34.9 3.4 %shard_map.81 = (bf16[768,512]{1,0:T(8,128)(2,1)S(1)}, f32[768,512]{1,0:T(8,128)S(1)}, bf16[1536,528]{1,0:T(8,128)(2,1)S(1)}, bf16[1536,528]{1,0:T(8,128)(2,1)S(1)}) custom-call(s32[9,8]{1,0:T(8,128)S(1)} %pad_add_fusion.meta, bf16[528,384]{1,0:T(8,128)(2,1)S(1)} %get-tuple-element.59.p0.refs_0_, bf16[528,384]{1,0:T(8,128)(2,1)S(1)} %collective-permute-done.1.p1.refs_1_, ...), custom_call_target="tpu_custom_call" | custom-call | flops 1 | bytes 1 | tf_op jit(solution)/shard_map/pallas_call | solution.py:290
  38.3 1.6 %collective-permute-start.7 = (bf16[768,512]{1,0:T(8,128)(2,1)S(1)}, bf16[768,512]{1,0:T(8,128)(2,1)S(1)}, u32[]{:S(2)}, u32[]{:S(2)}) collective-permute-start(bf16[768,512]{1,0:T(8,128)(2,1)S(1)} %get-tuple-element.75), channel_id=1, source_target_pairs={{0,4},{4,0},{8,12},{12,8},{16,20},{20,16},{24,28},{28,24},{1,5},{5... | collective-permute-start | bytes 2359304 | tf_op jit(solution)/shard_map/ppermute | solution.py:252
  40.7 3.0 %shard_map.82 = (bf16[528,512]{1,0:T(8,128)(2,1)S(1)}, f32[528,512]{1,0:T(8,128)S(1)}) custom-call(s32[9,8]{1,0:T(8,128)S(1)} %pad_add_fusion.meta, bf16[528,1032]{1,0:T(8,128)(2,1)S(1)} %get-tuple-element.65.pick, bf16[1032,1536]{1,0:T(8,128)(2,1)S(1)} %get-tuple-element.62.pre), custom_call_target="tpu_custom_call" | custom-call | flops 1 | bytes 1 | tf_op jit(solution)/shard_map/pallas_call | solution.py:283
  43.7 3.3 %shard_map.83 = (bf16[768,512]{1,0:T(8,128)(2,1)S(1)}, f32[768,512]{1,0:T(8,128)S(1)}) custom-call(s32[9,8]{1,0:T(8,128)S(1)} %pad_add_fusion.meta, bf16[1536,528]{1,0:T(8,128)(2,1)S(1)} %get-tuple-element.79.lhs_moved, bf16[1536,528]{1,0:T(8,128)(2,1)S(1)} %get-tuple-element.80.lhs_kept, bf16[528,1536]{1,0:T(8,128)(2,1)S(1)} %get-tuple-element.63.refs_8_.act_moved, ...), custom_call_target="tpu_custom_call" | custom-call | flops 1 | bytes 1 | tf_op jit(solution)/shard_map/pallas_call | solution.py:298
  47.0 3.0 %shard_map.84 = (bf16[528,512]{1,0:T(8,128)(2,1)S(1)}, f32[528,512]{1,0:T(8,128)S(1)}) custom-call(s32[9,8]{1,0:T(8,128)S(1)} %pad_add_fusion.meta, bf16[528,1032]{1,0:T(8,128)(2,1)S(1)} %get-tuple-element.65.pick, bf16[1032,1536]{1,0:T(8,128)(2,1)S(1)} %get-tuple-element.62.pre), custom_call_target="tpu_custom_call" | custom-call | flops 1 | bytes 1 | tf_op jit(solution)/shard_map/pallas_call | solution.py:283
  51.4 4.6 %collective-permute-start.9 = (bf16[528,768]{1,0:T(8,128)(2,1)S(1)}, bf16[528,768]{1,0:T(8,128)(2,1)S(1)}, u32[]{:S(2)}, u32[]{:S(2)}) collective-permute-start(bf16[528,768]{1,0:T(8,128)(2,1)S(1)} %get-tuple-element.72), channel_id=1, source_target_pairs={{0,8},{4,12},{24,16},{28,20},{1,9},{5,13},{25,17},{29,21},{2,10},{... | collective-permute-start | bytes 2433032 | tf_op jit(solution)/shard_map/ppermute | solution.py:256
  56.6 3.3 %shard_map.85 = (bf16[768,512]{1,0:T(8,128)(2,1)S(1)}, f32[768,512]{1,0:T(8,128)S(1)}) custom-call(s32[9,8]{1,0:T(8,128)S(1)} %pad_add_fusion.meta, bf16[1536,528]{1,0:T(8,128)(2,1)S(1)} %get-tuple-element.79.lhs_moved, bf16[1536,528]{1,0:T(8,128)(2,1)S(1)} %get-tuple-element.80.lhs_kept, bf16[528,1536]{1,0:T(8,128)(2,1)S(1)} %get-tuple-element.63.refs_8_.act_moved, ...), custom_call_target="tpu_custom_call" | custom-call | flops 1 | bytes 1 | tf_op jit(solution)/shard_map/pallas_call | solution.py:298
  60.6 3.5 %shard_map.86.kept = bf16[528,1536]{1,0:T(8,128)(2,1)S(1)} custom-call(s32[9,8]{1,0:T(8,128)S(1)} %pad_add_fusion.meta, bf16[528,384]{1,0:T(8,128)(2,1)S(1)} %get-tuple-element.67.refs_4_.p0, bf16[528,384]{1,0:T(8,128)(2,1)S(1)} %collective-permute-done.2.refs_5_.p1, bf16[528,384]{1,0:T(8,128)(2,1)S(1)} %collective-permute-done.4.refs_6_.p2, ...), custom_call_target="tpu_custom_call" | custom-call | flops 1 | bytes 1 | tf_op jit(solution)/shard_map/pallas_call | solution.py:305
  65.0 6.8 %collective-permute-done.14.outer_1 = bf16[528,768]{1,0:T(8,128)(2,1)S(1)} collective-permute-done((bf16[528,768]{1,0:T(8,128)(2,1)S(1)}, bf16[528,768]{1,0:T(8,128)(2,1)S(1)}, u32[]{:S(2)}, u32[]{:S(2)}) %collective-permute-start.14) | collective-permute-done | bytes 811040 | tf_op jit(solution)/shard_map/ppermute | solution.py:256
  74.9 5.1 %collective-permute-start.12 = (bf16[384,512]{1,0:T(8,128)(2,1)S(1)}, bf16[384,512]{1,0:T(8,128)(2,1)S(1)}, u32[]{:S(2)}, u32[]{:S(2)}) collective-permute-start(bf16[384,512]{1,0:T(8,128)(2,1)S(1)} %get-tuple-element.92), channel_id=1, source_target_pairs={{0,8},{4,12},{8,0},{12,4},{16,24},{20,28},{24,16},{28,20},{1,9},{5... | collective-permute-start | bytes 1179656 | tf_op jit(solution)/shard_map/ppermute | solution.py:252
  81.0 3.0 %collective-permute-start.18 = (bf16[384,512]{1,0:T(8,128)(2,1)S(1)}, bf16[384,512]{1,0:T(8,128)(2,1)S(1)}, u32[]{:S(2)}, u32[]{:S(2)}) collective-permute-start(bf16[384,512]{1,0:T(8,128)(2,1)S(1)} %get-tuple-element.95), channel_id=1, source_target_pairs={{0,8},{4,12},{8,0},{12,4},{16,24},{20,28},{24,16},{28,20},{1,9},{5... | collective-permute-start | bytes 1179656 | tf_op jit(solution)/shard_map/ppermute | solution.py:252
  83.9 19.2 %collective-permute-done.12.got = bf16[384,512]{1,0:T(8,128)(2,1)S(1)} collective-permute-done((bf16[384,512]{1,0:T(8,128)(2,1)S(1)}, bf16[384,512]{1,0:T(8,128)(2,1)S(1)}, u32[]{:S(2)}, u32[]{:S(2)}) %collective-permute-start.12) | collective-permute-done | bytes 393248 | tf_op jit(solution)/shard_map/ppermute | solution.py:252
  105.6 2.5 %collective-permute-start.21 = (bf16[384,512]{1,0:T(8,128)(2,1)S(1)}, bf16[384,512]{1,0:T(8,128)(2,1)S(1)}, u32[]{:S(2)}, u32[]{:S(2)}) collective-permute-start(bf16[384,512]{1,0:T(8,128)(2,1)S(1)} %get-tuple-element.105), channel_id=1, source_target_pairs={{0,8},{4,12},{8,0},{12,4},{16,24},{20,28},{24,16},{28,20},{1,9},{5... | collective-permute-start | bytes 1179656 | tf_op jit(solution)/shard_map/ppermute | solution.py:252
  108.1 7.9 %collective-permute-done.18.got = bf16[384,512]{1,0:T(8,128)(2,1)S(1)} collective-permute-done((bf16[384,512]{1,0:T(8,128)(2,1)S(1)}, bf16[384,512]{1,0:T(8,128)(2,1)S(1)}, u32[]{:S(2)}, u32[]{:S(2)}) %collective-permute-start.18) | collective-permute-done | bytes 393248 | tf_op jit(solution)/shard_map/ppermute | solution.py:252
  117.3 3.3 %shard_map.92 = bf16[720,1536]{1,0:T(8,128)(2,1)} custom-call(s32[9,8]{1,0:T(8,128)S(1)} %pad_add_fusion.meta, bf16[528,1536]{1,0:T(8,128)(2,1)S(1)} %shard_map.86.kept, bf16[528,768]{1,0:T(8,128)(2,1)S(1)} %collective-permute-done.11.inner_1, bf16[528,768]{1,0:T(8,128)(2,1)S(1)} %collective-permute-done.17.inner_2, ...), custom_call_target="tpu_custom_call" | custom-call | flops 1 | bytes 1 | tf_op jit(solution)/shard_map/pallas_call | solution.py:369
  120.7 5.8 %collective-permute-done.21.got = bf16[384,512]{1,0:T(8,128)(2,1)S(1)} collective-permute-done((bf16[384,512]{1,0:T(8,128)(2,1)S(1)}, bf16[384,512]{1,0:T(8,128)(2,1)S(1)}, u32[]{:S(2)}, u32[]{:S(2)}) %collective-permute-start.21) | collective-permute-done | bytes 393248 | tf_op jit(solution)/shard_map/ppermute | solution.py:252
  128.0 7.6 %collective-permute-done.22 = bf16[192,512]{1,0:T(8,128)(2,1)S(1)} collective-permute-done((bf16[192,512]{1,0:T(8,128)(2,1)S(1)}, bf16[192,512]{1,0:T(8,128)(2,1)S(1)}, u32[]{:S(2)}, u32[]{:S(2)}) %collective-permute-start.22) | collective-permute-done | bytes 196640 | tf_op jit(solution)/shard_map/ppermute | solution.py:252
  (50 shorter events, 18.6 us)
Async XLA Ops:
  1.4 19.9 %slice-start = ((s8[4718592]{0:T(1024)(128)(4,1)}), s8[4194304]{0:T(1024)(128)(4,1)S(1)}, s32[]{:S(2)}) async-start(s8[4718592]{0:T(1024)(128)(4,1)} %bitcast.2), calls=%async_computation | async-start | bytes 8388608
  5.1 14.4 %collective-permute-start.1 = (bf16[528,384]{1,0:T(8,128)(2,1)S(1)}, bf16[528,384]{1,0:T(8,128)(2,1)S(1)}, u32[]{:S(2)}, u32[]{:S(2)}) collective-permute-start(bf16[528,384]{1,0:T(8,128)(2,1)S(1)} %get-tuple-element.59.p0.refs_0_), channel_id=1, source_target_pairs={{0,1},{1,0},{2,3},{3,2},{4,5},{5,4},{6,7},{7,6},{8,9},{9,8},{10,11... | collective-permute-start | bytes 1216520 | tf_op jit(solution)/shard_map/ppermute | solution.py:252
  5.6 13.8 %collective-permute-start.2 = (bf16[528,384]{1,0:T(8,128)(2,1)S(1)}, bf16[528,384]{1,0:T(8,128)(2,1)S(1)}, u32[]{:S(2)}, u32[]{:S(2)}) collective-permute-start(bf16[528,384]{1,0:T(8,128)(2,1)S(1)} %get-tuple-element.67.refs_4_.p0), channel_id=1, source_target_pairs={{0,1},{1,0},{2,3},{3,2},{4,5},{5,4},{6,7},{7,6},{8,9},{9,8},{10,11... | collective-permute-start | bytes 1216520 | tf_op jit(solution)/shard_map/ppermute | solution.py:252
  5.7 13.8 %collective-permute-start = (bf16[528,384]{1,0:T(8,128)(2,1)S(1)}, bf16[528,384]{1,0:T(8,128)(2,1)S(1)}, u32[]{:S(2)}, u32[]{:S(2)}) collective-permute-start(bf16[528,384]{1,0:T(8,128)(2,1)S(1)} %get-tuple-element.59.p0.refs_0_), channel_id=1, source_target_pairs={{0,2},{1,3},{2,0},{3,1},{4,6},{5,7},{6,4},{7,5},{8,10},{9,11},{10,... | collective-permute-start | bytes 1216520 | tf_op jit(solution)/shard_map/ppermute | solution.py:252
  19.5 1.8 %collective-permute-start.3 = (bf16[528,384]{1,0:T(8,128)(2,1)S(1)}, bf16[528,384]{1,0:T(8,128)(2,1)S(1)}, u32[]{:S(2)}, u32[]{:S(2)}) collective-permute-start(bf16[528,384]{1,0:T(8,128)(2,1)S(1)} %collective-permute-done.p2.refs_2_), channel_id=1, source_target_pairs={{0,1},{1,0},{2,3},{3,2},{4,5},{5,4},{6,7},{7,6},{8,9},{9,8},{10,11... | collective-permute-start | bytes 1216520 | tf_op jit(solution)/shard_map/ppermute | solution.py:252
  19.6 11.8 %collective-permute-start.4 = (bf16[528,384]{1,0:T(8,128)(2,1)S(1)}, bf16[528,384]{1,0:T(8,128)(2,1)S(1)}, u32[]{:S(2)}, u32[]{:S(2)}) collective-permute-start(bf16[528,384]{1,0:T(8,128)(2,1)S(1)} %get-tuple-element.67.refs_4_.p0), channel_id=1, source_target_pairs={{0,2},{1,3},{2,0},{3,1},{4,6},{5,7},{6,4},{7,5},{8,10},{9,11},{10,... | collective-permute-start | bytes 1216520 | tf_op jit(solution)/shard_map/ppermute | solution.py:252
  24.8 25.3 %collective-permute-start.13 = (bf16[528,768]{1,0:T(8,128)(2,1)S(1)}, bf16[528,768]{1,0:T(8,128)(2,1)S(1)}, u32[]{:S(2)}, u32[]{:S(2)}) collective-permute-start(bf16[528,768]{1,0:T(8,128)(2,1)S(1)} %get-tuple-element.71), channel_id=1, source_target_pairs={{8,16},{12,20},{16,8},{20,12},{9,17},{13,21},{17,9},{21,13},{10,18... | collective-permute-start | bytes 2433032 | tf_op jit(solution)/shard_map/ppermute | solution.py:256
  31.4 3.5 %collective-permute-start.5 = (bf16[528,384]{1,0:T(8,128)(2,1)S(1)}, bf16[528,384]{1,0:T(8,128)(2,1)S(1)}, u32[]{:S(2)}, u32[]{:S(2)}) collective-permute-start(bf16[528,384]{1,0:T(8,128)(2,1)S(1)} %collective-permute-done.4.refs_6_.p2), channel_id=1, source_target_pairs={{0,1},{1,0},{2,3},{3,2},{4,5},{5,4},{6,7},{7,6},{8,9},{9,8},{10,11... | collective-permute-start | bytes 1216520 | tf_op jit(solution)/shard_map/ppermute | solution.py:252
  31.4 24.7 %collective-permute-start.6 = (bf16[528,768]{1,0:T(8,128)(2,1)S(1)}, bf16[528,768]{1,0:T(8,128)(2,1)S(1)}, u32[]{:S(2)}, u32[]{:S(2)}) collective-permute-start(bf16[528,768]{1,0:T(8,128)(2,1)S(1)} %get-tuple-element.71), channel_id=1, source_target_pairs={{0,8},{4,12},{24,16},{28,20},{1,9},{5,13},{25,17},{29,21},{2,10},{... | collective-permute-start | bytes 2433032 | tf_op jit(solution)/shard_map/ppermute | solution.py:256
  38.3 21.6 %collective-permute-start.7 = (bf16[768,512]{1,0:T(8,128)(2,1)S(1)}, bf16[768,512]{1,0:T(8,128)(2,1)S(1)}, u32[]{:S(2)}, u32[]{:S(2)}) collective-permute-start(bf16[768,512]{1,0:T(8,128)(2,1)S(1)} %get-tuple-element.75), channel_id=1, source_target_pairs={{0,4},{4,0},{8,12},{12,8},{16,20},{20,16},{24,28},{28,24},{1,5},{5... | collective-permute-start | bytes 2359304 | tf_op jit(solution)/shard_map/ppermute | solution.py:252
  39.8 25.2 %collective-permute-start.8 = (bf16[528,768]{1,0:T(8,128)(2,1)S(1)}, bf16[528,768]{1,0:T(8,128)(2,1)S(1)}, u32[]{:S(2)}, u32[]{:S(2)}) collective-permute-start(bf16[528,768]{1,0:T(8,128)(2,1)S(1)} %get-tuple-element.72), channel_id=1, source_target_pairs={{8,16},{12,20},{16,8},{20,12},{9,17},{13,21},{17,9},{21,13},{10,18... | collective-permute-start | bytes 2433032 | tf_op jit(solution)/shard_map/ppermute | solution.py:256
  50.1 21.8 %collective-permute-start.14 = (bf16[528,768]{1,0:T(8,128)(2,1)S(1)}, bf16[528,768]{1,0:T(8,128)(2,1)S(1)}, u32[]{:S(2)}, u32[]{:S(2)}) collective-permute-start(bf16[528,768]{1,0:T(8,128)(2,1)S(1)} %collective-permute-done.13), channel_id=1, source_target_pairs={{8,0},{12,4},{16,24},{20,28},{9,1},{13,5},{17,25},{21,29},{10,2},{... | collective-permute-start | bytes 2433032 | tf_op jit(solution)/shard_map/ppermute | solution.py:256
  51.4 22.4 %collective-permute-start.9 = (bf16[528,768]{1,0:T(8,128)(2,1)S(1)}, bf16[528,768]{1,0:T(8,128)(2,1)S(1)}, u32[]{:S(2)}, u32[]{:S(2)}) collective-permute-start(bf16[528,768]{1,0:T(8,128)(2,1)S(1)} %get-tuple-element.72), channel_id=1, source_target_pairs={{0,8},{4,12},{24,16},{28,20},{1,9},{5,13},{25,17},{29,21},{2,10},{... | collective-permute-start | bytes 2433032 | tf_op jit(solution)/shard_map/ppermute | solution.py:256
  56.0 18.9 %collective-permute-start.10 = (bf16[768,512]{1,0:T(8,128)(2,1)S(1)}, bf16[768,512]{1,0:T(8,128)(2,1)S(1)}, u32[]{:S(2)}, u32[]{:S(2)}) collective-permute-start(bf16[768,512]{1,0:T(8,128)(2,1)S(1)} %get-tuple-element.81), channel_id=1, source_target_pairs={{0,4},{4,0},{8,12},{12,8},{16,20},{20,16},{24,28},{28,24},{1,5},{5... | collective-permute-start | bytes 2359304 | tf_op jit(solution)/shard_map/ppermute | solution.py:252
  59.9 21.1 %collective-permute-start.11 = (bf16[528,768]{1,0:T(8,128)(2,1)S(1)}, bf16[528,768]{1,0:T(8,128)(2,1)S(1)}, u32[]{:S(2)}, u32[]{:S(2)}) collective-permute-start(bf16[528,768]{1,0:T(8,128)(2,1)S(1)} %collective-permute-done.6), channel_id=1, source_target_pairs={{8,16},{12,20},{16,8},{20,12},{9,17},{13,21},{17,9},{21,13},{10,18... | collective-permute-start | bytes 2433032 | tf_op jit(solution)/shard_map/ppermute | solution.py:256
  71.9 32.8 %collective-permute-start.15 = (bf16[528,768]{1,0:T(8,128)(2,1)S(1)}, bf16[528,768]{1,0:T(8,128)(2,1)S(1)}, u32[]{:S(2)}, u32[]{:S(2)}) collective-permute-start(bf16[528,768]{1,0:T(8,128)(2,1)S(1)} %collective-permute-done.8), channel_id=1, source_target_pairs={{8,0},{12,4},{16,24},{20,28},{9,1},{13,5},{17,25},{21,29},{10,2},{... | collective-permute-start | bytes 2433032 | tf_op jit(solution)/shard_map/ppermute | solution.py:256
  73.2 31.5 %collective-permute-start.16 = (bf16[768,512]{1,0:T(8,128)(2,1)S(1)}, bf16[768,512]{1,0:T(8,128)(2,1)S(1)}, u32[]{:S(2)}, u32[]{:S(2)}) collective-permute-start(bf16[768,512]{1,0:T(8,128)(2,1)S(1)} %get-tuple-element.104), channel_id=1, source_target_pairs={{0,4},{4,0},{8,12},{12,8},{16,20},{20,16},{24,28},{28,24},{1,5},{5... | collective-permute-start | bytes 2359304 | tf_op jit(solution)/shard_map/ppermute | solution.py:252
  73.8 34.4 %collective-permute-start.17 = (bf16[528,768]{1,0:T(8,128)(2,1)S(1)}, bf16[528,768]{1,0:T(8,128)(2,1)S(1)}, u32[]{:S(2)}, u32[]{:S(2)}) collective-permute-start(bf16[528,768]{1,0:T(8,128)(2,1)S(1)} %collective-permute-done.9), channel_id=1, source_target_pairs={{8,16},{12,20},{16,8},{20,12},{9,17},{13,21},{17,9},{21,13},{10,18... | collective-permute-start | bytes 2433032 | tf_op jit(solution)/shard_map/ppermute | solution.py:256
  74.9 28.3 %collective-permute-start.12 = (bf16[384,512]{1,0:T(8,128)(2,1)S(1)}, bf16[384,512]{1,0:T(8,128)(2,1)S(1)}, u32[]{:S(2)}, u32[]{:S(2)}) collective-permute-start(bf16[384,512]{1,0:T(8,128)(2,1)S(1)} %get-tuple-element.92), channel_id=1, source_target_pairs={{0,8},{4,12},{8,0},{12,4},{16,24},{20,28},{24,16},{28,20},{1,9},{5... | collective-permute-start | bytes 1179656 | tf_op jit(solution)/shard_map/ppermute | solution.py:252
  81.0 35.0 %collective-permute-start.18 = (bf16[384,512]{1,0:T(8,128)(2,1)S(1)}, bf16[384,512]{1,0:T(8,128)(2,1)S(1)}, u32[]{:S(2)}, u32[]{:S(2)}) collective-permute-start(bf16[384,512]{1,0:T(8,128)(2,1)S(1)} %get-tuple-element.95), channel_id=1, source_target_pairs={{0,8},{4,12},{8,0},{12,4},{16,24},{20,28},{24,16},{28,20},{1,9},{5... | collective-permute-start | bytes 1179656 | tf_op jit(solution)/shard_map/ppermute | solution.py:252
  104.0 13.3 %collective-permute-start.19 = (bf16[192,512]{1,0:T(8,128)(2,1)S(1)}, bf16[192,512]{1,0:T(8,128)(2,1)S(1)}, u32[]{:S(2)}, u32[]{:S(2)}) collective-permute-start(bf16[192,512]{1,0:T(8,128)(2,1)S(1)} %get-tuple-element.99), channel_id=1, source_target_pairs={{0,16},{4,20},{8,24},{12,28},{16,0},{20,4},{24,8},{28,12},{1,17},{... | collective-permute-start | bytes 589832 | tf_op jit(solution)/shard_map/ppermute | solution.py:252
  105.6 20.9 %collective-permute-start.21 = (bf16[384,512]{1,0:T(8,128)(2,1)S(1)}, bf16[384,512]{1,0:T(8,128)(2,1)S(1)}, u32[]{:S(2)}, u32[]{:S(2)}) collective-permute-start(bf16[384,512]{1,0:T(8,128)(2,1)S(1)} %get-tuple-element.105), channel_id=1, source_target_pairs={{0,8},{4,12},{8,0},{12,4},{16,24},{20,28},{24,16},{28,20},{1,9},{5... | collective-permute-start | bytes 1179656 | tf_op jit(solution)/shard_map/ppermute | solution.py:252
  116.9 11.1 %collective-permute-start.20 = (bf16[192,512]{1,0:T(8,128)(2,1)S(1)}, bf16[192,512]{1,0:T(8,128)(2,1)S(1)}, u32[]{:S(2)}, u32[]{:S(2)}) collective-permute-start(bf16[192,512]{1,0:T(8,128)(2,1)S(1)} %get-tuple-element.109), channel_id=1, source_target_pairs={{0,16},{4,20},{8,24},{12,28},{16,0},{20,4},{24,8},{28,12},{1,17},{... | collective-permute-start | bytes 589832 | tf_op jit(solution)/shard_map/ppermute | solution.py:252
  127.3 8.3 %collective-permute-start.22 = (bf16[192,512]{1,0:T(8,128)(2,1)S(1)}, bf16[192,512]{1,0:T(8,128)(2,1)S(1)}, u32[]{:S(2)}, u32[]{:S(2)}) collective-permute-start(bf16[192,512]{1,0:T(8,128)(2,1)S(1)} %get-tuple-element.115), channel_id=1, source_target_pairs={{0,16},{4,20},{8,24},{12,28},{16,0},{20,4},{24,8},{28,12},{1,17},{... | collective-permute-start | bytes 589832 | tf_op jit(solution)/shard_map/ppermute | solution.py:252
  (1 other events, 12.6 us)

commit v17 on v16

--- a/solution.py
+++ b/solution.py
@@ -348,30 +348,30 @@
     send_b, keep_b = weight_again(after(meta, act_kb), part, act_m, act_kb)
     got_b = swapped(send_b, "dp", 1)
     act_kc, der_kc = gelu(after(meta, send_b), kept_pick, 2 * part, part)
-    outer_1 = routed(after(crossed_1, act_kc), to_outer)
-    send_c, keep_c = weight_again(after(meta, act_kc, relayed_1), 2 * part, act_m, act_kc)
+    outer_1 = routed(after(crossed_1, send_b), to_outer)
+    send_c, keep_c = weight_again(after(meta, act_kc, relayed_1, got_a, crossed_2), 2 * part, act_m, act_kc)
     (kept_grad,) = grads(after(meta, send_c), kept, (der_ka, der_kb, der_kc), (ff,))
     inner_1 = routed(after(relayed_1, send_c), across)
 
-    out_na, mine_a = near_step(after(meta, kept_grad), (keep_a,), (got_a,))
+    out_na, mine_a = near_step(after(meta, kept_grad, outer_1), (keep_a,), (got_a,))
     got_na = swapped(out_na, "dp", 2)
-    outer_2 = routed(after(crossed_2, out_na, outer_1), to_outer)
     inner_2 = routed(after(relayed_2, out_na), across)
-    out_nb, mine_b = near_step(after(meta, out_na, crossed_2, relayed_2), (keep_b,), (got_b,))
+    out_nb, mine_b = near_step(after(meta, got_na, relayed_2), (keep_b,), (got_b,))
     got_nb = swapped(out_nb, "dp", 2)
     got_c = swapped(after(send_c, out_na), "dp", 1)
     out_fa, own_a = far_step(after(meta, out_nb, inner_1), mine_a, got_na)
     got_fa = swapped(out_fa, "dp", 4)
-    out_nc, mine_c = near_step(after(meta, out_fa, outer_2), (keep_c,), (got_c,))
+    out_nc, mine_c = near_step(after(meta, out_fa), (keep_c,), (got_c,))
     got_nc = swapped(out_nc, "dp", 2)
     out_fb, own_b = far_step(after(meta, out_nc, inner_2), mine_b, got_nb)
     got_fb = swapped(out_fb, "dp", 4)
+    outer_2 = routed(after(crossed_2, got_nc), to_outer)
+    out_fc, own_c = far_step(after(meta, out_fb), mine_c, got_nc)
+    got_fc = swapped(out_fc, "dp", 4)
     hidden_grad = kernel_call(
         place_kernel, shape(BAL, ff), [IN_VMEM] * 5,
         pl.BlockSpec((BAL, 256), lambda i, *_: (0, i)), grid=(ff // 256,),
-    )(after(meta, out_fb), kept_grad, inner_1, inner_2, outer_1, outer_2)
-    out_fc, own_c = far_step(after(meta, out_fb), mine_c, got_nc)
-    got_fc = swapped(out_fc, "dp", 4)
+    )(after(meta, out_fc), kept_grad, inner_1, inner_2, outer_1, outer_2)
     total = [a + b.astype(F32) for a, b in ((own_a, got_fa), (own_b, got_fb), (own_c, got_fc))]
     down_grad = jnp.concatenate(total, axis=1) / math.sqrt(n * home)
 

time: 137 us -> 152 us (1.11)
  starting transfers between devices: 32.8 us -> 52.5 us
  waiting for transfers between devices: 55 us -> 50.3 us
    ppermute x15, starting transfers between devices: 19.1 us -> 38.7 us  [swapped(): return lax.ppermute(block, axis, [(i, i ^ distance) for i in range(n)])]
    ppermute x15, waiting for transfers between devices: 48.2 us -> 38.4 us  [swapped(): return lax.ppermute(block, axis, [(i, i ^ distance) for i in range(n)])]
    ppermute x8, waiting for transfers between devices: 6.84 us -> 11.9 us  [routed(): lax.ppermute(block, 'dp', [(2 * a + x, 2 * b + x) for a, b in pairs for x...]
  transfers between devices with their start and end apart: 23 -> 23, of which waited for: 8 -> 9; matrix products, arithmetic and copies ran while one was open for 0% -> 1% of each run, Pallas kernels for 31% -> 26%
where the time goes in v17:
time: 152 us
  starting transfers between devices  52.5 us (35%)
  waiting for transfers between devices  50.3 us (33%)
  Pallas kernels  46 us (30%)
  other arithmetic  1.99 us (1%)
    ppermute x15, starting transfers between devices, swapped(): return lax.ppermute(block, axis, [(i, i ^ distance) for i in range(n)])  38.7 us
    ppermute x15, waiting for transfers between devices, swapped(): return lax.ppermute(block, axis, [(i, i ^ distance) for i in range(n)])  38.4 us
    pallas_call x4, Pallas kernels, gelu(): kernel_call(functools.partial(gelu_kernel, base, block), [shape(rows, col...  16.8 us
    ppermute x8, starting transfers between devices, routed(): lax.ppermute(block, 'dp', [(2 * a + x, 2 * b + x) for a, b in pairs for x...  13.8 us
    ppermute x8, waiting for transfers between devices, routed(): lax.ppermute(block, 'dp', [(2 * a + x, 2 * b + x) for a, b in pairs for x...  11.9 us
    pallas_call x2, Pallas kernels, grads(): kernel_call(functools.partial(grad_kernel, len(slopes), 256), [shape(rows...  6.97 us
    pallas_call x2, Pallas kernels, weight_again(): kernel_call(functools.partial(again_kernel, base), [shape(features // 2,...  6.52 us
    pallas_call x1, Pallas kernels, shards(): kernel_call(first_kernel, [shape(SEND, width), shape(KEEP, width), shape(...  3.73 us
  transfers between devices with their start and end apart: 23, of which 9 were waited for; matrix products, arithmetic and copies ran while one was open for 1% of the time, Pallas kernels for 26%

profile of v17, /device:TPU:0, one launch (start us, length us, event | category | flops | bytes accessed | tf_op | source)
XLA Modules:
  0.0 151.7 jit_solution(5937183412161877431)
XLA Ops:
  1.4 3.7 %shard_map.77 = (bf16[528,384]{1,0:T(8,128)(2,1)S(1)}, bf16[528,384]{1,0:T(8,128)(2,1)S(1)}, bf16[528,1032]{1,0:T(8,128)(2,1)S(1)}, bf16[528,1032]{1,0:T(8,128)(2,1)S(1)}, bf16[1032,1536]{1,0:T(8,128)(2,1)S(1)}) custom-call(s32[9,8]{1,0:T(8,128)S(1)} %pad_add_fusion.meta, bf16[1032,384]{1,0:T(8,128)(2,1)} %cot_hbm.1, f32[1536]{0:T(1024)} %scale_hbm.1, ...), custom_call_target="tpu_custom_call" | custom-call | flops 1 | bytes 1 | tf_op jit(solution)/shard_map/pallas_call | solution.py:322
  8.6 7.8 %shard_map.78 = (bf16[528,1536]{1,0:T(8,128)(2,1)S(1)}, f32[528,1536]{1,0:T(8,128)S(1)}) custom-call(s32[9,8]{1,0:T(8,128)S(1)} %pad_add_fusion.meta, bf16[528,1032]{1,0:T(8,128)(2,1)S(1)} %get-tuple-element.62.pick, bf16[1032,1536]{1,0:T(8,128)(2,1)S(1)} %get-tuple-element.63.pre), custom_call_target="tpu_custom_call" | custom-call | flops 1 | bytes 1 | tf_op jit(solution)/shard_map/pallas_call | solution.py:283
  16.4 3.0 %shard_map.79 = (bf16[528,512]{1,0:T(8,128)(2,1)S(1)}, f32[528,512]{1,0:T(8,128)S(1)}) custom-call(s32[9,8]{1,0:T(8,128)S(1)} %pad_add_fusion.meta, bf16[528,1032]{1,0:T(8,128)(2,1)S(1)} %get-tuple-element.66.pick, bf16[1032,1536]{1,0:T(8,128)(2,1)S(1)} %get-tuple-element.63.pre), custom_call_target="tpu_custom_call" | custom-call | flops 1 | bytes 1 | tf_op jit(solution)/shard_map/pallas_call | solution.py:283
  21.3 3.5 %shard_map.80 = (bf16[528,768]{1,0:T(8,128)(2,1)S(1)}, bf16[528,768]{1,0:T(8,128)(2,1)S(1)}) custom-call(s32[9,8]{1,0:T(8,128)S(1)} %pad_add_fusion.meta, bf16[528,384]{1,0:T(8,128)(2,1)S(1)} %get-tuple-element.60.p0.refs_0_, bf16[528,384]{1,0:T(8,128)(2,1)S(1)} %collective-permute-done.1.p1.refs_1_, bf16[528,384]{1,0:T(8,128)(2,1)S(1)} %collective-permute-done.p2.refs_2_, ...), custom_call_target="tpu_custom_call" | custom-call | flops 1 | bytes 1 | tf_op jit(solution)/shard_map/pallas_call | solution.py:305
  25.5 5.8 %collective-permute-done.4.refs_6_.p2 = bf16[528,384]{1,0:T(8,128)(2,1)S(1)} collective-permute-done((bf16[528,384]{1,0:T(8,128)(2,1)S(1)}, bf16[528,384]{1,0:T(8,128)(2,1)S(1)}, u32[]{:S(2)}, u32[]{:S(2)}) %collective-permute-start.4) | collective-permute-done | bytes 405536 | tf_op jit(solution)/shard_map/ppermute | solution.py:252
  31.4 3.5 %collective-permute-start.6 = (bf16[528,768]{1,0:T(8,128)(2,1)S(1)}, bf16[528,768]{1,0:T(8,128)(2,1)S(1)}, u32[]{:S(2)}, u32[]{:S(2)}) collective-permute-start(bf16[528,768]{1,0:T(8,128)(2,1)S(1)} %get-tuple-element.72), channel_id=1, source_target_pairs={{0,8},{4,12},{24,16},{28,20},{1,9},{5,13},{25,17},{29,21},{2,10},{... | collective-permute-start | bytes 2433032 | tf_op jit(solution)/shard_map/ppermute | solution.py:256
  35.6 3.4 %shard_map.81 = (bf16[768,512]{1,0:T(8,128)(2,1)S(1)}, f32[768,512]{1,0:T(8,128)S(1)}, bf16[1536,528]{1,0:T(8,128)(2,1)S(1)}, bf16[1536,528]{1,0:T(8,128)(2,1)S(1)}) custom-call(s32[9,8]{1,0:T(8,128)S(1)} %pad_add_fusion.meta, bf16[528,384]{1,0:T(8,128)(2,1)S(1)} %get-tuple-element.60.p0.refs_0_, bf16[528,384]{1,0:T(8,128)(2,1)S(1)} %collective-permute-done.1.p1.refs_1_, ...), custom_call_target="tpu_custom_call" | custom-call | flops 1 | bytes 1 | tf_op jit(solution)/shard_map/pallas_call | solution.py:290
  40.5 3.0 %shard_map.82 = (bf16[528,512]{1,0:T(8,128)(2,1)S(1)}, f32[528,512]{1,0:T(8,128)S(1)}) custom-call(s32[9,8]{1,0:T(8,128)S(1)} %pad_add_fusion.meta, bf16[528,1032]{1,0:T(8,128)(2,1)S(1)} %get-tuple-element.66.pick, bf16[1032,1536]{1,0:T(8,128)(2,1)S(1)} %get-tuple-element.63.pre), custom_call_target="tpu_custom_call" | custom-call | flops 1 | bytes 1 | tf_op jit(solution)/shard_map/pallas_call | solution.py:283
  43.6 3.3 %shard_map.83 = (bf16[768,512]{1,0:T(8,128)(2,1)S(1)}, f32[768,512]{1,0:T(8,128)S(1)}) custom-call(s32[9,8]{1,0:T(8,128)S(1)} %pad_add_fusion.meta, bf16[1536,528]{1,0:T(8,128)(2,1)S(1)} %get-tuple-element.80.lhs_moved, bf16[1536,528]{1,0:T(8,128)(2,1)S(1)} %get-tuple-element.81.lhs_kept, bf16[528,1536]{1,0:T(8,128)(2,1)S(1)} %get-tuple-element.64.refs_8_.act_moved, ...), custom_call_target="tpu_custom_call" | custom-call | flops 1 | bytes 1 | tf_op jit(solution)/shard_map/pallas_call | solution.py:298
  48.3 4.6 %collective-permute-start.12 = (bf16[528,768]{1,0:T(8,128)(2,1)S(1)}, bf16[528,768]{1,0:T(8,128)(2,1)S(1)}, u32[]{:S(2)}, u32[]{:S(2)}) collective-permute-start(bf16[528,768]{1,0:T(8,128)(2,1)S(1)} %get-tuple-element.73), channel_id=1, source_target_pairs={{0,8},{4,12},{24,16},{28,20},{1,9},{5,13},{25,17},{29,21},{2,10},{... | collective-permute-start | bytes 2433032 | tf_op jit(solution)/shard_map/ppermute | solution.py:256
  53.0 3.0 %shard_map.84 = (bf16[528,512]{1,0:T(8,128)(2,1)S(1)}, f32[528,512]{1,0:T(8,128)S(1)}) custom-call(s32[9,8]{1,0:T(8,128)S(1)} %pad_add_fusion.meta, bf16[528,1032]{1,0:T(8,128)(2,1)S(1)} %get-tuple-element.66.pick, bf16[1032,1536]{1,0:T(8,128)(2,1)S(1)} %get-tuple-element.63.pre), custom_call_target="tpu_custom_call" | custom-call | flops 1 | bytes 1 | tf_op jit(solution)/shard_map/pallas_call | solution.py:283
  58.7 3.3 %shard_map.85 = (bf16[768,512]{1,0:T(8,128)(2,1)S(1)}, f32[768,512]{1,0:T(8,128)S(1)}) custom-call(s32[9,8]{1,0:T(8,128)S(1)} %pad_add_fusion.meta, bf16[1536,528]{1,0:T(8,128)(2,1)S(1)} %get-tuple-element.80.lhs_moved, bf16[1536,528]{1,0:T(8,128)(2,1)S(1)} %get-tuple-element.81.lhs_kept, bf16[528,1536]{1,0:T(8,128)(2,1)S(1)} %get-tuple-element.64.refs_8_.act_moved, ...), custom_call_target="tpu_custom_call" | custom-call | flops 1 | bytes 1 | tf_op jit(solution)/shard_map/pallas_call | solution.py:298
  64.3 3.5 %shard_map.86.kept = bf16[528,1536]{1,0:T(8,128)(2,1)S(1)} custom-call(s32[9,8]{1,0:T(8,128)S(1)} %pad_add_fusion.meta, bf16[528,384]{1,0:T(8,128)(2,1)S(1)} %get-tuple-element.68.refs_4_.p0, bf16[528,384]{1,0:T(8,128)(2,1)S(1)} %collective-permute-done.2.refs_5_.p1, bf16[528,384]{1,0:T(8,128)(2,1)S(1)} %collective-permute-done.4.refs_6_.p2, ...), custom_call_target="tpu_custom_call" | custom-call | flops 1 | bytes 1 | tf_op jit(solution)/shard_map/pallas_call | solution.py:305
  70.9 10.6 %collective-permute-start.11 = (bf16[384,512]{1,0:T(8,128)(2,1)S(1)}, bf16[384,512]{1,0:T(8,128)(2,1)S(1)}, u32[]{:S(2)}, u32[]{:S(2)}) collective-permute-start(bf16[384,512]{1,0:T(8,128)(2,1)S(1)} %get-tuple-element.94), channel_id=1, source_target_pairs={{0,8},{4,12},{8,0},{12,4},{16,24},{20,28},{24,16},{28,20},{1,9},{5... | collective-permute-start | bytes 1179656 | tf_op jit(solution)/shard_map/ppermute | solution.py:252
  81.5 7.5 %collective-permute-done.11.got = bf16[384,512]{1,0:T(8,128)(2,1)S(1)} collective-permute-done((bf16[384,512]{1,0:T(8,128)(2,1)S(1)}, bf16[384,512]{1,0:T(8,128)(2,1)S(1)}, u32[]{:S(2)}, u32[]{:S(2)}) %collective-permute-start.11) | collective-permute-done | bytes 393248 | tf_op jit(solution)/shard_map/ppermute | solution.py:252
  89.9 4.1 %collective-permute-start.17 = (bf16[384,512]{1,0:T(8,128)(2,1)S(1)}, bf16[384,512]{1,0:T(8,128)(2,1)S(1)}, u32[]{:S(2)}, u32[]{:S(2)}) collective-permute-start(bf16[384,512]{1,0:T(8,128)(2,1)S(1)} %get-tuple-element.97), channel_id=1, source_target_pairs={{0,8},{4,12},{8,0},{12,4},{16,24},{20,28},{24,16},{28,20},{1,9},{5... | collective-permute-start | bytes 1179656 | tf_op jit(solution)/shard_map/ppermute | solution.py:252
  94.9 3.6 %collective-permute-done.15.refs_1_ = bf16[768,512]{1,0:T(8,128)(2,1)S(1)} collective-permute-done((bf16[768,512]{1,0:T(8,128)(2,1)S(1)}, bf16[768,512]{1,0:T(8,128)(2,1)S(1)}, u32[]{:S(2)}, u32[]{:S(2)}) %collective-permute-start.15) | collective-permute-done | bytes 786464 | tf_op jit(solution)/shard_map/ppermute | solution.py:252
  99.5 9.5 %collective-permute-start.18 = (bf16[384,512]{1,0:T(8,128)(2,1)S(1)}, bf16[384,512]{1,0:T(8,128)(2,1)S(1)}, u32[]{:S(2)}, u32[]{:S(2)}) collective-permute-start(bf16[384,512]{1,0:T(8,128)(2,1)S(1)} %get-tuple-element.105), channel_id=1, source_target_pairs={{0,8},{4,12},{8,0},{12,4},{16,24},{20,28},{24,16},{28,20},{1,9},{5... | collective-permute-start | bytes 1179656 | tf_op jit(solution)/shard_map/ppermute | solution.py:252
  109.7 3.0 %collective-permute-start.21 = (bf16[192,512]{1,0:T(8,128)(2,1)S(1)}, bf16[192,512]{1,0:T(8,128)(2,1)S(1)}, u32[]{:S(2)}, u32[]{:S(2)}) collective-permute-start(bf16[192,512]{1,0:T(8,128)(2,1)S(1)} %get-tuple-element.109), channel_id=1, source_target_pairs={{0,16},{4,20},{8,24},{12,28},{16,0},{20,4},{24,8},{28,12},{1,17},{... | collective-permute-start | bytes 589832 | tf_op jit(solution)/shard_map/ppermute | solution.py:252
  112.7 10.8 %collective-permute-done.18.got = bf16[384,512]{1,0:T(8,128)(2,1)S(1)} collective-permute-done((bf16[384,512]{1,0:T(8,128)(2,1)S(1)}, bf16[384,512]{1,0:T(8,128)(2,1)S(1)}, u32[]{:S(2)}, u32[]{:S(2)}) %collective-permute-start.18) | collective-permute-done | bytes 393248 | tf_op jit(solution)/shard_map/ppermute | solution.py:252
  125.7 3.8 %collective-permute-start.22 = (bf16[192,512]{1,0:T(8,128)(2,1)S(1)}, bf16[192,512]{1,0:T(8,128)(2,1)S(1)}, u32[]{:S(2)}, u32[]{:S(2)}) collective-permute-start(bf16[192,512]{1,0:T(8,128)(2,1)S(1)} %get-tuple-element.112), channel_id=1, source_target_pairs={{0,16},{4,20},{8,24},{12,28},{16,0},{20,4},{24,8},{28,12},{1,17},{... | collective-permute-start | bytes 589832 | tf_op jit(solution)/shard_map/ppermute | solution.py:252
  129.5 6.7 %collective-permute-done.22 = bf16[192,512]{1,0:T(8,128)(2,1)S(1)} collective-permute-done((bf16[192,512]{1,0:T(8,128)(2,1)S(1)}, bf16[192,512]{1,0:T(8,128)(2,1)S(1)}, u32[]{:S(2)}, u32[]{:S(2)}) %collective-permute-start.22) | collective-permute-done | bytes 196640 | tf_op jit(solution)/shard_map/ppermute | solution.py:252
  137.4 11.0 %collective-permute-done.19.outer_2 = bf16[528,768]{1,0:T(8,128)(2,1)S(1)} collective-permute-done((bf16[528,768]{1,0:T(8,128)(2,1)S(1)}, bf16[528,768]{1,0:T(8,128)(2,1)S(1)}, u32[]{:S(2)}, u32[]{:S(2)}) %collective-permute-start.19) | collective-permute-done | bytes 811040 | tf_op jit(solution)/shard_map/ppermute | solution.py:256
  148.4 3.3 %shard_map.93 = bf16[720,1536]{1,0:T(8,128)(2,1)} custom-call(s32[9,8]{1,0:T(8,128)S(1)} %pad_add_fusion.meta, bf16[528,1536]{1,0:T(8,128)(2,1)S(1)} %shard_map.86.kept, bf16[528,768]{1,0:T(8,128)(2,1)S(1)} %collective-permute-done.14.inner_1, bf16[528,768]{1,0:T(8,128)(2,1)S(1)} %collective-permute-done.16.inner_2, ...), custom_call_target="tpu_custom_call" | custom-call | flops 1 | bytes 1 | tf_op jit(solution)/shard_map/pallas_call | solution.py:371
  (50 shorter events, 25.6 us)
Async XLA Ops:
  1.4 19.9 %slice-start = ((s8[4718592]{0:T(1024)(128)(4,1)}), s8[4194304]{0:T(1024)(128)(4,1)S(1)}, s32[]{:S(2)}) async-start(s8[4718592]{0:T(1024)(128)(4,1)} %bitcast.2), calls=%async_computation | async-start | bytes 8388608
  5.1 14.4 %collective-permute-start.1 = (bf16[528,384]{1,0:T(8,128)(2,1)S(1)}, bf16[528,384]{1,0:T(8,128)(2,1)S(1)}, u32[]{:S(2)}, u32[]{:S(2)}) collective-permute-start(bf16[528,384]{1,0:T(8,128)(2,1)S(1)} %get-tuple-element.60.p0.refs_0_), channel_id=1, source_target_pairs={{0,1},{1,0},{2,3},{3,2},{4,5},{5,4},{6,7},{7,6},{8,9},{9,8},{10,11... | collective-permute-start | bytes 1216520 | tf_op jit(solution)/shard_map/ppermute | solution.py:252
  5.6 13.8 %collective-permute-start.2 = (bf16[528,384]{1,0:T(8,128)(2,1)S(1)}, bf16[528,384]{1,0:T(8,128)(2,1)S(1)}, u32[]{:S(2)}, u32[]{:S(2)}) collective-permute-start(bf16[528,384]{1,0:T(8,128)(2,1)S(1)} %get-tuple-element.68.refs_4_.p0), channel_id=1, source_target_pairs={{0,1},{1,0},{2,3},{3,2},{4,5},{5,4},{6,7},{7,6},{8,9},{9,8},{10,11... | collective-permute-start | bytes 1216520 | tf_op jit(solution)/shard_map/ppermute | solution.py:252
  5.7 13.8 %collective-permute-start = (bf16[528,384]{1,0:T(8,128)(2,1)S(1)}, bf16[528,384]{1,0:T(8,128)(2,1)S(1)}, u32[]{:S(2)}, u32[]{:S(2)}) collective-permute-start(bf16[528,384]{1,0:T(8,128)(2,1)S(1)} %get-tuple-element.60.p0.refs_0_), channel_id=1, source_target_pairs={{0,2},{1,3},{2,0},{3,1},{4,6},{5,7},{6,4},{7,5},{8,10},{9,11},{10,... | collective-permute-start | bytes 1216520 | tf_op jit(solution)/shard_map/ppermute | solution.py:252
  19.5 1.8 %collective-permute-start.3 = (bf16[528,384]{1,0:T(8,128)(2,1)S(1)}, bf16[528,384]{1,0:T(8,128)(2,1)S(1)}, u32[]{:S(2)}, u32[]{:S(2)}) collective-permute-start(bf16[528,384]{1,0:T(8,128)(2,1)S(1)} %collective-permute-done.p2.refs_2_), channel_id=1, source_target_pairs={{0,1},{1,0},{2,3},{3,2},{4,5},{5,4},{6,7},{7,6},{8,9},{9,8},{10,11... | collective-permute-start | bytes 1216520 | tf_op jit(solution)/shard_map/ppermute | solution.py:252
  19.6 11.8 %collective-permute-start.4 = (bf16[528,384]{1,0:T(8,128)(2,1)S(1)}, bf16[528,384]{1,0:T(8,128)(2,1)S(1)}, u32[]{:S(2)}, u32[]{:S(2)}) collective-permute-start(bf16[528,384]{1,0:T(8,128)(2,1)S(1)} %get-tuple-element.68.refs_4_.p0), channel_id=1, source_target_pairs={{0,2},{1,3},{2,0},{3,1},{4,6},{5,7},{6,4},{7,5},{8,10},{9,11},{10,... | collective-permute-start | bytes 1216520 | tf_op jit(solution)/shard_map/ppermute | solution.py:252
  24.8 22.1 %collective-permute-start.9 = (bf16[528,768]{1,0:T(8,128)(2,1)S(1)}, bf16[528,768]{1,0:T(8,128)(2,1)S(1)}, u32[]{:S(2)}, u32[]{:S(2)}) collective-permute-start(bf16[528,768]{1,0:T(8,128)(2,1)S(1)} %get-tuple-element.72), channel_id=1, source_target_pairs={{8,16},{12,20},{16,8},{20,12},{9,17},{13,21},{17,9},{21,13},{10,18... | collective-permute-start | bytes 2433032 | tf_op jit(solution)/shard_map/ppermute | solution.py:256
  31.4 4.3 %collective-permute-start.5 = (bf16[528,384]{1,0:T(8,128)(2,1)S(1)}, bf16[528,384]{1,0:T(8,128)(2,1)S(1)}, u32[]{:S(2)}, u32[]{:S(2)}) collective-permute-start(bf16[528,384]{1,0:T(8,128)(2,1)S(1)} %collective-permute-done.4.refs_6_.p2), channel_id=1, source_target_pairs={{0,1},{1,0},{2,3},{3,2},{4,5},{5,4},{6,7},{7,6},{8,9},{9,8},{10,11... | collective-permute-start | bytes 1216520 | tf_op jit(solution)/shard_map/ppermute | solution.py:252
  31.4 27.4 %collective-permute-start.6 = (bf16[528,768]{1,0:T(8,128)(2,1)S(1)}, bf16[528,768]{1,0:T(8,128)(2,1)S(1)}, u32[]{:S(2)}, u32[]{:S(2)}) collective-permute-start(bf16[528,768]{1,0:T(8,128)(2,1)S(1)} %get-tuple-element.72), channel_id=1, source_target_pairs={{0,8},{4,12},{24,16},{28,20},{1,9},{5,13},{25,17},{29,21},{2,10},{... | collective-permute-start | bytes 2433032 | tf_op jit(solution)/shard_map/ppermute | solution.py:256
  34.9 23.8 %collective-permute-start.8 = (bf16[528,768]{1,0:T(8,128)(2,1)S(1)}, bf16[528,768]{1,0:T(8,128)(2,1)S(1)}, u32[]{:S(2)}, u32[]{:S(2)}) collective-permute-start(bf16[528,768]{1,0:T(8,128)(2,1)S(1)} %get-tuple-element.73), channel_id=1, source_target_pairs={{8,16},{12,20},{16,8},{20,12},{9,17},{13,21},{17,9},{21,13},{10,18... | collective-permute-start | bytes 2433032 | tf_op jit(solution)/shard_map/ppermute | solution.py:256
  39.0 19.7 %collective-permute-start.7 = (bf16[768,512]{1,0:T(8,128)(2,1)S(1)}, bf16[768,512]{1,0:T(8,128)(2,1)S(1)}, u32[]{:S(2)}, u32[]{:S(2)}) collective-permute-start(bf16[768,512]{1,0:T(8,128)(2,1)S(1)} %get-tuple-element.76), channel_id=1, source_target_pairs={{0,4},{4,0},{8,12},{12,8},{16,20},{20,16},{24,28},{28,24},{1,5},{5... | collective-permute-start | bytes 2359304 | tf_op jit(solution)/shard_map/ppermute | solution.py:252
  46.8 21.8 %collective-permute-start.10 = (bf16[528,768]{1,0:T(8,128)(2,1)S(1)}, bf16[528,768]{1,0:T(8,128)(2,1)S(1)}, u32[]{:S(2)}, u32[]{:S(2)}) collective-permute-start(bf16[528,768]{1,0:T(8,128)(2,1)S(1)} %collective-permute-done.9), channel_id=1, source_target_pairs={{8,0},{12,4},{16,24},{20,28},{9,1},{13,5},{17,25},{21,29},{10,2},{... | collective-permute-start | bytes 2433032 | tf_op jit(solution)/shard_map/ppermute | solution.py:256
  48.3 21.9 %collective-permute-start.12 = (bf16[528,768]{1,0:T(8,128)(2,1)S(1)}, bf16[528,768]{1,0:T(8,128)(2,1)S(1)}, u32[]{:S(2)}, u32[]{:S(2)}) collective-permute-start(bf16[528,768]{1,0:T(8,128)(2,1)S(1)} %get-tuple-element.73), channel_id=1, source_target_pairs={{0,8},{4,12},{24,16},{28,20},{1,9},{5,13},{25,17},{29,21},{2,10},{... | collective-permute-start | bytes 2433032 | tf_op jit(solution)/shard_map/ppermute | solution.py:256
  62.0 32.1 %collective-permute-start.14 = (bf16[528,768]{1,0:T(8,128)(2,1)S(1)}, bf16[528,768]{1,0:T(8,128)(2,1)S(1)}, u32[]{:S(2)}, u32[]{:S(2)}) collective-permute-start(bf16[528,768]{1,0:T(8,128)(2,1)S(1)} %collective-permute-done.6), channel_id=1, source_target_pairs={{8,16},{12,20},{16,8},{20,12},{9,17},{13,21},{17,9},{21,13},{10,18... | collective-permute-start | bytes 2433032 | tf_op jit(solution)/shard_map/ppermute | solution.py:256
  62.7 26.3 %collective-permute-start.13 = (bf16[768,512]{1,0:T(8,128)(2,1)S(1)}, bf16[768,512]{1,0:T(8,128)(2,1)S(1)}, u32[]{:S(2)}, u32[]{:S(2)}) collective-permute-start(bf16[768,512]{1,0:T(8,128)(2,1)S(1)} %get-tuple-element.82), channel_id=1, source_target_pairs={{0,4},{4,0},{8,12},{12,8},{16,20},{20,16},{24,28},{28,24},{1,5},{5... | collective-permute-start | bytes 2359304 | tf_op jit(solution)/shard_map/ppermute | solution.py:252
  69.6 28.9 %collective-permute-start.15 = (bf16[768,512]{1,0:T(8,128)(2,1)S(1)}, bf16[768,512]{1,0:T(8,128)(2,1)S(1)}, u32[]{:S(2)}, u32[]{:S(2)}) collective-permute-start(bf16[768,512]{1,0:T(8,128)(2,1)S(1)} %get-tuple-element.104), channel_id=1, source_target_pairs={{0,4},{4,0},{8,12},{12,8},{16,20},{20,16},{24,28},{28,24},{1,5},{5... | collective-permute-start | bytes 2359304 | tf_op jit(solution)/shard_map/ppermute | solution.py:252
  70.2 38.7 %collective-permute-start.16 = (bf16[528,768]{1,0:T(8,128)(2,1)S(1)}, bf16[528,768]{1,0:T(8,128)(2,1)S(1)}, u32[]{:S(2)}, u32[]{:S(2)}) collective-permute-start(bf16[528,768]{1,0:T(8,128)(2,1)S(1)} %collective-permute-done.12), channel_id=1, source_target_pairs={{8,16},{12,20},{16,8},{20,12},{9,17},{13,21},{17,9},{21,13},{10,18... | collective-permute-start | bytes 2433032 | tf_op jit(solution)/shard_map/ppermute | solution.py:256
  70.9 18.1 %collective-permute-start.11 = (bf16[384,512]{1,0:T(8,128)(2,1)S(1)}, bf16[384,512]{1,0:T(8,128)(2,1)S(1)}, u32[]{:S(2)}, u32[]{:S(2)}) collective-permute-start(bf16[384,512]{1,0:T(8,128)(2,1)S(1)} %get-tuple-element.94), channel_id=1, source_target_pairs={{0,8},{4,12},{8,0},{12,4},{16,24},{20,28},{24,16},{28,20},{1,9},{5... | collective-permute-start | bytes 1179656 | tf_op jit(solution)/shard_map/ppermute | solution.py:252
  89.9 19.0 %collective-permute-start.17 = (bf16[384,512]{1,0:T(8,128)(2,1)S(1)}, bf16[384,512]{1,0:T(8,128)(2,1)S(1)}, u32[]{:S(2)}, u32[]{:S(2)}) collective-permute-start(bf16[384,512]{1,0:T(8,128)(2,1)S(1)} %get-tuple-element.97), channel_id=1, source_target_pairs={{0,8},{4,12},{8,0},{12,4},{16,24},{20,28},{24,16},{28,20},{1,9},{5... | collective-permute-start | bytes 1179656 | tf_op jit(solution)/shard_map/ppermute | solution.py:252
  99.5 24.0 %collective-permute-start.18 = (bf16[384,512]{1,0:T(8,128)(2,1)S(1)}, bf16[384,512]{1,0:T(8,128)(2,1)S(1)}, u32[]{:S(2)}, u32[]{:S(2)}) collective-permute-start(bf16[384,512]{1,0:T(8,128)(2,1)S(1)} %get-tuple-element.105), channel_id=1, source_target_pairs={{0,8},{4,12},{8,0},{12,4},{16,24},{20,28},{24,16},{28,20},{1,9},{5... | collective-permute-start | bytes 1179656 | tf_op jit(solution)/shard_map/ppermute | solution.py:252
  108.9 15.9 %collective-permute-start.20 = (bf16[192,512]{1,0:T(8,128)(2,1)S(1)}, bf16[192,512]{1,0:T(8,128)(2,1)S(1)}, u32[]{:S(2)}, u32[]{:S(2)}) collective-permute-start(bf16[192,512]{1,0:T(8,128)(2,1)S(1)} %get-tuple-element.101), channel_id=1, source_target_pairs={{0,16},{4,20},{8,24},{12,28},{16,0},{20,4},{24,8},{28,12},{1,17},{... | collective-permute-start | bytes 589832 | tf_op jit(solution)/shard_map/ppermute | solution.py:252
  109.7 19.7 %collective-permute-start.21 = (bf16[192,512]{1,0:T(8,128)(2,1)S(1)}, bf16[192,512]{1,0:T(8,128)(2,1)S(1)}, u32[]{:S(2)}, u32[]{:S(2)}) collective-permute-start(bf16[192,512]{1,0:T(8,128)(2,1)S(1)} %get-tuple-element.109), channel_id=1, source_target_pairs={{0,16},{4,20},{8,24},{12,28},{16,0},{20,4},{24,8},{28,12},{1,17},{... | collective-permute-start | bytes 589832 | tf_op jit(solution)/shard_map/ppermute | solution.py:252
  123.5 24.9 %collective-permute-start.19 = (bf16[528,768]{1,0:T(8,128)(2,1)S(1)}, bf16[528,768]{1,0:T(8,128)(2,1)S(1)}, u32[]{:S(2)}, u32[]{:S(2)}) collective-permute-start(bf16[528,768]{1,0:T(8,128)(2,1)S(1)} %collective-permute-done.8), channel_id=1, source_target_pairs={{8,0},{12,4},{16,24},{20,28},{9,1},{13,5},{17,25},{21,29},{10,2},{... | collective-permute-start | bytes 2433032 | tf_op jit(solution)/shard_map/ppermute | solution.py:256
  125.7 10.5 %collective-permute-start.22 = (bf16[192,512]{1,0:T(8,128)(2,1)S(1)}, bf16[192,512]{1,0:T(8,128)(2,1)S(1)}, u32[]{:S(2)}, u32[]{:S(2)}) collective-permute-start(bf16[192,512]{1,0:T(8,128)(2,1)S(1)} %get-tuple-element.112), channel_id=1, source_target_pairs={{0,16},{4,20},{8,24},{12,28},{16,0},{20,4},{24,8},{28,12},{1,17},{... | collective-permute-start | bytes 589832 | tf_op jit(solution)/shard_map/ppermute | solution.py:252
  (1 other events, 12.6 us)

commit v18 on v13

--- a/solution.py
+++ b/solution.py
@@ -11,7 +11,7 @@
 SEND = 528
 KEEP = 528
 TILE = 16
-EARLY = 48
+EARLY = 96
 LATE = SEND - EARLY
 SLOTS = 4
 BAL = 720
@@ -396,7 +396,7 @@
 
     act_l, der_l = gelu(after(meta, keep_01), late_pick, part, 2 * part)
     moving_b, moving_c = grads(after(meta, act_l), lates, 0, 0, LATE, part, (der_l,), (part, part))
-    act_rb, der_rb = gelu(after(meta, moving_b), rest_pick, part, part)
+    act_rb, der_rb = gelu(after(meta, moving_b, gots_a[0]), rest_pick, part, part)
     send_b, keep_b = weight_again(after(meta, act_rb, arrived_a), 0, act_l, act_rb, 1)
     got_b = swapped(send_b, "dp", 1)
     arrived_b = swapped(after(moving_b, send_b), "dp", n // 2)
@@ -411,16 +411,16 @@
     *sends_c, keep_c01, keep_c23 = weight_again(after(meta, early_yc), part, act_l, act_rc, 2)
     gots_c = [swapped(send, "dp", 1) for send in sends_c]
 
-    (kept_grad,) = grads(after(meta, keep_c01), rests, EARLY, EARLY, KEEP, 0, (der_ra, der_rb, der_rc), (ff,))
+    out_nb, mine_b = near_step(after(meta, keep_c01, arrived_b, got_na), (keep_b,), (got_b,))
+    got_nb = swapped(out_nb, "dp", 2)
+    arrived_c = swapped(after(moving_c, out_nb), "dp", n // 2)
+    (kept_grad,) = grads(after(meta, out_nb), rests, EARLY, EARLY, KEEP, 0, (der_ra, der_rb, der_rc), (ff,))
     early_grad = kernel_call(
         functools.partial(early_kernel, 256), shape(EARLY, ff), [IN_VMEM] * 5, IN_VMEM,
         [vmem((EARLY, features), BF), vmem((EARLY, 256), F32)],
     )(after(meta, kept_grad), arrived_early, early_c, early_y, early_yc, down_weight)
 
-    out_nb, mine_b = near_step(after(meta, early_grad, arrived_b, got_na), (keep_b,), (got_b,))
-    got_nb = swapped(out_nb, "dp", 2)
-    arrived_c = swapped(after(moving_c, out_nb), "dp", n // 2)
-    out_fa, own_a = far_step(after(meta, out_nb), mine_a, got_na)
+    out_fa, own_a = far_step(after(meta, early_grad), mine_a, got_na)
     got_fa = swapped(out_fa, "dp", 4)
     out_nc, mine_c = near_step(after(meta, out_fa), (keep_c01, keep_c23), gots_c)
     got_nc = swapped(out_nc, "dp", 2)

time: 136 us -> 137 us (level); the launches traced: 134 us -> 137 us
  waiting for transfers between devices: 57.2 us -> 61.8 us
  starting transfers between devices: 24.1 us -> 21.7 us
    ppermute x24, waiting for transfers between devices: 57.2 us -> 61.8 us  [swapped(): return lax.ppermute(block, axis, [(i, i ^ distance) for i in range(n)])]
    ppermute x24, starting transfers between devices: 24.1 us -> 21.7 us  [swapped(): return lax.ppermute(block, axis, [(i, i ^ distance) for i in range(n)])]
  transfers between devices with their start and end apart: 24 -> 24, of which waited for: 15 -> 14; matrix products, arithmetic and copies ran while one was open for 0% -> 0% of each run, Pallas kernels for 34% -> 34%
where the time goes in v18:
time: 137 us
  waiting for transfers between devices  61.8 us (45%)
  Pallas kernels  50.3 us (37%)
  starting transfers between devices  21.7 us (16%)
  other arithmetic  1.99 us (1%)
    ppermute x24, waiting for transfers between devices, swapped(): return lax.ppermute(block, axis, [(i, i ^ distance) for i in range(n)])  61.8 us
    ppermute x24, starting transfers between devices, swapped(): return lax.ppermute(block, axis, [(i, i ^ distance) for i in range(n)])  21.7 us
    pallas_call x5, Pallas kernels, gelu(): kernel_call(functools.partial(gelu_kernel, base, block), [shape(rows, col...  17.6 us
    pallas_call x3, Pallas kernels, grads(): kernel_call(functools.partial(grad_kernel, first_row, first_slope, base,...  7.37 us
    pallas_call x2, Pallas kernels, weight_again(): kernel_call(functools.partial(again_kernel, base), [shape(rows, part)] *...  5.77 us
    pallas_call x1, Pallas kernels, shards(): kernel_call(first_kernel, [shape(LATE, width), shape(others, width), shap...  4.47 us
    pallas_call x1, Pallas kernels, shards(): kernel_call(functools.partial(early_kernel, 256), shape(EARLY, ff), [IN_V...  3.35 us
    pallas_call x1, Pallas kernels, shards(): kernel_call(functools.partial(place_kernel, (part,) * 3), shape(BAL, ff),...  3.3 us
  transfers between devices with their start and end apart: 24, of which 14 were waited for; matrix products, arithmetic and copies ran while one was open for 0% of the time, Pallas kernels for 34%

profile of v18, /device:TPU:0, one launch (start us, length us, event | category | flops | bytes accessed | tf_op | source)
XLA Modules:
  0.0 136.7 jit_solution(2703495244103126187)
XLA Ops:
  1.4 4.5 %shard_map.77 = (bf16[432,384]{1,0:T(8,128)(2,1)S(1)}, bf16[624,384]{1,0:T(8,128)(2,1)S(1)}, bf16[96,1920]{1,0:T(8,128)(2,1)S(1)}, bf16[432,1032]{1,0:T(8,128)(2...) custom-call(s32[9,8]{1,0:T(8,128)S(1)} %pad_add_fusion.meta, bf16[1032,384]{1,0:T(8,128)(2,1)} %cot_hbm.1, ...), custom_call_target="tpu_custom_call" | custom-call | flops 1 | bytes 1 | tf_op jit(solution)/shard_map/pallas_call | solution.py:370
  6.4 3.6 %collective-permute-start = (bf16[96,1920]{1,0:T(8,128)(2,1)S(1)}, bf16[96,1920]{1,0:T(8,128)(2,1)S(1)}, u32[]{:S(2)}, u32[]{:S(2)}) collective-permute-start(bf16[96,1920]{1,0:T(8,128)(2,1)S(1)} %get-tuple-element.69), channel_id=1, source_target_pairs={{0,16},{4,20},{8,24},{12,28},{16,0},{20,4},{24,8},{28,12},{1,17},{... | collective-permute-start | bytes 1105928 | tf_op jit(solution)/shard_map/ppermute | solution.py:301
  12.2 2.8 %shard_map.78 = (bf16[432,512]{1,0:T(8,128)(2,1)S(1)}, f32[432,512]{1,0:T(8,128)S(1)}) custom-call(s32[9,8]{1,0:T(8,128)S(1)} %pad_add_fusion.meta, bf16[432,1032]{1,0:T(8,128)(2,1)S(1)} %get-tuple-element.72.pick, bf16[1032,1536]{1,0:T(8,128)(2,1)S(1)} %get-tuple-element.73.pre), custom_call_target="tpu_custom_call" | custom-call | flops 1 | bytes 1 | tf_op jit(solution)/shard_map/pallas_call | solution.py:329
  15.0 3.4 %shard_map.79 = (bf16[624,512]{1,0:T(8,128)(2,1)S(1)}, f32[624,512]{1,0:T(8,128)S(1)}) custom-call(s32[9,8]{1,0:T(8,128)S(1)} %pad_add_fusion.meta, bf16[624,1032]{1,0:T(8,128)(2,1)S(1)} %get-tuple-element.76.pick, bf16[1032,1536]{1,0:T(8,128)(2,1)S(1)} %get-tuple-element.73.pre), custom_call_target="tpu_custom_call" | custom-call | flops 1 | bytes 1 | tf_op jit(solution)/shard_map/pallas_call | solution.py:329
  18.4 2.3 %collective-permute-done.1.p2.refs_2_ = bf16[432,384]{1,0:T(8,128)(2,1)S(1)} collective-permute-done((bf16[432,384]{1,0:T(8,128)(2,1)S(1)}, bf16[432,384]{1,0:T(8,128)(2,1)S(1)}, u32[]{:S(2)}, u32[]{:S(2)}) %collective-permute-start.1) | collective-permute-done | bytes 331808 | tf_op jit(solution)/shard_map/ppermute | solution.py:301
  20.8 6.3 %collective-permute-done.own = bf16[96,1920]{1,0:T(8,128)(2,1)S(1)} collective-permute-done((bf16[96,1920]{1,0:T(8,128)(2,1)S(1)}, bf16[96,1920]{1,0:T(8,128)(2,1)S(1)}, u32[]{:S(2)}, u32[]{:S(2)}) %collective-permute-start) | collective-permute-done | bytes 368672 | tf_op jit(solution)/shard_map/ppermute | solution.py:301
  32.3 3.0 %shard_map.81 = (bf16[384,512]{1,0:T(8,128)(2,1)S(1)}, bf16[384,512]{1,0:T(8,128)(2,1)S(1)}, f32[384,512]{1,0:T(8,128)S(1)}, f32[384,512]{1,0:T(8,128)S(1)}, bf1...) custom-call(s32[9,8]{1,0:T(8,128)S(1)} %pad_add_fusion.meta, ...), custom_call_target="tpu_custom_call" | custom-call | flops 1 | bytes 1 | tf_op jit(solution)/shard_map/pallas_call | solution.py:336
  36.9 4.6 %shard_map.82 = (bf16[432,1024]{1,0:T(8,128)(2,1)S(1)}, f32[432,1024]{1,0:T(8,128)S(1)}) custom-call(s32[9,8]{1,0:T(8,128)S(1)} %pad_add_fusion.meta, bf16[432,1032]{1,0:T(8,128)(2,1)S(1)} %get-tuple-element.72.pick, bf16[1032,1536]{1,0:T(8,128)(2,1)S(1)} %get-tuple-element.73.pre), custom_call_target="tpu_custom_call" | custom-call | flops 1 | bytes 1 | tf_op jit(solution)/shard_map/pallas_call | solution.py:329
  42.1 2.3 %shard_map.83 = (bf16[432,512]{1,0:T(8,128)(2,1)S(1)}, bf16[432,512]{1,0:T(8,128)(2,1)S(1)}) custom-call(s32[9,8]{1,0:T(8,128)S(1)} %pad_add_fusion.meta, bf16[432,384]{1,0:T(8,128)(2,1)S(1)} %get-tuple-element.70.p0.refs_0_, bf16[432,384]{1,0:T(8,128)(2,1)S(1)} %collective-permute-done.2.p1.refs_1_, bf16[432,384]{1,0:T(8,128)(2,1)S(1)} %collective-permute-done.1.p2.refs_2_, ...), custom_call_target="tpu_custom_call" | custom-call | flops 1 | bytes 1 | tf_op jit(solution)/shard_map/pallas_call | solution.py:352
  44.4 2.9 %collective-permute-done.7.refs_2_ = bf16[384,512]{1,0:T(8,128)(2,1)S(1)} collective-permute-done((bf16[384,512]{1,0:T(8,128)(2,1)S(1)}, bf16[384,512]{1,0:T(8,128)(2,1)S(1)}, u32[]{:S(2)}, u32[]{:S(2)}) %collective-permute-start.7) | collective-permute-done | bytes 393248 | tf_op jit(solution)/shard_map/ppermute | solution.py:301
  47.3 3.4 %shard_map.84 = (bf16[624,512]{1,0:T(8,128)(2,1)S(1)}, f32[624,512]{1,0:T(8,128)S(1)}) custom-call(s32[9,8]{1,0:T(8,128)S(1)} %pad_add_fusion.meta, bf16[624,1032]{1,0:T(8,128)(2,1)S(1)} %get-tuple-element.76.pick, bf16[1032,1536]{1,0:T(8,128)(2,1)S(1)} %get-tuple-element.73.pre), custom_call_target="tpu_custom_call" | custom-call | flops 1 | bytes 1 | tf_op jit(solution)/shard_map/pallas_call | solution.py:329
  50.7 2.7 %collective-permute-done.8.rest_0_ = bf16[432,512]{1,0:T(8,128)(2,1)S(1)} collective-permute-done((bf16[432,512]{1,0:T(8,128)(2,1)S(1)}, bf16[432,512]{1,0:T(8,128)(2,1)S(1)}, u32[]{:S(2)}, u32[]{:S(2)}) %collective-permute-start.8) | collective-permute-done | bytes 442400 | tf_op jit(solution)/shard_map/ppermute | solution.py:301
  53.4 2.9 %shard_map.85 = (bf16[768,512]{1,0:T(8,128)(2,1)S(1)}, f32[768,512]{1,0:T(8,128)S(1)}) custom-call(s32[9,8]{1,0:T(8,128)S(1)} %pad_add_fusion.meta, bf16[1536,432]{1,0:T(8,128)(2,1)S(1)} %get-tuple-element.94.lhs_moved, bf16[1536,624]{1,0:T(8,128)(2,1)S(1)} %get-tuple-element.95.lhs_kept, bf16[432,1024]{1,0:T(8,128)(2,1)S(1)} %get-tuple-element.86.act_moved, ...), custom_call_target="tpu_custom_call" | custom-call | flops 1 | bytes 1 | tf_op jit(solution)/shard_map/pallas_call | solution.py:345
  62.3 3.4 %shard_map.87 = (bf16[624,512]{1,0:T(8,128)(2,1)S(1)}, f32[624,512]{1,0:T(8,128)S(1)}) custom-call(s32[9,8]{1,0:T(8,128)S(1)} %pad_add_fusion.meta, bf16[624,1032]{1,0:T(8,128)(2,1)S(1)} %get-tuple-element.76.pick, bf16[1032,1536]{1,0:T(8,128)(2,1)S(1)} %get-tuple-element.73.pre), custom_call_target="tpu_custom_call" | custom-call | flops 1 | bytes 1 | tf_op jit(solution)/shard_map/pallas_call | solution.py:329
  67.2 2.9 %shard_map.88 = (bf16[384,512]{1,0:T(8,128)(2,1)S(1)}, bf16[384,512]{1,0:T(8,128)(2,1)S(1)}, f32[384,512]{1,0:T(8,128)S(1)}, f32[384,512]{1,0:T(8,128)S(1)}) custom-call(s32[9,8]{1,0:T(8,128)S(1)} %pad_add_fusion.meta, bf16[1536,432]{1,0:T(8,128)(2,1)S(1)} %get-tuple-element.94.lhs_moved, bf16[1536,624]{1,0:T(8,128)(2,1)S(1)} %get-tuple-element.95.lhs_kept, ...), custom_call_target="tpu_custom_call" | custom-call | flops 1 | bytes 1 | tf_op jit(solution)/shard_map/pallas_call | solution.py:345
  72.2 6.7 %collective-permute-done.14.got = bf16[384,512]{1,0:T(8,128)(2,1)S(1)} collective-permute-done((bf16[384,512]{1,0:T(8,128)(2,1)S(1)}, bf16[384,512]{1,0:T(8,128)(2,1)S(1)}, u32[]{:S(2)}, u32[]{:S(2)}) %collective-permute-start.14) | collective-permute-done | bytes 393248 | tf_op jit(solution)/shard_map/ppermute | solution.py:301
  80.2 3.5 %shard_map.90.kept = bf16[528,1536]{1,0:T(8,128)(2,1)S(1)} custom-call(s32[9,8]{1,0:T(8,128)S(1)} %pad_add_fusion.meta, bf16[624,384]{1,0:T(8,128)(2,1)S(1)} %get-tuple-element.78.refs_4_.p0, bf16[624,384]{1,0:T(8,128)(2,1)S(1)} %collective-permute-done.3.refs_5_.p1, bf16[624,384]{1,0:T(8,128)(2,1)S(1)} %collective-permute-done.5.refs_6_.p2, ...), custom_call_target="tpu_custom_call" | custom-call | flops 1 | bytes 1 | tf_op jit(solution)/shard_map/pallas_call | solution.py:352
  83.7 3.4 %shard_map.91.early = bf16[96,1536]{1,0:T(8,128)(2,1)S(1)} custom-call(s32[9,8]{1,0:T(8,128)S(1)} %pad_add_fusion.meta, bf16[96,1920]{1,0:T(8,128)(2,1)S(1)} %collective-permute-done.own, bf16[96,384]{1,0:T(8,128)(2,1)S(1)} %collective-permute-done.11.p1, bf16[96,384]{1,0:T(8,128)(2,1)S(1)} %collective-permute-done.10.p2, ...), custom_call_target="tpu_custom_call" | custom-call | flops 1 | bytes 1 | tf_op jit(solution)/shard_map/pallas_call | solution.py:418
  87.8 2.7 %collective-permute-start.19 = (bf16[192,512]{1,0:T(8,128)(2,1)S(1)}, bf16[192,512]{1,0:T(8,128)(2,1)S(1)}, u32[]{:S(2)}, u32[]{:S(2)}) collective-permute-start(bf16[192,512]{1,0:T(8,128)(2,1)S(1)} %get-tuple-element.118), channel_id=1, source_target_pairs={{0,16},{4,20},{8,24},{12,28},{16,0},{20,4},{24,8},{28,12},{1,17},{... | collective-permute-start | bytes 589832 | tf_op jit(solution)/shard_map/ppermute | solution.py:301
  96.4 13.9 %collective-permute-done.19 = bf16[192,512]{1,0:T(8,128)(2,1)S(1)} collective-permute-done((bf16[192,512]{1,0:T(8,128)(2,1)S(1)}, bf16[192,512]{1,0:T(8,128)(2,1)S(1)}, u32[]{:S(2)}, u32[]{:S(2)}) %collective-permute-start.19) | collective-permute-done | bytes 196640 | tf_op jit(solution)/shard_map/ppermute | solution.py:301
  110.3 13.6 %collective-permute-done.20.rest_2_ = bf16[432,512]{1,0:T(8,128)(2,1)S(1)} collective-permute-done((bf16[432,512]{1,0:T(8,128)(2,1)S(1)}, bf16[432,512]{1,0:T(8,128)(2,1)S(1)}, u32[]{:S(2)}, u32[]{:S(2)}) %collective-permute-start.20) | collective-permute-done | bytes 442400 | tf_op jit(solution)/shard_map/ppermute | solution.py:301
  124.9 3.3 %shard_map.96 = bf16[720,1536]{1,0:T(8,128)(2,1)} custom-call(s32[9,8]{1,0:T(8,128)S(1)} %pad_add_fusion.meta, bf16[528,1536]{1,0:T(8,128)(2,1)S(1)} %shard_map.90.kept, bf16[96,1536]{1,0:T(8,128)(2,1)S(1)} %shard_map.91.early, bf16[432,512]{1,0:T(8,128)(2,1)S(1)} %collective-permute-done.8.rest_0_, bf16[432,512]{1,0:T(8,128)(2,1)S(1)} %collective-permute-done.13.rest_1_, ...), custom_call_target="tpu_custom_call" | custom-call | flops 1 | bytes 1 | tf_op jit(solution)/shard_map/pallas_call | solution.py:434
  128.2 4.2 %collective-permute-done.22 = bf16[192,512]{1,0:T(8,128)(2,1)S(1)} collective-permute-done((bf16[192,512]{1,0:T(8,128)(2,1)S(1)}, bf16[192,512]{1,0:T(8,128)(2,1)S(1)}, u32[]{:S(2)}, u32[]{:S(2)}) %collective-permute-start.22) | collective-permute-done | bytes 196640 | tf_op jit(solution)/shard_map/ppermute | solution.py:301
  132.5 3.0 %collective-permute-done.23 = bf16[192,512]{1,0:T(8,128)(2,1)S(1)} collective-permute-done((bf16[192,512]{1,0:T(8,128)(2,1)S(1)}, bf16[192,512]{1,0:T(8,128)(2,1)S(1)}, u32[]{:S(2)}, u32[]{:S(2)}) %collective-permute-start.23) | collective-permute-done | bytes 196640 | tf_op jit(solution)/shard_map/ppermute | solution.py:301
  (56 shorter events, 30.4 us)
Async XLA Ops:
  5.8 21.3 %collective-permute-start.3 = (bf16[624,384]{1,0:T(8,128)(2,1)S(1)}, bf16[624,384]{1,0:T(8,128)(2,1)S(1)}, u32[]{:S(2)}, u32[]{:S(2)}) collective-permute-start(bf16[624,384]{1,0:T(8,128)(2,1)S(1)} %get-tuple-element.78.refs_4_.p0), channel_id=1, source_target_pairs={{0,1},{1,0},{2,3},{3,2},{4,5},{5,4},{6,7},{7,6},{8,9},{9,8},{10,11... | collective-permute-start | bytes 1437704 | tf_op jit(solution)/shard_map/ppermute | solution.py:301
  6.4 20.7 %collective-permute-start = (bf16[96,1920]{1,0:T(8,128)(2,1)S(1)}, bf16[96,1920]{1,0:T(8,128)(2,1)S(1)}, u32[]{:S(2)}, u32[]{:S(2)}) collective-permute-start(bf16[96,1920]{1,0:T(8,128)(2,1)S(1)} %get-tuple-element.69), channel_id=1, source_target_pairs={{0,16},{4,20},{8,24},{12,28},{16,0},{20,4},{24,8},{28,12},{1,17},{... | collective-permute-start | bytes 1105928 | tf_op jit(solution)/shard_map/ppermute | solution.py:301
  10.0 8.4 %collective-permute-start.2 = (bf16[432,384]{1,0:T(8,128)(2,1)S(1)}, bf16[432,384]{1,0:T(8,128)(2,1)S(1)}, u32[]{:S(2)}, u32[]{:S(2)}) collective-permute-start(bf16[432,384]{1,0:T(8,128)(2,1)S(1)} %get-tuple-element.70.p0.refs_0_), channel_id=1, source_target_pairs={{0,1},{1,0},{2,3},{3,2},{4,5},{5,4},{6,7},{7,6},{8,9},{9,8},{10,11... | collective-permute-start | bytes 995336 | tf_op jit(solution)/shard_map/ppermute | solution.py:301
  10.2 10.6 %collective-permute-start.1 = (bf16[432,384]{1,0:T(8,128)(2,1)S(1)}, bf16[432,384]{1,0:T(8,128)(2,1)S(1)}, u32[]{:S(2)}, u32[]{:S(2)}) collective-permute-start(bf16[432,384]{1,0:T(8,128)(2,1)S(1)} %get-tuple-element.70.p0.refs_0_), channel_id=1, source_target_pairs={{0,2},{1,3},{2,0},{3,1},{4,6},{5,7},{6,4},{7,5},{8,10},{9,11},{10,... | collective-permute-start | bytes 995336 | tf_op jit(solution)/shard_map/ppermute | solution.py:301
  11.7 18.8 %collective-permute-start.5 = (bf16[624,384]{1,0:T(8,128)(2,1)S(1)}, bf16[624,384]{1,0:T(8,128)(2,1)S(1)}, u32[]{:S(2)}, u32[]{:S(2)}) collective-permute-start(bf16[624,384]{1,0:T(8,128)(2,1)S(1)} %get-tuple-element.78.refs_4_.p0), channel_id=1, source_target_pairs={{0,2},{1,3},{2,0},{3,1},{4,6},{5,7},{6,4},{7,5},{8,10},{9,11},{10,... | collective-permute-start | bytes 1437704 | tf_op jit(solution)/shard_map/ppermute | solution.py:301
  27.1 1.6 %collective-permute-start.4 = (bf16[432,384]{1,0:T(8,128)(2,1)S(1)}, bf16[432,384]{1,0:T(8,128)(2,1)S(1)}, u32[]{:S(2)}, u32[]{:S(2)}) collective-permute-start(bf16[432,384]{1,0:T(8,128)(2,1)S(1)} %collective-permute-done.1.p2.refs_2_), channel_id=1, source_target_pairs={{0,1},{1,0},{2,3},{3,2},{4,5},{5,4},{6,7},{7,6},{8,9},{9,8},{10,11... | collective-permute-start | bytes 995336 | tf_op jit(solution)/shard_map/ppermute | solution.py:301
  30.5 1.8 %collective-permute-start.6 = (bf16[624,384]{1,0:T(8,128)(2,1)S(1)}, bf16[624,384]{1,0:T(8,128)(2,1)S(1)}, u32[]{:S(2)}, u32[]{:S(2)}) collective-permute-start(bf16[624,384]{1,0:T(8,128)(2,1)S(1)} %collective-permute-done.5.refs_6_.p2), channel_id=1, source_target_pairs={{0,1},{1,0},{2,3},{3,2},{4,5},{5,4},{6,7},{7,6},{8,9},{9,8},{10,11... | collective-permute-start | bytes 1437704 | tf_op jit(solution)/shard_map/ppermute | solution.py:301
  30.6 22.9 %collective-permute-start.8 = (bf16[432,512]{1,0:T(8,128)(2,1)S(1)}, bf16[432,512]{1,0:T(8,128)(2,1)S(1)}, u32[]{:S(2)}, u32[]{:S(2)}) collective-permute-start(bf16[432,512]{1,0:T(8,128)(2,1)S(1)} %shard_map.80), channel_id=1, source_target_pairs={{0,16},{4,20},{8,24},{12,28},{16,0},{20,4},{24,8},{28,12},{1,17},{... | collective-permute-start | bytes 1327112 | tf_op jit(solution)/shard_map/ppermute | solution.py:301
  35.3 12.0 %collective-permute-start.7 = (bf16[384,512]{1,0:T(8,128)(2,1)S(1)}, bf16[384,512]{1,0:T(8,128)(2,1)S(1)}, u32[]{:S(2)}, u32[]{:S(2)}) collective-permute-start(bf16[384,512]{1,0:T(8,128)(2,1)S(1)} %get-tuple-element.90), channel_id=1, source_target_pairs={{0,4},{4,0},{8,12},{12,8},{16,20},{20,16},{24,28},{28,24},{1,5},{5... | collective-permute-start | bytes 1179656 | tf_op jit(solution)/shard_map/ppermute | solution.py:301
  41.5 16.4 %collective-permute-start.9 = (bf16[384,512]{1,0:T(8,128)(2,1)S(1)}, bf16[384,512]{1,0:T(8,128)(2,1)S(1)}, u32[]{:S(2)}, u32[]{:S(2)}) collective-permute-start(bf16[384,512]{1,0:T(8,128)(2,1)S(1)} %get-tuple-element.99), channel_id=1, source_target_pairs={{0,4},{4,0},{8,12},{12,8},{16,20},{20,16},{24,28},{28,24},{1,5},{5... | collective-permute-start | bytes 1179656 | tf_op jit(solution)/shard_map/ppermute | solution.py:301
  56.3 22.6 %collective-permute-start.15 = (bf16[768,512]{1,0:T(8,128)(2,1)S(1)}, bf16[768,512]{1,0:T(8,128)(2,1)S(1)}, u32[]{:S(2)}, u32[]{:S(2)}) collective-permute-start(bf16[768,512]{1,0:T(8,128)(2,1)S(1)} %get-tuple-element.96), channel_id=1, source_target_pairs={{0,4},{4,0},{8,12},{12,8},{16,20},{20,16},{24,28},{28,24},{1,5},{5... | collective-permute-start | bytes 2359304 | tf_op jit(solution)/shard_map/ppermute | solution.py:301
  57.9 21.0 %collective-permute-start.13 = (bf16[432,512]{1,0:T(8,128)(2,1)S(1)}, bf16[432,512]{1,0:T(8,128)(2,1)S(1)}, u32[]{:S(2)}, u32[]{:S(2)}) collective-permute-start(bf16[432,512]{1,0:T(8,128)(2,1)S(1)} %get-tuple-element.107), channel_id=1, source_target_pairs={{0,16},{4,20},{8,24},{12,28},{16,0},{20,4},{24,8},{28,12},{1,17},{... | collective-permute-start | bytes 1327112 | tf_op jit(solution)/shard_map/ppermute | solution.py:301
  58.9 20.1 %collective-permute-start.14 = (bf16[384,512]{1,0:T(8,128)(2,1)S(1)}, bf16[384,512]{1,0:T(8,128)(2,1)S(1)}, u32[]{:S(2)}, u32[]{:S(2)}) collective-permute-start(bf16[384,512]{1,0:T(8,128)(2,1)S(1)} %get-tuple-element.100), channel_id=1, source_target_pairs={{0,8},{4,12},{8,0},{12,4},{16,24},{20,28},{24,16},{28,20},{1,9},{5... | collective-permute-start | bytes 1179656 | tf_op jit(solution)/shard_map/ppermute | solution.py:301
  60.7 5.0 %collective-permute-start.10 = (bf16[96,384]{1,0:T(8,128)(2,1)S(1)}, bf16[96,384]{1,0:T(8,128)(2,1)S(1)}, u32[]{:S(2)}, u32[]{:S(2)}) collective-permute-start(bf16[96,384]{1,0:T(8,128)(2,1)S(1)} %slice.4), channel_id=1, source_target_pairs={{0,2},{1,3},{2,0},{3,1},{4,6},{5,7},{6,4},{7,5},{8,10},{9,11},{10,... | collective-permute-start | bytes 221192 | tf_op jit(solution)/shard_map/ppermute | solution.py:301
  62.3 3.4 %collective-permute-start.11 = (bf16[96,384]{1,0:T(8,128)(2,1)S(1)}, bf16[96,384]{1,0:T(8,128)(2,1)S(1)}, u32[]{:S(2)}, u32[]{:S(2)}) collective-permute-start(bf16[96,384]{1,0:T(8,128)(2,1)S(1)} %slice.4), channel_id=1, source_target_pairs={{0,1},{1,0},{2,3},{3,2},{4,5},{5,4},{6,7},{7,6},{8,9},{9,8},{10,11... | collective-permute-start | bytes 221192 | tf_op jit(solution)/shard_map/ppermute | solution.py:301
  65.7 1.5 %collective-permute-start.12 = (bf16[96,384]{1,0:T(8,128)(2,1)S(1)}, bf16[96,384]{1,0:T(8,128)(2,1)S(1)}, u32[]{:S(2)}, u32[]{:S(2)}) collective-permute-start(bf16[96,384]{1,0:T(8,128)(2,1)S(1)} %collective-permute-done.10.p2), channel_id=1, source_target_pairs={{0,1},{1,0},{2,3},{3,2},{4,5},{5,4},{6,7},{7,6},{8,9},{9,8},{10,11... | collective-permute-start | bytes 221192 | tf_op jit(solution)/shard_map/ppermute | solution.py:301
  70.1 20.7 %collective-permute-start.16 = (bf16[384,512]{1,0:T(8,128)(2,1)S(1)}, bf16[384,512]{1,0:T(8,128)(2,1)S(1)}, u32[]{:S(2)}, u32[]{:S(2)}) collective-permute-start(bf16[384,512]{1,0:T(8,128)(2,1)S(1)} %get-tuple-element.121), channel_id=1, source_target_pairs={{0,4},{4,0},{8,12},{12,8},{16,20},{20,16},{24,28},{28,24},{1,5},{5... | collective-permute-start | bytes 1179656 | tf_op jit(solution)/shard_map/ppermute | solution.py:301
  70.7 21.6 %collective-permute-start.17 = (bf16[384,512]{1,0:T(8,128)(2,1)S(1)}, bf16[384,512]{1,0:T(8,128)(2,1)S(1)}, u32[]{:S(2)}, u32[]{:S(2)}) collective-permute-start(bf16[384,512]{1,0:T(8,128)(2,1)S(1)} %get-tuple-element.122), channel_id=1, source_target_pairs={{0,4},{4,0},{8,12},{12,8},{16,20},{20,16},{24,28},{28,24},{1,5},{5... | collective-permute-start | bytes 1179656 | tf_op jit(solution)/shard_map/ppermute | solution.py:301
  80.1 13.8 %collective-permute-start.18 = (bf16[384,512]{1,0:T(8,128)(2,1)S(1)}, bf16[384,512]{1,0:T(8,128)(2,1)S(1)}, u32[]{:S(2)}, u32[]{:S(2)}) collective-permute-start(bf16[384,512]{1,0:T(8,128)(2,1)S(1)} %get-tuple-element.110), channel_id=1, source_target_pairs={{0,8},{4,12},{8,0},{12,4},{16,24},{20,28},{24,16},{28,20},{1,9},{5... | collective-permute-start | bytes 1179656 | tf_op jit(solution)/shard_map/ppermute | solution.py:301
  87.8 22.4 %collective-permute-start.19 = (bf16[192,512]{1,0:T(8,128)(2,1)S(1)}, bf16[192,512]{1,0:T(8,128)(2,1)S(1)}, u32[]{:S(2)}, u32[]{:S(2)}) collective-permute-start(bf16[192,512]{1,0:T(8,128)(2,1)S(1)} %get-tuple-element.118), channel_id=1, source_target_pairs={{0,16},{4,20},{8,24},{12,28},{16,0},{20,4},{24,8},{28,12},{1,17},{... | collective-permute-start | bytes 589832 | tf_op jit(solution)/shard_map/ppermute | solution.py:301
  90.5 33.5 %collective-permute-start.20 = (bf16[432,512]{1,0:T(8,128)(2,1)S(1)}, bf16[432,512]{1,0:T(8,128)(2,1)S(1)}, u32[]{:S(2)}, u32[]{:S(2)}) collective-permute-start(bf16[432,512]{1,0:T(8,128)(2,1)S(1)} %get-tuple-element.128), channel_id=1, source_target_pairs={{0,16},{4,20},{8,24},{12,28},{16,0},{20,4},{24,8},{28,12},{1,17},{... | collective-permute-start | bytes 1327112 | tf_op jit(solution)/shard_map/ppermute | solution.py:301
  93.3 30.7 %collective-permute-start.21 = (bf16[384,512]{1,0:T(8,128)(2,1)S(1)}, bf16[384,512]{1,0:T(8,128)(2,1)S(1)}, u32[]{:S(2)}, u32[]{:S(2)}) collective-permute-start(bf16[384,512]{1,0:T(8,128)(2,1)S(1)} %get-tuple-element.123), channel_id=1, source_target_pairs={{0,8},{4,12},{8,0},{12,4},{16,24},{20,28},{24,16},{28,20},{1,9},{5... | collective-permute-start | bytes 1179656 | tf_op jit(solution)/shard_map/ppermute | solution.py:301
  94.7 37.7 %collective-permute-start.22 = (bf16[192,512]{1,0:T(8,128)(2,1)S(1)}, bf16[192,512]{1,0:T(8,128)(2,1)S(1)}, u32[]{:S(2)}, u32[]{:S(2)}) collective-permute-start(bf16[192,512]{1,0:T(8,128)(2,1)S(1)} %get-tuple-element.126), channel_id=1, source_target_pairs={{0,16},{4,20},{8,24},{12,28},{16,0},{20,4},{24,8},{28,12},{1,17},{... | collective-permute-start | bytes 589832 | tf_op jit(solution)/shard_map/ppermute | solution.py:301
  124.8 10.7 %collective-permute-start.23 = (bf16[192,512]{1,0:T(8,128)(2,1)S(1)}, bf16[192,512]{1,0:T(8,128)(2,1)S(1)}, u32[]{:S(2)}, u32[]{:S(2)}) collective-permute-start(bf16[192,512]{1,0:T(8,128)(2,1)S(1)} %get-tuple-element.131), channel_id=1, source_target_pairs={{0,16},{4,20},{8,24},{12,28},{16,0},{20,4},{24,8},{28,12},{1,17},{... | collective-permute-start | bytes 589832 | tf_op jit(solution)/shard_map/ppermute | solution.py:301
  (2 other events, 43.9 us)

commit v19 on v18

--- a/solution.py
+++ b/solution.py
@@ -11,7 +11,7 @@
 SEND = 528
 KEEP = 528
 TILE = 16
-EARLY = 96
+EARLY = 48
 LATE = SEND - EARLY
 SLOTS = 4
 BAL = 720
@@ -414,15 +414,15 @@
     out_nb, mine_b = near_step(after(meta, keep_c01, arrived_b, got_na), (keep_b,), (got_b,))
     got_nb = swapped(out_nb, "dp", 2)
     arrived_c = swapped(after(moving_c, out_nb), "dp", n // 2)
-    (kept_grad,) = grads(after(meta, out_nb), rests, EARLY, EARLY, KEEP, 0, (der_ra, der_rb, der_rc), (ff,))
+    out_fa, own_a = far_step(after(meta, out_nb), mine_a, got_na)
+    got_fa = swapped(out_fa, "dp", 4)
+    (kept_grad,) = grads(after(meta, out_fa), rests, EARLY, EARLY, KEEP, 0, (der_ra, der_rb, der_rc), (ff,))
     early_grad = kernel_call(
         functools.partial(early_kernel, 256), shape(EARLY, ff), [IN_VMEM] * 5, IN_VMEM,
         [vmem((EARLY, features), BF), vmem((EARLY, 256), F32)],
     )(after(meta, kept_grad), arrived_early, early_c, early_y, early_yc, down_weight)
 
-    out_fa, own_a = far_step(after(meta, early_grad), mine_a, got_na)
-    got_fa = swapped(out_fa, "dp", 4)
-    out_nc, mine_c = near_step(after(meta, out_fa), (keep_c01, keep_c23), gots_c)
+    out_nc, mine_c = near_step(after(meta, early_grad), (keep_c01, keep_c23), gots_c)
     got_nc = swapped(out_nc, "dp", 2)
     out_fb, own_b = far_step(after(meta, out_nc), mine_b, got_nb)
     got_fb = swapped(out_fb, "dp", 4)

time: 137 us -> 133 us (0.971)
  waiting for transfers between devices: 61.8 us -> 52.8 us
  starting transfers between devices: 21.7 us -> 26.9 us
    ppermute x24, waiting for transfers between devices: 61.8 us -> 52.8 us  [swapped(): return lax.ppermute(block, axis, [(i, i ^ distance) for i in range(n)])]
    ppermute x24, starting transfers between devices: 21.7 us -> 26.9 us  [swapped(): return lax.ppermute(block, axis, [(i, i ^ distance) for i in range(n)])]
  transfers between devices with their start and end apart: 24 -> 24, of which waited for: 14 -> 11; matrix products, arithmetic and copies ran while one was open for 0% -> 0% of each run, Pallas kernels for 34% -> 34%
where the time goes in v19:
time: 133 us
  waiting for transfers between devices  52.8 us (40%)
  Pallas kernels  50 us (38%)
  starting transfers between devices  26.9 us (20%)
  other arithmetic  1.98 us (1%)
    ppermute x24, waiting for transfers between devices, swapped(): return lax.ppermute(block, axis, [(i, i ^ distance) for i in range(n)])  52.8 us
    ppermute x24, starting transfers between devices, swapped(): return lax.ppermute(block, axis, [(i, i ^ distance) for i in range(n)])  26.9 us
    pallas_call x5, Pallas kernels, gelu(): kernel_call(functools.partial(gelu_kernel, base, block), [shape(rows, col...  17.7 us
    pallas_call x3, Pallas kernels, grads(): kernel_call(functools.partial(grad_kernel, first_row, first_slope, base,...  7.62 us
    pallas_call x2, Pallas kernels, weight_again(): kernel_call(functools.partial(again_kernel, base), [shape(rows, part)] *...  5.7 us
    pallas_call x1, Pallas kernels, shards(): kernel_call(first_kernel, [shape(LATE, width), shape(others, width), shap...  4.44 us
    pallas_call x1, Pallas kernels, shards(): kernel_call(functools.partial(place_kernel, (part,) * 3), shape(BAL, ff),...  3.29 us
    pallas_call x1, Pallas kernels, weight_first(): kernel_call(functools.partial(weight_kernel, 4), [shape(width, part)] * 2...  2.93 us
  transfers between devices with their start and end apart: 24, of which 11 were waited for; matrix products, arithmetic and copies ran while one was open for 0% of the time, Pallas kernels for 34%

profile of v19, /device:TPU:0, one launch (start us, length us, event | category | flops | bytes accessed | tf_op | source)
XLA Modules:
  0.0 132.6 jit_solution(2770568002829116471)
XLA Ops:
  1.4 4.4 %shard_map.77 = (bf16[480,384]{1,0:T(8,128)(2,1)S(1)}, bf16[576,384]{1,0:T(8,128)(2,1)S(1)}, bf16[48,1920]{1,0:T(8,128)(2,1)S(1)}, bf16[480,1032]{1,0:T(8,128)(2...) custom-call(s32[9,8]{1,0:T(8,128)S(1)} %pad_add_fusion.meta, bf16[1032,384]{1,0:T(8,128)(2,1)} %cot_hbm.1, ...), custom_call_target="tpu_custom_call" | custom-call | flops 1 | bytes 1 | tf_op jit(solution)/shard_map/pallas_call | solution.py:370
  6.4 2.9 %collective-permute-start.1 = (bf16[480,384]{1,0:T(8,128)(2,1)S(1)}, bf16[480,384]{1,0:T(8,128)(2,1)S(1)}, u32[]{:S(2)}, u32[]{:S(2)}) collective-permute-start(bf16[480,384]{1,0:T(8,128)(2,1)S(1)} %get-tuple-element.70.p0.refs_0_), channel_id=1, source_target_pairs={{0,2},{1,3},{2,0},{3,1},{4,6},{5,7},{6,4},{7,5},{8,10},{9,11},{10,... | collective-permute-start | bytes 1105928 | tf_op jit(solution)/shard_map/ppermute | solution.py:301
  9.4 2.6 %collective-permute-start = (bf16[48,1920]{1,0:T(8,128)(2,1)S(1)}, bf16[48,1920]{1,0:T(8,128)(2,1)S(1)}, u32[]{:S(2)}, u32[]{:S(2)}) collective-permute-start(bf16[48,1920]{1,0:T(8,128)(2,1)S(1)} %get-tuple-element.69), channel_id=1, source_target_pairs={{0,16},{4,20},{8,24},{12,28},{16,0},{20,4},{24,8},{28,12},{1,17},{... | collective-permute-start | bytes 552968 | tf_op jit(solution)/shard_map/ppermute | solution.py:301
  12.4 3.0 %shard_map.78 = (bf16[480,512]{1,0:T(8,128)(2,1)S(1)}, f32[480,512]{1,0:T(8,128)S(1)}) custom-call(s32[9,8]{1,0:T(8,128)S(1)} %pad_add_fusion.meta, bf16[480,1032]{1,0:T(8,128)(2,1)S(1)} %get-tuple-element.72.pick, bf16[1032,1536]{1,0:T(8,128)(2,1)S(1)} %get-tuple-element.73.pre), custom_call_target="tpu_custom_call" | custom-call | flops 1 | bytes 1 | tf_op jit(solution)/shard_map/pallas_call | solution.py:329
  15.5 3.2 %shard_map.79 = (bf16[576,512]{1,0:T(8,128)(2,1)S(1)}, f32[576,512]{1,0:T(8,128)S(1)}) custom-call(s32[9,8]{1,0:T(8,128)S(1)} %pad_add_fusion.meta, bf16[576,1032]{1,0:T(8,128)(2,1)S(1)} %get-tuple-element.76.pick, bf16[1032,1536]{1,0:T(8,128)(2,1)S(1)} %get-tuple-element.73.pre), custom_call_target="tpu_custom_call" | custom-call | flops 1 | bytes 1 | tf_op jit(solution)/shard_map/pallas_call | solution.py:329
  24.0 3.6 %collective-permute-done.5.refs_6_.p2 = bf16[576,384]{1,0:T(8,128)(2,1)S(1)} collective-permute-done((bf16[576,384]{1,0:T(8,128)(2,1)S(1)}, bf16[576,384]{1,0:T(8,128)(2,1)S(1)}, u32[]{:S(2)}, u32[]{:S(2)}) %collective-permute-start.5) | collective-permute-done | bytes 442400 | tf_op jit(solution)/shard_map/ppermute | solution.py:301
  27.7 2.8 %collective-permute-start.8 = (bf16[480,512]{1,0:T(8,128)(2,1)S(1)}, bf16[480,512]{1,0:T(8,128)(2,1)S(1)}, u32[]{:S(2)}, u32[]{:S(2)}) collective-permute-start(bf16[480,512]{1,0:T(8,128)(2,1)S(1)} %shard_map.80), channel_id=1, source_target_pairs={{0,16},{4,20},{8,24},{12,28},{16,0},{20,4},{24,8},{28,12},{1,17},{... | collective-permute-start | bytes 1474568 | tf_op jit(solution)/shard_map/ppermute | solution.py:301
  30.5 2.9 %shard_map.81 = (bf16[384,512]{1,0:T(8,128)(2,1)S(1)}, bf16[384,512]{1,0:T(8,128)(2,1)S(1)}, f32[384,512]{1,0:T(8,128)S(1)}, f32[384,512]{1,0:T(8,128)S(1)}, bf1...) custom-call(s32[9,8]{1,0:T(8,128)S(1)} %pad_add_fusion.meta, ...), custom_call_target="tpu_custom_call" | custom-call | flops 1 | bytes 1 | tf_op jit(solution)/shard_map/pallas_call | solution.py:336
  35.0 5.0 %shard_map.82 = (bf16[480,1024]{1,0:T(8,128)(2,1)S(1)}, f32[480,1024]{1,0:T(8,128)S(1)}) custom-call(s32[9,8]{1,0:T(8,128)S(1)} %pad_add_fusion.meta, bf16[480,1032]{1,0:T(8,128)(2,1)S(1)} %get-tuple-element.72.pick, bf16[1032,1536]{1,0:T(8,128)(2,1)S(1)} %get-tuple-element.73.pre), custom_call_target="tpu_custom_call" | custom-call | flops 1 | bytes 1 | tf_op jit(solution)/shard_map/pallas_call | solution.py:329
  40.6 2.5 %shard_map.83 = (bf16[480,512]{1,0:T(8,128)(2,1)S(1)}, bf16[480,512]{1,0:T(8,128)(2,1)S(1)}) custom-call(s32[9,8]{1,0:T(8,128)S(1)} %pad_add_fusion.meta, bf16[480,384]{1,0:T(8,128)(2,1)S(1)} %get-tuple-element.70.p0.refs_0_, bf16[480,384]{1,0:T(8,128)(2,1)S(1)} %collective-permute-done.2.p1.refs_1_, bf16[480,384]{1,0:T(8,128)(2,1)S(1)} %collective-permute-done.1.p2.refs_2_, ...), custom_call_target="tpu_custom_call" | custom-call | flops 1 | bytes 1 | tf_op jit(solution)/shard_map/pallas_call | solution.py:352
  45.4 3.2 %shard_map.84 = (bf16[576,512]{1,0:T(8,128)(2,1)S(1)}, f32[576,512]{1,0:T(8,128)S(1)}) custom-call(s32[9,8]{1,0:T(8,128)S(1)} %pad_add_fusion.meta, bf16[576,1032]{1,0:T(8,128)(2,1)S(1)} %get-tuple-element.76.pick, bf16[1032,1536]{1,0:T(8,128)(2,1)S(1)} %get-tuple-element.73.pre), custom_call_target="tpu_custom_call" | custom-call | flops 1 | bytes 1 | tf_op jit(solution)/shard_map/pallas_call | solution.py:329
  48.6 4.2 %collective-permute-done.8.rest_0_ = bf16[480,512]{1,0:T(8,128)(2,1)S(1)} collective-permute-done((bf16[480,512]{1,0:T(8,128)(2,1)S(1)}, bf16[480,512]{1,0:T(8,128)(2,1)S(1)}, u32[]{:S(2)}, u32[]{:S(2)}) %collective-permute-start.8) | collective-permute-done | bytes 491552 | tf_op jit(solution)/shard_map/ppermute | solution.py:301
  52.9 2.9 %shard_map.85 = (bf16[768,512]{1,0:T(8,128)(2,1)S(1)}, f32[768,512]{1,0:T(8,128)S(1)}) custom-call(s32[9,8]{1,0:T(8,128)S(1)} %pad_add_fusion.meta, bf16[1536,480]{1,0:T(8,128)(2,1)S(1)} %get-tuple-element.94.lhs_moved, bf16[1536,576]{1,0:T(8,128)(2,1)S(1)} %get-tuple-element.95.lhs_kept, bf16[480,1024]{1,0:T(8,128)(2,1)S(1)} %get-tuple-element.86.act_moved, ...), custom_call_target="tpu_custom_call" | custom-call | flops 1 | bytes 1 | tf_op jit(solution)/shard_map/pallas_call | solution.py:345
  58.3 4.1 %collective-permute-start.14 = (bf16[384,512]{1,0:T(8,128)(2,1)S(1)}, bf16[384,512]{1,0:T(8,128)(2,1)S(1)}, u32[]{:S(2)}, u32[]{:S(2)}) collective-permute-start(bf16[384,512]{1,0:T(8,128)(2,1)S(1)} %get-tuple-element.100), channel_id=1, source_target_pairs={{0,8},{4,12},{8,0},{12,4},{16,24},{20,28},{24,16},{28,20},{1,9},{5... | collective-permute-start | bytes 1179656 | tf_op jit(solution)/shard_map/ppermute | solution.py:301
  64.0 3.2 %shard_map.87 = (bf16[576,512]{1,0:T(8,128)(2,1)S(1)}, f32[576,512]{1,0:T(8,128)S(1)}) custom-call(s32[9,8]{1,0:T(8,128)S(1)} %pad_add_fusion.meta, bf16[576,1032]{1,0:T(8,128)(2,1)S(1)} %get-tuple-element.76.pick, bf16[1032,1536]{1,0:T(8,128)(2,1)S(1)} %get-tuple-element.73.pre), custom_call_target="tpu_custom_call" | custom-call | flops 1 | bytes 1 | tf_op jit(solution)/shard_map/pallas_call | solution.py:329
  68.6 2.9 %shard_map.88 = (bf16[384,512]{1,0:T(8,128)(2,1)S(1)}, bf16[384,512]{1,0:T(8,128)(2,1)S(1)}, f32[384,512]{1,0:T(8,128)S(1)}, f32[384,512]{1,0:T(8,128)S(1)}) custom-call(s32[9,8]{1,0:T(8,128)S(1)} %pad_add_fusion.meta, bf16[1536,480]{1,0:T(8,128)(2,1)S(1)} %get-tuple-element.94.lhs_moved, bf16[1536,576]{1,0:T(8,128)(2,1)S(1)} %get-tuple-element.95.lhs_kept, ...), custom_call_target="tpu_custom_call" | custom-call | flops 1 | bytes 1 | tf_op jit(solution)/shard_map/pallas_call | solution.py:345
  73.6 2.6 %collective-permute-done.14.got = bf16[384,512]{1,0:T(8,128)(2,1)S(1)} collective-permute-done((bf16[384,512]{1,0:T(8,128)(2,1)S(1)}, bf16[384,512]{1,0:T(8,128)(2,1)S(1)}, u32[]{:S(2)}, u32[]{:S(2)}) %collective-permute-start.14) | collective-permute-done | bytes 393248 | tf_op jit(solution)/shard_map/ppermute | solution.py:301
  76.2 5.2 %collective-permute-done.13.rest_1_ = bf16[480,512]{1,0:T(8,128)(2,1)S(1)} collective-permute-done((bf16[480,512]{1,0:T(8,128)(2,1)S(1)}, bf16[480,512]{1,0:T(8,128)(2,1)S(1)}, u32[]{:S(2)}, u32[]{:S(2)}) %collective-permute-start.13) | collective-permute-done | bytes 491552 | tf_op jit(solution)/shard_map/ppermute | solution.py:301
  86.5 3.5 %shard_map.91.kept = bf16[528,1536]{1,0:T(8,128)(2,1)S(1)} custom-call(s32[9,8]{1,0:T(8,128)S(1)} %pad_add_fusion.meta, bf16[576,384]{1,0:T(8,128)(2,1)S(1)} %get-tuple-element.78.refs_4_.p0, bf16[576,384]{1,0:T(8,128)(2,1)S(1)} %collective-permute-done.3.refs_5_.p1, bf16[576,384]{1,0:T(8,128)(2,1)S(1)} %collective-permute-done.5.refs_6_.p2, ...), custom_call_target="tpu_custom_call" | custom-call | flops 1 | bytes 1 | tf_op jit(solution)/shard_map/pallas_call | solution.py:352
  89.9 2.9 %shard_map.92.early = bf16[48,1536]{1,0:T(8,128)(2,1)S(1)} custom-call(s32[9,8]{1,0:T(8,128)S(1)} %pad_add_fusion.meta, bf16[48,1920]{1,0:T(8,128)(2,1)S(1)} %collective-permute-done.own, bf16[48,384]{1,0:T(8,128)(2,1)S(1)} %collective-permute-done.11.p1, bf16[48,384]{1,0:T(8,128)(2,1)S(1)} %collective-permute-done.10.p2, ...), custom_call_target="tpu_custom_call" | custom-call | flops 1 | bytes 1 | tf_op jit(solution)/shard_map/pallas_call | solution.py:420
  95.8 5.7 %collective-permute-done.18.got = bf16[384,512]{1,0:T(8,128)(2,1)S(1)} collective-permute-done((bf16[384,512]{1,0:T(8,128)(2,1)S(1)}, bf16[384,512]{1,0:T(8,128)(2,1)S(1)}, u32[]{:S(2)}, u32[]{:S(2)}) %collective-permute-start.18) | collective-permute-done | bytes 393248 | tf_op jit(solution)/shard_map/ppermute | solution.py:301
  102.4 20.4 %collective-permute-done.19 = bf16[192,512]{1,0:T(8,128)(2,1)S(1)} collective-permute-done((bf16[192,512]{1,0:T(8,128)(2,1)S(1)}, bf16[192,512]{1,0:T(8,128)(2,1)S(1)}, u32[]{:S(2)}, u32[]{:S(2)}) %collective-permute-start.19) | collective-permute-done | bytes 196640 | tf_op jit(solution)/shard_map/ppermute | solution.py:301
  123.8 3.3 %shard_map.96 = bf16[720,1536]{1,0:T(8,128)(2,1)} custom-call(s32[9,8]{1,0:T(8,128)S(1)} %pad_add_fusion.meta, bf16[528,1536]{1,0:T(8,128)(2,1)S(1)} %shard_map.91.kept, bf16[48,1536]{1,0:T(8,128)(2,1)S(1)} %shard_map.92.early, bf16[480,512]{1,0:T(8,128)(2,1)S(1)} %collective-permute-done.8.rest_0_, bf16[480,512]{1,0:T(8,128)(2,1)S(1)} %collective-permute-done.13.rest_1_, ...), custom_call_target="tpu_custom_call" | custom-call | flops 1 | bytes 1 | tf_op jit(solution)/shard_map/pallas_call | solution.py:434
  127.2 4.2 %collective-permute-done.23 = bf16[192,512]{1,0:T(8,128)(2,1)S(1)} collective-permute-done((bf16[192,512]{1,0:T(8,128)(2,1)S(1)}, bf16[192,512]{1,0:T(8,128)(2,1)S(1)}, u32[]{:S(2)}, u32[]{:S(2)}) %collective-permute-start.23) | collective-permute-done | bytes 196640 | tf_op jit(solution)/shard_map/ppermute | solution.py:301
  (56 shorter events, 30.3 us)
Async XLA Ops:
  5.8 14.7 %collective-permute-start.3 = (bf16[576,384]{1,0:T(8,128)(2,1)S(1)}, bf16[576,384]{1,0:T(8,128)(2,1)S(1)}, u32[]{:S(2)}, u32[]{:S(2)}) collective-permute-start(bf16[576,384]{1,0:T(8,128)(2,1)S(1)} %get-tuple-element.78.refs_4_.p0), channel_id=1, source_target_pairs={{0,1},{1,0},{2,3},{3,2},{4,5},{5,4},{6,7},{7,6},{8,9},{9,8},{10,11... | collective-permute-start | bytes 1327112 | tf_op jit(solution)/shard_map/ppermute | solution.py:301
  6.3 14.2 %collective-permute-start.2 = (bf16[480,384]{1,0:T(8,128)(2,1)S(1)}, bf16[480,384]{1,0:T(8,128)(2,1)S(1)}, u32[]{:S(2)}, u32[]{:S(2)}) collective-permute-start(bf16[480,384]{1,0:T(8,128)(2,1)S(1)} %get-tuple-element.70.p0.refs_0_), channel_id=1, source_target_pairs={{0,1},{1,0},{2,3},{3,2},{4,5},{5,4},{6,7},{7,6},{8,9},{9,8},{10,11... | collective-permute-start | bytes 1105928 | tf_op jit(solution)/shard_map/ppermute | solution.py:301
  6.4 14.1 %collective-permute-start.1 = (bf16[480,384]{1,0:T(8,128)(2,1)S(1)}, bf16[480,384]{1,0:T(8,128)(2,1)S(1)}, u32[]{:S(2)}, u32[]{:S(2)}) collective-permute-start(bf16[480,384]{1,0:T(8,128)(2,1)S(1)} %get-tuple-element.70.p0.refs_0_), channel_id=1, source_target_pairs={{0,2},{1,3},{2,0},{3,1},{4,6},{5,7},{6,4},{7,5},{8,10},{9,11},{10,... | collective-permute-start | bytes 1105928 | tf_op jit(solution)/shard_map/ppermute | solution.py:301
  9.4 11.2 %collective-permute-start = (bf16[48,1920]{1,0:T(8,128)(2,1)S(1)}, bf16[48,1920]{1,0:T(8,128)(2,1)S(1)}, u32[]{:S(2)}, u32[]{:S(2)}) collective-permute-start(bf16[48,1920]{1,0:T(8,128)(2,1)S(1)} %get-tuple-element.69), channel_id=1, source_target_pairs={{0,16},{4,20},{8,24},{12,28},{16,0},{20,4},{24,8},{28,12},{1,17},{... | collective-permute-start | bytes 552968 | tf_op jit(solution)/shard_map/ppermute | solution.py:301
  11.9 15.7 %collective-permute-start.5 = (bf16[576,384]{1,0:T(8,128)(2,1)S(1)}, bf16[576,384]{1,0:T(8,128)(2,1)S(1)}, u32[]{:S(2)}, u32[]{:S(2)}) collective-permute-start(bf16[576,384]{1,0:T(8,128)(2,1)S(1)} %get-tuple-element.78.refs_4_.p0), channel_id=1, source_target_pairs={{0,2},{1,3},{2,0},{3,1},{4,6},{5,7},{6,4},{7,5},{8,10},{9,11},{10,... | collective-permute-start | bytes 1327112 | tf_op jit(solution)/shard_map/ppermute | solution.py:301
  20.6 1.8 %collective-permute-start.4 = (bf16[480,384]{1,0:T(8,128)(2,1)S(1)}, bf16[480,384]{1,0:T(8,128)(2,1)S(1)}, u32[]{:S(2)}, u32[]{:S(2)}) collective-permute-start(bf16[480,384]{1,0:T(8,128)(2,1)S(1)} %collective-permute-done.1.p2.refs_2_), channel_id=1, source_target_pairs={{0,1},{1,0},{2,3},{3,2},{4,5},{5,4},{6,7},{7,6},{8,9},{9,8},{10,11... | collective-permute-start | bytes 1105928 | tf_op jit(solution)/shard_map/ppermute | solution.py:301
  27.7 2.8 %collective-permute-start.6 = (bf16[576,384]{1,0:T(8,128)(2,1)S(1)}, bf16[576,384]{1,0:T(8,128)(2,1)S(1)}, u32[]{:S(2)}, u32[]{:S(2)}) collective-permute-start(bf16[576,384]{1,0:T(8,128)(2,1)S(1)} %collective-permute-done.5.refs_6_.p2), channel_id=1, source_target_pairs={{0,1},{1,0},{2,3},{3,2},{4,5},{5,4},{6,7},{7,6},{8,9},{9,8},{10,11... | collective-permute-start | bytes 1327112 | tf_op jit(solution)/shard_map/ppermute | solution.py:301
  27.7 25.2 %collective-permute-start.8 = (bf16[480,512]{1,0:T(8,128)(2,1)S(1)}, bf16[480,512]{1,0:T(8,128)(2,1)S(1)}, u32[]{:S(2)}, u32[]{:S(2)}) collective-permute-start(bf16[480,512]{1,0:T(8,128)(2,1)S(1)} %shard_map.80), channel_id=1, source_target_pairs={{0,16},{4,20},{8,24},{12,28},{16,0},{20,4},{24,8},{28,12},{1,17},{... | collective-permute-start | bytes 1474568 | tf_op jit(solution)/shard_map/ppermute | solution.py:301
  33.4 12.0 %collective-permute-start.7 = (bf16[384,512]{1,0:T(8,128)(2,1)S(1)}, bf16[384,512]{1,0:T(8,128)(2,1)S(1)}, u32[]{:S(2)}, u32[]{:S(2)}) collective-permute-start(bf16[384,512]{1,0:T(8,128)(2,1)S(1)} %get-tuple-element.90), channel_id=1, source_target_pairs={{0,4},{4,0},{8,12},{12,8},{16,20},{20,16},{24,28},{28,24},{1,5},{5... | collective-permute-start | bytes 1179656 | tf_op jit(solution)/shard_map/ppermute | solution.py:301
  40.0 17.4 %collective-permute-start.9 = (bf16[384,512]{1,0:T(8,128)(2,1)S(1)}, bf16[384,512]{1,0:T(8,128)(2,1)S(1)}, u32[]{:S(2)}, u32[]{:S(2)}) collective-permute-start(bf16[384,512]{1,0:T(8,128)(2,1)S(1)} %get-tuple-element.99), channel_id=1, source_target_pairs={{0,4},{4,0},{8,12},{12,8},{16,20},{20,16},{24,28},{28,24},{1,5},{5... | collective-permute-start | bytes 1179656 | tf_op jit(solution)/shard_map/ppermute | solution.py:301
  55.8 25.6 %collective-permute-start.15 = (bf16[768,512]{1,0:T(8,128)(2,1)S(1)}, bf16[768,512]{1,0:T(8,128)(2,1)S(1)}, u32[]{:S(2)}, u32[]{:S(2)}) collective-permute-start(bf16[768,512]{1,0:T(8,128)(2,1)S(1)} %get-tuple-element.96), channel_id=1, source_target_pairs={{0,4},{4,0},{8,12},{12,8},{16,20},{20,16},{24,28},{28,24},{1,5},{5... | collective-permute-start | bytes 2359304 | tf_op jit(solution)/shard_map/ppermute | solution.py:301
  57.4 24.0 %collective-permute-start.13 = (bf16[480,512]{1,0:T(8,128)(2,1)S(1)}, bf16[480,512]{1,0:T(8,128)(2,1)S(1)}, u32[]{:S(2)}, u32[]{:S(2)}) collective-permute-start(bf16[480,512]{1,0:T(8,128)(2,1)S(1)} %get-tuple-element.107), channel_id=1, source_target_pairs={{0,16},{4,20},{8,24},{12,28},{16,0},{20,4},{24,8},{28,12},{1,17},{... | collective-permute-start | bytes 1474568 | tf_op jit(solution)/shard_map/ppermute | solution.py:301
  58.3 17.9 %collective-permute-start.14 = (bf16[384,512]{1,0:T(8,128)(2,1)S(1)}, bf16[384,512]{1,0:T(8,128)(2,1)S(1)}, u32[]{:S(2)}, u32[]{:S(2)}) collective-permute-start(bf16[384,512]{1,0:T(8,128)(2,1)S(1)} %get-tuple-element.100), channel_id=1, source_target_pairs={{0,8},{4,12},{8,0},{12,4},{16,24},{20,28},{24,16},{28,20},{1,9},{5... | collective-permute-start | bytes 1179656 | tf_op jit(solution)/shard_map/ppermute | solution.py:301
  62.4 4.7 %collective-permute-start.10 = (bf16[48,384]{1,0:T(8,128)(2,1)S(1)}, bf16[48,384]{1,0:T(8,128)(2,1)S(1)}, u32[]{:S(2)}, u32[]{:S(2)}) collective-permute-start(bf16[48,384]{1,0:T(8,128)(2,1)S(1)} %slice.4), channel_id=1, source_target_pairs={{0,2},{1,3},{2,0},{3,1},{4,6},{5,7},{6,4},{7,5},{8,10},{9,11},{10,... | collective-permute-start | bytes 110600 | tf_op jit(solution)/shard_map/ppermute | solution.py:301
  63.9 3.2 %collective-permute-start.11 = (bf16[48,384]{1,0:T(8,128)(2,1)S(1)}, bf16[48,384]{1,0:T(8,128)(2,1)S(1)}, u32[]{:S(2)}, u32[]{:S(2)}) collective-permute-start(bf16[48,384]{1,0:T(8,128)(2,1)S(1)} %slice.4), channel_id=1, source_target_pairs={{0,1},{1,0},{2,3},{3,2},{4,5},{5,4},{6,7},{7,6},{8,9},{9,8},{10,11... | collective-permute-start | bytes 110600 | tf_op jit(solution)/shard_map/ppermute | solution.py:301
  67.2 1.4 %collective-permute-start.12 = (bf16[48,384]{1,0:T(8,128)(2,1)S(1)}, bf16[48,384]{1,0:T(8,128)(2,1)S(1)}, u32[]{:S(2)}, u32[]{:S(2)}) collective-permute-start(bf16[48,384]{1,0:T(8,128)(2,1)S(1)} %collective-permute-done.10.p2), channel_id=1, source_target_pairs={{0,1},{1,0},{2,3},{3,2},{4,5},{5,4},{6,7},{7,6},{8,9},{9,8},{10,11... | collective-permute-start | bytes 110600 | tf_op jit(solution)/shard_map/ppermute | solution.py:301
  71.5 21.4 %collective-permute-start.16 = (bf16[384,512]{1,0:T(8,128)(2,1)S(1)}, bf16[384,512]{1,0:T(8,128)(2,1)S(1)}, u32[]{:S(2)}, u32[]{:S(2)}) collective-permute-start(bf16[384,512]{1,0:T(8,128)(2,1)S(1)} %get-tuple-element.121), channel_id=1, source_target_pairs={{0,4},{4,0},{8,12},{12,8},{16,20},{20,16},{24,28},{28,24},{1,5},{5... | collective-permute-start | bytes 1179656 | tf_op jit(solution)/shard_map/ppermute | solution.py:301
  72.1 20.8 %collective-permute-start.17 = (bf16[384,512]{1,0:T(8,128)(2,1)S(1)}, bf16[384,512]{1,0:T(8,128)(2,1)S(1)}, u32[]{:S(2)}, u32[]{:S(2)}) collective-permute-start(bf16[384,512]{1,0:T(8,128)(2,1)S(1)} %get-tuple-element.122), channel_id=1, source_target_pairs={{0,4},{4,0},{8,12},{12,8},{16,20},{20,16},{24,28},{28,24},{1,5},{5... | collective-permute-start | bytes 1179656 | tf_op jit(solution)/shard_map/ppermute | solution.py:301
  82.3 19.2 %collective-permute-start.18 = (bf16[384,512]{1,0:T(8,128)(2,1)S(1)}, bf16[384,512]{1,0:T(8,128)(2,1)S(1)}, u32[]{:S(2)}, u32[]{:S(2)}) collective-permute-start(bf16[384,512]{1,0:T(8,128)(2,1)S(1)} %get-tuple-element.110), channel_id=1, source_target_pairs={{0,8},{4,12},{8,0},{12,4},{16,24},{20,28},{24,16},{28,20},{1,9},{5... | collective-permute-start | bytes 1179656 | tf_op jit(solution)/shard_map/ppermute | solution.py:301
  82.4 40.5 %collective-permute-start.20 = (bf16[480,512]{1,0:T(8,128)(2,1)S(1)}, bf16[480,512]{1,0:T(8,128)(2,1)S(1)}, u32[]{:S(2)}, u32[]{:S(2)}) collective-permute-start(bf16[480,512]{1,0:T(8,128)(2,1)S(1)} %get-tuple-element.128), channel_id=1, source_target_pairs={{0,16},{4,20},{8,24},{12,28},{16,0},{20,4},{24,8},{28,12},{1,17},{... | collective-permute-start | bytes 1474568 | tf_op jit(solution)/shard_map/ppermute | solution.py:301
  85.8 37.0 %collective-permute-start.19 = (bf16[192,512]{1,0:T(8,128)(2,1)S(1)}, bf16[192,512]{1,0:T(8,128)(2,1)S(1)}, u32[]{:S(2)}, u32[]{:S(2)}) collective-permute-start(bf16[192,512]{1,0:T(8,128)(2,1)S(1)} %get-tuple-element.113), channel_id=1, source_target_pairs={{0,16},{4,20},{8,24},{12,28},{16,0},{20,4},{24,8},{28,12},{1,17},{... | collective-permute-start | bytes 589832 | tf_op jit(solution)/shard_map/ppermute | solution.py:301
  93.8 29.1 %collective-permute-start.21 = (bf16[384,512]{1,0:T(8,128)(2,1)S(1)}, bf16[384,512]{1,0:T(8,128)(2,1)S(1)}, u32[]{:S(2)}, u32[]{:S(2)}) collective-permute-start(bf16[384,512]{1,0:T(8,128)(2,1)S(1)} %get-tuple-element.123), channel_id=1, source_target_pairs={{0,8},{4,12},{8,0},{12,4},{16,24},{20,28},{24,16},{28,20},{1,9},{5... | collective-permute-start | bytes 1179656 | tf_op jit(solution)/shard_map/ppermute | solution.py:301
  102.4 24.7 %collective-permute-start.22 = (bf16[192,512]{1,0:T(8,128)(2,1)S(1)}, bf16[192,512]{1,0:T(8,128)(2,1)S(1)}, u32[]{:S(2)}, u32[]{:S(2)}) collective-permute-start(bf16[192,512]{1,0:T(8,128)(2,1)S(1)} %get-tuple-element.126), channel_id=1, source_target_pairs={{0,16},{4,20},{8,24},{12,28},{16,0},{20,4},{24,8},{28,12},{1,17},{... | collective-permute-start | bytes 589832 | tf_op jit(solution)/shard_map/ppermute | solution.py:301
  123.7 7.7 %collective-permute-start.23 = (bf16[192,512]{1,0:T(8,128)(2,1)S(1)}, bf16[192,512]{1,0:T(8,128)(2,1)S(1)}, u32[]{:S(2)}, u32[]{:S(2)}) collective-permute-start(bf16[192,512]{1,0:T(8,128)(2,1)S(1)} %get-tuple-element.131), channel_id=1, source_target_pairs={{0,16},{4,20},{8,24},{12,28},{16,0},{20,4},{24,8},{28,12},{1,17},{... | collective-permute-start | bytes 589832 | tf_op jit(solution)/shard_map/ppermute | solution.py:301
  (2 other events, 30.8 us)

commit v20 on v19

--- a/solution.py
+++ b/solution.py
@@ -426,8 +426,9 @@
     got_nc = swapped(out_nc, "dp", 2)
     out_fb, own_b = far_step(after(meta, out_nc), mine_b, got_nb)
     got_fb = swapped(out_fb, "dp", 4)
-    out_fc, own_c = far_step(after(meta, out_fb, got_fa, arrived_c), mine_c, got_nc)
+    out_fc, own_c = far_step(after(meta, out_fb), mine_c, got_nc)
     got_fc = swapped(out_fc, "dp", 4)
+    got_fa, got_fb = after(got_fa, out_fc), after(got_fb, out_fc)
     total = [a + b.astype(F32) for a, b in ((own_a, got_fa), (own_b, got_fb), (own_c, got_fc))]
     down_grad = jnp.concatenate(total, axis=1) / math.sqrt(n * home)
 

time: 133 us -> 133 us (level)
  waiting for transfers between devices: 52.8 us -> 51.2 us
  starting transfers between devices: 26.9 us -> 28.3 us
    ppermute x24, waiting for transfers between devices: 52.8 us -> 51.2 us  [swapped(): return lax.ppermute(block, axis, [(i, i ^ distance) for i in range(n)])]
    ppermute x24, starting transfers between devices: 26.9 us -> 28.3 us  [swapped(): return lax.ppermute(block, axis, [(i, i ^ distance) for i in range(n)])]
  transfers between devices with their start and end apart: 24 -> 24, of which waited for: 11 -> 13; matrix products, arithmetic and copies ran while one was open for 0% -> 0% of each run, Pallas kernels for 34% -> 34%
where the time goes in v20:
time: 133 us; the launch traced here: 132 us
  waiting for transfers between devices  51.2 us (38%)
  Pallas kernels  50 us (38%)
  starting transfers between devices  28.3 us (21%)
  other arithmetic  1.99 us (1%)
    ppermute x24, waiting for transfers between devices, swapped(): return lax.ppermute(block, axis, [(i, i ^ distance) for i in range(n)])  51.2 us
    ppermute x24, starting transfers between devices, swapped(): return lax.ppermute(block, axis, [(i, i ^ distance) for i in range(n)])  28.3 us
    pallas_call x5, Pallas kernels, gelu(): kernel_call(functools.partial(gelu_kernel, base, block), [shape(rows, col...  17.7 us
    pallas_call x3, Pallas kernels, grads(): kernel_call(functools.partial(grad_kernel, first_row, first_slope, base,...  7.63 us
    pallas_call x2, Pallas kernels, weight_again(): kernel_call(functools.partial(again_kernel, base), [shape(rows, part)] *...  5.7 us
    pallas_call x1, Pallas kernels, shards(): kernel_call(first_kernel, [shape(LATE, width), shape(others, width), shap...  4.44 us
    pallas_call x1, Pallas kernels, shards(): kernel_call(functools.partial(place_kernel, (part,) * 3), shape(BAL, ff),...  3.29 us
    pallas_call x1, Pallas kernels, weight_first(): kernel_call(functools.partial(weight_kernel, 4), [shape(width, part)] * 2...  2.93 us
  transfers between devices with their start and end apart: 24, of which 13 were waited for; matrix products, arithmetic and copies ran while one was open for 0% of the time, Pallas kernels for 34%

profile of v20, /device:TPU:0, one launch (start us, length us, event | category | flops | bytes accessed | tf_op | source)
XLA Modules:
  0.0 132.4 jit_solution(46038726956940247)
XLA Ops:
  1.4 4.4 %shard_map.77 = (bf16[480,384]{1,0:T(8,128)(2,1)S(1)}, bf16[576,384]{1,0:T(8,128)(2,1)S(1)}, bf16[48,1920]{1,0:T(8,128)(2,1)S(1)}, bf16[480,1032]{1,0:T(8,128)(2...) custom-call(s32[9,8]{1,0:T(8,128)S(1)} %pad_add_fusion.meta, bf16[1032,384]{1,0:T(8,128)(2,1)} %cot_hbm.1, ...), custom_call_target="tpu_custom_call" | custom-call | flops 1 | bytes 1 | tf_op jit(solution)/shard_map/pallas_call | solution.py:370
  6.4 2.9 %collective-permute-start.1 = (bf16[480,384]{1,0:T(8,128)(2,1)S(1)}, bf16[480,384]{1,0:T(8,128)(2,1)S(1)}, u32[]{:S(2)}, u32[]{:S(2)}) collective-permute-start(bf16[480,384]{1,0:T(8,128)(2,1)S(1)} %get-tuple-element.72.p0.refs_0_), channel_id=1, source_target_pairs={{0,2},{1,3},{2,0},{3,1},{4,6},{5,7},{6,4},{7,5},{8,10},{9,11},{10,... | collective-permute-start | bytes 1105928 | tf_op jit(solution)/shard_map/ppermute | solution.py:301
  9.4 2.6 %collective-permute-start = (bf16[48,1920]{1,0:T(8,128)(2,1)S(1)}, bf16[48,1920]{1,0:T(8,128)(2,1)S(1)}, u32[]{:S(2)}, u32[]{:S(2)}) collective-permute-start(bf16[48,1920]{1,0:T(8,128)(2,1)S(1)} %get-tuple-element.71), channel_id=1, source_target_pairs={{0,16},{4,20},{8,24},{12,28},{16,0},{20,4},{24,8},{28,12},{1,17},{... | collective-permute-start | bytes 552968 | tf_op jit(solution)/shard_map/ppermute | solution.py:301
  12.4 3.0 %shard_map.78 = (bf16[480,512]{1,0:T(8,128)(2,1)S(1)}, f32[480,512]{1,0:T(8,128)S(1)}) custom-call(s32[9,8]{1,0:T(8,128)S(1)} %pad_add_fusion.meta, bf16[480,1032]{1,0:T(8,128)(2,1)S(1)} %get-tuple-element.74.pick, bf16[1032,1536]{1,0:T(8,128)(2,1)S(1)} %get-tuple-element.75.pre), custom_call_target="tpu_custom_call" | custom-call | flops 1 | bytes 1 | tf_op jit(solution)/shard_map/pallas_call | solution.py:329
  15.5 3.2 %shard_map.79 = (bf16[576,512]{1,0:T(8,128)(2,1)S(1)}, f32[576,512]{1,0:T(8,128)S(1)}) custom-call(s32[9,8]{1,0:T(8,128)S(1)} %pad_add_fusion.meta, bf16[576,1032]{1,0:T(8,128)(2,1)S(1)} %get-tuple-element.78.pick, bf16[1032,1536]{1,0:T(8,128)(2,1)S(1)} %get-tuple-element.75.pre), custom_call_target="tpu_custom_call" | custom-call | flops 1 | bytes 1 | tf_op jit(solution)/shard_map/pallas_call | solution.py:329
  24.0 3.6 %collective-permute-done.5.refs_6_.p2 = bf16[576,384]{1,0:T(8,128)(2,1)S(1)} collective-permute-done((bf16[576,384]{1,0:T(8,128)(2,1)S(1)}, bf16[576,384]{1,0:T(8,128)(2,1)S(1)}, u32[]{:S(2)}, u32[]{:S(2)}) %collective-permute-start.5) | collective-permute-done | bytes 442400 | tf_op jit(solution)/shard_map/ppermute | solution.py:301
  27.7 2.8 %collective-permute-start.8 = (bf16[480,512]{1,0:T(8,128)(2,1)S(1)}, bf16[480,512]{1,0:T(8,128)(2,1)S(1)}, u32[]{:S(2)}, u32[]{:S(2)}) collective-permute-start(bf16[480,512]{1,0:T(8,128)(2,1)S(1)} %shard_map.80), channel_id=1, source_target_pairs={{0,16},{4,20},{8,24},{12,28},{16,0},{20,4},{24,8},{28,12},{1,17},{... | collective-permute-start | bytes 1474568 | tf_op jit(solution)/shard_map/ppermute | solution.py:301
  30.5 2.9 %shard_map.81 = (bf16[384,512]{1,0:T(8,128)(2,1)S(1)}, bf16[384,512]{1,0:T(8,128)(2,1)S(1)}, f32[384,512]{1,0:T(8,128)S(1)}, f32[384,512]{1,0:T(8,128)S(1)}, bf1...) custom-call(s32[9,8]{1,0:T(8,128)S(1)} %pad_add_fusion.meta, ...), custom_call_target="tpu_custom_call" | custom-call | flops 1 | bytes 1 | tf_op jit(solution)/shard_map/pallas_call | solution.py:336
  35.0 5.0 %shard_map.82 = (bf16[480,1024]{1,0:T(8,128)(2,1)S(1)}, f32[480,1024]{1,0:T(8,128)S(1)}) custom-call(s32[9,8]{1,0:T(8,128)S(1)} %pad_add_fusion.meta, bf16[480,1032]{1,0:T(8,128)(2,1)S(1)} %get-tuple-element.74.pick, bf16[1032,1536]{1,0:T(8,128)(2,1)S(1)} %get-tuple-element.75.pre), custom_call_target="tpu_custom_call" | custom-call | flops 1 | bytes 1 | tf_op jit(solution)/shard_map/pallas_call | solution.py:329
  45.4 3.2 %shard_map.84 = (bf16[576,512]{1,0:T(8,128)(2,1)S(1)}, f32[576,512]{1,0:T(8,128)S(1)}) custom-call(s32[9,8]{1,0:T(8,128)S(1)} %pad_add_fusion.meta, bf16[576,1032]{1,0:T(8,128)(2,1)S(1)} %get-tuple-element.78.pick, bf16[1032,1536]{1,0:T(8,128)(2,1)S(1)} %get-tuple-element.75.pre), custom_call_target="tpu_custom_call" | custom-call | flops 1 | bytes 1 | tf_op jit(solution)/shard_map/pallas_call | solution.py:329
  48.6 4.2 %collective-permute-done.8.rest_0_ = bf16[480,512]{1,0:T(8,128)(2,1)S(1)} collective-permute-done((bf16[480,512]{1,0:T(8,128)(2,1)S(1)}, bf16[480,512]{1,0:T(8,128)(2,1)S(1)}, u32[]{:S(2)}, u32[]{:S(2)}) %collective-permute-start.8) | collective-permute-done | bytes 491552 | tf_op jit(solution)/shard_map/ppermute | solution.py:301
  52.9 2.9 %shard_map.85 = (bf16[768,512]{1,0:T(8,128)(2,1)S(1)}, f32[768,512]{1,0:T(8,128)S(1)}) custom-call(s32[9,8]{1,0:T(8,128)S(1)} %pad_add_fusion.meta, bf16[1536,480]{1,0:T(8,128)(2,1)S(1)} %get-tuple-element.96.lhs_moved, bf16[1536,576]{1,0:T(8,128)(2,1)S(1)} %get-tuple-element.97.lhs_kept, bf16[480,1024]{1,0:T(8,128)(2,1)S(1)} %get-tuple-element.88.act_moved, ...), custom_call_target="tpu_custom_call" | custom-call | flops 1 | bytes 1 | tf_op jit(solution)/shard_map/pallas_call | solution.py:345
  58.3 4.1 %collective-permute-start.14 = (bf16[384,512]{1,0:T(8,128)(2,1)S(1)}, bf16[384,512]{1,0:T(8,128)(2,1)S(1)}, u32[]{:S(2)}, u32[]{:S(2)}) collective-permute-start(bf16[384,512]{1,0:T(8,128)(2,1)S(1)} %get-tuple-element.102), channel_id=1, source_target_pairs={{0,8},{4,12},{8,0},{12,4},{16,24},{20,28},{24,16},{28,20},{1,9},{5... | collective-permute-start | bytes 1179656 | tf_op jit(solution)/shard_map/ppermute | solution.py:301
  64.0 3.2 %shard_map.87 = (bf16[576,512]{1,0:T(8,128)(2,1)S(1)}, f32[576,512]{1,0:T(8,128)S(1)}) custom-call(s32[9,8]{1,0:T(8,128)S(1)} %pad_add_fusion.meta, bf16[576,1032]{1,0:T(8,128)(2,1)S(1)} %get-tuple-element.78.pick, bf16[1032,1536]{1,0:T(8,128)(2,1)S(1)} %get-tuple-element.75.pre), custom_call_target="tpu_custom_call" | custom-call | flops 1 | bytes 1 | tf_op jit(solution)/shard_map/pallas_call | solution.py:329
  68.6 2.9 %shard_map.88 = (bf16[384,512]{1,0:T(8,128)(2,1)S(1)}, bf16[384,512]{1,0:T(8,128)(2,1)S(1)}, f32[384,512]{1,0:T(8,128)S(1)}, f32[384,512]{1,0:T(8,128)S(1)}) custom-call(s32[9,8]{1,0:T(8,128)S(1)} %pad_add_fusion.meta, bf16[1536,480]{1,0:T(8,128)(2,1)S(1)} %get-tuple-element.96.lhs_moved, bf16[1536,576]{1,0:T(8,128)(2,1)S(1)} %get-tuple-element.97.lhs_kept, ...), custom_call_target="tpu_custom_call" | custom-call | flops 1 | bytes 1 | tf_op jit(solution)/shard_map/pallas_call | solution.py:345
  73.6 2.6 %collective-permute-done.14.got = bf16[384,512]{1,0:T(8,128)(2,1)S(1)} collective-permute-done((bf16[384,512]{1,0:T(8,128)(2,1)S(1)}, bf16[384,512]{1,0:T(8,128)(2,1)S(1)}, u32[]{:S(2)}, u32[]{:S(2)}) %collective-permute-start.14) | collective-permute-done | bytes 393248 | tf_op jit(solution)/shard_map/ppermute | solution.py:301
  76.2 5.2 %collective-permute-done.13.rest_1_ = bf16[480,512]{1,0:T(8,128)(2,1)S(1)} collective-permute-done((bf16[480,512]{1,0:T(8,128)(2,1)S(1)}, bf16[480,512]{1,0:T(8,128)(2,1)S(1)}, u32[]{:S(2)}, u32[]{:S(2)}) %collective-permute-start.13) | collective-permute-done | bytes 491552 | tf_op jit(solution)/shard_map/ppermute | solution.py:301
  85.8 3.5 %shard_map.91.kept = bf16[528,1536]{1,0:T(8,128)(2,1)S(1)} custom-call(s32[9,8]{1,0:T(8,128)S(1)} %pad_add_fusion.meta, bf16[576,384]{1,0:T(8,128)(2,1)S(1)} %get-tuple-element.80.refs_4_.p0, bf16[576,384]{1,0:T(8,128)(2,1)S(1)} %collective-permute-done.3.refs_5_.p1, bf16[576,384]{1,0:T(8,128)(2,1)S(1)} %collective-permute-done.5.refs_6_.p2, ...), custom_call_target="tpu_custom_call" | custom-call | flops 1 | bytes 1 | tf_op jit(solution)/shard_map/pallas_call | solution.py:352
  89.3 2.9 %shard_map.92.early = bf16[48,1536]{1,0:T(8,128)(2,1)S(1)} custom-call(s32[9,8]{1,0:T(8,128)S(1)} %pad_add_fusion.meta, bf16[48,1920]{1,0:T(8,128)(2,1)S(1)} %collective-permute-done.own, bf16[48,384]{1,0:T(8,128)(2,1)S(1)} %collective-permute-done.11.p1, bf16[48,384]{1,0:T(8,128)(2,1)S(1)} %collective-permute-done.10.p2, ...), custom_call_target="tpu_custom_call" | custom-call | flops 1 | bytes 1 | tf_op jit(solution)/shard_map/pallas_call | solution.py:420
  93.9 3.4 %collective-permute-start.21 = (bf16[192,512]{1,0:T(8,128)(2,1)S(1)}, bf16[192,512]{1,0:T(8,128)(2,1)S(1)}, u32[]{:S(2)}, u32[]{:S(2)}) collective-permute-start(bf16[192,512]{1,0:T(8,128)(2,1)S(1)} %get-tuple-element.115), channel_id=1, source_target_pairs={{0,16},{4,20},{8,24},{12,28},{16,0},{20,4},{24,8},{28,12},{1,17},{... | collective-permute-start | bytes 589832 | tf_op jit(solution)/shard_map/ppermute | solution.py:301
  97.3 4.2 %collective-permute-done.18.got = bf16[384,512]{1,0:T(8,128)(2,1)S(1)} collective-permute-done((bf16[384,512]{1,0:T(8,128)(2,1)S(1)}, bf16[384,512]{1,0:T(8,128)(2,1)S(1)}, u32[]{:S(2)}, u32[]{:S(2)}) %collective-permute-start.18) | collective-permute-done | bytes 393248 | tf_op jit(solution)/shard_map/ppermute | solution.py:301
  102.4 14.8 %collective-permute-done.19.got = bf16[384,512]{1,0:T(8,128)(2,1)S(1)} collective-permute-done((bf16[384,512]{1,0:T(8,128)(2,1)S(1)}, bf16[384,512]{1,0:T(8,128)(2,1)S(1)}, u32[]{:S(2)}, u32[]{:S(2)}) %collective-permute-start.19) | collective-permute-done | bytes 393248 | tf_op jit(solution)/shard_map/ppermute | solution.py:301
  118.1 6.8 %collective-permute-done.21 = bf16[192,512]{1,0:T(8,128)(2,1)S(1)} collective-permute-done((bf16[192,512]{1,0:T(8,128)(2,1)S(1)}, bf16[192,512]{1,0:T(8,128)(2,1)S(1)}, u32[]{:S(2)}, u32[]{:S(2)}) %collective-permute-start.21) | collective-permute-done | bytes 196640 | tf_op jit(solution)/shard_map/ppermute | solution.py:301
  125.0 3.3 %shard_map.96 = bf16[720,1536]{1,0:T(8,128)(2,1)} custom-call(s32[9,8]{1,0:T(8,128)S(1)} %pad_add_fusion.meta, bf16[528,1536]{1,0:T(8,128)(2,1)S(1)} %shard_map.91.kept, bf16[48,1536]{1,0:T(8,128)(2,1)S(1)} %shard_map.92.early, bf16[480,512]{1,0:T(8,128)(2,1)S(1)} %collective-permute-done.8.rest_0_, bf16[480,512]{1,0:T(8,128)(2,1)S(1)} %collective-permute-done.13.rest_1_, ...), custom_call_target="tpu_custom_call" | custom-call | flops 1 | bytes 1 | tf_op jit(solution)/shard_map/pallas_call | solution.py:435
  (55 shorter events, 33.7 us)
Async XLA Ops:
  5.8 14.7 %collective-permute-start.3 = (bf16[576,384]{1,0:T(8,128)(2,1)S(1)}, bf16[576,384]{1,0:T(8,128)(2,1)S(1)}, u32[]{:S(2)}, u32[]{:S(2)}) collective-permute-start(bf16[576,384]{1,0:T(8,128)(2,1)S(1)} %get-tuple-element.80.refs_4_.p0), channel_id=1, source_target_pairs={{0,1},{1,0},{2,3},{3,2},{4,5},{5,4},{6,7},{7,6},{8,9},{9,8},{10,11... | collective-permute-start | bytes 1327112 | tf_op jit(solution)/shard_map/ppermute | solution.py:301
  6.3 14.2 %collective-permute-start.2 = (bf16[480,384]{1,0:T(8,128)(2,1)S(1)}, bf16[480,384]{1,0:T(8,128)(2,1)S(1)}, u32[]{:S(2)}, u32[]{:S(2)}) collective-permute-start(bf16[480,384]{1,0:T(8,128)(2,1)S(1)} %get-tuple-element.72.p0.refs_0_), channel_id=1, source_target_pairs={{0,1},{1,0},{2,3},{3,2},{4,5},{5,4},{6,7},{7,6},{8,9},{9,8},{10,11... | collective-permute-start | bytes 1105928 | tf_op jit(solution)/shard_map/ppermute | solution.py:301
  6.4 14.1 %collective-permute-start.1 = (bf16[480,384]{1,0:T(8,128)(2,1)S(1)}, bf16[480,384]{1,0:T(8,128)(2,1)S(1)}, u32[]{:S(2)}, u32[]{:S(2)}) collective-permute-start(bf16[480,384]{1,0:T(8,128)(2,1)S(1)} %get-tuple-element.72.p0.refs_0_), channel_id=1, source_target_pairs={{0,2},{1,3},{2,0},{3,1},{4,6},{5,7},{6,4},{7,5},{8,10},{9,11},{10,... | collective-permute-start | bytes 1105928 | tf_op jit(solution)/shard_map/ppermute | solution.py:301
  9.4 11.2 %collective-permute-start = (bf16[48,1920]{1,0:T(8,128)(2,1)S(1)}, bf16[48,1920]{1,0:T(8,128)(2,1)S(1)}, u32[]{:S(2)}, u32[]{:S(2)}) collective-permute-start(bf16[48,1920]{1,0:T(8,128)(2,1)S(1)} %get-tuple-element.71), channel_id=1, source_target_pairs={{0,16},{4,20},{8,24},{12,28},{16,0},{20,4},{24,8},{28,12},{1,17},{... | collective-permute-start | bytes 552968 | tf_op jit(solution)/shard_map/ppermute | solution.py:301
  11.9 15.7 %collective-permute-start.5 = (bf16[576,384]{1,0:T(8,128)(2,1)S(1)}, bf16[576,384]{1,0:T(8,128)(2,1)S(1)}, u32[]{:S(2)}, u32[]{:S(2)}) collective-permute-start(bf16[576,384]{1,0:T(8,128)(2,1)S(1)} %get-tuple-element.80.refs_4_.p0), channel_id=1, source_target_pairs={{0,2},{1,3},{2,0},{3,1},{4,6},{5,7},{6,4},{7,5},{8,10},{9,11},{10,... | collective-permute-start | bytes 1327112 | tf_op jit(solution)/shard_map/ppermute | solution.py:301
  20.6 1.8 %collective-permute-start.4 = (bf16[480,384]{1,0:T(8,128)(2,1)S(1)}, bf16[480,384]{1,0:T(8,128)(2,1)S(1)}, u32[]{:S(2)}, u32[]{:S(2)}) collective-permute-start(bf16[480,384]{1,0:T(8,128)(2,1)S(1)} %collective-permute-done.1.p2.refs_2_), channel_id=1, source_target_pairs={{0,1},{1,0},{2,3},{3,2},{4,5},{5,4},{6,7},{7,6},{8,9},{9,8},{10,11... | collective-permute-start | bytes 1105928 | tf_op jit(solution)/shard_map/ppermute | solution.py:301
  27.7 2.8 %collective-permute-start.6 = (bf16[576,384]{1,0:T(8,128)(2,1)S(1)}, bf16[576,384]{1,0:T(8,128)(2,1)S(1)}, u32[]{:S(2)}, u32[]{:S(2)}) collective-permute-start(bf16[576,384]{1,0:T(8,128)(2,1)S(1)} %collective-permute-done.5.refs_6_.p2), channel_id=1, source_target_pairs={{0,1},{1,0},{2,3},{3,2},{4,5},{5,4},{6,7},{7,6},{8,9},{9,8},{10,11... | collective-permute-start | bytes 1327112 | tf_op jit(solution)/shard_map/ppermute | solution.py:301
  27.7 25.2 %collective-permute-start.8 = (bf16[480,512]{1,0:T(8,128)(2,1)S(1)}, bf16[480,512]{1,0:T(8,128)(2,1)S(1)}, u32[]{:S(2)}, u32[]{:S(2)}) collective-permute-start(bf16[480,512]{1,0:T(8,128)(2,1)S(1)} %shard_map.80), channel_id=1, source_target_pairs={{0,16},{4,20},{8,24},{12,28},{16,0},{20,4},{24,8},{28,12},{1,17},{... | collective-permute-start | bytes 1474568 | tf_op jit(solution)/shard_map/ppermute | solution.py:301
  33.4 12.0 %collective-permute-start.7 = (bf16[384,512]{1,0:T(8,128)(2,1)S(1)}, bf16[384,512]{1,0:T(8,128)(2,1)S(1)}, u32[]{:S(2)}, u32[]{:S(2)}) collective-permute-start(bf16[384,512]{1,0:T(8,128)(2,1)S(1)} %get-tuple-element.92), channel_id=1, source_target_pairs={{0,4},{4,0},{8,12},{12,8},{16,20},{20,16},{24,28},{28,24},{1,5},{5... | collective-permute-start | bytes 1179656 | tf_op jit(solution)/shard_map/ppermute | solution.py:301
  40.0 17.4 %collective-permute-start.9 = (bf16[384,512]{1,0:T(8,128)(2,1)S(1)}, bf16[384,512]{1,0:T(8,128)(2,1)S(1)}, u32[]{:S(2)}, u32[]{:S(2)}) collective-permute-start(bf16[384,512]{1,0:T(8,128)(2,1)S(1)} %get-tuple-element.101), channel_id=1, source_target_pairs={{0,4},{4,0},{8,12},{12,8},{16,20},{20,16},{24,28},{28,24},{1,5},{5... | collective-permute-start | bytes 1179656 | tf_op jit(solution)/shard_map/ppermute | solution.py:301
  55.8 25.6 %collective-permute-start.15 = (bf16[768,512]{1,0:T(8,128)(2,1)S(1)}, bf16[768,512]{1,0:T(8,128)(2,1)S(1)}, u32[]{:S(2)}, u32[]{:S(2)}) collective-permute-start(bf16[768,512]{1,0:T(8,128)(2,1)S(1)} %get-tuple-element.98), channel_id=1, source_target_pairs={{0,4},{4,0},{8,12},{12,8},{16,20},{20,16},{24,28},{28,24},{1,5},{5... | collective-permute-start | bytes 2359304 | tf_op jit(solution)/shard_map/ppermute | solution.py:301
  57.4 24.0 %collective-permute-start.13 = (bf16[480,512]{1,0:T(8,128)(2,1)S(1)}, bf16[480,512]{1,0:T(8,128)(2,1)S(1)}, u32[]{:S(2)}, u32[]{:S(2)}) collective-permute-start(bf16[480,512]{1,0:T(8,128)(2,1)S(1)} %get-tuple-element.109), channel_id=1, source_target_pairs={{0,16},{4,20},{8,24},{12,28},{16,0},{20,4},{24,8},{28,12},{1,17},{... | collective-permute-start | bytes 1474568 | tf_op jit(solution)/shard_map/ppermute | solution.py:301
  58.3 17.9 %collective-permute-start.14 = (bf16[384,512]{1,0:T(8,128)(2,1)S(1)}, bf16[384,512]{1,0:T(8,128)(2,1)S(1)}, u32[]{:S(2)}, u32[]{:S(2)}) collective-permute-start(bf16[384,512]{1,0:T(8,128)(2,1)S(1)} %get-tuple-element.102), channel_id=1, source_target_pairs={{0,8},{4,12},{8,0},{12,4},{16,24},{20,28},{24,16},{28,20},{1,9},{5... | collective-permute-start | bytes 1179656 | tf_op jit(solution)/shard_map/ppermute | solution.py:301
  62.4 4.7 %collective-permute-start.10 = (bf16[48,384]{1,0:T(8,128)(2,1)S(1)}, bf16[48,384]{1,0:T(8,128)(2,1)S(1)}, u32[]{:S(2)}, u32[]{:S(2)}) collective-permute-start(bf16[48,384]{1,0:T(8,128)(2,1)S(1)} %slice.4), channel_id=1, source_target_pairs={{0,2},{1,3},{2,0},{3,1},{4,6},{5,7},{6,4},{7,5},{8,10},{9,11},{10,... | collective-permute-start | bytes 110600 | tf_op jit(solution)/shard_map/ppermute | solution.py:301
  63.9 3.2 %collective-permute-start.11 = (bf16[48,384]{1,0:T(8,128)(2,1)S(1)}, bf16[48,384]{1,0:T(8,128)(2,1)S(1)}, u32[]{:S(2)}, u32[]{:S(2)}) collective-permute-start(bf16[48,384]{1,0:T(8,128)(2,1)S(1)} %slice.4), channel_id=1, source_target_pairs={{0,1},{1,0},{2,3},{3,2},{4,5},{5,4},{6,7},{7,6},{8,9},{9,8},{10,11... | collective-permute-start | bytes 110600 | tf_op jit(solution)/shard_map/ppermute | solution.py:301
  67.2 1.4 %collective-permute-start.12 = (bf16[48,384]{1,0:T(8,128)(2,1)S(1)}, bf16[48,384]{1,0:T(8,128)(2,1)S(1)}, u32[]{:S(2)}, u32[]{:S(2)}) collective-permute-start(bf16[48,384]{1,0:T(8,128)(2,1)S(1)} %collective-permute-done.10.p2), channel_id=1, source_target_pairs={{0,1},{1,0},{2,3},{3,2},{4,5},{5,4},{6,7},{7,6},{8,9},{9,8},{10,11... | collective-permute-start | bytes 110600 | tf_op jit(solution)/shard_map/ppermute | solution.py:301
  71.5 20.7 %collective-permute-start.16 = (bf16[384,512]{1,0:T(8,128)(2,1)S(1)}, bf16[384,512]{1,0:T(8,128)(2,1)S(1)}, u32[]{:S(2)}, u32[]{:S(2)}) collective-permute-start(bf16[384,512]{1,0:T(8,128)(2,1)S(1)} %get-tuple-element.123), channel_id=1, source_target_pairs={{0,4},{4,0},{8,12},{12,8},{16,20},{20,16},{24,28},{28,24},{1,5},{5... | collective-permute-start | bytes 1179656 | tf_op jit(solution)/shard_map/ppermute | solution.py:301
  72.1 20.1 %collective-permute-start.17 = (bf16[384,512]{1,0:T(8,128)(2,1)S(1)}, bf16[384,512]{1,0:T(8,128)(2,1)S(1)}, u32[]{:S(2)}, u32[]{:S(2)}) collective-permute-start(bf16[384,512]{1,0:T(8,128)(2,1)S(1)} %get-tuple-element.124), channel_id=1, source_target_pairs={{0,4},{4,0},{8,12},{12,8},{16,20},{20,16},{24,28},{28,24},{1,5},{5... | collective-permute-start | bytes 1179656 | tf_op jit(solution)/shard_map/ppermute | solution.py:301
  82.3 19.2 %collective-permute-start.18 = (bf16[384,512]{1,0:T(8,128)(2,1)S(1)}, bf16[384,512]{1,0:T(8,128)(2,1)S(1)}, u32[]{:S(2)}, u32[]{:S(2)}) collective-permute-start(bf16[384,512]{1,0:T(8,128)(2,1)S(1)} %get-tuple-element.112), channel_id=1, source_target_pairs={{0,8},{4,12},{8,0},{12,4},{16,24},{20,28},{24,16},{28,20},{1,9},{5... | collective-permute-start | bytes 1179656 | tf_op jit(solution)/shard_map/ppermute | solution.py:301
  82.4 42.6 %collective-permute-start.20 = (bf16[480,512]{1,0:T(8,128)(2,1)S(1)}, bf16[480,512]{1,0:T(8,128)(2,1)S(1)}, u32[]{:S(2)}, u32[]{:S(2)}) collective-permute-start(bf16[480,512]{1,0:T(8,128)(2,1)S(1)} %get-tuple-element.134), channel_id=1, source_target_pairs={{0,16},{4,20},{8,24},{12,28},{16,0},{20,4},{24,8},{28,12},{1,17},{... | collective-permute-start | bytes 1474568 | tf_op jit(solution)/shard_map/ppermute | solution.py:301
  93.1 24.1 %collective-permute-start.19 = (bf16[384,512]{1,0:T(8,128)(2,1)S(1)}, bf16[384,512]{1,0:T(8,128)(2,1)S(1)}, u32[]{:S(2)}, u32[]{:S(2)}) collective-permute-start(bf16[384,512]{1,0:T(8,128)(2,1)S(1)} %get-tuple-element.125), channel_id=1, source_target_pairs={{0,8},{4,12},{8,0},{12,4},{16,24},{20,28},{24,16},{28,20},{1,9},{5... | collective-permute-start | bytes 1179656 | tf_op jit(solution)/shard_map/ppermute | solution.py:301
  93.9 31.0 %collective-permute-start.21 = (bf16[192,512]{1,0:T(8,128)(2,1)S(1)}, bf16[192,512]{1,0:T(8,128)(2,1)S(1)}, u32[]{:S(2)}, u32[]{:S(2)}) collective-permute-start(bf16[192,512]{1,0:T(8,128)(2,1)S(1)} %get-tuple-element.115), channel_id=1, source_target_pairs={{0,16},{4,20},{8,24},{12,28},{16,0},{20,4},{24,8},{28,12},{1,17},{... | collective-permute-start | bytes 589832 | tf_op jit(solution)/shard_map/ppermute | solution.py:301
  102.4 26.7 %collective-permute-start.22 = (bf16[192,512]{1,0:T(8,128)(2,1)S(1)}, bf16[192,512]{1,0:T(8,128)(2,1)S(1)}, u32[]{:S(2)}, u32[]{:S(2)}) collective-permute-start(bf16[192,512]{1,0:T(8,128)(2,1)S(1)} %get-tuple-element.128), channel_id=1, source_target_pairs={{0,16},{4,20},{8,24},{12,28},{16,0},{20,4},{24,8},{28,12},{1,17},{... | collective-permute-start | bytes 589832 | tf_op jit(solution)/shard_map/ppermute | solution.py:301
  118.0 13.2 %collective-permute-start.23 = (bf16[192,512]{1,0:T(8,128)(2,1)S(1)}, bf16[192,512]{1,0:T(8,128)(2,1)S(1)}, u32[]{:S(2)}, u32[]{:S(2)}) collective-permute-start(bf16[192,512]{1,0:T(8,128)(2,1)S(1)} %get-tuple-element.131), channel_id=1, source_target_pairs={{0,16},{4,20},{8,24},{12,28},{16,0},{20,4},{24,8},{28,12},{1,17},{... | collective-permute-start | bytes 589832 | tf_op jit(solution)/shard_map/ppermute | solution.py:301
  (2 other events, 30.8 us)

commit v21 on v20

--- a/solution.py
+++ b/solution.py
@@ -11,7 +11,7 @@
 SEND = 528
 KEEP = 528
 TILE = 16
-EARLY = 48
+EARLY = 96
 LATE = SEND - EARLY
 SLOTS = 4
 BAL = 720

time: 133 us -> 129 us (0.970)
  starting transfers between devices: 28.3 us -> 21.4 us
  waiting for transfers between devices: 51.2 us -> 54.3 us
    ppermute x24, starting transfers between devices: 28.3 us -> 21.4 us  [swapped(): return lax.ppermute(block, axis, [(i, i ^ distance) for i in range(n)])]
    ppermute x24, waiting for transfers between devices: 51.2 us -> 54.3 us  [swapped(): return lax.ppermute(block, axis, [(i, i ^ distance) for i in range(n)])]
  transfers between devices with their start and end apart: 24 -> 24, of which waited for: 13 -> 14; matrix products, arithmetic and copies ran while one was open for 0% -> 0% of each run, Pallas kernels for 34% -> 36%
where the time goes in v21:
time: 129 us
  waiting for transfers between devices  54.3 us (42%)
  Pallas kernels  50.3 us (39%)
  starting transfers between devices  21.4 us (17%)
  other arithmetic  2.01 us (2%)
    ppermute x24, waiting for transfers between devices, swapped(): return lax.ppermute(block, axis, [(i, i ^ distance) for i in range(n)])  54.3 us
    ppermute x24, starting transfers between devices, swapped(): return lax.ppermute(block, axis, [(i, i ^ distance) for i in range(n)])  21.4 us
    pallas_call x5, Pallas kernels, gelu(): kernel_call(functools.partial(gelu_kernel, base, block), [shape(rows, col...  17.6 us
    pallas_call x3, Pallas kernels, grads(): kernel_call(functools.partial(grad_kernel, first_row, first_slope, base,...  7.37 us
    pallas_call x2, Pallas kernels, weight_again(): kernel_call(functools.partial(again_kernel, base), [shape(rows, part)] *...  5.77 us
    pallas_call x1, Pallas kernels, shards(): kernel_call(first_kernel, [shape(LATE, width), shape(others, width), shap...  4.47 us
    pallas_call x1, Pallas kernels, shards(): kernel_call(functools.partial(early_kernel, 256), shape(EARLY, ff), [IN_V...  3.36 us
    pallas_call x1, Pallas kernels, shards(): kernel_call(functools.partial(place_kernel, (part,) * 3), shape(BAL, ff),...  3.29 us
  transfers between devices with their start and end apart: 24, of which 14 were waited for; matrix products, arithmetic and copies ran while one was open for 0% of the time, Pallas kernels for 36%

profile of v21, /device:TPU:0, one launch (start us, length us, event | category | flops | bytes accessed | tf_op | source)
XLA Modules:
  0.0 128.9 jit_solution(15345086476101069390)
XLA Ops:
  1.4 4.5 %shard_map.77 = (bf16[432,384]{1,0:T(8,128)(2,1)S(1)}, bf16[624,384]{1,0:T(8,128)(2,1)S(1)}, bf16[96,1920]{1,0:T(8,128)(2,1)S(1)}, bf16[432,1032]{1,0:T(8,128)(2...) custom-call(s32[9,8]{1,0:T(8,128)S(1)} %pad_add_fusion.meta, bf16[1032,384]{1,0:T(8,128)(2,1)} %cot_hbm.1, ...), custom_call_target="tpu_custom_call" | custom-call | flops 1 | bytes 1 | tf_op jit(solution)/shard_map/pallas_call | solution.py:370
  6.4 3.6 %collective-permute-start = (bf16[96,1920]{1,0:T(8,128)(2,1)S(1)}, bf16[96,1920]{1,0:T(8,128)(2,1)S(1)}, u32[]{:S(2)}, u32[]{:S(2)}) collective-permute-start(bf16[96,1920]{1,0:T(8,128)(2,1)S(1)} %get-tuple-element.71), channel_id=1, source_target_pairs={{0,16},{4,20},{8,24},{12,28},{16,0},{20,4},{24,8},{28,12},{1,17},{... | collective-permute-start | bytes 1105928 | tf_op jit(solution)/shard_map/ppermute | solution.py:301
  12.2 2.8 %shard_map.78 = (bf16[432,512]{1,0:T(8,128)(2,1)S(1)}, f32[432,512]{1,0:T(8,128)S(1)}) custom-call(s32[9,8]{1,0:T(8,128)S(1)} %pad_add_fusion.meta, bf16[432,1032]{1,0:T(8,128)(2,1)S(1)} %get-tuple-element.74.pick, bf16[1032,1536]{1,0:T(8,128)(2,1)S(1)} %get-tuple-element.75.pre), custom_call_target="tpu_custom_call" | custom-call | flops 1 | bytes 1 | tf_op jit(solution)/shard_map/pallas_call | solution.py:329
  15.0 3.4 %shard_map.79 = (bf16[624,512]{1,0:T(8,128)(2,1)S(1)}, f32[624,512]{1,0:T(8,128)S(1)}) custom-call(s32[9,8]{1,0:T(8,128)S(1)} %pad_add_fusion.meta, bf16[624,1032]{1,0:T(8,128)(2,1)S(1)} %get-tuple-element.78.pick, bf16[1032,1536]{1,0:T(8,128)(2,1)S(1)} %get-tuple-element.75.pre), custom_call_target="tpu_custom_call" | custom-call | flops 1 | bytes 1 | tf_op jit(solution)/shard_map/pallas_call | solution.py:329
  18.4 2.3 %collective-permute-done.1.p2.refs_2_ = bf16[432,384]{1,0:T(8,128)(2,1)S(1)} collective-permute-done((bf16[432,384]{1,0:T(8,128)(2,1)S(1)}, bf16[432,384]{1,0:T(8,128)(2,1)S(1)}, u32[]{:S(2)}, u32[]{:S(2)}) %collective-permute-start.1) | collective-permute-done | bytes 331808 | tf_op jit(solution)/shard_map/ppermute | solution.py:301
  20.8 6.3 %collective-permute-done.own = bf16[96,1920]{1,0:T(8,128)(2,1)S(1)} collective-permute-done((bf16[96,1920]{1,0:T(8,128)(2,1)S(1)}, bf16[96,1920]{1,0:T(8,128)(2,1)S(1)}, u32[]{:S(2)}, u32[]{:S(2)}) %collective-permute-start) | collective-permute-done | bytes 368672 | tf_op jit(solution)/shard_map/ppermute | solution.py:301
  32.3 3.0 %shard_map.81 = (bf16[384,512]{1,0:T(8,128)(2,1)S(1)}, bf16[384,512]{1,0:T(8,128)(2,1)S(1)}, f32[384,512]{1,0:T(8,128)S(1)}, f32[384,512]{1,0:T(8,128)S(1)}, bf1...) custom-call(s32[9,8]{1,0:T(8,128)S(1)} %pad_add_fusion.meta, ...), custom_call_target="tpu_custom_call" | custom-call | flops 1 | bytes 1 | tf_op jit(solution)/shard_map/pallas_call | solution.py:336
  36.9 4.6 %shard_map.82 = (bf16[432,1024]{1,0:T(8,128)(2,1)S(1)}, f32[432,1024]{1,0:T(8,128)S(1)}) custom-call(s32[9,8]{1,0:T(8,128)S(1)} %pad_add_fusion.meta, bf16[432,1032]{1,0:T(8,128)(2,1)S(1)} %get-tuple-element.74.pick, bf16[1032,1536]{1,0:T(8,128)(2,1)S(1)} %get-tuple-element.75.pre), custom_call_target="tpu_custom_call" | custom-call | flops 1 | bytes 1 | tf_op jit(solution)/shard_map/pallas_call | solution.py:329
  42.1 2.3 %shard_map.83 = (bf16[432,512]{1,0:T(8,128)(2,1)S(1)}, bf16[432,512]{1,0:T(8,128)(2,1)S(1)}) custom-call(s32[9,8]{1,0:T(8,128)S(1)} %pad_add_fusion.meta, bf16[432,384]{1,0:T(8,128)(2,1)S(1)} %get-tuple-element.72.p0.refs_0_, bf16[432,384]{1,0:T(8,128)(2,1)S(1)} %collective-permute-done.2.p1.refs_1_, bf16[432,384]{1,0:T(8,128)(2,1)S(1)} %collective-permute-done.1.p2.refs_2_, ...), custom_call_target="tpu_custom_call" | custom-call | flops 1 | bytes 1 | tf_op jit(solution)/shard_map/pallas_call | solution.py:352
  44.4 2.9 %collective-permute-done.7.refs_2_ = bf16[384,512]{1,0:T(8,128)(2,1)S(1)} collective-permute-done((bf16[384,512]{1,0:T(8,128)(2,1)S(1)}, bf16[384,512]{1,0:T(8,128)(2,1)S(1)}, u32[]{:S(2)}, u32[]{:S(2)}) %collective-permute-start.7) | collective-permute-done | bytes 393248 | tf_op jit(solution)/shard_map/ppermute | solution.py:301
  47.3 3.4 %shard_map.84 = (bf16[624,512]{1,0:T(8,128)(2,1)S(1)}, f32[624,512]{1,0:T(8,128)S(1)}) custom-call(s32[9,8]{1,0:T(8,128)S(1)} %pad_add_fusion.meta, bf16[624,1032]{1,0:T(8,128)(2,1)S(1)} %get-tuple-element.78.pick, bf16[1032,1536]{1,0:T(8,128)(2,1)S(1)} %get-tuple-element.75.pre), custom_call_target="tpu_custom_call" | custom-call | flops 1 | bytes 1 | tf_op jit(solution)/shard_map/pallas_call | solution.py:329
  50.7 2.7 %collective-permute-done.8.rest_0_ = bf16[432,512]{1,0:T(8,128)(2,1)S(1)} collective-permute-done((bf16[432,512]{1,0:T(8,128)(2,1)S(1)}, bf16[432,512]{1,0:T(8,128)(2,1)S(1)}, u32[]{:S(2)}, u32[]{:S(2)}) %collective-permute-start.8) | collective-permute-done | bytes 442400 | tf_op jit(solution)/shard_map/ppermute | solution.py:301
  53.4 2.9 %shard_map.85 = (bf16[768,512]{1,0:T(8,128)(2,1)S(1)}, f32[768,512]{1,0:T(8,128)S(1)}) custom-call(s32[9,8]{1,0:T(8,128)S(1)} %pad_add_fusion.meta, bf16[1536,432]{1,0:T(8,128)(2,1)S(1)} %get-tuple-element.96.lhs_moved, bf16[1536,624]{1,0:T(8,128)(2,1)S(1)} %get-tuple-element.97.lhs_kept, bf16[432,1024]{1,0:T(8,128)(2,1)S(1)} %get-tuple-element.88.act_moved, ...), custom_call_target="tpu_custom_call" | custom-call | flops 1 | bytes 1 | tf_op jit(solution)/shard_map/pallas_call | solution.py:345
  62.3 3.4 %shard_map.87 = (bf16[624,512]{1,0:T(8,128)(2,1)S(1)}, f32[624,512]{1,0:T(8,128)S(1)}) custom-call(s32[9,8]{1,0:T(8,128)S(1)} %pad_add_fusion.meta, bf16[624,1032]{1,0:T(8,128)(2,1)S(1)} %get-tuple-element.78.pick, bf16[1032,1536]{1,0:T(8,128)(2,1)S(1)} %get-tuple-element.75.pre), custom_call_target="tpu_custom_call" | custom-call | flops 1 | bytes 1 | tf_op jit(solution)/shard_map/pallas_call | solution.py:329
  67.2 2.9 %shard_map.88 = (bf16[384,512]{1,0:T(8,128)(2,1)S(1)}, bf16[384,512]{1,0:T(8,128)(2,1)S(1)}, f32[384,512]{1,0:T(8,128)S(1)}, f32[384,512]{1,0:T(8,128)S(1)}) custom-call(s32[9,8]{1,0:T(8,128)S(1)} %pad_add_fusion.meta, bf16[1536,432]{1,0:T(8,128)(2,1)S(1)} %get-tuple-element.96.lhs_moved, bf16[1536,624]{1,0:T(8,128)(2,1)S(1)} %get-tuple-element.97.lhs_kept, ...), custom_call_target="tpu_custom_call" | custom-call | flops 1 | bytes 1 | tf_op jit(solution)/shard_map/pallas_call | solution.py:345
  72.2 6.7 %collective-permute-done.14.got = bf16[384,512]{1,0:T(8,128)(2,1)S(1)} collective-permute-done((bf16[384,512]{1,0:T(8,128)(2,1)S(1)}, bf16[384,512]{1,0:T(8,128)(2,1)S(1)}, u32[]{:S(2)}, u32[]{:S(2)}) %collective-permute-start.14) | collective-permute-done | bytes 393248 | tf_op jit(solution)/shard_map/ppermute | solution.py:301
  80.0 2.6 %collective-permute-start.20 = (bf16[432,512]{1,0:T(8,128)(2,1)S(1)}, bf16[432,512]{1,0:T(8,128)(2,1)S(1)}, u32[]{:S(2)}, u32[]{:S(2)}) collective-permute-start(bf16[432,512]{1,0:T(8,128)(2,1)S(1)} %get-tuple-element.134), channel_id=1, source_target_pairs={{0,16},{4,20},{8,24},{12,28},{16,0},{20,4},{24,8},{28,12},{1,17},{... | collective-permute-start | bytes 1327112 | tf_op jit(solution)/shard_map/ppermute | solution.py:301
  83.6 3.5 %shard_map.91.kept = bf16[528,1536]{1,0:T(8,128)(2,1)S(1)} custom-call(s32[9,8]{1,0:T(8,128)S(1)} %pad_add_fusion.meta, bf16[624,384]{1,0:T(8,128)(2,1)S(1)} %get-tuple-element.80.refs_4_.p0, bf16[624,384]{1,0:T(8,128)(2,1)S(1)} %collective-permute-done.3.refs_5_.p1, bf16[624,384]{1,0:T(8,128)(2,1)S(1)} %collective-permute-done.5.refs_6_.p2, ...), custom_call_target="tpu_custom_call" | custom-call | flops 1 | bytes 1 | tf_op jit(solution)/shard_map/pallas_call | solution.py:352
  87.1 3.4 %shard_map.92.early = bf16[96,1536]{1,0:T(8,128)(2,1)S(1)} custom-call(s32[9,8]{1,0:T(8,128)S(1)} %pad_add_fusion.meta, bf16[96,1920]{1,0:T(8,128)(2,1)S(1)} %collective-permute-done.own, bf16[96,384]{1,0:T(8,128)(2,1)S(1)} %collective-permute-done.11.p1, bf16[96,384]{1,0:T(8,128)(2,1)S(1)} %collective-permute-done.10.p2, ...), custom_call_target="tpu_custom_call" | custom-call | flops 1 | bytes 1 | tf_op jit(solution)/shard_map/pallas_call | solution.py:420
  95.5 4.3 %collective-permute-done.18.got = bf16[384,512]{1,0:T(8,128)(2,1)S(1)} collective-permute-done((bf16[384,512]{1,0:T(8,128)(2,1)S(1)}, bf16[384,512]{1,0:T(8,128)(2,1)S(1)}, u32[]{:S(2)}, u32[]{:S(2)}) %collective-permute-start.18) | collective-permute-done | bytes 393248 | tf_op jit(solution)/shard_map/ppermute | solution.py:301
  100.7 14.9 %collective-permute-done.19.got = bf16[384,512]{1,0:T(8,128)(2,1)S(1)} collective-permute-done((bf16[384,512]{1,0:T(8,128)(2,1)S(1)}, bf16[384,512]{1,0:T(8,128)(2,1)S(1)}, u32[]{:S(2)}, u32[]{:S(2)}) %collective-permute-start.19) | collective-permute-done | bytes 393248 | tf_op jit(solution)/shard_map/ppermute | solution.py:301
  116.5 3.3 %shard_map.96 = bf16[720,1536]{1,0:T(8,128)(2,1)} custom-call(s32[9,8]{1,0:T(8,128)S(1)} %pad_add_fusion.meta, bf16[528,1536]{1,0:T(8,128)(2,1)S(1)} %shard_map.91.kept, bf16[96,1536]{1,0:T(8,128)(2,1)S(1)} %shard_map.92.early, bf16[432,512]{1,0:T(8,128)(2,1)S(1)} %collective-permute-done.8.rest_0_, bf16[432,512]{1,0:T(8,128)(2,1)S(1)} %collective-permute-done.13.rest_1_, ...), custom_call_target="tpu_custom_call" | custom-call | flops 1 | bytes 1 | tf_op jit(solution)/shard_map/pallas_call | solution.py:435
  119.7 4.8 %collective-permute-done.22 = bf16[192,512]{1,0:T(8,128)(2,1)S(1)} collective-permute-done((bf16[192,512]{1,0:T(8,128)(2,1)S(1)}, bf16[192,512]{1,0:T(8,128)(2,1)S(1)}, u32[]{:S(2)}, u32[]{:S(2)}) %collective-permute-start.22) | collective-permute-done | bytes 196640 | tf_op jit(solution)/shard_map/ppermute | solution.py:301
  124.7 3.0 %collective-permute-done.23 = bf16[192,512]{1,0:T(8,128)(2,1)S(1)} collective-permute-done((bf16[192,512]{1,0:T(8,128)(2,1)S(1)}, bf16[192,512]{1,0:T(8,128)(2,1)S(1)}, u32[]{:S(2)}, u32[]{:S(2)}) %collective-permute-start.23) | collective-permute-done | bytes 196640 | tf_op jit(solution)/shard_map/ppermute | solution.py:301
  (55 shorter events, 30.5 us)
Async XLA Ops:
  5.8 21.3 %collective-permute-start.3 = (bf16[624,384]{1,0:T(8,128)(2,1)S(1)}, bf16[624,384]{1,0:T(8,128)(2,1)S(1)}, u32[]{:S(2)}, u32[]{:S(2)}) collective-permute-start(bf16[624,384]{1,0:T(8,128)(2,1)S(1)} %get-tuple-element.80.refs_4_.p0), channel_id=1, source_target_pairs={{0,1},{1,0},{2,3},{3,2},{4,5},{5,4},{6,7},{7,6},{8,9},{9,8},{10,11... | collective-permute-start | bytes 1437704 | tf_op jit(solution)/shard_map/ppermute | solution.py:301
  6.4 20.7 %collective-permute-start = (bf16[96,1920]{1,0:T(8,128)(2,1)S(1)}, bf16[96,1920]{1,0:T(8,128)(2,1)S(1)}, u32[]{:S(2)}, u32[]{:S(2)}) collective-permute-start(bf16[96,1920]{1,0:T(8,128)(2,1)S(1)} %get-tuple-element.71), channel_id=1, source_target_pairs={{0,16},{4,20},{8,24},{12,28},{16,0},{20,4},{24,8},{28,12},{1,17},{... | collective-permute-start | bytes 1105928 | tf_op jit(solution)/shard_map/ppermute | solution.py:301
  10.0 8.4 %collective-permute-start.2 = (bf16[432,384]{1,0:T(8,128)(2,1)S(1)}, bf16[432,384]{1,0:T(8,128)(2,1)S(1)}, u32[]{:S(2)}, u32[]{:S(2)}) collective-permute-start(bf16[432,384]{1,0:T(8,128)(2,1)S(1)} %get-tuple-element.72.p0.refs_0_), channel_id=1, source_target_pairs={{0,1},{1,0},{2,3},{3,2},{4,5},{5,4},{6,7},{7,6},{8,9},{9,8},{10,11... | collective-permute-start | bytes 995336 | tf_op jit(solution)/shard_map/ppermute | solution.py:301
  10.2 10.6 %collective-permute-start.1 = (bf16[432,384]{1,0:T(8,128)(2,1)S(1)}, bf16[432,384]{1,0:T(8,128)(2,1)S(1)}, u32[]{:S(2)}, u32[]{:S(2)}) collective-permute-start(bf16[432,384]{1,0:T(8,128)(2,1)S(1)} %get-tuple-element.72.p0.refs_0_), channel_id=1, source_target_pairs={{0,2},{1,3},{2,0},{3,1},{4,6},{5,7},{6,4},{7,5},{8,10},{9,11},{10,... | collective-permute-start | bytes 995336 | tf_op jit(solution)/shard_map/ppermute | solution.py:301
  11.7 18.8 %collective-permute-start.5 = (bf16[624,384]{1,0:T(8,128)(2,1)S(1)}, bf16[624,384]{1,0:T(8,128)(2,1)S(1)}, u32[]{:S(2)}, u32[]{:S(2)}) collective-permute-start(bf16[624,384]{1,0:T(8,128)(2,1)S(1)} %get-tuple-element.80.refs_4_.p0), channel_id=1, source_target_pairs={{0,2},{1,3},{2,0},{3,1},{4,6},{5,7},{6,4},{7,5},{8,10},{9,11},{10,... | collective-permute-start | bytes 1437704 | tf_op jit(solution)/shard_map/ppermute | solution.py:301
  27.1 1.6 %collective-permute-start.4 = (bf16[432,384]{1,0:T(8,128)(2,1)S(1)}, bf16[432,384]{1,0:T(8,128)(2,1)S(1)}, u32[]{:S(2)}, u32[]{:S(2)}) collective-permute-start(bf16[432,384]{1,0:T(8,128)(2,1)S(1)} %collective-permute-done.1.p2.refs_2_), channel_id=1, source_target_pairs={{0,1},{1,0},{2,3},{3,2},{4,5},{5,4},{6,7},{7,6},{8,9},{9,8},{10,11... | collective-permute-start | bytes 995336 | tf_op jit(solution)/shard_map/ppermute | solution.py:301
  30.5 1.8 %collective-permute-start.6 = (bf16[624,384]{1,0:T(8,128)(2,1)S(1)}, bf16[624,384]{1,0:T(8,128)(2,1)S(1)}, u32[]{:S(2)}, u32[]{:S(2)}) collective-permute-start(bf16[624,384]{1,0:T(8,128)(2,1)S(1)} %collective-permute-done.5.refs_6_.p2), channel_id=1, source_target_pairs={{0,1},{1,0},{2,3},{3,2},{4,5},{5,4},{6,7},{7,6},{8,9},{9,8},{10,11... | collective-permute-start | bytes 1437704 | tf_op jit(solution)/shard_map/ppermute | solution.py:301
  30.6 22.9 %collective-permute-start.8 = (bf16[432,512]{1,0:T(8,128)(2,1)S(1)}, bf16[432,512]{1,0:T(8,128)(2,1)S(1)}, u32[]{:S(2)}, u32[]{:S(2)}) collective-permute-start(bf16[432,512]{1,0:T(8,128)(2,1)S(1)} %shard_map.80), channel_id=1, source_target_pairs={{0,16},{4,20},{8,24},{12,28},{16,0},{20,4},{24,8},{28,12},{1,17},{... | collective-permute-start | bytes 1327112 | tf_op jit(solution)/shard_map/ppermute | solution.py:301
  35.3 12.0 %collective-permute-start.7 = (bf16[384,512]{1,0:T(8,128)(2,1)S(1)}, bf16[384,512]{1,0:T(8,128)(2,1)S(1)}, u32[]{:S(2)}, u32[]{:S(2)}) collective-permute-start(bf16[384,512]{1,0:T(8,128)(2,1)S(1)} %get-tuple-element.92), channel_id=1, source_target_pairs={{0,4},{4,0},{8,12},{12,8},{16,20},{20,16},{24,28},{28,24},{1,5},{5... | collective-permute-start | bytes 1179656 | tf_op jit(solution)/shard_map/ppermute | solution.py:301
  41.5 16.4 %collective-permute-start.9 = (bf16[384,512]{1,0:T(8,128)(2,1)S(1)}, bf16[384,512]{1,0:T(8,128)(2,1)S(1)}, u32[]{:S(2)}, u32[]{:S(2)}) collective-permute-start(bf16[384,512]{1,0:T(8,128)(2,1)S(1)} %get-tuple-element.101), channel_id=1, source_target_pairs={{0,4},{4,0},{8,12},{12,8},{16,20},{20,16},{24,28},{28,24},{1,5},{5... | collective-permute-start | bytes 1179656 | tf_op jit(solution)/shard_map/ppermute | solution.py:301
  56.3 22.6 %collective-permute-start.15 = (bf16[768,512]{1,0:T(8,128)(2,1)S(1)}, bf16[768,512]{1,0:T(8,128)(2,1)S(1)}, u32[]{:S(2)}, u32[]{:S(2)}) collective-permute-start(bf16[768,512]{1,0:T(8,128)(2,1)S(1)} %get-tuple-element.98), channel_id=1, source_target_pairs={{0,4},{4,0},{8,12},{12,8},{16,20},{20,16},{24,28},{28,24},{1,5},{5... | collective-permute-start | bytes 2359304 | tf_op jit(solution)/shard_map/ppermute | solution.py:301
  57.9 21.0 %collective-permute-start.13 = (bf16[432,512]{1,0:T(8,128)(2,1)S(1)}, bf16[432,512]{1,0:T(8,128)(2,1)S(1)}, u32[]{:S(2)}, u32[]{:S(2)}) collective-permute-start(bf16[432,512]{1,0:T(8,128)(2,1)S(1)} %get-tuple-element.109), channel_id=1, source_target_pairs={{0,16},{4,20},{8,24},{12,28},{16,0},{20,4},{24,8},{28,12},{1,17},{... | collective-permute-start | bytes 1327112 | tf_op jit(solution)/shard_map/ppermute | solution.py:301
  58.9 20.1 %collective-permute-start.14 = (bf16[384,512]{1,0:T(8,128)(2,1)S(1)}, bf16[384,512]{1,0:T(8,128)(2,1)S(1)}, u32[]{:S(2)}, u32[]{:S(2)}) collective-permute-start(bf16[384,512]{1,0:T(8,128)(2,1)S(1)} %get-tuple-element.102), channel_id=1, source_target_pairs={{0,8},{4,12},{8,0},{12,4},{16,24},{20,28},{24,16},{28,20},{1,9},{5... | collective-permute-start | bytes 1179656 | tf_op jit(solution)/shard_map/ppermute | solution.py:301
  60.7 5.0 %collective-permute-start.10 = (bf16[96,384]{1,0:T(8,128)(2,1)S(1)}, bf16[96,384]{1,0:T(8,128)(2,1)S(1)}, u32[]{:S(2)}, u32[]{:S(2)}) collective-permute-start(bf16[96,384]{1,0:T(8,128)(2,1)S(1)} %slice.4), channel_id=1, source_target_pairs={{0,2},{1,3},{2,0},{3,1},{4,6},{5,7},{6,4},{7,5},{8,10},{9,11},{10,... | collective-permute-start | bytes 221192 | tf_op jit(solution)/shard_map/ppermute | solution.py:301
  62.3 3.4 %collective-permute-start.11 = (bf16[96,384]{1,0:T(8,128)(2,1)S(1)}, bf16[96,384]{1,0:T(8,128)(2,1)S(1)}, u32[]{:S(2)}, u32[]{:S(2)}) collective-permute-start(bf16[96,384]{1,0:T(8,128)(2,1)S(1)} %slice.4), channel_id=1, source_target_pairs={{0,1},{1,0},{2,3},{3,2},{4,5},{5,4},{6,7},{7,6},{8,9},{9,8},{10,11... | collective-permute-start | bytes 221192 | tf_op jit(solution)/shard_map/ppermute | solution.py:301
  65.7 1.5 %collective-permute-start.12 = (bf16[96,384]{1,0:T(8,128)(2,1)S(1)}, bf16[96,384]{1,0:T(8,128)(2,1)S(1)}, u32[]{:S(2)}, u32[]{:S(2)}) collective-permute-start(bf16[96,384]{1,0:T(8,128)(2,1)S(1)} %collective-permute-done.10.p2), channel_id=1, source_target_pairs={{0,1},{1,0},{2,3},{3,2},{4,5},{5,4},{6,7},{7,6},{8,9},{9,8},{10,11... | collective-permute-start | bytes 221192 | tf_op jit(solution)/shard_map/ppermute | solution.py:301
  70.1 20.3 %collective-permute-start.16 = (bf16[384,512]{1,0:T(8,128)(2,1)S(1)}, bf16[384,512]{1,0:T(8,128)(2,1)S(1)}, u32[]{:S(2)}, u32[]{:S(2)}) collective-permute-start(bf16[384,512]{1,0:T(8,128)(2,1)S(1)} %get-tuple-element.123), channel_id=1, source_target_pairs={{0,4},{4,0},{8,12},{12,8},{16,20},{20,16},{24,28},{28,24},{1,5},{5... | collective-permute-start | bytes 1179656 | tf_op jit(solution)/shard_map/ppermute | solution.py:301
  70.7 21.6 %collective-permute-start.17 = (bf16[384,512]{1,0:T(8,128)(2,1)S(1)}, bf16[384,512]{1,0:T(8,128)(2,1)S(1)}, u32[]{:S(2)}, u32[]{:S(2)}) collective-permute-start(bf16[384,512]{1,0:T(8,128)(2,1)S(1)} %get-tuple-element.124), channel_id=1, source_target_pairs={{0,4},{4,0},{8,12},{12,8},{16,20},{20,16},{24,28},{28,24},{1,5},{5... | collective-permute-start | bytes 1179656 | tf_op jit(solution)/shard_map/ppermute | solution.py:301
  79.9 19.9 %collective-permute-start.18 = (bf16[384,512]{1,0:T(8,128)(2,1)S(1)}, bf16[384,512]{1,0:T(8,128)(2,1)S(1)}, u32[]{:S(2)}, u32[]{:S(2)}) collective-permute-start(bf16[384,512]{1,0:T(8,128)(2,1)S(1)} %get-tuple-element.112), channel_id=1, source_target_pairs={{0,8},{4,12},{8,0},{12,4},{16,24},{20,28},{24,16},{28,20},{1,9},{5... | collective-permute-start | bytes 1179656 | tf_op jit(solution)/shard_map/ppermute | solution.py:301
  80.0 36.5 %collective-permute-start.20 = (bf16[432,512]{1,0:T(8,128)(2,1)S(1)}, bf16[432,512]{1,0:T(8,128)(2,1)S(1)}, u32[]{:S(2)}, u32[]{:S(2)}) collective-permute-start(bf16[432,512]{1,0:T(8,128)(2,1)S(1)} %get-tuple-element.134), channel_id=1, source_target_pairs={{0,16},{4,20},{8,24},{12,28},{16,0},{20,4},{24,8},{28,12},{1,17},{... | collective-permute-start | bytes 1327112 | tf_op jit(solution)/shard_map/ppermute | solution.py:301
  93.3 22.2 %collective-permute-start.19 = (bf16[384,512]{1,0:T(8,128)(2,1)S(1)}, bf16[384,512]{1,0:T(8,128)(2,1)S(1)}, u32[]{:S(2)}, u32[]{:S(2)}) collective-permute-start(bf16[384,512]{1,0:T(8,128)(2,1)S(1)} %get-tuple-element.125), channel_id=1, source_target_pairs={{0,8},{4,12},{8,0},{12,4},{16,24},{20,28},{24,16},{28,20},{1,9},{5... | collective-permute-start | bytes 1179656 | tf_op jit(solution)/shard_map/ppermute | solution.py:301
  93.4 23.1 %collective-permute-start.21 = (bf16[192,512]{1,0:T(8,128)(2,1)S(1)}, bf16[192,512]{1,0:T(8,128)(2,1)S(1)}, u32[]{:S(2)}, u32[]{:S(2)}) collective-permute-start(bf16[192,512]{1,0:T(8,128)(2,1)S(1)} %get-tuple-element.115), channel_id=1, source_target_pairs={{0,16},{4,20},{8,24},{12,28},{16,0},{20,4},{24,8},{28,12},{1,17},{... | collective-permute-start | bytes 589832 | tf_op jit(solution)/shard_map/ppermute | solution.py:301
  100.6 24.0 %collective-permute-start.22 = (bf16[192,512]{1,0:T(8,128)(2,1)S(1)}, bf16[192,512]{1,0:T(8,128)(2,1)S(1)}, u32[]{:S(2)}, u32[]{:S(2)}) collective-permute-start(bf16[192,512]{1,0:T(8,128)(2,1)S(1)} %get-tuple-element.128), channel_id=1, source_target_pairs={{0,16},{4,20},{8,24},{12,28},{16,0},{20,4},{24,8},{28,12},{1,17},{... | collective-permute-start | bytes 589832 | tf_op jit(solution)/shard_map/ppermute | solution.py:301
  116.4 11.3 %collective-permute-start.23 = (bf16[192,512]{1,0:T(8,128)(2,1)S(1)}, bf16[192,512]{1,0:T(8,128)(2,1)S(1)}, u32[]{:S(2)}, u32[]{:S(2)}) collective-permute-start(bf16[192,512]{1,0:T(8,128)(2,1)S(1)} %get-tuple-element.131), channel_id=1, source_target_pairs={{0,16},{4,20},{8,24},{12,28},{16,0},{20,4},{24,8},{28,12},{1,17},{... | collective-permute-start | bytes 589832 | tf_op jit(solution)/shard_map/ppermute | solution.py:301
  (2 other events, 43.9 us)

commit v22 on v21

--- a/solution.py
+++ b/solution.py
@@ -397,11 +397,11 @@
     act_l, der_l = gelu(after(meta, keep_01), late_pick, part, 2 * part)
     moving_b, moving_c = grads(after(meta, act_l), lates, 0, 0, LATE, part, (der_l,), (part, part))
     act_rb, der_rb = gelu(after(meta, moving_b, gots_a[0]), rest_pick, part, part)
-    send_b, keep_b = weight_again(after(meta, act_rb, arrived_a), 0, act_l, act_rb, 1)
-    got_b = swapped(send_b, "dp", 1)
-    arrived_b = swapped(after(moving_b, send_b), "dp", n // 2)
-
-    out_na, mine_a = near_step(after(meta, send_b), (keep_01, keep_23), gots_a)
+    arrived_b = swapped(moving_b, "dp", n // 2)
+    *sends_b, keep_b01, keep_b23 = weight_again(after(meta, act_rb, arrived_a), 0, act_l, act_rb, 2)
+    gots_b = [swapped(send, "dp", 1) for send in sends_b]
+
+    out_na, mine_a = near_step(after(meta, keep_b01), (keep_01, keep_23), gots_a)
     got_na = swapped(out_na, "dp", 2)
     early_sent = after(arrived_early[:, :width], out_na)
     early_c, early_y = swapped(early_sent, "tensor", 1), swapped(early_sent, "tensor", 2)
@@ -411,7 +411,7 @@
     *sends_c, keep_c01, keep_c23 = weight_again(after(meta, early_yc), part, act_l, act_rc, 2)
     gots_c = [swapped(send, "dp", 1) for send in sends_c]
 
-    out_nb, mine_b = near_step(after(meta, keep_c01, arrived_b, got_na), (keep_b,), (got_b,))
+    out_nb, mine_b = near_step(after(meta, keep_c01, arrived_b, got_na), (keep_b01, keep_b23), gots_b)
     got_nb = swapped(out_nb, "dp", 2)
     arrived_c = swapped(after(moving_c, out_nb), "dp", n // 2)
     out_fa, own_a = far_step(after(meta, out_nb), mine_a, got_na)

time: 129 us -> 137 us (1.062)
  waiting for transfers between devices: 54.3 us -> 59.8 us
  starting transfers between devices: 21.4 us -> 23.7 us
    ppermute x24 -> x25, waiting for transfers between devices: 54.3 us -> 59.8 us  [swapped(): return lax.ppermute(block, axis, [(i, i ^ distance) for i in range(n)])]
    ppermute x24 -> x25, starting transfers between devices: 21.4 us -> 23.7 us  [swapped(): return lax.ppermute(block, axis, [(i, i ^ distance) for i in range(n)])]
  transfers between devices with their start and end apart: 24 -> 25, of which waited for: 14 -> 14; matrix products, arithmetic and copies ran while one was open for 0% -> 0% of each run, Pallas kernels for 36% -> 34%
where the time goes in v22:
time: 137 us
  waiting for transfers between devices  59.8 us (44%)
  Pallas kernels  50.3 us (37%)
  starting transfers between devices  23.7 us (17%)
  other arithmetic  2 us (1%)
    ppermute x25, waiting for transfers between devices, swapped(): return lax.ppermute(block, axis, [(i, i ^ distance) for i in range(n)])  59.8 us
    ppermute x25, starting transfers between devices, swapped(): return lax.ppermute(block, axis, [(i, i ^ distance) for i in range(n)])  23.7 us
    pallas_call x5, Pallas kernels, gelu(): kernel_call(functools.partial(gelu_kernel, base, block), [shape(rows, col...  17.6 us
    pallas_call x3, Pallas kernels, grads(): kernel_call(functools.partial(grad_kernel, first_row, first_slope, base,...  7.37 us
    pallas_call x2, Pallas kernels, weight_again(): kernel_call(functools.partial(again_kernel, base), [shape(rows, part)] *...  5.77 us
    pallas_call x1, Pallas kernels, shards(): kernel_call(first_kernel, [shape(LATE, width), shape(others, width), shap...  4.47 us
    pallas_call x1, Pallas kernels, shards(): kernel_call(functools.partial(early_kernel, 256), shape(EARLY, ff), [IN_V...  3.35 us
    pallas_call x1, Pallas kernels, shards(): kernel_call(functools.partial(place_kernel, (part,) * 3), shape(BAL, ff),...  3.29 us
  transfers between devices with their start and end apart: 25, of which 14 were waited for; matrix products, arithmetic and copies ran while one was open for 0% of the time, Pallas kernels for 34%

profile of v22, /device:TPU:0, one launch (start us, length us, event | category | flops | bytes accessed | tf_op | source)
XLA Modules:
  0.0 136.7 jit_solution(14513605640675461830)
XLA Ops:
  1.4 4.5 %shard_map.77 = (bf16[432,384]{1,0:T(8,128)(2,1)S(1)}, bf16[624,384]{1,0:T(8,128)(2,1)S(1)}, bf16[96,1920]{1,0:T(8,128)(2,1)S(1)}, bf16[432,1032]{1,0:T(8,128)(2...) custom-call(s32[9,8]{1,0:T(8,128)S(1)} %pad_add_fusion.meta, bf16[1032,384]{1,0:T(8,128)(2,1)} %cot_hbm.1, ...), custom_call_target="tpu_custom_call" | custom-call | flops 1 | bytes 1 | tf_op jit(solution)/shard_map/pallas_call | solution.py:370
  6.4 3.6 %collective-permute-start = (bf16[96,1920]{1,0:T(8,128)(2,1)S(1)}, bf16[96,1920]{1,0:T(8,128)(2,1)S(1)}, u32[]{:S(2)}, u32[]{:S(2)}) collective-permute-start(bf16[96,1920]{1,0:T(8,128)(2,1)S(1)} %get-tuple-element.72), channel_id=1, source_target_pairs={{0,16},{4,20},{8,24},{12,28},{16,0},{20,4},{24,8},{28,12},{1,17},{... | collective-permute-start | bytes 1105928 | tf_op jit(solution)/shard_map/ppermute | solution.py:301
  12.2 2.8 %shard_map.78 = (bf16[432,512]{1,0:T(8,128)(2,1)S(1)}, f32[432,512]{1,0:T(8,128)S(1)}) custom-call(s32[9,8]{1,0:T(8,128)S(1)} %pad_add_fusion.meta, bf16[432,1032]{1,0:T(8,128)(2,1)S(1)} %get-tuple-element.75.pick, bf16[1032,1536]{1,0:T(8,128)(2,1)S(1)} %get-tuple-element.76.pre), custom_call_target="tpu_custom_call" | custom-call | flops 1 | bytes 1 | tf_op jit(solution)/shard_map/pallas_call | solution.py:329
  15.0 3.4 %shard_map.79 = (bf16[624,512]{1,0:T(8,128)(2,1)S(1)}, f32[624,512]{1,0:T(8,128)S(1)}) custom-call(s32[9,8]{1,0:T(8,128)S(1)} %pad_add_fusion.meta, bf16[624,1032]{1,0:T(8,128)(2,1)S(1)} %get-tuple-element.79.pick, bf16[1032,1536]{1,0:T(8,128)(2,1)S(1)} %get-tuple-element.76.pre), custom_call_target="tpu_custom_call" | custom-call | flops 1 | bytes 1 | tf_op jit(solution)/shard_map/pallas_call | solution.py:329
  18.4 2.3 %collective-permute-done.1.p2.refs_2_ = bf16[432,384]{1,0:T(8,128)(2,1)S(1)} collective-permute-done((bf16[432,384]{1,0:T(8,128)(2,1)S(1)}, bf16[432,384]{1,0:T(8,128)(2,1)S(1)}, u32[]{:S(2)}, u32[]{:S(2)}) %collective-permute-start.1) | collective-permute-done | bytes 331808 | tf_op jit(solution)/shard_map/ppermute | solution.py:301
  20.8 6.3 %collective-permute-done.own = bf16[96,1920]{1,0:T(8,128)(2,1)S(1)} collective-permute-done((bf16[96,1920]{1,0:T(8,128)(2,1)S(1)}, bf16[96,1920]{1,0:T(8,128)(2,1)S(1)}, u32[]{:S(2)}, u32[]{:S(2)}) %collective-permute-start) | collective-permute-done | bytes 368672 | tf_op jit(solution)/shard_map/ppermute | solution.py:301
  32.3 3.0 %shard_map.81 = (bf16[384,512]{1,0:T(8,128)(2,1)S(1)}, bf16[384,512]{1,0:T(8,128)(2,1)S(1)}, f32[384,512]{1,0:T(8,128)S(1)}, f32[384,512]{1,0:T(8,128)S(1)}, bf1...) custom-call(s32[9,8]{1,0:T(8,128)S(1)} %pad_add_fusion.meta, ...), custom_call_target="tpu_custom_call" | custom-call | flops 1 | bytes 1 | tf_op jit(solution)/shard_map/pallas_call | solution.py:336
  37.4 4.6 %shard_map.82 = (bf16[432,1024]{1,0:T(8,128)(2,1)S(1)}, f32[432,1024]{1,0:T(8,128)S(1)}) custom-call(s32[9,8]{1,0:T(8,128)S(1)} %pad_add_fusion.meta, bf16[432,1032]{1,0:T(8,128)(2,1)S(1)} %get-tuple-element.75.pick, bf16[1032,1536]{1,0:T(8,128)(2,1)S(1)} %get-tuple-element.76.pre), custom_call_target="tpu_custom_call" | custom-call | flops 1 | bytes 1 | tf_op jit(solution)/shard_map/pallas_call | solution.py:329
  42.0 2.3 %shard_map.83 = (bf16[432,512]{1,0:T(8,128)(2,1)S(1)}, bf16[432,512]{1,0:T(8,128)(2,1)S(1)}) custom-call(s32[9,8]{1,0:T(8,128)S(1)} %pad_add_fusion.meta, bf16[432,384]{1,0:T(8,128)(2,1)S(1)} %get-tuple-element.73.p0.refs_0_, bf16[432,384]{1,0:T(8,128)(2,1)S(1)} %collective-permute-done.2.p1.refs_1_, bf16[432,384]{1,0:T(8,128)(2,1)S(1)} %collective-permute-done.1.p2.refs_2_, ...), custom_call_target="tpu_custom_call" | custom-call | flops 1 | bytes 1 | tf_op jit(solution)/shard_map/pallas_call | solution.py:352
  47.3 3.4 %shard_map.84 = (bf16[624,512]{1,0:T(8,128)(2,1)S(1)}, f32[624,512]{1,0:T(8,128)S(1)}) custom-call(s32[9,8]{1,0:T(8,128)S(1)} %pad_add_fusion.meta, bf16[624,1032]{1,0:T(8,128)(2,1)S(1)} %get-tuple-element.79.pick, bf16[1032,1536]{1,0:T(8,128)(2,1)S(1)} %get-tuple-element.76.pre), custom_call_target="tpu_custom_call" | custom-call | flops 1 | bytes 1 | tf_op jit(solution)/shard_map/pallas_call | solution.py:329
  50.7 12.7 %collective-permute-done.8.rest_0_ = bf16[432,512]{1,0:T(8,128)(2,1)S(1)} collective-permute-done((bf16[432,512]{1,0:T(8,128)(2,1)S(1)}, bf16[432,512]{1,0:T(8,128)(2,1)S(1)}, u32[]{:S(2)}, u32[]{:S(2)}) %collective-permute-start.8) | collective-permute-done | bytes 442400 | tf_op jit(solution)/shard_map/ppermute | solution.py:301
  63.4 2.9 %shard_map.85 = (bf16[384,512]{1,0:T(8,128)(2,1)S(1)}, bf16[384,512]{1,0:T(8,128)(2,1)S(1)}, f32[384,512]{1,0:T(8,128)S(1)}, f32[384,512]{1,0:T(8,128)S(1)}) custom-call(s32[9,8]{1,0:T(8,128)S(1)} %pad_add_fusion.meta, bf16[1536,432]{1,0:T(8,128)(2,1)S(1)} %get-tuple-element.97.lhs_moved, bf16[1536,624]{1,0:T(8,128)(2,1)S(1)} %get-tuple-element.98.lhs_kept, ...), custom_call_target="tpu_custom_call" | custom-call | flops 1 | bytes 1 | tf_op jit(solution)/shard_map/pallas_call | solution.py:345
  71.6 3.4 %shard_map.87 = (bf16[624,512]{1,0:T(8,128)(2,1)S(1)}, f32[624,512]{1,0:T(8,128)S(1)}) custom-call(s32[9,8]{1,0:T(8,128)S(1)} %pad_add_fusion.meta, bf16[624,1032]{1,0:T(8,128)(2,1)S(1)} %get-tuple-element.79.pick, bf16[1032,1536]{1,0:T(8,128)(2,1)S(1)} %get-tuple-element.76.pre), custom_call_target="tpu_custom_call" | custom-call | flops 1 | bytes 1 | tf_op jit(solution)/shard_map/pallas_call | solution.py:329
  76.5 2.9 %shard_map.88 = (bf16[384,512]{1,0:T(8,128)(2,1)S(1)}, bf16[384,512]{1,0:T(8,128)(2,1)S(1)}, f32[384,512]{1,0:T(8,128)S(1)}, f32[384,512]{1,0:T(8,128)S(1)}) custom-call(s32[9,8]{1,0:T(8,128)S(1)} %pad_add_fusion.meta, bf16[1536,432]{1,0:T(8,128)(2,1)S(1)} %get-tuple-element.97.lhs_moved, bf16[1536,624]{1,0:T(8,128)(2,1)S(1)} %get-tuple-element.98.lhs_kept, ...), custom_call_target="tpu_custom_call" | custom-call | flops 1 | bytes 1 | tf_op jit(solution)/shard_map/pallas_call | solution.py:345
  81.5 7.9 %collective-permute-done.16.refs_3_ = bf16[384,512]{1,0:T(8,128)(2,1)S(1)} collective-permute-done((bf16[384,512]{1,0:T(8,128)(2,1)S(1)}, bf16[384,512]{1,0:T(8,128)(2,1)S(1)}, u32[]{:S(2)}, u32[]{:S(2)}) %collective-permute-start.16) | collective-permute-done | bytes 393248 | tf_op jit(solution)/shard_map/ppermute | solution.py:301
  90.3 2.1 %collective-permute-start.19 = (bf16[384,512]{1,0:T(8,128)(2,1)S(1)}, bf16[384,512]{1,0:T(8,128)(2,1)S(1)}, u32[]{:S(2)}, u32[]{:S(2)}) collective-permute-start(bf16[384,512]{1,0:T(8,128)(2,1)S(1)} %get-tuple-element.114), channel_id=1, source_target_pairs={{0,8},{4,12},{8,0},{12,4},{16,24},{20,28},{24,16},{28,20},{1,9},{5... | collective-permute-start | bytes 1179656 | tf_op jit(solution)/shard_map/ppermute | solution.py:301
  93.5 3.5 %shard_map.91.kept = bf16[528,1536]{1,0:T(8,128)(2,1)S(1)} custom-call(s32[9,8]{1,0:T(8,128)S(1)} %pad_add_fusion.meta, bf16[624,384]{1,0:T(8,128)(2,1)S(1)} %get-tuple-element.81.refs_4_.p0, bf16[624,384]{1,0:T(8,128)(2,1)S(1)} %collective-permute-done.3.refs_5_.p1, bf16[624,384]{1,0:T(8,128)(2,1)S(1)} %collective-permute-done.5.refs_6_.p2, ...), custom_call_target="tpu_custom_call" | custom-call | flops 1 | bytes 1 | tf_op jit(solution)/shard_map/pallas_call | solution.py:352
  96.9 3.4 %shard_map.92.early = bf16[96,1536]{1,0:T(8,128)(2,1)S(1)} custom-call(s32[9,8]{1,0:T(8,128)S(1)} %pad_add_fusion.meta, bf16[96,1920]{1,0:T(8,128)(2,1)S(1)} %collective-permute-done.own, bf16[96,384]{1,0:T(8,128)(2,1)S(1)} %collective-permute-done.11.p1, bf16[96,384]{1,0:T(8,128)(2,1)S(1)} %collective-permute-done.10.p2, ...), custom_call_target="tpu_custom_call" | custom-call | flops 1 | bytes 1 | tf_op jit(solution)/shard_map/pallas_call | solution.py:420
  100.3 3.6 %collective-permute-done.18.refs_3_ = bf16[384,512]{1,0:T(8,128)(2,1)S(1)} collective-permute-done((bf16[384,512]{1,0:T(8,128)(2,1)S(1)}, bf16[384,512]{1,0:T(8,128)(2,1)S(1)}, u32[]{:S(2)}, u32[]{:S(2)}) %collective-permute-start.18) | collective-permute-done | bytes 393248 | tf_op jit(solution)/shard_map/ppermute | solution.py:301
  108.1 2.4 %collective-permute-start.23 = (bf16[192,512]{1,0:T(8,128)(2,1)S(1)}, bf16[192,512]{1,0:T(8,128)(2,1)S(1)}, u32[]{:S(2)}, u32[]{:S(2)}) collective-permute-start(bf16[192,512]{1,0:T(8,128)(2,1)S(1)} %get-tuple-element.130), channel_id=1, source_target_pairs={{0,16},{4,20},{8,24},{12,28},{16,0},{20,4},{24,8},{28,12},{1,17},{... | collective-permute-start | bytes 589832 | tf_op jit(solution)/shard_map/ppermute | solution.py:301
  110.5 11.7 %collective-permute-done.20.got = bf16[384,512]{1,0:T(8,128)(2,1)S(1)} collective-permute-done((bf16[384,512]{1,0:T(8,128)(2,1)S(1)}, bf16[384,512]{1,0:T(8,128)(2,1)S(1)}, u32[]{:S(2)}, u32[]{:S(2)}) %collective-permute-start.20) | collective-permute-done | bytes 393248 | tf_op jit(solution)/shard_map/ppermute | solution.py:301
  123.6 3.3 %shard_map.96 = bf16[720,1536]{1,0:T(8,128)(2,1)} custom-call(s32[9,8]{1,0:T(8,128)S(1)} %pad_add_fusion.meta, bf16[528,1536]{1,0:T(8,128)(2,1)S(1)} %shard_map.91.kept, bf16[96,1536]{1,0:T(8,128)(2,1)S(1)} %shard_map.92.early, bf16[432,512]{1,0:T(8,128)(2,1)S(1)} %collective-permute-done.8.rest_0_, bf16[432,512]{1,0:T(8,128)(2,1)S(1)} %collective-permute-done.13.rest_1_, ...), custom_call_target="tpu_custom_call" | custom-call | flops 1 | bytes 1 | tf_op jit(solution)/shard_map/pallas_call | solution.py:435
  126.9 5.8 %collective-permute-done.23 = bf16[192,512]{1,0:T(8,128)(2,1)S(1)} collective-permute-done((bf16[192,512]{1,0:T(8,128)(2,1)S(1)}, bf16[192,512]{1,0:T(8,128)(2,1)S(1)}, u32[]{:S(2)}, u32[]{:S(2)}) %collective-permute-start.23) | collective-permute-done | bytes 196640 | tf_op jit(solution)/shard_map/ppermute | solution.py:301
  132.8 2.7 %collective-permute-done.24 = bf16[192,512]{1,0:T(8,128)(2,1)S(1)} collective-permute-done((bf16[192,512]{1,0:T(8,128)(2,1)S(1)}, bf16[192,512]{1,0:T(8,128)(2,1)S(1)}, u32[]{:S(2)}, u32[]{:S(2)}) %collective-permute-start.24) | collective-permute-done | bytes 196640 | tf_op jit(solution)/shard_map/ppermute | solution.py:301
  (57 shorter events, 31.4 us)
Async XLA Ops:
  5.8 21.3 %collective-permute-start.3 = (bf16[624,384]{1,0:T(8,128)(2,1)S(1)}, bf16[624,384]{1,0:T(8,128)(2,1)S(1)}, u32[]{:S(2)}, u32[]{:S(2)}) collective-permute-start(bf16[624,384]{1,0:T(8,128)(2,1)S(1)} %get-tuple-element.81.refs_4_.p0), channel_id=1, source_target_pairs={{0,1},{1,0},{2,3},{3,2},{4,5},{5,4},{6,7},{7,6},{8,9},{9,8},{10,11... | collective-permute-start | bytes 1437704 | tf_op jit(solution)/shard_map/ppermute | solution.py:301
  6.4 20.7 %collective-permute-start = (bf16[96,1920]{1,0:T(8,128)(2,1)S(1)}, bf16[96,1920]{1,0:T(8,128)(2,1)S(1)}, u32[]{:S(2)}, u32[]{:S(2)}) collective-permute-start(bf16[96,1920]{1,0:T(8,128)(2,1)S(1)} %get-tuple-element.72), channel_id=1, source_target_pairs={{0,16},{4,20},{8,24},{12,28},{16,0},{20,4},{24,8},{28,12},{1,17},{... | collective-permute-start | bytes 1105928 | tf_op jit(solution)/shard_map/ppermute | solution.py:301
  10.0 8.4 %collective-permute-start.2 = (bf16[432,384]{1,0:T(8,128)(2,1)S(1)}, bf16[432,384]{1,0:T(8,128)(2,1)S(1)}, u32[]{:S(2)}, u32[]{:S(2)}) collective-permute-start(bf16[432,384]{1,0:T(8,128)(2,1)S(1)} %get-tuple-element.73.p0.refs_0_), channel_id=1, source_target_pairs={{0,1},{1,0},{2,3},{3,2},{4,5},{5,4},{6,7},{7,6},{8,9},{9,8},{10,11... | collective-permute-start | bytes 995336 | tf_op jit(solution)/shard_map/ppermute | solution.py:301
  10.2 10.6 %collective-permute-start.1 = (bf16[432,384]{1,0:T(8,128)(2,1)S(1)}, bf16[432,384]{1,0:T(8,128)(2,1)S(1)}, u32[]{:S(2)}, u32[]{:S(2)}) collective-permute-start(bf16[432,384]{1,0:T(8,128)(2,1)S(1)} %get-tuple-element.73.p0.refs_0_), channel_id=1, source_target_pairs={{0,2},{1,3},{2,0},{3,1},{4,6},{5,7},{6,4},{7,5},{8,10},{9,11},{10,... | collective-permute-start | bytes 995336 | tf_op jit(solution)/shard_map/ppermute | solution.py:301
  11.7 18.8 %collective-permute-start.5 = (bf16[624,384]{1,0:T(8,128)(2,1)S(1)}, bf16[624,384]{1,0:T(8,128)(2,1)S(1)}, u32[]{:S(2)}, u32[]{:S(2)}) collective-permute-start(bf16[624,384]{1,0:T(8,128)(2,1)S(1)} %get-tuple-element.81.refs_4_.p0), channel_id=1, source_target_pairs={{0,2},{1,3},{2,0},{3,1},{4,6},{5,7},{6,4},{7,5},{8,10},{9,11},{10,... | collective-permute-start | bytes 1437704 | tf_op jit(solution)/shard_map/ppermute | solution.py:301
  27.1 1.6 %collective-permute-start.4 = (bf16[432,384]{1,0:T(8,128)(2,1)S(1)}, bf16[432,384]{1,0:T(8,128)(2,1)S(1)}, u32[]{:S(2)}, u32[]{:S(2)}) collective-permute-start(bf16[432,384]{1,0:T(8,128)(2,1)S(1)} %collective-permute-done.1.p2.refs_2_), channel_id=1, source_target_pairs={{0,1},{1,0},{2,3},{3,2},{4,5},{5,4},{6,7},{7,6},{8,9},{9,8},{10,11... | collective-permute-start | bytes 995336 | tf_op jit(solution)/shard_map/ppermute | solution.py:301
  30.5 1.8 %collective-permute-start.6 = (bf16[624,384]{1,0:T(8,128)(2,1)S(1)}, bf16[624,384]{1,0:T(8,128)(2,1)S(1)}, u32[]{:S(2)}, u32[]{:S(2)}) collective-permute-start(bf16[624,384]{1,0:T(8,128)(2,1)S(1)} %collective-permute-done.5.refs_6_.p2), channel_id=1, source_target_pairs={{0,1},{1,0},{2,3},{3,2},{4,5},{5,4},{6,7},{7,6},{8,9},{9,8},{10,11... | collective-permute-start | bytes 1437704 | tf_op jit(solution)/shard_map/ppermute | solution.py:301
  30.6 32.8 %collective-permute-start.8 = (bf16[432,512]{1,0:T(8,128)(2,1)S(1)}, bf16[432,512]{1,0:T(8,128)(2,1)S(1)}, u32[]{:S(2)}, u32[]{:S(2)}) collective-permute-start(bf16[432,512]{1,0:T(8,128)(2,1)S(1)} %shard_map.80), channel_id=1, source_target_pairs={{0,16},{4,20},{8,24},{12,28},{16,0},{20,4},{24,8},{28,12},{1,17},{... | collective-permute-start | bytes 1327112 | tf_op jit(solution)/shard_map/ppermute | solution.py:301
  35.3 12.0 %collective-permute-start.7 = (bf16[384,512]{1,0:T(8,128)(2,1)S(1)}, bf16[384,512]{1,0:T(8,128)(2,1)S(1)}, u32[]{:S(2)}, u32[]{:S(2)}) collective-permute-start(bf16[384,512]{1,0:T(8,128)(2,1)S(1)} %get-tuple-element.93), channel_id=1, source_target_pairs={{0,4},{4,0},{8,12},{12,8},{16,20},{20,16},{24,28},{28,24},{1,5},{5... | collective-permute-start | bytes 1179656 | tf_op jit(solution)/shard_map/ppermute | solution.py:301
  36.9 29.4 %collective-permute-start.9 = (bf16[384,512]{1,0:T(8,128)(2,1)S(1)}, bf16[384,512]{1,0:T(8,128)(2,1)S(1)}, u32[]{:S(2)}, u32[]{:S(2)}) collective-permute-start(bf16[384,512]{1,0:T(8,128)(2,1)S(1)} %get-tuple-element.102), channel_id=1, source_target_pairs={{0,4},{4,0},{8,12},{12,8},{16,20},{20,16},{24,28},{28,24},{1,5},{5... | collective-permute-start | bytes 1179656 | tf_op jit(solution)/shard_map/ppermute | solution.py:301
  44.3 36.8 %collective-permute-start.13 = (bf16[432,512]{1,0:T(8,128)(2,1)S(1)}, bf16[432,512]{1,0:T(8,128)(2,1)S(1)}, u32[]{:S(2)}, u32[]{:S(2)}) collective-permute-start(bf16[432,512]{1,0:T(8,128)(2,1)S(1)} %get-tuple-element.92), channel_id=1, source_target_pairs={{0,16},{4,20},{8,24},{12,28},{16,0},{20,4},{24,8},{28,12},{1,17},{... | collective-permute-start | bytes 1327112 | tf_op jit(solution)/shard_map/ppermute | solution.py:301
  67.2 4.4 %collective-permute-start.10 = (bf16[96,384]{1,0:T(8,128)(2,1)S(1)}, bf16[96,384]{1,0:T(8,128)(2,1)S(1)}, u32[]{:S(2)}, u32[]{:S(2)}) collective-permute-start(bf16[96,384]{1,0:T(8,128)(2,1)S(1)} %slice.4), channel_id=1, source_target_pairs={{0,2},{1,3},{2,0},{3,1},{4,6},{5,7},{6,4},{7,5},{8,10},{9,11},{10,... | collective-permute-start | bytes 221192 | tf_op jit(solution)/shard_map/ppermute | solution.py:301
  68.9 12.6 %collective-permute-start.14 = (bf16[384,512]{1,0:T(8,128)(2,1)S(1)}, bf16[384,512]{1,0:T(8,128)(2,1)S(1)}, u32[]{:S(2)}, u32[]{:S(2)}) collective-permute-start(bf16[384,512]{1,0:T(8,128)(2,1)S(1)} %get-tuple-element.103), channel_id=1, source_target_pairs={{0,8},{4,12},{8,0},{12,4},{16,24},{20,28},{24,16},{28,20},{1,9},{5... | collective-permute-start | bytes 1179656 | tf_op jit(solution)/shard_map/ppermute | solution.py:301
  68.9 12.6 %collective-permute-start.15 = (bf16[384,512]{1,0:T(8,128)(2,1)S(1)}, bf16[384,512]{1,0:T(8,128)(2,1)S(1)}, u32[]{:S(2)}, u32[]{:S(2)}) collective-permute-start(bf16[384,512]{1,0:T(8,128)(2,1)S(1)} %get-tuple-element.112), channel_id=1, source_target_pairs={{0,4},{4,0},{8,12},{12,8},{16,20},{20,16},{24,28},{28,24},{1,5},{5... | collective-permute-start | bytes 1179656 | tf_op jit(solution)/shard_map/ppermute | solution.py:301
  70.4 19.0 %collective-permute-start.16 = (bf16[384,512]{1,0:T(8,128)(2,1)S(1)}, bf16[384,512]{1,0:T(8,128)(2,1)S(1)}, u32[]{:S(2)}, u32[]{:S(2)}) collective-permute-start(bf16[384,512]{1,0:T(8,128)(2,1)S(1)} %get-tuple-element.113), channel_id=1, source_target_pairs={{0,4},{4,0},{8,12},{12,8},{16,20},{20,16},{24,28},{28,24},{1,5},{5... | collective-permute-start | bytes 1179656 | tf_op jit(solution)/shard_map/ppermute | solution.py:301
  71.6 3.4 %collective-permute-start.11 = (bf16[96,384]{1,0:T(8,128)(2,1)S(1)}, bf16[96,384]{1,0:T(8,128)(2,1)S(1)}, u32[]{:S(2)}, u32[]{:S(2)}) collective-permute-start(bf16[96,384]{1,0:T(8,128)(2,1)S(1)} %slice.4), channel_id=1, source_target_pairs={{0,1},{1,0},{2,3},{3,2},{4,5},{5,4},{6,7},{7,6},{8,9},{9,8},{10,11... | collective-permute-start | bytes 221192 | tf_op jit(solution)/shard_map/ppermute | solution.py:301
  79.4 20.9 %collective-permute-start.17 = (bf16[384,512]{1,0:T(8,128)(2,1)S(1)}, bf16[384,512]{1,0:T(8,128)(2,1)S(1)}, u32[]{:S(2)}, u32[]{:S(2)}) collective-permute-start(bf16[384,512]{1,0:T(8,128)(2,1)S(1)} %get-tuple-element.125), channel_id=1, source_target_pairs={{0,4},{4,0},{8,12},{12,8},{16,20},{20,16},{24,28},{28,24},{1,5},{5... | collective-permute-start | bytes 1179656 | tf_op jit(solution)/shard_map/ppermute | solution.py:301
  81.1 22.8 %collective-permute-start.18 = (bf16[384,512]{1,0:T(8,128)(2,1)S(1)}, bf16[384,512]{1,0:T(8,128)(2,1)S(1)}, u32[]{:S(2)}, u32[]{:S(2)}) collective-permute-start(bf16[384,512]{1,0:T(8,128)(2,1)S(1)} %get-tuple-element.126), channel_id=1, source_target_pairs={{0,4},{4,0},{8,12},{12,8},{16,20},{20,16},{24,28},{28,24},{1,5},{5... | collective-permute-start | bytes 1179656 | tf_op jit(solution)/shard_map/ppermute | solution.py:301
  90.3 16.9 %collective-permute-start.19 = (bf16[384,512]{1,0:T(8,128)(2,1)S(1)}, bf16[384,512]{1,0:T(8,128)(2,1)S(1)}, u32[]{:S(2)}, u32[]{:S(2)}) collective-permute-start(bf16[384,512]{1,0:T(8,128)(2,1)S(1)} %get-tuple-element.114), channel_id=1, source_target_pairs={{0,8},{4,12},{8,0},{12,4},{16,24},{20,28},{24,16},{28,20},{1,9},{5... | collective-permute-start | bytes 1179656 | tf_op jit(solution)/shard_map/ppermute | solution.py:301
  92.4 31.2 %collective-permute-start.21 = (bf16[432,512]{1,0:T(8,128)(2,1)S(1)}, bf16[432,512]{1,0:T(8,128)(2,1)S(1)}, u32[]{:S(2)}, u32[]{:S(2)}) collective-permute-start(bf16[432,512]{1,0:T(8,128)(2,1)S(1)} %get-tuple-element.136), channel_id=1, source_target_pairs={{0,16},{4,20},{8,24},{12,28},{16,0},{20,4},{24,8},{28,12},{1,17},{... | collective-permute-start | bytes 1327112 | tf_op jit(solution)/shard_map/ppermute | solution.py:301
  104.9 17.3 %collective-permute-start.20 = (bf16[384,512]{1,0:T(8,128)(2,1)S(1)}, bf16[384,512]{1,0:T(8,128)(2,1)S(1)}, u32[]{:S(2)}, u32[]{:S(2)}) collective-permute-start(bf16[384,512]{1,0:T(8,128)(2,1)S(1)} %get-tuple-element.127), channel_id=1, source_target_pairs={{0,8},{4,12},{8,0},{12,4},{16,24},{20,28},{24,16},{28,20},{1,9},{5... | collective-permute-start | bytes 1179656 | tf_op jit(solution)/shard_map/ppermute | solution.py:301
  106.7 20.2 %collective-permute-start.22 = (bf16[192,512]{1,0:T(8,128)(2,1)S(1)}, bf16[192,512]{1,0:T(8,128)(2,1)S(1)}, u32[]{:S(2)}, u32[]{:S(2)}) collective-permute-start(bf16[192,512]{1,0:T(8,128)(2,1)S(1)} %get-tuple-element.117), channel_id=1, source_target_pairs={{0,16},{4,20},{8,24},{12,28},{16,0},{20,4},{24,8},{28,12},{1,17},{... | collective-permute-start | bytes 589832 | tf_op jit(solution)/shard_map/ppermute | solution.py:301
  108.1 24.6 %collective-permute-start.23 = (bf16[192,512]{1,0:T(8,128)(2,1)S(1)}, bf16[192,512]{1,0:T(8,128)(2,1)S(1)}, u32[]{:S(2)}, u32[]{:S(2)}) collective-permute-start(bf16[192,512]{1,0:T(8,128)(2,1)S(1)} %get-tuple-element.130), channel_id=1, source_target_pairs={{0,16},{4,20},{8,24},{12,28},{16,0},{20,4},{24,8},{28,12},{1,17},{... | collective-permute-start | bytes 589832 | tf_op jit(solution)/shard_map/ppermute | solution.py:301
  123.0 12.5 %collective-permute-start.24 = (bf16[192,512]{1,0:T(8,128)(2,1)S(1)}, bf16[192,512]{1,0:T(8,128)(2,1)S(1)}, u32[]{:S(2)}, u32[]{:S(2)}) collective-permute-start(bf16[192,512]{1,0:T(8,128)(2,1)S(1)} %get-tuple-element.133), channel_id=1, source_target_pairs={{0,16},{4,20},{8,24},{12,28},{16,0},{20,4},{24,8},{28,12},{1,17},{... | collective-permute-start | bytes 589832 | tf_op jit(solution)/shard_map/ppermute | solution.py:301
  (3 other events, 45.4 us)
